TPU v7x, 32 devices: a whole 2x2x4 slice. The times are simulated.
32 devices in a mesh: grp: 4 (over x, core), reg: 8 (over z, y).
Axes of the slice: x: 2, y: 2, z: 4, core: 2. Of those that a mesh axis runs over, the one named last changes fastest.
Arguments:
- grain_pos: float32 [3, 524288], P(None, ('grp', 'reg')), may hold values from -6 to 6
- grain_vel: float32 [3, 524288], P(None, ('grp', 'reg')), may hold values from -6 to 6
- grain_vol: float32 [524288], P(('grp', 'reg')), may hold values from 0.5 to 2
- drag_coef: float32 [524288], P(('grp', 'reg')), may hold values from 0.2 to 2
- grain_count: int32 [32], P(('grp', 'reg')), may hold values from 0 to 16384, as said below
- contact_rows: int32 [8, 524288], P(None, ('grp', 'reg')), may hold values from -1 to 255, as said below
- contact_stiff: float32 [8, 524288], P(None, ('grp', 'reg')), may hold values from 0.05 to 0.5
- partner_block: int32 [4096], P(('grp', 'reg')), may hold values from 0 to 191, as said below
- halo_list: int32 [2, 131072], P(None, ('grp', 'reg')), may hold values from 0 to 16383, as said below
- grain_cell: int32 [524288], P(('grp', 'reg')), may hold values from 0 to 127
- tile_cell_block: int32 [4096], P(('grp', 'reg')), may hold values from 0 to 2047
- pressure_old: float32 [32, 128, 512], P('reg'), may hold values from -6 to 6
- pressure_source: float32 [32, 128, 512], P('reg'), may hold values from -6 to 6
- solid_old: float32 [32, 128, 512], P('reg'), may hold values from 0 to 1.5
Outputs:
- new_vel: float32 [3, 524288], P(None, ('grp', 'reg'))
Inputs may be any that keep to these rules, and one draw needn't show every extreme that they name: `grain_count`: devices of the last grp index hold no grains; a device's live grains fill its first slots; some device holds 16384. `contact_rows`: for a live grain in block t, entries 0 to 127 name grains of block t and entries 128 to 255 name grains of block partner_block[t]; every named grain is live; -1 marks an empty slot. Entries of slots that are not live carry no meaning. `partner_block`: blocks below 128 are the device's own, the next 32 are those received from the lower region, the last 32 those from the upper region; a block holding live grains never names a region that does not exist. `halo_list`: every entry names a live grain of its device where the device holds grains, else 0.
All inputs are finite; a program needn't handle non-finite values.
Results may differ from a plain program's by a relative error of at most 0.0003.
Values sent between devices are 32-bit elements; how exact they have to be, the bound alone decides.
No kernel may reach another device: no remote copies, remote signals or barrier semaphores. Data moves between devices by JAX's collectives and lax.ppermute only.
A program may use at most 64 MiB of HBM per device.

v0:
```python
import jax
import jax.numpy as jnp
from jax import lax
from jax.sharding import PartitionSpec as P

BLOCK = 128
ITERS = 4
HALO = 4096


SPRING = 1.0
DAMPING = 0.5
TIME_STEP = 0.5


def with_halo(shard, sides, width):
    for axis, dim in sides:
        count, length = (lax.axis_size(axis), shard.shape[dim])
        up = [(i, (i + 1) % count) for i in range(count - 1)]
        down = [(j, i) for i, j in up]
        last = lax.slice_in_dim(shard, length - width, length, axis=dim)
        initial = lax.slice_in_dim(shard, 0, width, axis=dim)
        before = lax.ppermute(last, axis, up)
        after = lax.ppermute(initial, axis, down)
        shard = jnp.concatenate([before, shard, after], axis=dim)
    return shard


def neighbours(padded):
    summed = padded[2:, 1:-1, 1:-1] + padded[:-2, 1:-1, 1:-1]
    summed = summed + padded[1:-1, 2:, 1:-1] + padded[1:-1, :-2, 1:-1]
    return summed + padded[1:-1, 1:-1, 2:] + padded[1:-1, 1:-1, :-2]


def rim_whole(pressure):
    padded = with_halo(pressure, (("reg", 0),), 1)
    return jnp.pad(padded, ((0, 0), (1, 1), (1, 1)))


def relax(pressure, source, solid_before, solid_now, drag_sum, extend):
    porous = 1.0 / (1.0 + solid_now)
    diagonal = 6.0 * porous + drag_sum + 1.0
    driving = source + solid_now - solid_before
    for sweep_index in range(ITERS):
        pressure = (driving + porous * neighbours(extend(pressure))) / diagonal
    return (pressure, 1.0 / (porous + drag_sum))


def place_blocks(tile_rows, block_ids, block_count, grid_shape):
    placing = (block_ids[:, None] == lax.broadcasted_iota(jnp.int32, (1, block_count), 1)).astype(
        jnp.float32
    )
    placed = jnp.einsum("ltc,tb->lbc", tile_rows, placing, precision=lax.Precision.HIGHEST)
    return placed.reshape((tile_rows.shape[0],) + grid_shape)


def contact_forces(grain_state, extended, contact_rows, contact_stiff, partner_block):
    slots_here = grain_state.shape[1]
    tiles_here = slots_here // BLOCK
    per_step = 8
    slot_count = contact_rows.shape[0]
    partner = jnp.take(extended.reshape(6, -1, BLOCK), partner_block, axis=1)
    paired = jnp.concatenate([grain_state.reshape(6, tiles_here, BLOCK), partner], 2)
    rows_tiled = contact_rows.reshape(slot_count, tiles_here, BLOCK)
    stiff_tiled = contact_stiff.reshape(slot_count, tiles_here, BLOCK)
    columns = lax.broadcasted_iota(jnp.int32, (per_step, BLOCK, 2 * BLOCK), 2)

    def step_forces(step_index, forces):
        first_tile = step_index * per_step
        pair_step = lax.dynamic_slice_in_dim(paired, first_tile, per_step, 1)
        rows_step = lax.dynamic_slice_in_dim(rows_tiled, first_tile, per_step, 1)
        stiff_step = lax.dynamic_slice_in_dim(stiff_tiled, first_tile, per_step, 1)
        weights = jnp.zeros((per_step, BLOCK, 2 * BLOCK), jnp.float32)
        for slot_index in range(slot_count):
            weights = weights + jnp.where(
                rows_step[slot_index][:, :, None] == columns,
                stiff_step[slot_index][:, :, None],
                0.0,
            )
        summed = jnp.einsum("tij,ctj->cti", weights, pair_step, precision=lax.Precision.HIGHEST)
        stiff_total = jnp.sum(jnp.where(rows_step >= 0, stiff_step, 0.0), 0)
        own_rows = pair_step[:, :, :BLOCK]
        spring = SPRING * (stiff_total * own_rows[:3] - summed[:3])
        damper = DAMPING * (summed[3:] - stiff_total * own_rows[3:])
        return lax.dynamic_update_slice_in_dim(forces, spring + damper, first_tile, 1)

    zero_forces = jnp.zeros((3, tiles_here, BLOCK), jnp.float32)
    forces = lax.fori_loop(0, tiles_here // per_step, step_forces, zero_forces)
    return forces.reshape(3, slots_here)


def on_device(
    grain_pos,
    grain_vel,
    grain_vol,
    drag_coef,
    grain_count,
    contact_rows,
    contact_stiff,
    partner_block,
    halo_list,
    grain_cell,
    tile_cell_block,
    pressure_old,
    pressure_source,
    solid_old,
):
    held_grains = grain_count[0]
    slots_here = grain_pos.shape[1]
    tiles_here = slots_here // BLOCK
    live_mask = (jnp.arange(slots_here) < held_grains).astype(jnp.float32)
    grain_state = jnp.concatenate([grain_pos, grain_vel], 0)
    outgoing = jnp.take(grain_state, halo_list.reshape(-1), axis=1)
    rimmed = with_halo(outgoing, (("reg", 1),), HALO)
    extended = jnp.concatenate([grain_state, rimmed[:, :HALO], rimmed[:, 3 * HALO :]], 1)
    contact = contact_forces(grain_state, extended, contact_rows, contact_stiff, partner_block)
    grid_shape = pressure_old.shape
    block_count = pressure_old.size // BLOCK
    inner = (
        grain_cell.reshape(tiles_here, BLOCK)[:, :, None]
        == lax.broadcasted_iota(jnp.int32, (1, 1, BLOCK), 2)
    ).astype(jnp.float32)
    loads = jnp.stack([grain_vol * live_mask, drag_coef * live_mask]).reshape(2, tiles_here, BLOCK)
    tile_loads = jnp.einsum("ltg,tgc->ltc", loads, inner, precision=lax.Precision.HIGHEST)
    part_fields = place_blocks(tile_loads, tile_cell_block, block_count, grid_shape)
    solid_part, drag_part = (part_fields[0], part_fields[1])
    solid_now, drag_sum = lax.psum((solid_part, drag_part), "grp")
    pressure, weight = relax(
        pressure_old, pressure_source, solid_old, solid_now, drag_sum, rim_whole
    )
    padded = with_halo(pressure, (("reg", 0),), 1)
    padded = jnp.pad(padded, ((0, 0), (1, 1), (1, 1)))
    grad_x = 0.5 * (padded[2:, 1:-1, 1:-1] - padded[:-2, 1:-1, 1:-1])
    grad_y = 0.5 * (padded[1:-1, 2:, 1:-1] - padded[1:-1, :-2, 1:-1])
    grad_z = 0.5 * (padded[1:-1, 1:-1, 2:] - padded[1:-1, 1:-1, :-2])
    fields = jnp.stack([grad_x, grad_y, grad_z, weight]).reshape(4, block_count, BLOCK)
    picking = (
        tile_cell_block[:, None] == lax.broadcasted_iota(jnp.int32, (1, block_count), 1)
    ).astype(jnp.float32)
    tile_fields = jnp.einsum("lbc,tb->ltc", fields, picking, precision=lax.Precision.HIGHEST)
    at_grain = jnp.einsum(
        "ltc,tgc->ltg", tile_fields, inner, precision=lax.Precision.HIGHEST
    ).reshape(4, slots_here)
    gradient = at_grain[:3]
    fluid_vel = -gradient * at_grain[3]
    force = contact - grain_vol * gradient + drag_coef * (fluid_vel - grain_vel)
    return (grain_vel + TIME_STEP * force / grain_vol) * live_mask


def solution(mesh):
    in_specs = (
        P(None, ("grp", "reg")),
        P(None, ("grp", "reg")),
        P(("grp", "reg")),
        P(("grp", "reg")),
        P(("grp", "reg")),
        P(None, ("grp", "reg")),
        P(None, ("grp", "reg")),
        P(("grp", "reg")),
        P(None, ("grp", "reg")),
        P(("grp", "reg")),
        P(("grp", "reg")),
        P("reg", None, None),
        P("reg", None, None),
        P("reg", None, None),
    )
    out_specs = P(None, ("grp", "reg"))
    return jax.shard_map(
        on_device, mesh=mesh, in_specs=in_specs, out_specs=out_specs, check_vma=False
    )
```

profile of v0, /device:TPU:0, one launch (start us, length us, event | category | flops | bytes accessed | tf_op | source)
XLA Modules:
  0.0 303.7 jit_solution(16163357141205119206)
XLA Ops:
  8.9 6.2 %collective-permute-start.3 = (f32[1,128,512]{2,1,0:T(8,128)S(1)}, f32[1,128,512]{2,1,0:T(8,128)}, u32[]{:S(2)}, u32[]{:S(2)}) collective-permute-start(f32[1,128,512]{2,1,0:T(8,128)S(1)} %get-tuple-element.216), channel_id=1, source_target_pairs={{0,1},{1,2},{2,3},{3,4},{4,5},{5,6},{6,7},{8,9},{9,10},{10,11},{11... | collective-permute-start | bytes 786440 | tf_op jit(solution)/shard_map/ppermute | solution.py:23
  16.7 6.5 %fusion.76 = f32[2,128,128]{2,0,1:T(2,128)S(1)} fusion(s32[128,128]{1,0:T(8,128)} %bitcast.111, f32[1,128,128]{2,0,1:T(1,128)S(1)} %bitcast.109, f32[1,128,128]{2,0,1:T(1,128)S(1)} %bitcast.110), kind=kOutput, calls=%fused_computation.122 | convolution fusion | flops 52461568 | bytes 327680 | tf_op jit(solution)/shard_map/ltg,tgc->ltc/dot_general | solution.py:124
  27.7 5.3 %copy.24 = f32[6,16384]{0,1:T(8,128)} copy(f32[6,16384]{1,0:T(8,128)S(1)} %get-tuple-element.219) | data formatting | bytes 786432 | tf_op jit(solution)/shard_map/concatenate | solution.py:112
  33.2 31.1 %gather_fusion = f32[8192,6]{1,0:T(8,128)} fusion(f32[6,16384]{0,1:T(8,128)} %copy.24, s32[8192]{0:T(1024)S(1)} %broadcast_clamp_fusion), kind=kCustom, calls=%fused_computation | custom fusion | bytes 425984 | tf_op jit(solution)/shard_map/jit(_take)/gather | solution.py:113
  64.3 6.2 %select_bitcast_fusion = f32[6,8192]{0,1:T(8,128)S(1)} fusion(f32[8192,6]{1,0:T(8,128)} %gather_fusion, pred[8192]{0:T(1024)(128)(4,1)S(1)} %compare_and_fusion), kind=kLoop, calls=%fused_computation.99 | loop fusion | flops 49152 | bytes 401408 | tf_op jit(solution)/shard_map/jit(_take)/select_n | solution.py:113
  75.0 4.7 %collective-permute-start = (f32[6,4096]{1,0:T(8,128)}, f32[6,4096]{1,0:T(8,128)}, u32[]{:S(2)}, u32[]{:S(2)}) collective-permute-start(f32[6,4096]{1,0:T(8,128)} %copy.25), channel_id=1, source_target_pairs={{0,1},{1,2},{2,3},{3,4},{4,5},{5,6},{6,7},{8,9},{9,10},{10,11},{11... | collective-permute-start | bytes 294920 | tf_op jit(solution)/shard_map/ppermute | solution.py:23
  90.5 5.2 %collective-permute-start.5 = (f32[1,128,512]{2,1,0:T(8,128)S(1)}, f32[1,128,512]{2,1,0:T(8,128)S(1)}, u32[]{:S(2)}, u32[]{:S(2)}) collective-permute-start(f32[1,128,512]{2,1,0:T(8,128)S(1)} %get-tuple-element.214), channel_id=1, source_target_pairs={{0,1},{1,2},{2,3},{3,4},{4,5},{5,6},{6,7},{8,9},{9,10},{10,11},{11... | collective-permute-start | bytes 786440 | tf_op jit(solution)/shard_map/ppermute | solution.py:23
  99.1 5.8 %collective-permute-done.5 = f32[1,128,512]{2,1,0:T(8,128)S(1)} collective-permute-done((f32[1,128,512]{2,1,0:T(8,128)S(1)}, f32[1,128,512]{2,1,0:T(8,128)S(1)}, u32[]{:S(2)}, u32[]{:S(2)}) %collective-permute-start.5) | collective-permute-done | bytes 262176 | tf_op jit(solution)/shard_map/ppermute | solution.py:23
  109.8 5.7 %collective-permute-start.7 = (f32[1,128,512]{2,1,0:T(8,128)}, f32[1,128,512]{2,1,0:T(8,128)}, u32[]{:S(2)}, u32[]{:S(2)}) collective-permute-start(f32[1,128,512]{2,1,0:T(8,128)} %get-tuple-element.212), channel_id=1, source_target_pairs={{0,1},{1,2},{2,3},{3,4},{4,5},{5,6},{6,7},{8,9},{9,10},{10,11},{11... | collective-permute-start | bytes 786440 | tf_op jit(solution)/shard_map/ppermute | solution.py:23
  131.0 5.2 %collective-permute-start.9 = (f32[1,128,512]{2,1,0:T(8,128)S(1)}, f32[1,128,512]{2,1,0:T(8,128)S(1)}, u32[]{:S(2)}, u32[]{:S(2)}) collective-permute-start(f32[1,128,512]{2,1,0:T(8,128)S(1)} %get-tuple-element.210), channel_id=1, source_target_pairs={{0,1},{1,2},{2,3},{3,4},{4,5},{5,6},{6,7},{8,9},{9,10},{10,11},{11... | collective-permute-start | bytes 786440 | tf_op jit(solution)/shard_map/ppermute | solution.py:23
  140.6 5.8 %collective-permute-done.9 = f32[1,128,512]{2,1,0:T(8,128)S(1)} collective-permute-done((f32[1,128,512]{2,1,0:T(8,128)S(1)}, f32[1,128,512]{2,1,0:T(8,128)S(1)}, u32[]{:S(2)}, u32[]{:S(2)}) %collective-permute-start.9) | collective-permute-done | bytes 262176 | tf_op jit(solution)/shard_map/ppermute | solution.py:23
  152.3 5.0 %collective-permute-start.11 = (f32[1,128,512]{2,1,0:T(8,128)}, f32[1,128,512]{2,1,0:T(8,128)S(1)}, u32[]{:S(2)}, u32[]{:S(2)}) collective-permute-start(f32[1,128,512]{2,1,0:T(8,128)} %get-tuple-element.208), channel_id=1, source_target_pairs={{0,1},{1,2},{2,3},{3,4},{4,5},{5,6},{6,7},{8,9},{9,10},{10,11},{11... | collective-permute-start | bytes 786440 | tf_op jit(solution)/shard_map/ppermute | solution.py:23
  157.4 119.8 %while.15 = (s32[]{:T(128)}, f32[3,128,128]{2,0,1:T(4,128)S(1)}, s32[8,128,128]{2,1,0:T(8,128)}, f32[8,128,128]{2,1,0:T(8,128)}, f32[6,128,256]{2,0,1:T(8,128)},...) while((s32[]{:T(128)}, f32[3,128,128]{2,0,1:T(4,128)S(1)}, ...), condition=%wide.region_2.3_spmd.clone.clone, body=%wide.region_0.0_spmd.clone.clone.sunk | while | flops 24945676 | bytes 434535 | solution.py:88
  173.9 4.3 %convolution_bitcast_fusion.3 = f32[6,8,128]{2,0,1:T(8,128)S(1)} fusion(f32[8,128]{1,0:T(8,128)S(1)} %get-tuple-element.269, s32[8,128]{1,0:T(8,128)S(1)} %get-tuple-element.270, f32[8,128]{1,0:T(8,128)S(1)} %get-tuple-element.271, s32[8,128]{1,0:T(8,128)S(1)} %get-tuple-element.272, f32[8,128]{1,0:T(8,128)S(1)} %get-tuple-element.273, ...), kind=kOutput, calls=%fused_computation.11.clone.1 | convolution fusion | flops 24903680 | bytes 155652 | tf_op jit(solution)/shard_map/while/body/eval_jaxpr/tij,ctj->cti/dot_general | solution.py:80
  181.4 4.3 %convolution_bitcast_fusion.3 = f32[6,8,128]{2,0,1:T(8,128)S(1)} fusion(f32[8,128]{1,0:T(8,128)S(1)} %get-tuple-element.269, s32[8,128]{1,0:T(8,128)S(1)} %get-tuple-element.270, f32[8,128]{1,0:T(8,128)S(1)} %get-tuple-element.271, s32[8,128]{1,0:T(8,128)S(1)} %get-tuple-element.272, f32[8,128]{1,0:T(8,128)S(1)} %get-tuple-element.273, ...), kind=kOutput, calls=%fused_computation.11.clone.1 | convolution fusion | flops 24903680 | bytes 155652 | tf_op jit(solution)/shard_map/while/body/eval_jaxpr/tij,ctj->cti/dot_general | solution.py:80
  188.9 4.3 %convolution_bitcast_fusion.3 = f32[6,8,128]{2,0,1:T(8,128)S(1)} fusion(f32[8,128]{1,0:T(8,128)S(1)} %get-tuple-element.269, s32[8,128]{1,0:T(8,128)S(1)} %get-tuple-element.270, f32[8,128]{1,0:T(8,128)S(1)} %get-tuple-element.271, s32[8,128]{1,0:T(8,128)S(1)} %get-tuple-element.272, f32[8,128]{1,0:T(8,128)S(1)} %get-tuple-element.273, ...), kind=kOutput, calls=%fused_computation.11.clone.1 | convolution fusion | flops 24903680 | bytes 155652 | tf_op jit(solution)/shard_map/while/body/eval_jaxpr/tij,ctj->cti/dot_general | solution.py:80
  196.4 4.3 %convolution_bitcast_fusion.3 = f32[6,8,128]{2,0,1:T(8,128)S(1)} fusion(f32[8,128]{1,0:T(8,128)S(1)} %get-tuple-element.269, s32[8,128]{1,0:T(8,128)S(1)} %get-tuple-element.270, f32[8,128]{1,0:T(8,128)S(1)} %get-tuple-element.271, s32[8,128]{1,0:T(8,128)S(1)} %get-tuple-element.272, f32[8,128]{1,0:T(8,128)S(1)} %get-tuple-element.273, ...), kind=kOutput, calls=%fused_computation.11.clone.1 | convolution fusion | flops 24903680 | bytes 155652 | tf_op jit(solution)/shard_map/while/body/eval_jaxpr/tij,ctj->cti/dot_general | solution.py:80
  211.3 4.3 %convolution_bitcast_fusion.3 = f32[6,8,128]{2,0,1:T(8,128)S(1)} fusion(f32[8,128]{1,0:T(8,128)S(1)} %get-tuple-element.269, s32[8,128]{1,0:T(8,128)S(1)} %get-tuple-element.270, f32[8,128]{1,0:T(8,128)S(1)} %get-tuple-element.271, s32[8,128]{1,0:T(8,128)S(1)} %get-tuple-element.272, f32[8,128]{1,0:T(8,128)S(1)} %get-tuple-element.273, ...), kind=kOutput, calls=%fused_computation.11.clone.1 | convolution fusion | flops 24903680 | bytes 155652 | tf_op jit(solution)/shard_map/while/body/eval_jaxpr/tij,ctj->cti/dot_general | solution.py:80
  226.3 4.3 %convolution_bitcast_fusion.3 = f32[6,8,128]{2,0,1:T(8,128)S(1)} fusion(f32[8,128]{1,0:T(8,128)S(1)} %get-tuple-element.269, s32[8,128]{1,0:T(8,128)S(1)} %get-tuple-element.270, f32[8,128]{1,0:T(8,128)S(1)} %get-tuple-element.271, s32[8,128]{1,0:T(8,128)S(1)} %get-tuple-element.272, f32[8,128]{1,0:T(8,128)S(1)} %get-tuple-element.273, ...), kind=kOutput, calls=%fused_computation.11.clone.1 | convolution fusion | flops 24903680 | bytes 155652 | tf_op jit(solution)/shard_map/while/body/eval_jaxpr/tij,ctj->cti/dot_general | solution.py:80
  233.8 4.3 %convolution_bitcast_fusion.3 = f32[6,8,128]{2,0,1:T(8,128)S(1)} fusion(f32[8,128]{1,0:T(8,128)S(1)} %get-tuple-element.269, s32[8,128]{1,0:T(8,128)S(1)} %get-tuple-element.270, f32[8,128]{1,0:T(8,128)S(1)} %get-tuple-element.271, s32[8,128]{1,0:T(8,128)S(1)} %get-tuple-element.272, f32[8,128]{1,0:T(8,128)S(1)} %get-tuple-element.273, ...), kind=kOutput, calls=%fused_computation.11.clone.1 | convolution fusion | flops 24903680 | bytes 155652 | tf_op jit(solution)/shard_map/while/body/eval_jaxpr/tij,ctj->cti/dot_general | solution.py:80
  248.7 4.3 %convolution_bitcast_fusion.3 = f32[6,8,128]{2,0,1:T(8,128)S(1)} fusion(f32[8,128]{1,0:T(8,128)S(1)} %get-tuple-element.269, s32[8,128]{1,0:T(8,128)S(1)} %get-tuple-element.270, f32[8,128]{1,0:T(8,128)S(1)} %get-tuple-element.271, s32[8,128]{1,0:T(8,128)S(1)} %get-tuple-element.272, f32[8,128]{1,0:T(8,128)S(1)} %get-tuple-element.273, ...), kind=kOutput, calls=%fused_computation.11.clone.1 | convolution fusion | flops 24903680 | bytes 155652 | tf_op jit(solution)/shard_map/while/body/eval_jaxpr/tij,ctj->cti/dot_general | solution.py:80
  263.7 4.3 %convolution_bitcast_fusion.3 = f32[6,8,128]{2,0,1:T(8,128)S(1)} fusion(f32[8,128]{1,0:T(8,128)S(1)} %get-tuple-element.269, s32[8,128]{1,0:T(8,128)S(1)} %get-tuple-element.270, f32[8,128]{1,0:T(8,128)S(1)} %get-tuple-element.271, s32[8,128]{1,0:T(8,128)S(1)} %get-tuple-element.272, f32[8,128]{1,0:T(8,128)S(1)} %get-tuple-element.273, ...), kind=kOutput, calls=%fused_computation.11.clone.1 | convolution fusion | flops 24903680 | bytes 155652 | tf_op jit(solution)/shard_map/while/body/eval_jaxpr/tij,ctj->cti/dot_general | solution.py:80
  271.2 4.3 %convolution_bitcast_fusion.3 = f32[6,8,128]{2,0,1:T(8,128)S(1)} fusion(f32[8,128]{1,0:T(8,128)S(1)} %get-tuple-element.269, s32[8,128]{1,0:T(8,128)S(1)} %get-tuple-element.270, f32[8,128]{1,0:T(8,128)S(1)} %get-tuple-element.271, s32[8,128]{1,0:T(8,128)S(1)} %get-tuple-element.272, f32[8,128]{1,0:T(8,128)S(1)} %get-tuple-element.273, ...), kind=kOutput, calls=%fused_computation.11.clone.1 | convolution fusion | flops 24903680 | bytes 155652 | tf_op jit(solution)/shard_map/while/body/eval_jaxpr/tij,ctj->cti/dot_general | solution.py:80
  287.8 8.0 %fusion.72 = f32[4,128,128]{2,0,1:T(4,128)S(1)} fusion(s32[128,128]{1,0:T(8,128)S(1)} %bitcast.112, f32[4,128,128]{2,1,0:T(8,128)S(1)} %fusion.73), kind=kOutput, calls=%fused_computation.120 | convolution fusion | flops 102760448 | bytes 589824 | tf_op jit(solution)/shard_map/ltc,tgc->ltg/dot_general | solution.py:141
  (179 shorter events, 144.9 us)
Async XLA Ops:
  6.5 78.5 %all-reduce.8.cloned.1.call-start = ((), (), s32[]{:S(2)}) async-start(), calls=%async_computation | async-start | bytes 4194304 | tf_op jit(solution)/shard_map/psum | solution.py:127
  7.6 74.7 %collective-permute-start.2 = (f32[1,128,512]{2,1,0:T(8,128)S(1)}, f32[1,128,512]{2,1,0:T(8,128)S(1)}, u32[]{:S(2)}, u32[]{:S(2)}) collective-permute-start(f32[1,128,512]{2,1,0:T(8,128)S(1)} %get-tuple-element.217), channel_id=1, source_target_pairs={{1,0},{2,1},{3,2},{4,3},{5,4},{6,5},{7,6},{9,8},{10,9},{11,10},{12... | collective-permute-start | bytes 786440 | tf_op jit(solution)/shard_map/ppermute | solution.py:24
  8.9 74.1 %collective-permute-start.3 = (f32[1,128,512]{2,1,0:T(8,128)S(1)}, f32[1,128,512]{2,1,0:T(8,128)}, u32[]{:S(2)}, u32[]{:S(2)}) collective-permute-start(f32[1,128,512]{2,1,0:T(8,128)S(1)} %get-tuple-element.216), channel_id=1, source_target_pairs={{0,1},{1,2},{2,3},{3,4},{4,5},{5,6},{6,7},{8,9},{9,10},{10,11},{11... | collective-permute-start | bytes 786440 | tf_op jit(solution)/shard_map/ppermute | solution.py:23
  16.7 6.5 %copy-start.18 = (s32[128]{0:T(128)S(1)}, s32[128]{0:T(128)}, u32[]{:S(2)}) copy-start(s32[128]{0:T(128)} %param.26) | copy-start | bytes 1540
  75.0 42.3 %collective-permute-start = (f32[6,4096]{1,0:T(8,128)}, f32[6,4096]{1,0:T(8,128)}, u32[]{:S(2)}, u32[]{:S(2)}) collective-permute-start(f32[6,4096]{1,0:T(8,128)} %copy.25), channel_id=1, source_target_pairs={{0,1},{1,2},{2,3},{3,4},{4,5},{5,6},{6,7},{8,9},{9,10},{10,11},{11... | collective-permute-start | bytes 294920 | tf_op jit(solution)/shard_map/ppermute | solution.py:23
  81.0 36.3 %collective-permute-start.1 = (f32[6,4096]{1,0:T(8,128)}, f32[6,4096]{1,0:T(8,128)}, u32[]{:S(2)}, u32[]{:S(2)}) collective-permute-start(f32[6,4096]{1,0:T(8,128)} %copy.26), channel_id=1, source_target_pairs={{1,0},{2,1},{3,2},{4,3},{5,4},{6,5},{7,6},{9,8},{10,9},{11,10},{12... | collective-permute-start | bytes 294920 | tf_op jit(solution)/shard_map/ppermute | solution.py:24
  85.0 10.6 %copy-start.20 = (s32[128]{0:T(128)S(1)}, s32[128]{0:T(128)}, u32[]{:S(2)}) copy-start(s32[128]{0:T(128)} %param.23) | copy-start | bytes 1540
  89.0 16.5 %copy-start = (f32[4,128,512]{2,1,0:T(8,128)S(1)}, f32[4,128,512]{2,1,0:T(8,128)}, u32[]{:S(2)}) copy-start(f32[4,128,512]{2,1,0:T(8,128)} %get-tuple-element.180) | copy-start | bytes 3145732
  89.0 16.5 %copy-start.1 = (f32[4,128,512]{2,1,0:T(8,128)S(1)}, f32[4,128,512]{2,1,0:T(8,128)}, u32[]{:S(2)}) copy-start(f32[4,128,512]{2,1,0:T(8,128)} %get-tuple-element.181) | copy-start | bytes 3145732
  89.0 10.1 %collective-permute-start.4 = (f32[1,128,512]{2,1,0:T(8,128)S(1)}, f32[1,128,512]{2,1,0:T(8,128)S(1)}, u32[]{:S(2)}, u32[]{:S(2)}) collective-permute-start(f32[1,128,512]{2,1,0:T(8,128)S(1)} %get-tuple-element.215), channel_id=1, source_target_pairs={{1,0},{2,1},{3,2},{4,3},{5,4},{6,5},{7,6},{9,8},{10,9},{11,10},{12... | collective-permute-start | bytes 786440 | tf_op jit(solution)/shard_map/ppermute | solution.py:24
  90.5 14.4 %collective-permute-start.5 = (f32[1,128,512]{2,1,0:T(8,128)S(1)}, f32[1,128,512]{2,1,0:T(8,128)S(1)}, u32[]{:S(2)}, u32[]{:S(2)}) collective-permute-start(f32[1,128,512]{2,1,0:T(8,128)S(1)} %get-tuple-element.214), channel_id=1, source_target_pairs={{0,1},{1,2},{2,3},{3,4},{4,5},{5,6},{6,7},{8,9},{9,10},{10,11},{11... | collective-permute-start | bytes 786440 | tf_op jit(solution)/shard_map/ppermute | solution.py:23
  105.5 10.0 %copy-start.13 = (f32[8,16384]{1,0:T(8,128)S(1)}, f32[8,16384]{1,0:T(8,128)}, u32[]{:S(2)}) copy-start(f32[8,16384]{1,0:T(8,128)} %param.22) | copy-start | bytes 1572868
  107.7 8.7 %copy-start.14 = (s32[8,16384]{1,0:T(8,128)S(1)}, s32[8,16384]{1,0:T(8,128)}, u32[]{:S(2)}) copy-start(s32[8,16384]{1,0:T(8,128)} %param.21) | copy-start | bytes 1572868
  108.5 13.5 %collective-permute-start.6 = (f32[1,128,512]{2,1,0:T(8,128)}, f32[1,128,512]{2,1,0:T(8,128)}, u32[]{:S(2)}, u32[]{:S(2)}) collective-permute-start(f32[1,128,512]{2,1,0:T(8,128)} %get-tuple-element.213), channel_id=1, source_target_pairs={{1,0},{2,1},{3,2},{4,3},{5,4},{6,5},{7,6},{9,8},{10,9},{11,10},{12... | collective-permute-start | bytes 786440 | tf_op jit(solution)/shard_map/ppermute | solution.py:24
  109.8 15.7 %collective-permute-start.7 = (f32[1,128,512]{2,1,0:T(8,128)}, f32[1,128,512]{2,1,0:T(8,128)}, u32[]{:S(2)}, u32[]{:S(2)}) collective-permute-start(f32[1,128,512]{2,1,0:T(8,128)} %get-tuple-element.212), channel_id=1, source_target_pairs={{0,1},{1,2},{2,3},{3,4},{4,5},{5,6},{6,7},{8,9},{9,10},{10,11},{11... | collective-permute-start | bytes 786440 | tf_op jit(solution)/shard_map/ppermute | solution.py:23
  127.4 8.8 %copy-start.9 = (f32[128,6,128]{2,1,0:T(8,128)S(1)}, f32[128,6,128]{2,1,0:T(8,128)}, u32[]{:S(2)}) copy-start(f32[128,6,128]{2,1,0:T(8,128)} %gather_fusion.1) | copy-start | bytes 1179652
  129.6 6.9 %copy-start.8 = (f32[6,128,128]{2,0,1:T(8,128)S(1)}, f32[6,128,128]{2,0,1:T(8,128)}, u32[]{:S(2)}) copy-start(f32[6,128,128]{2,0,1:T(8,128)} %get-tuple-element.218) | copy-start | bytes 1179652
  129.6 11.0 %collective-permute-start.8 = (f32[1,128,512]{2,1,0:T(8,128)S(1)}, f32[1,128,512]{2,1,0:T(8,128)S(1)}, u32[]{:S(2)}, u32[]{:S(2)}) collective-permute-start(f32[1,128,512]{2,1,0:T(8,128)S(1)} %get-tuple-element.211), channel_id=1, source_target_pairs={{1,0},{2,1},{3,2},{4,3},{5,4},{6,5},{7,6},{9,8},{10,9},{11,10},{12... | collective-permute-start | bytes 786440 | tf_op jit(solution)/shard_map/ppermute | solution.py:24
  131.0 15.3 %collective-permute-start.9 = (f32[1,128,512]{2,1,0:T(8,128)S(1)}, f32[1,128,512]{2,1,0:T(8,128)S(1)}, u32[]{:S(2)}, u32[]{:S(2)}) collective-permute-start(f32[1,128,512]{2,1,0:T(8,128)S(1)} %get-tuple-element.210), channel_id=1, source_target_pairs={{0,1},{1,2},{2,3},{3,4},{4,5},{5,6},{6,7},{8,9},{9,10},{10,11},{11... | collective-permute-start | bytes 786440 | tf_op jit(solution)/shard_map/ppermute | solution.py:23
  151.0 127.3 %collective-permute-start.10 = (f32[1,128,512]{2,1,0:T(8,128)}, f32[1,128,512]{2,1,0:T(8,128)S(1)}, u32[]{:S(2)}, u32[]{:S(2)}) collective-permute-start(f32[1,128,512]{2,1,0:T(8,128)} %get-tuple-element.209), channel_id=1, source_target_pairs={{1,0},{2,1},{3,2},{4,3},{5,4},{6,5},{7,6},{9,8},{10,9},{11,10},{12... | collective-permute-start | bytes 786440 | tf_op jit(solution)/shard_map/ppermute | solution.py:24
  152.3 126.0 %collective-permute-start.11 = (f32[1,128,512]{2,1,0:T(8,128)}, f32[1,128,512]{2,1,0:T(8,128)S(1)}, u32[]{:S(2)}, u32[]{:S(2)}) collective-permute-start(f32[1,128,512]{2,1,0:T(8,128)} %get-tuple-element.208), channel_id=1, source_target_pairs={{0,1},{1,2},{2,3},{3,4},{4,5},{5,6},{6,7},{8,9},{9,10},{10,11},{11... | collective-permute-start | bytes 786440 | tf_op jit(solution)/shard_map/ppermute | solution.py:23
  157.4 119.8 %copy-start.6 = (f32[4,128,512]{2,1,0:T(8,128)S(1)}, f32[4,128,512]{2,1,0:T(8,128)}, u32[]{:S(2)}) copy-start(f32[4,128,512]{2,1,0:T(8,128)} %get-tuple-element.203) | copy-start | bytes 3145732
  287.8 8.1 %copy-start.15 = (f32[16384]{0:T(1024)S(1)}, f32[16384]{0:T(1024)}, u32[]{:S(2)}) copy-start(f32[16384]{0:T(1024)} %param.19) | copy-start | bytes 196612
  287.8 8.1 %copy-start.16 = (f32[16384]{0:T(1024)S(1)}, f32[16384]{0:T(1024)}, u32[]{:S(2)}) copy-start(f32[16384]{0:T(1024)} %param.18) | copy-start | bytes 196612
  (10 other events, 22.5 us)
Sparse Core Ops, SparseCore 0:
  26.9 52.4 all-reduce.7
where the time goes:
time: 309 us; the launch traced here: 304 us
  matrix products  88.1 us (29%)
  local copies, waits for them, and re-layouts  83.7 us (27%)
  other arithmetic  55.5 us (18%)
  starting transfers between devices  40.1 us (13%)
  waiting for transfers between devices  21.5 us (7%)
  between operations  14.6 us (5%)
    dot_general x16, matrix products, step_forces(): jnp.einsum('tij,ctj->cti', weights, pair_step, precision=lax.Precision.HI...  69 us
    ppermute x6, starting transfers between devices, with_halo(): before = lax.ppermute(last, axis, up)  32.1 us
    gather x1, local copies, waits for them, and re-layouts, on_device(): outgoing = jnp.take(grain_state, halo_list.reshape(-1), axis=1)  31.1 us
    ppermute x6, waiting for transfers between devices, with_halo(): before = lax.ppermute(last, axis, up)  15 us
    dynamic_update_slice x16, other arithmetic, step_forces(): lax.dynamic_update_slice_in_dim(forces, spring + damper, first_tile, 1)  13.7 us
    reduce_sum x16, other arithmetic, step_forces(): stiff_total = jnp.sum(jnp.where(rows_step >= 0, stiff_step, 0.0), 0)  13.1 us
    broadcast_in_dim x16, local copies, waits for them, and re-layouts, step_forces(): jnp.where(rows_step[slot_index][:, :, None] == columns, stiff_step[slot_i...  12 us
    eq x16, local copies, waits for them, and re-layouts, step_forces(): rows_step[slot_index][:, :, None] == columns  11.7 us
  transfers between devices with their start and end apart: 13, of which 5 were waited for; matrix products, arithmetic and copies ran while one was open for 65% of the time, Pallas kernels for 0%

commit v1 on v0

v1 whole, which is shorter than its diff:
```python
import functools

import jax
import jax.numpy as jnp
from jax import lax
from jax.experimental import pallas as pl
from jax.experimental.pallas import tpu as pltpu
from jax.sharding import PartitionSpec as P

BLOCK = 128
SUB = 8
CORES = 2
SPRING = 1.0
DAMPING = 0.5
TIME_STEP = 0.5

VMEM = pl.BlockSpec(memory_space=pltpu.VMEM)
SMEM = pl.BlockSpec(memory_space=pltpu.SMEM)
F32 = jnp.float32
BF16 = jnp.bfloat16


def iota(shape, dim):
    return lax.broadcasted_iota(jnp.int32, shape, dim)


def shaped(*dims):
    return jax.ShapeDtypeStruct(dims, F32)


def call(kernel, outs, specs, args, scratch=(), flops=0, size=0):
    return pl.pallas_call(
        kernel,
        out_shape=outs,
        in_specs=specs,
        out_specs=jax.tree.map(lambda _: VMEM, outs),
        scratch_shapes=list(scratch),
        compiler_params=pltpu.CompilerParams(vmem_limit_bytes=40 * 1024 * 1024),
        cost_estimate=pl.CostEstimate(flops=flops, bytes_accessed=size, transcendentals=0),
    )(*args)


def lanes_of(source, index):
    return jnp.take_along_axis(source, index, axis=1, mode="promise_in_bounds")


def thirds(value):
    high = value.astype(BF16)
    rest = value - high.astype(F32)
    middle = rest.astype(BF16)
    low = (rest - middle.astype(F32)).astype(BF16)
    return high, middle, low


def deposit_kernel(count, cell, vol, drag, ids, out):
    tiles = cell.shape[0]
    sub = iota((SUB, BLOCK), 0)
    rows_c = iota((BLOCK, BLOCK), 0)
    even = sub % 2 == 0
    low_pair = sub % 4 < 2

    def step(group, carry):
        first = pl.multiple_of(group * SUB, SUB)
        slot = (first + sub) * BLOCK + iota((SUB, BLOCK), 1)
        live = slot < count[0]
        cells = cell[pl.ds(first, SUB), :]
        parts = thirds(jnp.where(live, vol[pl.ds(first, SUB), :], 0.0)) + thirds(
            jnp.where(live, drag[pl.ds(first, SUB), :], 0.0)
        )
        parts = [part.astype(F32) for part in parts]
        left = jnp.concatenate([jnp.where(even, part, 0.0) for part in parts], 0)
        right = jnp.concatenate([jnp.where(even, 0.0, part) for part in parts], 0)
        loads = jnp.concatenate([left, right], 1).astype(BF16)
        sums = [jnp.zeros((SUB, BLOCK), F32), jnp.zeros((SUB, BLOCK), F32)]
        for quad in range(SUB // 4):
            hot = [
                jnp.where(
                    rows_c == jnp.broadcast_to(cells[t : t + 1, :], (BLOCK, BLOCK)), 1.0, 0.0
                ).astype(BF16)
                for t in range(4 * quad, 4 * quad + 4)
            ]
            picked = jnp.concatenate(
                [jnp.concatenate(hot[:2], 1), jnp.concatenate(hot[2:], 1)], 0
            )
            placed = lax.dot_general(
                loads, picked, (((1,), (1,)), ((), ())), preferred_element_type=F32
            )
            for field in range(2):
                base = field * 3 * SUB
                total = placed[base : base + SUB] + placed[base + SUB : base + 2 * SUB]
                total = total + placed[base + 2 * SUB : base + 3 * SUB]
                chosen = jnp.where(low_pair, total[:, :BLOCK], total[:, BLOCK:])
                sums[field] = jnp.where(sub // 4 == quad, chosen, sums[field])
        out[pl.ds(first, SUB), :BLOCK] = sums[0]
        out[pl.ds(first, SUB), BLOCK:] = sums[1]
        return carry

    lax.fori_loop(0, tiles // SUB, step, 0, unroll=2)
    out[tiles : tiles + SUB, :BLOCK] = jnp.broadcast_to(ids[...].astype(F32), (SUB, BLOCK))
    out[tiles : tiles + SUB, BLOCK:] = jnp.zeros((SUB, BLOCK), F32)


def halo_kernel(pos, vel, lists, state, down, up, index):
    tiles = pos.shape[1] // BLOCK
    rows = lists.shape[1] // BLOCK
    for tile in range(tiles):
        lanes = slice(tile * BLOCK, (tile + 1) * BLOCK)
        mixed = SPRING * pos[:, lanes] - DAMPING * vel[:, lanes]
        for axis in range(3):
            state[axis * tiles + tile : axis * tiles + tile + 1, :] = mixed[axis : axis + 1]
    for side in range(2):
        for row in range(rows):
            index[side * rows + row : side * rows + row + 1, :] = lists[
                side : side + 1, row * BLOCK : (row + 1) * BLOCK
            ]
    groups = 2 * rows // SUB
    named = [index[g * SUB : (g + 1) * SUB, :] for g in range(groups)]
    block = [lax.shift_right_logical(value, 7) for value in named]
    lane = [value & (BLOCK - 1) for value in named]

    def step(source, sums):
        new = []
        spread = [
            jnp.broadcast_to(state[pl.ds(axis * tiles + source, 1), :], (SUB, BLOCK))
            for axis in range(3)
        ]
        for g in range(groups):
            here = block[g] == source
            for axis in range(3):
                new.append(
                    jnp.where(here, lanes_of(spread[axis], lane[g]), sums[3 * g + axis])
                )
        return tuple(new)

    zero = jnp.zeros((SUB, BLOCK), F32)
    sums = lax.fori_loop(0, tiles, step, (zero,) * (3 * groups), unroll=2)
    for side, out in enumerate((down, up)):
        for axis in range(3):
            for g in range(groups // 2):
                first = axis * rows + g * SUB
                out[first : first + SUB, :] = sums[3 * (side * groups // 2 + g) + axis]


def contact_kernel(partner, state, lower, upper, named, stiff, out, extended):
    tiles = state.shape[0] // 3
    rows = lower.shape[0] // 3
    blocks = tiles + 2 * rows
    for axis in range(3):
        extended[axis * blocks : axis * blocks + tiles, :] = state[
            axis * tiles : (axis + 1) * tiles, :
        ]
        for place, side in enumerate((lower, upper)):
            first = axis * blocks + tiles + place * rows
            extended[first : first + rows, :] = side[axis * rows : (axis + 1) * rows, :]

    def step(tile, carry):
        lanes = pl.ds(pl.multiple_of(tile * BLOCK, BLOCK), BLOCK)
        entry = named[:, lanes]
        weight = jnp.where(entry >= 0, stiff[:, lanes], 0.0)
        own = entry < BLOCK
        lane = entry & (BLOCK - 1)
        other = partner[tile]
        for axis in range(3):
            mine = jnp.broadcast_to(extended[pl.ds(axis * blocks + tile, 1), :], entry.shape)
            theirs = jnp.broadcast_to(extended[pl.ds(axis * blocks + other, 1), :], entry.shape)
            met = jnp.where(own, lanes_of(mine, lane), lanes_of(theirs, lane))
            pull = jnp.sum(weight * (mine - met), axis=0, keepdims=True)
            out[pl.ds(axis * tiles + tile, 1), :] = pull
        return carry

    lax.fori_loop(0, tiles, step, 0, unroll=4)


def shifted(plane):
    height, width = plane.shape
    row = iota(plane.shape, 0)
    column = iota(plane.shape, 1)
    above = jnp.where(row == 0, 0.0, pltpu.roll(plane, 1, 0))
    below = jnp.where(row == height - 1, 0.0, pltpu.roll(plane, height - 1, 0))
    left = jnp.where(column == 0, 0.0, pltpu.roll(plane, 1, 1))
    right = jnp.where(column == width - 1, 0.0, pltpu.roll(plane, width - 1, 1))
    return above, below, left, right


def sweep(plane_at, constant, factor, new, low, high):
    count = new.shape[0]
    for x in range(count):
        above, below, left, right = shifted(plane_at(x))
        near = plane_at(x - 1) + plane_at(x + 1) + above + below + left + right
        value = constant[x] + factor[x] * near
        new[x] = value
        if x == 0:
            low[...] = value
        if x == count - 1:
            high[...] = value


def first_kernel(
    start, mine, second, third, pressure, source, solid_before, before, after,
    constant, factor, new, low, high, weight,
):
    tiles = mine.shape[0] - SUB
    planes, height, width = new.shape
    full = pressure.shape[1]
    zones = width // BLOCK
    first = pl.multiple_of(start[0], SUB)
    parts = [thirds(group[:tiles, :]) for group in (mine, second, third)]
    loads = [jnp.concatenate([part[i] for part in parts], 0) for i in range(3)]
    ids = jnp.concatenate([group[tiles : tiles + 1, :BLOCK] for group in (mine, second, third)], 1)
    ids = ids.astype(jnp.int32)

    def gathered(wanted):
        hot = jnp.where(wanted == jnp.broadcast_to(ids, wanted.shape), 1.0, 0.0).astype(BF16)
        total = jnp.dot(hot, loads[2], preferred_element_type=F32)
        total = total + jnp.dot(hot, loads[1], preferred_element_type=F32)
        total = total + jnp.dot(hot, loads[0], preferred_element_type=F32)
        return total[:, :BLOCK], total[:, BLOCK:]

    row = iota((height, 3 * tiles), 0) * zones
    for x in range(planes):
        for zone in range(zones):
            lanes = slice(zone * BLOCK, (zone + 1) * BLOCK)
            solid, drag = gathered(row + ((x * full + first) * zones + zone))
            porous = 1.0 / (1.0 + solid)
            inverse = 1.0 / (6.0 * porous + drag + 1.0)
            driving = source[x, pl.ds(first, height), lanes] + solid
            driving = driving - solid_before[x, pl.ds(first, height), lanes]
            constant[x, :, lanes] = driving * inverse
            factor[x, :, lanes] = porous * inverse

    def plane_at(x):
        if x < 0:
            return before[...]
        if x == planes:
            return after[...]
        return pressure[x, pl.ds(first, height), :]

    sweep(plane_at, constant, factor, new, low, high)
    own = jnp.transpose(jnp.broadcast_to(ids[:, :tiles], (tiles, tiles)).astype(F32))
    own = own.astype(jnp.int32)
    solid, drag = gathered(jnp.concatenate([own] * 3, 1))
    weight[...] = 1.0 / (1.0 / (1.0 + solid) + drag)


def sweep_kernel(old, before, after, constant, factor, new, low, high):
    planes = new.shape[0]

    def plane_at(x):
        if x < 0:
            return before[...]
        if x == planes:
            return after[...]
        return old[x]

    sweep(plane_at, constant, factor, new, low, high)


def pick_rows(place, ids, fields, out, height, full, width, own_rows):
    first, owner = place[0], place[1]
    zones = width // BLOCK

    def step(tile, carry):
        block = ids[tile]
        zone = block % zones
        line = block // zones
        x, y = line // full, line % full
        here = y // own_rows == owner
        inside = jnp.where(here, y - first, 0)
        row = fields[pl.ds((x * zones + zone) * height + inside, 1), :]
        out[pl.ds(tile, 1), :] = jnp.where(here, row, 0.0)
        return carry

    lax.fori_loop(0, out.shape[0], step, 0, unroll=8)


def cross_kernel(full, own_rows, place, ids_a, ids_b, ids_c, pressure, out_a, out_b, out_c, fields):
    planes, height, width = pressure.shape
    zones = width // BLOCK
    for x in range(planes):
        above, below, left, right = shifted(pressure[x])
        grad_y = 0.5 * (below - above)
        grad_z = 0.5 * (right - left)
        for zone in range(zones):
            rows = slice((x * zones + zone) * height, (x * zones + zone + 1) * height)
            lanes = slice(zone * BLOCK, (zone + 1) * BLOCK)
            fields[rows, :BLOCK] = grad_y[:, lanes]
            fields[rows, BLOCK:] = grad_z[:, lanes]
    for ids, out in ((ids_a, out_a), (ids_b, out_b), (ids_c, out_c)):
        pick_rows(place, ids, fields, out, height, full, width, own_rows)


def along_kernel(
    full, own_rows, place, ids_a, ids_b, ids_c, pressure, before, after, out_a, out_b, out_c, fields
):
    planes, height, width = pressure.shape
    zones = width // BLOCK
    for x in range(planes):
        behind = before[...] if x == 0 else pressure[x - 1]
        ahead = after[...] if x == planes - 1 else pressure[x + 1]
        grad_x = 0.5 * (ahead - behind)
        for zone in range(zones):
            rows = slice((x * zones + zone) * height, (x * zones + zone + 1) * height)
            fields[rows, :] = grad_x[:, zone * BLOCK : (zone + 1) * BLOCK]
    for ids, out in ((ids_a, out_a), (ids_b, out_b), (ids_c, out_c)):
        pick_rows(place, ids, fields, out, height, full, width, own_rows)


def final_kernel(
    count, along_a, along_b, along_c, cross_a, cross_b, cross_c, weight, contact, vel, vol, drag,
    cell, out,
):
    tiles = cell.shape[0]
    cells = cell[...]
    cross = cross_a[...] + cross_b[...] + cross_c[...]
    fields = [along_a[...] + along_b[...] + along_c[...], cross[:, :BLOCK], cross[:, BLOCK:]]
    heft = lanes_of(weight[...], cells)
    slot = iota(cells.shape, 0) * BLOCK + iota(cells.shape, 1)
    live = slot < count[0]
    volume = vol[...]
    push = TIME_STEP / volume
    for axis in range(3):
        gradient = lanes_of(fields[axis], cells)
        own = jnp.concatenate(
            [vel[axis : axis + 1, t * BLOCK : (t + 1) * BLOCK] for t in range(tiles)], 0
        )
        fluid = -gradient * heft
        force = contact[axis * tiles : (axis + 1) * tiles, :] - volume * gradient
        force = force + drag[...] * (fluid - own)
        new = jnp.where(live, own + force * push, 0.0)
        for t in range(tiles):
            out[axis : axis + 1, t * BLOCK : (t + 1) * BLOCK] = new[t : t + 1, :]


def on_device(
    grain_pos,
    grain_vel,
    grain_vol,
    drag_coef,
    grain_count,
    contact_rows,
    contact_stiff,
    partner_block,
    halo_list,
    grain_cell,
    tile_cell_block,
    pressure_old,
    pressure_source,
    solid_old,
):
    groups, regions = lax.axis_size("grp"), lax.axis_size("reg")
    holding = groups - 1
    halves = groups // CORES
    slots = grain_pos.shape[1]
    tiles = slots // BLOCK
    planes, full, width = pressure_old.shape
    own_rows = full // halves
    height = min(full, own_rows + SUB * min(2, halves - 1))
    group = lax.axis_index("grp")
    half = group // CORES
    first = jnp.clip(half * own_rows - SUB, 0, full - height).astype(jnp.int32)
    start = first.reshape(1)
    owner = jnp.where(group % CORES == 0, half, -1).astype(jnp.int32)
    place = jnp.stack([first, owner])

    def send(value, pairs):
        return lax.ppermute(value, ("grp", "reg"), [(a[0] * regions + a[1], b[0] * regions + b[1]) for a, b in pairs])

    def along_reg(value, step, members):
        pairs = [
            ((g, r), (g, r + step)) for g in members for r in range(regions) if 0 <= r + step < regions
        ]
        return send(value, pairs)

    def along_grp(value, step, members):
        pairs = [((g, r), ((g + step) % holding, r)) for g in members for r in range(regions)]
        return send(value, pairs)

    owners = range(0, groups, CORES)
    holders = range(holding)

    count = grain_count
    cell = grain_cell.reshape(tiles, BLOCK)
    vol = grain_vol.reshape(tiles, BLOCK)
    drag = drag_coef.reshape(tiles, BLOCK)
    ids = tile_cell_block.reshape(1, tiles)
    field_bytes = 4 * planes * height * width

    mine = call(
        deposit_kernel, shaped(tiles + SUB, 2 * BLOCK), [SMEM] + [VMEM] * 4,
        (count, cell, vol, drag, ids), flops=2 * 32 * 48 * 65536, size=5 * 4 * slots,
    )
    second = along_grp(mine, 1, holders)
    third = along_grp(mine, 2, holders)
    ids_b = second[tiles, :BLOCK].astype(jnp.int32)
    ids_c = third[tiles, :BLOCK].astype(jnp.int32)

    def edge(x):
        return lax.dynamic_slice(pressure_old, (x, first, 0), (1, height, width))[0]

    before = along_reg(edge(planes - 1), 1, owners)
    after = along_reg(edge(0), -1, owners)

    rows = halo_list.shape[1] // BLOCK
    state, down, up = call(
        halo_kernel, (shaped(3 * tiles, BLOCK), shaped(3 * rows, BLOCK), shaped(3 * rows, BLOCK)),
        [VMEM] * 3, (grain_pos, grain_vel, halo_list),
        [pltpu.VMEM((2 * rows, BLOCK), jnp.int32)], flops=8 * 3 * 16384 * 128, size=4 * 4 * 3 * slots,
    )
    lower = along_reg(up, 1, holders)
    upper = along_reg(down, -1, holders)

    field = shaped(planes, height, width)
    plane = shaped(height, width)
    constant, factor, pressure, low, high, weight = call(
        first_kernel, (field, field, field, plane, plane, shaped(tiles, BLOCK)),
        [SMEM] + [VMEM] * 8,
        (start, mine, second, third, pressure_old, pressure_source, solid_old, before, after),
        flops=planes * height * 4 * 384 * 256 * 6, size=9 * field_bytes,
    )
    for _ in range(3):
        before = along_reg(high, 1, owners)
        after = along_reg(low, -1, owners)
        pressure, low, high = call(
            sweep_kernel, (field, plane, plane), [VMEM] * 5,
            (pressure, before, after, constant, factor),
            flops=8 * field_bytes // 4, size=5 * field_bytes,
        )
    before = along_reg(high, 1, owners)
    after = along_reg(low, -1, owners)

    contact = call(
        contact_kernel, shaped(3 * tiles, BLOCK), [SMEM] + [VMEM] * 5,
        (partner_block, state, lower, upper, contact_rows, contact_stiff),
        [pltpu.VMEM((3 * (tiles + 2 * rows), BLOCK), F32)],
        flops=60 * 8 * slots, size=4 * 20 * slots,
    )
    pair = shaped(tiles, 2 * BLOCK)
    cross_a, cross_b, cross_c = call(
        functools.partial(cross_kernel, full, own_rows), (pair, pair, pair), [SMEM] * 4 + [VMEM],
        (place, tile_cell_block, ids_b, ids_c, pressure),
        [pltpu.VMEM((planes * height * width // BLOCK, 2 * BLOCK), F32)],
        flops=4 * field_bytes, size=3 * field_bytes,
    )
    cross_b = along_grp(cross_b, -1, owners)
    cross_c = along_grp(cross_c, -2, owners)
    single = shaped(tiles, BLOCK)
    along_a, along_b, along_c = call(
        functools.partial(along_kernel, full, own_rows), (single,) * 3, [SMEM] * 4 + [VMEM] * 3,
        (place, tile_cell_block, ids_b, ids_c, pressure, before, after),
        [pltpu.VMEM((planes * height * width // BLOCK, BLOCK), F32)],
        flops=field_bytes, size=2 * field_bytes,
    )
    along_b = along_grp(along_b, -1, owners)
    along_c = along_grp(along_c, -2, owners)
    return call(
        final_kernel, shaped(3, slots), [SMEM] + [VMEM] * 12,
        (
            count, along_a, along_b, along_c, cross_a, cross_b, cross_c, weight, contact, grain_vel,
            vol, drag, cell,
        ),
        flops=60 * slots, size=4 * 20 * slots,
    )


def solution(mesh):
    in_specs = (
        P(None, ("grp", "reg")),
        P(None, ("grp", "reg")),
        P(("grp", "reg")),
        P(("grp", "reg")),
        P(("grp", "reg")),
        P(None, ("grp", "reg")),
        P(None, ("grp", "reg")),
        P(("grp", "reg")),
        P(None, ("grp", "reg")),
        P(("grp", "reg")),
        P(("grp", "reg")),
        P("reg", None, None),
        P("reg", None, None),
        P("reg", None, None),
    )
    out_specs = P(None, ("grp", "reg"))
    return jax.shard_map(
        on_device, mesh=mesh, in_specs=in_specs, out_specs=out_specs, check_vma=False
    )
```

time: 309 us -> 124 us (0.40); the launches traced: 304 us -> 124 us
  matrix products: 88.1 us -> 0 us
  local copies, waits for them, and re-layouts: 83.7 us -> 7.43 us
  other arithmetic: 55.5 us -> 0.09 us
  Pallas kernels: 0 us -> 37.8 us
  between operations: 14.6 us -> 1.09 us
  starting transfers between devices: 40.1 us -> 52.4 us
  waiting for transfers between devices: 21.5 us -> 24.8 us
    dot_general x20 -> x0, matrix products: 88.1 us -> none  [the longest x16 69 us: step_forces(): jnp.einsum('tij,ctj->cti', weights, pair_step, precision=lax.Precision.HI...]
    pallas_call x0 -> x10, Pallas kernels: none -> 37.8 us  [call(): pl.pallas_call(kernel, out_shape=outs, in_specs=specs, out_specs=jax.tree...]
    gather x2 -> x0, local copies, waits for them, and re-layouts: 33.7 us -> none  [the longest x1 31.1 us: on_device(): outgoing = jnp.take(grain_state, halo_list.reshape(-1), axis=1)]
    dynamic_update_slice x16 -> x0, other arithmetic: 13.7 us -> none  [step_forces(): lax.dynamic_update_slice_in_dim(forces, spring + damper, first_tile, 1)]
    reduce_sum x16 -> x0, other arithmetic: 13.1 us -> none  [step_forces(): stiff_total = jnp.sum(jnp.where(rows_step >= 0, stiff_step, 0.0), 0)]
    ppermute x12 -> x18, starting transfers between devices: 40.1 us -> 52.4 us  [send(): lax.ppermute(value, ('grp', 'reg'), [(a[0] * regions + a[1], b[0] * regio...]
    broadcast_in_dim x17 -> x0, local copies, waits for them, and re-layouts: 12 us -> none  [the longest x16 12 us: step_forces(): jnp.where(rows_step[slot_index][:, :, None] == columns, stiff_step[slot_i...]
    eq x16 -> x0, local copies, waits for them, and re-layouts: 11.7 us -> none  [step_forces(): rows_step[slot_index][:, :, None] == columns]
  transfers between devices with their start and end apart: 13 -> 18, of which waited for: 5 -> 9; matrix products, arithmetic and copies ran while one was open for 65% -> 0% of each run, Pallas kernels for 0% -> 27%
where the time goes in v1:
time: 124 us
  starting transfers between devices  52.4 us (42%)
  Pallas kernels  37.8 us (30%)
  waiting for transfers between devices  24.8 us (20%)
  local copies, waits for them, and re-layouts  7.43 us (6%)
    ppermute x18, starting transfers between devices, send(): lax.ppermute(value, ('grp', 'reg'), [(a[0] * regions + a[1], b[0] * regio...  52.4 us
    pallas_call x10, Pallas kernels, call(): pl.pallas_call(kernel, out_shape=outs, in_specs=specs, out_specs=jax.tree...  37.8 us
    ppermute x18, waiting for transfers between devices, send(): lax.ppermute(value, ('grp', 'reg'), [(a[0] * regions + a[1], b[0] * regio...  24.8 us
    unnamed x34, local copies, waits for them, and re-layouts  6.31 us
  transfers between devices with their start and end apart: 18, of which 9 were waited for; matrix products, arithmetic and copies ran while one was open for 0% of the time, Pallas kernels for 27%

profile of v1, /device:TPU:0, one launch (start us, length us, event | category | flops | bytes accessed | tf_op | source)
XLA Modules:
  0.0 123.6 jit_solution(14769702249768749789)
XLA Ops:
  1.1 4.9 %collective-permute-start.2 = (f32[72,512]{1,0:T(8,128)S(1)}, f32[72,512]{1,0:T(8,128)S(1)}, u32[]{:S(2)}, u32[]{:S(2)}) collective-permute-start(f32[72,512]{1,0:T(8,128)S(1)} %get-tuple-element.54), channel_id=1, source_target_pairs={{0,1},{1,2},{2,3},{3,4},{4,5},{5,6},{6,7},{16,17},{17,18},{18,19},... | collective-permute-start | bytes 442376 | tf_op jit(solution)/shard_map/ppermute | solution.py:366
  11.1 2.2 %shard_map.136.mine = f32[136,256]{1,0:T(8,128)S(1)} custom-call(s32[1]{0:T(128)S(6)} %copy.15.count, s32[128,128]{1,0:T(8,128)S(1)} %bitcast.14, f32[128,128]{1,0:T(8,128)S(1)} %bitcast.16, f32[128,128]{1,0:T(8,128)S(1)} %bitcast.18, s32[1,128]{1,0:T(1,128)S(1)} %bitcast.20), custom_call_target="tpu_custom_call" | custom-call | flops 201326592 | bytes 327680 | tf_op jit(solution)/shard_map/pallas_call | solution.py:32
  13.3 1.9 %collective-permute-start = (f32[136,256]{1,0:T(8,128)S(1)}, f32[136,256]{1,0:T(8,128)S(1)}, u32[]{:S(2)}, u32[]{:S(2)}) collective-permute-start(f32[136,256]{1,0:T(8,128)S(1)} %shard_map.136.mine), channel_id=1, source_target_pairs={{0,8},{1,9},{2,10},{3,11},{4,12},{5,13},{6,14},{7,15},{8,16},{9,17... | collective-permute-start | bytes 417800 | tf_op jit(solution)/shard_map/ppermute | solution.py:366
  15.3 3.9 %collective-permute-start.1 = (f32[136,256]{1,0:T(8,128)S(1)}, f32[136,256]{1,0:T(8,128)S(1)}, u32[]{:S(2)}, u32[]{:S(2)}) collective-permute-start(f32[136,256]{1,0:T(8,128)S(1)} %shard_map.136.mine), channel_id=1, source_target_pairs={{0,16},{1,17},{2,18},{3,19},{4,20},{5,21},{6,22},{7,23},{8,0},{9,1... | collective-permute-start | bytes 417800 | tf_op jit(solution)/shard_map/ppermute | solution.py:366
  20.3 1.5 %collective-permute-done.1.third = f32[136,256]{1,0:T(8,128)S(1)} collective-permute-done((f32[136,256]{1,0:T(8,128)S(1)}, f32[136,256]{1,0:T(8,128)S(1)}, u32[]{:S(2)}, u32[]{:S(2)}) %collective-permute-start.1) | collective-permute-done | bytes 139296 | tf_op jit(solution)/shard_map/ppermute | solution.py:366
  24.2 1.8 %shard_map.137 = (f32[4,72,512]{2,1,0:T(8,128)S(1)}, f32[4,72,512]{2,1,0:T(8,128)S(1)}, f32[4,72,512]{2,1,0:T(8,128)S(1)}, f32[72,512]{1,0:T(8,128)S(1)}, f32[72,512]{1,0:T(8,128)S(1)}, /*index=5*/f32[128,128]{1,0:T(8,128)S(1)}) custom-call(s32[1]{0:T(128)} %bitcast.start, f32[136,256]{1,0:T(8,128)S(1)} %shard_map.136.mine, ...), custom_call_target="tpu_custom_call" | custom-call | flops 679477248 | bytes 5308416 | tf_op jit(solution)/shard_map/pallas_call | solution.py:32
  26.1 4.6 %collective-permute-start.4 = (f32[72,512]{1,0:T(8,128)S(1)}, f32[72,512]{1,0:T(8,128)S(1)}, u32[]{:S(2)}, u32[]{:S(2)}) collective-permute-start(f32[72,512]{1,0:T(8,128)S(1)} %get-tuple-element.30), channel_id=1, source_target_pairs={{0,1},{1,2},{2,3},{3,4},{4,5},{5,6},{6,7},{16,17},{17,18},{18,19},... | collective-permute-start | bytes 442376 | tf_op jit(solution)/shard_map/ppermute | solution.py:366
  31.9 1.3 %collective-permute-done.4.before = f32[72,512]{1,0:T(8,128)S(1)} collective-permute-done((f32[72,512]{1,0:T(8,128)S(1)}, f32[72,512]{1,0:T(8,128)S(1)}, u32[]{:S(2)}, u32[]{:S(2)}) %collective-permute-start.4) | collective-permute-done | bytes 147488 | tf_op jit(solution)/shard_map/ppermute | solution.py:366
  33.3 4.8 %collective-permute-done.5.after = f32[72,512]{1,0:T(8,128)S(1)} collective-permute-done((f32[72,512]{1,0:T(8,128)S(1)}, f32[72,512]{1,0:T(8,128)S(1)}, u32[]{:S(2)}, u32[]{:S(2)}) %collective-permute-start.5) | collective-permute-done | bytes 147488 | tf_op jit(solution)/shard_map/ppermute | solution.py:366
  38.5 4.8 %collective-permute-start.6 = (f32[72,512]{1,0:T(8,128)S(1)}, f32[72,512]{1,0:T(8,128)S(1)}, u32[]{:S(2)}, u32[]{:S(2)}) collective-permute-start(f32[72,512]{1,0:T(8,128)S(1)} %get-tuple-element.35), channel_id=1, source_target_pairs={{0,1},{1,2},{2,3},{3,4},{4,5},{5,6},{6,7},{16,17},{17,18},{18,19},... | collective-permute-start | bytes 442376 | tf_op jit(solution)/shard_map/ppermute | solution.py:366
  46.0 4.4 %collective-permute-done.7.after = f32[72,512]{1,0:T(8,128)S(1)} collective-permute-done((f32[72,512]{1,0:T(8,128)S(1)}, f32[72,512]{1,0:T(8,128)S(1)}, u32[]{:S(2)}, u32[]{:S(2)}) %collective-permute-start.7) | collective-permute-done | bytes 147488 | tf_op jit(solution)/shard_map/ppermute | solution.py:366
  50.9 2.9 %collective-permute-start.8 = (f32[72,512]{1,0:T(8,128)S(1)}, f32[72,512]{1,0:T(8,128)S(1)}, u32[]{:S(2)}, u32[]{:S(2)}) collective-permute-start(f32[72,512]{1,0:T(8,128)S(1)} %get-tuple-element.38), channel_id=1, source_target_pairs={{0,1},{1,2},{2,3},{3,4},{4,5},{5,6},{6,7},{16,17},{17,18},{18,19},... | collective-permute-start | bytes 442376 | tf_op jit(solution)/shard_map/ppermute | solution.py:366
  56.4 4.4 %collective-permute-done.9.after = f32[72,512]{1,0:T(8,128)S(1)} collective-permute-done((f32[72,512]{1,0:T(8,128)S(1)}, f32[72,512]{1,0:T(8,128)S(1)}, u32[]{:S(2)}, u32[]{:S(2)}) %collective-permute-start.9) | collective-permute-done | bytes 147488 | tf_op jit(solution)/shard_map/ppermute | solution.py:366
  61.3 4.8 %collective-permute-start.10 = (f32[72,512]{1,0:T(8,128)S(1)}, f32[72,512]{1,0:T(8,128)S(1)}, u32[]{:S(2)}, u32[]{:S(2)}) collective-permute-start(f32[72,512]{1,0:T(8,128)S(1)} %get-tuple-element.41), channel_id=1, source_target_pairs={{0,1},{1,2},{2,3},{3,4},{4,5},{5,6},{6,7},{16,17},{17,18},{18,19},... | collective-permute-start | bytes 442376 | tf_op jit(solution)/shard_map/ppermute | solution.py:366
  68.1 8.8 %shard_map.142 = (f32[128,256]{1,0:T(8,128)S(1)}, f32[128,256]{1,0:T(8,128)S(1)}, f32[128,256]{1,0:T(8,128)S(1)}) custom-call(s32[2]{0:T(128)S(1)} %pad_add_fusion.place, s32[128]{0:T(128)S(1)} %copy-done.15, s32[128]{0:T(128)S(1)} %fusion.1.ids_b, s32[128]{0:T(128)S(1)} %fusion.ids_c, f32[4,72,512]{2,1,0:T(8,128)S(1)} %get-tuple-element.40.pressure), custom_call_target="tpu_custom_call" | custom-call | flops 2359296 | bytes 1769472 | tf_op jit(solution)/shard_map/pallas_call | solution.py:32
  76.9 4.4 %collective-permute-start.14 = (f32[128,256]{1,0:T(8,128)S(1)}, f32[128,256]{1,0:T(8,128)S(1)}, u32[]{:S(2)}, u32[]{:S(2)}) collective-permute-start(f32[128,256]{1,0:T(8,128)S(1)} %get-tuple-element.47), channel_id=1, source_target_pairs={{0,16},{1,17},{2,18},{3,19},{4,20},{5,21},{6,22},{7,23},{16,8},{17... | collective-permute-start | bytes 393224 | tf_op jit(solution)/shard_map/ppermute | solution.py:366
  81.2 1.9 %collective-permute-start.15 = (f32[128,256]{1,0:T(8,128)S(1)}, f32[128,256]{1,0:T(8,128)S(1)}, u32[]{:S(2)}, u32[]{:S(2)}) collective-permute-start(f32[128,256]{1,0:T(8,128)S(1)} %get-tuple-element.48), channel_id=1, source_target_pairs={{0,8},{1,9},{2,10},{3,11},{4,12},{5,13},{6,14},{7,15},{16,0},{17,1... | collective-permute-start | bytes 393224 | tf_op jit(solution)/shard_map/ppermute | solution.py:366
  83.2 10.9 %shard_map.143 = (f32[384,128]{1,0:T(8,128)S(1)}, f32[96,128]{1,0:T(8,128)S(1)}, f32[96,128]{1,0:T(8,128)S(1)}) custom-call(f32[3,16384]{1,0:T(4,128)S(1)} %copy-done.6, f32[3,16384]{1,0:T(4,128)S(1)} %copy-done.1, s32[2,4096]{1,0:T(2,128)S(1)} %copy-done.13), custom_call_target="tpu_custom_call" | custom-call | flops 50331648 | bytes 786432 | tf_op jit(solution)/shard_map/pallas_call | solution.py:32
  94.1 4.7 %collective-permute-start.16 = (f32[96,128]{1,0:T(8,128)S(1)}, f32[96,128]{1,0:T(8,128)S(1)}, u32[]{:S(2)}, u32[]{:S(2)}) collective-permute-start(f32[96,128]{1,0:T(8,128)S(1)} %get-tuple-element.51), channel_id=1, source_target_pairs={{0,1},{1,2},{2,3},{3,4},{4,5},{5,6},{6,7},{8,9},{9,10},{10,11},{11... | collective-permute-start | bytes 147464 | tf_op jit(solution)/shard_map/ppermute | solution.py:366
  98.8 7.6 %shard_map.141 = (f32[128,128]{1,0:T(8,128)S(1)}, f32[128,128]{1,0:T(8,128)S(1)}, f32[128,128]{1,0:T(8,128)S(1)}) custom-call(s32[2]{0:T(128)S(1)} %pad_add_fusion.place, s32[128]{0:T(128)S(1)} %copy-done.15, s32[128]{0:T(128)S(1)} %fusion.1.ids_b, s32[128]{0:T(128)S(1)} %fusion.ids_c, f32[4,72,512]{2,1,0:T(8,128)S(1)} %get-tuple-element.40.pressure, ...), custom_call_target="tpu_custom_call" | custom-call | flops 589824 | bytes 1179648 | tf_op jit(solution)/shard_map/pallas_call | solution.py:32
  106.4 3.9 %collective-permute-start.12 = (f32[128,128]{1,0:T(8,128)S(1)}, f32[128,128]{1,0:T(8,128)S(1)}, u32[]{:S(2)}, u32[]{:S(2)}) collective-permute-start(f32[128,128]{1,0:T(8,128)S(1)} %get-tuple-element.44), channel_id=1, source_target_pairs={{0,16},{1,17},{2,18},{3,19},{4,20},{5,21},{6,22},{7,23},{16,8},{17... | collective-permute-start | bytes 196616 | tf_op jit(solution)/shard_map/ppermute | solution.py:366
  110.3 1.9 %collective-permute-start.13 = (f32[128,128]{1,0:T(8,128)S(1)}, f32[128,128]{1,0:T(8,128)S(1)}, u32[]{:S(2)}, u32[]{:S(2)}) collective-permute-start(f32[128,128]{1,0:T(8,128)S(1)} %get-tuple-element.45), channel_id=1, source_target_pairs={{0,8},{1,9},{2,10},{3,11},{4,12},{5,13},{6,14},{7,15},{16,0},{17,1... | collective-permute-start | bytes 196616 | tf_op jit(solution)/shard_map/ppermute | solution.py:366
  113.6 4.7 %collective-permute-done.17.upper = f32[96,128]{1,0:T(8,128)S(1)} collective-permute-done((f32[96,128]{1,0:T(8,128)S(1)}, f32[96,128]{1,0:T(8,128)S(1)}, u32[]{:S(2)}, u32[]{:S(2)}) %collective-permute-start.17) | collective-permute-done | bytes 49184 | tf_op jit(solution)/shard_map/ppermute | solution.py:366
  118.3 4.2 %shard_map.144.contact = f32[384,128]{1,0:T(8,128)S(1)} custom-call(s32[128]{0:T(128)S(1)} %copy-done.16, f32[384,128]{1,0:T(8,128)S(1)} %get-tuple-element.50.state, f32[96,128]{1,0:T(8,128)S(1)} %collective-permute-done.16.lower, f32[96,128]{1,0:T(8,128)S(1)} %collective-permute-done.17.upper, s32[8,16384]{1,0:T(8,128)S(1)} %copy-done.4, ...), custom_call_target="tpu_custom_call" | custom-call | flops 7864320 | bytes 1310720 | tf_op jit(solution)/shard_map/pallas_call | solution.py:32
  (60 shorter events, 21.4 us)
Async XLA Ops:
  0.0 21.8 %copy-start = (f32[4,128,512]{2,1,0:T(8,128)S(1)}, f32[4,128,512]{2,1,0:T(8,128)}, u32[]{:S(2)}) copy-start(f32[4,128,512]{2,1,0:T(8,128)} %pressure.1) | copy-start | bytes 3145732
  1.1 20.7 %collective-permute-start.2 = (f32[72,512]{1,0:T(8,128)S(1)}, f32[72,512]{1,0:T(8,128)S(1)}, u32[]{:S(2)}, u32[]{:S(2)}) collective-permute-start(f32[72,512]{1,0:T(8,128)S(1)} %get-tuple-element.54), channel_id=1, source_target_pairs={{0,1},{1,2},{2,3},{3,4},{4,5},{5,6},{6,7},{16,17},{17,18},{18,19},... | collective-permute-start | bytes 442376 | tf_op jit(solution)/shard_map/ppermute | solution.py:366
  6.0 15.8 %collective-permute-start.3 = (f32[72,512]{1,0:T(8,128)S(1)}, f32[72,512]{1,0:T(8,128)S(1)}, u32[]{:S(2)}, u32[]{:S(2)}) collective-permute-start(f32[72,512]{1,0:T(8,128)S(1)} %get-tuple-element.53), channel_id=1, source_target_pairs={{1,0},{2,1},{3,2},{4,3},{5,4},{6,5},{7,6},{17,16},{18,17},{19,18},... | collective-permute-start | bytes 442376 | tf_op jit(solution)/shard_map/ppermute | solution.py:366
  13.3 6.9 %collective-permute-start = (f32[136,256]{1,0:T(8,128)S(1)}, f32[136,256]{1,0:T(8,128)S(1)}, u32[]{:S(2)}, u32[]{:S(2)}) collective-permute-start(f32[136,256]{1,0:T(8,128)S(1)} %shard_map.136.mine), channel_id=1, source_target_pairs={{0,8},{1,9},{2,10},{3,11},{4,12},{5,13},{6,14},{7,15},{8,16},{9,17... | collective-permute-start | bytes 417800 | tf_op jit(solution)/shard_map/ppermute | solution.py:366
  15.3 6.5 %collective-permute-start.1 = (f32[136,256]{1,0:T(8,128)S(1)}, f32[136,256]{1,0:T(8,128)S(1)}, u32[]{:S(2)}, u32[]{:S(2)}) collective-permute-start(f32[136,256]{1,0:T(8,128)S(1)} %shard_map.136.mine), channel_id=1, source_target_pairs={{0,16},{1,17},{2,18},{3,19},{4,20},{5,21},{6,22},{7,23},{8,0},{9,1... | collective-permute-start | bytes 417800 | tf_op jit(solution)/shard_map/ppermute | solution.py:366
  26.1 7.2 %collective-permute-start.4 = (f32[72,512]{1,0:T(8,128)S(1)}, f32[72,512]{1,0:T(8,128)S(1)}, u32[]{:S(2)}, u32[]{:S(2)}) collective-permute-start(f32[72,512]{1,0:T(8,128)S(1)} %get-tuple-element.30), channel_id=1, source_target_pairs={{0,1},{1,2},{2,3},{3,4},{4,5},{5,6},{6,7},{16,17},{17,18},{18,19},... | collective-permute-start | bytes 442376 | tf_op jit(solution)/shard_map/ppermute | solution.py:366
  30.6 7.4 %collective-permute-start.5 = (f32[72,512]{1,0:T(8,128)S(1)}, f32[72,512]{1,0:T(8,128)S(1)}, u32[]{:S(2)}, u32[]{:S(2)}) collective-permute-start(f32[72,512]{1,0:T(8,128)S(1)} %get-tuple-element.31), channel_id=1, source_target_pairs={{1,0},{2,1},{3,2},{4,3},{5,4},{6,5},{7,6},{17,16},{18,17},{19,18},... | collective-permute-start | bytes 442376 | tf_op jit(solution)/shard_map/ppermute | solution.py:366
  38.5 7.5 %collective-permute-start.6 = (f32[72,512]{1,0:T(8,128)S(1)}, f32[72,512]{1,0:T(8,128)S(1)}, u32[]{:S(2)}, u32[]{:S(2)}) collective-permute-start(f32[72,512]{1,0:T(8,128)S(1)} %get-tuple-element.35), channel_id=1, source_target_pairs={{0,1},{1,2},{2,3},{3,4},{4,5},{5,6},{6,7},{16,17},{17,18},{18,19},... | collective-permute-start | bytes 442376 | tf_op jit(solution)/shard_map/ppermute | solution.py:366
  43.4 7.0 %collective-permute-start.7 = (f32[72,512]{1,0:T(8,128)S(1)}, f32[72,512]{1,0:T(8,128)S(1)}, u32[]{:S(2)}, u32[]{:S(2)}) collective-permute-start(f32[72,512]{1,0:T(8,128)S(1)} %get-tuple-element.36), channel_id=1, source_target_pairs={{1,0},{2,1},{3,2},{4,3},{5,4},{6,5},{7,6},{17,16},{18,17},{19,18},... | collective-permute-start | bytes 442376 | tf_op jit(solution)/shard_map/ppermute | solution.py:366
  50.9 5.6 %collective-permute-start.8 = (f32[72,512]{1,0:T(8,128)S(1)}, f32[72,512]{1,0:T(8,128)S(1)}, u32[]{:S(2)}, u32[]{:S(2)}) collective-permute-start(f32[72,512]{1,0:T(8,128)S(1)} %get-tuple-element.38), channel_id=1, source_target_pairs={{0,1},{1,2},{2,3},{3,4},{4,5},{5,6},{6,7},{16,17},{17,18},{18,19},... | collective-permute-start | bytes 442376 | tf_op jit(solution)/shard_map/ppermute | solution.py:366
  53.8 7.0 %collective-permute-start.9 = (f32[72,512]{1,0:T(8,128)S(1)}, f32[72,512]{1,0:T(8,128)S(1)}, u32[]{:S(2)}, u32[]{:S(2)}) collective-permute-start(f32[72,512]{1,0:T(8,128)S(1)} %get-tuple-element.39), channel_id=1, source_target_pairs={{1,0},{2,1},{3,2},{4,3},{5,4},{6,5},{7,6},{17,16},{18,17},{19,18},... | collective-permute-start | bytes 442376 | tf_op jit(solution)/shard_map/ppermute | solution.py:366
  61.3 37.5 %collective-permute-start.10 = (f32[72,512]{1,0:T(8,128)S(1)}, f32[72,512]{1,0:T(8,128)S(1)}, u32[]{:S(2)}, u32[]{:S(2)}) collective-permute-start(f32[72,512]{1,0:T(8,128)S(1)} %get-tuple-element.41), channel_id=1, source_target_pairs={{0,1},{1,2},{2,3},{3,4},{4,5},{5,6},{6,7},{16,17},{17,18},{18,19},... | collective-permute-start | bytes 442376 | tf_op jit(solution)/shard_map/ppermute | solution.py:366
  66.1 32.7 %collective-permute-start.11 = (f32[72,512]{1,0:T(8,128)S(1)}, f32[72,512]{1,0:T(8,128)S(1)}, u32[]{:S(2)}, u32[]{:S(2)}) collective-permute-start(f32[72,512]{1,0:T(8,128)S(1)} %get-tuple-element.42), channel_id=1, source_target_pairs={{1,0},{2,1},{3,2},{4,3},{5,4},{6,5},{7,6},{17,16},{18,17},{19,18},... | collective-permute-start | bytes 442376 | tf_op jit(solution)/shard_map/ppermute | solution.py:366
  68.1 15.1 %copy-start.1 = (f32[3,16384]{1,0:T(4,128)S(1)}, f32[3,16384]{1,0:T(4,128)}, u32[]{:S(2)}) copy-start(f32[3,16384]{1,0:T(4,128)} %vel.3) | copy-start | bytes 589828
  68.1 15.1 %copy-start.6 = (f32[3,16384]{1,0:T(4,128)S(1)}, f32[3,16384]{1,0:T(4,128)}, u32[]{:S(2)}) copy-start(f32[3,16384]{1,0:T(4,128)} %pos.1) | copy-start | bytes 589828
  68.1 15.1 %copy-start.13 = (s32[2,4096]{1,0:T(2,128)S(1)}, s32[2,4096]{1,0:T(2,128)}, u32[]{:S(2)}) copy-start(s32[2,4096]{1,0:T(2,128)} %lists.1) | copy-start | bytes 98308
  76.9 45.7 %collective-permute-start.14 = (f32[128,256]{1,0:T(8,128)S(1)}, f32[128,256]{1,0:T(8,128)S(1)}, u32[]{:S(2)}, u32[]{:S(2)}) collective-permute-start(f32[128,256]{1,0:T(8,128)S(1)} %get-tuple-element.47), channel_id=1, source_target_pairs={{0,16},{1,17},{2,18},{3,19},{4,20},{5,21},{6,22},{7,23},{16,8},{17... | collective-permute-start | bytes 393224 | tf_op jit(solution)/shard_map/ppermute | solution.py:366
  81.2 41.3 %collective-permute-start.15 = (f32[128,256]{1,0:T(8,128)S(1)}, f32[128,256]{1,0:T(8,128)S(1)}, u32[]{:S(2)}, u32[]{:S(2)}) collective-permute-start(f32[128,256]{1,0:T(8,128)S(1)} %get-tuple-element.48), channel_id=1, source_target_pairs={{0,8},{1,9},{2,10},{3,11},{4,12},{5,13},{6,14},{7,15},{16,0},{17,1... | collective-permute-start | bytes 393224 | tf_op jit(solution)/shard_map/ppermute | solution.py:366
  83.2 35.1 %copy-start.5 = (f32[8,16384]{1,0:T(8,128)S(1)}, f32[8,16384]{1,0:T(8,128)}, u32[]{:S(2)}) copy-start(f32[8,16384]{1,0:T(8,128)} %stiff.1) | copy-start | bytes 1572868
  94.1 24.2 %copy-start.4 = (s32[8,16384]{1,0:T(8,128)S(1)}, s32[8,16384]{1,0:T(8,128)}, u32[]{:S(2)}) copy-start(s32[8,16384]{1,0:T(8,128)} %named.1) | copy-start | bytes 1572868
  94.1 18.2 %collective-permute-start.16 = (f32[96,128]{1,0:T(8,128)S(1)}, f32[96,128]{1,0:T(8,128)S(1)}, u32[]{:S(2)}, u32[]{:S(2)}) collective-permute-start(f32[96,128]{1,0:T(8,128)S(1)} %get-tuple-element.51), channel_id=1, source_target_pairs={{0,1},{1,2},{2,3},{3,4},{4,5},{5,6},{6,7},{8,9},{9,10},{10,11},{11... | collective-permute-start | bytes 147464 | tf_op jit(solution)/shard_map/ppermute | solution.py:366
  106.4 16.1 %collective-permute-start.12 = (f32[128,128]{1,0:T(8,128)S(1)}, f32[128,128]{1,0:T(8,128)S(1)}, u32[]{:S(2)}, u32[]{:S(2)}) collective-permute-start(f32[128,128]{1,0:T(8,128)S(1)} %get-tuple-element.44), channel_id=1, source_target_pairs={{0,16},{1,17},{2,18},{3,19},{4,20},{5,21},{6,22},{7,23},{16,8},{17... | collective-permute-start | bytes 196616 | tf_op jit(solution)/shard_map/ppermute | solution.py:366
  110.3 12.2 %collective-permute-start.13 = (f32[128,128]{1,0:T(8,128)S(1)}, f32[128,128]{1,0:T(8,128)S(1)}, u32[]{:S(2)}, u32[]{:S(2)}) collective-permute-start(f32[128,128]{1,0:T(8,128)S(1)} %get-tuple-element.45), channel_id=1, source_target_pairs={{0,8},{1,9},{2,10},{3,11},{4,12},{5,13},{6,14},{7,15},{16,0},{17,1... | collective-permute-start | bytes 196616 | tf_op jit(solution)/shard_map/ppermute | solution.py:366
  112.3 6.0 %collective-permute-start.17 = (f32[96,128]{1,0:T(8,128)S(1)}, f32[96,128]{1,0:T(8,128)S(1)}, u32[]{:S(2)}, u32[]{:S(2)}) collective-permute-start(f32[96,128]{1,0:T(8,128)S(1)} %get-tuple-element.52), channel_id=1, source_target_pairs={{1,0},{2,1},{3,2},{4,3},{5,4},{6,5},{7,6},{9,8},{10,9},{11,10},{12... | collective-permute-start | bytes 147464 | tf_op jit(solution)/shard_map/ppermute | solution.py:366
  (11 other events, 25.1 us)

commit v2 on v1

--- a/solution.py
+++ b/solution.py
@@ -10,6 +10,7 @@
 BLOCK = 128
 SUB = 8
 CORES = 2
+ITERS = 4
 SPRING = 1.0
 DAMPING = 0.5
 TIME_STEP = 0.5
@@ -182,31 +183,10 @@
     return above, below, left, right
 
 
-def sweep(plane_at, constant, factor, new, low, high):
-    count = new.shape[0]
-    for x in range(count):
-        above, below, left, right = shifted(plane_at(x))
-        near = plane_at(x - 1) + plane_at(x + 1) + above + below + left + right
-        value = constant[x] + factor[x] * near
-        new[x] = value
-        if x == 0:
-            low[...] = value
-        if x == count - 1:
-            high[...] = value
-
-
-def first_kernel(
-    start, mine, second, third, pressure, source, solid_before, before, after,
-    constant, factor, new, low, high, weight,
-):
-    tiles = mine.shape[0] - SUB
-    planes, height, width = new.shape
-    full = pressure.shape[1]
-    zones = width // BLOCK
-    first = pl.multiple_of(start[0], SUB)
-    parts = [thirds(group[:tiles, :]) for group in (mine, second, third)]
+def placed(groups, tiles):
+    parts = [thirds(group[:tiles, :]) for group in groups]
     loads = [jnp.concatenate([part[i] for part in parts], 0) for i in range(3)]
-    ids = jnp.concatenate([group[tiles : tiles + 1, :BLOCK] for group in (mine, second, third)], 1)
+    ids = jnp.concatenate([group[tiles : tiles + 1, :BLOCK] for group in groups], 1)
     ids = ids.astype(jnp.int32)
 
     def gathered(wanted):
@@ -216,110 +196,138 @@
         total = total + jnp.dot(hot, loads[0], preferred_element_type=F32)
         return total[:, :BLOCK], total[:, BLOCK:]
 
-    row = iota((height, 3 * tiles), 0) * zones
-    for x in range(planes):
+    return ids, gathered
+
+
+def coefficients(gathered, tiles, first, full, driven, constant, factor, base, present):
+    planes, height, width = driven.shape
+    zones = width // BLOCK
+    shape = (zones * height, 3 * tiles)
+    line = iota(shape, 0)
+    block = (line % height) * zones + line // height + first * zones
+
+    def plane(x, carry):
+        solid, drag = gathered(block + x * (full * zones))
+        porous = 1.0 / (1.0 + solid)
+        inverse = 1.0 / (6.0 * porous + drag + 1.0)
+        if present is not None:
+            inverse = jnp.where(present, inverse, 0.0)
+        scale = porous * inverse
         for zone in range(zones):
             lanes = slice(zone * BLOCK, (zone + 1) * BLOCK)
-            solid, drag = gathered(row + ((x * full + first) * zones + zone))
-            porous = 1.0 / (1.0 + solid)
-            inverse = 1.0 / (6.0 * porous + drag + 1.0)
-            driving = source[x, pl.ds(first, height), lanes] + solid
-            driving = driving - solid_before[x, pl.ds(first, height), lanes]
-            constant[x, :, lanes] = driving * inverse
-            factor[x, :, lanes] = porous * inverse
-
-    def plane_at(x):
-        if x < 0:
-            return before[...]
-        if x == planes:
-            return after[...]
-        return pressure[x, pl.ds(first, height), :]
-
-    sweep(plane_at, constant, factor, new, low, high)
+            rows = slice(zone * height, (zone + 1) * height)
+            driving = driven[x, :, lanes] + solid[rows]
+            constant[base + x, :, lanes] = driving * inverse[rows]
+            factor[base + x, :, lanes] = scale[rows]
+        return carry
+
+    lax.fori_loop(0, planes, plane, 0)
+
+
+def own_kernel(full, place, mine, second, third, driven, constant, factor, weight, joined):
+    stride = mine.shape[0]
+    tiles = stride - SUB
+    groups = (mine, second, third)
+    for index, group in enumerate(groups):
+        joined[index * stride : (index + 1) * stride, :] = group[...]
+    ids, gathered = placed(groups, tiles)
+    coefficients(gathered, tiles, place[0], full, driven, constant, factor, 0, None)
     own = jnp.transpose(jnp.broadcast_to(ids[:, :tiles], (tiles, tiles)).astype(F32))
-    own = own.astype(jnp.int32)
-    solid, drag = gathered(jnp.concatenate([own] * 3, 1))
+    solid, drag = gathered(jnp.concatenate([own.astype(jnp.int32)] * 3, 1))
     weight[...] = 1.0 / (1.0 / (1.0 + solid) + drag)
 
 
-def sweep_kernel(old, before, after, constant, factor, new, low, high):
-    planes = new.shape[0]
-
-    def plane_at(x):
-        if x < 0:
-            return before[...]
-        if x == planes:
-            return after[...]
-        return old[x]
-
-    sweep(plane_at, constant, factor, new, low, high)
-
-
-def pick_rows(place, ids, fields, out, height, full, width, own_rows):
-    first, owner = place[0], place[1]
-    zones = width // BLOCK
-
-    def step(tile, carry):
-        block = ids[tile]
-        zone = block % zones
-        line = block // zones
-        x, y = line // full, line % full
-        here = y // own_rows == owner
-        inside = jnp.where(here, y - first, 0)
-        row = fields[pl.ds((x * zones + zone) * height + inside, 1), :]
-        out[pl.ds(tile, 1), :] = jnp.where(here, row, 0.0)
-        return carry
-
-    lax.fori_loop(0, out.shape[0], step, 0, unroll=8)
-
-
-def cross_kernel(full, own_rows, place, ids_a, ids_b, ids_c, pressure, out_a, out_b, out_c, fields):
-    planes, height, width = pressure.shape
-    zones = width // BLOCK
-    for x in range(planes):
-        above, below, left, right = shifted(pressure[x])
-        grad_y = 0.5 * (below - above)
-        grad_z = 0.5 * (right - left)
-        for zone in range(zones):
-            rows = slice((x * zones + zone) * height, (x * zones + zone + 1) * height)
-            lanes = slice(zone * BLOCK, (zone + 1) * BLOCK)
-            fields[rows, :BLOCK] = grad_y[:, lanes]
-            fields[rows, BLOCK:] = grad_z[:, lanes]
-    for ids, out in ((ids_a, out_a), (ids_b, out_b), (ids_c, out_c)):
-        pick_rows(place, ids, fields, out, height, full, width, own_rows)
-
-
-def along_kernel(
-    full, own_rows, place, ids_a, ids_b, ids_c, pressure, before, after, out_a, out_b, out_c, fields
+def solve_kernel(
+    full, sweeps, place, rows_at, joined_lower, joined_upper, driven_near, driven_far, pressure,
+    near, far, beyond, own_constant, own_factor, out_a, out_b, out_c,
+    driven, constant, factor, old, new, fields,
 ):
     planes, height, width = pressure.shape
     zones = width // BLOCK
-    for x in range(planes):
-        behind = before[...] if x == 0 else pressure[x - 1]
-        ahead = after[...] if x == planes - 1 else pressure[x + 1]
-        grad_x = 0.5 * (ahead - behind)
+    stride = joined_lower.shape[0] // 3
+    tiles = stride - SUB
+    odd, lower, upper = place[1] == 1, place[2] == 1, place[3] == 1
+    rim = sweeps + 1
+
+    @pl.when(odd)
+    def _():
+        driven[:planes] = driven_near[...]
+        driven[planes:] = driven_far[...]
+        old[0] = beyond[...]
+        old[1 : 1 + planes] = near[...]
+        old[rim + planes : rim + 2 * planes + 1] = far[...]
+
+    @pl.when(jnp.logical_not(odd))
+    def _():
+        driven[:planes] = driven_far[...]
+        driven[planes:] = driven_near[...]
+        old[: 1 + planes] = far[...]
+        old[rim + planes : rim + 2 * planes] = near[...]
+        old[rim + 2 * planes] = beyond[...]
+
+    old[rim : rim + planes] = pressure[...]
+    constant[planes : 2 * planes] = own_constant[...]
+    factor[planes : 2 * planes] = own_factor[...]
+    for index, (joined, present) in enumerate(((joined_lower, lower), (joined_upper, upper))):
+        groups = [joined.at[i * stride : (i + 1) * stride] for i in range(3)]
+        _, gathered = placed(groups, tiles)
+        coefficients(
+            gathered, tiles, place[0], full, driven.at[index * planes : (index + 1) * planes],
+            constant, factor, 2 * index * planes, present,
+        )
+
+    def sweep(source, target, depth):
+        def plane(x, carry):
+            centre = source[x]
+            above, below, left, right = shifted(centre)
+            around = source[x - 1] + source[x + 1] + above + below + left + right
+            target[x] = constant[x - 1] + factor[x - 1] * around
+            return carry
+
+        lax.fori_loop(depth, 3 * planes + 2 - depth, plane, 0)
+
+    for index in range(sweeps):
+        source, target = (old, new) if index % 2 == 0 else (new, old)
+        sweep(source, target, index + 1)
+    last = old if sweeps % 2 == 0 else new
+
+    def gradient(x, carry):
+        centre = last[rim + x]
+        above, below, left, right = shifted(centre)
+        grads = (last[rim + x + 1] - last[rim + x - 1], below - above, right - left)
         for zone in range(zones):
-            rows = slice((x * zones + zone) * height, (x * zones + zone + 1) * height)
-            fields[rows, :] = grad_x[:, zone * BLOCK : (zone + 1) * BLOCK]
-    for ids, out in ((ids_a, out_a), (ids_b, out_b), (ids_c, out_c)):
-        pick_rows(place, ids, fields, out, height, full, width, own_rows)
+            first = pl.multiple_of((x * zones + zone) * height, SUB)
+            for axis, grad in enumerate(grads):
+                fields[pl.ds(first, height), axis * BLOCK : (axis + 1) * BLOCK] = (
+                    0.5 * grad[:, zone * BLOCK : (zone + 1) * BLOCK]
+                )
+        return carry
+
+    lax.fori_loop(0, planes, gradient, 0)
+    none = planes * zones * height
+    fields[none : none + SUB, :] = jnp.zeros((SUB, 3 * BLOCK), F32)
+
+    def pick(tile, carry):
+        for index, out in enumerate((out_a, out_b, out_c)):
+            out[pl.ds(tile, 1), :] = fields[pl.ds(rows_at[index * tiles + tile], 1), :]
+        return carry
+
+    lax.fori_loop(0, tiles, pick, 0, unroll=8)
 
 
 def final_kernel(
-    count, along_a, along_b, along_c, cross_a, cross_b, cross_c, weight, contact, vel, vol, drag,
-    cell, out,
+    count, grads_a, grads_b, grads_c, weight, contact, vel, vol, drag, cell, out,
 ):
     tiles = cell.shape[0]
     cells = cell[...]
-    cross = cross_a[...] + cross_b[...] + cross_c[...]
-    fields = [along_a[...] + along_b[...] + along_c[...], cross[:, :BLOCK], cross[:, BLOCK:]]
     heft = lanes_of(weight[...], cells)
     slot = iota(cells.shape, 0) * BLOCK + iota(cells.shape, 1)
     live = slot < count[0]
     volume = vol[...]
     push = TIME_STEP / volume
     for axis in range(3):
-        gradient = lanes_of(fields[axis], cells)
+        lanes = slice(axis * BLOCK, (axis + 1) * BLOCK)
+        gradient = lanes_of(grads_a[:, lanes] + grads_b[:, lanes] + grads_c[:, lanes], cells)
         own = jnp.concatenate(
             [vel[axis : axis + 1, t * BLOCK : (t + 1) * BLOCK] for t in range(tiles)], 0
         )
@@ -353,30 +361,33 @@
     slots = grain_pos.shape[1]
     tiles = slots // BLOCK
     planes, full, width = pressure_old.shape
+    zones = width // BLOCK
     own_rows = full // halves
     height = min(full, own_rows + SUB * min(2, halves - 1))
-    group = lax.axis_index("grp")
+    group, region = lax.axis_index("grp"), lax.axis_index("reg")
     half = group // CORES
-    first = jnp.clip(half * own_rows - SUB, 0, full - height).astype(jnp.int32)
-    start = first.reshape(1)
-    owner = jnp.where(group % CORES == 0, half, -1).astype(jnp.int32)
-    place = jnp.stack([first, owner])
+    first = jnp.clip(half * own_rows - SUB, 0, full - height)
+    odd = region % 2 == 1
+    place = jnp.stack([first, odd, region > 0, region < regions - 1]).astype(jnp.int32)
+    owners = range(0, groups, CORES)
+    holders = range(holding)
 
     def send(value, pairs):
-        return lax.ppermute(value, ("grp", "reg"), [(a[0] * regions + a[1], b[0] * regions + b[1]) for a, b in pairs])
-
-    def along_reg(value, step, members):
+        flat = [(a[0] * regions + a[1], b[0] * regions + b[1]) for a, b in pairs]
+        return lax.ppermute(value, ("grp", "reg"), flat)
+
+    def along_reg(value, members, goes):
         pairs = [
-            ((g, r), (g, r + step)) for g in members for r in range(regions) if 0 <= r + step < regions
+            ((g, r), (g, r + goes[r % 2]))
+            for g in members
+            for r in range(regions)
+            if 0 <= r + goes[r % 2] < regions
         ]
         return send(value, pairs)
 
     def along_grp(value, step, members):
         pairs = [((g, r), ((g + step) % holding, r)) for g in members for r in range(regions)]
         return send(value, pairs)
-
-    owners = range(0, groups, CORES)
-    holders = range(holding)
 
     count = grain_count
     cell = grain_cell.reshape(tiles, BLOCK)
@@ -391,14 +402,34 @@
     )
     second = along_grp(mine, 1, holders)
     third = along_grp(mine, 2, holders)
-    ids_b = second[tiles, :BLOCK].astype(jnp.int32)
-    ids_c = third[tiles, :BLOCK].astype(jnp.int32)
-
-    def edge(x):
-        return lax.dynamic_slice(pressure_old, (x, first, 0), (1, height, width))[0]
-
-    before = along_reg(edge(planes - 1), 1, owners)
-    after = along_reg(edge(0), -1, owners)
+
+    def window(whole):
+        return lax.dynamic_slice(whole, (0, first, 0), (planes, height, width))
+
+    driven = window(pressure_source) - window(solid_old)
+    pressure = window(pressure_old)
+    driven_near = along_reg(driven, owners, (1, -1))
+    near = along_reg(pressure, owners, (1, -1))
+    ends = jnp.where(odd, pressure[planes - 1], pressure[0])
+    beyond = along_reg(ends, owners, (-2, 2))
+    driven_far = along_reg(driven_near, owners, (2, -2))
+    inner = jnp.where(odd, pressure[:1], pressure[planes - 1 :])
+    far = along_reg(
+        jnp.where(
+            odd, jnp.concatenate([near, inner], 0), jnp.concatenate([inner, near], 0)
+        ),
+        owners, (2, -2),
+    )
+
+    field = shaped(planes, height, width)
+    constant, factor, weight, joined = call(
+        functools.partial(own_kernel, full),
+        (field, field, shaped(tiles, BLOCK), shaped(3 * (tiles + SUB), 2 * BLOCK)),
+        [SMEM] + [VMEM] * 4, (place, mine, second, third, driven),
+        flops=planes * height * 4 * 384 * 256 * 6, size=9 * field_bytes,
+    )
+    joined_lower = along_reg(joined, owners, (1, 1))
+    joined_upper = along_reg(joined, owners, (-1, -1))
 
     rows = halo_list.shape[1] // BLOCK
     state, down, up = call(
@@ -406,27 +437,34 @@
         [VMEM] * 3, (grain_pos, grain_vel, halo_list),
         [pltpu.VMEM((2 * rows, BLOCK), jnp.int32)], flops=8 * 3 * 16384 * 128, size=4 * 4 * 3 * slots,
     )
-    lower = along_reg(up, 1, holders)
-    upper = along_reg(down, -1, holders)
-
-    field = shaped(planes, height, width)
-    plane = shaped(height, width)
-    constant, factor, pressure, low, high, weight = call(
-        first_kernel, (field, field, field, plane, plane, shaped(tiles, BLOCK)),
-        [SMEM] + [VMEM] * 8,
-        (start, mine, second, third, pressure_old, pressure_source, solid_old, before, after),
-        flops=planes * height * 4 * 384 * 256 * 6, size=9 * field_bytes,
-    )
-    for _ in range(3):
-        before = along_reg(high, 1, owners)
-        after = along_reg(low, -1, owners)
-        pressure, low, high = call(
-            sweep_kernel, (field, plane, plane), [VMEM] * 5,
-            (pressure, before, after, constant, factor),
-            flops=8 * field_bytes // 4, size=5 * field_bytes,
-        )
-    before = along_reg(high, 1, owners)
-    after = along_reg(low, -1, owners)
+    lower = along_reg(up, holders, (1, 1))
+    upper = along_reg(down, holders, (-1, -1))
+
+    blocks = jnp.concatenate(
+        [tile_cell_block, second[tiles, :BLOCK].astype(jnp.int32), third[tiles, :BLOCK].astype(jnp.int32)]
+    )
+    line, zone = blocks // zones, blocks % zones
+    x, y = line // full, line % full
+    held = (y // own_rows == half) & (group % CORES == 0)
+    rows_at = jnp.where(held, (x * zones + zone) * height + y - first, planes * zones * height)
+
+    grads = shaped(tiles, 3 * BLOCK)
+    window_of = lambda count: pltpu.VMEM((count, height, width), F32)
+    grads_a, grads_b, grads_c = call(
+        functools.partial(solve_kernel, full, ITERS), (grads,) * 3, [SMEM] * 2 + [VMEM] * 10,
+        (
+            place, rows_at, joined_lower, joined_upper, driven_near, driven_far, pressure, near, far,
+            beyond, constant, factor,
+        ),
+        [
+            window_of(2 * planes), window_of(3 * planes), window_of(3 * planes),
+            window_of(3 * planes + 2), window_of(3 * planes + 2),
+            pltpu.VMEM((planes * zones * height + SUB, 3 * BLOCK), F32),
+        ],
+        flops=2 * planes * height * 4 * 384 * 256 * 6, size=20 * field_bytes,
+    )
+    grads_b = along_grp(grads_b, -1, owners)
+    grads_c = along_grp(grads_c, -2, owners)
 
     contact = call(
         contact_kernel, shaped(3 * tiles, BLOCK), [SMEM] + [VMEM] * 5,
@@ -434,30 +472,9 @@
         [pltpu.VMEM((3 * (tiles + 2 * rows), BLOCK), F32)],
         flops=60 * 8 * slots, size=4 * 20 * slots,
     )
-    pair = shaped(tiles, 2 * BLOCK)
-    cross_a, cross_b, cross_c = call(
-        functools.partial(cross_kernel, full, own_rows), (pair, pair, pair), [SMEM] * 4 + [VMEM],
-        (place, tile_cell_block, ids_b, ids_c, pressure),
-        [pltpu.VMEM((planes * height * width // BLOCK, 2 * BLOCK), F32)],
-        flops=4 * field_bytes, size=3 * field_bytes,
-    )
-    cross_b = along_grp(cross_b, -1, owners)
-    cross_c = along_grp(cross_c, -2, owners)
-    single = shaped(tiles, BLOCK)
-    along_a, along_b, along_c = call(
-        functools.partial(along_kernel, full, own_rows), (single,) * 3, [SMEM] * 4 + [VMEM] * 3,
-        (place, tile_cell_block, ids_b, ids_c, pressure, before, after),
-        [pltpu.VMEM((planes * height * width // BLOCK, BLOCK), F32)],
-        flops=field_bytes, size=2 * field_bytes,
-    )
-    along_b = along_grp(along_b, -1, owners)
-    along_c = along_grp(along_c, -2, owners)
     return call(
-        final_kernel, shaped(3, slots), [SMEM] + [VMEM] * 12,
-        (
-            count, along_a, along_b, along_c, cross_a, cross_b, cross_c, weight, contact, grain_vel,
-            vol, drag, cell,
-        ),
+        final_kernel, shaped(3, slots), [SMEM] + [VMEM] * 9,
+        (count, grads_a, grads_b, grads_c, weight, contact, grain_vel, vol, drag, cell),
         flops=60 * slots, size=4 * 20 * slots,
     )
 

time: 124 us -> 93.9 us (0.76)
  starting transfers between devices: 52.4 us -> 37.3 us
  waiting for transfers between devices: 24.8 us -> 14.1 us
  local copies, waits for them, and re-layouts: 7.43 us -> 1.93 us
  other arithmetic: 0.09 us -> 5.38 us
  Pallas kernels: 37.8 us -> 33.6 us
    ppermute x18 -> x13, starting transfers between devices: 52.4 us -> 37.3 us  [send(): return lax.ppermute(value, ('grp', 'reg'), flat)]
    ppermute x18 -> x13, waiting for transfers between devices: 24.8 us -> 14.1 us  [send(): return lax.ppermute(value, ('grp', 'reg'), flat)]
    unnamed x34 -> x22, local copies, waits for them, and re-layouts: 6.31 us -> 0.68 us
    pallas_call x10 -> x6, Pallas kernels: 37.8 us -> 33.6 us  [call(): pl.pallas_call(kernel, out_shape=outs, in_specs=specs, out_specs=jax.tree...]
    select_n x0 -> x3, other arithmetic: none -> 2.69 us  [the longest x1 1.7 us: on_device(): ends = jnp.where(odd, pressure[planes - 1], pressure[0])]
    convert_element_type x2, other arithmetic: 0.01 us -> 1.36 us  [the longest x1 0.68 us: on_device(): third[tiles, :BLOCK].astype(jnp.int32)]
    dynamic_slice x0 -> x1, local copies, waits for them, and re-layouts: none -> 1.25 us  [window(): return lax.dynamic_slice(whole, (0, first, 0), (planes, height, width))]
    sub x0 -> x1, other arithmetic: none -> 1.25 us  [on_device(): driven = window(pressure_source) - window(solid_old)]
  transfers between devices with their start and end apart: 18 -> 13, of which waited for: 9 -> 4; matrix products, arithmetic and copies ran while one was open for 0% -> 6% of each run, Pallas kernels for 27% -> 23%
where the time goes in v2:
time: 93.9 us; the launch traced here: 93.3 us
  starting transfers between devices  37.3 us (40%)
  Pallas kernels  33.6 us (36%)
  waiting for transfers between devices  14.1 us (15%)
  other arithmetic  5.38 us (6%)
  local copies, waits for them, and re-layouts  1.93 us (2%)
  between operations  1.03 us (1%)
    ppermute x13, starting transfers between devices, send(): return lax.ppermute(value, ('grp', 'reg'), flat)  37.3 us
    pallas_call x6, Pallas kernels, call(): pl.pallas_call(kernel, out_shape=outs, in_specs=specs, out_specs=jax.tree...  33.6 us
    ppermute x13, waiting for transfers between devices, send(): return lax.ppermute(value, ('grp', 'reg'), flat)  14.1 us
  transfers between devices with their start and end apart: 13, of which 4 were waited for; matrix products, arithmetic and copies ran while one was open for 6% of the time, Pallas kernels for 23%

profile of v2, /device:TPU:0, one launch (start us, length us, event | category | flops | bytes accessed | tf_op | source)
XLA Modules:
  0.0 93.3 jit_solution(10139644088877310859)
XLA Ops:
  0.0 1.3 %constant_dynamic-slice_fusion.pressure = f32[4,72,512]{2,1,0:T(8,128)S(1)} fusion(f32[4,128,512]{2,1,0:T(8,128)} %param.25, s32[]{:T(128)} %min.4), kind=kLoop, calls=%fused_computation.33 | loop fusion | bytes 1179652 | tf_op jit(solution)/shard_map/dynamic_slice | solution.py:407
  1.3 5.0 %collective-permute-start.6 = (f32[4,72,512]{2,1,0:T(8,128)S(1)}, f32[4,72,512]{2,1,0:T(8,128)S(1)}, u32[]{:S(2)}, u32[]{:S(2)}) collective-permute-start(f32[4,72,512]{2,1,0:T(8,128)S(1)} %constant_dynamic-slice_fusion.pressure), channel_id=1, source_target_pairs={{0,1},{1,0},{2,3},{3,2},{4,5},{5,4},{6,7},{7,6},{16,17},{17,16},{1... | collective-permute-start | bytes 1769480 | tf_op jit(solution)/shard_map/ppermute | solution.py:377
  6.3 1.2 %dynamic-slice_subtract_fusion.driven = f32[4,72,512]{2,1,0:T(8,128)S(1)} fusion(f32[4,128,512]{2,1,0:T(8,128)S(1)} %copy-done.10, s32[]{:T(128)} %min.4, f32[4,128,512]{2,1,0:T(8,128)} %param.26), kind=kLoop, calls=%fused_computation.1 | loop fusion | flops 147456 | bytes 1769476 | tf_op jit(solution)/shard_map/sub | solution.py:409
  7.6 1.9 %collective-permute-start.4 = (f32[4,72,512]{2,1,0:T(8,128)S(1)}, f32[4,72,512]{2,1,0:T(8,128)S(1)}, u32[]{:S(2)}, u32[]{:S(2)}) collective-permute-start(f32[4,72,512]{2,1,0:T(8,128)S(1)} %dynamic-slice_subtract_fusion.driven), channel_id=1, source_target_pairs={{0,1},{1,0},{2,3},{3,2},{4,5},{5,4},{6,7},{7,6},{16,17},{17,16},{1... | collective-permute-start | bytes 1769480 | tf_op jit(solution)/shard_map/ppermute | solution.py:377
  10.8 2.9 %shard_map.136.mine = f32[136,256]{1,0:T(8,128)} custom-call(s32[1]{0:T(128)S(6)} %copy.15.count, s32[128,128]{1,0:T(8,128)S(1)} %bitcast.14, f32[128,128]{1,0:T(8,128)S(1)} %bitcast.16, f32[128,128]{1,0:T(8,128)S(1)} %bitcast.18, s32[1,128]{1,0:T(1,128)S(1)} %bitcast.20), custom_call_target="tpu_custom_call" | custom-call | flops 201326592 | bytes 327680 | tf_op jit(solution)/shard_map/pallas_call | solution.py:33
  13.7 1.9 %collective-permute-start = (f32[136,256]{1,0:T(8,128)}, f32[136,256]{1,0:T(8,128)}, u32[]{:S(2)}, u32[]{:S(2)}) collective-permute-start(f32[136,256]{1,0:T(8,128)} %shard_map.136.mine), channel_id=1, source_target_pairs={{0,8},{1,9},{2,10},{3,11},{4,12},{5,13},{6,14},{7,15},{8,16},{9,17... | collective-permute-start | bytes 417800 | tf_op jit(solution)/shard_map/ppermute | solution.py:377
  15.6 3.9 %collective-permute-start.1 = (f32[136,256]{1,0:T(8,128)}, f32[136,256]{1,0:T(8,128)}, u32[]{:S(2)}, u32[]{:S(2)}) collective-permute-start(f32[136,256]{1,0:T(8,128)} %shard_map.136.mine), channel_id=1, source_target_pairs={{0,16},{1,17},{2,18},{3,19},{4,20},{5,21},{6,22},{7,23},{8,0},{9,1... | collective-permute-start | bytes 417800 | tf_op jit(solution)/shard_map/ppermute | solution.py:377
  19.5 1.7 %select_bitcast_fusion = (f32[72,512]{1,0:T(8,128)}, f32[1,72,512]{2,1,0:T(8,128)S(1)}) fusion(f32[4,128,512]{2,1,0:T(8,128)} %param.25, s32[]{:T(128)} %min.4, s32[]{:T(128)S(6)} %add.42, pred[]{:T(512)S(6)} %eq.18), kind=kLoop, calls=%fused_computation.2 | loop fusion | flops 73728 | bytes 589833 | tf_op jit(solution)/shard_map/jit(_where)/select_n | solution.py:413
  21.2 1.3 %collective-permute-start.8 = (f32[72,512]{1,0:T(8,128)}, f32[72,512]{1,0:T(8,128)S(1)}, u32[]{:S(2)}, u32[]{:S(2)}) collective-permute-start(f32[72,512]{1,0:T(8,128)} %get-tuple-element.25), channel_id=1, source_target_pairs={{1,3},{2,0},{3,5},{4,2},{5,7},{6,4},{17,19},{18,16},{19,21},{20,18... | collective-permute-start | bytes 442376 | tf_op jit(solution)/shard_map/ppermute | solution.py:377
  23.5 4.6 %collective-permute-start.7 = (f32[5,72,512]{2,1,0:T(8,128)}, f32[5,72,512]{2,1,0:T(8,128)S(1)}, u32[]{:S(2)}, u32[]{:S(2)}) collective-permute-start(f32[5,72,512]{2,1,0:T(8,128)} %maximum_select_fusion), channel_id=1, source_target_pairs={{0,2},{2,4},{3,1},{4,6},{5,3},{7,5},{16,18},{18,20},{19,17},{20,22... | collective-permute-start | bytes 2211848 | tf_op jit(solution)/shard_map/ppermute | solution.py:377
  28.2 3.9 %collective-permute-start.5 = (f32[4,72,512]{2,1,0:T(8,128)S(1)}, f32[4,72,512]{2,1,0:T(8,128)S(1)}, u32[]{:S(2)}, u32[]{:S(2)}) collective-permute-start(f32[4,72,512]{2,1,0:T(8,128)S(1)} %collective-permute-done.4.driven_near), channel_id=1, source_target_pairs={{0,2},{2,4},{3,1},{4,6},{5,3},{7,5},{16,18},{18,20},{19,17},{20,22... | collective-permute-start | bytes 1769480 | tf_op jit(solution)/shard_map/ppermute | solution.py:377
  32.2 3.2 %shard_map.137 = (f32[4,72,512]{2,1,0:T(8,128)S(1)}, f32[4,72,512]{2,1,0:T(8,128)S(1)}, f32[128,128]{1,0:T(8,128)S(1)}, f32[408,256]{1,0:T(8,128)S(1)}) custom-call(s32[4]{0:T(128)S(1)} %pad_add_fusion.1.place, f32[136,256]{1,0:T(8,128)} %shard_map.136.mine, f32[136,256]{1,0:T(8,128)} %collective-permute-done.second, ...), custom_call_target="tpu_custom_call" | custom-call | flops 679477248 | bytes 5308416 | tf_op jit(solution)/shard_map/pallas_call | solution.py:33
  35.4 1.3 %collective-permute-start.2 = (f32[408,256]{1,0:T(8,128)S(1)}, f32[408,256]{1,0:T(8,128)S(1)}, u32[]{:S(2)}, u32[]{:S(2)}) collective-permute-start(f32[408,256]{1,0:T(8,128)S(1)} %get-tuple-element.15), channel_id=1, source_target_pairs={{0,1},{1,2},{2,3},{3,4},{4,5},{5,6},{6,7},{16,17},{17,18},{18,19},... | collective-permute-start | bytes 1253384 | tf_op jit(solution)/shard_map/ppermute | solution.py:377
  36.7 1.3 %collective-permute-start.3 = (f32[408,256]{1,0:T(8,128)S(1)}, f32[408,256]{1,0:T(8,128)S(1)}, u32[]{:S(2)}, u32[]{:S(2)}) collective-permute-start(f32[408,256]{1,0:T(8,128)S(1)} %get-tuple-element.15), channel_id=1, source_target_pairs={{1,0},{2,1},{3,2},{4,3},{5,4},{6,5},{7,6},{17,16},{18,17},{19,18},... | collective-permute-start | bytes 1253384 | tf_op jit(solution)/shard_map/ppermute | solution.py:377
  39.4 2.8 %collective-permute-done.2.joined_lower = f32[408,256]{1,0:T(8,128)S(1)} collective-permute-done((f32[408,256]{1,0:T(8,128)S(1)}, f32[408,256]{1,0:T(8,128)S(1)}, u32[]{:S(2)}, u32[]{:S(2)}) %collective-permute-start.2) | collective-permute-done | bytes 417824 | tf_op jit(solution)/shard_map/ppermute | solution.py:377
  42.2 6.0 %collective-permute-done.3.joined_upper = f32[408,256]{1,0:T(8,128)S(1)} collective-permute-done((f32[408,256]{1,0:T(8,128)S(1)}, f32[408,256]{1,0:T(8,128)S(1)}, u32[]{:S(2)}, u32[]{:S(2)}) %collective-permute-start.3) | collective-permute-done | bytes 417824 | tf_op jit(solution)/shard_map/ppermute | solution.py:377
  48.3 11.4 %shard_map.138 = (f32[128,384]{1,0:T(8,128)S(1)}, f32[128,384]{1,0:T(8,128)S(1)}, f32[128,384]{1,0:T(8,128)S(1)}) custom-call(s32[4]{0:T(128)S(1)} %pad_add_fusion.1.place, s32[384]{0:T(512)S(1)} %fusion.7.rows_at, f32[408,256]{1,0:T(8,128)S(1)} %collective-permute-done.2.joined_lower, f32[408,256]{1,0:T(8,128)S(1)} %collective-permute-done.3.joined_upper, ...), custom_call_target="tpu_custom_call" | custom-call | flops 1358954496 | bytes 11796480 | tf_op jit(solution)/shard_map/pallas_call | solution.py:33
  59.7 2.1 %collective-permute-start.10 = (f32[128,384]{1,0:T(8,128)S(1)}, f32[128,384]{1,0:T(8,128)S(1)}, u32[]{:S(2)}, u32[]{:S(2)}) collective-permute-start(f32[128,384]{1,0:T(8,128)S(1)} %get-tuple-element.20), channel_id=1, source_target_pairs={{0,8},{1,9},{2,10},{3,11},{4,12},{5,13},{6,14},{7,15},{16,0},{17,1... | collective-permute-start | bytes 589832 | tf_op jit(solution)/shard_map/ppermute | solution.py:377
  61.8 3.9 %collective-permute-start.9 = (f32[128,384]{1,0:T(8,128)S(1)}, f32[128,384]{1,0:T(8,128)S(1)}, u32[]{:S(2)}, u32[]{:S(2)}) collective-permute-start(f32[128,384]{1,0:T(8,128)S(1)} %get-tuple-element.19), channel_id=1, source_target_pairs={{0,16},{1,17},{2,18},{3,19},{4,20},{5,21},{6,22},{7,23},{16,8},{17... | collective-permute-start | bytes 589832 | tf_op jit(solution)/shard_map/ppermute | solution.py:377
  65.7 10.9 %shard_map.139 = (f32[384,128]{1,0:T(8,128)S(1)}, f32[96,128]{1,0:T(8,128)S(1)}, f32[96,128]{1,0:T(8,128)S(1)}) custom-call(f32[3,16384]{1,0:T(4,128)S(1)} %copy-done.3, f32[3,16384]{1,0:T(4,128)S(1)} %copy-done, s32[2,4096]{1,0:T(2,128)S(1)} %copy-done.7), custom_call_target="tpu_custom_call" | custom-call | flops 50331648 | bytes 786432 | tf_op jit(solution)/shard_map/pallas_call | solution.py:33
  76.7 4.8 %collective-permute-start.11 = (f32[96,128]{1,0:T(8,128)S(1)}, f32[96,128]{1,0:T(8,128)S(1)}, u32[]{:S(2)}, u32[]{:S(2)}) collective-permute-start(f32[96,128]{1,0:T(8,128)S(1)} %get-tuple-element.23), channel_id=1, source_target_pairs={{0,1},{1,2},{2,3},{3,4},{4,5},{5,6},{6,7},{8,9},{9,10},{10,11},{11... | collective-permute-start | bytes 147464 | tf_op jit(solution)/shard_map/ppermute | solution.py:377
  81.5 1.3 %collective-permute-start.12 = (f32[96,128]{1,0:T(8,128)S(1)}, f32[96,128]{1,0:T(8,128)S(1)}, u32[]{:S(2)}, u32[]{:S(2)}) collective-permute-start(f32[96,128]{1,0:T(8,128)S(1)} %get-tuple-element.24), channel_id=1, source_target_pairs={{1,0},{2,1},{3,2},{4,3},{5,4},{6,5},{7,6},{9,8},{10,9},{11,10},{12... | collective-permute-start | bytes 147464 | tf_op jit(solution)/shard_map/ppermute | solution.py:377
  83.2 4.8 %collective-permute-done.12.upper = f32[96,128]{1,0:T(8,128)S(1)} collective-permute-done((f32[96,128]{1,0:T(8,128)S(1)}, f32[96,128]{1,0:T(8,128)S(1)}, u32[]{:S(2)}, u32[]{:S(2)}) %collective-permute-start.12) | collective-permute-done | bytes 49184 | tf_op jit(solution)/shard_map/ppermute | solution.py:377
  88.0 4.2 %shard_map.140.contact = f32[384,128]{1,0:T(8,128)S(1)} custom-call(s32[128]{0:T(128)S(1)} %copy-done.8, f32[384,128]{1,0:T(8,128)S(1)} %get-tuple-element.22.state, f32[96,128]{1,0:T(8,128)S(1)} %collective-permute-done.11.lower, f32[96,128]{1,0:T(8,128)S(1)} %collective-permute-done.12.upper, s32[8,16384]{1,0:T(8,128)S(1)} %copy-done.1, ...), custom_call_target="tpu_custom_call" | custom-call | flops 7864320 | bytes 1310720 | tf_op jit(solution)/shard_map/pallas_call | solution.py:33
  (38 shorter events, 4.5 us)
Async XLA Ops:
  0.0 6.3 %copy-start.10 = (f32[4,128,512]{2,1,0:T(8,128)S(1)}, f32[4,128,512]{2,1,0:T(8,128)}, u32[]{:S(2)}) copy-start(f32[4,128,512]{2,1,0:T(8,128)} %param.27) | copy-start | bytes 3145732
  1.3 8.9 %copy-start.4 = (s32[16384]{0:T(1024)S(1)}, s32[16384]{0:T(1024)}, u32[]{:S(2)}) copy-start(s32[16384]{0:T(1024)} %param.23) | copy-start | bytes 196612
  1.3 8.9 %copy-start.5 = (f32[16384]{0:T(1024)S(1)}, f32[16384]{0:T(1024)}, u32[]{:S(2)}) copy-start(f32[16384]{0:T(1024)} %param.16) | copy-start | bytes 196612
  1.3 8.9 %copy-start.6 = (f32[16384]{0:T(1024)S(1)}, f32[16384]{0:T(1024)}, u32[]{:S(2)}) copy-start(f32[16384]{0:T(1024)} %param.17) | copy-start | bytes 196612
  1.3 21.2 %collective-permute-start.6 = (f32[4,72,512]{2,1,0:T(8,128)S(1)}, f32[4,72,512]{2,1,0:T(8,128)S(1)}, u32[]{:S(2)}, u32[]{:S(2)}) collective-permute-start(f32[4,72,512]{2,1,0:T(8,128)S(1)} %constant_dynamic-slice_fusion.pressure), channel_id=1, source_target_pairs={{0,1},{1,0},{2,3},{3,2},{4,5},{5,4},{6,7},{7,6},{16,17},{17,16},{1... | collective-permute-start | bytes 1769480 | tf_op jit(solution)/shard_map/ppermute | solution.py:377
  7.6 20.7 %collective-permute-start.4 = (f32[4,72,512]{2,1,0:T(8,128)S(1)}, f32[4,72,512]{2,1,0:T(8,128)S(1)}, u32[]{:S(2)}, u32[]{:S(2)}) collective-permute-start(f32[4,72,512]{2,1,0:T(8,128)S(1)} %dynamic-slice_subtract_fusion.driven), channel_id=1, source_target_pairs={{0,1},{1,0},{2,3},{3,2},{4,5},{5,4},{6,7},{7,6},{16,17},{17,16},{1... | collective-permute-start | bytes 1769480 | tf_op jit(solution)/shard_map/ppermute | solution.py:377
  10.2 0.7 copy-start.9
  13.7 18.5 %collective-permute-start = (f32[136,256]{1,0:T(8,128)}, f32[136,256]{1,0:T(8,128)}, u32[]{:S(2)}, u32[]{:S(2)}) collective-permute-start(f32[136,256]{1,0:T(8,128)} %shard_map.136.mine), channel_id=1, source_target_pairs={{0,8},{1,9},{2,10},{3,11},{4,12},{5,13},{6,14},{7,15},{8,16},{9,17... | collective-permute-start | bytes 417800 | tf_op jit(solution)/shard_map/ppermute | solution.py:377
  15.6 16.6 %collective-permute-start.1 = (f32[136,256]{1,0:T(8,128)}, f32[136,256]{1,0:T(8,128)}, u32[]{:S(2)}, u32[]{:S(2)}) collective-permute-start(f32[136,256]{1,0:T(8,128)} %shard_map.136.mine), channel_id=1, source_target_pairs={{0,16},{1,17},{2,18},{3,19},{4,20},{5,21},{6,22},{7,23},{8,0},{9,1... | collective-permute-start | bytes 417800 | tf_op jit(solution)/shard_map/ppermute | solution.py:377
  21.2 18.1 %collective-permute-start.8 = (f32[72,512]{1,0:T(8,128)}, f32[72,512]{1,0:T(8,128)S(1)}, u32[]{:S(2)}, u32[]{:S(2)}) collective-permute-start(f32[72,512]{1,0:T(8,128)} %get-tuple-element.25), channel_id=1, source_target_pairs={{1,3},{2,0},{3,5},{4,2},{5,7},{6,4},{17,19},{18,16},{19,21},{20,18... | collective-permute-start | bytes 442376 | tf_op jit(solution)/shard_map/ppermute | solution.py:377
  23.5 24.7 %collective-permute-start.7 = (f32[5,72,512]{2,1,0:T(8,128)}, f32[5,72,512]{2,1,0:T(8,128)S(1)}, u32[]{:S(2)}, u32[]{:S(2)}) collective-permute-start(f32[5,72,512]{2,1,0:T(8,128)} %maximum_select_fusion), channel_id=1, source_target_pairs={{0,2},{2,4},{3,1},{4,6},{5,3},{7,5},{16,18},{18,20},{19,17},{20,22... | collective-permute-start | bytes 2211848 | tf_op jit(solution)/shard_map/ppermute | solution.py:377
  28.2 20.0 %collective-permute-start.5 = (f32[4,72,512]{2,1,0:T(8,128)S(1)}, f32[4,72,512]{2,1,0:T(8,128)S(1)}, u32[]{:S(2)}, u32[]{:S(2)}) collective-permute-start(f32[4,72,512]{2,1,0:T(8,128)S(1)} %collective-permute-done.4.driven_near), channel_id=1, source_target_pairs={{0,2},{2,4},{3,1},{4,6},{5,3},{7,5},{16,18},{18,20},{19,17},{20,22... | collective-permute-start | bytes 1769480 | tf_op jit(solution)/shard_map/ppermute | solution.py:377
  35.4 6.8 %collective-permute-start.2 = (f32[408,256]{1,0:T(8,128)S(1)}, f32[408,256]{1,0:T(8,128)S(1)}, u32[]{:S(2)}, u32[]{:S(2)}) collective-permute-start(f32[408,256]{1,0:T(8,128)S(1)} %get-tuple-element.15), channel_id=1, source_target_pairs={{0,1},{1,2},{2,3},{3,4},{4,5},{5,6},{6,7},{16,17},{17,18},{18,19},... | collective-permute-start | bytes 1253384 | tf_op jit(solution)/shard_map/ppermute | solution.py:377
  36.7 11.5 %collective-permute-start.3 = (f32[408,256]{1,0:T(8,128)S(1)}, f32[408,256]{1,0:T(8,128)S(1)}, u32[]{:S(2)}, u32[]{:S(2)}) collective-permute-start(f32[408,256]{1,0:T(8,128)S(1)} %get-tuple-element.15), channel_id=1, source_target_pairs={{1,0},{2,1},{3,2},{4,3},{5,4},{6,5},{7,6},{17,16},{18,17},{19,18},... | collective-permute-start | bytes 1253384 | tf_op jit(solution)/shard_map/ppermute | solution.py:377
  48.2 17.5 %copy-start = (f32[3,16384]{1,0:T(4,128)S(1)}, f32[3,16384]{1,0:T(4,128)}, u32[]{:S(2)}) copy-start(f32[3,16384]{1,0:T(4,128)} %vel.3) | copy-start | bytes 589828
  48.2 17.5 %copy-start.3 = (f32[3,16384]{1,0:T(4,128)S(1)}, f32[3,16384]{1,0:T(4,128)}, u32[]{:S(2)}) copy-start(f32[3,16384]{1,0:T(4,128)} %pos.1) | copy-start | bytes 589828
  48.2 17.5 %copy-start.7 = (s32[2,4096]{1,0:T(2,128)S(1)}, s32[2,4096]{1,0:T(2,128)}, u32[]{:S(2)}) copy-start(s32[2,4096]{1,0:T(2,128)} %lists.1) | copy-start | bytes 98308
  48.2 39.8 %copy-start.2 = (f32[8,16384]{1,0:T(8,128)S(1)}, f32[8,16384]{1,0:T(8,128)}, u32[]{:S(2)}) copy-start(f32[8,16384]{1,0:T(8,128)} %stiff.1) | copy-start | bytes 1572868
  59.7 28.3 %copy-start.1 = (s32[8,16384]{1,0:T(8,128)S(1)}, s32[8,16384]{1,0:T(8,128)}, u32[]{:S(2)}) copy-start(s32[8,16384]{1,0:T(8,128)} %named.1) | copy-start | bytes 1572868
  59.7 32.5 %collective-permute-start.10 = (f32[128,384]{1,0:T(8,128)S(1)}, f32[128,384]{1,0:T(8,128)S(1)}, u32[]{:S(2)}, u32[]{:S(2)}) collective-permute-start(f32[128,384]{1,0:T(8,128)S(1)} %get-tuple-element.20), channel_id=1, source_target_pairs={{0,8},{1,9},{2,10},{3,11},{4,12},{5,13},{6,14},{7,15},{16,0},{17,1... | collective-permute-start | bytes 589832 | tf_op jit(solution)/shard_map/ppermute | solution.py:377
  61.8 30.5 %collective-permute-start.9 = (f32[128,384]{1,0:T(8,128)S(1)}, f32[128,384]{1,0:T(8,128)S(1)}, u32[]{:S(2)}, u32[]{:S(2)}) collective-permute-start(f32[128,384]{1,0:T(8,128)S(1)} %get-tuple-element.19), channel_id=1, source_target_pairs={{0,16},{1,17},{2,18},{3,19},{4,20},{5,21},{6,22},{7,23},{16,8},{17... | collective-permute-start | bytes 589832 | tf_op jit(solution)/shard_map/ppermute | solution.py:377
  76.7 6.6 %collective-permute-start.11 = (f32[96,128]{1,0:T(8,128)S(1)}, f32[96,128]{1,0:T(8,128)S(1)}, u32[]{:S(2)}, u32[]{:S(2)}) collective-permute-start(f32[96,128]{1,0:T(8,128)S(1)} %get-tuple-element.23), channel_id=1, source_target_pairs={{0,1},{1,2},{2,3},{3,4},{4,5},{5,6},{6,7},{8,9},{9,10},{10,11},{11... | collective-permute-start | bytes 147464 | tf_op jit(solution)/shard_map/ppermute | solution.py:377
  81.5 6.5 %copy-start.8 = (s32[128]{0:T(128)S(1)}, s32[128]{0:T(128)}, u32[]{:S(2)}) copy-start(s32[128]{0:T(128)} %partner.1) | copy-start | bytes 1540
  81.5 6.5 %collective-permute-start.12 = (f32[96,128]{1,0:T(8,128)S(1)}, f32[96,128]{1,0:T(8,128)S(1)}, u32[]{:S(2)}, u32[]{:S(2)}) collective-permute-start(f32[96,128]{1,0:T(8,128)S(1)} %get-tuple-element.24), channel_id=1, source_target_pairs={{1,0},{2,1},{3,2},{4,3},{5,4},{6,5},{7,6},{9,8},{10,9},{11,10},{12... | collective-permute-start | bytes 147464 | tf_op jit(solution)/shard_map/ppermute | solution.py:377

commit v3 on v2

--- a/solution.py
+++ b/solution.py
@@ -17,6 +17,7 @@
 
 VMEM = pl.BlockSpec(memory_space=pltpu.VMEM)
 SMEM = pl.BlockSpec(memory_space=pltpu.SMEM)
+ANY = pl.BlockSpec(memory_space=pl.ANY)
 F32 = jnp.float32
 BF16 = jnp.bfloat16
 
@@ -45,16 +46,26 @@
     return jnp.take_along_axis(source, index, axis=1, mode="promise_in_bounds")
 
 
-def thirds(value):
+def halves_of(value):
     high = value.astype(BF16)
-    rest = value - high.astype(F32)
-    middle = rest.astype(BF16)
-    low = (rest - middle.astype(F32)).astype(BF16)
-    return high, middle, low
-
-
-def deposit_kernel(count, cell, vol, drag, ids, out):
+    return high, (value - high.astype(F32)).astype(BF16)
+
+
+def entry_kernel(
+    count, place, cell, vol, drag, ids, pressure_old, source, solid_before,
+    out, pressure, driven, ends, solid, sems,
+):
     tiles = cell.shape[0]
+    planes, height, _ = pressure.shape
+    rows = pl.ds(pl.multiple_of(place[0], SUB), height)
+    copies = [
+        pltpu.make_async_copy(whole.at[:, rows, :], part, sems.at[index])
+        for index, (whole, part) in enumerate(
+            ((pressure_old, pressure), (source, driven), (solid_before, solid))
+        )
+    ]
+    for copy in copies:
+        copy.start()
     sub = iota((SUB, BLOCK), 0)
     rows_c = iota((BLOCK, BLOCK), 0)
     even = sub % 2 == 0
@@ -65,7 +76,7 @@
         slot = (first + sub) * BLOCK + iota((SUB, BLOCK), 1)
         live = slot < count[0]
         cells = cell[pl.ds(first, SUB), :]
-        parts = thirds(jnp.where(live, vol[pl.ds(first, SUB), :], 0.0)) + thirds(
+        parts = halves_of(jnp.where(live, vol[pl.ds(first, SUB), :], 0.0)) + halves_of(
             jnp.where(live, drag[pl.ds(first, SUB), :], 0.0)
         )
         parts = [part.astype(F32) for part in parts]
@@ -87,9 +98,8 @@
                 loads, picked, (((1,), (1,)), ((), ())), preferred_element_type=F32
             )
             for field in range(2):
-                base = field * 3 * SUB
+                base = field * 2 * SUB
                 total = placed[base : base + SUB] + placed[base + SUB : base + 2 * SUB]
-                total = total + placed[base + 2 * SUB : base + 3 * SUB]
                 chosen = jnp.where(low_pair, total[:, :BLOCK], total[:, BLOCK:])
                 sums[field] = jnp.where(sub // 4 == quad, chosen, sums[field])
         out[pl.ds(first, SUB), :BLOCK] = sums[0]
@@ -99,9 +109,20 @@
     lax.fori_loop(0, tiles // SUB, step, 0, unroll=2)
     out[tiles : tiles + SUB, :BLOCK] = jnp.broadcast_to(ids[...].astype(F32), (SUB, BLOCK))
     out[tiles : tiles + SUB, BLOCK:] = jnp.zeros((SUB, BLOCK), F32)
-
-
-def halo_kernel(pos, vel, lists, state, down, up, index):
+    for copy in copies:
+        copy.wait()
+    driven[...] = driven[...] - solid[...]
+
+    @pl.when(place[1] == 1)
+    def _():
+        ends[...] = pressure[planes - 1]
+
+    @pl.when(place[1] != 1)
+    def _():
+        ends[...] = pressure[0]
+
+
+def halo_kernel(pos, vel, lists, state, down, up):
     tiles = pos.shape[1] // BLOCK
     rows = lists.shape[1] // BLOCK
     for tile in range(tiles):
@@ -109,37 +130,35 @@
         mixed = SPRING * pos[:, lanes] - DAMPING * vel[:, lanes]
         for axis in range(3):
             state[axis * tiles + tile : axis * tiles + tile + 1, :] = mixed[axis : axis + 1]
-    for side in range(2):
-        for row in range(rows):
-            index[side * rows + row : side * rows + row + 1, :] = lists[
-                side : side + 1, row * BLOCK : (row + 1) * BLOCK
-            ]
-    groups = 2 * rows // SUB
-    named = [index[g * SUB : (g + 1) * SUB, :] for g in range(groups)]
-    block = [lax.shift_right_logical(value, 7) for value in named]
-    lane = [value & (BLOCK - 1) for value in named]
-
-    def step(source, sums):
-        new = []
-        spread = [
-            jnp.broadcast_to(state[pl.ds(axis * tiles + source, 1), :], (SUB, BLOCK))
-            for axis in range(3)
-        ]
-        for g in range(groups):
-            here = block[g] == source
+    turned = [
+        jnp.concatenate(halves_of(jnp.transpose(state[axis * tiles : (axis + 1) * tiles, :])), 1)
+        for axis in range(3)
+    ]
+    turned = jnp.concatenate(turned, 0)
+    span = 2 * BLOCK
+    row = iota((BLOCK, span), 0)
+
+    for side, out in enumerate((down, up)):
+
+        def step(part, carry):
+            named = lists[side : side + 1, pl.ds(pl.multiple_of(part * span, span), span)]
+            block = lax.shift_right_logical(named, 7)
+            lane = named & (BLOCK - 1)
+            hot = jnp.where(row == jnp.broadcast_to(block, row.shape), 1.0, 0.0).astype(BF16)
+            found = jnp.dot(
+                turned, jnp.concatenate([hot, hot], 0), preferred_element_type=F32
+            )
+            here = row == jnp.broadcast_to(lane, row.shape)
             for axis in range(3):
-                new.append(
-                    jnp.where(here, lanes_of(spread[axis], lane[g]), sums[3 * g + axis])
-                )
-        return tuple(new)
-
-    zero = jnp.zeros((SUB, BLOCK), F32)
-    sums = lax.fori_loop(0, tiles, step, (zero,) * (3 * groups), unroll=2)
-    for side, out in enumerate((down, up)):
-        for axis in range(3):
-            for g in range(groups // 2):
-                first = axis * rows + g * SUB
-                out[first : first + SUB, :] = sums[3 * (side * groups // 2 + g) + axis]
+                value = jnp.where(here, found[axis * BLOCK : (axis + 1) * BLOCK], 0.0)
+                value = jnp.sum(value, axis=0, keepdims=True)
+                for half in range(2):
+                    out[pl.ds(axis * rows + 2 * part + half, 1), :] = value[
+                        :, half * BLOCK : (half + 1) * BLOCK
+                    ]
+            return carry
+
+        lax.fori_loop(0, rows // 2, step, 0, unroll=2)
 
 
 def contact_kernel(partner, state, lower, upper, named, stiff, out, extended):
@@ -184,16 +203,16 @@
 
 
 def placed(groups, tiles):
-    parts = [thirds(group[:tiles, :]) for group in groups]
-    loads = [jnp.concatenate([part[i] for part in parts], 0) for i in range(3)]
+    parts = [halves_of(group[:tiles, :]) for group in groups]
+    loads = jnp.concatenate([part[i] for i in range(2) for part in parts], 0)
     ids = jnp.concatenate([group[tiles : tiles + 1, :BLOCK] for group in groups], 1)
     ids = ids.astype(jnp.int32)
 
     def gathered(wanted):
         hot = jnp.where(wanted == jnp.broadcast_to(ids, wanted.shape), 1.0, 0.0).astype(BF16)
-        total = jnp.dot(hot, loads[2], preferred_element_type=F32)
-        total = total + jnp.dot(hot, loads[1], preferred_element_type=F32)
-        total = total + jnp.dot(hot, loads[0], preferred_element_type=F32)
+        total = jnp.dot(
+            jnp.concatenate([hot, hot], 1), loads, preferred_element_type=F32
+        )
         return total[:, :BLOCK], total[:, BLOCK:]
 
     return ids, gathered
@@ -224,23 +243,32 @@
     lax.fori_loop(0, planes, plane, 0)
 
 
-def own_kernel(full, place, mine, second, third, driven, constant, factor, weight, joined):
+def own_kernel(full, own_rows, place, mine, second, third, driven, constant, factor, weight, rows_at):
     stride = mine.shape[0]
     tiles = stride - SUB
-    groups = (mine, second, third)
-    for index, group in enumerate(groups):
-        joined[index * stride : (index + 1) * stride, :] = group[...]
-    ids, gathered = placed(groups, tiles)
+    planes, height, width = driven.shape
+    zones = width // BLOCK
+    ids, gathered = placed((mine, second, third), tiles)
     coefficients(gathered, tiles, place[0], full, driven, constant, factor, 0, None)
-    own = jnp.transpose(jnp.broadcast_to(ids[:, :tiles], (tiles, tiles)).astype(F32))
-    solid, drag = gathered(jnp.concatenate([own.astype(jnp.int32)] * 3, 1))
+    turned = [
+        jnp.transpose(
+            jnp.broadcast_to(ids[:, i * tiles : (i + 1) * tiles], (BLOCK, tiles)).astype(F32)
+        ).astype(jnp.int32)
+        for i in range(3)
+    ]
+    solid, drag = gathered(jnp.concatenate([turned[0]] * 3, 1))
     weight[...] = 1.0 / (1.0 / (1.0 + solid) + drag)
+    for i, block in enumerate(turned):
+        line, zone = block // zones, block % zones
+        x, y = line // full, line % full
+        row = (x * zones + zone) * height + y - place[0]
+        rows_at[i * tiles : (i + 1) * tiles, :] = jnp.where(y // own_rows == place[4], row, -1)
 
 
 def solve_kernel(
     full, sweeps, place, rows_at, joined_lower, joined_upper, driven_near, driven_far, pressure,
     near, far, beyond, own_constant, own_factor, out_a, out_b, out_c,
-    driven, constant, factor, old, new, fields,
+    driven, constant, factor, old, new, fields, sems,
 ):
     planes, height, width = pressure.shape
     zones = width // BLOCK
@@ -249,25 +277,50 @@
     odd, lower, upper = place[1] == 1, place[2] == 1, place[3] == 1
     rim = sweeps + 1
 
-    @pl.when(odd)
-    def _():
-        driven[:planes] = driven_near[...]
-        driven[planes:] = driven_far[...]
-        old[0] = beyond[...]
-        old[1 : 1 + planes] = near[...]
-        old[rim + planes : rim + 2 * planes + 1] = far[...]
-
-    @pl.when(jnp.logical_not(odd))
-    def _():
-        driven[:planes] = driven_far[...]
-        driven[planes:] = driven_near[...]
-        old[: 1 + planes] = far[...]
-        old[rim + planes : rim + 2 * planes] = near[...]
-        old[rim + 2 * planes] = beyond[...]
-
-    old[rim : rim + planes] = pressure[...]
-    constant[planes : 2 * planes] = own_constant[...]
-    factor[planes : 2 * planes] = own_factor[...]
+    def copies(moves, base):
+        return [
+            pltpu.make_async_copy(source, target, sems.at[base + index])
+            for index, (source, target) in enumerate(moves)
+        ]
+
+    always = copies(
+        (
+            (pressure, old.at[rim : rim + planes]),
+            (own_constant, constant.at[planes : 2 * planes]),
+            (own_factor, factor.at[planes : 2 * planes]),
+        ),
+        0,
+    )
+    of_odd = (
+        (driven_near, driven.at[:planes]),
+        (driven_far, driven.at[planes:]),
+        (beyond, old.at[0]),
+        (near, old.at[1 : 1 + planes]),
+        (far, old.at[rim + planes : rim + 2 * planes + 1]),
+    )
+    of_even = (
+        (driven_far, driven.at[:planes]),
+        (driven_near, driven.at[planes:]),
+        (beyond, old.at[rim + 2 * planes]),
+        (near, old.at[rim + planes : rim + 2 * planes]),
+        (far, old.at[: 1 + planes]),
+    )
+
+    def each(act, chosen):
+        @pl.when(odd)
+        def _():
+            for copy in copies(of_odd[chosen], len(always) + (chosen.start or 0)):
+                act(copy)
+
+        @pl.when(jnp.logical_not(odd))
+        def _():
+            for copy in copies(of_even[chosen], len(always) + (chosen.start or 0)):
+                act(copy)
+
+    each(lambda copy: copy.start(), slice(None))
+    for copy in always:
+        copy.start()
+    each(lambda copy: copy.wait(), slice(0, 2))
     for index, (joined, present) in enumerate(((joined_lower, lower), (joined_upper, upper))):
         groups = [joined.at[i * stride : (i + 1) * stride] for i in range(3)]
         _, gathered = placed(groups, tiles)
@@ -275,6 +328,9 @@
             gathered, tiles, place[0], full, driven.at[index * planes : (index + 1) * planes],
             constant, factor, 2 * index * planes, present,
         )
+    each(lambda copy: copy.wait(), slice(2, 5))
+    for copy in always:
+        copy.wait()
 
     def sweep(source, target, depth):
         def plane(x, carry):
@@ -304,15 +360,16 @@
         return carry
 
     lax.fori_loop(0, planes, gradient, 0)
-    none = planes * zones * height
-    fields[none : none + SUB, :] = jnp.zeros((SUB, 3 * BLOCK), F32)
-
-    def pick(tile, carry):
-        for index, out in enumerate((out_a, out_b, out_c)):
-            out[pl.ds(tile, 1), :] = fields[pl.ds(rows_at[index * tiles + tile], 1), :]
-        return carry
-
-    lax.fori_loop(0, tiles, pick, 0, unroll=8)
+    span = 3 * BLOCK
+    wanted = jnp.concatenate([rows_at[...]] * 3, 1)
+    column = iota(wanted.shape, 1)
+    total = jnp.zeros((3 * tiles, span), F32)
+    for part in range(planes * zones * height // span):
+        hot = jnp.where(wanted == column + part * span, 1.0, 0.0).astype(BF16)
+        for piece in halves_of(fields[part * span : (part + 1) * span, :]):
+            total = total + jnp.dot(hot, piece, preferred_element_type=F32)
+    for index, out in enumerate((out_a, out_b, out_c)):
+        out[...] = total[index * tiles : (index + 1) * tiles]
 
 
 def final_kernel(
@@ -368,7 +425,9 @@
     half = group // CORES
     first = jnp.clip(half * own_rows - SUB, 0, full - height)
     odd = region % 2 == 1
-    place = jnp.stack([first, odd, region > 0, region < regions - 1]).astype(jnp.int32)
+    place = jnp.stack(
+        [first, odd, region > 0, region < regions - 1, jnp.where(group % CORES == 0, half, -1)]
+    ).astype(jnp.int32)
     owners = range(0, groups, CORES)
     holders = range(holding)
 
@@ -396,22 +455,22 @@
     ids = tile_cell_block.reshape(1, tiles)
     field_bytes = 4 * planes * height * width
 
-    mine = call(
-        deposit_kernel, shaped(tiles + SUB, 2 * BLOCK), [SMEM] + [VMEM] * 4,
-        (count, cell, vol, drag, ids), flops=2 * 32 * 48 * 65536, size=5 * 4 * slots,
+    field = shaped(planes, height, width)
+    mine, pressure, driven, ends = call(
+        entry_kernel, (shaped(tiles + SUB, 2 * BLOCK), field, field, shaped(height, width)),
+        [SMEM] * 2 + [VMEM] * 4 + [ANY] * 3,
+        (count, place, cell, vol, drag, ids, pressure_old, pressure_source, solid_old),
+        [pltpu.VMEM((planes, height, width), F32), pltpu.SemaphoreType.DMA((3,))],
+        flops=2 * 32 * 48 * 65536, size=5 * 4 * slots,
     )
     second = along_grp(mine, 1, holders)
     third = along_grp(mine, 2, holders)
-
-    def window(whole):
-        return lax.dynamic_slice(whole, (0, first, 0), (planes, height, width))
-
-    driven = window(pressure_source) - window(solid_old)
-    pressure = window(pressure_old)
+    near = along_reg(pressure, owners, (1, -1))
     driven_near = along_reg(driven, owners, (1, -1))
-    near = along_reg(pressure, owners, (1, -1))
-    ends = jnp.where(odd, pressure[planes - 1], pressure[0])
     beyond = along_reg(ends, owners, (-2, 2))
+    joined = jnp.concatenate([mine, second, third], 0)
+    joined_lower = along_reg(joined, owners, (1, 1))
+    joined_upper = along_reg(joined, owners, (-1, -1))
     driven_far = along_reg(driven_near, owners, (2, -2))
     inner = jnp.where(odd, pressure[:1], pressure[planes - 1 :])
     far = along_reg(
@@ -421,37 +480,28 @@
         owners, (2, -2),
     )
 
-    field = shaped(planes, height, width)
-    constant, factor, weight, joined = call(
-        functools.partial(own_kernel, full),
-        (field, field, shaped(tiles, BLOCK), shaped(3 * (tiles + SUB), 2 * BLOCK)),
+    constant, factor, weight, rows_at = call(
+        functools.partial(own_kernel, full, own_rows),
+        (
+            field, field, shaped(tiles, BLOCK),
+            jax.ShapeDtypeStruct((3 * tiles, BLOCK), jnp.int32),
+        ),
         [SMEM] + [VMEM] * 4, (place, mine, second, third, driven),
         flops=planes * height * 4 * 384 * 256 * 6, size=9 * field_bytes,
     )
-    joined_lower = along_reg(joined, owners, (1, 1))
-    joined_upper = along_reg(joined, owners, (-1, -1))
 
     rows = halo_list.shape[1] // BLOCK
     state, down, up = call(
         halo_kernel, (shaped(3 * tiles, BLOCK), shaped(3 * rows, BLOCK), shaped(3 * rows, BLOCK)),
-        [VMEM] * 3, (grain_pos, grain_vel, halo_list),
-        [pltpu.VMEM((2 * rows, BLOCK), jnp.int32)], flops=8 * 3 * 16384 * 128, size=4 * 4 * 3 * slots,
+        [VMEM] * 3, (grain_pos, grain_vel, halo_list), flops=8 * 3 * 16384 * 128, size=4 * 4 * 3 * slots,
     )
     lower = along_reg(up, holders, (1, 1))
     upper = along_reg(down, holders, (-1, -1))
-
-    blocks = jnp.concatenate(
-        [tile_cell_block, second[tiles, :BLOCK].astype(jnp.int32), third[tiles, :BLOCK].astype(jnp.int32)]
-    )
-    line, zone = blocks // zones, blocks % zones
-    x, y = line // full, line % full
-    held = (y // own_rows == half) & (group % CORES == 0)
-    rows_at = jnp.where(held, (x * zones + zone) * height + y - first, planes * zones * height)
 
     grads = shaped(tiles, 3 * BLOCK)
     window_of = lambda count: pltpu.VMEM((count, height, width), F32)
     grads_a, grads_b, grads_c = call(
-        functools.partial(solve_kernel, full, ITERS), (grads,) * 3, [SMEM] * 2 + [VMEM] * 10,
+        functools.partial(solve_kernel, full, ITERS), (grads,) * 3, [SMEM] + [VMEM] * 3 + [ANY] * 8,
         (
             place, rows_at, joined_lower, joined_upper, driven_near, driven_far, pressure, near, far,
             beyond, constant, factor,
@@ -459,7 +509,8 @@
         [
             window_of(2 * planes), window_of(3 * planes), window_of(3 * planes),
             window_of(3 * planes + 2), window_of(3 * planes + 2),
-            pltpu.VMEM((planes * zones * height + SUB, 3 * BLOCK), F32),
+            pltpu.VMEM((planes * zones * height, 3 * BLOCK), F32),
+            pltpu.SemaphoreType.DMA((8,)),
         ],
         flops=2 * planes * height * 4 * 384 * 256 * 6, size=20 * field_bytes,
     )

time: 93.9 us -> 86.5 us (0.921)
  Pallas kernels: 33.6 us -> 27.3 us
  other arithmetic: 5.38 us -> 0.09 us
  local copies, waits for them, and re-layouts: 1.93 us -> 6.19 us
  starting transfers between devices: 37.3 us -> 33.6 us
  waiting for transfers between devices: 14.1 us -> 17.6 us
    pallas_call x6, Pallas kernels: 33.6 us -> 27.3 us  [call(): pl.pallas_call(kernel, out_shape=outs, in_specs=specs, out_specs=jax.tree...]
    unnamed x22 -> x32, local copies, waits for them, and re-layouts: 0.68 us -> 6.09 us
    ppermute x13, starting transfers between devices: 37.3 us -> 33.6 us  [send(): return lax.ppermute(value, ('grp', 'reg'), flat)]
    ppermute x13, waiting for transfers between devices: 14.1 us -> 17.6 us  [send(): return lax.ppermute(value, ('grp', 'reg'), flat)]
    select_n x2 -> x1, other arithmetic: 1.74 us -> 0.02 us  [on_device(): inner = jnp.where(odd, pressure[:1], pressure[planes - 1:])]
    convert_element_type x2 -> x0, other arithmetic: 1.36 us -> none  [the longest x1 0.68 us: on_device(): third[tiles, :BLOCK].astype(jnp.int32)]
    dynamic_slice x1 -> x0, local copies, waits for them, and re-layouts: 1.25 us -> none  [window(): return lax.dynamic_slice(whole, (0, first, 0), (planes, height, width))]
    sub x1 -> x0, other arithmetic: 1.25 us -> none  [on_device(): driven = window(pressure_source) - window(solid_old)]
  transfers between devices with their start and end apart: 13 -> 13, of which waited for: 4 -> 4; matrix products, arithmetic and copies ran while one was open for 6% -> 0% of each run, Pallas kernels for 23% -> 13%
where the time goes in v3:
time: 86.5 us; the launch traced here: 85.8 us
  starting transfers between devices  33.6 us (39%)
  Pallas kernels  27.3 us (32%)
  waiting for transfers between devices  17.6 us (20%)
  local copies, waits for them, and re-layouts  6.19 us (7%)
  between operations  1.03 us (1%)
    ppermute x13, starting transfers between devices, send(): return lax.ppermute(value, ('grp', 'reg'), flat)  33.6 us
    pallas_call x6, Pallas kernels, call(): pl.pallas_call(kernel, out_shape=outs, in_specs=specs, out_specs=jax.tree...  27.3 us
    ppermute x13, waiting for transfers between devices, send(): return lax.ppermute(value, ('grp', 'reg'), flat)  17.6 us
    unnamed x32, local copies, waits for them, and re-layouts  6.09 us
  transfers between devices with their start and end apart: 13, of which 4 were waited for; matrix products, arithmetic and copies ran while one was open for 0% of the time, Pallas kernels for 13%

profile of v3, /device:TPU:0, one launch (start us, length us, event | category | flops | bytes accessed | tf_op | source)
XLA Modules:
  0.0 85.8 jit_solution(18161320991051953157)
XLA Ops:
  1.4 1.2 %copy-done.1 = f32[4,128,512]{2,1,0:T(8,128)S(1)} copy-done((f32[4,128,512]{2,1,0:T(8,128)S(1)}, f32[4,128,512]{2,1,0:T(8,128)}, u32[]{:S(2)}) %copy-start.1) | copy-done | bytes 1048600
  2.7 1.2 %copy-done.2 = f32[4,128,512]{2,1,0:T(8,128)S(1)} copy-done((f32[4,128,512]{2,1,0:T(8,128)S(1)}, f32[4,128,512]{2,1,0:T(8,128)}, u32[]{:S(2)}) %copy-start.2) | copy-done | bytes 1048600
  3.9 1.2 %copy-done.3 = f32[4,128,512]{2,1,0:T(8,128)S(1)} copy-done((f32[4,128,512]{2,1,0:T(8,128)S(1)}, f32[4,128,512]{2,1,0:T(8,128)}, u32[]{:S(2)}) %copy-start.3) | copy-done | bytes 1048600
  6.8 3.0 %shard_map.136 = (f32[136,256]{1,0:T(8,128)S(1)}, f32[4,72,512]{2,1,0:T(8,128)S(1)}, f32[4,72,512]{2,1,0:T(8,128)S(1)}, f32[72,512]{1,0:T(8,128)S(1)}) custom-call(s32[1]{0:T(128)S(6)} %copy.17.count, s32[5]{0:T(128)S(1)} %stack.35.place, s32[128,128]{1,0:T(8,128)S(1)} %bitcast.9, f32[128,128]{1,0:T(8,128)S(1)} %bitcast.11, f32[128,128]{1,0:T(8,128)S(1)} %bitcast.13, ...), custom_call_target="tpu_custom_call" | custom-call | flops 201326592 | bytes 327680 | tf_op jit(solution)/shard_map/pallas_call | solution.py:34
  9.8 4.9 %collective-permute-start.6 = (f32[4,72,512]{2,1,0:T(8,128)S(1)}, f32[4,72,512]{2,1,0:T(8,128)S(1)}, u32[]{:S(2)}, u32[]{:S(2)}) collective-permute-start(f32[4,72,512]{2,1,0:T(8,128)S(1)} %get-tuple-element.22.pressure), channel_id=1, source_target_pairs={{0,1},{1,0},{2,3},{3,2},{4,5},{5,4},{6,7},{7,6},{16,17},{17,16},{1... | collective-permute-start | bytes 1769480 | tf_op jit(solution)/shard_map/ppermute | solution.py:436
  14.7 1.9 %collective-permute-start.4 = (f32[4,72,512]{2,1,0:T(8,128)S(1)}, f32[4,72,512]{2,1,0:T(8,128)S(1)}, u32[]{:S(2)}, u32[]{:S(2)}) collective-permute-start(f32[4,72,512]{2,1,0:T(8,128)S(1)} %get-tuple-element.20.driven), channel_id=1, source_target_pairs={{0,1},{1,0},{2,3},{3,2},{4,5},{5,4},{6,7},{7,6},{16,17},{17,16},{1... | collective-permute-start | bytes 1769480 | tf_op jit(solution)/shard_map/ppermute | solution.py:436
  16.6 1.9 %collective-permute-start = (f32[136,256]{1,0:T(8,128)S(1)}, f32[136,256]{1,0:T(8,128)S(1)}, u32[]{:S(2)}, u32[]{:S(2)}) collective-permute-start(f32[136,256]{1,0:T(8,128)S(1)} %get-tuple-element.19.mine), channel_id=1, source_target_pairs={{0,8},{1,9},{2,10},{3,11},{4,12},{5,13},{6,14},{7,15},{8,16},{9,17... | collective-permute-start | bytes 417800 | tf_op jit(solution)/shard_map/ppermute | solution.py:436
  18.6 3.9 %collective-permute-start.1 = (f32[136,256]{1,0:T(8,128)S(1)}, f32[136,256]{1,0:T(8,128)S(1)}, u32[]{:S(2)}, u32[]{:S(2)}) collective-permute-start(f32[136,256]{1,0:T(8,128)S(1)} %get-tuple-element.19.mine), channel_id=1, source_target_pairs={{0,16},{1,17},{2,18},{3,19},{4,20},{5,21},{6,22},{7,23},{8,0},{9,1... | collective-permute-start | bytes 417800 | tf_op jit(solution)/shard_map/ppermute | solution.py:436
  22.6 4.0 %collective-permute-start.7 = (f32[5,72,512]{2,1,0:T(8,128)S(1)}, f32[5,72,512]{2,1,0:T(8,128)S(1)}, u32[]{:S(2)}, u32[]{:S(2)}) collective-permute-start(f32[5,72,512]{2,1,0:T(8,128)S(1)} %maximum_select_fusion), channel_id=1, source_target_pairs={{0,2},{2,4},{3,1},{4,6},{5,3},{7,5},{16,18},{18,20},{19,17},{20,22... | collective-permute-start | bytes 2211848 | tf_op jit(solution)/shard_map/ppermute | solution.py:436
  26.7 2.2 %collective-permute-done.4.driven_near = f32[4,72,512]{2,1,0:T(8,128)S(1)} collective-permute-done((f32[4,72,512]{2,1,0:T(8,128)S(1)}, f32[4,72,512]{2,1,0:T(8,128)S(1)}, u32[]{:S(2)}, u32[]{:S(2)}) %collective-permute-start.4) | collective-permute-done | bytes 589856 | tf_op jit(solution)/shard_map/ppermute | solution.py:436
  28.9 4.0 %collective-permute-start.5 = (f32[4,72,512]{2,1,0:T(8,128)S(1)}, f32[4,72,512]{2,1,0:T(8,128)S(1)}, u32[]{:S(2)}, u32[]{:S(2)}) collective-permute-start(f32[4,72,512]{2,1,0:T(8,128)S(1)} %collective-permute-done.4.driven_near), channel_id=1, source_target_pairs={{0,2},{2,4},{3,1},{4,6},{5,3},{7,5},{16,18},{18,20},{19,17},{20,22... | collective-permute-start | bytes 1769480 | tf_op jit(solution)/shard_map/ppermute | solution.py:436
  32.9 1.3 %collective-permute-start.2 = (f32[408,256]{1,0:T(8,128)S(1)}, f32[408,256]{1,0:T(8,128)S(1)}, u32[]{:S(2)}, u32[]{:S(2)}) collective-permute-start(f32[408,256]{1,0:T(8,128)S(1)} %constant_dynamic-update-slice_fusion), channel_id=1, source_target_pairs={{0,1},{1,2},{2,3},{3,4},{4,5},{5,6},{6,7},{16,17},{17,18},{18,19},... | collective-permute-start | bytes 1253384 | tf_op jit(solution)/shard_map/ppermute | solution.py:436
  34.3 1.3 %collective-permute-start.3 = (f32[408,256]{1,0:T(8,128)S(1)}, f32[408,256]{1,0:T(8,128)S(1)}, u32[]{:S(2)}, u32[]{:S(2)}) collective-permute-start(f32[408,256]{1,0:T(8,128)S(1)} %constant_dynamic-update-slice_fusion), channel_id=1, source_target_pairs={{1,0},{2,1},{3,2},{4,3},{5,4},{6,5},{7,6},{17,16},{18,17},{19,18},... | collective-permute-start | bytes 1253384 | tf_op jit(solution)/shard_map/ppermute | solution.py:436
  35.6 1.3 %collective-permute-start.8 = (f32[72,512]{1,0:T(8,128)S(1)}, f32[72,512]{1,0:T(8,128)S(1)}, u32[]{:S(2)}, u32[]{:S(2)}) collective-permute-start(f32[72,512]{1,0:T(8,128)S(1)} %get-tuple-element.23), channel_id=1, source_target_pairs={{1,3},{2,0},{3,5},{4,2},{5,7},{6,4},{17,19},{18,16},{19,21},{20,18... | collective-permute-start | bytes 442376 | tf_op jit(solution)/shard_map/ppermute | solution.py:436
  36.9 2.5 %shard_map.137 = (f32[4,72,512]{2,1,0:T(8,128)S(1)}, f32[4,72,512]{2,1,0:T(8,128)S(1)}, f32[128,128]{1,0:T(8,128)S(1)}, s32[384,128]{1,0:T(8,128)S(1)}) custom-call(s32[5]{0:T(128)S(1)} %stack.35.place, f32[136,256]{1,0:T(8,128)S(1)} %get-tuple-element.19.mine, f32[136,256]{1,0:T(8,128)S(1)} %collective-permute-done.second, ...), custom_call_target="tpu_custom_call" | custom-call | flops 679477248 | bytes 5308416 | tf_op jit(solution)/shard_map/pallas_call | solution.py:34
  39.3 9.5 %collective-permute-done.8.beyond = f32[72,512]{1,0:T(8,128)S(1)} collective-permute-done((f32[72,512]{1,0:T(8,128)S(1)}, f32[72,512]{1,0:T(8,128)S(1)}, u32[]{:S(2)}, u32[]{:S(2)}) %collective-permute-start.8) | collective-permute-done | bytes 147488 | tf_op jit(solution)/shard_map/ppermute | solution.py:436
  48.9 11.8 %shard_map.138 = (f32[128,384]{1,0:T(8,128)S(1)}, f32[128,384]{1,0:T(8,128)S(1)}, f32[128,384]{1,0:T(8,128)S(1)}) custom-call(s32[5]{0:T(128)S(1)} %stack.35.place, s32[384,128]{1,0:T(8,128)S(1)} %get-tuple-element.21.rows_at, f32[408,256]{1,0:T(8,128)S(1)} %collective-permute-done.2.joined_lower, f32[408,256]{1,0:T(8,128)S(1)} %collective-permute-done.3.joined_upper, ...), custom_call_target="tpu_custom_call" | custom-call | flops 1358954496 | bytes 11796480 | tf_op jit(solution)/shard_map/pallas_call | solution.py:34
  60.7 2.1 %collective-permute-start.10 = (f32[128,384]{1,0:T(8,128)S(1)}, f32[128,384]{1,0:T(8,128)S(1)}, u32[]{:S(2)}, u32[]{:S(2)}) collective-permute-start(f32[128,384]{1,0:T(8,128)S(1)} %get-tuple-element.28), channel_id=1, source_target_pairs={{0,8},{1,9},{2,10},{3,11},{4,12},{5,13},{6,14},{7,15},{16,0},{17,1... | collective-permute-start | bytes 589832 | tf_op jit(solution)/shard_map/ppermute | solution.py:436
  62.7 3.9 %collective-permute-start.9 = (f32[128,384]{1,0:T(8,128)S(1)}, f32[128,384]{1,0:T(8,128)S(1)}, u32[]{:S(2)}, u32[]{:S(2)}) collective-permute-start(f32[128,384]{1,0:T(8,128)S(1)} %get-tuple-element.27), channel_id=1, source_target_pairs={{0,16},{1,17},{2,18},{3,19},{4,20},{5,21},{6,22},{7,23},{16,8},{17... | collective-permute-start | bytes 589832 | tf_op jit(solution)/shard_map/ppermute | solution.py:436
  66.7 4.8 %shard_map.139 = (f32[384,128]{1,0:T(8,128)S(1)}, f32[96,128]{1,0:T(8,128)S(1)}, f32[96,128]{1,0:T(8,128)S(1)}) custom-call(f32[3,16384]{1,0:T(4,128)S(1)} %copy-done.6, f32[3,16384]{1,0:T(4,128)S(1)} %copy-done, s32[2,4096]{1,0:T(2,128)S(1)} %copy-done.12), custom_call_target="tpu_custom_call" | custom-call | flops 50331648 | bytes 786432 | tf_op jit(solution)/shard_map/pallas_call | solution.py:34
  71.6 1.8 %collective-permute-start.11 = (f32[96,128]{1,0:T(8,128)S(1)}, f32[96,128]{1,0:T(8,128)S(1)}, u32[]{:S(2)}, u32[]{:S(2)}) collective-permute-start(f32[96,128]{1,0:T(8,128)S(1)} %get-tuple-element.31), channel_id=1, source_target_pairs={{0,1},{1,2},{2,3},{3,4},{4,5},{5,6},{6,7},{8,9},{9,10},{10,11},{11... | collective-permute-start | bytes 147464 | tf_op jit(solution)/shard_map/ppermute | solution.py:436
  73.3 1.3 %collective-permute-start.12 = (f32[96,128]{1,0:T(8,128)S(1)}, f32[96,128]{1,0:T(8,128)S(1)}, u32[]{:S(2)}, u32[]{:S(2)}) collective-permute-start(f32[96,128]{1,0:T(8,128)S(1)} %get-tuple-element.32), channel_id=1, source_target_pairs={{1,0},{2,1},{3,2},{4,3},{5,4},{6,5},{7,6},{9,8},{10,9},{11,10},{12... | collective-permute-start | bytes 147464 | tf_op jit(solution)/shard_map/ppermute | solution.py:436
  75.1 5.4 %collective-permute-done.12.upper = f32[96,128]{1,0:T(8,128)S(1)} collective-permute-done((f32[96,128]{1,0:T(8,128)S(1)}, f32[96,128]{1,0:T(8,128)S(1)}, u32[]{:S(2)}, u32[]{:S(2)}) %collective-permute-start.12) | collective-permute-done | bytes 49184 | tf_op jit(solution)/shard_map/ppermute | solution.py:436
  80.5 4.2 %shard_map.140.contact = f32[384,128]{1,0:T(8,128)S(1)} custom-call(s32[128]{0:T(128)S(1)} %copy-done.13, f32[384,128]{1,0:T(8,128)S(1)} %get-tuple-element.30.state, f32[96,128]{1,0:T(8,128)S(1)} %collective-permute-done.11.lower, f32[96,128]{1,0:T(8,128)S(1)} %collective-permute-done.12.upper, s32[8,16384]{1,0:T(8,128)S(1)} %copy-done.4, ...), custom_call_target="tpu_custom_call" | custom-call | flops 7864320 | bytes 1310720 | tf_op jit(solution)/shard_map/pallas_call | solution.py:34
  (44 shorter events, 4.1 us)
Async XLA Ops:
  1.4 1.2 %copy-start.1 = (f32[4,128,512]{2,1,0:T(8,128)S(1)}, f32[4,128,512]{2,1,0:T(8,128)}, u32[]{:S(2)}) copy-start(f32[4,128,512]{2,1,0:T(8,128)} %pressure_old.1) | copy-start | bytes 3145732
  2.7 1.2 %copy-start.2 = (f32[4,128,512]{2,1,0:T(8,128)S(1)}, f32[4,128,512]{2,1,0:T(8,128)}, u32[]{:S(2)}) copy-start(f32[4,128,512]{2,1,0:T(8,128)} %source.1) | copy-start | bytes 3145732
  3.9 1.2 %copy-start.3 = (f32[4,128,512]{2,1,0:T(8,128)S(1)}, f32[4,128,512]{2,1,0:T(8,128)}, u32[]{:S(2)}) copy-start(f32[4,128,512]{2,1,0:T(8,128)} %solid_before.1) | copy-start | bytes 3145732
  9.8 12.7 %collective-permute-start.6 = (f32[4,72,512]{2,1,0:T(8,128)S(1)}, f32[4,72,512]{2,1,0:T(8,128)S(1)}, u32[]{:S(2)}, u32[]{:S(2)}) collective-permute-start(f32[4,72,512]{2,1,0:T(8,128)S(1)} %get-tuple-element.22.pressure), channel_id=1, source_target_pairs={{0,1},{1,0},{2,3},{3,2},{4,5},{5,4},{6,7},{7,6},{16,17},{17,16},{1... | collective-permute-start | bytes 1769480 | tf_op jit(solution)/shard_map/ppermute | solution.py:436
  14.7 14.2 %collective-permute-start.4 = (f32[4,72,512]{2,1,0:T(8,128)S(1)}, f32[4,72,512]{2,1,0:T(8,128)S(1)}, u32[]{:S(2)}, u32[]{:S(2)}) collective-permute-start(f32[4,72,512]{2,1,0:T(8,128)S(1)} %get-tuple-element.20.driven), channel_id=1, source_target_pairs={{0,1},{1,0},{2,3},{3,2},{4,5},{5,4},{6,7},{7,6},{16,17},{17,16},{1... | collective-permute-start | bytes 1769480 | tf_op jit(solution)/shard_map/ppermute | solution.py:436
  16.6 16.2 %collective-permute-start = (f32[136,256]{1,0:T(8,128)S(1)}, f32[136,256]{1,0:T(8,128)S(1)}, u32[]{:S(2)}, u32[]{:S(2)}) collective-permute-start(f32[136,256]{1,0:T(8,128)S(1)} %get-tuple-element.19.mine), channel_id=1, source_target_pairs={{0,8},{1,9},{2,10},{3,11},{4,12},{5,13},{6,14},{7,15},{8,16},{9,17... | collective-permute-start | bytes 417800 | tf_op jit(solution)/shard_map/ppermute | solution.py:436
  18.6 14.3 %collective-permute-start.1 = (f32[136,256]{1,0:T(8,128)S(1)}, f32[136,256]{1,0:T(8,128)S(1)}, u32[]{:S(2)}, u32[]{:S(2)}) collective-permute-start(f32[136,256]{1,0:T(8,128)S(1)} %get-tuple-element.19.mine), channel_id=1, source_target_pairs={{0,16},{1,17},{2,18},{3,19},{4,20},{5,21},{6,22},{7,23},{8,0},{9,1... | collective-permute-start | bytes 417800 | tf_op jit(solution)/shard_map/ppermute | solution.py:436
  22.6 26.2 %collective-permute-start.7 = (f32[5,72,512]{2,1,0:T(8,128)S(1)}, f32[5,72,512]{2,1,0:T(8,128)S(1)}, u32[]{:S(2)}, u32[]{:S(2)}) collective-permute-start(f32[5,72,512]{2,1,0:T(8,128)S(1)} %maximum_select_fusion), channel_id=1, source_target_pairs={{0,2},{2,4},{3,1},{4,6},{5,3},{7,5},{16,18},{18,20},{19,17},{20,22... | collective-permute-start | bytes 2211848 | tf_op jit(solution)/shard_map/ppermute | solution.py:436
  28.9 19.9 %collective-permute-start.5 = (f32[4,72,512]{2,1,0:T(8,128)S(1)}, f32[4,72,512]{2,1,0:T(8,128)S(1)}, u32[]{:S(2)}, u32[]{:S(2)}) collective-permute-start(f32[4,72,512]{2,1,0:T(8,128)S(1)} %collective-permute-done.4.driven_near), channel_id=1, source_target_pairs={{0,2},{2,4},{3,1},{4,6},{5,3},{7,5},{16,18},{18,20},{19,17},{20,22... | collective-permute-start | bytes 1769480 | tf_op jit(solution)/shard_map/ppermute | solution.py:436
  32.9 15.9 %collective-permute-start.2 = (f32[408,256]{1,0:T(8,128)S(1)}, f32[408,256]{1,0:T(8,128)S(1)}, u32[]{:S(2)}, u32[]{:S(2)}) collective-permute-start(f32[408,256]{1,0:T(8,128)S(1)} %constant_dynamic-update-slice_fusion), channel_id=1, source_target_pairs={{0,1},{1,2},{2,3},{3,4},{4,5},{5,6},{6,7},{16,17},{17,18},{18,19},... | collective-permute-start | bytes 1253384 | tf_op jit(solution)/shard_map/ppermute | solution.py:436
  34.3 14.6 %collective-permute-start.3 = (f32[408,256]{1,0:T(8,128)S(1)}, f32[408,256]{1,0:T(8,128)S(1)}, u32[]{:S(2)}, u32[]{:S(2)}) collective-permute-start(f32[408,256]{1,0:T(8,128)S(1)} %constant_dynamic-update-slice_fusion), channel_id=1, source_target_pairs={{1,0},{2,1},{3,2},{4,3},{5,4},{6,5},{7,6},{17,16},{18,17},{19,18},... | collective-permute-start | bytes 1253384 | tf_op jit(solution)/shard_map/ppermute | solution.py:436
  35.6 13.2 %collective-permute-start.8 = (f32[72,512]{1,0:T(8,128)S(1)}, f32[72,512]{1,0:T(8,128)S(1)}, u32[]{:S(2)}, u32[]{:S(2)}) collective-permute-start(f32[72,512]{1,0:T(8,128)S(1)} %get-tuple-element.23), channel_id=1, source_target_pairs={{1,3},{2,0},{3,5},{4,2},{5,7},{6,4},{17,19},{18,16},{19,21},{20,18... | collective-permute-start | bytes 442376 | tf_op jit(solution)/shard_map/ppermute | solution.py:436
  48.8 17.9 %copy-start = (f32[3,16384]{1,0:T(4,128)S(1)}, f32[3,16384]{1,0:T(4,128)}, u32[]{:S(2)}) copy-start(f32[3,16384]{1,0:T(4,128)} %vel.3) | copy-start | bytes 589828
  48.8 17.9 %copy-start.6 = (f32[3,16384]{1,0:T(4,128)S(1)}, f32[3,16384]{1,0:T(4,128)}, u32[]{:S(2)}) copy-start(f32[3,16384]{1,0:T(4,128)} %pos.1) | copy-start | bytes 589828
  48.8 17.9 %copy-start.12 = (s32[2,4096]{1,0:T(2,128)S(1)}, s32[2,4096]{1,0:T(2,128)}, u32[]{:S(2)}) copy-start(s32[2,4096]{1,0:T(2,128)} %lists.1) | copy-start | bytes 98308
  48.9 31.6 %copy-start.5 = (f32[8,16384]{1,0:T(8,128)S(1)}, f32[8,16384]{1,0:T(8,128)}, u32[]{:S(2)}) copy-start(f32[8,16384]{1,0:T(8,128)} %stiff.1) | copy-start | bytes 1572868
  60.7 19.8 %copy-start.4 = (s32[8,16384]{1,0:T(8,128)S(1)}, s32[8,16384]{1,0:T(8,128)}, u32[]{:S(2)}) copy-start(s32[8,16384]{1,0:T(8,128)} %named.1) | copy-start | bytes 1572868
  60.7 24.1 %collective-permute-start.10 = (f32[128,384]{1,0:T(8,128)S(1)}, f32[128,384]{1,0:T(8,128)S(1)}, u32[]{:S(2)}, u32[]{:S(2)}) collective-permute-start(f32[128,384]{1,0:T(8,128)S(1)} %get-tuple-element.28), channel_id=1, source_target_pairs={{0,8},{1,9},{2,10},{3,11},{4,12},{5,13},{6,14},{7,15},{16,0},{17,1... | collective-permute-start | bytes 589832 | tf_op jit(solution)/shard_map/ppermute | solution.py:436
  62.7 22.0 %collective-permute-start.9 = (f32[128,384]{1,0:T(8,128)S(1)}, f32[128,384]{1,0:T(8,128)S(1)}, u32[]{:S(2)}, u32[]{:S(2)}) collective-permute-start(f32[128,384]{1,0:T(8,128)S(1)} %get-tuple-element.27), channel_id=1, source_target_pairs={{0,16},{1,17},{2,18},{3,19},{4,20},{5,21},{6,22},{7,23},{16,8},{17... | collective-permute-start | bytes 589832 | tf_op jit(solution)/shard_map/ppermute | solution.py:436
  71.6 3.5 %collective-permute-start.11 = (f32[96,128]{1,0:T(8,128)S(1)}, f32[96,128]{1,0:T(8,128)S(1)}, u32[]{:S(2)}, u32[]{:S(2)}) collective-permute-start(f32[96,128]{1,0:T(8,128)S(1)} %get-tuple-element.31), channel_id=1, source_target_pairs={{0,1},{1,2},{2,3},{3,4},{4,5},{5,6},{6,7},{8,9},{9,10},{10,11},{11... | collective-permute-start | bytes 147464 | tf_op jit(solution)/shard_map/ppermute | solution.py:436
  73.3 7.2 %copy-start.13 = (s32[128]{0:T(128)S(1)}, s32[128]{0:T(128)}, u32[]{:S(2)}) copy-start(s32[128]{0:T(128)} %partner.1) | copy-start | bytes 1540
  73.3 7.2 %collective-permute-start.12 = (f32[96,128]{1,0:T(8,128)S(1)}, f32[96,128]{1,0:T(8,128)S(1)}, u32[]{:S(2)}, u32[]{:S(2)}) collective-permute-start(f32[96,128]{1,0:T(8,128)S(1)} %get-tuple-element.32), channel_id=1, source_target_pairs={{1,0},{2,1},{3,2},{4,3},{5,4},{6,5},{7,6},{9,8},{10,9},{11,10},{12... | collective-permute-start | bytes 147464 | tf_op jit(solution)/shard_map/ppermute | solution.py:436
  80.5 4.3 %copy-start.9 = (f32[16384]{0:T(1024)S(1)}, f32[16384]{0:T(1024)}, u32[]{:S(2)}) copy-start(f32[16384]{0:T(1024)} %param.16) | copy-start | bytes 196612
  80.5 4.3 %copy-start.11 = (f32[16384]{0:T(1024)S(1)}, f32[16384]{0:T(1024)}, u32[]{:S(2)}) copy-start(f32[16384]{0:T(1024)} %param.17) | copy-start | bytes 196612
  (4 other events, 3.2 us)

commit v4 on v3

--- a/solution.py
+++ b/solution.py
@@ -18,6 +18,7 @@
 VMEM = pl.BlockSpec(memory_space=pltpu.VMEM)
 SMEM = pl.BlockSpec(memory_space=pltpu.SMEM)
 ANY = pl.BlockSpec(memory_space=pl.ANY)
+HBM = pl.BlockSpec(memory_space=pltpu.HBM)
 F32 = jnp.float32
 BF16 = jnp.bfloat16
 
@@ -30,14 +31,14 @@
     return jax.ShapeDtypeStruct(dims, F32)
 
 
-def call(kernel, outs, specs, args, scratch=(), flops=0, size=0):
+def call(kernel, outs, specs, args, scratch=(), flops=0, size=0, limit=40_000_000):
     return pl.pallas_call(
         kernel,
         out_shape=outs,
         in_specs=specs,
         out_specs=jax.tree.map(lambda _: VMEM, outs),
         scratch_shapes=list(scratch),
-        compiler_params=pltpu.CompilerParams(vmem_limit_bytes=40 * 1024 * 1024),
+        compiler_params=pltpu.CompilerParams(vmem_limit_bytes=limit),
         cost_estimate=pl.CostEstimate(flops=flops, bytes_accessed=size, transcendentals=0),
     )(*args)
 
@@ -52,20 +53,24 @@
 
 
 def entry_kernel(
-    count, place, cell, vol, drag, ids, pressure_old, source, solid_before,
-    out, pressure, driven, ends, solid, sems,
+    count, place, cell_at, vol_at, drag_at, ids, pressure_old, source, solid_before,
+    out, pressure, driven, ends, solid, cell, vol, drag, sems,
 ):
     tiles = cell.shape[0]
     planes, height, _ = pressure.shape
     rows = pl.ds(pl.multiple_of(place[0], SUB), height)
+    moves = [(cell_at, cell), (vol_at, vol), (drag_at, drag)] + [
+        (whole.at[:, rows, :], part)
+        for whole, part in ((pressure_old, pressure), (source, driven), (solid_before, solid))
+    ]
     copies = [
-        pltpu.make_async_copy(whole.at[:, rows, :], part, sems.at[index])
-        for index, (whole, part) in enumerate(
-            ((pressure_old, pressure), (source, driven), (solid_before, solid))
-        )
+        pltpu.make_async_copy(whole, part, sems.at[index])
+        for index, (whole, part) in enumerate(moves)
     ]
     for copy in copies:
         copy.start()
+    for copy in copies[:3]:
+        copy.wait()
     sub = iota((SUB, BLOCK), 0)
     rows_c = iota((BLOCK, BLOCK), 0)
     even = sub % 2 == 0
@@ -109,7 +114,7 @@
     lax.fori_loop(0, tiles // SUB, step, 0, unroll=2)
     out[tiles : tiles + SUB, :BLOCK] = jnp.broadcast_to(ids[...].astype(F32), (SUB, BLOCK))
     out[tiles : tiles + SUB, BLOCK:] = jnp.zeros((SUB, BLOCK), F32)
-    for copy in copies:
+    for copy in copies[3:]:
         copy.wait()
     driven[...] = driven[...] - solid[...]
 
@@ -161,7 +166,7 @@
         lax.fori_loop(0, rows // 2, step, 0, unroll=2)
 
 
-def contact_kernel(partner, state, lower, upper, named, stiff, out, extended):
+def contact_kernel(partner, state, lower, upper, named, stiff, _, out, extended):
     tiles = state.shape[0] // 3
     rows = lower.shape[0] // 3
     blocks = tiles + 2 * rows
@@ -243,7 +248,9 @@
     lax.fori_loop(0, planes, plane, 0)
 
 
-def own_kernel(full, own_rows, place, mine, second, third, driven, constant, factor, weight, rows_at):
+def own_kernel(
+    full, own_rows, place, mine, second, third, driven, _, constant, factor, weight, rows_at
+):
     stride = mine.shape[0]
     tiles = stride - SUB
     planes, height, width = driven.shape
@@ -266,81 +273,47 @@
 
 
 def solve_kernel(
-    full, sweeps, place, rows_at, joined_lower, joined_upper, driven_near, driven_far, pressure,
-    near, far, beyond, own_constant, own_factor, out_a, out_b, out_c,
-    driven, constant, factor, old, new, fields, sems,
+    full, sweeps, place, rows_at, joined_near, joined_far, driven_near, driven_far, pressure,
+    near, far, beyond, own_constant, own_factor, _lower, _upper, out_a, out_b, out_c,
+    constant, factor, old, new, fields,
 ):
     planes, height, width = pressure.shape
     zones = width // BLOCK
-    stride = joined_lower.shape[0] // 3
+    stride = joined_near.shape[0] // 3
     tiles = stride - SUB
     odd, lower, upper = place[1] == 1, place[2] == 1, place[3] == 1
     rim = sweeps + 1
-
-    def copies(moves, base):
-        return [
-            pltpu.make_async_copy(source, target, sems.at[base + index])
-            for index, (source, target) in enumerate(moves)
-        ]
-
-    always = copies(
-        (
-            (pressure, old.at[rim : rim + planes]),
-            (own_constant, constant.at[planes : 2 * planes]),
-            (own_factor, factor.at[planes : 2 * planes]),
-        ),
-        0,
-    )
-    of_odd = (
-        (driven_near, driven.at[:planes]),
-        (driven_far, driven.at[planes:]),
-        (beyond, old.at[0]),
-        (near, old.at[1 : 1 + planes]),
-        (far, old.at[rim + planes : rim + 2 * planes + 1]),
-    )
-    of_even = (
-        (driven_far, driven.at[:planes]),
-        (driven_near, driven.at[planes:]),
-        (beyond, old.at[rim + 2 * planes]),
-        (near, old.at[rim + planes : rim + 2 * planes]),
-        (far, old.at[: 1 + planes]),
-    )
-
-    def each(act, chosen):
-        @pl.when(odd)
-        def _():
-            for copy in copies(of_odd[chosen], len(always) + (chosen.start or 0)):
-                act(copy)
-
-        @pl.when(jnp.logical_not(odd))
-        def _():
-            for copy in copies(of_even[chosen], len(always) + (chosen.start or 0)):
-                act(copy)
-
-    each(lambda copy: copy.start(), slice(None))
-    for copy in always:
-        copy.start()
-    each(lambda copy: copy.wait(), slice(0, 2))
-    for index, (joined, present) in enumerate(((joined_lower, lower), (joined_upper, upper))):
+    for joined, driven, below, present in (
+        (joined_near, driven_near, odd, jnp.where(odd, place[2], place[3])),
+        (joined_far, driven_far, jnp.logical_not(odd), jnp.where(odd, place[3], place[2])),
+    ):
         groups = [joined.at[i * stride : (i + 1) * stride] for i in range(3)]
         _, gathered = placed(groups, tiles)
         coefficients(
-            gathered, tiles, place[0], full, driven.at[index * planes : (index + 1) * planes],
-            constant, factor, 2 * index * planes, present,
+            gathered, tiles, place[0], full, driven, constant, factor,
+            jnp.where(below, 0, planes), present == 1,
         )
-    each(lambda copy: copy.wait(), slice(2, 5))
-    for copy in always:
-        copy.wait()
+    old[pl.ds(jnp.where(odd, 1, rim + planes), planes)] = near[...]
+    old[pl.ds(jnp.where(odd, rim + planes, 0), planes + 1)] = far[...]
+    old[pl.ds(jnp.where(odd, 0, rim + 2 * planes), 1)] = beyond[...][None]
+    old[rim : rim + planes] = pressure[...]
 
     def sweep(source, target, depth):
-        def plane(x, carry):
-            centre = source[x]
-            above, below, left, right = shifted(centre)
-            around = source[x - 1] + source[x + 1] + above + below + left + right
-            target[x] = constant[x - 1] + factor[x - 1] * around
-            return carry
-
-        lax.fori_loop(depth, 3 * planes + 2 - depth, plane, 0)
+        def over(constants, factors, shift):
+            def plane(x, carry):
+                centre = source[x]
+                above, below, left, right = shifted(centre)
+                around = source[x - 1] + source[x + 1] + above + below + left + right
+                target[x] = constants[x - shift] + factors[x - shift] * around
+                return carry
+
+            return plane
+
+        lax.fori_loop(depth, rim, over(constant, factor, 1), 0)
+        lax.fori_loop(rim, rim + planes, over(own_constant, own_factor, rim), 0)
+        lax.fori_loop(
+            rim + planes, 3 * planes + 2 - depth, over(constant, factor, 1 + planes), 0
+        )
 
     for index in range(sweeps):
         source, target = (old, new) if index % 2 == 0 else (new, old)
@@ -458,10 +431,14 @@
     field = shaped(planes, height, width)
     mine, pressure, driven, ends = call(
         entry_kernel, (shaped(tiles + SUB, 2 * BLOCK), field, field, shaped(height, width)),
-        [SMEM] * 2 + [VMEM] * 4 + [ANY] * 3,
+        [SMEM] * 2 + [HBM] * 3 + [VMEM] + [HBM] * 3,
         (count, place, cell, vol, drag, ids, pressure_old, pressure_source, solid_old),
-        [pltpu.VMEM((planes, height, width), F32), pltpu.SemaphoreType.DMA((3,))],
-        flops=2 * 32 * 48 * 65536, size=5 * 4 * slots,
+        [
+            pltpu.VMEM((planes, height, width), F32), pltpu.VMEM((tiles, BLOCK), jnp.int32),
+            pltpu.VMEM((tiles, BLOCK), F32), pltpu.VMEM((tiles, BLOCK), F32),
+            pltpu.SemaphoreType.DMA((6,)),
+        ],
+        flops=2 * 32 * 48 * 65536, size=5 * 4 * slots, limit=61_500_000,
     )
     second = along_grp(mine, 1, holders)
     third = along_grp(mine, 2, holders)
@@ -469,8 +446,8 @@
     driven_near = along_reg(driven, owners, (1, -1))
     beyond = along_reg(ends, owners, (-2, 2))
     joined = jnp.concatenate([mine, second, third], 0)
-    joined_lower = along_reg(joined, owners, (1, 1))
-    joined_upper = along_reg(joined, owners, (-1, -1))
+    joined_near = along_reg(joined, owners, (1, -1))
+    joined_far = along_reg(joined, owners, (-1, 1))
     driven_far = along_reg(driven_near, owners, (2, -2))
     inner = jnp.where(odd, pressure[:1], pressure[planes - 1 :])
     far = along_reg(
@@ -480,37 +457,36 @@
         owners, (2, -2),
     )
 
+    rows = halo_list.shape[1] // BLOCK
+    state, down, up = call(
+        halo_kernel, (shaped(3 * tiles, BLOCK), shaped(3 * rows, BLOCK), shaped(3 * rows, BLOCK)),
+        [VMEM] * 3, (grain_pos, grain_vel, halo_list), flops=8 * 3 * 16384 * 128, size=4 * 4 * 3 * slots,
+    )
+    lower = along_reg(up, holders, (1, 1))
+    upper = along_reg(down, holders, (-1, -1))
+
     constant, factor, weight, rows_at = call(
         functools.partial(own_kernel, full, own_rows),
         (
             field, field, shaped(tiles, BLOCK),
             jax.ShapeDtypeStruct((3 * tiles, BLOCK), jnp.int32),
         ),
-        [SMEM] + [VMEM] * 4, (place, mine, second, third, driven),
+        [SMEM] + [VMEM] * 4 + [ANY], (place, mine, second, third, driven, state),
         flops=planes * height * 4 * 384 * 256 * 6, size=9 * field_bytes,
     )
-
-    rows = halo_list.shape[1] // BLOCK
-    state, down, up = call(
-        halo_kernel, (shaped(3 * tiles, BLOCK), shaped(3 * rows, BLOCK), shaped(3 * rows, BLOCK)),
-        [VMEM] * 3, (grain_pos, grain_vel, halo_list), flops=8 * 3 * 16384 * 128, size=4 * 4 * 3 * slots,
-    )
-    lower = along_reg(up, holders, (1, 1))
-    upper = along_reg(down, holders, (-1, -1))
 
     grads = shaped(tiles, 3 * BLOCK)
     window_of = lambda count: pltpu.VMEM((count, height, width), F32)
     grads_a, grads_b, grads_c = call(
-        functools.partial(solve_kernel, full, ITERS), (grads,) * 3, [SMEM] + [VMEM] * 3 + [ANY] * 8,
+        functools.partial(solve_kernel, full, ITERS), (grads,) * 3, [SMEM] + [VMEM] * 11 + [ANY] * 2,
         (
-            place, rows_at, joined_lower, joined_upper, driven_near, driven_far, pressure, near, far,
-            beyond, constant, factor,
+            place, rows_at, joined_near, joined_far, driven_near, driven_far, pressure, near, far,
+            beyond, constant, factor, lower, upper,
         ),
         [
-            window_of(2 * planes), window_of(3 * planes), window_of(3 * planes),
+            window_of(2 * planes), window_of(2 * planes),
             window_of(3 * planes + 2), window_of(3 * planes + 2),
             pltpu.VMEM((planes * zones * height, 3 * BLOCK), F32),
-            pltpu.SemaphoreType.DMA((8,)),
         ],
         flops=2 * planes * height * 4 * 384 * 256 * 6, size=20 * field_bytes,
     )
@@ -518,8 +494,8 @@
     grads_c = along_grp(grads_c, -2, owners)
 
     contact = call(
-        contact_kernel, shaped(3 * tiles, BLOCK), [SMEM] + [VMEM] * 5,
-        (partner_block, state, lower, upper, contact_rows, contact_stiff),
+        contact_kernel, shaped(3 * tiles, BLOCK), [SMEM] + [VMEM] * 5 + [ANY],
+        (partner_block, state, lower, upper, contact_rows, contact_stiff, grads_a),
         [pltpu.VMEM((3 * (tiles + 2 * rows), BLOCK), F32)],
         flops=60 * 8 * slots, size=4 * 20 * slots,
     )

time: 86.5 us -> 83.6 us (0.966)
  local copies, waits for them, and re-layouts: 6.19 us -> 0.72 us
  starting transfers between devices: 33.6 us -> 36.4 us
  waiting for transfers between devices: 17.6 us -> 15.3 us
  Pallas kernels: 27.3 us -> 28.6 us
  other arithmetic: 0.09 us -> 1.07 us
    unnamed x32 -> x30, local copies, waits for them, and re-layouts: 6.09 us -> 0.1 us
    ppermute x13, starting transfers between devices: 33.6 us -> 36.4 us  [send(): return lax.ppermute(value, ('grp', 'reg'), flat)]
    ppermute x13, waiting for transfers between devices: 17.6 us -> 15.3 us  [send(): return lax.ppermute(value, ('grp', 'reg'), flat)]
    pallas_call x6, Pallas kernels: 27.3 us -> 28.6 us  [call(): pl.pallas_call(kernel, out_shape=outs, in_specs=specs, out_specs=jax.tree...]
    select_n x1, other arithmetic: 0.02 us -> 1 us  [on_device(): inner = jnp.where(odd, pressure[:1], pressure[planes - 1:])]
  transfers between devices with their start and end apart: 13 -> 13, of which waited for: 4 -> 5; matrix products, arithmetic and copies ran while one was open for 0% -> 1% of each run, Pallas kernels for 13% -> 14%
where the time goes in v4:
time: 83.6 us; the launch traced here: 83.1 us
  starting transfers between devices  36.4 us (44%)
  Pallas kernels  28.6 us (34%)
  waiting for transfers between devices  15.3 us (18%)
  other arithmetic  1.07 us (1%)
  between operations  1.07 us (1%)
    ppermute x13, starting transfers between devices, send(): return lax.ppermute(value, ('grp', 'reg'), flat)  36.4 us
    pallas_call x6, Pallas kernels, call(): pl.pallas_call(kernel, out_shape=outs, in_specs=specs, out_specs=jax.tree...  28.6 us
    ppermute x13, waiting for transfers between devices, send(): return lax.ppermute(value, ('grp', 'reg'), flat)  15.3 us
  transfers between devices with their start and end apart: 13, of which 5 were waited for; matrix products, arithmetic and copies ran while one was open for 1% of the time, Pallas kernels for 14%

profile of v4, /device:TPU:0, one launch (start us, length us, event | category | flops | bytes accessed | tf_op | source)
XLA Modules:
  0.0 83.1 jit_solution(13829744544950790985)
XLA Ops:
  1.3 5.0 %shard_map.136 = (f32[136,256]{1,0:T(8,128)}, f32[4,72,512]{2,1,0:T(8,128)}, f32[4,72,512]{2,1,0:T(8,128)}, f32[72,512]{1,0:T(8,128)}) custom-call(s32[1]{0:T(128)S(6)} %copy.17.count, s32[5]{0:T(128)} %stack.35.place, s32[128,128]{1,0:T(8,128)} %bitcast.9, f32[128,128]{1,0:T(8,128)} %bitcast.11, f32[128,128]{1,0:T(8,128)} %bitcast.13, s32[1,128]{1,0:T(1,128)} %bitcast.15, ...), custom_call_target="tpu_custom_call" | custom-call | flops 201326592 | bytes 327680 | tf_op jit(solution)/shard_map/pallas_call | solution.py:35
  6.2 4.9 %collective-permute-start.6 = (f32[4,72,512]{2,1,0:T(8,128)}, f32[4,72,512]{2,1,0:T(8,128)S(1)}, u32[]{:S(2)}, u32[]{:S(2)}) collective-permute-start(f32[4,72,512]{2,1,0:T(8,128)} %get-tuple-element.23.pressure), channel_id=1, source_target_pairs={{0,1},{1,0},{2,3},{3,2},{4,5},{5,4},{6,7},{7,6},{16,17},{17,16},{1... | collective-permute-start | bytes 1769480 | tf_op jit(solution)/shard_map/ppermute | solution.py:409
  11.1 1.9 %collective-permute-start.4 = (f32[4,72,512]{2,1,0:T(8,128)}, f32[4,72,512]{2,1,0:T(8,128)S(1)}, u32[]{:S(2)}, u32[]{:S(2)}) collective-permute-start(f32[4,72,512]{2,1,0:T(8,128)} %get-tuple-element.20.driven), channel_id=1, source_target_pairs={{0,1},{1,0},{2,3},{3,2},{4,5},{5,4},{6,7},{7,6},{16,17},{17,16},{1... | collective-permute-start | bytes 1769480 | tf_op jit(solution)/shard_map/ppermute | solution.py:409
  13.0 1.9 %collective-permute-start = (f32[136,256]{1,0:T(8,128)}, f32[136,256]{1,0:T(8,128)S(1)}, u32[]{:S(2)}, u32[]{:S(2)}) collective-permute-start(f32[136,256]{1,0:T(8,128)} %get-tuple-element.19.mine), channel_id=1, source_target_pairs={{0,8},{1,9},{2,10},{3,11},{4,12},{5,13},{6,14},{7,15},{8,16},{9,17... | collective-permute-start | bytes 417800 | tf_op jit(solution)/shard_map/ppermute | solution.py:409
  15.0 3.9 %collective-permute-start.1 = (f32[136,256]{1,0:T(8,128)}, f32[136,256]{1,0:T(8,128)S(1)}, u32[]{:S(2)}, u32[]{:S(2)}) collective-permute-start(f32[136,256]{1,0:T(8,128)} %get-tuple-element.19.mine), channel_id=1, source_target_pairs={{0,16},{1,17},{2,18},{3,19},{4,20},{5,21},{6,22},{7,23},{8,0},{9,1... | collective-permute-start | bytes 417800 | tf_op jit(solution)/shard_map/ppermute | solution.py:409
  18.9 1.0 %slice_select_fusion = f32[1,72,512]{2,1,0:T(8,128)S(1)} fusion(f32[4,72,512]{2,1,0:T(8,128)} %get-tuple-element.23.pressure, pred[]{:T(512)S(6)} %eq.9), kind=kLoop, calls=%fused_computation.1 | loop fusion | flops 36864 | bytes 442369 | tf_op jit(solution)/shard_map/jit(_where)/select_n | solution.py:452
  20.0 4.1 %collective-permute-start.7 = (f32[5,72,512]{2,1,0:T(8,128)S(1)}, f32[5,72,512]{2,1,0:T(8,128)S(1)}, u32[]{:S(2)}, u32[]{:S(2)}) collective-permute-start(f32[5,72,512]{2,1,0:T(8,128)S(1)} %maximum_select_fusion), channel_id=1, source_target_pairs={{0,2},{2,4},{3,1},{4,6},{5,3},{7,5},{16,18},{18,20},{19,17},{20,22... | collective-permute-start | bytes 2211848 | tf_op jit(solution)/shard_map/ppermute | solution.py:409
  24.2 1.3 %collective-permute-done.4.driven_near = f32[4,72,512]{2,1,0:T(8,128)S(1)} collective-permute-done((f32[4,72,512]{2,1,0:T(8,128)}, f32[4,72,512]{2,1,0:T(8,128)S(1)}, u32[]{:S(2)}, u32[]{:S(2)}) %collective-permute-start.4) | collective-permute-done | bytes 589856 | tf_op jit(solution)/shard_map/ppermute | solution.py:409
  25.5 4.0 %collective-permute-start.5 = (f32[4,72,512]{2,1,0:T(8,128)S(1)}, f32[4,72,512]{2,1,0:T(8,128)S(1)}, u32[]{:S(2)}, u32[]{:S(2)}) collective-permute-start(f32[4,72,512]{2,1,0:T(8,128)S(1)} %collective-permute-done.4.driven_near), channel_id=1, source_target_pairs={{0,2},{2,4},{3,1},{4,6},{5,3},{7,5},{16,18},{18,20},{19,17},{20,22... | collective-permute-start | bytes 1769480 | tf_op jit(solution)/shard_map/ppermute | solution.py:409
  29.6 2.1 %collective-permute-start.2 = (f32[408,256]{1,0:T(8,128)S(1)}, f32[408,256]{1,0:T(8,128)S(1)}, u32[]{:S(2)}, u32[]{:S(2)}) collective-permute-start(f32[408,256]{1,0:T(8,128)S(1)} %constant_dynamic-update-slice_fusion), channel_id=1, source_target_pairs={{0,1},{1,0},{2,3},{3,2},{4,5},{5,4},{6,7},{7,6},{16,17},{17,16},{1... | collective-permute-start | bytes 1253384 | tf_op jit(solution)/shard_map/ppermute | solution.py:409
  32.4 4.8 %shard_map.137 = (f32[384,128]{1,0:T(8,128)S(1)}, f32[96,128]{1,0:T(8,128)S(1)}, f32[96,128]{1,0:T(8,128)S(1)}) custom-call(f32[3,16384]{1,0:T(4,128)S(1)} %copy-done.4, f32[3,16384]{1,0:T(4,128)S(1)} %copy-done.1, s32[2,4096]{1,0:T(2,128)S(1)} %copy-done.9), custom_call_target="tpu_custom_call" | custom-call | flops 50331648 | bytes 786432 | tf_op jit(solution)/shard_map/pallas_call | solution.py:35
  37.2 1.3 %collective-permute-start.10 = (f32[96,128]{1,0:T(8,128)S(1)}, f32[96,128]{1,0:T(8,128)S(1)}, u32[]{:S(2)}, u32[]{:S(2)}) collective-permute-start(f32[96,128]{1,0:T(8,128)S(1)} %get-tuple-element.28), channel_id=1, source_target_pairs={{1,0},{2,1},{3,2},{4,3},{5,4},{6,5},{7,6},{9,8},{10,9},{11,10},{12... | collective-permute-start | bytes 147464 | tf_op jit(solution)/shard_map/ppermute | solution.py:409
  38.5 7.3 %collective-permute-done.10._upper.upper = f32[96,128]{1,0:T(8,128)S(1)} collective-permute-done((f32[96,128]{1,0:T(8,128)S(1)}, f32[96,128]{1,0:T(8,128)S(1)}, u32[]{:S(2)}, u32[]{:S(2)}) %collective-permute-start.10) | collective-permute-done | bytes 49184 | tf_op jit(solution)/shard_map/ppermute | solution.py:409
  45.8 4.8 %collective-permute-start.9 = (f32[96,128]{1,0:T(8,128)S(1)}, f32[96,128]{1,0:T(8,128)S(1)}, u32[]{:S(2)}, u32[]{:S(2)}) collective-permute-start(f32[96,128]{1,0:T(8,128)S(1)} %get-tuple-element.27), channel_id=1, source_target_pairs={{0,1},{1,2},{2,3},{3,4},{4,5},{5,6},{6,7},{8,9},{9,10},{10,11},{11... | collective-permute-start | bytes 147464 | tf_op jit(solution)/shard_map/ppermute | solution.py:409
  50.6 1.7 %collective-permute-done.9._lower.lower = f32[96,128]{1,0:T(8,128)S(1)} collective-permute-done((f32[96,128]{1,0:T(8,128)S(1)}, f32[96,128]{1,0:T(8,128)S(1)}, u32[]{:S(2)}, u32[]{:S(2)}) %collective-permute-start.9) | collective-permute-done | bytes 49184 | tf_op jit(solution)/shard_map/ppermute | solution.py:409
  52.4 1.4 %collective-permute-start.8 = (f32[72,512]{1,0:T(8,128)S(1)}, f32[72,512]{1,0:T(8,128)S(1)}, u32[]{:S(2)}, u32[]{:S(2)}) collective-permute-start(f32[72,512]{1,0:T(8,128)S(1)} %copy-done.13), channel_id=1, source_target_pairs={{1,3},{2,0},{3,5},{4,2},{5,7},{6,4},{17,19},{18,16},{19,21},{20,18... | collective-permute-start | bytes 442376 | tf_op jit(solution)/shard_map/ppermute | solution.py:409
  53.8 2.5 %shard_map.138 = (f32[4,72,512]{2,1,0:T(8,128)S(1)}, f32[4,72,512]{2,1,0:T(8,128)S(1)}, f32[128,128]{1,0:T(8,128)S(1)}, s32[384,128]{1,0:T(8,128)S(1)}) custom-call(s32[5]{0:T(128)S(1)} %copy-done.10, f32[136,256]{1,0:T(8,128)S(1)} %copy-done.8, f32[136,256]{1,0:T(8,128)S(1)} %collective-permute-done.second, f32[136,256]{1,0:T(8,128)S(1)} %collective-permute-done.1.third, ...), custom_call_target="tpu_custom_call" | custom-call | flops 679477248 | bytes 5308416 | tf_op jit(solution)/shard_map/pallas_call | solution.py:35
  56.3 3.6 %collective-permute-done.8.beyond = f32[72,512]{1,0:T(8,128)S(1)} collective-permute-done((f32[72,512]{1,0:T(8,128)S(1)}, f32[72,512]{1,0:T(8,128)S(1)}, u32[]{:S(2)}, u32[]{:S(2)}) %collective-permute-start.8) | collective-permute-done | bytes 147488 | tf_op jit(solution)/shard_map/ppermute | solution.py:409
  60.0 11.1 %shard_map.139 = (f32[128,384]{1,0:T(8,128)S(1)}, f32[128,384]{1,0:T(8,128)S(1)}, f32[128,384]{1,0:T(8,128)S(1)}) custom-call(s32[5]{0:T(128)S(1)} %copy-done.10, s32[384,128]{1,0:T(8,128)S(1)} %get-tuple-element.22.rows_at, f32[408,256]{1,0:T(8,128)S(1)} %collective-permute-done.2.joined_near, f32[408,256]{1,0:T(8,128)S(1)} %collective-permute-done.3.joined_far, ...), custom_call_target="tpu_custom_call" | custom-call | flops 1358954496 | bytes 11796480 | tf_op jit(solution)/shard_map/pallas_call | solution.py:35
  71.1 3.4 %collective-permute-start.11 = (f32[128,384]{1,0:T(8,128)S(1)}, f32[128,384]{1,0:T(8,128)S(1)}, u32[]{:S(2)}, u32[]{:S(2)}) collective-permute-start(f32[128,384]{1,0:T(8,128)S(1)} %get-tuple-element.30), channel_id=1, source_target_pairs={{0,16},{1,17},{2,18},{3,19},{4,20},{5,21},{6,22},{7,23},{16,8},{17... | collective-permute-start | bytes 589832 | tf_op jit(solution)/shard_map/ppermute | solution.py:409
  74.5 1.9 %collective-permute-start.12 = (f32[128,384]{1,0:T(8,128)S(1)}, f32[128,384]{1,0:T(8,128)S(1)}, u32[]{:S(2)}, u32[]{:S(2)}) collective-permute-start(f32[128,384]{1,0:T(8,128)S(1)} %get-tuple-element.31), channel_id=1, source_target_pairs={{0,8},{1,9},{2,10},{3,11},{4,12},{5,13},{6,14},{7,15},{16,0},{17,1... | collective-permute-start | bytes 589832 | tf_op jit(solution)/shard_map/ppermute | solution.py:409
  76.5 4.2 %shard_map.140.contact = f32[384,128]{1,0:T(8,128)S(1)} custom-call(s32[128]{0:T(128)S(1)} %copy-done.11, f32[384,128]{1,0:T(8,128)S(1)} %get-tuple-element.21._.state, f32[96,128]{1,0:T(8,128)S(1)} %collective-permute-done.9._lower.lower, f32[96,128]{1,0:T(8,128)S(1)} %collective-permute-done.10._upper.upper, s32[8,16384]{1,0:T(8,128)S(1)} %copy-done.2, ...), custom_call_target="tpu_custom_call" | custom-call | flops 7864320 | bytes 1310720 | tf_op jit(solution)/shard_map/pallas_call | solution.py:35
  80.7 1.4 %collective-permute-done.12.grads_c = f32[128,384]{1,0:T(8,128)S(1)} collective-permute-done((f32[128,384]{1,0:T(8,128)S(1)}, f32[128,384]{1,0:T(8,128)S(1)}, u32[]{:S(2)}, u32[]{:S(2)}) %collective-permute-start.12) | collective-permute-done | bytes 196640 | tf_op jit(solution)/shard_map/ppermute | solution.py:409
  82.1 1.0 %shard_map.141 = f32[3,16384]{1,0:T(4,128)} custom-call(s32[1]{0:T(128)S(6)} %copy.17.count, f32[128,384]{1,0:T(8,128)S(1)} %get-tuple-element.29._.grads_a, f32[128,384]{1,0:T(8,128)S(1)} %collective-permute-done.11.grads_b, f32[128,384]{1,0:T(8,128)S(1)} %collective-permute-done.12.grads_c, f32[128,128]{1,0:T(8,128)S(1)} %get-tuple-element.32.weight, ...), custom_call_target="tpu_custom_call" | custom-call | flops 983040 | bytes 1310720 | tf_op jit(solution)/shard_map/pallas_call | solution.py:35
  (42 shorter events, 1.5 us)
Async XLA Ops:
  6.2 13.7 %collective-permute-start.6 = (f32[4,72,512]{2,1,0:T(8,128)}, f32[4,72,512]{2,1,0:T(8,128)S(1)}, u32[]{:S(2)}, u32[]{:S(2)}) collective-permute-start(f32[4,72,512]{2,1,0:T(8,128)} %get-tuple-element.23.pressure), channel_id=1, source_target_pairs={{0,1},{1,0},{2,3},{3,2},{4,5},{5,4},{6,7},{7,6},{16,17},{17,16},{1... | collective-permute-start | bytes 1769480 | tf_op jit(solution)/shard_map/ppermute | solution.py:409
  11.1 14.4 %collective-permute-start.4 = (f32[4,72,512]{2,1,0:T(8,128)}, f32[4,72,512]{2,1,0:T(8,128)S(1)}, u32[]{:S(2)}, u32[]{:S(2)}) collective-permute-start(f32[4,72,512]{2,1,0:T(8,128)} %get-tuple-element.20.driven), channel_id=1, source_target_pairs={{0,1},{1,0},{2,3},{3,2},{4,5},{5,4},{6,7},{7,6},{16,17},{17,16},{1... | collective-permute-start | bytes 1769480 | tf_op jit(solution)/shard_map/ppermute | solution.py:409
  13.0 16.5 %collective-permute-start = (f32[136,256]{1,0:T(8,128)}, f32[136,256]{1,0:T(8,128)S(1)}, u32[]{:S(2)}, u32[]{:S(2)}) collective-permute-start(f32[136,256]{1,0:T(8,128)} %get-tuple-element.19.mine), channel_id=1, source_target_pairs={{0,8},{1,9},{2,10},{3,11},{4,12},{5,13},{6,14},{7,15},{8,16},{9,17... | collective-permute-start | bytes 417800 | tf_op jit(solution)/shard_map/ppermute | solution.py:409
  15.0 14.6 %collective-permute-start.1 = (f32[136,256]{1,0:T(8,128)}, f32[136,256]{1,0:T(8,128)S(1)}, u32[]{:S(2)}, u32[]{:S(2)}) collective-permute-start(f32[136,256]{1,0:T(8,128)} %get-tuple-element.19.mine), channel_id=1, source_target_pairs={{0,16},{1,17},{2,18},{3,19},{4,20},{5,21},{6,22},{7,23},{8,0},{9,1... | collective-permute-start | bytes 417800 | tf_op jit(solution)/shard_map/ppermute | solution.py:409
  19.9 4.3 %copy-start.8 = (f32[136,256]{1,0:T(8,128)S(1)}, f32[136,256]{1,0:T(8,128)}, u32[]{:S(2)}) copy-start(f32[136,256]{1,0:T(8,128)} %get-tuple-element.19.mine) | copy-start | bytes 417796
  19.9 33.8 %copy-start.12 = (f32[4,72,512]{2,1,0:T(8,128)S(1)}, f32[4,72,512]{2,1,0:T(8,128)}, u32[]{:S(2)}) copy-start(f32[4,72,512]{2,1,0:T(8,128)} %get-tuple-element.20.driven) | copy-start | bytes 1769476
  20.0 39.9 %collective-permute-start.7 = (f32[5,72,512]{2,1,0:T(8,128)S(1)}, f32[5,72,512]{2,1,0:T(8,128)S(1)}, u32[]{:S(2)}, u32[]{:S(2)}) collective-permute-start(f32[5,72,512]{2,1,0:T(8,128)S(1)} %maximum_select_fusion), channel_id=1, source_target_pairs={{0,2},{2,4},{3,1},{4,6},{5,3},{7,5},{16,18},{18,20},{19,17},{20,22... | collective-permute-start | bytes 2211848 | tf_op jit(solution)/shard_map/ppermute | solution.py:409
  24.2 8.1 %copy-start.1 = (f32[3,16384]{1,0:T(4,128)S(1)}, f32[3,16384]{1,0:T(4,128)}, u32[]{:S(2)}) copy-start(f32[3,16384]{1,0:T(4,128)} %vel.3) | copy-start | bytes 589828
  24.2 8.1 %copy-start.4 = (f32[3,16384]{1,0:T(4,128)S(1)}, f32[3,16384]{1,0:T(4,128)}, u32[]{:S(2)}) copy-start(f32[3,16384]{1,0:T(4,128)} %pos.1) | copy-start | bytes 589828
  25.5 34.4 %collective-permute-start.5 = (f32[4,72,512]{2,1,0:T(8,128)S(1)}, f32[4,72,512]{2,1,0:T(8,128)S(1)}, u32[]{:S(2)}, u32[]{:S(2)}) collective-permute-start(f32[4,72,512]{2,1,0:T(8,128)S(1)} %collective-permute-done.4.driven_near), channel_id=1, source_target_pairs={{0,2},{2,4},{3,1},{4,6},{5,3},{7,5},{16,18},{18,20},{19,17},{20,22... | collective-permute-start | bytes 1769480 | tf_op jit(solution)/shard_map/ppermute | solution.py:409
  29.6 22.8 %copy-start.13 = (f32[72,512]{1,0:T(8,128)S(1)}, f32[72,512]{1,0:T(8,128)}, u32[]{:S(2)}) copy-start(f32[72,512]{1,0:T(8,128)} %get-tuple-element.24) | copy-start | bytes 442372
  29.6 30.3 %collective-permute-start.2 = (f32[408,256]{1,0:T(8,128)S(1)}, f32[408,256]{1,0:T(8,128)S(1)}, u32[]{:S(2)}, u32[]{:S(2)}) collective-permute-start(f32[408,256]{1,0:T(8,128)S(1)} %constant_dynamic-update-slice_fusion), channel_id=1, source_target_pairs={{0,1},{1,0},{2,3},{3,2},{4,5},{5,4},{6,7},{7,6},{16,17},{17,16},{1... | collective-permute-start | bytes 1253384 | tf_op jit(solution)/shard_map/ppermute | solution.py:409
  31.6 28.3 %collective-permute-start.3 = (f32[408,256]{1,0:T(8,128)S(1)}, f32[408,256]{1,0:T(8,128)S(1)}, u32[]{:S(2)}, u32[]{:S(2)}) collective-permute-start(f32[408,256]{1,0:T(8,128)S(1)} %constant_dynamic-update-slice_fusion), channel_id=1, source_target_pairs={{1,2},{2,1},{3,4},{4,3},{5,6},{6,5},{17,18},{18,17},{19,20},{20,19... | collective-permute-start | bytes 1253384 | tf_op jit(solution)/shard_map/ppermute | solution.py:409
  37.2 8.6 %collective-permute-start.10 = (f32[96,128]{1,0:T(8,128)S(1)}, f32[96,128]{1,0:T(8,128)S(1)}, u32[]{:S(2)}, u32[]{:S(2)}) collective-permute-start(f32[96,128]{1,0:T(8,128)S(1)} %get-tuple-element.28), channel_id=1, source_target_pairs={{1,0},{2,1},{3,2},{4,3},{5,4},{6,5},{7,6},{9,8},{10,9},{11,10},{12... | collective-permute-start | bytes 147464 | tf_op jit(solution)/shard_map/ppermute | solution.py:409
  45.8 6.5 %collective-permute-start.9 = (f32[96,128]{1,0:T(8,128)S(1)}, f32[96,128]{1,0:T(8,128)S(1)}, u32[]{:S(2)}, u32[]{:S(2)}) collective-permute-start(f32[96,128]{1,0:T(8,128)S(1)} %get-tuple-element.27), channel_id=1, source_target_pairs={{0,1},{1,2},{2,3},{3,4},{4,5},{5,6},{6,7},{8,9},{9,10},{10,11},{11... | collective-permute-start | bytes 147464 | tf_op jit(solution)/shard_map/ppermute | solution.py:409
  52.4 7.6 %collective-permute-start.8 = (f32[72,512]{1,0:T(8,128)S(1)}, f32[72,512]{1,0:T(8,128)S(1)}, u32[]{:S(2)}, u32[]{:S(2)}) collective-permute-start(f32[72,512]{1,0:T(8,128)S(1)} %copy-done.13), channel_id=1, source_target_pairs={{1,3},{2,0},{3,5},{4,2},{5,7},{6,4},{17,19},{18,16},{19,21},{20,18... | collective-permute-start | bytes 442376 | tf_op jit(solution)/shard_map/ppermute | solution.py:409
  53.8 6.2 %copy-start = (f32[4,72,512]{2,1,0:T(8,128)S(1)}, f32[4,72,512]{2,1,0:T(8,128)}, u32[]{:S(2)}) copy-start(f32[4,72,512]{2,1,0:T(8,128)} %get-tuple-element.23.pressure) | copy-start | bytes 1769476
  60.0 16.5 %copy-start.2 = (s32[8,16384]{1,0:T(8,128)S(1)}, s32[8,16384]{1,0:T(8,128)}, u32[]{:S(2)}) copy-start(s32[8,16384]{1,0:T(8,128)} %named.1) | copy-start | bytes 1572868
  60.0 16.5 %copy-start.3 = (f32[8,16384]{1,0:T(8,128)S(1)}, f32[8,16384]{1,0:T(8,128)}, u32[]{:S(2)}) copy-start(f32[8,16384]{1,0:T(8,128)} %stiff.1) | copy-start | bytes 1572868
  71.1 9.6 %collective-permute-start.11 = (f32[128,384]{1,0:T(8,128)S(1)}, f32[128,384]{1,0:T(8,128)S(1)}, u32[]{:S(2)}, u32[]{:S(2)}) collective-permute-start(f32[128,384]{1,0:T(8,128)S(1)} %get-tuple-element.30), channel_id=1, source_target_pairs={{0,16},{1,17},{2,18},{3,19},{4,20},{5,21},{6,22},{7,23},{16,8},{17... | collective-permute-start | bytes 589832 | tf_op jit(solution)/shard_map/ppermute | solution.py:409
  74.5 7.6 %collective-permute-start.12 = (f32[128,384]{1,0:T(8,128)S(1)}, f32[128,384]{1,0:T(8,128)S(1)}, u32[]{:S(2)}, u32[]{:S(2)}) collective-permute-start(f32[128,384]{1,0:T(8,128)S(1)} %get-tuple-element.31), channel_id=1, source_target_pairs={{0,8},{1,9},{2,10},{3,11},{4,12},{5,13},{6,14},{7,15},{16,0},{17,1... | collective-permute-start | bytes 589832 | tf_op jit(solution)/shard_map/ppermute | solution.py:409
  76.4 5.6 %copy-start.5 = (s32[16384]{0:T(1024)S(1)}, s32[16384]{0:T(1024)}, u32[]{:S(2)}) copy-start(s32[16384]{0:T(1024)} %param.23) | copy-start | bytes 196612
  76.5 5.6 %copy-start.6 = (f32[16384]{0:T(1024)S(1)}, f32[16384]{0:T(1024)}, u32[]{:S(2)}) copy-start(f32[16384]{0:T(1024)} %param.16) | copy-start | bytes 196612
  76.5 5.6 %copy-start.7 = (f32[16384]{0:T(1024)S(1)}, f32[16384]{0:T(1024)}, u32[]{:S(2)}) copy-start(f32[16384]{0:T(1024)} %param.17) | copy-start | bytes 196612
  (3 other events, 6.2 us)

commit v5 on v4

--- a/solution.py
+++ b/solution.py
@@ -207,7 +207,14 @@
     return above, below, left, right
 
 
-def placed(groups, tiles):
+def inverse_of(value):
+    near = pl.reciprocal(value, approx=True)
+    return near * (2.0 - value * near)
+
+
+def placed(joined, tiles):
+    stride = tiles + SUB
+    groups = [joined.at[i * stride : (i + 1) * stride] for i in range(joined.shape[0] // stride)]
     parts = [halves_of(group[:tiles, :]) for group in groups]
     loads = jnp.concatenate([part[i] for i in range(2) for part in parts], 0)
     ids = jnp.concatenate([group[tiles : tiles + 1, :BLOCK] for group in groups], 1)
@@ -232,11 +239,11 @@
 
     def plane(x, carry):
         solid, drag = gathered(block + x * (full * zones))
-        porous = 1.0 / (1.0 + solid)
-        inverse = 1.0 / (6.0 * porous + drag + 1.0)
+        voids = 1.0 + solid
+        scale = inverse_of(6.0 + (drag + 1.0) * voids)
         if present is not None:
-            inverse = jnp.where(present, inverse, 0.0)
-        scale = porous * inverse
+            scale = jnp.where(present, scale, 0.0)
+        inverse = voids * scale
         for zone in range(zones):
             lanes = slice(zone * BLOCK, (zone + 1) * BLOCK)
             rows = slice(zone * height, (zone + 1) * height)
@@ -249,13 +256,12 @@
 
 
 def own_kernel(
-    full, own_rows, place, mine, second, third, driven, _, constant, factor, weight, rows_at
+    full, own_rows, place, joined, driven, _, constant, factor, weight, rows_at
 ):
-    stride = mine.shape[0]
-    tiles = stride - SUB
+    tiles = weight.shape[0]
     planes, height, width = driven.shape
     zones = width // BLOCK
-    ids, gathered = placed((mine, second, third), tiles)
+    ids, gathered = placed(joined, tiles)
     coefficients(gathered, tiles, place[0], full, driven, constant, factor, 0, None)
     turned = [
         jnp.transpose(
@@ -263,9 +269,15 @@
         ).astype(jnp.int32)
         for i in range(3)
     ]
-    solid, drag = gathered(jnp.concatenate([turned[0]] * 3, 1))
+
+    def before(places):
+        index = lax.rem(place[5] + 3 - places, 3)
+        return jnp.where(index == 0, turned[0], jnp.where(index == 1, turned[1], turned[2]))
+
+    solid, drag = gathered(jnp.concatenate([before(0)] * 3, 1))
     weight[...] = 1.0 / (1.0 / (1.0 + solid) + drag)
-    for i, block in enumerate(turned):
+    for i in range(3):
+        block = before(i)
         line, zone = block // zones, block % zones
         x, y = line // full, line % full
         row = (x * zones + zone) * height + y - place[0]
@@ -274,7 +286,7 @@
 
 def solve_kernel(
     full, sweeps, place, rows_at, joined_near, joined_far, driven_near, driven_far, pressure,
-    near, far, beyond, own_constant, own_factor, _lower, _upper, out_a, out_b, out_c,
+    near, far, beyond, own_constant, own_factor, out_a, out_b, out_c,
     constant, factor, old, new, fields,
 ):
     planes, height, width = pressure.shape
@@ -287,8 +299,7 @@
         (joined_near, driven_near, odd, jnp.where(odd, place[2], place[3])),
         (joined_far, driven_far, jnp.logical_not(odd), jnp.where(odd, place[3], place[2])),
     ):
-        groups = [joined.at[i * stride : (i + 1) * stride] for i in range(3)]
-        _, gathered = placed(groups, tiles)
+        _, gathered = placed(joined, tiles)
         coefficients(
             gathered, tiles, place[0], full, driven, constant, factor,
             jnp.where(below, 0, planes), present == 1,
@@ -399,7 +410,7 @@
     first = jnp.clip(half * own_rows - SUB, 0, full - height)
     odd = region % 2 == 1
     place = jnp.stack(
-        [first, odd, region > 0, region < regions - 1, jnp.where(group % CORES == 0, half, -1)]
+        [first, odd, region > 0, region < regions - 1, jnp.where(group % CORES == 0, half, -1), group]
     ).astype(jnp.int32)
     owners = range(0, groups, CORES)
     holders = range(holding)
@@ -440,12 +451,11 @@
         ],
         flops=2 * 32 * 48 * 65536, size=5 * 4 * slots, limit=61_500_000,
     )
-    second = along_grp(mine, 1, holders)
-    third = along_grp(mine, 2, holders)
+    gathered = lax.all_gather(mine, "grp")
+    joined = gathered[:holding].reshape(holding * (tiles + SUB), 2 * BLOCK)
     near = along_reg(pressure, owners, (1, -1))
     driven_near = along_reg(driven, owners, (1, -1))
     beyond = along_reg(ends, owners, (-2, 2))
-    joined = jnp.concatenate([mine, second, third], 0)
     joined_near = along_reg(joined, owners, (1, -1))
     joined_far = along_reg(joined, owners, (-1, 1))
     driven_far = along_reg(driven_near, owners, (2, -2))
@@ -471,17 +481,17 @@
             field, field, shaped(tiles, BLOCK),
             jax.ShapeDtypeStruct((3 * tiles, BLOCK), jnp.int32),
         ),
-        [SMEM] + [VMEM] * 4 + [ANY], (place, mine, second, third, driven, state),
+        [SMEM] + [VMEM] * 2 + [ANY], (place, joined, driven, state),
         flops=planes * height * 4 * 384 * 256 * 6, size=9 * field_bytes,
     )
 
     grads = shaped(tiles, 3 * BLOCK)
     window_of = lambda count: pltpu.VMEM((count, height, width), F32)
     grads_a, grads_b, grads_c = call(
-        functools.partial(solve_kernel, full, ITERS), (grads,) * 3, [SMEM] + [VMEM] * 11 + [ANY] * 2,
+        functools.partial(solve_kernel, full, ITERS), (grads,) * 3, [SMEM] + [VMEM] * 11,
         (
             place, rows_at, joined_near, joined_far, driven_near, driven_far, pressure, near, far,
-            beyond, constant, factor, lower, upper,
+            beyond, constant, factor,
         ),
         [
             window_of(2 * planes), window_of(2 * planes),

time: 83.6 us -> 85.4 us (1.022)
  the two profiles are of different devices: /device:TPU:0 before, /device:TPU:18 now
where the time goes in v5:
time: 85.4 us; the launch traced here: 85 us
  starting transfers between devices  33.3 us (39%)
  Pallas kernels  28.6 us (33%)
  waiting for transfers between devices  12.8 us (15%)
  blocking collectives  6.73 us (8%)
  local copies, waits for them, and re-layouts  1.45 us (2%)
  other arithmetic  1.07 us (1%)
  between operations  1.02 us (1%)
    ppermute x11, starting transfers between devices, send(): return lax.ppermute(value, ('grp', 'reg'), flat)  33.3 us
    pallas_call x6, Pallas kernels, call(): pl.pallas_call(kernel, out_shape=outs, in_specs=specs, out_specs=jax.tree...  28.6 us
    ppermute x11, waiting for transfers between devices, send(): return lax.ppermute(value, ('grp', 'reg'), flat)  12.8 us
    all_gather x1, blocking collectives, on_device(): gathered = lax.all_gather(mine, 'grp')  6.73 us
  transfers between devices with their start and end apart: 11, of which 3 were waited for; matrix products, arithmetic and copies ran while one was open for 1% of the time, Pallas kernels for 14%

profile of v5, /device:TPU:18, one launch (start us, length us, event | category | flops | bytes accessed | tf_op | source)
XLA Modules:
  0.0 85.0 jit_solution(14033891862579262689)
XLA Ops:
  0.7 0.7 stack.39.place
  1.3 5.0 %shard_map.136 = (f32[136,256]{1,0:T(8,128)}, f32[4,72,512]{2,1,0:T(8,128)}, f32[4,72,512]{2,1,0:T(8,128)}, f32[72,512]{1,0:T(8,128)}) custom-call(s32[1]{0:T(128)S(6)} %copy.15.count, s32[6]{0:T(128)} %stack.39.place, s32[128,128]{1,0:T(8,128)} %bitcast.10, f32[128,128]{1,0:T(8,128)} %bitcast.12, f32[128,128]{1,0:T(8,128)} %bitcast.14, s32[1,128]{1,0:T(1,128)} %bitcast.16, ...), custom_call_target="tpu_custom_call" | custom-call | flops 201326592 | bytes 327680 | tf_op jit(solution)/shard_map/pallas_call | solution.py:35
  6.3 3.4 %collective-permute-start.4 = (f32[4,72,512]{2,1,0:T(8,128)}, f32[4,72,512]{2,1,0:T(8,128)S(1)}, u32[]{:S(2)}, u32[]{:S(2)}) collective-permute-start(f32[4,72,512]{2,1,0:T(8,128)} %get-tuple-element.23.pressure), channel_id=1, source_target_pairs={{0,1},{1,0},{2,3},{3,2},{4,5},{5,4},{6,7},{7,6},{16,17},{17,16},{1... | collective-permute-start | bytes 1769480 | tf_op jit(solution)/shard_map/ppermute | solution.py:420
  9.7 2.4 %collective-permute-start.2 = (f32[4,72,512]{2,1,0:T(8,128)}, f32[4,72,512]{2,1,0:T(8,128)S(1)}, u32[]{:S(2)}, u32[]{:S(2)}) collective-permute-start(f32[4,72,512]{2,1,0:T(8,128)} %get-tuple-element.20.driven), channel_id=1, source_target_pairs={{0,1},{1,0},{2,3},{3,2},{4,5},{5,4},{6,7},{7,6},{16,17},{17,16},{1... | collective-permute-start | bytes 1769480 | tf_op jit(solution)/shard_map/ppermute | solution.py:420
  12.2 1.0 %slice_select_fusion = f32[1,72,512]{2,1,0:T(8,128)S(1)} fusion(f32[4,72,512]{2,1,0:T(8,128)} %get-tuple-element.23.pressure, pred[]{:T(512)S(6)} %eq.9), kind=kLoop, calls=%fused_computation.1 | loop fusion | flops 36864 | bytes 442369 | tf_op jit(solution)/shard_map/jit(_where)/select_n | solution.py:462
  13.2 5.1 %collective-permute-done.4.near = f32[4,72,512]{2,1,0:T(8,128)S(1)} collective-permute-done((f32[4,72,512]{2,1,0:T(8,128)}, f32[4,72,512]{2,1,0:T(8,128)S(1)}, u32[]{:S(2)}, u32[]{:S(2)}) %collective-permute-start.4) | collective-permute-done | bytes 589856 | tf_op jit(solution)/shard_map/ppermute | solution.py:420
  18.4 3.5 %collective-permute-start.5 = (f32[5,72,512]{2,1,0:T(8,128)S(1)}, f32[5,72,512]{2,1,0:T(8,128)S(1)}, u32[]{:S(2)}, u32[]{:S(2)}) collective-permute-start(f32[5,72,512]{2,1,0:T(8,128)S(1)} %maximum_select_fusion), channel_id=1, source_target_pairs={{0,2},{2,4},{3,1},{4,6},{5,3},{7,5},{16,18},{18,20},{19,17},{20,22... | collective-permute-start | bytes 2211848 | tf_op jit(solution)/shard_map/ppermute | solution.py:420
  21.9 2.8 %collective-permute-done.2.driven_near = f32[4,72,512]{2,1,0:T(8,128)S(1)} collective-permute-done((f32[4,72,512]{2,1,0:T(8,128)}, f32[4,72,512]{2,1,0:T(8,128)S(1)}, u32[]{:S(2)}, u32[]{:S(2)}) %collective-permute-start.2) | collective-permute-done | bytes 589856 | tf_op jit(solution)/shard_map/ppermute | solution.py:420
  24.6 3.5 %collective-permute-start.3 = (f32[4,72,512]{2,1,0:T(8,128)S(1)}, f32[4,72,512]{2,1,0:T(8,128)S(1)}, u32[]{:S(2)}, u32[]{:S(2)}) collective-permute-start(f32[4,72,512]{2,1,0:T(8,128)S(1)} %collective-permute-done.2.driven_near), channel_id=1, source_target_pairs={{0,2},{2,4},{3,1},{4,6},{5,3},{7,5},{16,18},{18,20},{19,17},{20,22... | collective-permute-start | bytes 1769480 | tf_op jit(solution)/shard_map/ppermute | solution.py:420
  28.1 6.7 %all-gather = f32[544,256]{1,0:T(8,128)S(1)} all-gather(f32[136,256]{1,0:T(8,128)S(1)} %copy-done.12), channel_id=2, replica_groups=mesh['grp'=4,'reg'=8] {'grp'}, dimensions={0}, use_global_device_ids=true | all-gather | bytes 696320 | tf_op jit(solution)/shard_map/all_gather | solution.py:454
  34.9 2.4 %collective-permute-start = (f32[408,256]{1,0:T(8,128)S(1)}, f32[408,256]{1,0:T(8,128)S(1)}, u32[]{:S(2)}, u32[]{:S(2)}) collective-permute-start(f32[408,256]{1,0:T(8,128)S(1)} %slice.13.joined), channel_id=1, source_target_pairs={{0,1},{1,0},{2,3},{3,2},{4,5},{5,4},{6,7},{7,6},{16,17},{17,16},{1... | collective-permute-start | bytes 1253384 | tf_op jit(solution)/shard_map/ppermute | solution.py:420
  37.3 3.4 %collective-permute-start.1 = (f32[408,256]{1,0:T(8,128)S(1)}, f32[408,256]{1,0:T(8,128)S(1)}, u32[]{:S(2)}, u32[]{:S(2)}) collective-permute-start(f32[408,256]{1,0:T(8,128)S(1)} %slice.13.joined), channel_id=1, source_target_pairs={{1,2},{2,1},{3,4},{4,3},{5,6},{6,5},{17,18},{18,17},{19,20},{20,19... | collective-permute-start | bytes 1253384 | tf_op jit(solution)/shard_map/ppermute | solution.py:420
  40.8 2.4 %collective-permute-start.6 = (f32[72,512]{1,0:T(8,128)S(1)}, f32[72,512]{1,0:T(8,128)S(1)}, u32[]{:S(2)}, u32[]{:S(2)}) collective-permute-start(f32[72,512]{1,0:T(8,128)S(1)} %copy-done.13), channel_id=1, source_target_pairs={{1,3},{2,0},{3,5},{4,2},{5,7},{6,4},{17,19},{18,16},{19,21},{20,18... | collective-permute-start | bytes 442376 | tf_op jit(solution)/shard_map/ppermute | solution.py:420
  43.2 4.8 %shard_map.137 = (f32[384,128]{1,0:T(8,128)S(1)}, f32[96,128]{1,0:T(8,128)S(1)}, f32[96,128]{1,0:T(8,128)S(1)}) custom-call(f32[3,16384]{1,0:T(4,128)S(1)} %copy-done.4, f32[3,16384]{1,0:T(4,128)S(1)} %copy-done.1, s32[2,4096]{1,0:T(2,128)S(1)} %copy-done.8), custom_call_target="tpu_custom_call" | custom-call | flops 50331648 | bytes 786432 | tf_op jit(solution)/shard_map/pallas_call | solution.py:35
  48.1 0.7 copy-done.9
  48.7 2.6 %shard_map.138 = (f32[4,72,512]{2,1,0:T(8,128)S(1)}, f32[4,72,512]{2,1,0:T(8,128)S(1)}, f32[128,128]{1,0:T(8,128)S(1)}, s32[384,128]{1,0:T(8,128)S(1)}) custom-call(s32[6]{0:T(128)S(1)} %copy-done.9, f32[408,256]{1,0:T(8,128)S(1)} %slice.13.joined, f32[4,72,512]{2,1,0:T(8,128)S(1)} %copy-done.11, f32[384,128]{1,0:T(8,128)S(1)} %get-tuple-element.21._.state), custom_call_target="tpu_custom_call" | custom-call | flops 679477248 | bytes 5308416 | tf_op jit(solution)/shard_map/pallas_call | solution.py:35
  51.4 11.1 %shard_map.139 = (f32[128,384]{1,0:T(8,128)S(1)}, f32[128,384]{1,0:T(8,128)S(1)}, f32[128,384]{1,0:T(8,128)S(1)}) custom-call(s32[6]{0:T(128)S(1)} %copy-done.9, s32[384,128]{1,0:T(8,128)S(1)} %get-tuple-element.22.rows_at, f32[408,256]{1,0:T(8,128)S(1)} %collective-permute-done.joined_near, f32[408,256]{1,0:T(8,128)S(1)} %collective-permute-done.1.joined_far, ...), custom_call_target="tpu_custom_call" | custom-call | flops 1358954496 | bytes 11796480 | tf_op jit(solution)/shard_map/pallas_call | solution.py:35
  62.5 1.9 %collective-permute-start.7 = (f32[128,384]{1,0:T(8,128)S(1)}, f32[128,384]{1,0:T(8,128)S(1)}, u32[]{:S(2)}, u32[]{:S(2)}) collective-permute-start(f32[128,384]{1,0:T(8,128)S(1)} %get-tuple-element.28), channel_id=1, source_target_pairs={{0,16},{1,17},{2,18},{3,19},{4,20},{5,21},{6,22},{7,23},{16,8},{17... | collective-permute-start | bytes 589832 | tf_op jit(solution)/shard_map/ppermute | solution.py:420
  64.4 3.9 %collective-permute-start.8 = (f32[128,384]{1,0:T(8,128)S(1)}, f32[128,384]{1,0:T(8,128)S(1)}, u32[]{:S(2)}, u32[]{:S(2)}) collective-permute-start(f32[128,384]{1,0:T(8,128)S(1)} %get-tuple-element.29), channel_id=1, source_target_pairs={{0,8},{1,9},{2,10},{3,11},{4,12},{5,13},{6,14},{7,15},{16,0},{17,1... | collective-permute-start | bytes 589832 | tf_op jit(solution)/shard_map/ppermute | solution.py:420
  68.3 4.4 %collective-permute-start.10 = (f32[96,128]{1,0:T(8,128)S(1)}, f32[96,128]{1,0:T(8,128)S(1)}, u32[]{:S(2)}, u32[]{:S(2)}) collective-permute-start(f32[96,128]{1,0:T(8,128)S(1)} %get-tuple-element.32), channel_id=1, source_target_pairs={{1,0},{2,1},{3,2},{4,3},{5,4},{6,5},{7,6},{9,8},{10,9},{11,10},{12... | collective-permute-start | bytes 147464 | tf_op jit(solution)/shard_map/ppermute | solution.py:420
  72.8 1.9 %collective-permute-start.9 = (f32[96,128]{1,0:T(8,128)S(1)}, f32[96,128]{1,0:T(8,128)S(1)}, u32[]{:S(2)}, u32[]{:S(2)}) collective-permute-start(f32[96,128]{1,0:T(8,128)S(1)} %get-tuple-element.31), channel_id=1, source_target_pairs={{0,1},{1,2},{2,3},{3,4},{4,5},{5,6},{6,7},{8,9},{9,10},{10,11},{11... | collective-permute-start | bytes 147464 | tf_op jit(solution)/shard_map/ppermute | solution.py:420
  74.7 4.9 %collective-permute-done.9.lower = f32[96,128]{1,0:T(8,128)S(1)} collective-permute-done((f32[96,128]{1,0:T(8,128)S(1)}, f32[96,128]{1,0:T(8,128)S(1)}, u32[]{:S(2)}, u32[]{:S(2)}) %collective-permute-start.9) | collective-permute-done | bytes 49184 | tf_op jit(solution)/shard_map/ppermute | solution.py:420
  79.7 4.2 %shard_map.140.contact = f32[384,128]{1,0:T(8,128)S(1)} custom-call(s32[128]{0:T(128)S(1)} %copy-done.10, f32[384,128]{1,0:T(8,128)S(1)} %get-tuple-element.21._.state, f32[96,128]{1,0:T(8,128)S(1)} %collective-permute-done.9.lower, f32[96,128]{1,0:T(8,128)S(1)} %collective-permute-done.10.upper, s32[8,16384]{1,0:T(8,128)S(1)} %copy-done.2, ...), custom_call_target="tpu_custom_call" | custom-call | flops 7864320 | bytes 1310720 | tf_op jit(solution)/shard_map/pallas_call | solution.py:35
  84.0 1.0 %shard_map.141 = f32[3,16384]{1,0:T(4,128)} custom-call(s32[1]{0:T(128)S(6)} %copy.15.count, f32[128,384]{1,0:T(8,128)S(1)} %get-tuple-element.27._.grads_a, f32[128,384]{1,0:T(8,128)S(1)} %collective-permute-done.7.grads_b, f32[128,384]{1,0:T(8,128)S(1)} %collective-permute-done.8.grads_c, f32[128,128]{1,0:T(8,128)S(1)} %get-tuple-element.30.weight, ...), custom_call_target="tpu_custom_call" | custom-call | flops 983040 | bytes 1310720 | tf_op jit(solution)/shard_map/pallas_call | solution.py:35
  (37 shorter events, 0.2 us)
Async XLA Ops:
  6.3 12.0 %collective-permute-start.4 = (f32[4,72,512]{2,1,0:T(8,128)}, f32[4,72,512]{2,1,0:T(8,128)S(1)}, u32[]{:S(2)}, u32[]{:S(2)}) collective-permute-start(f32[4,72,512]{2,1,0:T(8,128)} %get-tuple-element.23.pressure), channel_id=1, source_target_pairs={{0,1},{1,0},{2,3},{3,2},{4,5},{5,4},{6,7},{7,6},{16,17},{17,16},{1... | collective-permute-start | bytes 1769480 | tf_op jit(solution)/shard_map/ppermute | solution.py:420
  9.7 14.9 %collective-permute-start.2 = (f32[4,72,512]{2,1,0:T(8,128)}, f32[4,72,512]{2,1,0:T(8,128)S(1)}, u32[]{:S(2)}, u32[]{:S(2)}) collective-permute-start(f32[4,72,512]{2,1,0:T(8,128)} %get-tuple-element.20.driven), channel_id=1, source_target_pairs={{0,1},{1,0},{2,3},{3,2},{4,5},{5,4},{6,7},{7,6},{16,17},{17,16},{1... | collective-permute-start | bytes 1769480 | tf_op jit(solution)/shard_map/ppermute | solution.py:420
  13.2 14.9 %copy-start.12 = (f32[136,256]{1,0:T(8,128)S(1)}, f32[136,256]{1,0:T(8,128)}, u32[]{:S(2)}) copy-start(f32[136,256]{1,0:T(8,128)} %get-tuple-element.19) | copy-start | bytes 417796
  18.4 33.0 %collective-permute-start.5 = (f32[5,72,512]{2,1,0:T(8,128)S(1)}, f32[5,72,512]{2,1,0:T(8,128)S(1)}, u32[]{:S(2)}, u32[]{:S(2)}) collective-permute-start(f32[5,72,512]{2,1,0:T(8,128)S(1)} %maximum_select_fusion), channel_id=1, source_target_pairs={{0,2},{2,4},{3,1},{4,6},{5,3},{7,5},{16,18},{18,20},{19,17},{20,22... | collective-permute-start | bytes 2211848 | tf_op jit(solution)/shard_map/ppermute | solution.py:420
  24.6 26.7 %collective-permute-start.3 = (f32[4,72,512]{2,1,0:T(8,128)S(1)}, f32[4,72,512]{2,1,0:T(8,128)S(1)}, u32[]{:S(2)}, u32[]{:S(2)}) collective-permute-start(f32[4,72,512]{2,1,0:T(8,128)S(1)} %collective-permute-done.2.driven_near), channel_id=1, source_target_pairs={{0,2},{2,4},{3,1},{4,6},{5,3},{7,5},{16,18},{18,20},{19,17},{20,22... | collective-permute-start | bytes 1769480 | tf_op jit(solution)/shard_map/ppermute | solution.py:420
  28.1 12.7 %copy-start.13 = (f32[72,512]{1,0:T(8,128)S(1)}, f32[72,512]{1,0:T(8,128)}, u32[]{:S(2)}) copy-start(f32[72,512]{1,0:T(8,128)} %get-tuple-element.24) | copy-start | bytes 442372
  34.8 8.3 %copy-start.1 = (f32[3,16384]{1,0:T(4,128)S(1)}, f32[3,16384]{1,0:T(4,128)}, u32[]{:S(2)}) copy-start(f32[3,16384]{1,0:T(4,128)} %vel.3) | copy-start | bytes 589828
  34.8 8.3 %copy-start.4 = (f32[3,16384]{1,0:T(4,128)S(1)}, f32[3,16384]{1,0:T(4,128)}, u32[]{:S(2)}) copy-start(f32[3,16384]{1,0:T(4,128)} %pos.1) | copy-start | bytes 589828
  34.9 8.3 %copy-start.8 = (s32[2,4096]{1,0:T(2,128)S(1)}, s32[2,4096]{1,0:T(2,128)}, u32[]{:S(2)}) copy-start(s32[2,4096]{1,0:T(2,128)} %lists.1) | copy-start | bytes 98308
  34.9 13.2 %copy-start.11 = (f32[4,72,512]{2,1,0:T(8,128)S(1)}, f32[4,72,512]{2,1,0:T(8,128)}, u32[]{:S(2)}) copy-start(f32[4,72,512]{2,1,0:T(8,128)} %get-tuple-element.20.driven) | copy-start | bytes 1769476
  34.9 16.4 %collective-permute-start = (f32[408,256]{1,0:T(8,128)S(1)}, f32[408,256]{1,0:T(8,128)S(1)}, u32[]{:S(2)}, u32[]{:S(2)}) collective-permute-start(f32[408,256]{1,0:T(8,128)S(1)} %slice.13.joined), channel_id=1, source_target_pairs={{0,1},{1,0},{2,3},{3,2},{4,5},{5,4},{6,7},{7,6},{16,17},{17,16},{1... | collective-permute-start | bytes 1253384 | tf_op jit(solution)/shard_map/ppermute | solution.py:420
  37.3 14.0 %collective-permute-start.1 = (f32[408,256]{1,0:T(8,128)S(1)}, f32[408,256]{1,0:T(8,128)S(1)}, u32[]{:S(2)}, u32[]{:S(2)}) collective-permute-start(f32[408,256]{1,0:T(8,128)S(1)} %slice.13.joined), channel_id=1, source_target_pairs={{1,2},{2,1},{3,4},{4,3},{5,6},{6,5},{17,18},{18,17},{19,20},{20,19... | collective-permute-start | bytes 1253384 | tf_op jit(solution)/shard_map/ppermute | solution.py:420
  40.8 10.5 %collective-permute-start.6 = (f32[72,512]{1,0:T(8,128)S(1)}, f32[72,512]{1,0:T(8,128)S(1)}, u32[]{:S(2)}, u32[]{:S(2)}) collective-permute-start(f32[72,512]{1,0:T(8,128)S(1)} %copy-done.13), channel_id=1, source_target_pairs={{1,3},{2,0},{3,5},{4,2},{5,7},{6,4},{17,19},{18,16},{19,21},{20,18... | collective-permute-start | bytes 442376 | tf_op jit(solution)/shard_map/ppermute | solution.py:420
  48.7 2.6 %copy-start = (f32[4,72,512]{2,1,0:T(8,128)S(1)}, f32[4,72,512]{2,1,0:T(8,128)}, u32[]{:S(2)}) copy-start(f32[4,72,512]{2,1,0:T(8,128)} %get-tuple-element.23.pressure) | copy-start | bytes 1769476
  51.4 28.3 %copy-start.2 = (s32[8,16384]{1,0:T(8,128)S(1)}, s32[8,16384]{1,0:T(8,128)}, u32[]{:S(2)}) copy-start(s32[8,16384]{1,0:T(8,128)} %named.1) | copy-start | bytes 1572868
  51.4 28.3 %copy-start.3 = (f32[8,16384]{1,0:T(8,128)S(1)}, f32[8,16384]{1,0:T(8,128)}, u32[]{:S(2)}) copy-start(f32[8,16384]{1,0:T(8,128)} %stiff.1) | copy-start | bytes 1572868
  62.5 21.5 %collective-permute-start.7 = (f32[128,384]{1,0:T(8,128)S(1)}, f32[128,384]{1,0:T(8,128)S(1)}, u32[]{:S(2)}, u32[]{:S(2)}) collective-permute-start(f32[128,384]{1,0:T(8,128)S(1)} %get-tuple-element.28), channel_id=1, source_target_pairs={{0,16},{1,17},{2,18},{3,19},{4,20},{5,21},{6,22},{7,23},{16,8},{17... | collective-permute-start | bytes 589832 | tf_op jit(solution)/shard_map/ppermute | solution.py:420
  64.4 19.6 %collective-permute-start.8 = (f32[128,384]{1,0:T(8,128)S(1)}, f32[128,384]{1,0:T(8,128)S(1)}, u32[]{:S(2)}, u32[]{:S(2)}) collective-permute-start(f32[128,384]{1,0:T(8,128)S(1)} %get-tuple-element.29), channel_id=1, source_target_pairs={{0,8},{1,9},{2,10},{3,11},{4,12},{5,13},{6,14},{7,15},{16,0},{17,1... | collective-permute-start | bytes 589832 | tf_op jit(solution)/shard_map/ppermute | solution.py:420
  68.3 6.4 %collective-permute-start.10 = (f32[96,128]{1,0:T(8,128)S(1)}, f32[96,128]{1,0:T(8,128)S(1)}, u32[]{:S(2)}, u32[]{:S(2)}) collective-permute-start(f32[96,128]{1,0:T(8,128)S(1)} %get-tuple-element.32), channel_id=1, source_target_pairs={{1,0},{2,1},{3,2},{4,3},{5,4},{6,5},{7,6},{9,8},{10,9},{11,10},{12... | collective-permute-start | bytes 147464 | tf_op jit(solution)/shard_map/ppermute | solution.py:420
  72.8 6.9 %copy-start.10 = (s32[128]{0:T(128)S(1)}, s32[128]{0:T(128)}, u32[]{:S(2)}) copy-start(s32[128]{0:T(128)} %partner.1) | copy-start | bytes 1540
  72.8 6.9 %collective-permute-start.9 = (f32[96,128]{1,0:T(8,128)S(1)}, f32[96,128]{1,0:T(8,128)S(1)}, u32[]{:S(2)}, u32[]{:S(2)}) collective-permute-start(f32[96,128]{1,0:T(8,128)S(1)} %get-tuple-element.31), channel_id=1, source_target_pairs={{0,1},{1,2},{2,3},{3,4},{4,5},{5,6},{6,7},{8,9},{9,10},{10,11},{11... | collective-permute-start | bytes 147464 | tf_op jit(solution)/shard_map/ppermute | solution.py:420
  79.7 4.3 %copy-start.5 = (s32[16384]{0:T(1024)S(1)}, s32[16384]{0:T(1024)}, u32[]{:S(2)}) copy-start(s32[16384]{0:T(1024)} %param.23) | copy-start | bytes 196612
  79.7 4.3 %copy-start.6 = (f32[16384]{0:T(1024)S(1)}, f32[16384]{0:T(1024)}, u32[]{:S(2)}) copy-start(f32[16384]{0:T(1024)} %param.16) | copy-start | bytes 196612
  79.7 4.3 %copy-start.7 = (f32[16384]{0:T(1024)S(1)}, f32[16384]{0:T(1024)}, u32[]{:S(2)}) copy-start(f32[16384]{0:T(1024)} %param.17) | copy-start | bytes 196612
  (1 other events, 0.7 us)

commit v6 on v5

--- a/solution.py
+++ b/solution.py
@@ -52,25 +52,32 @@
     return high, (value - high.astype(F32)).astype(BF16)
 
 
-def entry_kernel(
-    count, place, cell_at, vol_at, drag_at, ids, pressure_old, source, solid_before,
-    out, pressure, driven, ends, solid, cell, vol, drag, sems,
-):
-    tiles = cell.shape[0]
-    planes, height, _ = pressure.shape
+def window_kernel(place, pressure_old, source, solid_before, window, ends, inner, solid, sems):
+    planes, height, _ = solid.shape
     rows = pl.ds(pl.multiple_of(place[0], SUB), height)
-    moves = [(cell_at, cell), (vol_at, vol), (drag_at, drag)] + [
-        (whole.at[:, rows, :], part)
-        for whole, part in ((pressure_old, pressure), (source, driven), (solid_before, solid))
-    ]
+    moves = ((pressure_old, window.at[:planes]), (source, window.at[planes:]), (solid_before, solid))
     copies = [
-        pltpu.make_async_copy(whole, part, sems.at[index])
+        pltpu.make_async_copy(whole.at[:, rows, :], part, sems.at[index])
         for index, (whole, part) in enumerate(moves)
     ]
     for copy in copies:
         copy.start()
-    for copy in copies[:3]:
+    for copy in copies:
         copy.wait()
+    window[planes:] = window[planes:] - solid[...]
+    odd = place[1]
+    ends[...] = window[odd * (planes - 1)]
+    inner[...] = window[(1 - odd) * (planes - 1)]
+
+
+def forward_kernel(near, inner, _joined, _beyond, out):
+    count = near.shape[0]
+    out[:count] = near[...]
+    out[count] = inner[...]
+
+
+def deposit_kernel(count, cell, vol, drag, ids, _, out):
+    tiles = cell.shape[0]
     sub = iota((SUB, BLOCK), 0)
     rows_c = iota((BLOCK, BLOCK), 0)
     even = sub % 2 == 0
@@ -111,20 +118,9 @@
         out[pl.ds(first, SUB), BLOCK:] = sums[1]
         return carry
 
-    lax.fori_loop(0, tiles // SUB, step, 0, unroll=2)
+    lax.fori_loop(0, tiles // SUB, step, 0, unroll=4)
     out[tiles : tiles + SUB, :BLOCK] = jnp.broadcast_to(ids[...].astype(F32), (SUB, BLOCK))
     out[tiles : tiles + SUB, BLOCK:] = jnp.zeros((SUB, BLOCK), F32)
-    for copy in copies[3:]:
-        copy.wait()
-    driven[...] = driven[...] - solid[...]
-
-    @pl.when(place[1] == 1)
-    def _():
-        ends[...] = pressure[planes - 1]
-
-    @pl.when(place[1] != 1)
-    def _():
-        ends[...] = pressure[0]
 
 
 def halo_kernel(pos, vel, lists, state, down, up):
@@ -163,7 +159,7 @@
                     ]
             return carry
 
-        lax.fori_loop(0, rows // 2, step, 0, unroll=2)
+        lax.fori_loop(0, rows // 2, step, 0, unroll=4)
 
 
 def contact_kernel(partner, state, lower, upper, named, stiff, _, out, extended):
@@ -230,14 +226,14 @@
     return ids, gathered
 
 
-def coefficients(gathered, tiles, first, full, driven, constant, factor, base, present):
-    planes, height, width = driven.shape
+def coefficients(gathered, tiles, first, full, driven, planes, constant, factor, base, present):
+    _, height, width = driven.shape
     zones = width // BLOCK
     shape = (zones * height, 3 * tiles)
     line = iota(shape, 0)
     block = (line % height) * zones + line // height + first * zones
 
-    def plane(x, carry):
+    for x in range(planes):
         solid, drag = gathered(block + x * (full * zones))
         voids = 1.0 + solid
         scale = inverse_of(6.0 + (drag + 1.0) * voids)
@@ -247,22 +243,17 @@
         for zone in range(zones):
             lanes = slice(zone * BLOCK, (zone + 1) * BLOCK)
             rows = slice(zone * height, (zone + 1) * height)
-            driving = driven[x, :, lanes] + solid[rows]
+            driving = driven[planes + x, :, lanes] + solid[rows]
             constant[base + x, :, lanes] = driving * inverse[rows]
             factor[base + x, :, lanes] = scale[rows]
-        return carry
-
-    lax.fori_loop(0, planes, plane, 0)
-
-
-def own_kernel(
-    full, own_rows, place, joined, driven, _, constant, factor, weight, rows_at
-):
+
+
+def own_kernel(full, own_rows, place, joined, window, _, constant, factor, weight, rows_at):
     tiles = weight.shape[0]
-    planes, height, width = driven.shape
+    planes, height, width = constant.shape
     zones = width // BLOCK
     ids, gathered = placed(joined, tiles)
-    coefficients(gathered, tiles, place[0], full, driven, constant, factor, 0, None)
+    coefficients(gathered, tiles, place[0], full, window, planes, constant, factor, 0, None)
     turned = [
         jnp.transpose(
             jnp.broadcast_to(ids[:, i * tiles : (i + 1) * tiles], (BLOCK, tiles)).astype(F32)
@@ -285,29 +276,29 @@
 
 
 def solve_kernel(
-    full, sweeps, place, rows_at, joined_near, joined_far, driven_near, driven_far, pressure,
-    near, far, beyond, own_constant, own_factor, out_a, out_b, out_c,
+    full, sweeps, place, rows_at, joined_near, joined_far, window, near, far, beyond,
+    own_constant, own_factor, _lower, _upper, out_a, out_b, out_c,
     constant, factor, old, new, fields,
 ):
-    planes, height, width = pressure.shape
+    planes, height, width = own_constant.shape
     zones = width // BLOCK
-    stride = joined_near.shape[0] // 3
-    tiles = stride - SUB
-    odd, lower, upper = place[1] == 1, place[2] == 1, place[3] == 1
+    tiles = joined_near.shape[0] // 3 - SUB
+    odd = place[1] == 1
     rim = sweeps + 1
     for joined, driven, below, present in (
-        (joined_near, driven_near, odd, jnp.where(odd, place[2], place[3])),
-        (joined_far, driven_far, jnp.logical_not(odd), jnp.where(odd, place[3], place[2])),
+        (joined_near, near, odd, jnp.where(odd, place[2], place[3])),
+        (joined_far, far, jnp.logical_not(odd), jnp.where(odd, place[3], place[2])),
     ):
         _, gathered = placed(joined, tiles)
         coefficients(
-            gathered, tiles, place[0], full, driven, constant, factor,
+            gathered, tiles, place[0], full, driven, planes, constant, factor,
             jnp.where(below, 0, planes), present == 1,
         )
-    old[pl.ds(jnp.where(odd, 1, rim + planes), planes)] = near[...]
-    old[pl.ds(jnp.where(odd, rim + planes, 0), planes + 1)] = far[...]
+    old[pl.ds(jnp.where(odd, 1, rim + planes), planes)] = near[:planes]
+    old[pl.ds(jnp.where(odd, rim + planes, 1), planes)] = far[:planes]
+    old[pl.ds(jnp.where(odd, rim + 2 * planes, 0), 1)] = far[2 * planes :]
     old[pl.ds(jnp.where(odd, 0, rim + 2 * planes), 1)] = beyond[...][None]
-    old[rim : rim + planes] = pressure[...]
+    old[rim : rim + planes] = window[:planes]
 
     def sweep(source, target, depth):
         def over(constants, factors, shift):
@@ -320,10 +311,10 @@
 
             return plane
 
-        lax.fori_loop(depth, rim, over(constant, factor, 1), 0)
-        lax.fori_loop(rim, rim + planes, over(own_constant, own_factor, rim), 0)
+        lax.fori_loop(depth, rim, over(constant, factor, 1), 0, unroll=2)
+        lax.fori_loop(rim, rim + planes, over(own_constant, own_factor, rim), 0, unroll=2)
         lax.fori_loop(
-            rim + planes, 3 * planes + 2 - depth, over(constant, factor, 1 + planes), 0
+            rim + planes, 3 * planes + 2 - depth, over(constant, factor, 1 + planes), 0, unroll=2
         )
 
     for index in range(sweeps):
@@ -343,15 +334,12 @@
                 )
         return carry
 
-    lax.fori_loop(0, planes, gradient, 0)
-    span = 3 * BLOCK
-    wanted = jnp.concatenate([rows_at[...]] * 3, 1)
-    column = iota(wanted.shape, 1)
-    total = jnp.zeros((3 * tiles, span), F32)
-    for part in range(planes * zones * height // span):
-        hot = jnp.where(wanted == column + part * span, 1.0, 0.0).astype(BF16)
-        for piece in halves_of(fields[part * span : (part + 1) * span, :]):
-            total = total + jnp.dot(hot, piece, preferred_element_type=F32)
+    lax.fori_loop(0, planes, gradient, 0, unroll=2)
+    wanted = jnp.concatenate([rows_at[...]] * (planes * zones * height // BLOCK), 1)
+    hot = jnp.where(wanted == iota(wanted.shape, 1), 1.0, 0.0).astype(BF16)
+    pieces = jnp.concatenate(halves_of(fields[...]), 1)
+    total = jnp.dot(hot, pieces, preferred_element_type=F32)
+    total = total[:, : 3 * BLOCK] + total[:, 3 * BLOCK :]
     for index, out in enumerate((out_a, out_b, out_c)):
         out[...] = total[index * tiles : (index + 1) * tiles]
 
@@ -440,29 +428,28 @@
     field_bytes = 4 * planes * height * width
 
     field = shaped(planes, height, width)
-    mine, pressure, driven, ends = call(
-        entry_kernel, (shaped(tiles + SUB, 2 * BLOCK), field, field, shaped(height, width)),
-        [SMEM] * 2 + [HBM] * 3 + [VMEM] + [HBM] * 3,
-        (count, place, cell, vol, drag, ids, pressure_old, pressure_source, solid_old),
-        [
-            pltpu.VMEM((planes, height, width), F32), pltpu.VMEM((tiles, BLOCK), jnp.int32),
-            pltpu.VMEM((tiles, BLOCK), F32), pltpu.VMEM((tiles, BLOCK), F32),
-            pltpu.SemaphoreType.DMA((6,)),
-        ],
-        flops=2 * 32 * 48 * 65536, size=5 * 4 * slots, limit=61_500_000,
-    )
-    gathered = lax.all_gather(mine, "grp")
-    joined = gathered[:holding].reshape(holding * (tiles + SUB), 2 * BLOCK)
-    near = along_reg(pressure, owners, (1, -1))
-    driven_near = along_reg(driven, owners, (1, -1))
-    beyond = along_reg(ends, owners, (-2, 2))
+    plane = shaped(height, width)
+    window, ends, inner = call(
+        window_kernel, (shaped(2 * planes, height, width), plane, plane), [SMEM] + [HBM] * 3,
+        (place, pressure_old, pressure_source, solid_old),
+        [pltpu.VMEM((planes, height, width), F32), pltpu.SemaphoreType.DMA((3,))],
+        flops=field_bytes, size=6 * field_bytes, limit=61_500_000,
+    )
+    near = along_reg(window, owners, (1, -1))
+    mine = call(
+        deposit_kernel, shaped(tiles + SUB, 2 * BLOCK), [SMEM] + [VMEM] * 4 + [ANY],
+        (count, cell, vol, drag, ids, ends), flops=2 * 32 * 48 * 65536, size=5 * 4 * slots,
+    )
+    joined = lax.all_gather(mine, "grp")
+    joined = joined[:holding].reshape(holding * (tiles + SUB), 2 * BLOCK)
     joined_near = along_reg(joined, owners, (1, -1))
     joined_far = along_reg(joined, owners, (-1, 1))
-    driven_far = along_reg(driven_near, owners, (2, -2))
-    inner = jnp.where(odd, pressure[:1], pressure[planes - 1 :])
+    beyond = along_reg(ends, owners, (-2, 2))
     far = along_reg(
-        jnp.where(
-            odd, jnp.concatenate([near, inner], 0), jnp.concatenate([inner, near], 0)
+        call(
+            forward_kernel, shaped(2 * planes + 1, height, width), [VMEM] * 2 + [ANY] * 2,
+            (near, inner, joined, beyond),
+            size=5 * field_bytes,
         ),
         owners, (2, -2),
     )
@@ -481,17 +468,18 @@
             field, field, shaped(tiles, BLOCK),
             jax.ShapeDtypeStruct((3 * tiles, BLOCK), jnp.int32),
         ),
-        [SMEM] + [VMEM] * 2 + [ANY], (place, joined, driven, state),
+        [SMEM] + [VMEM] * 2 + [ANY], (place, joined, window, state),
         flops=planes * height * 4 * 384 * 256 * 6, size=9 * field_bytes,
     )
 
     grads = shaped(tiles, 3 * BLOCK)
     window_of = lambda count: pltpu.VMEM((count, height, width), F32)
     grads_a, grads_b, grads_c = call(
-        functools.partial(solve_kernel, full, ITERS), (grads,) * 3, [SMEM] + [VMEM] * 11,
+        functools.partial(solve_kernel, full, ITERS), (grads,) * 3,
+        [SMEM] + [VMEM] * 9 + [ANY] * 2,
         (
-            place, rows_at, joined_near, joined_far, driven_near, driven_far, pressure, near, far,
-            beyond, constant, factor,
+            place, rows_at, joined_near, joined_far, window, near, far, beyond, constant, factor,
+            lower, upper,
         ),
         [
             window_of(2 * planes), window_of(2 * planes),

time: 85.4 us -> 67.1 us (0.79)
  the two profiles are of different devices: /device:TPU:18 before, /device:TPU:0 now
where the time goes in v6:
time: 67.1 us; the launch traced here: 66.7 us
  starting transfers between devices  26.2 us (39%)
  Pallas kernels  23.9 us (36%)
  blocking collectives  7.35 us (11%)
  waiting for transfers between devices  6.6 us (10%)
  local copies, waits for them, and re-layouts  1.62 us (2%)
  between operations  0.97 us (1%)
    ppermute x9, starting transfers between devices, send(): return lax.ppermute(value, ('grp', 'reg'), flat)  26.2 us
    pallas_call x8, Pallas kernels, call(): pl.pallas_call(kernel, out_shape=outs, in_specs=specs, out_specs=jax.tree...  23.9 us
    all_gather x1, blocking collectives, on_device(): joined = lax.all_gather(mine, 'grp')  7.35 us
    ppermute x9, waiting for transfers between devices, send(): return lax.ppermute(value, ('grp', 'reg'), flat)  6.6 us
  transfers between devices with their start and end apart: 9, of which 3 were waited for; matrix products, arithmetic and copies ran while one was open for 0% of the time, Pallas kernels for 17%

profile of v6, /device:TPU:0, one launch (start us, length us, event | category | flops | bytes accessed | tf_op | source)
XLA Modules:
  0.0 66.7 jit_solution(1567195418855660470)
XLA Ops:
  0.0 0.6 stack.39.place
  0.6 3.4 %shard_map.136 = (f32[8,72,512]{2,1,0:T(8,128)}, f32[72,512]{1,0:T(8,128)}, f32[72,512]{1,0:T(8,128)}) custom-call(s32[6]{0:T(128)} %stack.39.place, f32[4,128,512]{2,1,0:T(8,128)} %pressure_old.1, f32[4,128,512]{2,1,0:T(8,128)} %source.1, f32[4,128,512]{2,1,0:T(8,128)} %solid_before.1), custom_call_target="tpu_custom_call" | custom-call | flops 589824 | bytes 3538944 | tf_op jit(solution)/shard_map/pallas_call | solution.py:35
  4.1 5.0 %collective-permute-start.2 = (f32[8,72,512]{2,1,0:T(8,128)}, f32[8,72,512]{2,1,0:T(8,128)S(1)}, u32[]{:S(2)}, u32[]{:S(2)}) collective-permute-start(f32[8,72,512]{2,1,0:T(8,128)} %get-tuple-element.19.window), channel_id=1, source_target_pairs={{0,1},{1,0},{2,3},{3,2},{4,5},{5,4},{6,7},{7,6},{16,17},{17,16},{1... | collective-permute-start | bytes 3538952 | tf_op jit(solution)/shard_map/ppermute | solution.py:408
  9.1 1.3 %collective-permute-start.3 = (f32[72,512]{1,0:T(8,128)}, f32[72,512]{1,0:T(8,128)S(1)}, u32[]{:S(2)}, u32[]{:S(2)}) collective-permute-start(f32[72,512]{1,0:T(8,128)} %get-tuple-element.18._), channel_id=1, source_target_pairs={{1,3},{2,0},{3,5},{4,2},{5,7},{6,4},{17,19},{18,16},{19,21},{20,18... | collective-permute-start | bytes 442376 | tf_op jit(solution)/shard_map/ppermute | solution.py:408
  11.1 0.9 %copy-done.12 = f32[72,512]{1,0:T(8,128)S(1)} copy-done((f32[72,512]{1,0:T(8,128)S(1)}, f32[72,512]{1,0:T(8,128)}, u32[]{:S(2)}) %copy-start.12) | copy-done | bytes 147480
  12.0 1.7 %shard_map.137 = f32[136,256]{1,0:T(8,128)S(1)} custom-call(s32[1]{0:T(128)S(6)} %copy.15.count, s32[128,128]{1,0:T(8,128)S(1)} %bitcast.10, f32[128,128]{1,0:T(8,128)S(1)} %bitcast.12, f32[128,128]{1,0:T(8,128)S(1)} %bitcast.14, s32[1,128]{1,0:T(1,128)S(1)} %bitcast.16, f32[72,512]{1,0:T(8,128)S(1)} %copy-done.12), custom_call_target="tpu_custom_call" | custom-call | flops 201326592 | bytes 327680 | tf_op jit(solution)/shard_map/pallas_call | solution.py:35
  13.7 7.3 %all-gather = f32[544,256]{1,0:T(8,128)S(1)} all-gather(f32[136,256]{1,0:T(8,128)S(1)} %shard_map.137), channel_id=2, replica_groups=mesh['grp'=4,'reg'=8] {'grp'}, dimensions={0}, use_global_device_ids=true | all-gather | bytes 696320 | tf_op jit(solution)/shard_map/all_gather | solution.py:443
  21.1 2.4 %collective-permute-done.2.near = f32[8,72,512]{2,1,0:T(8,128)S(1)} collective-permute-done((f32[8,72,512]{2,1,0:T(8,128)}, f32[8,72,512]{2,1,0:T(8,128)S(1)}, u32[]{:S(2)}, u32[]{:S(2)}) %collective-permute-start.2) | collective-permute-done | bytes 1179680 | tf_op jit(solution)/shard_map/ppermute | solution.py:408
  23.5 0.1 shard_map.140
  23.6 4.2 %collective-permute-start.4 = (f32[9,72,512]{2,1,0:T(8,128)S(1)}, f32[9,72,512]{2,1,0:T(8,128)S(1)}, u32[]{:S(2)}, u32[]{:S(2)}) collective-permute-start(f32[9,72,512]{2,1,0:T(8,128)S(1)} %shard_map.140), channel_id=1, source_target_pairs={{0,2},{2,4},{3,1},{4,6},{5,3},{7,5},{16,18},{18,20},{19,17},{20,22... | collective-permute-start | bytes 3981320 | tf_op jit(solution)/shard_map/ppermute | solution.py:408
  27.8 1.9 %collective-permute-start = (f32[408,256]{1,0:T(8,128)S(1)}, f32[408,256]{1,0:T(8,128)S(1)}, u32[]{:S(2)}, u32[]{:S(2)}) collective-permute-start(f32[408,256]{1,0:T(8,128)S(1)} %slice.5.joined._joined), channel_id=1, source_target_pairs={{0,1},{1,0},{2,3},{3,2},{4,5},{5,4},{6,7},{7,6},{16,17},{17,16},{1... | collective-permute-start | bytes 1253384 | tf_op jit(solution)/shard_map/ppermute | solution.py:408
  29.7 0.7 %collective-permute-start.1 = (f32[408,256]{1,0:T(8,128)S(1)}, f32[408,256]{1,0:T(8,128)S(1)}, u32[]{:S(2)}, u32[]{:S(2)}) collective-permute-start(f32[408,256]{1,0:T(8,128)S(1)} %slice.5.joined._joined), channel_id=1, source_target_pairs={{1,2},{2,1},{3,4},{4,3},{5,6},{6,5},{17,18},{18,17},{19,20},{20,19... | collective-permute-start | bytes 1253384 | tf_op jit(solution)/shard_map/ppermute | solution.py:408
  30.4 3.5 %shard_map.138 = (f32[384,128]{1,0:T(8,128)S(1)}, f32[96,128]{1,0:T(8,128)S(1)}, f32[96,128]{1,0:T(8,128)S(1)}) custom-call(f32[3,16384]{1,0:T(4,128)S(1)} %copy-done.4, f32[3,16384]{1,0:T(4,128)S(1)} %copy-done.1, s32[2,4096]{1,0:T(2,128)S(1)} %copy-done.9), custom_call_target="tpu_custom_call" | custom-call | flops 50331648 | bytes 786432 | tf_op jit(solution)/shard_map/pallas_call | solution.py:35
  34.0 6.5 %collective-permute-start.5 = (f32[96,128]{1,0:T(8,128)S(1)}, f32[96,128]{1,0:T(8,128)S(1)}, u32[]{:S(2)}, u32[]{:S(2)}) collective-permute-start(f32[96,128]{1,0:T(8,128)S(1)} %get-tuple-element.25), channel_id=1, source_target_pairs={{0,1},{1,2},{2,3},{3,4},{4,5},{5,6},{6,7},{8,9},{9,10},{10,11},{11... | collective-permute-start | bytes 147464 | tf_op jit(solution)/shard_map/ppermute | solution.py:408
  40.5 1.3 %collective-permute-start.6 = (f32[96,128]{1,0:T(8,128)S(1)}, f32[96,128]{1,0:T(8,128)S(1)}, u32[]{:S(2)}, u32[]{:S(2)}) collective-permute-start(f32[96,128]{1,0:T(8,128)S(1)} %get-tuple-element.26), channel_id=1, source_target_pairs={{1,0},{2,1},{3,2},{4,3},{5,4},{6,5},{7,6},{9,8},{10,9},{11,10},{12... | collective-permute-start | bytes 147464 | tf_op jit(solution)/shard_map/ppermute | solution.py:408
  41.8 1.8 %shard_map.139 = (f32[4,72,512]{2,1,0:T(8,128)S(1)}, f32[4,72,512]{2,1,0:T(8,128)S(1)}, f32[128,128]{1,0:T(8,128)S(1)}, s32[384,128]{1,0:T(8,128)S(1)}) custom-call(s32[6]{0:T(128)S(1)} %copy-done.10, f32[408,256]{1,0:T(8,128)S(1)} %slice.5.joined._joined, f32[8,72,512]{2,1,0:T(8,128)S(1)} %copy-done, f32[384,128]{1,0:T(8,128)S(1)} %get-tuple-element.20._.state), custom_call_target="tpu_custom_call" | custom-call | flops 679477248 | bytes 5308416 | tf_op jit(solution)/shard_map/pallas_call | solution.py:35
  43.6 2.8 %collective-permute-done.6._upper.upper = f32[96,128]{1,0:T(8,128)S(1)} collective-permute-done((f32[96,128]{1,0:T(8,128)S(1)}, f32[96,128]{1,0:T(8,128)S(1)}, u32[]{:S(2)}, u32[]{:S(2)}) %collective-permute-start.6) | collective-permute-done | bytes 49184 | tf_op jit(solution)/shard_map/ppermute | solution.py:408
  46.5 0.0 copy-start.2
  46.5 8.2 %shard_map.141 = (f32[128,384]{1,0:T(8,128)S(1)}, f32[128,384]{1,0:T(8,128)S(1)}, f32[128,384]{1,0:T(8,128)S(1)}) custom-call(s32[6]{0:T(128)S(1)} %copy-done.10, s32[384,128]{1,0:T(8,128)S(1)} %get-tuple-element.21.rows_at, f32[408,256]{1,0:T(8,128)S(1)} %collective-permute-done.joined_near, f32[408,256]{1,0:T(8,128)S(1)} %collective-permute-done.1.joined_far, ...), custom_call_target="tpu_custom_call" | custom-call | flops 1358954496 | bytes 11796480 | tf_op jit(solution)/shard_map/pallas_call | solution.py:35
  54.7 3.4 %collective-permute-start.7 = (f32[128,384]{1,0:T(8,128)S(1)}, f32[128,384]{1,0:T(8,128)S(1)}, u32[]{:S(2)}, u32[]{:S(2)}) collective-permute-start(f32[128,384]{1,0:T(8,128)S(1)} %get-tuple-element.28), channel_id=1, source_target_pairs={{0,16},{1,17},{2,18},{3,19},{4,20},{5,21},{6,22},{7,23},{16,8},{17... | collective-permute-start | bytes 589832 | tf_op jit(solution)/shard_map/ppermute | solution.py:408
  58.1 1.9 %collective-permute-start.8 = (f32[128,384]{1,0:T(8,128)S(1)}, f32[128,384]{1,0:T(8,128)S(1)}, u32[]{:S(2)}, u32[]{:S(2)}) collective-permute-start(f32[128,384]{1,0:T(8,128)S(1)} %get-tuple-element.29), channel_id=1, source_target_pairs={{0,8},{1,9},{2,10},{3,11},{4,12},{5,13},{6,14},{7,15},{16,0},{17,1... | collective-permute-start | bytes 589832 | tf_op jit(solution)/shard_map/ppermute | solution.py:408
  60.1 4.2 %shard_map.142.contact = f32[384,128]{1,0:T(8,128)S(1)} custom-call(s32[128]{0:T(128)S(1)} %copy-done.11, f32[384,128]{1,0:T(8,128)S(1)} %get-tuple-element.20._.state, f32[96,128]{1,0:T(8,128)S(1)} %collective-permute-done.5._lower.lower, f32[96,128]{1,0:T(8,128)S(1)} %collective-permute-done.6._upper.upper, s32[8,16384]{1,0:T(8,128)S(1)} %copy-done.2, ...), custom_call_target="tpu_custom_call" | custom-call | flops 7864320 | bytes 1310720 | tf_op jit(solution)/shard_map/pallas_call | solution.py:35
  64.3 1.4 %collective-permute-done.8.grads_c = f32[128,384]{1,0:T(8,128)S(1)} collective-permute-done((f32[128,384]{1,0:T(8,128)S(1)}, f32[128,384]{1,0:T(8,128)S(1)}, u32[]{:S(2)}, u32[]{:S(2)}) %collective-permute-start.8) | collective-permute-done | bytes 196640 | tf_op jit(solution)/shard_map/ppermute | solution.py:408
  65.7 1.0 %shard_map.143 = f32[3,16384]{1,0:T(4,128)} custom-call(s32[1]{0:T(128)S(6)} %copy.15.count, f32[128,384]{1,0:T(8,128)S(1)} %get-tuple-element.27._.grads_a, f32[128,384]{1,0:T(8,128)S(1)} %collective-permute-done.7.grads_b, f32[128,384]{1,0:T(8,128)S(1)} %collective-permute-done.8.grads_c, f32[128,128]{1,0:T(8,128)S(1)} %get-tuple-element.30.weight, ...), custom_call_target="tpu_custom_call" | custom-call | flops 983040 | bytes 1310720 | tf_op jit(solution)/shard_map/pallas_call | solution.py:35
  (33 shorter events, 0.1 us)
Async XLA Ops:
  0.6 10.4 %copy-start.6 = (s32[16384]{0:T(1024)S(1)}, s32[16384]{0:T(1024)}, u32[]{:S(2)}) copy-start(s32[16384]{0:T(1024)} %param.23) | copy-start | bytes 196612
  0.6 10.4 %copy-start.7 = (f32[16384]{0:T(1024)S(1)}, f32[16384]{0:T(1024)}, u32[]{:S(2)}) copy-start(f32[16384]{0:T(1024)} %param.16) | copy-start | bytes 196612
  0.6 10.4 %copy-start.8 = (f32[16384]{0:T(1024)S(1)}, f32[16384]{0:T(1024)}, u32[]{:S(2)}) copy-start(f32[16384]{0:T(1024)} %param.17) | copy-start | bytes 196612
  0.6 10.4 %copy-start.13 = (s32[128]{0:T(128)S(1)}, s32[128]{0:T(128)}, u32[]{:S(2)}) copy-start(s32[128]{0:T(128)} %param.24) | copy-start | bytes 1540
  4.0 19.4 %copy-start.5 = (f32[72,512]{1,0:T(8,128)S(1)}, f32[72,512]{1,0:T(8,128)}, u32[]{:S(2)}) copy-start(f32[72,512]{1,0:T(8,128)} %get-tuple-element.22.inner) | copy-start | bytes 442372
  4.1 19.4 %collective-permute-start.2 = (f32[8,72,512]{2,1,0:T(8,128)}, f32[8,72,512]{2,1,0:T(8,128)S(1)}, u32[]{:S(2)}, u32[]{:S(2)}) collective-permute-start(f32[8,72,512]{2,1,0:T(8,128)} %get-tuple-element.19.window), channel_id=1, source_target_pairs={{0,1},{1,0},{2,3},{3,2},{4,5},{5,4},{6,7},{7,6},{16,17},{17,16},{1... | collective-permute-start | bytes 3538952 | tf_op jit(solution)/shard_map/ppermute | solution.py:408
  9.1 12.0 %collective-permute-start.3 = (f32[72,512]{1,0:T(8,128)}, f32[72,512]{1,0:T(8,128)S(1)}, u32[]{:S(2)}, u32[]{:S(2)}) collective-permute-start(f32[72,512]{1,0:T(8,128)} %get-tuple-element.18._), channel_id=1, source_target_pairs={{1,3},{2,0},{3,5},{4,2},{5,7},{6,4},{17,19},{18,16},{19,21},{20,18... | collective-permute-start | bytes 442376 | tf_op jit(solution)/shard_map/ppermute | solution.py:408
  11.1 0.9 %copy-start.12 = (f32[72,512]{1,0:T(8,128)S(1)}, f32[72,512]{1,0:T(8,128)}, u32[]{:S(2)}) copy-start(f32[72,512]{1,0:T(8,128)} %get-tuple-element.18._) | copy-start | bytes 442372
  23.4 7.0 %copy-start.1 = (f32[3,16384]{1,0:T(4,128)S(1)}, f32[3,16384]{1,0:T(4,128)}, u32[]{:S(2)}) copy-start(f32[3,16384]{1,0:T(4,128)} %vel.3) | copy-start | bytes 589828
  23.4 7.0 %copy-start.4 = (f32[3,16384]{1,0:T(4,128)S(1)}, f32[3,16384]{1,0:T(4,128)}, u32[]{:S(2)}) copy-start(f32[3,16384]{1,0:T(4,128)} %pos.1) | copy-start | bytes 589828
  23.5 7.0 %copy-start.9 = (s32[2,4096]{1,0:T(2,128)S(1)}, s32[2,4096]{1,0:T(2,128)}, u32[]{:S(2)}) copy-start(s32[2,4096]{1,0:T(2,128)} %lists.1) | copy-start | bytes 98308
  23.5 18.3 %copy-start = (f32[8,72,512]{2,1,0:T(8,128)S(1)}, f32[8,72,512]{2,1,0:T(8,128)}, u32[]{:S(2)}) copy-start(f32[8,72,512]{2,1,0:T(8,128)} %get-tuple-element.19.window) | copy-start | bytes 3538948
  23.5 18.3 %copy-start.10 = (s32[6]{0:T(128)S(1)}, s32[6]{0:T(128)}, u32[]{:S(2)}) copy-start(s32[6]{0:T(128)} %stack.39.place) | copy-start | bytes 76
  23.6 22.9 %collective-permute-start.4 = (f32[9,72,512]{2,1,0:T(8,128)S(1)}, f32[9,72,512]{2,1,0:T(8,128)S(1)}, u32[]{:S(2)}, u32[]{:S(2)}) collective-permute-start(f32[9,72,512]{2,1,0:T(8,128)S(1)} %shard_map.140), channel_id=1, source_target_pairs={{0,2},{2,4},{3,1},{4,6},{5,3},{7,5},{16,18},{18,20},{19,17},{20,22... | collective-permute-start | bytes 3981320 | tf_op jit(solution)/shard_map/ppermute | solution.py:408
  27.8 18.7 %collective-permute-start = (f32[408,256]{1,0:T(8,128)S(1)}, f32[408,256]{1,0:T(8,128)S(1)}, u32[]{:S(2)}, u32[]{:S(2)}) collective-permute-start(f32[408,256]{1,0:T(8,128)S(1)} %slice.5.joined._joined), channel_id=1, source_target_pairs={{0,1},{1,0},{2,3},{3,2},{4,5},{5,4},{6,7},{7,6},{16,17},{17,16},{1... | collective-permute-start | bytes 1253384 | tf_op jit(solution)/shard_map/ppermute | solution.py:408
  29.7 16.7 %collective-permute-start.1 = (f32[408,256]{1,0:T(8,128)S(1)}, f32[408,256]{1,0:T(8,128)S(1)}, u32[]{:S(2)}, u32[]{:S(2)}) collective-permute-start(f32[408,256]{1,0:T(8,128)S(1)} %slice.5.joined._joined), channel_id=1, source_target_pairs={{1,2},{2,1},{3,4},{4,3},{5,6},{6,5},{17,18},{18,17},{19,20},{20,19... | collective-permute-start | bytes 1253384 | tf_op jit(solution)/shard_map/ppermute | solution.py:408
  34.0 9.7 %collective-permute-start.5 = (f32[96,128]{1,0:T(8,128)S(1)}, f32[96,128]{1,0:T(8,128)S(1)}, u32[]{:S(2)}, u32[]{:S(2)}) collective-permute-start(f32[96,128]{1,0:T(8,128)S(1)} %get-tuple-element.25), channel_id=1, source_target_pairs={{0,1},{1,2},{2,3},{3,4},{4,5},{5,6},{6,7},{8,9},{9,10},{10,11},{11... | collective-permute-start | bytes 147464 | tf_op jit(solution)/shard_map/ppermute | solution.py:408
  40.5 6.0 %collective-permute-start.6 = (f32[96,128]{1,0:T(8,128)S(1)}, f32[96,128]{1,0:T(8,128)S(1)}, u32[]{:S(2)}, u32[]{:S(2)}) collective-permute-start(f32[96,128]{1,0:T(8,128)S(1)} %get-tuple-element.26), channel_id=1, source_target_pairs={{1,0},{2,1},{3,2},{4,3},{5,4},{6,5},{7,6},{9,8},{10,9},{11,10},{12... | collective-permute-start | bytes 147464 | tf_op jit(solution)/shard_map/ppermute | solution.py:408
  46.5 13.6 %copy-start.2 = (s32[8,16384]{1,0:T(8,128)S(1)}, s32[8,16384]{1,0:T(8,128)}, u32[]{:S(2)}) copy-start(s32[8,16384]{1,0:T(8,128)} %named.1) | copy-start | bytes 1572868
  46.5 13.6 %copy-start.3 = (f32[8,16384]{1,0:T(8,128)S(1)}, f32[8,16384]{1,0:T(8,128)}, u32[]{:S(2)}) copy-start(f32[8,16384]{1,0:T(8,128)} %stiff.1) | copy-start | bytes 1572868
  46.5 13.6 %copy-start.11 = (s32[128]{0:T(128)S(1)}, s32[128]{0:T(128)}, u32[]{:S(2)}) copy-start(s32[128]{0:T(128)} %partner.1) | copy-start | bytes 1540
  54.7 9.6 %collective-permute-start.7 = (f32[128,384]{1,0:T(8,128)S(1)}, f32[128,384]{1,0:T(8,128)S(1)}, u32[]{:S(2)}, u32[]{:S(2)}) collective-permute-start(f32[128,384]{1,0:T(8,128)S(1)} %get-tuple-element.28), channel_id=1, source_target_pairs={{0,16},{1,17},{2,18},{3,19},{4,20},{5,21},{6,22},{7,23},{16,8},{17... | collective-permute-start | bytes 589832 | tf_op jit(solution)/shard_map/ppermute | solution.py:408
  58.1 7.6 %collective-permute-start.8 = (f32[128,384]{1,0:T(8,128)S(1)}, f32[128,384]{1,0:T(8,128)S(1)}, u32[]{:S(2)}, u32[]{:S(2)}) collective-permute-start(f32[128,384]{1,0:T(8,128)S(1)} %get-tuple-element.29), channel_id=1, source_target_pairs={{0,8},{1,9},{2,10},{3,11},{4,12},{5,13},{6,14},{7,15},{16,0},{17,1... | collective-permute-start | bytes 589832 | tf_op jit(solution)/shard_map/ppermute | solution.py:408

commit v7 on v6

--- a/solution.py
+++ b/solution.py
@@ -43,6 +43,20 @@
     )(*args)
 
 
+class Place:
+    def __init__(self, full, height):
+        groups, regions = lax.axis_size("grp"), lax.axis_size("reg")
+        self.group, region = lax.axis_index("grp"), lax.axis_index("reg")
+        self.half = self.group // CORES
+        self.own_rows = full // (groups // CORES)
+        first = jnp.clip(self.half * self.own_rows - SUB, 0, full - height)
+        self.first = pl.multiple_of(first, SUB)
+        self.sweeps = self.group % CORES == 0
+        self.parity = region % 2
+        self.odd = self.parity == 1
+        self.lower, self.upper = region > 0, region < regions - 1
+
+
 def lanes_of(source, index):
     return jnp.take_along_axis(source, index, axis=1, mode="promise_in_bounds")
 
@@ -52,22 +66,26 @@
     return high, (value - high.astype(F32)).astype(BF16)
 
 
-def window_kernel(place, pressure_old, source, solid_before, window, ends, inner, solid, sems):
+def window_kernel(pressure_old, source, solid_before, window, ends, inner, dummy, solid, sems):
     planes, height, _ = solid.shape
-    rows = pl.ds(pl.multiple_of(place[0], SUB), height)
-    moves = ((pressure_old, window.at[:planes]), (source, window.at[planes:]), (solid_before, solid))
-    copies = [
-        pltpu.make_async_copy(whole.at[:, rows, :], part, sems.at[index])
-        for index, (whole, part) in enumerate(moves)
-    ]
+    place = Place(pressure_old.shape[1], height)
+    rows = pl.ds(place.first, height)
+    copies = []
+    for x in range(planes):
+        for whole, part in (
+            (pressure_old, window.at[x]), (source, window.at[planes + x]), (solid_before, solid.at[x])
+        ):
+            copies.append(
+                pltpu.make_async_copy(whole.at[x, rows, :], part, sems.at[len(copies)])
+            )
     for copy in copies:
         copy.start()
+    dummy[...] = jnp.zeros(dummy.shape, F32)
     for copy in copies:
         copy.wait()
     window[planes:] = window[planes:] - solid[...]
-    odd = place[1]
-    ends[...] = window[odd * (planes - 1)]
-    inner[...] = window[(1 - odd) * (planes - 1)]
+    ends[...] = window[place.parity * (planes - 1)]
+    inner[...] = window[(1 - place.parity) * (planes - 1)]
 
 
 def forward_kernel(near, inner, _joined, _beyond, out):
@@ -123,7 +141,8 @@
     out[tiles : tiles + SUB, BLOCK:] = jnp.zeros((SUB, BLOCK), F32)
 
 
-def halo_kernel(pos, vel, lists, state, down, up):
+def halo_kernel(pos, vel, lists, _, state, near, far, dummy):
+    dummy[...] = jnp.zeros(dummy.shape, F32)
     tiles = pos.shape[1] // BLOCK
     rows = lists.shape[1] // BLOCK
     for tile in range(tiles):
@@ -139,10 +158,13 @@
     span = 2 * BLOCK
     row = iota((BLOCK, span), 0)
 
-    for side, out in enumerate((down, up)):
+    odd = lax.axis_index("reg") % 2
+    for away, out in enumerate((near, far)):
+        side = 1 - odd if away == 0 else odd
 
         def step(part, carry):
-            named = lists[side : side + 1, pl.ds(pl.multiple_of(part * span, span), span)]
+            named = lists[:, pl.ds(pl.multiple_of(part * span, span), span)]
+            named = jnp.where(side == 0, named[:1], named[1:])
             block = lax.shift_right_logical(named, 7)
             lane = named & (BLOCK - 1)
             hot = jnp.where(row == jnp.broadcast_to(block, row.shape), 1.0, 0.0).astype(BF16)
@@ -162,17 +184,36 @@
         lax.fori_loop(0, rows // 2, step, 0, unroll=4)
 
 
-def contact_kernel(partner, state, lower, upper, named, stiff, _, out, extended):
+def message_kernel(joined, halo_near, halo_far, near, far):
+    half = halo_near.shape[0] // 2
+    rows = near.shape[0] - half
+    for halo, out in ((halo_near, near), (halo_far, far)):
+        out[:rows, :] = joined[:rows, :]
+        out[rows:, :BLOCK] = halo[:half, :]
+        out[rows:, BLOCK:] = halo[half:, :]
+
+
+def contact_kernel(
+    partner, state, message_near, message_far, halo_near, halo_far, named, stiff, _, out, extended
+):
     tiles = state.shape[0] // 3
-    rows = lower.shape[0] // 3
+    rows = halo_near.shape[0] // 3
     blocks = tiles + 2 * rows
+    base = message_near.shape[0] - 3 * rows // 2
+    odd = lax.axis_index("reg") % 2
+    sweeps = lax.axis_index("grp") % CORES == 0
     for axis in range(3):
         extended[axis * blocks : axis * blocks + tiles, :] = state[
             axis * tiles : (axis + 1) * tiles, :
         ]
-        for place, side in enumerate((lower, upper)):
-            first = axis * blocks + tiles + place * rows
-            extended[first : first + rows, :] = side[axis * rows : (axis + 1) * rows, :]
+    for message, halo, upper in (
+        (message_near, halo_near, 1 - odd), (message_far, halo_far, odd)
+    ):
+        carried = jnp.concatenate([message[base:, :BLOCK], message[base:, BLOCK:]], 0)
+        carried = jnp.where(sweeps, carried, halo[...])
+        for axis in range(3):
+            first = pl.multiple_of(axis * blocks + tiles + upper * rows, SUB)
+            extended[pl.ds(first, rows), :] = carried[axis * rows : (axis + 1) * rows]
 
     def step(tile, carry):
         lanes = pl.ds(pl.multiple_of(tile * BLOCK, BLOCK), BLOCK)
@@ -194,12 +235,16 @@
 
 def shifted(plane):
     height, width = plane.shape
-    row = iota(plane.shape, 0)
-    column = iota(plane.shape, 1)
-    above = jnp.where(row == 0, 0.0, pltpu.roll(plane, 1, 0))
-    below = jnp.where(row == height - 1, 0.0, pltpu.roll(plane, height - 1, 0))
-    left = jnp.where(column == 0, 0.0, pltpu.roll(plane, 1, 1))
-    right = jnp.where(column == width - 1, 0.0, pltpu.roll(plane, width - 1, 1))
+    row = iota((SUB, width), 0)
+    column = iota((height, BLOCK), 1)
+    above, below = pltpu.roll(plane, 1, 0), pltpu.roll(plane, height - 1, 0)
+    left, right = pltpu.roll(plane, 1, 1), pltpu.roll(plane, width - 1, 1)
+    above = jnp.concatenate([jnp.where(row == 0, 0.0, above[:SUB]), above[SUB:]], 0)
+    below = jnp.concatenate([below[:-SUB], jnp.where(row == SUB - 1, 0.0, below[-SUB:])], 0)
+    left = jnp.concatenate([jnp.where(column == 0, 0.0, left[:, :BLOCK]), left[:, BLOCK:]], 1)
+    right = jnp.concatenate(
+        [right[:, :-BLOCK], jnp.where(column == BLOCK - 1, 0.0, right[:, -BLOCK:])], 1
+    )
     return above, below, left, right
 
 
@@ -210,7 +255,7 @@
 
 def placed(joined, tiles):
     stride = tiles + SUB
-    groups = [joined.at[i * stride : (i + 1) * stride] for i in range(joined.shape[0] // stride)]
+    groups = [joined.at[i * stride : (i + 1) * stride] for i in range(3)]
     parts = [halves_of(group[:tiles, :]) for group in groups]
     loads = jnp.concatenate([part[i] for i in range(2) for part in parts], 0)
     ids = jnp.concatenate([group[tiles : tiles + 1, :BLOCK] for group in groups], 1)
@@ -248,12 +293,13 @@
             factor[base + x, :, lanes] = scale[rows]
 
 
-def own_kernel(full, own_rows, place, joined, window, _, constant, factor, weight, rows_at):
+def own_kernel(full, joined, window, _, constant, factor, weight, rows_at):
     tiles = weight.shape[0]
     planes, height, width = constant.shape
+    place = Place(full, height)
     zones = width // BLOCK
     ids, gathered = placed(joined, tiles)
-    coefficients(gathered, tiles, place[0], full, window, planes, constant, factor, 0, None)
+    coefficients(gathered, tiles, place.first, full, window, planes, constant, factor, 0, None)
     turned = [
         jnp.transpose(
             jnp.broadcast_to(ids[:, i * tiles : (i + 1) * tiles], (BLOCK, tiles)).astype(F32)
@@ -262,7 +308,7 @@
     ]
 
     def before(places):
-        index = lax.rem(place[5] + 3 - places, 3)
+        index = lax.rem(place.group + 3 - places, 3)
         return jnp.where(index == 0, turned[0], jnp.where(index == 1, turned[1], turned[2]))
 
     solid, drag = gathered(jnp.concatenate([before(0)] * 3, 1))
@@ -271,28 +317,30 @@
         block = before(i)
         line, zone = block // zones, block % zones
         x, y = line // full, line % full
-        row = (x * zones + zone) * height + y - place[0]
-        rows_at[i * tiles : (i + 1) * tiles, :] = jnp.where(y // own_rows == place[4], row, -1)
+        row = (x * zones + zone) * height + y - place.first
+        held = y // place.own_rows == jnp.where(place.sweeps, place.half, -1)
+        rows_at[i * tiles : (i + 1) * tiles, :] = jnp.where(held, row, -1)
 
 
 def solve_kernel(
-    full, sweeps, place, rows_at, joined_near, joined_far, window, near, far, beyond,
-    own_constant, own_factor, _lower, _upper, out_a, out_b, out_c,
+    full, sweeps, rows_at, joined_near, joined_far, window, near, far, beyond,
+    own_constant, own_factor, _near, _far, out_a, out_b, out_c,
     constant, factor, old, new, fields,
 ):
     planes, height, width = own_constant.shape
     zones = width // BLOCK
-    tiles = joined_near.shape[0] // 3 - SUB
-    odd = place[1] == 1
+    tiles = out_a.shape[0]
+    place = Place(full, height)
+    odd = place.odd
     rim = sweeps + 1
     for joined, driven, below, present in (
-        (joined_near, near, odd, jnp.where(odd, place[2], place[3])),
-        (joined_far, far, jnp.logical_not(odd), jnp.where(odd, place[3], place[2])),
+        (joined_near, near, odd, jnp.where(odd, place.lower, place.upper)),
+        (joined_far, far, jnp.logical_not(odd), jnp.where(odd, place.upper, place.lower)),
     ):
         _, gathered = placed(joined, tiles)
         coefficients(
-            gathered, tiles, place[0], full, driven, planes, constant, factor,
-            jnp.where(below, 0, planes), present == 1,
+            gathered, tiles, place.first, full, driven, planes, constant, factor,
+            jnp.where(below, 0, planes), present,
         )
     old[pl.ds(jnp.where(odd, 1, rim + planes), planes)] = near[:planes]
     old[pl.ds(jnp.where(odd, rim + planes, 1), planes)] = far[:planes]
@@ -393,13 +441,6 @@
     zones = width // BLOCK
     own_rows = full // halves
     height = min(full, own_rows + SUB * min(2, halves - 1))
-    group, region = lax.axis_index("grp"), lax.axis_index("reg")
-    half = group // CORES
-    first = jnp.clip(half * own_rows - SUB, 0, full - height)
-    odd = region % 2 == 1
-    place = jnp.stack(
-        [first, odd, region > 0, region < regions - 1, jnp.where(group % CORES == 0, half, -1), group]
-    ).astype(jnp.int32)
     owners = range(0, groups, CORES)
     holders = range(holding)
 
@@ -429,21 +470,33 @@
 
     field = shaped(planes, height, width)
     plane = shaped(height, width)
-    window, ends, inner = call(
-        window_kernel, (shaped(2 * planes, height, width), plane, plane), [SMEM] + [HBM] * 3,
-        (place, pressure_old, pressure_source, solid_old),
-        [pltpu.VMEM((planes, height, width), F32), pltpu.SemaphoreType.DMA((3,))],
+    window, ends, inner, dummy = call(
+        window_kernel, (shaped(2 * planes, height, width), plane, plane, shaped(SUB, BLOCK)),
+        [HBM] * 3, (pressure_old, pressure_source, solid_old),
+        [pltpu.VMEM((planes, height, width), F32), pltpu.SemaphoreType.DMA((3 * planes,))],
         flops=field_bytes, size=6 * field_bytes, limit=61_500_000,
     )
     near = along_reg(window, owners, (1, -1))
+    rows = halo_list.shape[1] // BLOCK
+    halo = shaped(3 * rows, BLOCK)
+    state, halo_near, halo_far, after_halo = call(
+        halo_kernel, (shaped(3 * tiles, BLOCK), halo, halo, shaped(SUB, BLOCK)),
+        [VMEM] * 4, (grain_pos, grain_vel, halo_list, dummy), flops=8 * 3 * 16384 * 128,
+        size=4 * 4 * 3 * slots,
+    )
     mine = call(
-        deposit_kernel, shaped(tiles + SUB, 2 * BLOCK), [SMEM] + [VMEM] * 4 + [ANY],
-        (count, cell, vol, drag, ids, ends), flops=2 * 32 * 48 * 65536, size=5 * 4 * slots,
+        deposit_kernel, shaped(tiles + SUB, 2 * BLOCK), [SMEM] + [VMEM] * 5,
+        (count, cell, vol, drag, ids, after_halo), flops=2 * 32 * 48 * 65536, size=5 * 4 * slots,
     )
     joined = lax.all_gather(mine, "grp")
-    joined = joined[:holding].reshape(holding * (tiles + SUB), 2 * BLOCK)
-    joined_near = along_reg(joined, owners, (1, -1))
-    joined_far = along_reg(joined, owners, (-1, 1))
+    joined = joined.reshape(groups * (tiles + SUB), 2 * BLOCK)
+    message = shaped(holding * (tiles + SUB) + 3 * rows // 2, 2 * BLOCK)
+    message_near, message_far = call(
+        message_kernel, (message,) * 2, [VMEM] * 3, (joined, halo_near, halo_far),
+        size=8 * 2 * BLOCK * 500,
+    )
+    message_near = along_reg(message_near, owners, (1, -1))
+    message_far = along_reg(message_far, owners, (-1, 1))
     beyond = along_reg(ends, owners, (-2, 2))
     far = along_reg(
         call(
@@ -454,21 +507,16 @@
         owners, (2, -2),
     )
 
-    rows = halo_list.shape[1] // BLOCK
-    state, down, up = call(
-        halo_kernel, (shaped(3 * tiles, BLOCK), shaped(3 * rows, BLOCK), shaped(3 * rows, BLOCK)),
-        [VMEM] * 3, (grain_pos, grain_vel, halo_list), flops=8 * 3 * 16384 * 128, size=4 * 4 * 3 * slots,
-    )
-    lower = along_reg(up, holders, (1, 1))
-    upper = along_reg(down, holders, (-1, -1))
-
+    others = [g for g in holders if g not in owners]
+    halo_near = along_reg(halo_near, others, (1, -1))
+    halo_far = along_reg(halo_far, others, (-1, 1))
     constant, factor, weight, rows_at = call(
-        functools.partial(own_kernel, full, own_rows),
+        functools.partial(own_kernel, full),
         (
             field, field, shaped(tiles, BLOCK),
             jax.ShapeDtypeStruct((3 * tiles, BLOCK), jnp.int32),
         ),
-        [SMEM] + [VMEM] * 2 + [ANY], (place, joined, window, state),
+        [VMEM] * 3, (joined, window, dummy),
         flops=planes * height * 4 * 384 * 256 * 6, size=9 * field_bytes,
     )
 
@@ -476,10 +524,10 @@
     window_of = lambda count: pltpu.VMEM((count, height, width), F32)
     grads_a, grads_b, grads_c = call(
         functools.partial(solve_kernel, full, ITERS), (grads,) * 3,
-        [SMEM] + [VMEM] * 9 + [ANY] * 2,
+        [VMEM] * 9 + [ANY] * 2,
         (
-            place, rows_at, joined_near, joined_far, window, near, far, beyond, constant, factor,
-            lower, upper,
+            rows_at, message_near, message_far, window, near, far, beyond, constant, factor,
+            halo_near, halo_far,
         ),
         [
             window_of(2 * planes), window_of(2 * planes),
@@ -492,8 +540,11 @@
     grads_c = along_grp(grads_c, -2, owners)
 
     contact = call(
-        contact_kernel, shaped(3 * tiles, BLOCK), [SMEM] + [VMEM] * 5 + [ANY],
-        (partner_block, state, lower, upper, contact_rows, contact_stiff, grads_a),
+        contact_kernel, shaped(3 * tiles, BLOCK), [SMEM] + [VMEM] * 7 + [ANY],
+        (
+            partner_block, state, message_near, message_far, halo_near, halo_far, contact_rows,
+            contact_stiff, grads_a,
+        ),
         [pltpu.VMEM((3 * (tiles + 2 * rows), BLOCK), F32)],
         flops=60 * 8 * slots, size=4 * 20 * slots,
     )

time: 67.1 us -> 62.5 us (0.931)
  starting transfers between devices: 26.2 us -> 19.6 us
  waiting for transfers between devices: 6.6 us -> 11.2 us
  Pallas kernels: 23.9 us -> 22.3 us
  local copies, waits for them, and re-layouts: 1.62 us -> 0.72 us
    ppermute x9, starting transfers between devices: 26.2 us -> 19.6 us  [send(): return lax.ppermute(value, ('grp', 'reg'), flat)]
    ppermute x9, waiting for transfers between devices: 6.6 us -> 11.2 us  [send(): return lax.ppermute(value, ('grp', 'reg'), flat)]
    pallas_call x8 -> x9, Pallas kernels: 23.9 us -> 22.3 us  [call(): pl.pallas_call(kernel, out_shape=outs, in_specs=specs, out_specs=jax.tree...]
where the time goes in v7:
time: 62.5 us; the launch traced here: 62.1 us
  Pallas kernels  22.3 us (36%)
  starting transfers between devices  19.6 us (31%)
  waiting for transfers between devices  11.2 us (18%)
  blocking collectives  7.36 us (12%)
  between operations  0.95 us (2%)
  local copies, waits for them, and re-layouts  0.72 us (1%)
    pallas_call x9, Pallas kernels, call(): pl.pallas_call(kernel, out_shape=outs, in_specs=specs, out_specs=jax.tree...  22.3 us
    ppermute x9, starting transfers between devices, send(): return lax.ppermute(value, ('grp', 'reg'), flat)  19.6 us
    ppermute x9, waiting for transfers between devices, send(): return lax.ppermute(value, ('grp', 'reg'), flat)  11.2 us
    all_gather x1, blocking collectives, on_device(): joined = lax.all_gather(mine, 'grp')  7.36 us
  transfers between devices with their start and end apart: 9, of which 3 were waited for; matrix products, arithmetic and copies ran while one was open for 0% of the time, Pallas kernels for 17%

profile of v7, /device:TPU:0, one launch (start us, length us, event | category | flops | bytes accessed | tf_op | source)
XLA Modules:
  0.0 62.1 jit_solution(17898349890988950328)
XLA Ops:
  0.0 2.8 %shard_map.136 = (f32[8,72,512]{2,1,0:T(8,128)}, f32[72,512]{1,0:T(8,128)}, f32[72,512]{1,0:T(8,128)}, f32[8,128]{1,0:T(8,128)}) custom-call(f32[4,128,512]{2,1,0:T(8,128)} %pressure_old.1, f32[4,128,512]{2,1,0:T(8,128)} %source.1, f32[4,128,512]{2,1,0:T(8,128)} %solid_before.1), custom_call_target="tpu_custom_call" | custom-call | flops 589824 | bytes 3538944 | tf_op jit(solution)/shard_map/pallas_call | solution.py:35
  2.9 5.0 %collective-permute-start.2 = (f32[8,72,512]{2,1,0:T(8,128)}, f32[8,72,512]{2,1,0:T(8,128)S(1)}, u32[]{:S(2)}, u32[]{:S(2)}) collective-permute-start(f32[8,72,512]{2,1,0:T(8,128)} %get-tuple-element.24.window), channel_id=1, source_target_pairs={{0,1},{1,0},{2,3},{3,2},{4,5},{5,4},{6,7},{7,6},{16,17},{17,16},{1... | collective-permute-start | bytes 3538952 | tf_op jit(solution)/shard_map/ppermute | solution.py:449
  7.9 1.3 %collective-permute-start.3 = (f32[72,512]{1,0:T(8,128)}, f32[72,512]{1,0:T(8,128)S(1)}, u32[]{:S(2)}, u32[]{:S(2)}) collective-permute-start(f32[72,512]{1,0:T(8,128)} %get-tuple-element.31), channel_id=1, source_target_pairs={{1,3},{2,0},{3,5},{4,2},{5,7},{6,4},{17,19},{18,16},{19,21},{20,18... | collective-permute-start | bytes 442376 | tf_op jit(solution)/shard_map/ppermute | solution.py:449
  9.9 0.7 %copy-done.10 = f32[8,128]{1,0:T(8,128)S(1)} copy-done((f32[8,128]{1,0:T(8,128)S(1)}, f32[8,128]{1,0:T(8,128)}, u32[]{:S(2)}) %copy-start.10) | copy-done | bytes 4120
  10.6 3.5 %shard_map.137 = (f32[384,128]{1,0:T(8,128)S(1)}, f32[96,128]{1,0:T(8,128)S(1)}, f32[96,128]{1,0:T(8,128)S(1)}, f32[8,128]{1,0:T(8,128)S(1)}) custom-call(f32[3,16384]{1,0:T(4,128)S(1)} %copy-done.4, f32[3,16384]{1,0:T(4,128)S(1)} %copy-done.1, s32[2,4096]{1,0:T(2,128)S(1)} %copy-done.9, f32[8,128]{1,0:T(8,128)S(1)} %copy-done.10), custom_call_target="tpu_custom_call" | custom-call | flops 50331648 | bytes 786432 | tf_op jit(solution)/shard_map/pallas_call | solution.py:35
  14.1 1.7 %shard_map.138 = f32[136,256]{1,0:T(8,128)S(1)} custom-call(s32[1]{0:T(128)S(6)} %copy.15.count, s32[128,128]{1,0:T(8,128)S(1)} %bitcast.4, f32[128,128]{1,0:T(8,128)S(1)} %bitcast.6, f32[128,128]{1,0:T(8,128)S(1)} %bitcast.8, s32[1,128]{1,0:T(1,128)S(1)} %bitcast.10, f32[8,128]{1,0:T(8,128)S(1)} %get-tuple-element.23._), custom_call_target="tpu_custom_call" | custom-call | flops 201326592 | bytes 327680 | tf_op jit(solution)/shard_map/pallas_call | solution.py:35
  15.8 7.4 %all-gather.joined._joined = f32[544,256]{1,0:T(8,128)S(1)} all-gather(f32[136,256]{1,0:T(8,128)S(1)} %shard_map.138), channel_id=2, replica_groups=mesh['grp'=4,'reg'=8] {'grp'}, dimensions={0}, use_global_device_ids=true | all-gather | bytes 696320 | tf_op jit(solution)/shard_map/all_gather | solution.py:491
  23.2 0.1 shard_map.141
  23.3 4.8 %collective-permute-start.4 = (f32[9,72,512]{2,1,0:T(8,128)S(1)}, f32[9,72,512]{2,1,0:T(8,128)S(1)}, u32[]{:S(2)}, u32[]{:S(2)}) collective-permute-start(f32[9,72,512]{2,1,0:T(8,128)S(1)} %shard_map.141), channel_id=1, source_target_pairs={{0,2},{2,4},{3,1},{4,6},{5,3},{7,5},{16,18},{18,20},{19,17},{20,22... | collective-permute-start | bytes 3981320 | tf_op jit(solution)/shard_map/ppermute | solution.py:449
  28.1 0.1 shard_map.140
  28.1 1.9 %collective-permute-start = (f32[456,256]{1,0:T(8,128)S(1)}, f32[456,256]{1,0:T(8,128)S(1)}, u32[]{:S(2)}, u32[]{:S(2)}) collective-permute-start(f32[456,256]{1,0:T(8,128)S(1)} %get-tuple-element.28), channel_id=1, source_target_pairs={{0,1},{1,0},{2,3},{3,2},{4,5},{5,4},{6,7},{7,6},{16,17},{17,16},{1... | collective-permute-start | bytes 1400840 | tf_op jit(solution)/shard_map/ppermute | solution.py:449
  30.1 0.7 %collective-permute-start.1 = (f32[456,256]{1,0:T(8,128)S(1)}, f32[456,256]{1,0:T(8,128)S(1)}, u32[]{:S(2)}, u32[]{:S(2)}) collective-permute-start(f32[456,256]{1,0:T(8,128)S(1)} %get-tuple-element.29), channel_id=1, source_target_pairs={{1,2},{2,1},{3,4},{4,3},{5,6},{6,5},{17,18},{18,17},{19,20},{20,19... | collective-permute-start | bytes 1400840 | tf_op jit(solution)/shard_map/ppermute | solution.py:449
  30.8 0.7 %collective-permute-start.5 = (f32[96,128]{1,0:T(8,128)S(1)}, f32[96,128]{1,0:T(8,128)S(1)}, u32[]{:S(2)}, u32[]{:S(2)}) collective-permute-start(f32[96,128]{1,0:T(8,128)S(1)} %get-tuple-element.26.halo_near), channel_id=1, source_target_pairs={{8,9},{9,8},{10,11},{11,10},{12,13},{13,12},{14,15},{15,14}} | collective-permute-start | bytes 147464 | tf_op jit(solution)/shard_map/ppermute | solution.py:449
  31.4 0.7 %collective-permute-start.6 = (f32[96,128]{1,0:T(8,128)S(1)}, f32[96,128]{1,0:T(8,128)S(1)}, u32[]{:S(2)}, u32[]{:S(2)}) collective-permute-start(f32[96,128]{1,0:T(8,128)S(1)} %get-tuple-element.27.halo_far), channel_id=1, source_target_pairs={{9,10},{10,9},{11,12},{12,11},{13,14},{14,13}} | collective-permute-start | bytes 147464 | tf_op jit(solution)/shard_map/ppermute | solution.py:449
  32.1 1.3 %shard_map.139 = (f32[4,72,512]{2,1,0:T(8,128)S(1)}, f32[4,72,512]{2,1,0:T(8,128)S(1)}, f32[128,128]{1,0:T(8,128)S(1)}, s32[384,128]{1,0:T(8,128)S(1)}) custom-call(f32[544,256]{1,0:T(8,128)S(1)} %all-gather.joined._joined, f32[8,72,512]{2,1,0:T(8,128)S(1)} %copy-done, f32[8,128]{1,0:T(8,128)S(1)} %copy-done.10), custom_call_target="tpu_custom_call" | custom-call | flops 679477248 | bytes 5308416 | tf_op jit(solution)/shard_map/pallas_call | solution.py:35
  33.4 0.0 collective-permute-done.6._far.halo_far
  33.4 8.3 %collective-permute-done.joined_near.message_near = f32[456,256]{1,0:T(8,128)S(1)} collective-permute-done((f32[456,256]{1,0:T(8,128)S(1)}, f32[456,256]{1,0:T(8,128)S(1)}, u32[]{:S(2)}, u32[]{:S(2)}) %collective-permute-start) | collective-permute-done | bytes 466976 | tf_op jit(solution)/shard_map/ppermute | solution.py:449
  41.8 1.5 %collective-permute-done.4.far = f32[9,72,512]{2,1,0:T(8,128)S(1)} collective-permute-done((f32[9,72,512]{2,1,0:T(8,128)S(1)}, f32[9,72,512]{2,1,0:T(8,128)S(1)}, u32[]{:S(2)}, u32[]{:S(2)}) %collective-permute-start.4) | collective-permute-done | bytes 1327136 | tf_op jit(solution)/shard_map/ppermute | solution.py:449
  43.3 7.6 %shard_map.142 = (f32[128,384]{1,0:T(8,128)S(1)}, f32[128,384]{1,0:T(8,128)S(1)}, f32[128,384]{1,0:T(8,128)S(1)}) custom-call(s32[384,128]{1,0:T(8,128)S(1)} %get-tuple-element.25.rows_at, f32[456,256]{1,0:T(8,128)S(1)} %collective-permute-done.joined_near.message_near, f32[456,256]{1,0:T(8,128)S(1)} %collective-permute-done.1.joined_far.message_far, ...), custom_call_target="tpu_custom_call" | custom-call | flops 1358954496 | bytes 11796480 | tf_op jit(solution)/shard_map/pallas_call | solution.py:35
  50.9 2.7 %collective-permute-start.7 = (f32[128,384]{1,0:T(8,128)S(1)}, f32[128,384]{1,0:T(8,128)S(1)}, u32[]{:S(2)}, u32[]{:S(2)}) collective-permute-start(f32[128,384]{1,0:T(8,128)S(1)} %get-tuple-element.35), channel_id=1, source_target_pairs={{0,16},{1,17},{2,18},{3,19},{4,20},{5,21},{6,22},{7,23},{16,8},{17... | collective-permute-start | bytes 589832 | tf_op jit(solution)/shard_map/ppermute | solution.py:449
  53.5 1.9 %collective-permute-start.8 = (f32[128,384]{1,0:T(8,128)S(1)}, f32[128,384]{1,0:T(8,128)S(1)}, u32[]{:S(2)}, u32[]{:S(2)}) collective-permute-start(f32[128,384]{1,0:T(8,128)S(1)} %get-tuple-element.36), channel_id=1, source_target_pairs={{0,8},{1,9},{2,10},{3,11},{4,12},{5,13},{6,14},{7,15},{16,0},{17,1... | collective-permute-start | bytes 589832 | tf_op jit(solution)/shard_map/ppermute | solution.py:449
  55.5 4.2 %shard_map.143.contact = f32[384,128]{1,0:T(8,128)S(1)} custom-call(s32[128]{0:T(128)S(1)} %copy-done.11, f32[384,128]{1,0:T(8,128)S(1)} %get-tuple-element.38.state, f32[456,256]{1,0:T(8,128)S(1)} %collective-permute-done.joined_near.message_near, f32[456,256]{1,0:T(8,128)S(1)} %collective-permute-done.1.joined_far.message_far, ...), custom_call_target="tpu_custom_call" | custom-call | flops 7864320 | bytes 1310720 | tf_op jit(solution)/shard_map/pallas_call | solution.py:35
  59.7 1.4 %collective-permute-done.8.grads_c = f32[128,384]{1,0:T(8,128)S(1)} collective-permute-done((f32[128,384]{1,0:T(8,128)S(1)}, f32[128,384]{1,0:T(8,128)S(1)}, u32[]{:S(2)}, u32[]{:S(2)}) %collective-permute-start.8) | collective-permute-done | bytes 196640 | tf_op jit(solution)/shard_map/ppermute | solution.py:449
  61.1 1.0 %shard_map.144 = f32[3,16384]{1,0:T(4,128)} custom-call(s32[1]{0:T(128)S(6)} %copy.15.count, f32[128,384]{1,0:T(8,128)S(1)} %get-tuple-element.34._.grads_a, f32[128,384]{1,0:T(8,128)S(1)} %collective-permute-done.7.grads_b, f32[128,384]{1,0:T(8,128)S(1)} %collective-permute-done.8.grads_c, f32[128,128]{1,0:T(8,128)S(1)} %get-tuple-element.37.weight, ...), custom_call_target="tpu_custom_call" | custom-call | flops 983040 | bytes 1310720 | tf_op jit(solution)/shard_map/pallas_call | solution.py:35
  (30 shorter events, 0.1 us)
Async XLA Ops:
  0.0 9.9 %copy-start.4 = (f32[3,16384]{1,0:T(4,128)S(1)}, f32[3,16384]{1,0:T(4,128)}, u32[]{:S(2)}) copy-start(f32[3,16384]{1,0:T(4,128)} %pos.1) | copy-start | bytes 589828
  0.0 9.9 %copy-start.1 = (f32[3,16384]{1,0:T(4,128)S(1)}, f32[3,16384]{1,0:T(4,128)}, u32[]{:S(2)}) copy-start(f32[3,16384]{1,0:T(4,128)} %vel.3) | copy-start | bytes 589828
  0.0 9.9 %copy-start.9 = (s32[2,4096]{1,0:T(2,128)S(1)}, s32[2,4096]{1,0:T(2,128)}, u32[]{:S(2)}) copy-start(s32[2,4096]{1,0:T(2,128)} %lists.1) | copy-start | bytes 98308
  0.0 14.1 %copy-start.6 = (s32[16384]{0:T(1024)S(1)}, s32[16384]{0:T(1024)}, u32[]{:S(2)}) copy-start(s32[16384]{0:T(1024)} %param.23) | copy-start | bytes 196612
  0.0 14.1 %copy-start.7 = (f32[16384]{0:T(1024)S(1)}, f32[16384]{0:T(1024)}, u32[]{:S(2)}) copy-start(f32[16384]{0:T(1024)} %param.16) | copy-start | bytes 196612
  0.0 14.1 %copy-start.8 = (f32[16384]{0:T(1024)S(1)}, f32[16384]{0:T(1024)}, u32[]{:S(2)}) copy-start(f32[16384]{0:T(1024)} %param.17) | copy-start | bytes 196612
  0.0 14.1 %copy-start.12 = (s32[128]{0:T(128)S(1)}, s32[128]{0:T(128)}, u32[]{:S(2)}) copy-start(s32[128]{0:T(128)} %param.24) | copy-start | bytes 1540
  2.9 20.3 %copy-start.5 = (f32[72,512]{1,0:T(8,128)S(1)}, f32[72,512]{1,0:T(8,128)}, u32[]{:S(2)}) copy-start(f32[72,512]{1,0:T(8,128)} %get-tuple-element.30.inner) | copy-start | bytes 442372
  2.9 20.3 %collective-permute-start.2 = (f32[8,72,512]{2,1,0:T(8,128)}, f32[8,72,512]{2,1,0:T(8,128)S(1)}, u32[]{:S(2)}, u32[]{:S(2)}) collective-permute-start(f32[8,72,512]{2,1,0:T(8,128)} %get-tuple-element.24.window), channel_id=1, source_target_pairs={{0,1},{1,0},{2,3},{3,2},{4,5},{5,4},{6,7},{7,6},{16,17},{17,16},{1... | collective-permute-start | bytes 3538952 | tf_op jit(solution)/shard_map/ppermute | solution.py:449
  7.9 15.3 %collective-permute-start.3 = (f32[72,512]{1,0:T(8,128)}, f32[72,512]{1,0:T(8,128)S(1)}, u32[]{:S(2)}, u32[]{:S(2)}) collective-permute-start(f32[72,512]{1,0:T(8,128)} %get-tuple-element.31), channel_id=1, source_target_pairs={{1,3},{2,0},{3,5},{4,2},{5,7},{6,4},{17,19},{18,16},{19,21},{20,18... | collective-permute-start | bytes 442376 | tf_op jit(solution)/shard_map/ppermute | solution.py:449
  9.9 0.7 %copy-start.10 = (f32[8,128]{1,0:T(8,128)S(1)}, f32[8,128]{1,0:T(8,128)}, u32[]{:S(2)}) copy-start(f32[8,128]{1,0:T(8,128)} %get-tuple-element.22._) | copy-start | bytes 12292
  23.2 8.9 %copy-start = (f32[8,72,512]{2,1,0:T(8,128)S(1)}, f32[8,72,512]{2,1,0:T(8,128)}, u32[]{:S(2)}) copy-start(f32[8,72,512]{2,1,0:T(8,128)} %get-tuple-element.24.window) | copy-start | bytes 3538948
  23.3 20.0 %collective-permute-start.4 = (f32[9,72,512]{2,1,0:T(8,128)S(1)}, f32[9,72,512]{2,1,0:T(8,128)S(1)}, u32[]{:S(2)}, u32[]{:S(2)}) collective-permute-start(f32[9,72,512]{2,1,0:T(8,128)S(1)} %shard_map.141), channel_id=1, source_target_pairs={{0,2},{2,4},{3,1},{4,6},{5,3},{7,5},{16,18},{18,20},{19,17},{20,22... | collective-permute-start | bytes 3981320 | tf_op jit(solution)/shard_map/ppermute | solution.py:449
  28.1 13.6 %collective-permute-start = (f32[456,256]{1,0:T(8,128)S(1)}, f32[456,256]{1,0:T(8,128)S(1)}, u32[]{:S(2)}, u32[]{:S(2)}) collective-permute-start(f32[456,256]{1,0:T(8,128)S(1)} %get-tuple-element.28), channel_id=1, source_target_pairs={{0,1},{1,0},{2,3},{3,2},{4,5},{5,4},{6,7},{7,6},{16,17},{17,16},{1... | collective-permute-start | bytes 1400840 | tf_op jit(solution)/shard_map/ppermute | solution.py:449
  30.1 11.7 %collective-permute-start.1 = (f32[456,256]{1,0:T(8,128)S(1)}, f32[456,256]{1,0:T(8,128)S(1)}, u32[]{:S(2)}, u32[]{:S(2)}) collective-permute-start(f32[456,256]{1,0:T(8,128)S(1)} %get-tuple-element.29), channel_id=1, source_target_pairs={{1,2},{2,1},{3,4},{4,3},{5,6},{6,5},{17,18},{18,17},{19,20},{20,19... | collective-permute-start | bytes 1400840 | tf_op jit(solution)/shard_map/ppermute | solution.py:449
  30.8 2.7 %collective-permute-start.5 = (f32[96,128]{1,0:T(8,128)S(1)}, f32[96,128]{1,0:T(8,128)S(1)}, u32[]{:S(2)}, u32[]{:S(2)}) collective-permute-start(f32[96,128]{1,0:T(8,128)S(1)} %get-tuple-element.26.halo_near), channel_id=1, source_target_pairs={{8,9},{9,8},{10,11},{11,10},{12,13},{13,12},{14,15},{15,14}} | collective-permute-start | bytes 147464 | tf_op jit(solution)/shard_map/ppermute | solution.py:449
  31.4 2.0 %collective-permute-start.6 = (f32[96,128]{1,0:T(8,128)S(1)}, f32[96,128]{1,0:T(8,128)S(1)}, u32[]{:S(2)}, u32[]{:S(2)}) collective-permute-start(f32[96,128]{1,0:T(8,128)S(1)} %get-tuple-element.27.halo_far), channel_id=1, source_target_pairs={{9,10},{10,9},{11,12},{12,11},{13,14},{14,13}} | collective-permute-start | bytes 147464 | tf_op jit(solution)/shard_map/ppermute | solution.py:449
  43.3 12.2 %copy-start.2 = (s32[8,16384]{1,0:T(8,128)S(1)}, s32[8,16384]{1,0:T(8,128)}, u32[]{:S(2)}) copy-start(s32[8,16384]{1,0:T(8,128)} %named.1) | copy-start | bytes 1572868
  43.3 12.2 %copy-start.3 = (f32[8,16384]{1,0:T(8,128)S(1)}, f32[8,16384]{1,0:T(8,128)}, u32[]{:S(2)}) copy-start(f32[8,16384]{1,0:T(8,128)} %stiff.1) | copy-start | bytes 1572868
  43.3 12.2 %copy-start.11 = (s32[128]{0:T(128)S(1)}, s32[128]{0:T(128)}, u32[]{:S(2)}) copy-start(s32[128]{0:T(128)} %partner.1) | copy-start | bytes 1540
  50.9 8.8 %collective-permute-start.7 = (f32[128,384]{1,0:T(8,128)S(1)}, f32[128,384]{1,0:T(8,128)S(1)}, u32[]{:S(2)}, u32[]{:S(2)}) collective-permute-start(f32[128,384]{1,0:T(8,128)S(1)} %get-tuple-element.35), channel_id=1, source_target_pairs={{0,16},{1,17},{2,18},{3,19},{4,20},{5,21},{6,22},{7,23},{16,8},{17... | collective-permute-start | bytes 589832 | tf_op jit(solution)/shard_map/ppermute | solution.py:449
  53.5 7.6 %collective-permute-start.8 = (f32[128,384]{1,0:T(8,128)S(1)}, f32[128,384]{1,0:T(8,128)S(1)}, u32[]{:S(2)}, u32[]{:S(2)}) collective-permute-start(f32[128,384]{1,0:T(8,128)S(1)} %get-tuple-element.36), channel_id=1, source_target_pairs={{0,8},{1,9},{2,10},{3,11},{4,12},{5,13},{6,14},{7,15},{16,0},{17,1... | collective-permute-start | bytes 589832 | tf_op jit(solution)/shard_map/ppermute | solution.py:449

commit v8 on v7

--- a/solution.py
+++ b/solution.py
@@ -66,7 +66,7 @@
     return high, (value - high.astype(F32)).astype(BF16)
 
 
-def window_kernel(pressure_old, source, solid_before, window, ends, inner, dummy, solid, sems):
+def window_kernel(pressure_old, source, solid_before, window, inner, dummy, solid, sems):
     planes, height, _ = solid.shape
     place = Place(pressure_old.shape[1], height)
     rows = pl.ds(place.first, height)
@@ -84,17 +84,18 @@
     for copy in copies:
         copy.wait()
     window[planes:] = window[planes:] - solid[...]
-    ends[...] = window[place.parity * (planes - 1)]
     inner[...] = window[(1 - place.parity) * (planes - 1)]
 
 
-def forward_kernel(near, inner, _joined, _beyond, out):
+def forward_kernel(near, inner, _halo, _second, _third, out, dummy):
+    dummy[...] = jnp.zeros(dummy.shape, F32)
     count = near.shape[0]
     out[:count] = near[...]
     out[count] = inner[...]
 
 
-def deposit_kernel(count, cell, vol, drag, ids, _, out):
+def deposit_kernel(count, cell, vol, drag, ids, _, out, dummy):
+    dummy[...] = jnp.zeros(dummy.shape, F32)
     tiles = cell.shape[0]
     sub = iota((SUB, BLOCK), 0)
     rows_c = iota((BLOCK, BLOCK), 0)
@@ -184,11 +185,14 @@
         lax.fori_loop(0, rows // 2, step, 0, unroll=4)
 
 
-def message_kernel(joined, halo_near, halo_far, near, far):
+def message_kernel(mine, second, third, halo_near, halo_far, _, near, far, dummy):
+    dummy[...] = jnp.zeros(dummy.shape, F32)
+    stride = mine.shape[0]
     half = halo_near.shape[0] // 2
     rows = near.shape[0] - half
     for halo, out in ((halo_near, near), (halo_far, far)):
-        out[:rows, :] = joined[:rows, :]
+        for index, group in enumerate((mine, second, third)):
+            out[index * stride : (index + 1) * stride, :] = group[...]
         out[rows:, :BLOCK] = halo[:half, :]
         out[rows:, BLOCK:] = halo[half:, :]
 
@@ -253,9 +257,7 @@
     return near * (2.0 - value * near)
 
 
-def placed(joined, tiles):
-    stride = tiles + SUB
-    groups = [joined.at[i * stride : (i + 1) * stride] for i in range(3)]
+def placed(groups, tiles):
     parts = [halves_of(group[:tiles, :]) for group in groups]
     loads = jnp.concatenate([part[i] for i in range(2) for part in parts], 0)
     ids = jnp.concatenate([group[tiles : tiles + 1, :BLOCK] for group in groups], 1)
@@ -293,12 +295,15 @@
             factor[base + x, :, lanes] = scale[rows]
 
 
-def own_kernel(full, joined, window, _, constant, factor, weight, rows_at):
+def own_kernel(
+    full, mine, second, third, window, _message, _near, _far, constant, factor, weight, rows_at, ends
+):
     tiles = weight.shape[0]
     planes, height, width = constant.shape
     place = Place(full, height)
     zones = width // BLOCK
-    ids, gathered = placed(joined, tiles)
+    ends[...] = window[place.parity * (planes - 1)]
+    ids, gathered = placed((mine, second, third), tiles)
     coefficients(gathered, tiles, place.first, full, window, planes, constant, factor, 0, None)
     turned = [
         jnp.transpose(
@@ -306,15 +311,10 @@
         ).astype(jnp.int32)
         for i in range(3)
     ]
-
-    def before(places):
-        index = lax.rem(place.group + 3 - places, 3)
-        return jnp.where(index == 0, turned[0], jnp.where(index == 1, turned[1], turned[2]))
-
-    solid, drag = gathered(jnp.concatenate([before(0)] * 3, 1))
+    solid, drag = gathered(jnp.concatenate([turned[0]] * 3, 1))
     weight[...] = 1.0 / (1.0 / (1.0 + solid) + drag)
     for i in range(3):
-        block = before(i)
+        block = turned[i]
         line, zone = block // zones, block % zones
         x, y = line // full, line % full
         row = (x * zones + zone) * height + y - place.first
@@ -324,7 +324,7 @@
 
 def solve_kernel(
     full, sweeps, rows_at, joined_near, joined_far, window, near, far, beyond,
-    own_constant, own_factor, _near, _far, out_a, out_b, out_c,
+    own_constant, own_factor, out_a, out_b, out_c,
     constant, factor, old, new, fields,
 ):
     planes, height, width = own_constant.shape
@@ -337,7 +337,9 @@
         (joined_near, near, odd, jnp.where(odd, place.lower, place.upper)),
         (joined_far, far, jnp.logical_not(odd), jnp.where(odd, place.upper, place.lower)),
     ):
-        _, gathered = placed(joined, tiles)
+        stride = tiles + SUB
+        groups = [joined.at[i * stride : (i + 1) * stride] for i in range(3)]
+        _, gathered = placed(groups, tiles)
         coefficients(
             gathered, tiles, place.first, full, driven, planes, constant, factor,
             jnp.where(below, 0, planes), present,
@@ -470,65 +472,59 @@
 
     field = shaped(planes, height, width)
     plane = shaped(height, width)
-    window, ends, inner, dummy = call(
-        window_kernel, (shaped(2 * planes, height, width), plane, plane, shaped(SUB, BLOCK)),
+    small = shaped(SUB, BLOCK)
+    window, inner, after_window = call(
+        window_kernel, (shaped(2 * planes, height, width), plane, small),
         [HBM] * 3, (pressure_old, pressure_source, solid_old),
         [pltpu.VMEM((planes, height, width), F32), pltpu.SemaphoreType.DMA((3 * planes,))],
         flops=field_bytes, size=6 * field_bytes, limit=61_500_000,
     )
     near = along_reg(window, owners, (1, -1))
+    mine, after_deposit = call(
+        deposit_kernel, (shaped(tiles + SUB, 2 * BLOCK), small), [SMEM] + [VMEM] * 5,
+        (count, cell, vol, drag, ids, after_window), flops=2 * 32 * 48 * 65536, size=5 * 4 * slots,
+    )
+    second = along_grp(mine, 1, holders)
+    third = along_grp(mine, 2, holders)
     rows = halo_list.shape[1] // BLOCK
     halo = shaped(3 * rows, BLOCK)
     state, halo_near, halo_far, after_halo = call(
-        halo_kernel, (shaped(3 * tiles, BLOCK), halo, halo, shaped(SUB, BLOCK)),
-        [VMEM] * 4, (grain_pos, grain_vel, halo_list, dummy), flops=8 * 3 * 16384 * 128,
+        halo_kernel, (shaped(3 * tiles, BLOCK), halo, halo, small),
+        [VMEM] * 4, (grain_pos, grain_vel, halo_list, after_deposit), flops=2 * 3 * 8 * BLOCK * BLOCK * slots // 4,
         size=4 * 4 * 3 * slots,
     )
-    mine = call(
-        deposit_kernel, shaped(tiles + SUB, 2 * BLOCK), [SMEM] + [VMEM] * 5,
-        (count, cell, vol, drag, ids, after_halo), flops=2 * 32 * 48 * 65536, size=5 * 4 * slots,
-    )
-    joined = lax.all_gather(mine, "grp")
-    joined = joined.reshape(groups * (tiles + SUB), 2 * BLOCK)
+    far, after_forward = call(
+        forward_kernel, (shaped(2 * planes + 1, height, width), small), [VMEM] * 5,
+        (near, inner, after_halo, second, third), size=5 * field_bytes,
+    )
+    far = along_reg(far, owners, (2, -2))
     message = shaped(holding * (tiles + SUB) + 3 * rows // 2, 2 * BLOCK)
-    message_near, message_far = call(
-        message_kernel, (message,) * 2, [VMEM] * 3, (joined, halo_near, halo_far),
-        size=8 * 2 * BLOCK * 500,
+    message_near, message_far, after_message = call(
+        message_kernel, (message, message, small), [VMEM] * 6,
+        (mine, second, third, halo_near, halo_far, after_forward), size=8 * 2 * BLOCK * 500,
     )
     message_near = along_reg(message_near, owners, (1, -1))
     message_far = along_reg(message_far, owners, (-1, 1))
-    beyond = along_reg(ends, owners, (-2, 2))
-    far = along_reg(
-        call(
-            forward_kernel, shaped(2 * planes + 1, height, width), [VMEM] * 2 + [ANY] * 2,
-            (near, inner, joined, beyond),
-            size=5 * field_bytes,
-        ),
-        owners, (2, -2),
-    )
-
     others = [g for g in holders if g not in owners]
     halo_near = along_reg(halo_near, others, (1, -1))
     halo_far = along_reg(halo_far, others, (-1, 1))
-    constant, factor, weight, rows_at = call(
+    constant, factor, weight, rows_at, ends = call(
         functools.partial(own_kernel, full),
         (
             field, field, shaped(tiles, BLOCK),
-            jax.ShapeDtypeStruct((3 * tiles, BLOCK), jnp.int32),
+            jax.ShapeDtypeStruct((3 * tiles, BLOCK), jnp.int32), plane,
         ),
-        [VMEM] * 3, (joined, window, dummy),
+        [VMEM] * 7, (mine, second, third, window, after_message, halo_near, halo_far),
         flops=planes * height * 4 * 384 * 256 * 6, size=9 * field_bytes,
     )
+    beyond = along_reg(ends, owners, (-2, 2))
 
     grads = shaped(tiles, 3 * BLOCK)
     window_of = lambda count: pltpu.VMEM((count, height, width), F32)
     grads_a, grads_b, grads_c = call(
         functools.partial(solve_kernel, full, ITERS), (grads,) * 3,
-        [VMEM] * 9 + [ANY] * 2,
-        (
-            rows_at, message_near, message_far, window, near, far, beyond, constant, factor,
-            halo_near, halo_far,
-        ),
+        [VMEM] * 9,
+        (rows_at, message_near, message_far, window, near, far, beyond, constant, factor),
         [
             window_of(2 * planes), window_of(2 * planes),
             window_of(3 * planes + 2), window_of(3 * planes + 2),

time: 62.5 us -> 61.9 us (level)
  blocking collectives: 7.36 us -> 0 us
  starting transfers between devices: 19.6 us -> 24.8 us
  waiting for transfers between devices: 11.2 us -> 12.7 us
    all_gather x1 -> x0, blocking collectives: 7.36 us -> none  [on_device(): joined = lax.all_gather(mine, 'grp')]
    ppermute x9 -> x11, starting transfers between devices: 19.6 us -> 24.8 us  [send(): return lax.ppermute(value, ('grp', 'reg'), flat)]
    ppermute x9 -> x11, waiting for transfers between devices: 11.2 us -> 12.7 us  [send(): return lax.ppermute(value, ('grp', 'reg'), flat)]
  transfers between devices with their start and end apart: 9 -> 11, of which waited for: 3 -> 4; matrix products, arithmetic and copies ran while one was open for 0% -> 0% of each run, Pallas kernels for 17% -> 17%
where the time goes in v8:
time: 61.9 us; the launch traced here: 61.5 us
  starting transfers between devices  24.8 us (40%)
  Pallas kernels  22.2 us (36%)
  waiting for transfers between devices  12.7 us (21%)
  between operations  0.99 us (2%)
  local copies, waits for them, and re-layouts  0.73 us (1%)
    ppermute x11, starting transfers between devices, send(): return lax.ppermute(value, ('grp', 'reg'), flat)  24.8 us
    pallas_call x9, Pallas kernels, call(): pl.pallas_call(kernel, out_shape=outs, in_specs=specs, out_specs=jax.tree...  22.2 us
    ppermute x11, waiting for transfers between devices, send(): return lax.ppermute(value, ('grp', 'reg'), flat)  12.7 us
  transfers between devices with their start and end apart: 11, of which 4 were waited for; matrix products, arithmetic and copies ran while one was open for 0% of the time, Pallas kernels for 17%

profile of v8, /device:TPU:0, one launch (start us, length us, event | category | flops | bytes accessed | tf_op | source)
XLA Modules:
  0.0 61.5 jit_solution(781298569611635383)
XLA Ops:
  0.0 2.8 %shard_map.136 = (f32[8,72,512]{2,1,0:T(8,128)}, f32[72,512]{1,0:T(8,128)}, f32[8,128]{1,0:T(8,128)}) custom-call(f32[4,128,512]{2,1,0:T(8,128)} %pressure_old.1, f32[4,128,512]{2,1,0:T(8,128)} %source.1, f32[4,128,512]{2,1,0:T(8,128)} %solid_before.1), custom_call_target="tpu_custom_call" | custom-call | flops 589824 | bytes 3538944 | tf_op jit(solution)/shard_map/pallas_call | solution.py:35
  2.9 4.9 %collective-permute-start.2 = (f32[8,72,512]{2,1,0:T(8,128)}, f32[8,72,512]{2,1,0:T(8,128)S(1)}, u32[]{:S(2)}, u32[]{:S(2)}) collective-permute-start(f32[8,72,512]{2,1,0:T(8,128)} %get-tuple-element.29.window), channel_id=1, source_target_pairs={{0,1},{1,0},{2,3},{3,2},{4,5},{5,4},{6,7},{7,6},{16,17},{17,16},{1... | collective-permute-start | bytes 3538952 | tf_op jit(solution)/shard_map/ppermute | solution.py:451
  8.5 0.7 %copy-done.11 = f32[8,128]{1,0:T(8,128)S(1)} copy-done((f32[8,128]{1,0:T(8,128)S(1)}, f32[8,128]{1,0:T(8,128)}, u32[]{:S(2)}) %copy-start.11) | copy-done | bytes 4120
  9.1 1.7 %shard_map.137 = (f32[136,256]{1,0:T(8,128)S(1)}, f32[8,128]{1,0:T(8,128)S(1)}) custom-call(s32[1]{0:T(128)S(6)} %copy.15.count, s32[128,128]{1,0:T(8,128)S(1)} %bitcast.4, f32[128,128]{1,0:T(8,128)S(1)} %bitcast.6, f32[128,128]{1,0:T(8,128)S(1)} %bitcast.8, s32[1,128]{1,0:T(1,128)S(1)} %bitcast.10, f32[8,128]{1,0:T(8,128)S(1)} %copy-done.11), custom_call_target="tpu_custom_call" | custom-call | flops 201326592 | bytes 327680 | tf_op jit(solution)/shard_map/pallas_call | solution.py:35
  10.8 3.4 %collective-permute-start.1 = (f32[136,256]{1,0:T(8,128)S(1)}, f32[136,256]{1,0:T(8,128)S(1)}, u32[]{:S(2)}, u32[]{:S(2)}) collective-permute-start(f32[136,256]{1,0:T(8,128)S(1)} %get-tuple-element.28.mine), channel_id=1, source_target_pairs={{0,16},{1,17},{2,18},{3,19},{4,20},{5,21},{6,22},{7,23},{8,0},{9,1... | collective-permute-start | bytes 417800 | tf_op jit(solution)/shard_map/ppermute | solution.py:451
  14.2 1.9 %collective-permute-start = (f32[136,256]{1,0:T(8,128)S(1)}, f32[136,256]{1,0:T(8,128)S(1)}, u32[]{:S(2)}, u32[]{:S(2)}) collective-permute-start(f32[136,256]{1,0:T(8,128)S(1)} %get-tuple-element.28.mine), channel_id=1, source_target_pairs={{0,8},{1,9},{2,10},{3,11},{4,12},{5,13},{6,14},{7,15},{8,16},{9,17... | collective-permute-start | bytes 417800 | tf_op jit(solution)/shard_map/ppermute | solution.py:451
  16.2 3.5 %shard_map.138 = (f32[384,128]{1,0:T(8,128)S(1)}, f32[96,128]{1,0:T(8,128)S(1)}, f32[96,128]{1,0:T(8,128)S(1)}, f32[8,128]{1,0:T(8,128)S(1)}) custom-call(f32[3,16384]{1,0:T(4,128)S(1)} %copy-done.9, f32[3,16384]{1,0:T(4,128)S(1)} %copy-done.3, s32[2,4096]{1,0:T(2,128)S(1)} %copy-done.10, f32[8,128]{1,0:T(8,128)S(1)} %get-tuple-element.30._), custom_call_target="tpu_custom_call" | custom-call | flops 3221225472 | bytes 786432 | tf_op jit(solution)/shard_map/pallas_call | solution.py:35
  19.8 1.4 %collective-permute-done._second.second = f32[136,256]{1,0:T(8,128)S(1)} collective-permute-done((f32[136,256]{1,0:T(8,128)S(1)}, f32[136,256]{1,0:T(8,128)S(1)}, u32[]{:S(2)}, u32[]{:S(2)}) %collective-permute-start) | collective-permute-done | bytes 139296 | tf_op jit(solution)/shard_map/ppermute | solution.py:451
  21.2 1.0 %collective-permute-done.2.near = f32[8,72,512]{2,1,0:T(8,128)S(1)} collective-permute-done((f32[8,72,512]{2,1,0:T(8,128)}, f32[8,72,512]{2,1,0:T(8,128)S(1)}, u32[]{:S(2)}, u32[]{:S(2)}) %collective-permute-start.2) | collective-permute-done | bytes 1179680 | tf_op jit(solution)/shard_map/ppermute | solution.py:451
  22.1 0.1 shard_map.139
  22.2 4.1 %collective-permute-start.7 = (f32[9,72,512]{2,1,0:T(8,128)S(1)}, f32[9,72,512]{2,1,0:T(8,128)S(1)}, u32[]{:S(2)}, u32[]{:S(2)}) collective-permute-start(f32[9,72,512]{2,1,0:T(8,128)S(1)} %get-tuple-element.40), channel_id=1, source_target_pairs={{0,2},{2,4},{3,1},{4,6},{5,3},{7,5},{16,18},{18,20},{19,17},{20,22... | collective-permute-start | bytes 3981320 | tf_op jit(solution)/shard_map/ppermute | solution.py:451
  26.4 1.9 %collective-permute-start.5 = (f32[456,256]{1,0:T(8,128)S(1)}, f32[456,256]{1,0:T(8,128)S(1)}, u32[]{:S(2)}, u32[]{:S(2)}) collective-permute-start(f32[456,256]{1,0:T(8,128)S(1)} %get-tuple-element.38), channel_id=1, source_target_pairs={{0,1},{1,0},{2,3},{3,2},{4,5},{5,4},{6,7},{7,6},{16,17},{17,16},{1... | collective-permute-start | bytes 1400840 | tf_op jit(solution)/shard_map/ppermute | solution.py:451
  28.3 0.7 %collective-permute-start.6 = (f32[456,256]{1,0:T(8,128)S(1)}, f32[456,256]{1,0:T(8,128)S(1)}, u32[]{:S(2)}, u32[]{:S(2)}) collective-permute-start(f32[456,256]{1,0:T(8,128)S(1)} %get-tuple-element.39), channel_id=1, source_target_pairs={{1,2},{2,1},{3,4},{4,3},{5,6},{6,5},{17,18},{18,17},{19,20},{20,19... | collective-permute-start | bytes 1400840 | tf_op jit(solution)/shard_map/ppermute | solution.py:451
  29.0 0.7 %collective-permute-start.3 = (f32[96,128]{1,0:T(8,128)S(1)}, f32[96,128]{1,0:T(8,128)S(1)}, u32[]{:S(2)}, u32[]{:S(2)}) collective-permute-start(f32[96,128]{1,0:T(8,128)S(1)} %get-tuple-element.31.halo_near), channel_id=1, source_target_pairs={{8,9},{9,8},{10,11},{11,10},{12,13},{13,12},{14,15},{15,14}} | collective-permute-start | bytes 147464 | tf_op jit(solution)/shard_map/ppermute | solution.py:451
  29.7 0.7 %collective-permute-start.4 = (f32[96,128]{1,0:T(8,128)S(1)}, f32[96,128]{1,0:T(8,128)S(1)}, u32[]{:S(2)}, u32[]{:S(2)}) collective-permute-start(f32[96,128]{1,0:T(8,128)S(1)} %get-tuple-element.32.halo_far), channel_id=1, source_target_pairs={{9,10},{10,9},{11,12},{12,11},{13,14},{14,13}} | collective-permute-start | bytes 147464 | tf_op jit(solution)/shard_map/ppermute | solution.py:451
  30.4 1.2 %shard_map.141 = (f32[4,72,512]{2,1,0:T(8,128)S(1)}, f32[4,72,512]{2,1,0:T(8,128)S(1)}, f32[128,128]{1,0:T(8,128)S(1)}, s32[384,128]{1,0:T(8,128)S(1)}, f32[72,512]{1,0:T(8,128)S(1)}) custom-call(f32[136,256]{1,0:T(8,128)S(1)} %get-tuple-element.28.mine, f32[136,256]{1,0:T(8,128)S(1)} %collective-permute-done._second.second, ...), custom_call_target="tpu_custom_call" | custom-call | flops 679477248 | bytes 5308416 | tf_op jit(solution)/shard_map/pallas_call | solution.py:35
  31.6 1.3 %collective-permute-start.8 = (f32[72,512]{1,0:T(8,128)S(1)}, f32[72,512]{1,0:T(8,128)S(1)}, u32[]{:S(2)}, u32[]{:S(2)}) collective-permute-start(f32[72,512]{1,0:T(8,128)S(1)} %get-tuple-element.41), channel_id=1, source_target_pairs={{1,3},{2,0},{3,5},{4,2},{5,7},{6,4},{17,19},{18,16},{19,21},{20,18... | collective-permute-start | bytes 442376 | tf_op jit(solution)/shard_map/ppermute | solution.py:451
  32.9 9.0 %collective-permute-done.8.beyond = f32[72,512]{1,0:T(8,128)S(1)} collective-permute-done((f32[72,512]{1,0:T(8,128)S(1)}, f32[72,512]{1,0:T(8,128)S(1)}, u32[]{:S(2)}, u32[]{:S(2)}) %collective-permute-start.8) | collective-permute-done | bytes 147488 | tf_op jit(solution)/shard_map/ppermute | solution.py:451
  41.9 7.6 %shard_map.142 = (f32[128,384]{1,0:T(8,128)S(1)}, f32[128,384]{1,0:T(8,128)S(1)}, f32[128,384]{1,0:T(8,128)S(1)}) custom-call(s32[384,128]{1,0:T(8,128)S(1)} %get-tuple-element.37.rows_at, f32[456,256]{1,0:T(8,128)S(1)} %collective-permute-done.5.joined_near.message_near, f32[456,256]{1,0:T(8,128)S(1)} %collective-permute-done.6.joined_far.message_far, ...), custom_call_target="tpu_custom_call" | custom-call | flops 1358954496 | bytes 11796480 | tf_op jit(solution)/shard_map/pallas_call | solution.py:35
  49.5 3.4 %collective-permute-start.9 = (f32[128,384]{1,0:T(8,128)S(1)}, f32[128,384]{1,0:T(8,128)S(1)}, u32[]{:S(2)}, u32[]{:S(2)}) collective-permute-start(f32[128,384]{1,0:T(8,128)S(1)} %get-tuple-element.45), channel_id=1, source_target_pairs={{0,16},{1,17},{2,18},{3,19},{4,20},{5,21},{6,22},{7,23},{16,8},{17... | collective-permute-start | bytes 589832 | tf_op jit(solution)/shard_map/ppermute | solution.py:451
  52.9 1.9 %collective-permute-start.10 = (f32[128,384]{1,0:T(8,128)S(1)}, f32[128,384]{1,0:T(8,128)S(1)}, u32[]{:S(2)}, u32[]{:S(2)}) collective-permute-start(f32[128,384]{1,0:T(8,128)S(1)} %get-tuple-element.46), channel_id=1, source_target_pairs={{0,8},{1,9},{2,10},{3,11},{4,12},{5,13},{6,14},{7,15},{16,0},{17,1... | collective-permute-start | bytes 589832 | tf_op jit(solution)/shard_map/ppermute | solution.py:451
  54.8 4.2 %shard_map.143.contact = f32[384,128]{1,0:T(8,128)S(1)} custom-call(s32[128]{0:T(128)S(1)} %copy-done.8, f32[384,128]{1,0:T(8,128)S(1)} %get-tuple-element.48.state, f32[456,256]{1,0:T(8,128)S(1)} %collective-permute-done.5.joined_near.message_near, f32[456,256]{1,0:T(8,128)S(1)} %collective-permute-done.6.joined_far.message_far, ...), custom_call_target="tpu_custom_call" | custom-call | flops 7864320 | bytes 1310720 | tf_op jit(solution)/shard_map/pallas_call | solution.py:35
  59.1 1.4 %collective-permute-done.10.grads_c = f32[128,384]{1,0:T(8,128)S(1)} collective-permute-done((f32[128,384]{1,0:T(8,128)S(1)}, f32[128,384]{1,0:T(8,128)S(1)}, u32[]{:S(2)}, u32[]{:S(2)}) %collective-permute-start.10) | collective-permute-done | bytes 196640 | tf_op jit(solution)/shard_map/ppermute | solution.py:451
  60.4 1.0 %shard_map.144 = f32[3,16384]{1,0:T(4,128)} custom-call(s32[1]{0:T(128)S(6)} %copy.15.count, f32[128,384]{1,0:T(8,128)S(1)} %get-tuple-element.44._.grads_a, f32[128,384]{1,0:T(8,128)S(1)} %collective-permute-done.9.grads_b, f32[128,384]{1,0:T(8,128)S(1)} %collective-permute-done.10.grads_c, f32[128,128]{1,0:T(8,128)S(1)} %get-tuple-element.47.weight, ...), custom_call_target="tpu_custom_call" | custom-call | flops 983040 | bytes 1310720 | tf_op jit(solution)/shard_map/pallas_call | solution.py:35
  (33 shorter events, 0.1 us)
Async XLA Ops:
  0.0 8.4 %copy-start.12 = (s32[128]{0:T(128)S(1)}, s32[128]{0:T(128)}, u32[]{:S(2)}) copy-start(s32[128]{0:T(128)} %param.24) | copy-start | bytes 1540
  0.0 8.4 %copy-start.5 = (s32[16384]{0:T(1024)S(1)}, s32[16384]{0:T(1024)}, u32[]{:S(2)}) copy-start(s32[16384]{0:T(1024)} %param.23) | copy-start | bytes 196612
  0.0 8.4 %copy-start.7 = (f32[16384]{0:T(1024)S(1)}, f32[16384]{0:T(1024)}, u32[]{:S(2)}) copy-start(f32[16384]{0:T(1024)} %param.17) | copy-start | bytes 196612
  0.0 8.4 %copy-start.6 = (f32[16384]{0:T(1024)S(1)}, f32[16384]{0:T(1024)}, u32[]{:S(2)}) copy-start(f32[16384]{0:T(1024)} %param.16) | copy-start | bytes 196612
  0.0 16.2 %copy-start.3 = (f32[3,16384]{1,0:T(4,128)S(1)}, f32[3,16384]{1,0:T(4,128)}, u32[]{:S(2)}) copy-start(f32[3,16384]{1,0:T(4,128)} %vel.3) | copy-start | bytes 589828
  0.0 16.2 %copy-start.10 = (s32[2,4096]{1,0:T(2,128)S(1)}, s32[2,4096]{1,0:T(2,128)}, u32[]{:S(2)}) copy-start(s32[2,4096]{1,0:T(2,128)} %lists.1) | copy-start | bytes 98308
  0.0 16.2 %copy-start.9 = (f32[3,16384]{1,0:T(4,128)S(1)}, f32[3,16384]{1,0:T(4,128)}, u32[]{:S(2)}) copy-start(f32[3,16384]{1,0:T(4,128)} %pos.1) | copy-start | bytes 589828
  2.9 19.3 %collective-permute-start.2 = (f32[8,72,512]{2,1,0:T(8,128)}, f32[8,72,512]{2,1,0:T(8,128)S(1)}, u32[]{:S(2)}, u32[]{:S(2)}) collective-permute-start(f32[8,72,512]{2,1,0:T(8,128)} %get-tuple-element.29.window), channel_id=1, source_target_pairs={{0,1},{1,0},{2,3},{3,2},{4,5},{5,4},{6,7},{7,6},{16,17},{17,16},{1... | collective-permute-start | bytes 3538952 | tf_op jit(solution)/shard_map/ppermute | solution.py:451
  8.4 0.7 %copy-start.11 = (f32[8,128]{1,0:T(8,128)S(1)}, f32[8,128]{1,0:T(8,128)}, u32[]{:S(2)}) copy-start(f32[8,128]{1,0:T(8,128)} %get-tuple-element.27._) | copy-start | bytes 12292
  10.8 8.9 %collective-permute-start.1 = (f32[136,256]{1,0:T(8,128)S(1)}, f32[136,256]{1,0:T(8,128)S(1)}, u32[]{:S(2)}, u32[]{:S(2)}) collective-permute-start(f32[136,256]{1,0:T(8,128)S(1)} %get-tuple-element.28.mine), channel_id=1, source_target_pairs={{0,16},{1,17},{2,18},{3,19},{4,20},{5,21},{6,22},{7,23},{8,0},{9,1... | collective-permute-start | bytes 417800 | tf_op jit(solution)/shard_map/ppermute | solution.py:451
  14.2 6.9 %collective-permute-start = (f32[136,256]{1,0:T(8,128)S(1)}, f32[136,256]{1,0:T(8,128)S(1)}, u32[]{:S(2)}, u32[]{:S(2)}) collective-permute-start(f32[136,256]{1,0:T(8,128)S(1)} %get-tuple-element.28.mine), channel_id=1, source_target_pairs={{0,8},{1,9},{2,10},{3,11},{4,12},{5,13},{6,14},{7,15},{8,16},{9,17... | collective-permute-start | bytes 417800 | tf_op jit(solution)/shard_map/ppermute | solution.py:451
  16.2 6.0 %copy-start.4 = (f32[72,512]{1,0:T(8,128)S(1)}, f32[72,512]{1,0:T(8,128)}, u32[]{:S(2)}) copy-start(f32[72,512]{1,0:T(8,128)} %get-tuple-element.33.inner) | copy-start | bytes 442372
  19.7 10.6 %copy-start = (f32[8,72,512]{2,1,0:T(8,128)S(1)}, f32[8,72,512]{2,1,0:T(8,128)}, u32[]{:S(2)}) copy-start(f32[8,72,512]{2,1,0:T(8,128)} %get-tuple-element.29.window) | copy-start | bytes 3538948
  22.2 19.6 %collective-permute-start.7 = (f32[9,72,512]{2,1,0:T(8,128)S(1)}, f32[9,72,512]{2,1,0:T(8,128)S(1)}, u32[]{:S(2)}, u32[]{:S(2)}) collective-permute-start(f32[9,72,512]{2,1,0:T(8,128)S(1)} %get-tuple-element.40), channel_id=1, source_target_pairs={{0,2},{2,4},{3,1},{4,6},{5,3},{7,5},{16,18},{18,20},{19,17},{20,22... | collective-permute-start | bytes 3981320 | tf_op jit(solution)/shard_map/ppermute | solution.py:451
  26.4 15.5 %collective-permute-start.5 = (f32[456,256]{1,0:T(8,128)S(1)}, f32[456,256]{1,0:T(8,128)S(1)}, u32[]{:S(2)}, u32[]{:S(2)}) collective-permute-start(f32[456,256]{1,0:T(8,128)S(1)} %get-tuple-element.38), channel_id=1, source_target_pairs={{0,1},{1,0},{2,3},{3,2},{4,5},{5,4},{6,7},{7,6},{16,17},{17,16},{1... | collective-permute-start | bytes 1400840 | tf_op jit(solution)/shard_map/ppermute | solution.py:451
  28.3 13.5 %collective-permute-start.6 = (f32[456,256]{1,0:T(8,128)S(1)}, f32[456,256]{1,0:T(8,128)S(1)}, u32[]{:S(2)}, u32[]{:S(2)}) collective-permute-start(f32[456,256]{1,0:T(8,128)S(1)} %get-tuple-element.39), channel_id=1, source_target_pairs={{1,2},{2,1},{3,4},{4,3},{5,6},{6,5},{17,18},{18,17},{19,20},{20,19... | collective-permute-start | bytes 1400840 | tf_op jit(solution)/shard_map/ppermute | solution.py:451
  29.0 1.3 %collective-permute-start.3 = (f32[96,128]{1,0:T(8,128)S(1)}, f32[96,128]{1,0:T(8,128)S(1)}, u32[]{:S(2)}, u32[]{:S(2)}) collective-permute-start(f32[96,128]{1,0:T(8,128)S(1)} %get-tuple-element.31.halo_near), channel_id=1, source_target_pairs={{8,9},{9,8},{10,11},{11,10},{12,13},{13,12},{14,15},{15,14}} | collective-permute-start | bytes 147464 | tf_op jit(solution)/shard_map/ppermute | solution.py:451
  29.7 0.7 %collective-permute-start.4 = (f32[96,128]{1,0:T(8,128)S(1)}, f32[96,128]{1,0:T(8,128)S(1)}, u32[]{:S(2)}, u32[]{:S(2)}) collective-permute-start(f32[96,128]{1,0:T(8,128)S(1)} %get-tuple-element.32.halo_far), channel_id=1, source_target_pairs={{9,10},{10,9},{11,12},{12,11},{13,14},{14,13}} | collective-permute-start | bytes 147464 | tf_op jit(solution)/shard_map/ppermute | solution.py:451
  31.6 10.3 %collective-permute-start.8 = (f32[72,512]{1,0:T(8,128)S(1)}, f32[72,512]{1,0:T(8,128)S(1)}, u32[]{:S(2)}, u32[]{:S(2)}) collective-permute-start(f32[72,512]{1,0:T(8,128)S(1)} %get-tuple-element.41), channel_id=1, source_target_pairs={{1,3},{2,0},{3,5},{4,2},{5,7},{6,4},{17,19},{18,16},{19,21},{20,18... | collective-permute-start | bytes 442376 | tf_op jit(solution)/shard_map/ppermute | solution.py:451
  41.8 13.0 %copy-start.1 = (s32[8,16384]{1,0:T(8,128)S(1)}, s32[8,16384]{1,0:T(8,128)}, u32[]{:S(2)}) copy-start(s32[8,16384]{1,0:T(8,128)} %named.1) | copy-start | bytes 1572868
  41.9 13.0 %copy-start.2 = (f32[8,16384]{1,0:T(8,128)S(1)}, f32[8,16384]{1,0:T(8,128)}, u32[]{:S(2)}) copy-start(f32[8,16384]{1,0:T(8,128)} %stiff.1) | copy-start | bytes 1572868
  41.9 13.0 %copy-start.8 = (s32[128]{0:T(128)S(1)}, s32[128]{0:T(128)}, u32[]{:S(2)}) copy-start(s32[128]{0:T(128)} %partner.1) | copy-start | bytes 1540
  49.5 9.6 %collective-permute-start.9 = (f32[128,384]{1,0:T(8,128)S(1)}, f32[128,384]{1,0:T(8,128)S(1)}, u32[]{:S(2)}, u32[]{:S(2)}) collective-permute-start(f32[128,384]{1,0:T(8,128)S(1)} %get-tuple-element.45), channel_id=1, source_target_pairs={{0,16},{1,17},{2,18},{3,19},{4,20},{5,21},{6,22},{7,23},{16,8},{17... | collective-permute-start | bytes 589832 | tf_op jit(solution)/shard_map/ppermute | solution.py:451
  52.9 7.6 %collective-permute-start.10 = (f32[128,384]{1,0:T(8,128)S(1)}, f32[128,384]{1,0:T(8,128)S(1)}, u32[]{:S(2)}, u32[]{:S(2)}) collective-permute-start(f32[128,384]{1,0:T(8,128)S(1)} %get-tuple-element.46), channel_id=1, source_target_pairs={{0,8},{1,9},{2,10},{3,11},{4,12},{5,13},{6,14},{7,15},{16,0},{17,1... | collective-permute-start | bytes 589832 | tf_op jit(solution)/shard_map/ppermute | solution.py:451

commit v9 on v8

--- a/solution.py
+++ b/solution.py
@@ -31,12 +31,12 @@
     return jax.ShapeDtypeStruct(dims, F32)
 
 
-def call(kernel, outs, specs, args, scratch=(), flops=0, size=0, limit=40_000_000):
+def call(kernel, outs, specs, args, scratch=(), flops=0, size=0, limit=40_000_000, place=VMEM):
     return pl.pallas_call(
         kernel,
         out_shape=outs,
         in_specs=specs,
-        out_specs=jax.tree.map(lambda _: VMEM, outs),
+        out_specs=jax.tree.map(lambda _: place, outs),
         scratch_shapes=list(scratch),
         compiler_params=pltpu.CompilerParams(vmem_limit_bytes=limit),
         cost_estimate=pl.CostEstimate(flops=flops, bytes_accessed=size, transcendentals=0),
@@ -66,25 +66,37 @@
     return high, (value - high.astype(F32)).astype(BF16)
 
 
-def window_kernel(pressure_old, source, solid_before, window, inner, dummy, solid, sems):
+def window_kernel(pressure_old, source, solid_before, window, inner, driven, solid, sems):
     planes, height, _ = solid.shape
     place = Place(pressure_old.shape[1], height)
     rows = pl.ds(place.first, height)
-    copies = []
-    for x in range(planes):
-        for whole, part in (
-            (pressure_old, window.at[x]), (source, window.at[planes + x]), (solid_before, solid.at[x])
-        ):
-            copies.append(
-                pltpu.make_async_copy(whole.at[x, rows, :], part, sems.at[len(copies)])
-            )
-    for copy in copies:
-        copy.start()
-    dummy[...] = jnp.zeros(dummy.shape, F32)
-    for copy in copies:
-        copy.wait()
-    window[planes:] = window[planes:] - solid[...]
-    inner[...] = window[(1 - place.parity) * (planes - 1)]
+    end = (1 - place.parity) * (planes - 1)
+    copy = lambda whole, part, index: pltpu.make_async_copy(whole, part, sems.at[index])
+    fetched = [
+        (
+            copy(source.at[x, rows, :], driven.at[x], 2 * x),
+            copy(solid_before.at[x, rows, :], solid.at[x], 2 * x + 1),
+        )
+        for x in range(planes)
+    ]
+    straight = [
+        copy(pressure_old.at[x, rows, :], window.at[x], 2 * planes + x) for x in range(planes)
+    ] + [copy(pressure_old.at[end, rows, :], inner, 3 * planes)]
+    for pair in fetched:
+        for one in pair:
+            one.start()
+    for one in straight:
+        one.start()
+    stored = [
+        copy(driven.at[x], window.at[planes + x], 3 * planes + 1 + x) for x in range(planes)
+    ]
+    for x, pair in enumerate(fetched):
+        for one in pair:
+            one.wait()
+        driven[x] = driven[x] - solid[x]
+        stored[x].start()
+    for one in straight + stored:
+        one.wait()
 
 
 def forward_kernel(near, inner, _halo, _second, _third, out, dummy):
@@ -94,7 +106,7 @@
     out[count] = inner[...]
 
 
-def deposit_kernel(count, cell, vol, drag, ids, _, out, dummy):
+def deposit_kernel(count, cell, vol, drag, ids, out, dummy):
     dummy[...] = jnp.zeros(dummy.shape, F32)
     tiles = cell.shape[0]
     sub = iota((SUB, BLOCK), 0)
@@ -182,7 +194,7 @@
                     ]
             return carry
 
-        lax.fori_loop(0, rows // 2, step, 0, unroll=4)
+        lax.fori_loop(0, rows // 2, step, 0, unroll=8)
 
 
 def message_kernel(mine, second, third, halo_near, halo_far, _, near, far, dummy):
@@ -361,10 +373,10 @@
 
             return plane
 
-        lax.fori_loop(depth, rim, over(constant, factor, 1), 0, unroll=2)
-        lax.fori_loop(rim, rim + planes, over(own_constant, own_factor, rim), 0, unroll=2)
+        lax.fori_loop(depth, rim, over(constant, factor, 1), 0, unroll=4)
+        lax.fori_loop(rim, rim + planes, over(own_constant, own_factor, rim), 0, unroll=4)
         lax.fori_loop(
-            rim + planes, 3 * planes + 2 - depth, over(constant, factor, 1 + planes), 0, unroll=2
+            rim + planes, 3 * planes + 2 - depth, over(constant, factor, 1 + planes), 0, unroll=4
         )
 
     for index in range(sweeps):
@@ -384,7 +396,7 @@
                 )
         return carry
 
-    lax.fori_loop(0, planes, gradient, 0, unroll=2)
+    lax.fori_loop(0, planes, gradient, 0, unroll=4)
     wanted = jnp.concatenate([rows_at[...]] * (planes * zones * height // BLOCK), 1)
     hot = jnp.where(wanted == iota(wanted.shape, 1), 1.0, 0.0).astype(BF16)
     pieces = jnp.concatenate(halves_of(fields[...]), 1)
@@ -473,16 +485,17 @@
     field = shaped(planes, height, width)
     plane = shaped(height, width)
     small = shaped(SUB, BLOCK)
-    window, inner, after_window = call(
-        window_kernel, (shaped(2 * planes, height, width), plane, small),
+    window, inner = call(
+        window_kernel, (shaped(2 * planes, height, width), plane),
         [HBM] * 3, (pressure_old, pressure_source, solid_old),
-        [pltpu.VMEM((planes, height, width), F32), pltpu.SemaphoreType.DMA((3 * planes,))],
-        flops=field_bytes, size=6 * field_bytes, limit=61_500_000,
+        [pltpu.VMEM((planes, height, width), F32)] * 2
+        + [pltpu.SemaphoreType.DMA((4 * planes + 1,))],
+        flops=field_bytes, size=6 * field_bytes, limit=61_950_000, place=HBM,
     )
     near = along_reg(window, owners, (1, -1))
     mine, after_deposit = call(
-        deposit_kernel, (shaped(tiles + SUB, 2 * BLOCK), small), [SMEM] + [VMEM] * 5,
-        (count, cell, vol, drag, ids, after_window), flops=2 * 32 * 48 * 65536, size=5 * 4 * slots,
+        deposit_kernel, (shaped(tiles + SUB, 2 * BLOCK), small), [SMEM] + [VMEM] * 4,
+        (count, cell, vol, drag, ids), flops=2 * 32 * 48 * 65536, size=5 * 4 * slots,
     )
     second = along_grp(mine, 1, holders)
     third = along_grp(mine, 2, holders)

time: 61.9 us -> 82.5 us (1.33)
  Pallas kernels: 22.2 us -> 42.6 us
  waiting for transfers between devices: 12.7 us -> 13.7 us
    pallas_call x9, Pallas kernels: 22.2 us -> 42.6 us  [call(): pl.pallas_call(kernel, out_shape=outs, in_specs=specs, out_specs=jax.tree...]
    ppermute x11, waiting for transfers between devices: 12.7 us -> 13.7 us  [send(): return lax.ppermute(value, ('grp', 'reg'), flat)]
  transfers between devices with their start and end apart: 11 -> 11, of which waited for: 4 -> 4; matrix products, arithmetic and copies ran while one was open for 0% -> 0% of each run, Pallas kernels for 17% -> 13%
where the time goes in v9:
time: 82.5 us; the launch traced here: 82.1 us
  Pallas kernels  42.6 us (52%)
  starting transfers between devices  24.8 us (30%)
  waiting for transfers between devices  13.7 us (17%)
  between operations  0.98 us (1%)
    pallas_call x9, Pallas kernels, call(): pl.pallas_call(kernel, out_shape=outs, in_specs=specs, out_specs=jax.tree...  42.6 us
    ppermute x11, starting transfers between devices, send(): return lax.ppermute(value, ('grp', 'reg'), flat)  24.8 us
    ppermute x11, waiting for transfers between devices, send(): return lax.ppermute(value, ('grp', 'reg'), flat)  13.7 us
  transfers between devices with their start and end apart: 11, of which 4 were waited for; matrix products, arithmetic and copies ran while one was open for 0% of the time, Pallas kernels for 13%

profile of v9, /device:TPU:0, one launch (start us, length us, event | category | flops | bytes accessed | tf_op | source)
XLA Modules:
  0.0 82.1 jit_solution(3258107956973206067)
XLA Ops:
  0.0 23.6 %shard_map.137 = (f32[8,72,512]{2,1,0:T(8,128)}, f32[72,512]{1,0:T(8,128)}) custom-call(f32[4,128,512]{2,1,0:T(8,128)} %pressure_old.1, f32[4,128,512]{2,1,0:T(8,128)} %source.1, f32[4,128,512]{2,1,0:T(8,128)} %solid_before.1), custom_call_target="tpu_custom_call" | custom-call | flops 589824 | bytes 3538944 | tf_op jit(solution)/shard_map/pallas_call | solution.py:35
  23.7 4.9 %collective-permute-start.2 = (f32[8,72,512]{2,1,0:T(8,128)}, f32[8,72,512]{2,1,0:T(8,128)S(1)}, u32[]{:S(2)}, u32[]{:S(2)}) collective-permute-start(f32[8,72,512]{2,1,0:T(8,128)} %get-tuple-element.27.window), channel_id=1, source_target_pairs={{0,1},{1,0},{2,3},{3,2},{4,5},{5,4},{6,7},{7,6},{16,17},{17,16},{1... | collective-permute-start | bytes 3538952 | tf_op jit(solution)/shard_map/ppermute | solution.py:463
  29.2 1.7 %shard_map.136 = (f32[136,256]{1,0:T(8,128)S(1)}, f32[8,128]{1,0:T(8,128)S(1)}) custom-call(s32[1]{0:T(128)S(6)} %copy.15.count, s32[128,128]{1,0:T(8,128)S(1)} %bitcast.4, f32[128,128]{1,0:T(8,128)S(1)} %bitcast.6, f32[128,128]{1,0:T(8,128)S(1)} %bitcast.8, s32[1,128]{1,0:T(1,128)S(1)} %bitcast.10), custom_call_target="tpu_custom_call" | custom-call | flops 201326592 | bytes 327680 | tf_op jit(solution)/shard_map/pallas_call | solution.py:35
  31.0 3.4 %collective-permute-start.1 = (f32[136,256]{1,0:T(8,128)S(1)}, f32[136,256]{1,0:T(8,128)S(1)}, u32[]{:S(2)}, u32[]{:S(2)}) collective-permute-start(f32[136,256]{1,0:T(8,128)S(1)} %get-tuple-element.26.mine), channel_id=1, source_target_pairs={{0,16},{1,17},{2,18},{3,19},{4,20},{5,21},{6,22},{7,23},{8,0},{9,1... | collective-permute-start | bytes 417800 | tf_op jit(solution)/shard_map/ppermute | solution.py:463
  34.4 1.9 %collective-permute-start = (f32[136,256]{1,0:T(8,128)S(1)}, f32[136,256]{1,0:T(8,128)S(1)}, u32[]{:S(2)}, u32[]{:S(2)}) collective-permute-start(f32[136,256]{1,0:T(8,128)S(1)} %get-tuple-element.26.mine), channel_id=1, source_target_pairs={{0,8},{1,9},{2,10},{3,11},{4,12},{5,13},{6,14},{7,15},{8,16},{9,17... | collective-permute-start | bytes 417800 | tf_op jit(solution)/shard_map/ppermute | solution.py:463
  36.3 3.2 %shard_map.138 = (f32[384,128]{1,0:T(8,128)S(1)}, f32[96,128]{1,0:T(8,128)S(1)}, f32[96,128]{1,0:T(8,128)S(1)}, f32[8,128]{1,0:T(8,128)S(1)}) custom-call(f32[3,16384]{1,0:T(4,128)S(1)} %copy-done.9, f32[3,16384]{1,0:T(4,128)S(1)} %copy-done.3, s32[2,4096]{1,0:T(2,128)S(1)} %copy-done.10, f32[8,128]{1,0:T(8,128)S(1)} %get-tuple-element.28._), custom_call_target="tpu_custom_call" | custom-call | flops 3221225472 | bytes 786432 | tf_op jit(solution)/shard_map/pallas_call | solution.py:35
  39.6 1.7 %collective-permute-done._second.second = f32[136,256]{1,0:T(8,128)S(1)} collective-permute-done((f32[136,256]{1,0:T(8,128)S(1)}, f32[136,256]{1,0:T(8,128)S(1)}, u32[]{:S(2)}, u32[]{:S(2)}) %collective-permute-start) | collective-permute-done | bytes 139296 | tf_op jit(solution)/shard_map/ppermute | solution.py:463
  41.3 1.6 %collective-permute-done.2.near = f32[8,72,512]{2,1,0:T(8,128)S(1)} collective-permute-done((f32[8,72,512]{2,1,0:T(8,128)}, f32[8,72,512]{2,1,0:T(8,128)S(1)}, u32[]{:S(2)}, u32[]{:S(2)}) %collective-permute-start.2) | collective-permute-done | bytes 1179680 | tf_op jit(solution)/shard_map/ppermute | solution.py:463
  42.9 0.1 shard_map.139
  43.0 4.1 %collective-permute-start.7 = (f32[9,72,512]{2,1,0:T(8,128)S(1)}, f32[9,72,512]{2,1,0:T(8,128)S(1)}, u32[]{:S(2)}, u32[]{:S(2)}) collective-permute-start(f32[9,72,512]{2,1,0:T(8,128)S(1)} %get-tuple-element.38), channel_id=1, source_target_pairs={{0,2},{2,4},{3,1},{4,6},{5,3},{7,5},{16,18},{18,20},{19,17},{20,22... | collective-permute-start | bytes 3981320 | tf_op jit(solution)/shard_map/ppermute | solution.py:463
  47.1 0.1 shard_map.140
  47.2 1.9 %collective-permute-start.5 = (f32[456,256]{1,0:T(8,128)S(1)}, f32[456,256]{1,0:T(8,128)S(1)}, u32[]{:S(2)}, u32[]{:S(2)}) collective-permute-start(f32[456,256]{1,0:T(8,128)S(1)} %get-tuple-element.36), channel_id=1, source_target_pairs={{0,1},{1,0},{2,3},{3,2},{4,5},{5,4},{6,7},{7,6},{16,17},{17,16},{1... | collective-permute-start | bytes 1400840 | tf_op jit(solution)/shard_map/ppermute | solution.py:463
  49.1 0.7 collective-permute-start.6
  49.8 0.7 collective-permute-start.3
  50.5 0.7 collective-permute-start.4
  51.2 1.2 %shard_map.141 = (f32[4,72,512]{2,1,0:T(8,128)S(1)}, f32[4,72,512]{2,1,0:T(8,128)S(1)}, f32[128,128]{1,0:T(8,128)S(1)}, s32[384,128]{1,0:T(8,128)S(1)}, f32[72,512]{1,0:T(8,128)S(1)}) custom-call(f32[136,256]{1,0:T(8,128)S(1)} %get-tuple-element.26.mine, f32[136,256]{1,0:T(8,128)S(1)} %collective-permute-done._second.second, ...), custom_call_target="tpu_custom_call" | custom-call | flops 679477248 | bytes 5308416 | tf_op jit(solution)/shard_map/pallas_call | solution.py:35
  52.4 1.3 %collective-permute-start.8 = (f32[72,512]{1,0:T(8,128)S(1)}, f32[72,512]{1,0:T(8,128)S(1)}, u32[]{:S(2)}, u32[]{:S(2)}) collective-permute-start(f32[72,512]{1,0:T(8,128)S(1)} %get-tuple-element.39), channel_id=1, source_target_pairs={{1,3},{2,0},{3,5},{4,2},{5,7},{6,4},{17,19},{18,16},{19,21},{20,18... | collective-permute-start | bytes 442376 | tf_op jit(solution)/shard_map/ppermute | solution.py:463
  53.7 9.0 %collective-permute-done.8.beyond = f32[72,512]{1,0:T(8,128)S(1)} collective-permute-done((f32[72,512]{1,0:T(8,128)S(1)}, f32[72,512]{1,0:T(8,128)S(1)}, u32[]{:S(2)}, u32[]{:S(2)}) %collective-permute-start.8) | collective-permute-done | bytes 147488 | tf_op jit(solution)/shard_map/ppermute | solution.py:463
  62.7 7.4 %shard_map.142 = (f32[128,384]{1,0:T(8,128)S(1)}, f32[128,384]{1,0:T(8,128)S(1)}, f32[128,384]{1,0:T(8,128)S(1)}) custom-call(s32[384,128]{1,0:T(8,128)S(1)} %get-tuple-element.35.rows_at, f32[456,256]{1,0:T(8,128)S(1)} %collective-permute-done.5.joined_near.message_near, f32[456,256]{1,0:T(8,128)S(1)} %collective-permute-done.6.joined_far.message_far, ...), custom_call_target="tpu_custom_call" | custom-call | flops 1358954496 | bytes 11796480 | tf_op jit(solution)/shard_map/pallas_call | solution.py:35
  70.1 3.4 %collective-permute-start.9 = (f32[128,384]{1,0:T(8,128)S(1)}, f32[128,384]{1,0:T(8,128)S(1)}, u32[]{:S(2)}, u32[]{:S(2)}) collective-permute-start(f32[128,384]{1,0:T(8,128)S(1)} %get-tuple-element.43), channel_id=1, source_target_pairs={{0,16},{1,17},{2,18},{3,19},{4,20},{5,21},{6,22},{7,23},{16,8},{17... | collective-permute-start | bytes 589832 | tf_op jit(solution)/shard_map/ppermute | solution.py:463
  73.6 1.9 %collective-permute-start.10 = (f32[128,384]{1,0:T(8,128)S(1)}, f32[128,384]{1,0:T(8,128)S(1)}, u32[]{:S(2)}, u32[]{:S(2)}) collective-permute-start(f32[128,384]{1,0:T(8,128)S(1)} %get-tuple-element.44), channel_id=1, source_target_pairs={{0,8},{1,9},{2,10},{3,11},{4,12},{5,13},{6,14},{7,15},{16,0},{17,1... | collective-permute-start | bytes 589832 | tf_op jit(solution)/shard_map/ppermute | solution.py:463
  75.5 4.2 %shard_map.143.contact = f32[384,128]{1,0:T(8,128)S(1)} custom-call(s32[128]{0:T(128)S(1)} %copy-done.8, f32[384,128]{1,0:T(8,128)S(1)} %get-tuple-element.46.state, f32[456,256]{1,0:T(8,128)S(1)} %collective-permute-done.5.joined_near.message_near, f32[456,256]{1,0:T(8,128)S(1)} %collective-permute-done.6.joined_far.message_far, ...), custom_call_target="tpu_custom_call" | custom-call | flops 7864320 | bytes 1310720 | tf_op jit(solution)/shard_map/pallas_call | solution.py:35
  79.7 1.4 %collective-permute-done.10.grads_c = f32[128,384]{1,0:T(8,128)S(1)} collective-permute-done((f32[128,384]{1,0:T(8,128)S(1)}, f32[128,384]{1,0:T(8,128)S(1)}, u32[]{:S(2)}, u32[]{:S(2)}) %collective-permute-start.10) | collective-permute-done | bytes 196640 | tf_op jit(solution)/shard_map/ppermute | solution.py:463
  81.1 1.0 %shard_map.144 = f32[3,16384]{1,0:T(4,128)} custom-call(s32[1]{0:T(128)S(6)} %copy.15.count, f32[128,384]{1,0:T(8,128)S(1)} %get-tuple-element.42._.grads_a, f32[128,384]{1,0:T(8,128)S(1)} %collective-permute-done.9.grads_b, f32[128,384]{1,0:T(8,128)S(1)} %collective-permute-done.10.grads_c, f32[128,128]{1,0:T(8,128)S(1)} %get-tuple-element.45.weight, ...), custom_call_target="tpu_custom_call" | custom-call | flops 983040 | bytes 1310720 | tf_op jit(solution)/shard_map/pallas_call | solution.py:35
  (31 shorter events, 0.1 us)
Async XLA Ops:
  0.0 29.2 %copy-start.11 = (s32[128]{0:T(128)S(1)}, s32[128]{0:T(128)}, u32[]{:S(2)}) copy-start(s32[128]{0:T(128)} %param.24) | copy-start | bytes 1540
  0.0 29.2 %copy-start.5 = (s32[16384]{0:T(1024)S(1)}, s32[16384]{0:T(1024)}, u32[]{:S(2)}) copy-start(s32[16384]{0:T(1024)} %param.23) | copy-start | bytes 196612
  0.0 29.2 %copy-start.7 = (f32[16384]{0:T(1024)S(1)}, f32[16384]{0:T(1024)}, u32[]{:S(2)}) copy-start(f32[16384]{0:T(1024)} %param.17) | copy-start | bytes 196612
  0.0 29.2 %copy-start.6 = (f32[16384]{0:T(1024)S(1)}, f32[16384]{0:T(1024)}, u32[]{:S(2)}) copy-start(f32[16384]{0:T(1024)} %param.16) | copy-start | bytes 196612
  0.0 36.3 %copy-start.3 = (f32[3,16384]{1,0:T(4,128)S(1)}, f32[3,16384]{1,0:T(4,128)}, u32[]{:S(2)}) copy-start(f32[3,16384]{1,0:T(4,128)} %vel.3) | copy-start | bytes 589828
  0.0 36.3 %copy-start.10 = (s32[2,4096]{1,0:T(2,128)S(1)}, s32[2,4096]{1,0:T(2,128)}, u32[]{:S(2)}) copy-start(s32[2,4096]{1,0:T(2,128)} %lists.1) | copy-start | bytes 98308
  0.0 36.3 %copy-start.9 = (f32[3,16384]{1,0:T(4,128)S(1)}, f32[3,16384]{1,0:T(4,128)}, u32[]{:S(2)}) copy-start(f32[3,16384]{1,0:T(4,128)} %pos.1) | copy-start | bytes 589828
  23.7 19.3 %collective-permute-start.2 = (f32[8,72,512]{2,1,0:T(8,128)}, f32[8,72,512]{2,1,0:T(8,128)S(1)}, u32[]{:S(2)}, u32[]{:S(2)}) collective-permute-start(f32[8,72,512]{2,1,0:T(8,128)} %get-tuple-element.27.window), channel_id=1, source_target_pairs={{0,1},{1,0},{2,3},{3,2},{4,5},{5,4},{6,7},{7,6},{16,17},{17,16},{1... | collective-permute-start | bytes 3538952 | tf_op jit(solution)/shard_map/ppermute | solution.py:463
  31.0 8.6 %collective-permute-start.1 = (f32[136,256]{1,0:T(8,128)S(1)}, f32[136,256]{1,0:T(8,128)S(1)}, u32[]{:S(2)}, u32[]{:S(2)}) collective-permute-start(f32[136,256]{1,0:T(8,128)S(1)} %get-tuple-element.26.mine), channel_id=1, source_target_pairs={{0,16},{1,17},{2,18},{3,19},{4,20},{5,21},{6,22},{7,23},{8,0},{9,1... | collective-permute-start | bytes 417800 | tf_op jit(solution)/shard_map/ppermute | solution.py:463
  34.4 6.9 %collective-permute-start = (f32[136,256]{1,0:T(8,128)S(1)}, f32[136,256]{1,0:T(8,128)S(1)}, u32[]{:S(2)}, u32[]{:S(2)}) collective-permute-start(f32[136,256]{1,0:T(8,128)S(1)} %get-tuple-element.26.mine), channel_id=1, source_target_pairs={{0,8},{1,9},{2,10},{3,11},{4,12},{5,13},{6,14},{7,15},{8,16},{9,17... | collective-permute-start | bytes 417800 | tf_op jit(solution)/shard_map/ppermute | solution.py:463
  36.3 6.6 %copy-start.4 = (f32[72,512]{1,0:T(8,128)S(1)}, f32[72,512]{1,0:T(8,128)}, u32[]{:S(2)}) copy-start(f32[72,512]{1,0:T(8,128)} %get-tuple-element.31.inner) | copy-start | bytes 442372
  39.6 11.6 %copy-start = (f32[8,72,512]{2,1,0:T(8,128)S(1)}, f32[8,72,512]{2,1,0:T(8,128)}, u32[]{:S(2)}) copy-start(f32[8,72,512]{2,1,0:T(8,128)} %get-tuple-element.27.window) | copy-start | bytes 3538948
  43.0 19.6 %collective-permute-start.7 = (f32[9,72,512]{2,1,0:T(8,128)S(1)}, f32[9,72,512]{2,1,0:T(8,128)S(1)}, u32[]{:S(2)}, u32[]{:S(2)}) collective-permute-start(f32[9,72,512]{2,1,0:T(8,128)S(1)} %get-tuple-element.38), channel_id=1, source_target_pairs={{0,2},{2,4},{3,1},{4,6},{5,3},{7,5},{16,18},{18,20},{19,17},{20,22... | collective-permute-start | bytes 3981320 | tf_op jit(solution)/shard_map/ppermute | solution.py:463
  47.2 15.5 %collective-permute-start.5 = (f32[456,256]{1,0:T(8,128)S(1)}, f32[456,256]{1,0:T(8,128)S(1)}, u32[]{:S(2)}, u32[]{:S(2)}) collective-permute-start(f32[456,256]{1,0:T(8,128)S(1)} %get-tuple-element.36), channel_id=1, source_target_pairs={{0,1},{1,0},{2,3},{3,2},{4,5},{5,4},{6,7},{7,6},{16,17},{17,16},{1... | collective-permute-start | bytes 1400840 | tf_op jit(solution)/shard_map/ppermute | solution.py:463
  49.1 13.5 %collective-permute-start.6 = (f32[456,256]{1,0:T(8,128)S(1)}, f32[456,256]{1,0:T(8,128)S(1)}, u32[]{:S(2)}, u32[]{:S(2)}) collective-permute-start(f32[456,256]{1,0:T(8,128)S(1)} %get-tuple-element.37), channel_id=1, source_target_pairs={{1,2},{2,1},{3,4},{4,3},{5,6},{6,5},{17,18},{18,17},{19,20},{20,19... | collective-permute-start | bytes 1400840 | tf_op jit(solution)/shard_map/ppermute | solution.py:463
  49.8 1.3 %collective-permute-start.3 = (f32[96,128]{1,0:T(8,128)S(1)}, f32[96,128]{1,0:T(8,128)S(1)}, u32[]{:S(2)}, u32[]{:S(2)}) collective-permute-start(f32[96,128]{1,0:T(8,128)S(1)} %get-tuple-element.29.halo_near), channel_id=1, source_target_pairs={{8,9},{9,8},{10,11},{11,10},{12,13},{13,12},{14,15},{15,14}} | collective-permute-start | bytes 147464 | tf_op jit(solution)/shard_map/ppermute | solution.py:463
  50.5 0.7 collective-permute-start.4
  52.4 10.3 %collective-permute-start.8 = (f32[72,512]{1,0:T(8,128)S(1)}, f32[72,512]{1,0:T(8,128)S(1)}, u32[]{:S(2)}, u32[]{:S(2)}) collective-permute-start(f32[72,512]{1,0:T(8,128)S(1)} %get-tuple-element.39), channel_id=1, source_target_pairs={{1,3},{2,0},{3,5},{4,2},{5,7},{6,4},{17,19},{18,16},{19,21},{20,18... | collective-permute-start | bytes 442376 | tf_op jit(solution)/shard_map/ppermute | solution.py:463
  62.7 12.8 %copy-start.1 = (s32[8,16384]{1,0:T(8,128)S(1)}, s32[8,16384]{1,0:T(8,128)}, u32[]{:S(2)}) copy-start(s32[8,16384]{1,0:T(8,128)} %named.1) | copy-start | bytes 1572868
  62.7 12.8 %copy-start.2 = (f32[8,16384]{1,0:T(8,128)S(1)}, f32[8,16384]{1,0:T(8,128)}, u32[]{:S(2)}) copy-start(f32[8,16384]{1,0:T(8,128)} %stiff.1) | copy-start | bytes 1572868
  62.7 12.8 %copy-start.8 = (s32[128]{0:T(128)S(1)}, s32[128]{0:T(128)}, u32[]{:S(2)}) copy-start(s32[128]{0:T(128)} %partner.1) | copy-start | bytes 1540
  70.1 9.6 %collective-permute-start.9 = (f32[128,384]{1,0:T(8,128)S(1)}, f32[128,384]{1,0:T(8,128)S(1)}, u32[]{:S(2)}, u32[]{:S(2)}) collective-permute-start(f32[128,384]{1,0:T(8,128)S(1)} %get-tuple-element.43), channel_id=1, source_target_pairs={{0,16},{1,17},{2,18},{3,19},{4,20},{5,21},{6,22},{7,23},{16,8},{17... | collective-permute-start | bytes 589832 | tf_op jit(solution)/shard_map/ppermute | solution.py:463
  73.6 7.6 %collective-permute-start.10 = (f32[128,384]{1,0:T(8,128)S(1)}, f32[128,384]{1,0:T(8,128)S(1)}, u32[]{:S(2)}, u32[]{:S(2)}) collective-permute-start(f32[128,384]{1,0:T(8,128)S(1)} %get-tuple-element.44), channel_id=1, source_target_pairs={{0,8},{1,9},{2,10},{3,11},{4,12},{5,13},{6,14},{7,15},{16,0},{17,1... | collective-permute-start | bytes 589832 | tf_op jit(solution)/shard_map/ppermute | solution.py:463

commit v10 on v9

--- a/solution.py
+++ b/solution.py
@@ -66,36 +66,35 @@
     return high, (value - high.astype(F32)).astype(BF16)
 
 
-def window_kernel(pressure_old, source, solid_before, window, inner, driven, solid, sems):
+def window_kernel(pressure_old, source, solid_before, window, inner, pressure, driven, solid, sems):
     planes, height, _ = solid.shape
     place = Place(pressure_old.shape[1], height)
     rows = pl.ds(place.first, height)
-    end = (1 - place.parity) * (planes - 1)
-    copy = lambda whole, part, index: pltpu.make_async_copy(whole, part, sems.at[index])
+    used = []
+
+    def copy(whole, part):
+        used.append(None)
+        return pltpu.make_async_copy(whole, part, sems.at[len(used) - 1])
+
     fetched = [
-        (
-            copy(source.at[x, rows, :], driven.at[x], 2 * x),
-            copy(solid_before.at[x, rows, :], solid.at[x], 2 * x + 1),
-        )
-        for x in range(planes)
+        [copy(whole.at[x, rows, :], part.at[x]) for x in range(planes)]
+        for whole, part in ((pressure_old, pressure), (source, driven), (solid_before, solid))
     ]
-    straight = [
-        copy(pressure_old.at[x, rows, :], window.at[x], 2 * planes + x) for x in range(planes)
-    ] + [copy(pressure_old.at[end, rows, :], inner, 3 * planes)]
-    for pair in fetched:
-        for one in pair:
-            one.start()
-    for one in straight:
-        one.start()
-    stored = [
-        copy(driven.at[x], window.at[planes + x], 3 * planes + 1 + x) for x in range(planes)
-    ]
-    for x, pair in enumerate(fetched):
-        for one in pair:
-            one.wait()
+    stored = [copy(pressure.at[x], window.at[x]) for x in range(planes)]
+    stored += [copy(driven.at[x], window.at[planes + x]) for x in range(planes)]
+    stored.append(copy(pressure.at[(1 - place.parity) * (planes - 1)], inner))
+    for x in range(planes):
+        for part in fetched:
+            part[x].start()
+    for x in range(planes):
+        fetched[0][x].wait()
+        stored[x].start()
+        fetched[1][x].wait()
+        fetched[2][x].wait()
         driven[x] = driven[x] - solid[x]
-        stored[x].start()
-    for one in straight + stored:
+        stored[planes + x].start()
+    stored[2 * planes].start()
+    for one in stored:
         one.wait()
 
 
@@ -308,7 +307,7 @@
 
 
 def own_kernel(
-    full, mine, second, third, window, _message, _near, _far, constant, factor, weight, rows_at, ends
+    full, mine, second, third, window, _message, _near, _far, constant, factor, weight, picks, ends
 ):
     tiles = weight.shape[0]
     planes, height, width = constant.shape
@@ -331,11 +330,13 @@
         x, y = line // full, line % full
         row = (x * zones + zone) * height + y - place.first
         held = y // place.own_rows == jnp.where(place.sweeps, place.half, -1)
-        rows_at[i * tiles : (i + 1) * tiles, :] = jnp.where(held, row, -1)
+        row = jnp.concatenate([jnp.where(held, row, -1)] * (picks.shape[1] // BLOCK), 1)
+        hot = jnp.where(row == iota(row.shape, 1), 1.0, 0.0).astype(BF16)
+        picks[i * tiles : (i + 1) * tiles, :] = hot
 
 
 def solve_kernel(
-    full, sweeps, rows_at, joined_near, joined_far, window, near, far, beyond,
+    full, sweeps, picks, joined_near, joined_far, window, near, far, beyond,
     own_constant, own_factor, out_a, out_b, out_c,
     constant, factor, old, new, fields,
 ):
@@ -397,10 +398,8 @@
         return carry
 
     lax.fori_loop(0, planes, gradient, 0, unroll=4)
-    wanted = jnp.concatenate([rows_at[...]] * (planes * zones * height // BLOCK), 1)
-    hot = jnp.where(wanted == iota(wanted.shape, 1), 1.0, 0.0).astype(BF16)
     pieces = jnp.concatenate(halves_of(fields[...]), 1)
-    total = jnp.dot(hot, pieces, preferred_element_type=F32)
+    total = jnp.dot(picks[...], pieces, preferred_element_type=F32)
     total = total[:, : 3 * BLOCK] + total[:, 3 * BLOCK :]
     for index, out in enumerate((out_a, out_b, out_c)):
         out[...] = total[index * tiles : (index + 1) * tiles]
@@ -488,8 +487,8 @@
     window, inner = call(
         window_kernel, (shaped(2 * planes, height, width), plane),
         [HBM] * 3, (pressure_old, pressure_source, solid_old),
-        [pltpu.VMEM((planes, height, width), F32)] * 2
-        + [pltpu.SemaphoreType.DMA((4 * planes + 1,))],
+        [pltpu.VMEM((planes, height, width), F32)] * 3
+        + [pltpu.SemaphoreType.DMA((5 * planes + 1,))],
         flops=field_bytes, size=6 * field_bytes, limit=61_950_000, place=HBM,
     )
     near = along_reg(window, owners, (1, -1))
@@ -521,11 +520,11 @@
     others = [g for g in holders if g not in owners]
     halo_near = along_reg(halo_near, others, (1, -1))
     halo_far = along_reg(halo_far, others, (-1, 1))
-    constant, factor, weight, rows_at, ends = call(
+    constant, factor, weight, picks, ends = call(
         functools.partial(own_kernel, full),
         (
             field, field, shaped(tiles, BLOCK),
-            jax.ShapeDtypeStruct((3 * tiles, BLOCK), jnp.int32), plane,
+            jax.ShapeDtypeStruct((3 * tiles, planes * zones * height), BF16), plane,
         ),
         [VMEM] * 7, (mine, second, third, window, after_message, halo_near, halo_far),
         flops=planes * height * 4 * 384 * 256 * 6, size=9 * field_bytes,
@@ -537,7 +536,7 @@
     grads_a, grads_b, grads_c = call(
         functools.partial(solve_kernel, full, ITERS), (grads,) * 3,
         [VMEM] * 9,
-        (rows_at, message_near, message_far, window, near, far, beyond, constant, factor),
+        (picks, message_near, message_far, window, near, far, beyond, constant, factor),
         [
             window_of(2 * planes), window_of(2 * planes),
             window_of(3 * planes + 2), window_of(3 * planes + 2),

time: 82.5 us -> 61.3 us (0.74)
  Pallas kernels: 42.6 us -> 21.6 us
    pallas_call x9, Pallas kernels: 42.6 us -> 21.6 us  [call(): pl.pallas_call(kernel, out_shape=outs, in_specs=specs, out_specs=jax.tree...]
  transfers between devices with their start and end apart: 11 -> 11, of which waited for: 4 -> 4; matrix products, arithmetic and copies ran while one was open for 0% -> 0% of each run, Pallas kernels for 13% -> 17%
where the time goes in v10:
time: 61.3 us; the launch traced here: 61 us
  starting transfers between devices  24.8 us (40%)
  Pallas kernels  21.6 us (35%)
  waiting for transfers between devices  13.5 us (22%)
  between operations  0.98 us (2%)
    ppermute x11, starting transfers between devices, send(): return lax.ppermute(value, ('grp', 'reg'), flat)  24.8 us
    pallas_call x9, Pallas kernels, call(): pl.pallas_call(kernel, out_shape=outs, in_specs=specs, out_specs=jax.tree...  21.6 us
    ppermute x11, waiting for transfers between devices, send(): return lax.ppermute(value, ('grp', 'reg'), flat)  13.5 us
  transfers between devices with their start and end apart: 11, of which 4 were waited for; matrix products, arithmetic and copies ran while one was open for 0% of the time, Pallas kernels for 17%

profile of v10, /device:TPU:0, one launch (start us, length us, event | category | flops | bytes accessed | tf_op | source)
XLA Modules:
  0.0 61.0 jit_solution(10208434801753490976)
XLA Ops:
  0.0 2.5 %shard_map.137 = (f32[8,72,512]{2,1,0:T(8,128)}, f32[72,512]{1,0:T(8,128)}) custom-call(f32[4,128,512]{2,1,0:T(8,128)} %pressure_old.1, f32[4,128,512]{2,1,0:T(8,128)} %source.1, f32[4,128,512]{2,1,0:T(8,128)} %solid_before.1), custom_call_target="tpu_custom_call" | custom-call | flops 589824 | bytes 3538944 | tf_op jit(solution)/shard_map/pallas_call | solution.py:35
  2.5 4.9 %collective-permute-start.2 = (f32[8,72,512]{2,1,0:T(8,128)}, f32[8,72,512]{2,1,0:T(8,128)S(1)}, u32[]{:S(2)}, u32[]{:S(2)}) collective-permute-start(f32[8,72,512]{2,1,0:T(8,128)} %get-tuple-element.27.window), channel_id=1, source_target_pairs={{0,1},{1,0},{2,3},{3,2},{4,5},{5,4},{6,7},{7,6},{16,17},{17,16},{1... | collective-permute-start | bytes 3538952 | tf_op jit(solution)/shard_map/ppermute | solution.py:462
  8.1 1.7 %shard_map.136 = (f32[136,256]{1,0:T(8,128)S(1)}, f32[8,128]{1,0:T(8,128)S(1)}) custom-call(s32[1]{0:T(128)S(6)} %copy.15.count, s32[128,128]{1,0:T(8,128)S(1)} %bitcast.4, f32[128,128]{1,0:T(8,128)S(1)} %bitcast.6, f32[128,128]{1,0:T(8,128)S(1)} %bitcast.8, s32[1,128]{1,0:T(1,128)S(1)} %bitcast.10), custom_call_target="tpu_custom_call" | custom-call | flops 201326592 | bytes 327680 | tf_op jit(solution)/shard_map/pallas_call | solution.py:35
  9.8 3.4 %collective-permute-start.1 = (f32[136,256]{1,0:T(8,128)S(1)}, f32[136,256]{1,0:T(8,128)S(1)}, u32[]{:S(2)}, u32[]{:S(2)}) collective-permute-start(f32[136,256]{1,0:T(8,128)S(1)} %get-tuple-element.26.mine), channel_id=1, source_target_pairs={{0,16},{1,17},{2,18},{3,19},{4,20},{5,21},{6,22},{7,23},{8,0},{9,1... | collective-permute-start | bytes 417800 | tf_op jit(solution)/shard_map/ppermute | solution.py:462
  13.2 1.9 %collective-permute-start = (f32[136,256]{1,0:T(8,128)S(1)}, f32[136,256]{1,0:T(8,128)S(1)}, u32[]{:S(2)}, u32[]{:S(2)}) collective-permute-start(f32[136,256]{1,0:T(8,128)S(1)} %get-tuple-element.26.mine), channel_id=1, source_target_pairs={{0,8},{1,9},{2,10},{3,11},{4,12},{5,13},{6,14},{7,15},{8,16},{9,17... | collective-permute-start | bytes 417800 | tf_op jit(solution)/shard_map/ppermute | solution.py:462
  15.2 3.2 %shard_map.138 = (f32[384,128]{1,0:T(8,128)S(1)}, f32[96,128]{1,0:T(8,128)S(1)}, f32[96,128]{1,0:T(8,128)S(1)}, f32[8,128]{1,0:T(8,128)S(1)}) custom-call(f32[3,16384]{1,0:T(4,128)S(1)} %copy-done.9, f32[3,16384]{1,0:T(4,128)S(1)} %copy-done.3, s32[2,4096]{1,0:T(2,128)S(1)} %copy-done.10, f32[8,128]{1,0:T(8,128)S(1)} %get-tuple-element.28._), custom_call_target="tpu_custom_call" | custom-call | flops 3221225472 | bytes 786432 | tf_op jit(solution)/shard_map/pallas_call | solution.py:35
  18.5 1.7 %collective-permute-done._second.second = f32[136,256]{1,0:T(8,128)S(1)} collective-permute-done((f32[136,256]{1,0:T(8,128)S(1)}, f32[136,256]{1,0:T(8,128)S(1)}, u32[]{:S(2)}, u32[]{:S(2)}) %collective-permute-start) | collective-permute-done | bytes 139296 | tf_op jit(solution)/shard_map/ppermute | solution.py:462
  20.2 1.6 %collective-permute-done.2.near = f32[8,72,512]{2,1,0:T(8,128)S(1)} collective-permute-done((f32[8,72,512]{2,1,0:T(8,128)}, f32[8,72,512]{2,1,0:T(8,128)S(1)}, u32[]{:S(2)}, u32[]{:S(2)}) %collective-permute-start.2) | collective-permute-done | bytes 1179680 | tf_op jit(solution)/shard_map/ppermute | solution.py:462
  21.8 0.1 shard_map.139
  21.9 4.1 %collective-permute-start.7 = (f32[9,72,512]{2,1,0:T(8,128)S(1)}, f32[9,72,512]{2,1,0:T(8,128)S(1)}, u32[]{:S(2)}, u32[]{:S(2)}) collective-permute-start(f32[9,72,512]{2,1,0:T(8,128)S(1)} %get-tuple-element.38), channel_id=1, source_target_pairs={{0,2},{2,4},{3,1},{4,6},{5,3},{7,5},{16,18},{18,20},{19,17},{20,22... | collective-permute-start | bytes 3981320 | tf_op jit(solution)/shard_map/ppermute | solution.py:462
  26.0 0.1 shard_map.140
  26.1 1.9 %collective-permute-start.5 = (f32[456,256]{1,0:T(8,128)S(1)}, f32[456,256]{1,0:T(8,128)S(1)}, u32[]{:S(2)}, u32[]{:S(2)}) collective-permute-start(f32[456,256]{1,0:T(8,128)S(1)} %get-tuple-element.36), channel_id=1, source_target_pairs={{0,1},{1,0},{2,3},{3,2},{4,5},{5,4},{6,7},{7,6},{16,17},{17,16},{1... | collective-permute-start | bytes 1400840 | tf_op jit(solution)/shard_map/ppermute | solution.py:462
  28.0 0.7 %collective-permute-start.6 = (f32[456,256]{1,0:T(8,128)S(1)}, f32[456,256]{1,0:T(8,128)S(1)}, u32[]{:S(2)}, u32[]{:S(2)}) collective-permute-start(f32[456,256]{1,0:T(8,128)S(1)} %get-tuple-element.37), channel_id=1, source_target_pairs={{1,2},{2,1},{3,4},{4,3},{5,6},{6,5},{17,18},{18,17},{19,20},{20,19... | collective-permute-start | bytes 1400840 | tf_op jit(solution)/shard_map/ppermute | solution.py:462
  28.7 0.7 %collective-permute-start.3 = (f32[96,128]{1,0:T(8,128)S(1)}, f32[96,128]{1,0:T(8,128)S(1)}, u32[]{:S(2)}, u32[]{:S(2)}) collective-permute-start(f32[96,128]{1,0:T(8,128)S(1)} %get-tuple-element.29.halo_near), channel_id=1, source_target_pairs={{8,9},{9,8},{10,11},{11,10},{12,13},{13,12},{14,15},{15,14}} | collective-permute-start | bytes 147464 | tf_op jit(solution)/shard_map/ppermute | solution.py:462
  29.4 0.7 %collective-permute-start.4 = (f32[96,128]{1,0:T(8,128)S(1)}, f32[96,128]{1,0:T(8,128)S(1)}, u32[]{:S(2)}, u32[]{:S(2)}) collective-permute-start(f32[96,128]{1,0:T(8,128)S(1)} %get-tuple-element.30.halo_far), channel_id=1, source_target_pairs={{9,10},{10,9},{11,12},{12,11},{13,14},{14,13}} | collective-permute-start | bytes 147464 | tf_op jit(solution)/shard_map/ppermute | solution.py:462
  30.1 1.4 %shard_map.141 = (f32[4,72,512]{2,1,0:T(8,128)S(1)}, f32[4,72,512]{2,1,0:T(8,128)S(1)}, f32[128,128]{1,0:T(8,128)S(1)}, bf16[384,1152]{1,0:T(8,128)(2,1)S(1)}, f32[72,512]{1,0:T(8,128)S(1)}) custom-call(f32[136,256]{1,0:T(8,128)S(1)} %get-tuple-element.26.mine, f32[136,256]{1,0:T(8,128)S(1)} %collective-permute-done._second.second, ...), custom_call_target="tpu_custom_call" | custom-call | flops 679477248 | bytes 5308416 | tf_op jit(solution)/shard_map/pallas_call | solution.py:35
  31.5 1.3 %collective-permute-start.8 = (f32[72,512]{1,0:T(8,128)S(1)}, f32[72,512]{1,0:T(8,128)S(1)}, u32[]{:S(2)}, u32[]{:S(2)}) collective-permute-start(f32[72,512]{1,0:T(8,128)S(1)} %get-tuple-element.39), channel_id=1, source_target_pairs={{1,3},{2,0},{3,5},{4,2},{5,7},{6,4},{17,19},{18,16},{19,21},{20,18... | collective-permute-start | bytes 442376 | tf_op jit(solution)/shard_map/ppermute | solution.py:462
  32.8 8.8 %collective-permute-done.8.beyond = f32[72,512]{1,0:T(8,128)S(1)} collective-permute-done((f32[72,512]{1,0:T(8,128)S(1)}, f32[72,512]{1,0:T(8,128)S(1)}, u32[]{:S(2)}, u32[]{:S(2)}) %collective-permute-start.8) | collective-permute-done | bytes 147488 | tf_op jit(solution)/shard_map/ppermute | solution.py:462
  41.6 7.4 %shard_map.142 = (f32[128,384]{1,0:T(8,128)S(1)}, f32[128,384]{1,0:T(8,128)S(1)}, f32[128,384]{1,0:T(8,128)S(1)}) custom-call(bf16[384,1152]{1,0:T(8,128)(2,1)S(1)} %get-tuple-element.35.picks, f32[456,256]{1,0:T(8,128)S(1)} %collective-permute-done.5.joined_near.message_near, f32[456,256]{1,0:T(8,128)S(1)} %collective-permute-done.6.joined_far.message_far, ...), custom_call_target="tpu_custom_call" | custom-call | flops 1358954496 | bytes 11796480 | tf_op jit(solution)/shard_map/pallas_call | solution.py:35
  49.0 3.4 %collective-permute-start.9 = (f32[128,384]{1,0:T(8,128)S(1)}, f32[128,384]{1,0:T(8,128)S(1)}, u32[]{:S(2)}, u32[]{:S(2)}) collective-permute-start(f32[128,384]{1,0:T(8,128)S(1)} %get-tuple-element.43), channel_id=1, source_target_pairs={{0,16},{1,17},{2,18},{3,19},{4,20},{5,21},{6,22},{7,23},{16,8},{17... | collective-permute-start | bytes 589832 | tf_op jit(solution)/shard_map/ppermute | solution.py:462
  52.4 1.9 %collective-permute-start.10 = (f32[128,384]{1,0:T(8,128)S(1)}, f32[128,384]{1,0:T(8,128)S(1)}, u32[]{:S(2)}, u32[]{:S(2)}) collective-permute-start(f32[128,384]{1,0:T(8,128)S(1)} %get-tuple-element.44), channel_id=1, source_target_pairs={{0,8},{1,9},{2,10},{3,11},{4,12},{5,13},{6,14},{7,15},{16,0},{17,1... | collective-permute-start | bytes 589832 | tf_op jit(solution)/shard_map/ppermute | solution.py:462
  54.3 4.2 %shard_map.143.contact = f32[384,128]{1,0:T(8,128)S(1)} custom-call(s32[128]{0:T(128)S(1)} %copy-done.8, f32[384,128]{1,0:T(8,128)S(1)} %get-tuple-element.46.state, f32[456,256]{1,0:T(8,128)S(1)} %collective-permute-done.5.joined_near.message_near, f32[456,256]{1,0:T(8,128)S(1)} %collective-permute-done.6.joined_far.message_far, ...), custom_call_target="tpu_custom_call" | custom-call | flops 7864320 | bytes 1310720 | tf_op jit(solution)/shard_map/pallas_call | solution.py:35
  58.6 1.4 %collective-permute-done.10.grads_c = f32[128,384]{1,0:T(8,128)S(1)} collective-permute-done((f32[128,384]{1,0:T(8,128)S(1)}, f32[128,384]{1,0:T(8,128)S(1)}, u32[]{:S(2)}, u32[]{:S(2)}) %collective-permute-start.10) | collective-permute-done | bytes 196640 | tf_op jit(solution)/shard_map/ppermute | solution.py:462
  59.9 1.0 %shard_map.144 = f32[3,16384]{1,0:T(4,128)} custom-call(s32[1]{0:T(128)S(6)} %copy.15.count, f32[128,384]{1,0:T(8,128)S(1)} %get-tuple-element.42._.grads_a, f32[128,384]{1,0:T(8,128)S(1)} %collective-permute-done.9.grads_b, f32[128,384]{1,0:T(8,128)S(1)} %collective-permute-done.10.grads_c, f32[128,128]{1,0:T(8,128)S(1)} %get-tuple-element.45.weight, ...), custom_call_target="tpu_custom_call" | custom-call | flops 983040 | bytes 1310720 | tf_op jit(solution)/shard_map/pallas_call | solution.py:35
  (31 shorter events, 0.1 us)
Async XLA Ops:
  0.0 8.1 %copy-start.11 = (s32[128]{0:T(128)S(1)}, s32[128]{0:T(128)}, u32[]{:S(2)}) copy-start(s32[128]{0:T(128)} %param.24) | copy-start | bytes 1540
  0.0 8.1 %copy-start.5 = (s32[16384]{0:T(1024)S(1)}, s32[16384]{0:T(1024)}, u32[]{:S(2)}) copy-start(s32[16384]{0:T(1024)} %param.23) | copy-start | bytes 196612
  0.0 8.1 %copy-start.7 = (f32[16384]{0:T(1024)S(1)}, f32[16384]{0:T(1024)}, u32[]{:S(2)}) copy-start(f32[16384]{0:T(1024)} %param.17) | copy-start | bytes 196612
  0.0 8.1 %copy-start.6 = (f32[16384]{0:T(1024)S(1)}, f32[16384]{0:T(1024)}, u32[]{:S(2)}) copy-start(f32[16384]{0:T(1024)} %param.16) | copy-start | bytes 196612
  0.0 15.2 %copy-start.3 = (f32[3,16384]{1,0:T(4,128)S(1)}, f32[3,16384]{1,0:T(4,128)}, u32[]{:S(2)}) copy-start(f32[3,16384]{1,0:T(4,128)} %vel.3) | copy-start | bytes 589828
  0.0 15.2 %copy-start.10 = (s32[2,4096]{1,0:T(2,128)S(1)}, s32[2,4096]{1,0:T(2,128)}, u32[]{:S(2)}) copy-start(s32[2,4096]{1,0:T(2,128)} %lists.1) | copy-start | bytes 98308
  0.0 15.2 %copy-start.9 = (f32[3,16384]{1,0:T(4,128)S(1)}, f32[3,16384]{1,0:T(4,128)}, u32[]{:S(2)}) copy-start(f32[3,16384]{1,0:T(4,128)} %pos.1) | copy-start | bytes 589828
  2.5 19.3 %collective-permute-start.2 = (f32[8,72,512]{2,1,0:T(8,128)}, f32[8,72,512]{2,1,0:T(8,128)S(1)}, u32[]{:S(2)}, u32[]{:S(2)}) collective-permute-start(f32[8,72,512]{2,1,0:T(8,128)} %get-tuple-element.27.window), channel_id=1, source_target_pairs={{0,1},{1,0},{2,3},{3,2},{4,5},{5,4},{6,7},{7,6},{16,17},{17,16},{1... | collective-permute-start | bytes 3538952 | tf_op jit(solution)/shard_map/ppermute | solution.py:462
  9.8 8.6 %collective-permute-start.1 = (f32[136,256]{1,0:T(8,128)S(1)}, f32[136,256]{1,0:T(8,128)S(1)}, u32[]{:S(2)}, u32[]{:S(2)}) collective-permute-start(f32[136,256]{1,0:T(8,128)S(1)} %get-tuple-element.26.mine), channel_id=1, source_target_pairs={{0,16},{1,17},{2,18},{3,19},{4,20},{5,21},{6,22},{7,23},{8,0},{9,1... | collective-permute-start | bytes 417800 | tf_op jit(solution)/shard_map/ppermute | solution.py:462
  13.2 6.9 %collective-permute-start = (f32[136,256]{1,0:T(8,128)S(1)}, f32[136,256]{1,0:T(8,128)S(1)}, u32[]{:S(2)}, u32[]{:S(2)}) collective-permute-start(f32[136,256]{1,0:T(8,128)S(1)} %get-tuple-element.26.mine), channel_id=1, source_target_pairs={{0,8},{1,9},{2,10},{3,11},{4,12},{5,13},{6,14},{7,15},{8,16},{9,17... | collective-permute-start | bytes 417800 | tf_op jit(solution)/shard_map/ppermute | solution.py:462
  15.2 6.6 %copy-start.4 = (f32[72,512]{1,0:T(8,128)S(1)}, f32[72,512]{1,0:T(8,128)}, u32[]{:S(2)}) copy-start(f32[72,512]{1,0:T(8,128)} %get-tuple-element.31.inner) | copy-start | bytes 442372
  18.5 11.6 %copy-start = (f32[8,72,512]{2,1,0:T(8,128)S(1)}, f32[8,72,512]{2,1,0:T(8,128)}, u32[]{:S(2)}) copy-start(f32[8,72,512]{2,1,0:T(8,128)} %get-tuple-element.27.window) | copy-start | bytes 3538948
  21.9 19.6 %collective-permute-start.7 = (f32[9,72,512]{2,1,0:T(8,128)S(1)}, f32[9,72,512]{2,1,0:T(8,128)S(1)}, u32[]{:S(2)}, u32[]{:S(2)}) collective-permute-start(f32[9,72,512]{2,1,0:T(8,128)S(1)} %get-tuple-element.38), channel_id=1, source_target_pairs={{0,2},{2,4},{3,1},{4,6},{5,3},{7,5},{16,18},{18,20},{19,17},{20,22... | collective-permute-start | bytes 3981320 | tf_op jit(solution)/shard_map/ppermute | solution.py:462
  26.1 15.5 %collective-permute-start.5 = (f32[456,256]{1,0:T(8,128)S(1)}, f32[456,256]{1,0:T(8,128)S(1)}, u32[]{:S(2)}, u32[]{:S(2)}) collective-permute-start(f32[456,256]{1,0:T(8,128)S(1)} %get-tuple-element.36), channel_id=1, source_target_pairs={{0,1},{1,0},{2,3},{3,2},{4,5},{5,4},{6,7},{7,6},{16,17},{17,16},{1... | collective-permute-start | bytes 1400840 | tf_op jit(solution)/shard_map/ppermute | solution.py:462
  28.0 13.5 %collective-permute-start.6 = (f32[456,256]{1,0:T(8,128)S(1)}, f32[456,256]{1,0:T(8,128)S(1)}, u32[]{:S(2)}, u32[]{:S(2)}) collective-permute-start(f32[456,256]{1,0:T(8,128)S(1)} %get-tuple-element.37), channel_id=1, source_target_pairs={{1,2},{2,1},{3,4},{4,3},{5,6},{6,5},{17,18},{18,17},{19,20},{20,19... | collective-permute-start | bytes 1400840 | tf_op jit(solution)/shard_map/ppermute | solution.py:462
  28.7 1.3 %collective-permute-start.3 = (f32[96,128]{1,0:T(8,128)S(1)}, f32[96,128]{1,0:T(8,128)S(1)}, u32[]{:S(2)}, u32[]{:S(2)}) collective-permute-start(f32[96,128]{1,0:T(8,128)S(1)} %get-tuple-element.29.halo_near), channel_id=1, source_target_pairs={{8,9},{9,8},{10,11},{11,10},{12,13},{13,12},{14,15},{15,14}} | collective-permute-start | bytes 147464 | tf_op jit(solution)/shard_map/ppermute | solution.py:462
  29.4 0.7 %collective-permute-start.4 = (f32[96,128]{1,0:T(8,128)S(1)}, f32[96,128]{1,0:T(8,128)S(1)}, u32[]{:S(2)}, u32[]{:S(2)}) collective-permute-start(f32[96,128]{1,0:T(8,128)S(1)} %get-tuple-element.30.halo_far), channel_id=1, source_target_pairs={{9,10},{10,9},{11,12},{12,11},{13,14},{14,13}} | collective-permute-start | bytes 147464 | tf_op jit(solution)/shard_map/ppermute | solution.py:462
  31.5 10.1 %collective-permute-start.8 = (f32[72,512]{1,0:T(8,128)S(1)}, f32[72,512]{1,0:T(8,128)S(1)}, u32[]{:S(2)}, u32[]{:S(2)}) collective-permute-start(f32[72,512]{1,0:T(8,128)S(1)} %get-tuple-element.39), channel_id=1, source_target_pairs={{1,3},{2,0},{3,5},{4,2},{5,7},{6,4},{17,19},{18,16},{19,21},{20,18... | collective-permute-start | bytes 442376 | tf_op jit(solution)/shard_map/ppermute | solution.py:462
  41.5 12.8 %copy-start.1 = (s32[8,16384]{1,0:T(8,128)S(1)}, s32[8,16384]{1,0:T(8,128)}, u32[]{:S(2)}) copy-start(s32[8,16384]{1,0:T(8,128)} %named.1) | copy-start | bytes 1572868
  41.6 12.8 %copy-start.2 = (f32[8,16384]{1,0:T(8,128)S(1)}, f32[8,16384]{1,0:T(8,128)}, u32[]{:S(2)}) copy-start(f32[8,16384]{1,0:T(8,128)} %stiff.1) | copy-start | bytes 1572868
  41.6 12.8 %copy-start.8 = (s32[128]{0:T(128)S(1)}, s32[128]{0:T(128)}, u32[]{:S(2)}) copy-start(s32[128]{0:T(128)} %partner.1) | copy-start | bytes 1540
  49.0 9.6 %collective-permute-start.9 = (f32[128,384]{1,0:T(8,128)S(1)}, f32[128,384]{1,0:T(8,128)S(1)}, u32[]{:S(2)}, u32[]{:S(2)}) collective-permute-start(f32[128,384]{1,0:T(8,128)S(1)} %get-tuple-element.43), channel_id=1, source_target_pairs={{0,16},{1,17},{2,18},{3,19},{4,20},{5,21},{6,22},{7,23},{16,8},{17... | collective-permute-start | bytes 589832 | tf_op jit(solution)/shard_map/ppermute | solution.py:462
  52.4 7.6 %collective-permute-start.10 = (f32[128,384]{1,0:T(8,128)S(1)}, f32[128,384]{1,0:T(8,128)S(1)}, u32[]{:S(2)}, u32[]{:S(2)}) collective-permute-start(f32[128,384]{1,0:T(8,128)S(1)} %get-tuple-element.44), channel_id=1, source_target_pairs={{0,8},{1,9},{2,10},{3,11},{4,12},{5,13},{6,14},{7,15},{16,0},{17,1... | collective-permute-start | bytes 589832 | tf_op jit(solution)/shard_map/ppermute | solution.py:462

commit v11 on v10

--- a/solution.py
+++ b/solution.py
@@ -53,7 +53,7 @@
         self.first = pl.multiple_of(first, SUB)
         self.sweeps = self.group % CORES == 0
         self.parity = region % 2
-        self.odd = self.parity == 1
+        self.odd, self.even = self.parity == 1, self.parity == 0
         self.lower, self.upper = region > 0, region < regions - 1
 
 
@@ -98,7 +98,7 @@
         one.wait()
 
 
-def forward_kernel(near, inner, _halo, _second, _third, out, dummy):
+def forward_kernel(near, inner, _halo, _second, _third, _near, _far, out, dummy):
     dummy[...] = jnp.zeros(dummy.shape, F32)
     count = near.shape[0]
     out[:count] = near[...]
@@ -196,8 +196,9 @@
         lax.fori_loop(0, rows // 2, step, 0, unroll=8)
 
 
-def message_kernel(mine, second, third, halo_near, halo_far, _, near, far, dummy):
+def message_kernel(mine, second, third, halo_near, halo_far, window, _, near, far, ends, dummy):
     dummy[...] = jnp.zeros(dummy.shape, F32)
+    ends[...] = window[(lax.axis_index("reg") % 2) * (window.shape[0] // 2 - 1)]
     stride = mine.shape[0]
     half = halo_near.shape[0] // 2
     rows = near.shape[0] - half
@@ -284,7 +285,7 @@
     return ids, gathered
 
 
-def coefficients(gathered, tiles, first, full, driven, planes, constant, factor, base, present):
+def coefficients(gathered, tiles, first, full, driven, planes, constant, factor, turned, present):
     _, height, width = driven.shape
     zones = width // BLOCK
     shape = (zones * height, 3 * tiles)
@@ -293,6 +294,7 @@
 
     for x in range(planes):
         solid, drag = gathered(block + x * (full * zones))
+        at = x if turned is None else jnp.where(turned, planes - 1 - x, x)
         voids = 1.0 + solid
         scale = inverse_of(6.0 + (drag + 1.0) * voids)
         if present is not None:
@@ -301,21 +303,20 @@
         for zone in range(zones):
             lanes = slice(zone * BLOCK, (zone + 1) * BLOCK)
             rows = slice(zone * height, (zone + 1) * height)
-            driving = driven[planes + x, :, lanes] + solid[rows]
-            constant[base + x, :, lanes] = driving * inverse[rows]
-            factor[base + x, :, lanes] = scale[rows]
+            driving = driven[x, :, lanes] + solid[rows]
+            constant[at, :, lanes] = driving * inverse[rows]
+            factor[at, :, lanes] = scale[rows]
 
 
 def own_kernel(
-    full, mine, second, third, window, _message, _near, _far, constant, factor, weight, picks, ends
+    full, mine, second, third, window, _message, constant, factor, weight, picks
 ):
     tiles = weight.shape[0]
     planes, height, width = constant.shape
     place = Place(full, height)
     zones = width // BLOCK
-    ends[...] = window[place.parity * (planes - 1)]
     ids, gathered = placed((mine, second, third), tiles)
-    coefficients(gathered, tiles, place.first, full, window, planes, constant, factor, 0, None)
+    coefficients(gathered, tiles, place.first, full, window.at[planes:], planes, constant, factor, place.even, None)
     turned = [
         jnp.transpose(
             jnp.broadcast_to(ids[:, i * tiles : (i + 1) * tiles], (BLOCK, tiles)).astype(F32)
@@ -335,65 +336,94 @@
         picks[i * tiles : (i + 1) * tiles, :] = hot
 
 
-def solve_kernel(
-    full, sweeps, picks, joined_near, joined_far, window, near, far, beyond,
-    own_constant, own_factor, out_a, out_b, out_c,
-    constant, factor, old, new, fields,
+def sweep(source, target, coefficient, start, stop):
+    def plane(at, carry):
+        above, below, left, right = shifted(source[at])
+        around = source[at - 1] + source[at + 1] + above + below + left + right
+        constant, factor = coefficient(at)
+        target[at] = constant + factor * around
+        return carry
+
+    lax.fori_loop(start, stop, plane, 0, unroll=4)
+
+
+def deposits_of(message, tiles):
+    stride = tiles + SUB
+    return placed([message.at[i * stride : (i + 1) * stride] for i in range(3)], tiles)[1]
+
+
+def near_kernel(
+    full, tiles, message, pressure, near, beyond, own_constant, own_factor, kept_even, kept_odd,
+    constant, factor, old, new,
+):
+    planes, height, width = own_constant.shape
+    place = Place(full, height)
+    rim = planes + 1
+    coefficients(
+        deposits_of(message, tiles), tiles, place.first, full, near.at[planes:], planes,
+        constant, factor, place.even, jnp.where(place.odd, place.lower, place.upper),
+    )
+    old[0] = beyond[...]
+    for x in range(planes):
+        at = jnp.where(place.even, planes - 1 - x, x)
+        old[1 + x] = near[at]
+        old[rim + x] = pressure[at]
+    buffers = (old, new)
+    for index in range(planes):
+        source, target = buffers[index % 2], buffers[(index + 1) % 2]
+        sweep(source, target, lambda at: (constant[at - 1], factor[at - 1]), 1 + index, rim)
+        sweep(
+            source, target, lambda at: (own_constant[at - rim], own_factor[at - rim]),
+            rim, 2 * planes - index,
+        )
+    kept_even[...] = old[planes : 2 * planes]
+    kept_odd[...] = new[planes : 2 * planes]
+
+
+def far_kernel(
+    full, tiles, picks, message, pressure, far, own_constant, own_factor, kept_even, kept_odd,
+    out_a, out_b, out_c, constant, factor, old, new, fields,
 ):
     planes, height, width = own_constant.shape
     zones = width // BLOCK
-    tiles = out_a.shape[0]
     place = Place(full, height)
-    odd = place.odd
-    rim = sweeps + 1
-    for joined, driven, below, present in (
-        (joined_near, near, odd, jnp.where(odd, place.lower, place.upper)),
-        (joined_far, far, jnp.logical_not(odd), jnp.where(odd, place.upper, place.lower)),
-    ):
-        stride = tiles + SUB
-        groups = [joined.at[i * stride : (i + 1) * stride] for i in range(3)]
-        _, gathered = placed(groups, tiles)
-        coefficients(
-            gathered, tiles, place.first, full, driven, planes, constant, factor,
-            jnp.where(below, 0, planes), present,
+    rim = planes + 1
+    coefficients(
+        deposits_of(message, tiles), tiles, place.first, full, far.at[planes : 2 * planes], planes,
+        constant, factor, place.even, jnp.where(place.odd, place.upper, place.lower),
+    )
+    old[planes : 2 * planes] = kept_even[...]
+    new[planes : 2 * planes] = kept_odd[...]
+    old[2 * planes] = pressure[jnp.where(place.even, 0, planes - 1)]
+    for x in range(planes):
+        at = jnp.where(place.even, planes - 1 - x, x)
+        old[rim + planes + x] = far[at]
+    old[rim + 2 * planes] = far[2 * planes]
+    buffers = (old, new)
+    edge = rim + planes
+    for index in range(planes):
+        source, target = buffers[index % 2], buffers[(index + 1) % 2]
+        sweep(
+            source, target, lambda at: (own_constant[at - rim], own_factor[at - rim]),
+            2 * planes - index, edge,
         )
-    old[pl.ds(jnp.where(odd, 1, rim + planes), planes)] = near[:planes]
-    old[pl.ds(jnp.where(odd, rim + planes, 1), planes)] = far[:planes]
-    old[pl.ds(jnp.where(odd, rim + 2 * planes, 0), 1)] = far[2 * planes :]
-    old[pl.ds(jnp.where(odd, 0, rim + 2 * planes), 1)] = beyond[...][None]
-    old[rim : rim + planes] = window[:planes]
-
-    def sweep(source, target, depth):
-        def over(constants, factors, shift):
-            def plane(x, carry):
-                centre = source[x]
-                above, below, left, right = shifted(centre)
-                around = source[x - 1] + source[x + 1] + above + below + left + right
-                target[x] = constants[x - shift] + factors[x - shift] * around
-                return carry
-
-            return plane
-
-        lax.fori_loop(depth, rim, over(constant, factor, 1), 0, unroll=4)
-        lax.fori_loop(rim, rim + planes, over(own_constant, own_factor, rim), 0, unroll=4)
-        lax.fori_loop(
-            rim + planes, 3 * planes + 2 - depth, over(constant, factor, 1 + planes), 0, unroll=4
+        sweep(
+            source, target, lambda at: (constant[at - edge], factor[at - edge]),
+            edge, edge + planes - index,
         )
-
-    for index in range(sweeps):
-        source, target = (old, new) if index % 2 == 0 else (new, old)
-        sweep(source, target, index + 1)
-    last = old if sweeps % 2 == 0 else new
+    last = buffers[planes % 2]
+    way = jnp.where(place.even, -0.5, 0.5)
 
     def gradient(x, carry):
-        centre = last[rim + x]
-        above, below, left, right = shifted(centre)
-        grads = (last[rim + x + 1] - last[rim + x - 1], below - above, right - left)
+        at = rim + x
+        above, below, left, right = shifted(last[at])
+        grads = (way * (last[at + 1] - last[at - 1]), 0.5 * (below - above), 0.5 * (right - left))
+        line = jnp.where(place.even, planes - 1 - x, x) * zones
         for zone in range(zones):
-            first = pl.multiple_of((x * zones + zone) * height, SUB)
+            first = pl.multiple_of((line + zone) * height, SUB)
             for axis, grad in enumerate(grads):
                 fields[pl.ds(first, height), axis * BLOCK : (axis + 1) * BLOCK] = (
-                    0.5 * grad[:, zone * BLOCK : (zone + 1) * BLOCK]
+                    grad[:, zone * BLOCK : (zone + 1) * BLOCK]
                 )
         return carry
 
@@ -451,7 +481,7 @@
     slots = grain_pos.shape[1]
     tiles = slots // BLOCK
     planes, full, width = pressure_old.shape
-    zones = width // BLOCK
+    assert planes == ITERS
     own_rows = full // halves
     height = min(full, own_rows + SUB * min(2, halves - 1))
     owners = range(0, groups, CORES)
@@ -505,44 +535,46 @@
         [VMEM] * 4, (grain_pos, grain_vel, halo_list, after_deposit), flops=2 * 3 * 8 * BLOCK * BLOCK * slots // 4,
         size=4 * 4 * 3 * slots,
     )
+    others = [g for g in holders if g not in owners]
+    came_near = along_reg(halo_near, others, (1, -1))
+    came_far = along_reg(halo_far, others, (-1, 1))
     far, after_forward = call(
-        forward_kernel, (shaped(2 * planes + 1, height, width), small), [VMEM] * 5,
-        (near, inner, after_halo, second, third), size=5 * field_bytes,
+        forward_kernel, (shaped(2 * planes + 1, height, width), small), [VMEM] * 7,
+        (near, inner, after_halo, second, third, came_near, came_far), size=5 * field_bytes,
     )
     far = along_reg(far, owners, (2, -2))
     message = shaped(holding * (tiles + SUB) + 3 * rows // 2, 2 * BLOCK)
-    message_near, message_far, after_message = call(
-        message_kernel, (message, message, small), [VMEM] * 6,
-        (mine, second, third, halo_near, halo_far, after_forward), size=8 * 2 * BLOCK * 500,
+    message_near, message_far, ends, after_message = call(
+        message_kernel, (message, message, plane, small), [VMEM] * 7,
+        (mine, second, third, halo_near, halo_far, window, after_forward), size=8 * 2 * BLOCK * 500,
     )
     message_near = along_reg(message_near, owners, (1, -1))
     message_far = along_reg(message_far, owners, (-1, 1))
-    others = [g for g in holders if g not in owners]
-    halo_near = along_reg(halo_near, others, (1, -1))
-    halo_far = along_reg(halo_far, others, (-1, 1))
-    constant, factor, weight, picks, ends = call(
+    beyond = along_reg(ends, owners, (-2, 2))
+    constant, factor, weight, picks = call(
         functools.partial(own_kernel, full),
         (
             field, field, shaped(tiles, BLOCK),
-            jax.ShapeDtypeStruct((3 * tiles, planes * zones * height), BF16), plane,
+            jax.ShapeDtypeStruct((3 * tiles, planes * height * width // BLOCK), BF16),
         ),
-        [VMEM] * 7, (mine, second, third, window, after_message, halo_near, halo_far),
+        [VMEM] * 5, (mine, second, third, window, after_message),
         flops=planes * height * 4 * 384 * 256 * 6, size=9 * field_bytes,
     )
-    beyond = along_reg(ends, owners, (-2, 2))
-
+    window_of = lambda count: pltpu.VMEM((count, height, width), F32)
+    kept_even, kept_odd = call(
+        functools.partial(near_kernel, full, tiles), (field, field), [VMEM] * 6,
+        (message_near, window, near, beyond, constant, factor),
+        [window_of(planes)] * 2 + [window_of(2 * planes + 1)] * 2,
+        flops=planes * height * 4 * 384 * 256 * 6, size=9 * field_bytes,
+    )
     grads = shaped(tiles, 3 * BLOCK)
-    window_of = lambda count: pltpu.VMEM((count, height, width), F32)
     grads_a, grads_b, grads_c = call(
-        functools.partial(solve_kernel, full, ITERS), (grads,) * 3,
-        [VMEM] * 9,
-        (picks, message_near, message_far, window, near, far, beyond, constant, factor),
-        [
-            window_of(2 * planes), window_of(2 * planes),
-            window_of(3 * planes + 2), window_of(3 * planes + 2),
-            pltpu.VMEM((planes * zones * height, 3 * BLOCK), F32),
-        ],
-        flops=2 * planes * height * 4 * 384 * 256 * 6, size=20 * field_bytes,
+        functools.partial(far_kernel, full, tiles), (grads,) * 3, [VMEM] * 8,
+        (picks, message_far, window, far, constant, factor, kept_even, kept_odd),
+        [window_of(planes)] * 2
+        + [window_of(3 * planes + 2)] * 2
+        + [pltpu.VMEM((planes * height * width // BLOCK, 3 * BLOCK), F32)],
+        flops=planes * height * 4 * 384 * 256 * 6, size=9 * field_bytes,
     )
     grads_b = along_grp(grads_b, -1, owners)
     grads_c = along_grp(grads_c, -2, owners)
@@ -550,7 +582,7 @@
     contact = call(
         contact_kernel, shaped(3 * tiles, BLOCK), [SMEM] + [VMEM] * 7 + [ANY],
         (
-            partner_block, state, message_near, message_far, halo_near, halo_far, contact_rows,
+            partner_block, state, message_near, message_far, came_near, came_far, contact_rows,
             contact_stiff, grads_a,
         ),
         [pltpu.VMEM((3 * (tiles + 2 * rows), BLOCK), F32)],

time: 61.3 us -> 62.3 us (1.016)
  Pallas kernels: 21.6 us -> 22.5 us
    pallas_call x9 -> x10, Pallas kernels: 21.6 us -> 22.5 us  [call(): pl.pallas_call(kernel, out_shape=outs, in_specs=specs, out_specs=jax.tree...]
  transfers between devices with their start and end apart: 11 -> 11, of which waited for: 4 -> 4; matrix products, arithmetic and copies ran while one was open for 0% -> 0% of each run, Pallas kernels for 17% -> 22%
where the time goes in v11:
time: 62.3 us; the launch traced here: 62 us
  starting transfers between devices  25 us (40%)
  Pallas kernels  22.5 us (36%)
  waiting for transfers between devices  13.4 us (22%)
  between operations  1 us (2%)
    ppermute x11, starting transfers between devices, send(): return lax.ppermute(value, ('grp', 'reg'), flat)  25 us
    pallas_call x10, Pallas kernels, call(): pl.pallas_call(kernel, out_shape=outs, in_specs=specs, out_specs=jax.tree...  22.5 us
    ppermute x11, waiting for transfers between devices, send(): return lax.ppermute(value, ('grp', 'reg'), flat)  13.4 us
  transfers between devices with their start and end apart: 11, of which 4 were waited for; matrix products, arithmetic and copies ran while one was open for 0% of the time, Pallas kernels for 22%

profile of v11, /device:TPU:0, one launch (start us, length us, event | category | flops | bytes accessed | tf_op | source)
XLA Modules:
  0.0 62.0 jit_solution(2503399767800003946)
XLA Ops:
  0.0 2.5 %shard_map.137 = (f32[8,72,512]{2,1,0:T(8,128)}, f32[72,512]{1,0:T(8,128)}) custom-call(f32[4,128,512]{2,1,0:T(8,128)} %pressure_old.1, f32[4,128,512]{2,1,0:T(8,128)} %source.1, f32[4,128,512]{2,1,0:T(8,128)} %solid_before.1), custom_call_target="tpu_custom_call" | custom-call | flops 589824 | bytes 3538944 | tf_op jit(solution)/shard_map/pallas_call | solution.py:35
  2.5 4.9 %collective-permute-start.2 = (f32[8,72,512]{2,1,0:T(8,128)}, f32[8,72,512]{2,1,0:T(8,128)S(1)}, u32[]{:S(2)}, u32[]{:S(2)}) collective-permute-start(f32[8,72,512]{2,1,0:T(8,128)} %get-tuple-element.29.window.pressure), channel_id=1, source_target_pairs={{0,1},{1,0},{2,3},{3,2},{4,5},{5,4},{6,7},{7,6},{16,17},{17,16},{1... | collective-permute-start | bytes 3538952 | tf_op jit(solution)/shard_map/ppermute | solution.py:492
  8.1 1.7 %shard_map.136 = (f32[136,256]{1,0:T(8,128)S(1)}, f32[8,128]{1,0:T(8,128)S(1)}) custom-call(s32[1]{0:T(128)S(6)} %copy.15.count, s32[128,128]{1,0:T(8,128)S(1)} %bitcast.4, f32[128,128]{1,0:T(8,128)S(1)} %bitcast.6, f32[128,128]{1,0:T(8,128)S(1)} %bitcast.8, s32[1,128]{1,0:T(1,128)S(1)} %bitcast.10), custom_call_target="tpu_custom_call" | custom-call | flops 201326592 | bytes 327680 | tf_op jit(solution)/shard_map/pallas_call | solution.py:35
  9.8 3.4 %collective-permute-start.1 = (f32[136,256]{1,0:T(8,128)S(1)}, f32[136,256]{1,0:T(8,128)S(1)}, u32[]{:S(2)}, u32[]{:S(2)}) collective-permute-start(f32[136,256]{1,0:T(8,128)S(1)} %get-tuple-element.28.mine), channel_id=1, source_target_pairs={{0,16},{1,17},{2,18},{3,19},{4,20},{5,21},{6,22},{7,23},{8,0},{9,1... | collective-permute-start | bytes 417800 | tf_op jit(solution)/shard_map/ppermute | solution.py:492
  13.2 1.9 %collective-permute-start = (f32[136,256]{1,0:T(8,128)S(1)}, f32[136,256]{1,0:T(8,128)S(1)}, u32[]{:S(2)}, u32[]{:S(2)}) collective-permute-start(f32[136,256]{1,0:T(8,128)S(1)} %get-tuple-element.28.mine), channel_id=1, source_target_pairs={{0,8},{1,9},{2,10},{3,11},{4,12},{5,13},{6,14},{7,15},{8,16},{9,17... | collective-permute-start | bytes 417800 | tf_op jit(solution)/shard_map/ppermute | solution.py:492
  15.2 3.2 %shard_map.138 = (f32[384,128]{1,0:T(8,128)S(1)}, f32[96,128]{1,0:T(8,128)S(1)}, f32[96,128]{1,0:T(8,128)S(1)}, f32[8,128]{1,0:T(8,128)S(1)}) custom-call(f32[3,16384]{1,0:T(4,128)S(1)} %copy-done.9, f32[3,16384]{1,0:T(4,128)S(1)} %copy-done.3, s32[2,4096]{1,0:T(2,128)S(1)} %copy-done.10, f32[8,128]{1,0:T(8,128)S(1)} %get-tuple-element.30._), custom_call_target="tpu_custom_call" | custom-call | flops 3221225472 | bytes 786432 | tf_op jit(solution)/shard_map/pallas_call | solution.py:35
  18.5 0.8 %collective-permute-start.3 = (f32[96,128]{1,0:T(8,128)S(1)}, f32[96,128]{1,0:T(8,128)S(1)}, u32[]{:S(2)}, u32[]{:S(2)}) collective-permute-start(f32[96,128]{1,0:T(8,128)S(1)} %get-tuple-element.31.halo_near), channel_id=1, source_target_pairs={{8,9},{9,8},{10,11},{11,10},{12,13},{13,12},{14,15},{15,14}} | collective-permute-start | bytes 147464 | tf_op jit(solution)/shard_map/ppermute | solution.py:492
  19.3 0.7 %collective-permute-start.4 = (f32[96,128]{1,0:T(8,128)S(1)}, f32[96,128]{1,0:T(8,128)S(1)}, u32[]{:S(2)}, u32[]{:S(2)}) collective-permute-start(f32[96,128]{1,0:T(8,128)S(1)} %get-tuple-element.32.halo_far), channel_id=1, source_target_pairs={{9,10},{10,9},{11,12},{12,11},{13,14},{14,13}} | collective-permute-start | bytes 147464 | tf_op jit(solution)/shard_map/ppermute | solution.py:492
  20.0 0.2 collective-permute-done._second.second
  20.2 1.6 %collective-permute-done.2.near = f32[8,72,512]{2,1,0:T(8,128)S(1)} collective-permute-done((f32[8,72,512]{2,1,0:T(8,128)}, f32[8,72,512]{2,1,0:T(8,128)S(1)}, u32[]{:S(2)}, u32[]{:S(2)}) %collective-permute-start.2) | collective-permute-done | bytes 1179680 | tf_op jit(solution)/shard_map/ppermute | solution.py:492
  21.8 0.1 shard_map.139
  21.9 4.1 %collective-permute-start.6 = (f32[9,72,512]{2,1,0:T(8,128)S(1)}, f32[9,72,512]{2,1,0:T(8,128)S(1)}, u32[]{:S(2)}, u32[]{:S(2)}) collective-permute-start(f32[9,72,512]{2,1,0:T(8,128)S(1)} %get-tuple-element.39), channel_id=1, source_target_pairs={{0,2},{2,4},{3,1},{4,6},{5,3},{7,5},{16,18},{18,20},{19,17},{20,22... | collective-permute-start | bytes 3981320 | tf_op jit(solution)/shard_map/ppermute | solution.py:492
  26.1 1.9 %collective-permute-start.7 = (f32[456,256]{1,0:T(8,128)S(1)}, f32[456,256]{1,0:T(8,128)S(1)}, u32[]{:S(2)}, u32[]{:S(2)}) collective-permute-start(f32[456,256]{1,0:T(8,128)S(1)} %get-tuple-element.42), channel_id=1, source_target_pairs={{0,1},{1,0},{2,3},{3,2},{4,5},{5,4},{6,7},{7,6},{16,17},{17,16},{1... | collective-permute-start | bytes 1400840 | tf_op jit(solution)/shard_map/ppermute | solution.py:492
  28.0 0.7 %collective-permute-start.5 = (f32[456,256]{1,0:T(8,128)S(1)}, f32[456,256]{1,0:T(8,128)S(1)}, u32[]{:S(2)}, u32[]{:S(2)}) collective-permute-start(f32[456,256]{1,0:T(8,128)S(1)} %get-tuple-element.38), channel_id=1, source_target_pairs={{1,2},{2,1},{3,4},{4,3},{5,6},{6,5},{17,18},{18,17},{19,20},{20,19... | collective-permute-start | bytes 1400840 | tf_op jit(solution)/shard_map/ppermute | solution.py:492
  28.7 1.3 %collective-permute-start.8 = (f32[72,512]{1,0:T(8,128)S(1)}, f32[72,512]{1,0:T(8,128)S(1)}, u32[]{:S(2)}, u32[]{:S(2)}) collective-permute-start(f32[72,512]{1,0:T(8,128)S(1)} %get-tuple-element.43), channel_id=1, source_target_pairs={{1,3},{2,0},{3,5},{4,2},{5,7},{6,4},{17,19},{18,16},{19,21},{20,18... | collective-permute-start | bytes 442376 | tf_op jit(solution)/shard_map/ppermute | solution.py:492
  30.0 1.4 %shard_map.141 = (f32[4,72,512]{2,1,0:T(8,128)S(1)}, f32[4,72,512]{2,1,0:T(8,128)S(1)}, f32[128,128]{1,0:T(8,128)S(1)}, bf16[384,1152]{1,0:T(8,128)(2,1)S(1)}) custom-call(f32[136,256]{1,0:T(8,128)S(1)} %get-tuple-element.28.mine, f32[136,256]{1,0:T(8,128)S(1)} %collective-permute-done._second.second, f32[136,256]{1,0:T(8,128)S(1)} %collective-permute-done.1._third.third, ...), custom_call_target="tpu_custom_call" | custom-call | flops 679477248 | bytes 5308416 | tf_op jit(solution)/shard_map/pallas_call | solution.py:35
  31.4 10.2 %collective-permute-done.8.beyond = f32[72,512]{1,0:T(8,128)S(1)} collective-permute-done((f32[72,512]{1,0:T(8,128)S(1)}, f32[72,512]{1,0:T(8,128)S(1)}, u32[]{:S(2)}, u32[]{:S(2)}) %collective-permute-start.8) | collective-permute-done | bytes 147488 | tf_op jit(solution)/shard_map/ppermute | solution.py:492
  41.6 3.2 %shard_map.142 = (f32[4,72,512]{2,1,0:T(8,128)S(1)}, f32[4,72,512]{2,1,0:T(8,128)S(1)}) custom-call(f32[456,256]{1,0:T(8,128)S(1)} %collective-permute-done.7.message.message_near, f32[8,72,512]{2,1,0:T(8,128)S(1)} %copy-done, f32[8,72,512]{2,1,0:T(8,128)S(1)} %collective-permute-done.2.near, f32[72,512]{1,0:T(8,128)S(1)} %collective-permute-done.8.beyond, ...), custom_call_target="tpu_custom_call" | custom-call | flops 679477248 | bytes 5308416 | tf_op jit(solution)/shard_map/pallas_call | solution.py:35
  44.9 5.1 %shard_map.143 = (f32[128,384]{1,0:T(8,128)S(1)}, f32[128,384]{1,0:T(8,128)S(1)}, f32[128,384]{1,0:T(8,128)S(1)}) custom-call(bf16[384,1152]{1,0:T(8,128)(2,1)S(1)} %get-tuple-element.37.picks, f32[456,256]{1,0:T(8,128)S(1)} %collective-permute-done.5.message.message_far, f32[8,72,512]{2,1,0:T(8,128)S(1)} %copy-done, ...), custom_call_target="tpu_custom_call" | custom-call | flops 679477248 | bytes 5308416 | tf_op jit(solution)/shard_map/pallas_call | solution.py:35
  50.0 3.4 %collective-permute-start.9 = (f32[128,384]{1,0:T(8,128)S(1)}, f32[128,384]{1,0:T(8,128)S(1)}, u32[]{:S(2)}, u32[]{:S(2)}) collective-permute-start(f32[128,384]{1,0:T(8,128)S(1)} %get-tuple-element.47), channel_id=1, source_target_pairs={{0,16},{1,17},{2,18},{3,19},{4,20},{5,21},{6,22},{7,23},{16,8},{17... | collective-permute-start | bytes 589832 | tf_op jit(solution)/shard_map/ppermute | solution.py:492
  53.4 1.9 %collective-permute-start.10 = (f32[128,384]{1,0:T(8,128)S(1)}, f32[128,384]{1,0:T(8,128)S(1)}, u32[]{:S(2)}, u32[]{:S(2)}) collective-permute-start(f32[128,384]{1,0:T(8,128)S(1)} %get-tuple-element.48), channel_id=1, source_target_pairs={{0,8},{1,9},{2,10},{3,11},{4,12},{5,13},{6,14},{7,15},{16,0},{17,1... | collective-permute-start | bytes 589832 | tf_op jit(solution)/shard_map/ppermute | solution.py:492
  55.3 4.2 %shard_map.144.contact = f32[384,128]{1,0:T(8,128)S(1)} custom-call(s32[128]{0:T(128)S(1)} %copy-done.8, f32[384,128]{1,0:T(8,128)S(1)} %get-tuple-element.50.state, f32[456,256]{1,0:T(8,128)S(1)} %collective-permute-done.7.message.message_near, f32[456,256]{1,0:T(8,128)S(1)} %collective-permute-done.5.message.message_far, ...), custom_call_target="tpu_custom_call" | custom-call | flops 7864320 | bytes 1310720 | tf_op jit(solution)/shard_map/pallas_call | solution.py:35
  59.6 1.4 %collective-permute-done.10.grads_c = f32[128,384]{1,0:T(8,128)S(1)} collective-permute-done((f32[128,384]{1,0:T(8,128)S(1)}, f32[128,384]{1,0:T(8,128)S(1)}, u32[]{:S(2)}, u32[]{:S(2)}) %collective-permute-start.10) | collective-permute-done | bytes 196640 | tf_op jit(solution)/shard_map/ppermute | solution.py:492
  60.9 1.0 %shard_map.145 = f32[3,16384]{1,0:T(4,128)} custom-call(s32[1]{0:T(128)S(6)} %copy.15.count, f32[128,384]{1,0:T(8,128)S(1)} %get-tuple-element.46._.grads_a, f32[128,384]{1,0:T(8,128)S(1)} %collective-permute-done.9.grads_b, f32[128,384]{1,0:T(8,128)S(1)} %collective-permute-done.10.grads_c, f32[128,128]{1,0:T(8,128)S(1)} %get-tuple-element.49.weight, ...), custom_call_target="tpu_custom_call" | custom-call | flops 983040 | bytes 1310720 | tf_op jit(solution)/shard_map/pallas_call | solution.py:35
  (32 shorter events, 0.1 us)
Async XLA Ops:
  0.0 8.1 %copy-start.11 = (s32[128]{0:T(128)S(1)}, s32[128]{0:T(128)}, u32[]{:S(2)}) copy-start(s32[128]{0:T(128)} %param.24) | copy-start | bytes 1540
  0.0 8.1 %copy-start.5 = (s32[16384]{0:T(1024)S(1)}, s32[16384]{0:T(1024)}, u32[]{:S(2)}) copy-start(s32[16384]{0:T(1024)} %param.23) | copy-start | bytes 196612
  0.0 8.1 %copy-start.7 = (f32[16384]{0:T(1024)S(1)}, f32[16384]{0:T(1024)}, u32[]{:S(2)}) copy-start(f32[16384]{0:T(1024)} %param.17) | copy-start | bytes 196612
  0.0 8.1 %copy-start.6 = (f32[16384]{0:T(1024)S(1)}, f32[16384]{0:T(1024)}, u32[]{:S(2)}) copy-start(f32[16384]{0:T(1024)} %param.16) | copy-start | bytes 196612
  0.0 15.2 %copy-start.3 = (f32[3,16384]{1,0:T(4,128)S(1)}, f32[3,16384]{1,0:T(4,128)}, u32[]{:S(2)}) copy-start(f32[3,16384]{1,0:T(4,128)} %vel.3) | copy-start | bytes 589828
  0.0 15.2 %copy-start.10 = (s32[2,4096]{1,0:T(2,128)S(1)}, s32[2,4096]{1,0:T(2,128)}, u32[]{:S(2)}) copy-start(s32[2,4096]{1,0:T(2,128)} %lists.1) | copy-start | bytes 98308
  0.0 15.2 %copy-start.9 = (f32[3,16384]{1,0:T(4,128)S(1)}, f32[3,16384]{1,0:T(4,128)}, u32[]{:S(2)}) copy-start(f32[3,16384]{1,0:T(4,128)} %pos.1) | copy-start | bytes 589828
  2.5 19.3 %collective-permute-start.2 = (f32[8,72,512]{2,1,0:T(8,128)}, f32[8,72,512]{2,1,0:T(8,128)S(1)}, u32[]{:S(2)}, u32[]{:S(2)}) collective-permute-start(f32[8,72,512]{2,1,0:T(8,128)} %get-tuple-element.29.window.pressure), channel_id=1, source_target_pairs={{0,1},{1,0},{2,3},{3,2},{4,5},{5,4},{6,7},{7,6},{16,17},{17,16},{1... | collective-permute-start | bytes 3538952 | tf_op jit(solution)/shard_map/ppermute | solution.py:492
  9.8 10.1 %collective-permute-start.1 = (f32[136,256]{1,0:T(8,128)S(1)}, f32[136,256]{1,0:T(8,128)S(1)}, u32[]{:S(2)}, u32[]{:S(2)}) collective-permute-start(f32[136,256]{1,0:T(8,128)S(1)} %get-tuple-element.28.mine), channel_id=1, source_target_pairs={{0,16},{1,17},{2,18},{3,19},{4,20},{5,21},{6,22},{7,23},{8,0},{9,1... | collective-permute-start | bytes 417800 | tf_op jit(solution)/shard_map/ppermute | solution.py:492
  13.2 6.9 %collective-permute-start = (f32[136,256]{1,0:T(8,128)S(1)}, f32[136,256]{1,0:T(8,128)S(1)}, u32[]{:S(2)}, u32[]{:S(2)}) collective-permute-start(f32[136,256]{1,0:T(8,128)S(1)} %get-tuple-element.28.mine), channel_id=1, source_target_pairs={{0,8},{1,9},{2,10},{3,11},{4,12},{5,13},{6,14},{7,15},{8,16},{9,17... | collective-permute-start | bytes 417800 | tf_op jit(solution)/shard_map/ppermute | solution.py:492
  15.2 6.6 %copy-start.4 = (f32[72,512]{1,0:T(8,128)S(1)}, f32[72,512]{1,0:T(8,128)}, u32[]{:S(2)}) copy-start(f32[72,512]{1,0:T(8,128)} %get-tuple-element.33.inner) | copy-start | bytes 442372
  18.5 7.5 %copy-start = (f32[8,72,512]{2,1,0:T(8,128)S(1)}, f32[8,72,512]{2,1,0:T(8,128)}, u32[]{:S(2)}) copy-start(f32[8,72,512]{2,1,0:T(8,128)} %get-tuple-element.29.window.pressure) | copy-start | bytes 3538948
  18.5 1.5 %collective-permute-start.3 = (f32[96,128]{1,0:T(8,128)S(1)}, f32[96,128]{1,0:T(8,128)S(1)}, u32[]{:S(2)}, u32[]{:S(2)}) collective-permute-start(f32[96,128]{1,0:T(8,128)S(1)} %get-tuple-element.31.halo_near), channel_id=1, source_target_pairs={{8,9},{9,8},{10,11},{11,10},{12,13},{13,12},{14,15},{15,14}} | collective-permute-start | bytes 147464 | tf_op jit(solution)/shard_map/ppermute | solution.py:492
  19.3 0.7 %collective-permute-start.4 = (f32[96,128]{1,0:T(8,128)S(1)}, f32[96,128]{1,0:T(8,128)S(1)}, u32[]{:S(2)}, u32[]{:S(2)}) collective-permute-start(f32[96,128]{1,0:T(8,128)S(1)} %get-tuple-element.32.halo_far), channel_id=1, source_target_pairs={{9,10},{10,9},{11,12},{12,11},{13,14},{14,13}} | collective-permute-start | bytes 147464 | tf_op jit(solution)/shard_map/ppermute | solution.py:492
  21.9 22.9 %collective-permute-start.6 = (f32[9,72,512]{2,1,0:T(8,128)S(1)}, f32[9,72,512]{2,1,0:T(8,128)S(1)}, u32[]{:S(2)}, u32[]{:S(2)}) collective-permute-start(f32[9,72,512]{2,1,0:T(8,128)S(1)} %get-tuple-element.39), channel_id=1, source_target_pairs={{0,2},{2,4},{3,1},{4,6},{5,3},{7,5},{16,18},{18,20},{19,17},{20,22... | collective-permute-start | bytes 3981320 | tf_op jit(solution)/shard_map/ppermute | solution.py:492
  26.1 15.5 %collective-permute-start.7 = (f32[456,256]{1,0:T(8,128)S(1)}, f32[456,256]{1,0:T(8,128)S(1)}, u32[]{:S(2)}, u32[]{:S(2)}) collective-permute-start(f32[456,256]{1,0:T(8,128)S(1)} %get-tuple-element.42), channel_id=1, source_target_pairs={{0,1},{1,0},{2,3},{3,2},{4,5},{5,4},{6,7},{7,6},{16,17},{17,16},{1... | collective-permute-start | bytes 1400840 | tf_op jit(solution)/shard_map/ppermute | solution.py:492
  28.0 16.8 %collective-permute-start.5 = (f32[456,256]{1,0:T(8,128)S(1)}, f32[456,256]{1,0:T(8,128)S(1)}, u32[]{:S(2)}, u32[]{:S(2)}) collective-permute-start(f32[456,256]{1,0:T(8,128)S(1)} %get-tuple-element.38), channel_id=1, source_target_pairs={{1,2},{2,1},{3,4},{4,3},{5,6},{6,5},{17,18},{18,17},{19,20},{20,19... | collective-permute-start | bytes 1400840 | tf_op jit(solution)/shard_map/ppermute | solution.py:492
  28.7 12.8 %collective-permute-start.8 = (f32[72,512]{1,0:T(8,128)S(1)}, f32[72,512]{1,0:T(8,128)S(1)}, u32[]{:S(2)}, u32[]{:S(2)}) collective-permute-start(f32[72,512]{1,0:T(8,128)S(1)} %get-tuple-element.43), channel_id=1, source_target_pairs={{1,3},{2,0},{3,5},{4,2},{5,7},{6,4},{17,19},{18,16},{19,21},{20,18... | collective-permute-start | bytes 442376 | tf_op jit(solution)/shard_map/ppermute | solution.py:492
  44.8 10.5 %copy-start.1 = (s32[8,16384]{1,0:T(8,128)S(1)}, s32[8,16384]{1,0:T(8,128)}, u32[]{:S(2)}) copy-start(s32[8,16384]{1,0:T(8,128)} %named.1) | copy-start | bytes 1572868
  44.8 10.5 %copy-start.2 = (f32[8,16384]{1,0:T(8,128)S(1)}, f32[8,16384]{1,0:T(8,128)}, u32[]{:S(2)}) copy-start(f32[8,16384]{1,0:T(8,128)} %stiff.1) | copy-start | bytes 1572868
  44.8 10.5 %copy-start.8 = (s32[128]{0:T(128)S(1)}, s32[128]{0:T(128)}, u32[]{:S(2)}) copy-start(s32[128]{0:T(128)} %partner.1) | copy-start | bytes 1540
  50.0 9.6 %collective-permute-start.9 = (f32[128,384]{1,0:T(8,128)S(1)}, f32[128,384]{1,0:T(8,128)S(1)}, u32[]{:S(2)}, u32[]{:S(2)}) collective-permute-start(f32[128,384]{1,0:T(8,128)S(1)} %get-tuple-element.47), channel_id=1, source_target_pairs={{0,16},{1,17},{2,18},{3,19},{4,20},{5,21},{6,22},{7,23},{16,8},{17... | collective-permute-start | bytes 589832 | tf_op jit(solution)/shard_map/ppermute | solution.py:492
  53.4 7.6 %collective-permute-start.10 = (f32[128,384]{1,0:T(8,128)S(1)}, f32[128,384]{1,0:T(8,128)S(1)}, u32[]{:S(2)}, u32[]{:S(2)}) collective-permute-start(f32[128,384]{1,0:T(8,128)S(1)} %get-tuple-element.48), channel_id=1, source_target_pairs={{0,8},{1,9},{2,10},{3,11},{4,12},{5,13},{6,14},{7,15},{16,0},{17,1... | collective-permute-start | bytes 589832 | tf_op jit(solution)/shard_map/ppermute | solution.py:492

commit v12 on v11

--- a/solution.py
+++ b/solution.py
@@ -491,9 +491,9 @@
         flat = [(a[0] * regions + a[1], b[0] * regions + b[1]) for a, b in pairs]
         return lax.ppermute(value, ("grp", "reg"), flat)
 
-    def along_reg(value, members, goes):
+    def along_reg(value, members, goes, core=0):
         pairs = [
-            ((g, r), (g, r + goes[r % 2]))
+            ((g + core, r), (g, r + goes[r % 2]))
             for g in members
             for r in range(regions)
             if 0 <= r + goes[r % 2] < regions
@@ -521,7 +521,7 @@
         + [pltpu.SemaphoreType.DMA((5 * planes + 1,))],
         flops=field_bytes, size=6 * field_bytes, limit=61_950_000, place=HBM,
     )
-    near = along_reg(window, owners, (1, -1))
+    near = along_reg(window, owners, (1, -1), core=1)
     mine, after_deposit = call(
         deposit_kernel, (shaped(tiles + SUB, 2 * BLOCK), small), [SMEM] + [VMEM] * 4,
         (count, cell, vol, drag, ids), flops=2 * 32 * 48 * 65536, size=5 * 4 * slots,
@@ -550,7 +550,7 @@
     )
     message_near = along_reg(message_near, owners, (1, -1))
     message_far = along_reg(message_far, owners, (-1, 1))
-    beyond = along_reg(ends, owners, (-2, 2))
+    beyond = along_reg(ends, owners, (-2, 2), core=1)
     constant, factor, weight, picks = call(
         functools.partial(own_kernel, full),
         (

time: 62.3 us -> 60.2 us (0.966)
  the two profiles are of different devices: /device:TPU:0 before, /device:TPU:16 now
where the time goes in v12:
time: 60.2 us; the launch traced here: 59.9 us
  starting transfers between devices  24.7 us (41%)
  Pallas kernels  22.5 us (37%)
  waiting for transfers between devices  11.5 us (19%)
  between operations  1.02 us (2%)
    ppermute x11, starting transfers between devices, send(): return lax.ppermute(value, ('grp', 'reg'), flat)  24.7 us
    pallas_call x10, Pallas kernels, call(): pl.pallas_call(kernel, out_shape=outs, in_specs=specs, out_specs=jax.tree...  22.5 us
    ppermute x11, waiting for transfers between devices, send(): return lax.ppermute(value, ('grp', 'reg'), flat)  11.5 us
  transfers between devices with their start and end apart: 11, of which 4 were waited for; matrix products, arithmetic and copies ran while one was open for 0% of the time, Pallas kernels for 23%

profile of v12, /device:TPU:16, one launch (start us, length us, event | category | flops | bytes accessed | tf_op | source)
XLA Modules:
  0.0 59.9 jit_solution(6332845109997644934)
XLA Ops:
  0.0 2.5 %shard_map.137 = (f32[8,72,512]{2,1,0:T(8,128)}, f32[72,512]{1,0:T(8,128)}) custom-call(f32[4,128,512]{2,1,0:T(8,128)} %pressure_old.1, f32[4,128,512]{2,1,0:T(8,128)} %source.1, f32[4,128,512]{2,1,0:T(8,128)} %solid_before.1), custom_call_target="tpu_custom_call" | custom-call | flops 589824 | bytes 3538944 | tf_op jit(solution)/shard_map/pallas_call | solution.py:35
  2.6 1.3 %collective-permute-start.2 = (f32[8,72,512]{2,1,0:T(8,128)}, f32[8,72,512]{2,1,0:T(8,128)S(1)}, u32[]{:S(2)}, u32[]{:S(2)}) collective-permute-start(f32[8,72,512]{2,1,0:T(8,128)} %get-tuple-element.29.window.pressure), channel_id=1, source_target_pairs={{8,1},{9,0},{10,3},{11,2},{12,5},{13,4},{14,7},{15,6},{24,17},{25,... | collective-permute-start | bytes 3538952 | tf_op jit(solution)/shard_map/ppermute | solution.py:492
  4.6 1.7 %shard_map.136 = (f32[136,256]{1,0:T(8,128)S(1)}, f32[8,128]{1,0:T(8,128)S(1)}) custom-call(s32[1]{0:T(128)S(6)} %copy.15.count, s32[128,128]{1,0:T(8,128)S(1)} %bitcast.4, f32[128,128]{1,0:T(8,128)S(1)} %bitcast.6, f32[128,128]{1,0:T(8,128)S(1)} %bitcast.8, s32[1,128]{1,0:T(1,128)S(1)} %bitcast.10), custom_call_target="tpu_custom_call" | custom-call | flops 201326592 | bytes 327680 | tf_op jit(solution)/shard_map/pallas_call | solution.py:35
  6.3 3.4 %collective-permute-start.1 = (f32[136,256]{1,0:T(8,128)S(1)}, f32[136,256]{1,0:T(8,128)S(1)}, u32[]{:S(2)}, u32[]{:S(2)}) collective-permute-start(f32[136,256]{1,0:T(8,128)S(1)} %get-tuple-element.28.mine), channel_id=1, source_target_pairs={{0,16},{1,17},{2,18},{3,19},{4,20},{5,21},{6,22},{7,23},{8,0},{9,1... | collective-permute-start | bytes 417800 | tf_op jit(solution)/shard_map/ppermute | solution.py:492
  9.7 2.7 %collective-permute-start = (f32[136,256]{1,0:T(8,128)S(1)}, f32[136,256]{1,0:T(8,128)S(1)}, u32[]{:S(2)}, u32[]{:S(2)}) collective-permute-start(f32[136,256]{1,0:T(8,128)S(1)} %get-tuple-element.28.mine), channel_id=1, source_target_pairs={{0,8},{1,9},{2,10},{3,11},{4,12},{5,13},{6,14},{7,15},{8,16},{9,17... | collective-permute-start | bytes 417800 | tf_op jit(solution)/shard_map/ppermute | solution.py:492
  12.5 3.2 %shard_map.138 = (f32[384,128]{1,0:T(8,128)S(1)}, f32[96,128]{1,0:T(8,128)S(1)}, f32[96,128]{1,0:T(8,128)S(1)}, f32[8,128]{1,0:T(8,128)S(1)}) custom-call(f32[3,16384]{1,0:T(4,128)S(1)} %copy-done.9, f32[3,16384]{1,0:T(4,128)S(1)} %copy-done.3, s32[2,4096]{1,0:T(2,128)S(1)} %copy-done.10, f32[8,128]{1,0:T(8,128)S(1)} %get-tuple-element.30._), custom_call_target="tpu_custom_call" | custom-call | flops 3221225472 | bytes 786432 | tf_op jit(solution)/shard_map/pallas_call | solution.py:35
  15.7 0.8 %collective-permute-start.3 = (f32[96,128]{1,0:T(8,128)S(1)}, f32[96,128]{1,0:T(8,128)S(1)}, u32[]{:S(2)}, u32[]{:S(2)}) collective-permute-start(f32[96,128]{1,0:T(8,128)S(1)} %get-tuple-element.31.halo_near), channel_id=1, source_target_pairs={{8,9},{9,8},{10,11},{11,10},{12,13},{13,12},{14,15},{15,14}} | collective-permute-start | bytes 147464 | tf_op jit(solution)/shard_map/ppermute | solution.py:492
  16.5 0.7 %collective-permute-start.4 = (f32[96,128]{1,0:T(8,128)S(1)}, f32[96,128]{1,0:T(8,128)S(1)}, u32[]{:S(2)}, u32[]{:S(2)}) collective-permute-start(f32[96,128]{1,0:T(8,128)S(1)} %get-tuple-element.32.halo_far), channel_id=1, source_target_pairs={{9,10},{10,9},{11,12},{12,11},{13,14},{14,13}} | collective-permute-start | bytes 147464 | tf_op jit(solution)/shard_map/ppermute | solution.py:492
  17.2 3.1 %collective-permute-done.2.near = f32[8,72,512]{2,1,0:T(8,128)S(1)} collective-permute-done((f32[8,72,512]{2,1,0:T(8,128)}, f32[8,72,512]{2,1,0:T(8,128)S(1)}, u32[]{:S(2)}, u32[]{:S(2)}) %collective-permute-start.2) | collective-permute-done | bytes 1179680 | tf_op jit(solution)/shard_map/ppermute | solution.py:492
  20.3 0.1 shard_map.139
  20.4 3.5 %collective-permute-start.6 = (f32[9,72,512]{2,1,0:T(8,128)S(1)}, f32[9,72,512]{2,1,0:T(8,128)S(1)}, u32[]{:S(2)}, u32[]{:S(2)}) collective-permute-start(f32[9,72,512]{2,1,0:T(8,128)S(1)} %get-tuple-element.39), channel_id=1, source_target_pairs={{0,2},{2,4},{3,1},{4,6},{5,3},{7,5},{16,18},{18,20},{19,17},{20,22... | collective-permute-start | bytes 3981320 | tf_op jit(solution)/shard_map/ppermute | solution.py:492
  24.0 2.3 %collective-permute-start.7 = (f32[456,256]{1,0:T(8,128)S(1)}, f32[456,256]{1,0:T(8,128)S(1)}, u32[]{:S(2)}, u32[]{:S(2)}) collective-permute-start(f32[456,256]{1,0:T(8,128)S(1)} %get-tuple-element.42), channel_id=1, source_target_pairs={{0,1},{1,0},{2,3},{3,2},{4,5},{5,4},{6,7},{7,6},{16,17},{17,16},{1... | collective-permute-start | bytes 1400840 | tf_op jit(solution)/shard_map/ppermute | solution.py:492
  26.3 3.4 %collective-permute-start.5 = (f32[456,256]{1,0:T(8,128)S(1)}, f32[456,256]{1,0:T(8,128)S(1)}, u32[]{:S(2)}, u32[]{:S(2)}) collective-permute-start(f32[456,256]{1,0:T(8,128)S(1)} %get-tuple-element.38), channel_id=1, source_target_pairs={{1,2},{2,1},{3,4},{4,3},{5,6},{6,5},{17,18},{18,17},{19,20},{20,19... | collective-permute-start | bytes 1400840 | tf_op jit(solution)/shard_map/ppermute | solution.py:492
  29.7 1.3 %collective-permute-start.8 = (f32[72,512]{1,0:T(8,128)S(1)}, f32[72,512]{1,0:T(8,128)S(1)}, u32[]{:S(2)}, u32[]{:S(2)}) collective-permute-start(f32[72,512]{1,0:T(8,128)S(1)} %get-tuple-element.43), channel_id=1, source_target_pairs={{9,3},{10,0},{11,5},{12,2},{13,7},{14,4},{25,19},{26,16},{27,21},{... | collective-permute-start | bytes 442376 | tf_op jit(solution)/shard_map/ppermute | solution.py:492
  31.0 1.4 %shard_map.141 = (f32[4,72,512]{2,1,0:T(8,128)S(1)}, f32[4,72,512]{2,1,0:T(8,128)S(1)}, f32[128,128]{1,0:T(8,128)S(1)}, bf16[384,1152]{1,0:T(8,128)(2,1)S(1)}) custom-call(f32[136,256]{1,0:T(8,128)S(1)} %get-tuple-element.28.mine, f32[136,256]{1,0:T(8,128)S(1)} %collective-permute-done._second.second, f32[136,256]{1,0:T(8,128)S(1)} %collective-permute-done.1._third.third, ...), custom_call_target="tpu_custom_call" | custom-call | flops 679477248 | bytes 5308416 | tf_op jit(solution)/shard_map/pallas_call | solution.py:35
  32.4 5.4 %collective-permute-done.8.beyond = f32[72,512]{1,0:T(8,128)S(1)} collective-permute-done((f32[72,512]{1,0:T(8,128)S(1)}, f32[72,512]{1,0:T(8,128)S(1)}, u32[]{:S(2)}, u32[]{:S(2)}) %collective-permute-start.8) | collective-permute-done | bytes 147488 | tf_op jit(solution)/shard_map/ppermute | solution.py:492
  37.8 1.6 %collective-permute-done.7.message.message_near = f32[456,256]{1,0:T(8,128)S(1)} collective-permute-done((f32[456,256]{1,0:T(8,128)S(1)}, f32[456,256]{1,0:T(8,128)S(1)}, u32[]{:S(2)}, u32[]{:S(2)}) %collective-permute-start.7) | collective-permute-done | bytes 466976 | tf_op jit(solution)/shard_map/ppermute | solution.py:492
  39.4 3.2 %shard_map.142 = (f32[4,72,512]{2,1,0:T(8,128)S(1)}, f32[4,72,512]{2,1,0:T(8,128)S(1)}) custom-call(f32[456,256]{1,0:T(8,128)S(1)} %collective-permute-done.7.message.message_near, f32[8,72,512]{2,1,0:T(8,128)S(1)} %copy-done, f32[8,72,512]{2,1,0:T(8,128)S(1)} %collective-permute-done.2.near, f32[72,512]{1,0:T(8,128)S(1)} %collective-permute-done.8.beyond, ...), custom_call_target="tpu_custom_call" | custom-call | flops 679477248 | bytes 5308416 | tf_op jit(solution)/shard_map/pallas_call | solution.py:35
  42.8 5.1 %shard_map.143 = (f32[128,384]{1,0:T(8,128)S(1)}, f32[128,384]{1,0:T(8,128)S(1)}, f32[128,384]{1,0:T(8,128)S(1)}) custom-call(bf16[384,1152]{1,0:T(8,128)(2,1)S(1)} %get-tuple-element.37.picks, f32[456,256]{1,0:T(8,128)S(1)} %collective-permute-done.5.message.message_far, f32[8,72,512]{2,1,0:T(8,128)S(1)} %copy-done, ...), custom_call_target="tpu_custom_call" | custom-call | flops 679477248 | bytes 5308416 | tf_op jit(solution)/shard_map/pallas_call | solution.py:35
  47.9 3.4 %collective-permute-start.9 = (f32[128,384]{1,0:T(8,128)S(1)}, f32[128,384]{1,0:T(8,128)S(1)}, u32[]{:S(2)}, u32[]{:S(2)}) collective-permute-start(f32[128,384]{1,0:T(8,128)S(1)} %get-tuple-element.47), channel_id=1, source_target_pairs={{0,16},{1,17},{2,18},{3,19},{4,20},{5,21},{6,22},{7,23},{16,8},{17... | collective-permute-start | bytes 589832 | tf_op jit(solution)/shard_map/ppermute | solution.py:492
  51.3 1.9 %collective-permute-start.10 = (f32[128,384]{1,0:T(8,128)S(1)}, f32[128,384]{1,0:T(8,128)S(1)}, u32[]{:S(2)}, u32[]{:S(2)}) collective-permute-start(f32[128,384]{1,0:T(8,128)S(1)} %get-tuple-element.48), channel_id=1, source_target_pairs={{0,8},{1,9},{2,10},{3,11},{4,12},{5,13},{6,14},{7,15},{16,0},{17,1... | collective-permute-start | bytes 589832 | tf_op jit(solution)/shard_map/ppermute | solution.py:492
  53.2 4.2 %shard_map.144.contact = f32[384,128]{1,0:T(8,128)S(1)} custom-call(s32[128]{0:T(128)S(1)} %copy-done.8, f32[384,128]{1,0:T(8,128)S(1)} %get-tuple-element.50.state, f32[456,256]{1,0:T(8,128)S(1)} %collective-permute-done.7.message.message_near, f32[456,256]{1,0:T(8,128)S(1)} %collective-permute-done.5.message.message_far, ...), custom_call_target="tpu_custom_call" | custom-call | flops 7864320 | bytes 1310720 | tf_op jit(solution)/shard_map/pallas_call | solution.py:35
  57.4 1.4 %collective-permute-done.10.grads_c = f32[128,384]{1,0:T(8,128)S(1)} collective-permute-done((f32[128,384]{1,0:T(8,128)S(1)}, f32[128,384]{1,0:T(8,128)S(1)}, u32[]{:S(2)}, u32[]{:S(2)}) %collective-permute-start.10) | collective-permute-done | bytes 196640 | tf_op jit(solution)/shard_map/ppermute | solution.py:492
  58.8 1.0 %shard_map.145 = f32[3,16384]{1,0:T(4,128)} custom-call(s32[1]{0:T(128)S(6)} %copy.15.count, f32[128,384]{1,0:T(8,128)S(1)} %get-tuple-element.46._.grads_a, f32[128,384]{1,0:T(8,128)S(1)} %collective-permute-done.9.grads_b, f32[128,384]{1,0:T(8,128)S(1)} %collective-permute-done.10.grads_c, f32[128,128]{1,0:T(8,128)S(1)} %get-tuple-element.49.weight, ...), custom_call_target="tpu_custom_call" | custom-call | flops 983040 | bytes 1310720 | tf_op jit(solution)/shard_map/pallas_call | solution.py:35
  (32 shorter events, 0.2 us)
Async XLA Ops:
  0.0 4.5 %copy-start.11 = (s32[128]{0:T(128)S(1)}, s32[128]{0:T(128)}, u32[]{:S(2)}) copy-start(s32[128]{0:T(128)} %param.24) | copy-start | bytes 1540
  0.0 4.5 %copy-start.5 = (s32[16384]{0:T(1024)S(1)}, s32[16384]{0:T(1024)}, u32[]{:S(2)}) copy-start(s32[16384]{0:T(1024)} %param.23) | copy-start | bytes 196612
  0.0 4.5 %copy-start.7 = (f32[16384]{0:T(1024)S(1)}, f32[16384]{0:T(1024)}, u32[]{:S(2)}) copy-start(f32[16384]{0:T(1024)} %param.17) | copy-start | bytes 196612
  0.0 4.5 %copy-start.6 = (f32[16384]{0:T(1024)S(1)}, f32[16384]{0:T(1024)}, u32[]{:S(2)}) copy-start(f32[16384]{0:T(1024)} %param.16) | copy-start | bytes 196612
  0.0 12.4 %copy-start.3 = (f32[3,16384]{1,0:T(4,128)S(1)}, f32[3,16384]{1,0:T(4,128)}, u32[]{:S(2)}) copy-start(f32[3,16384]{1,0:T(4,128)} %vel.3) | copy-start | bytes 589828
  0.0 12.4 %copy-start.10 = (s32[2,4096]{1,0:T(2,128)S(1)}, s32[2,4096]{1,0:T(2,128)}, u32[]{:S(2)}) copy-start(s32[2,4096]{1,0:T(2,128)} %lists.1) | copy-start | bytes 98308
  0.0 12.4 %copy-start.9 = (f32[3,16384]{1,0:T(4,128)S(1)}, f32[3,16384]{1,0:T(4,128)}, u32[]{:S(2)}) copy-start(f32[3,16384]{1,0:T(4,128)} %pos.1) | copy-start | bytes 589828
  2.6 17.7 %collective-permute-start.2 = (f32[8,72,512]{2,1,0:T(8,128)}, f32[8,72,512]{2,1,0:T(8,128)S(1)}, u32[]{:S(2)}, u32[]{:S(2)}) collective-permute-start(f32[8,72,512]{2,1,0:T(8,128)} %get-tuple-element.29.window.pressure), channel_id=1, source_target_pairs={{8,1},{9,0},{10,3},{11,2},{12,5},{13,4},{14,7},{15,6},{24,17},{25,... | collective-permute-start | bytes 3538952 | tf_op jit(solution)/shard_map/ppermute | solution.py:492
  6.3 11.0 %collective-permute-start.1 = (f32[136,256]{1,0:T(8,128)S(1)}, f32[136,256]{1,0:T(8,128)S(1)}, u32[]{:S(2)}, u32[]{:S(2)}) collective-permute-start(f32[136,256]{1,0:T(8,128)S(1)} %get-tuple-element.28.mine), channel_id=1, source_target_pairs={{0,16},{1,17},{2,18},{3,19},{4,20},{5,21},{6,22},{7,23},{8,0},{9,1... | collective-permute-start | bytes 417800 | tf_op jit(solution)/shard_map/ppermute | solution.py:492
  9.7 7.6 %collective-permute-start = (f32[136,256]{1,0:T(8,128)S(1)}, f32[136,256]{1,0:T(8,128)S(1)}, u32[]{:S(2)}, u32[]{:S(2)}) collective-permute-start(f32[136,256]{1,0:T(8,128)S(1)} %get-tuple-element.28.mine), channel_id=1, source_target_pairs={{0,8},{1,9},{2,10},{3,11},{4,12},{5,13},{6,14},{7,15},{8,16},{9,17... | collective-permute-start | bytes 417800 | tf_op jit(solution)/shard_map/ppermute | solution.py:492
  12.5 7.9 %copy-start.4 = (f32[72,512]{1,0:T(8,128)S(1)}, f32[72,512]{1,0:T(8,128)}, u32[]{:S(2)}) copy-start(f32[72,512]{1,0:T(8,128)} %get-tuple-element.33.inner) | copy-start | bytes 442372
  15.7 8.2 %copy-start = (f32[8,72,512]{2,1,0:T(8,128)S(1)}, f32[8,72,512]{2,1,0:T(8,128)}, u32[]{:S(2)}) copy-start(f32[8,72,512]{2,1,0:T(8,128)} %get-tuple-element.29.window.pressure) | copy-start | bytes 3538948
  15.7 1.5 %collective-permute-start.3 = (f32[96,128]{1,0:T(8,128)S(1)}, f32[96,128]{1,0:T(8,128)S(1)}, u32[]{:S(2)}, u32[]{:S(2)}) collective-permute-start(f32[96,128]{1,0:T(8,128)S(1)} %get-tuple-element.31.halo_near), channel_id=1, source_target_pairs={{8,9},{9,8},{10,11},{11,10},{12,13},{13,12},{14,15},{15,14}} | collective-permute-start | bytes 147464 | tf_op jit(solution)/shard_map/ppermute | solution.py:492
  16.5 0.7 %collective-permute-start.4 = (f32[96,128]{1,0:T(8,128)S(1)}, f32[96,128]{1,0:T(8,128)S(1)}, u32[]{:S(2)}, u32[]{:S(2)}) collective-permute-start(f32[96,128]{1,0:T(8,128)S(1)} %get-tuple-element.32.halo_far), channel_id=1, source_target_pairs={{9,10},{10,9},{11,12},{12,11},{13,14},{14,13}} | collective-permute-start | bytes 147464 | tf_op jit(solution)/shard_map/ppermute | solution.py:492
  20.4 22.3 %collective-permute-start.6 = (f32[9,72,512]{2,1,0:T(8,128)S(1)}, f32[9,72,512]{2,1,0:T(8,128)S(1)}, u32[]{:S(2)}, u32[]{:S(2)}) collective-permute-start(f32[9,72,512]{2,1,0:T(8,128)S(1)} %get-tuple-element.39), channel_id=1, source_target_pairs={{0,2},{2,4},{3,1},{4,6},{5,3},{7,5},{16,18},{18,20},{19,17},{20,22... | collective-permute-start | bytes 3981320 | tf_op jit(solution)/shard_map/ppermute | solution.py:492
  24.0 15.5 %collective-permute-start.7 = (f32[456,256]{1,0:T(8,128)S(1)}, f32[456,256]{1,0:T(8,128)S(1)}, u32[]{:S(2)}, u32[]{:S(2)}) collective-permute-start(f32[456,256]{1,0:T(8,128)S(1)} %get-tuple-element.42), channel_id=1, source_target_pairs={{0,1},{1,0},{2,3},{3,2},{4,5},{5,4},{6,7},{7,6},{16,17},{17,16},{1... | collective-permute-start | bytes 1400840 | tf_op jit(solution)/shard_map/ppermute | solution.py:492
  26.3 16.4 %collective-permute-start.5 = (f32[456,256]{1,0:T(8,128)S(1)}, f32[456,256]{1,0:T(8,128)S(1)}, u32[]{:S(2)}, u32[]{:S(2)}) collective-permute-start(f32[456,256]{1,0:T(8,128)S(1)} %get-tuple-element.38), channel_id=1, source_target_pairs={{1,2},{2,1},{3,4},{4,3},{5,6},{6,5},{17,18},{18,17},{19,20},{20,19... | collective-permute-start | bytes 1400840 | tf_op jit(solution)/shard_map/ppermute | solution.py:492
  29.7 8.1 %collective-permute-start.8 = (f32[72,512]{1,0:T(8,128)S(1)}, f32[72,512]{1,0:T(8,128)S(1)}, u32[]{:S(2)}, u32[]{:S(2)}) collective-permute-start(f32[72,512]{1,0:T(8,128)S(1)} %get-tuple-element.43), channel_id=1, source_target_pairs={{9,3},{10,0},{11,5},{12,2},{13,7},{14,4},{25,19},{26,16},{27,21},{... | collective-permute-start | bytes 442376 | tf_op jit(solution)/shard_map/ppermute | solution.py:492
  42.7 10.5 %copy-start.1 = (s32[8,16384]{1,0:T(8,128)S(1)}, s32[8,16384]{1,0:T(8,128)}, u32[]{:S(2)}) copy-start(s32[8,16384]{1,0:T(8,128)} %named.1) | copy-start | bytes 1572868
  42.7 10.5 %copy-start.2 = (f32[8,16384]{1,0:T(8,128)S(1)}, f32[8,16384]{1,0:T(8,128)}, u32[]{:S(2)}) copy-start(f32[8,16384]{1,0:T(8,128)} %stiff.1) | copy-start | bytes 1572868
  42.7 10.5 %copy-start.8 = (s32[128]{0:T(128)S(1)}, s32[128]{0:T(128)}, u32[]{:S(2)}) copy-start(s32[128]{0:T(128)} %partner.1) | copy-start | bytes 1540
  47.9 9.6 %collective-permute-start.9 = (f32[128,384]{1,0:T(8,128)S(1)}, f32[128,384]{1,0:T(8,128)S(1)}, u32[]{:S(2)}, u32[]{:S(2)}) collective-permute-start(f32[128,384]{1,0:T(8,128)S(1)} %get-tuple-element.47), channel_id=1, source_target_pairs={{0,16},{1,17},{2,18},{3,19},{4,20},{5,21},{6,22},{7,23},{16,8},{17... | collective-permute-start | bytes 589832 | tf_op jit(solution)/shard_map/ppermute | solution.py:492
  51.3 7.6 %collective-permute-start.10 = (f32[128,384]{1,0:T(8,128)S(1)}, f32[128,384]{1,0:T(8,128)S(1)}, u32[]{:S(2)}, u32[]{:S(2)}) collective-permute-start(f32[128,384]{1,0:T(8,128)S(1)} %get-tuple-element.48), channel_id=1, source_target_pairs={{0,8},{1,9},{2,10},{3,11},{4,12},{5,13},{6,14},{7,15},{16,0},{17,1... | collective-permute-start | bytes 589832 | tf_op jit(solution)/shard_map/ppermute | solution.py:492

commit v13 on v12

--- a/solution.py
+++ b/solution.py
@@ -11,6 +11,7 @@
 SUB = 8
 CORES = 2
 ITERS = 4
+HEAD = 1
 SPRING = 1.0
 DAMPING = 0.5
 TIME_STEP = 0.5
@@ -66,7 +67,9 @@
     return high, (value - high.astype(F32)).astype(BF16)
 
 
-def window_kernel(pressure_old, source, solid_before, window, inner, pressure, driven, solid, sems):
+def window_kernel(
+    pressure_old, source, solid_before, early, late, ends, inner, pressure, driven, solid, sems
+):
     planes, height, _ = solid.shape
     place = Place(pressure_old.shape[1], height)
     rows = pl.ds(place.first, height)
@@ -80,9 +83,13 @@
         [copy(whole.at[x, rows, :], part.at[x]) for x in range(planes)]
         for whole, part in ((pressure_old, pressure), (source, driven), (solid_before, solid))
     ]
-    stored = [copy(pressure.at[x], window.at[x]) for x in range(planes)]
-    stored += [copy(driven.at[x], window.at[planes + x]) for x in range(planes)]
-    stored.append(copy(pressure.at[(1 - place.parity) * (planes - 1)], inner))
+    stored = [copy(pressure.at[x], early.at[x]) for x in range(planes)]
+    for x in range(planes):
+        stored.append(copy(driven.at[x], early.at[planes + x] if x < HEAD else late.at[x - HEAD]))
+    sides = (
+        copy(pressure.at[place.parity * (planes - 1)], ends),
+        copy(pressure.at[(1 - place.parity) * (planes - 1)], inner),
+    )
     for x in range(planes):
         for part in fetched:
             part[x].start()
@@ -93,8 +100,11 @@
         fetched[2][x].wait()
         driven[x] = driven[x] - solid[x]
         stored[planes + x].start()
-    stored[2 * planes].start()
+    for one in sides:
+        one.start()
     for one in stored:
+        one.wait()
+    for one in sides:
         one.wait()
 
 
@@ -196,9 +206,8 @@
         lax.fori_loop(0, rows // 2, step, 0, unroll=8)
 
 
-def message_kernel(mine, second, third, halo_near, halo_far, window, _, near, far, ends, dummy):
+def message_kernel(mine, second, third, halo_near, halo_far, _, near, far, dummy):
     dummy[...] = jnp.zeros(dummy.shape, F32)
-    ends[...] = window[(lax.axis_index("reg") % 2) * (window.shape[0] // 2 - 1)]
     stride = mine.shape[0]
     half = halo_near.shape[0] // 2
     rows = near.shape[0] - half
@@ -285,8 +294,12 @@
     return ids, gathered
 
 
-def coefficients(gathered, tiles, first, full, driven, planes, constant, factor, turned, present):
-    _, height, width = driven.shape
+def driven_of(early, late, planes):
+    return lambda x: early[planes + x] if x < HEAD else late[x - HEAD]
+
+
+def coefficients(gathered, tiles, first, full, driven_at, constant, factor, turned, present):
+    planes, height, width = constant.shape
     zones = width // BLOCK
     shape = (zones * height, 3 * tiles)
     line = iota(shape, 0)
@@ -303,20 +316,23 @@
         for zone in range(zones):
             lanes = slice(zone * BLOCK, (zone + 1) * BLOCK)
             rows = slice(zone * height, (zone + 1) * height)
-            driving = driven[x, :, lanes] + solid[rows]
+            driving = driven_at(x)[:, lanes] + solid[rows]
             constant[at, :, lanes] = driving * inverse[rows]
             factor[at, :, lanes] = scale[rows]
 
 
 def own_kernel(
-    full, mine, second, third, window, _message, constant, factor, weight, picks
+    full, mine, second, third, early, late, _message, constant, factor, weight, picks
 ):
     tiles = weight.shape[0]
     planes, height, width = constant.shape
     place = Place(full, height)
     zones = width // BLOCK
     ids, gathered = placed((mine, second, third), tiles)
-    coefficients(gathered, tiles, place.first, full, window.at[planes:], planes, constant, factor, place.even, None)
+    coefficients(
+        gathered, tiles, place.first, full, driven_of(early, late, planes), constant, factor,
+        place.even, None,
+    )
     turned = [
         jnp.transpose(
             jnp.broadcast_to(ids[:, i * tiles : (i + 1) * tiles], (BLOCK, tiles)).astype(F32)
@@ -353,15 +369,15 @@
 
 
 def near_kernel(
-    full, tiles, message, pressure, near, beyond, own_constant, own_factor, kept_even, kept_odd,
+    full, tiles, message, pressure, near, near_late, beyond, own_constant, own_factor, kept_even, kept_odd,
     constant, factor, old, new,
 ):
     planes, height, width = own_constant.shape
     place = Place(full, height)
     rim = planes + 1
     coefficients(
-        deposits_of(message, tiles), tiles, place.first, full, near.at[planes:], planes,
-        constant, factor, place.even, jnp.where(place.odd, place.lower, place.upper),
+        deposits_of(message, tiles), tiles, place.first, full,
+        driven_of(near, near_late, planes), constant, factor, place.even, jnp.where(place.odd, place.lower, place.upper),
     )
     old[0] = beyond[...]
     for x in range(planes):
@@ -381,7 +397,7 @@
 
 
 def far_kernel(
-    full, tiles, picks, message, pressure, far, own_constant, own_factor, kept_even, kept_odd,
+    full, tiles, picks, message, pressure, far, far_late, own_constant, own_factor, kept_even, kept_odd,
     out_a, out_b, out_c, constant, factor, old, new, fields,
 ):
     planes, height, width = own_constant.shape
@@ -389,8 +405,8 @@
     place = Place(full, height)
     rim = planes + 1
     coefficients(
-        deposits_of(message, tiles), tiles, place.first, full, far.at[planes : 2 * planes], planes,
-        constant, factor, place.even, jnp.where(place.odd, place.upper, place.lower),
+        deposits_of(message, tiles), tiles, place.first, full,
+        driven_of(far, far_late, planes), constant, factor, place.even, jnp.where(place.odd, place.upper, place.lower),
     )
     old[planes : 2 * planes] = kept_even[...]
     new[planes : 2 * planes] = kept_odd[...]
@@ -398,7 +414,7 @@
     for x in range(planes):
         at = jnp.where(place.even, planes - 1 - x, x)
         old[rim + planes + x] = far[at]
-    old[rim + 2 * planes] = far[2 * planes]
+    old[rim + 2 * planes] = far[planes + HEAD]
     buffers = (old, new)
     edge = rim + planes
     for index in range(planes):
@@ -514,14 +530,20 @@
     field = shaped(planes, height, width)
     plane = shaped(height, width)
     small = shaped(SUB, BLOCK)
-    window, inner = call(
-        window_kernel, (shaped(2 * planes, height, width), plane),
+    early, late, ends, inner = call(
+        window_kernel,
+        (
+            shaped(planes + HEAD, height, width), shaped(planes - HEAD, height, width), plane,
+            plane,
+        ),
         [HBM] * 3, (pressure_old, pressure_source, solid_old),
         [pltpu.VMEM((planes, height, width), F32)] * 3
-        + [pltpu.SemaphoreType.DMA((5 * planes + 1,))],
+        + [pltpu.SemaphoreType.DMA((5 * planes + 2,))],
         flops=field_bytes, size=6 * field_bytes, limit=61_950_000, place=HBM,
     )
-    near = along_reg(window, owners, (1, -1), core=1)
+    near = along_reg(early, owners, (1, -1), core=1)
+    near_late = along_reg(late, owners, (1, -1), core=1)
+    beyond = along_reg(ends, owners, (-2, 2), core=1)
     mine, after_deposit = call(
         deposit_kernel, (shaped(tiles + SUB, 2 * BLOCK), small), [SMEM] + [VMEM] * 4,
         (count, cell, vol, drag, ids), flops=2 * 32 * 48 * 65536, size=5 * 4 * slots,
@@ -539,38 +561,38 @@
     came_near = along_reg(halo_near, others, (1, -1))
     came_far = along_reg(halo_far, others, (-1, 1))
     far, after_forward = call(
-        forward_kernel, (shaped(2 * planes + 1, height, width), small), [VMEM] * 7,
+        forward_kernel, (shaped(planes + HEAD + 1, height, width), small), [VMEM] * 7,
         (near, inner, after_halo, second, third, came_near, came_far), size=5 * field_bytes,
     )
     far = along_reg(far, owners, (2, -2))
+    far_late = along_reg(near_late, owners, (2, -2))
     message = shaped(holding * (tiles + SUB) + 3 * rows // 2, 2 * BLOCK)
-    message_near, message_far, ends, after_message = call(
-        message_kernel, (message, message, plane, small), [VMEM] * 7,
-        (mine, second, third, halo_near, halo_far, window, after_forward), size=8 * 2 * BLOCK * 500,
+    message_near, message_far, after_message = call(
+        message_kernel, (message, message, small), [VMEM] * 6,
+        (mine, second, third, halo_near, halo_far, after_forward), size=8 * 2 * BLOCK * 500,
     )
     message_near = along_reg(message_near, owners, (1, -1))
     message_far = along_reg(message_far, owners, (-1, 1))
-    beyond = along_reg(ends, owners, (-2, 2), core=1)
     constant, factor, weight, picks = call(
         functools.partial(own_kernel, full),
         (
             field, field, shaped(tiles, BLOCK),
             jax.ShapeDtypeStruct((3 * tiles, planes * height * width // BLOCK), BF16),
         ),
-        [VMEM] * 5, (mine, second, third, window, after_message),
+        [VMEM] * 6, (mine, second, third, early, late, after_message),
         flops=planes * height * 4 * 384 * 256 * 6, size=9 * field_bytes,
     )
     window_of = lambda count: pltpu.VMEM((count, height, width), F32)
     kept_even, kept_odd = call(
-        functools.partial(near_kernel, full, tiles), (field, field), [VMEM] * 6,
-        (message_near, window, near, beyond, constant, factor),
+        functools.partial(near_kernel, full, tiles), (field, field), [VMEM] * 7,
+        (message_near, early, near, near_late, beyond, constant, factor),
         [window_of(planes)] * 2 + [window_of(2 * planes + 1)] * 2,
         flops=planes * height * 4 * 384 * 256 * 6, size=9 * field_bytes,
     )
     grads = shaped(tiles, 3 * BLOCK)
     grads_a, grads_b, grads_c = call(
-        functools.partial(far_kernel, full, tiles), (grads,) * 3, [VMEM] * 8,
-        (picks, message_far, window, far, constant, factor, kept_even, kept_odd),
+        functools.partial(far_kernel, full, tiles), (grads,) * 3, [VMEM] * 9,
+        (picks, message_far, early, far, far_late, constant, factor, kept_even, kept_odd),
         [window_of(planes)] * 2
         + [window_of(3 * planes + 2)] * 2
         + [pltpu.VMEM((planes * height * width // BLOCK, 3 * BLOCK), F32)],

time: 60.2 us -> 67.8 us (1.13)
  the two profiles are of different devices: /device:TPU:16 before, /device:TPU:0 now
where the time goes in v13:
time: 67.8 us; the launch traced here: 67.4 us
  starting transfers between devices  30.9 us (46%)
  Pallas kernels  22.5 us (33%)
  waiting for transfers between devices  11.7 us (17%)
  local copies, waits for them, and re-layouts  1.3 us (2%)
  between operations  1.05 us (2%)
    ppermute x13, starting transfers between devices, send(): return lax.ppermute(value, ('grp', 'reg'), flat)  30.9 us
    pallas_call x10, Pallas kernels, call(): pl.pallas_call(kernel, out_shape=outs, in_specs=specs, out_specs=jax.tree...  22.5 us
    ppermute x13, waiting for transfers between devices, send(): return lax.ppermute(value, ('grp', 'reg'), flat)  11.7 us
  transfers between devices with their start and end apart: 13, of which 3 were waited for; matrix products, arithmetic and copies ran while one was open for 0% of the time, Pallas kernels for 21%

profile of v13, /device:TPU:0, one launch (start us, length us, event | category | flops | bytes accessed | tf_op | source)
XLA Modules:
  0.0 67.4 jit_solution(6268587537141421489)
XLA Ops:
  0.0 2.5 %shard_map.137 = (f32[5,72,512]{2,1,0:T(8,128)}, f32[3,72,512]{2,1,0:T(8,128)}, f32[72,512]{1,0:T(8,128)}, f32[72,512]{1,0:T(8,128)}) custom-call(f32[4,128,512]{2,1,0:T(8,128)} %pressure_old.1, f32[4,128,512]{2,1,0:T(8,128)} %source.1, f32[4,128,512]{2,1,0:T(8,128)} %solid_before.1), custom_call_target="tpu_custom_call" | custom-call | flops 589824 | bytes 3538944 | tf_op jit(solution)/shard_map/pallas_call | solution.py:36
  2.5 1.3 %collective-permute-start.2 = (f32[5,72,512]{2,1,0:T(8,128)}, f32[5,72,512]{2,1,0:T(8,128)S(1)}, u32[]{:S(2)}, u32[]{:S(2)}) collective-permute-start(f32[5,72,512]{2,1,0:T(8,128)} %get-tuple-element.30.early.pressure), channel_id=1, source_target_pairs={{8,1},{9,0},{10,3},{11,2},{12,5},{13,4},{14,7},{15,6},{24,17},{25,... | collective-permute-start | bytes 2211848 | tf_op jit(solution)/shard_map/ppermute | solution.py:508
  5.1 1.7 %shard_map.136 = (f32[136,256]{1,0:T(8,128)S(1)}, f32[8,128]{1,0:T(8,128)S(1)}) custom-call(s32[1]{0:T(128)S(6)} %copy.15.count, s32[128,128]{1,0:T(8,128)S(1)} %bitcast.4, f32[128,128]{1,0:T(8,128)S(1)} %bitcast.6, f32[128,128]{1,0:T(8,128)S(1)} %bitcast.8, s32[1,128]{1,0:T(1,128)S(1)} %bitcast.10), custom_call_target="tpu_custom_call" | custom-call | flops 201326592 | bytes 327680 | tf_op jit(solution)/shard_map/pallas_call | solution.py:36
  6.8 5.7 %collective-permute-start = (f32[136,256]{1,0:T(8,128)S(1)}, f32[136,256]{1,0:T(8,128)S(1)}, u32[]{:S(2)}, u32[]{:S(2)}) collective-permute-start(f32[136,256]{1,0:T(8,128)S(1)} %get-tuple-element.29.mine), channel_id=1, source_target_pairs={{0,8},{1,9},{2,10},{3,11},{4,12},{5,13},{6,14},{7,15},{8,16},{9,17... | collective-permute-start | bytes 417800 | tf_op jit(solution)/shard_map/ppermute | solution.py:508
  12.5 1.9 %collective-permute-start.1 = (f32[136,256]{1,0:T(8,128)S(1)}, f32[136,256]{1,0:T(8,128)S(1)}, u32[]{:S(2)}, u32[]{:S(2)}) collective-permute-start(f32[136,256]{1,0:T(8,128)S(1)} %get-tuple-element.29.mine), channel_id=1, source_target_pairs={{0,16},{1,17},{2,18},{3,19},{4,20},{5,21},{6,22},{7,23},{8,0},{9,1... | collective-permute-start | bytes 417800 | tf_op jit(solution)/shard_map/ppermute | solution.py:508
  14.5 3.2 %shard_map.138 = (f32[384,128]{1,0:T(8,128)S(1)}, f32[96,128]{1,0:T(8,128)S(1)}, f32[96,128]{1,0:T(8,128)S(1)}, f32[8,128]{1,0:T(8,128)S(1)}) custom-call(f32[3,16384]{1,0:T(4,128)S(1)} %copy-done.10, f32[3,16384]{1,0:T(4,128)S(1)} %copy-done.3, s32[2,4096]{1,0:T(2,128)S(1)} %copy-done.11, f32[8,128]{1,0:T(8,128)S(1)} %get-tuple-element.32._), custom_call_target="tpu_custom_call" | custom-call | flops 3221225472 | bytes 786432 | tf_op jit(solution)/shard_map/pallas_call | solution.py:36
  17.7 0.7 collective-permute-start.3
  18.4 0.7 collective-permute-start.4
  19.1 1.3 %collective-permute-start.7 = (f32[3,72,512]{2,1,0:T(8,128)S(1)}, f32[3,72,512]{2,1,0:T(8,128)S(1)}, u32[]{:S(2)}, u32[]{:S(2)}) collective-permute-start(f32[3,72,512]{2,1,0:T(8,128)S(1)} %copy-done.9), channel_id=1, source_target_pairs={{8,1},{9,0},{10,3},{11,2},{12,5},{13,4},{14,7},{15,6},{24,17},{25,... | collective-permute-start | bytes 1327112 | tf_op jit(solution)/shard_map/ppermute | solution.py:508
  20.5 3.7 %collective-permute-start.6 = (f32[6,72,512]{2,1,0:T(8,128)S(1)}, f32[6,72,512]{2,1,0:T(8,128)S(1)}, u32[]{:S(2)}, u32[]{:S(2)}) collective-permute-start(f32[6,72,512]{2,1,0:T(8,128)S(1)} %get-tuple-element.41), channel_id=1, source_target_pairs={{0,2},{2,4},{3,1},{4,6},{5,3},{7,5},{16,18},{18,20},{19,17},{20,22... | collective-permute-start | bytes 2654216 | tf_op jit(solution)/shard_map/ppermute | solution.py:508
  24.3 1.9 %collective-permute-start.9 = (f32[456,256]{1,0:T(8,128)S(1)}, f32[456,256]{1,0:T(8,128)S(1)}, u32[]{:S(2)}, u32[]{:S(2)}) collective-permute-start(f32[456,256]{1,0:T(8,128)S(1)} %get-tuple-element.44), channel_id=1, source_target_pairs={{0,1},{1,0},{2,3},{3,2},{4,5},{5,4},{6,7},{7,6},{16,17},{17,16},{1... | collective-permute-start | bytes 1400840 | tf_op jit(solution)/shard_map/ppermute | solution.py:508
  26.2 0.7 %collective-permute-start.5 = (f32[456,256]{1,0:T(8,128)S(1)}, f32[456,256]{1,0:T(8,128)S(1)}, u32[]{:S(2)}, u32[]{:S(2)}) collective-permute-start(f32[456,256]{1,0:T(8,128)S(1)} %get-tuple-element.40), channel_id=1, source_target_pairs={{1,2},{2,1},{3,4},{4,3},{5,6},{6,5},{17,18},{18,17},{19,20},{20,19... | collective-permute-start | bytes 1400840 | tf_op jit(solution)/shard_map/ppermute | solution.py:508
  26.9 7.1 %collective-permute-done.7.near_late = f32[3,72,512]{2,1,0:T(8,128)S(1)} collective-permute-done((f32[3,72,512]{2,1,0:T(8,128)S(1)}, f32[3,72,512]{2,1,0:T(8,128)S(1)}, u32[]{:S(2)}, u32[]{:S(2)}) %collective-permute-start.7) | collective-permute-done | bytes 442400 | tf_op jit(solution)/shard_map/ppermute | solution.py:508
  34.1 8.6 %collective-permute-start.8 = (f32[3,72,512]{2,1,0:T(8,128)S(1)}, f32[3,72,512]{2,1,0:T(8,128)S(1)}, u32[]{:S(2)}, u32[]{:S(2)}) collective-permute-start(f32[3,72,512]{2,1,0:T(8,128)S(1)} %collective-permute-done.7.near_late), channel_id=1, source_target_pairs={{0,2},{2,4},{3,1},{4,6},{5,3},{7,5},{16,18},{18,20},{19,17},{20,22... | collective-permute-start | bytes 1327112 | tf_op jit(solution)/shard_map/ppermute | solution.py:508
  42.6 1.3 %collective-permute-start.10 = (f32[72,512]{1,0:T(8,128)S(1)}, f32[72,512]{1,0:T(8,128)S(1)}, u32[]{:S(2)}, u32[]{:S(2)}) collective-permute-start(f32[72,512]{1,0:T(8,128)S(1)} %copy-done.13), channel_id=1, source_target_pairs={{9,3},{10,0},{11,5},{12,2},{13,7},{14,4},{25,19},{26,16},{27,21},{... | collective-permute-start | bytes 442376 | tf_op jit(solution)/shard_map/ppermute | solution.py:508
  43.9 1.4 %shard_map.141 = (f32[4,72,512]{2,1,0:T(8,128)S(1)}, f32[4,72,512]{2,1,0:T(8,128)S(1)}, f32[128,128]{1,0:T(8,128)S(1)}, bf16[384,1152]{1,0:T(8,128)(2,1)S(1)}) custom-call(f32[136,256]{1,0:T(8,128)S(1)} %get-tuple-element.29.mine, f32[136,256]{1,0:T(8,128)S(1)} %collective-permute-done._second.second, f32[136,256]{1,0:T(8,128)S(1)} %collective-permute-done.1._third.third, ...), custom_call_target="tpu_custom_call" | custom-call | flops 679477248 | bytes 5308416 | tf_op jit(solution)/shard_map/pallas_call | solution.py:36
  45.3 3.8 %collective-permute-done.10.beyond = f32[72,512]{1,0:T(8,128)S(1)} collective-permute-done((f32[72,512]{1,0:T(8,128)S(1)}, f32[72,512]{1,0:T(8,128)S(1)}, u32[]{:S(2)}, u32[]{:S(2)}) %collective-permute-start.10) | collective-permute-done | bytes 147488 | tf_op jit(solution)/shard_map/ppermute | solution.py:508
  49.1 3.2 %shard_map.142 = (f32[4,72,512]{2,1,0:T(8,128)S(1)}, f32[4,72,512]{2,1,0:T(8,128)S(1)}) custom-call(f32[456,256]{1,0:T(8,128)S(1)} %collective-permute-done.9.message.message_near, f32[5,72,512]{2,1,0:T(8,128)S(1)} %copy-done, f32[5,72,512]{2,1,0:T(8,128)S(1)} %collective-permute-done.2.near, f32[3,72,512]{2,1,0:T(8,128)S(1)} %collective-permute-done.7.near_late, ...), custom_call_target="tpu_custom_call" | custom-call | flops 679477248 | bytes 5308416 | tf_op jit(solution)/shard_map/pallas_call | solution.py:36
  52.4 5.1 %shard_map.143 = (f32[128,384]{1,0:T(8,128)S(1)}, f32[128,384]{1,0:T(8,128)S(1)}, f32[128,384]{1,0:T(8,128)S(1)}) custom-call(bf16[384,1152]{1,0:T(8,128)(2,1)S(1)} %get-tuple-element.39.picks, f32[456,256]{1,0:T(8,128)S(1)} %collective-permute-done.5.message.message_far, f32[5,72,512]{2,1,0:T(8,128)S(1)} %copy-done, ...), custom_call_target="tpu_custom_call" | custom-call | flops 679477248 | bytes 5308416 | tf_op jit(solution)/shard_map/pallas_call | solution.py:36
  57.5 1.3 %collective-permute-start.11 = (f32[128,384]{1,0:T(8,128)S(1)}, f32[128,384]{1,0:T(8,128)S(1)}, u32[]{:S(2)}, u32[]{:S(2)}) collective-permute-start(f32[128,384]{1,0:T(8,128)S(1)} %get-tuple-element.49), channel_id=1, source_target_pairs={{0,16},{1,17},{2,18},{3,19},{4,20},{5,21},{6,22},{7,23},{16,8},{17... | collective-permute-start | bytes 589832 | tf_op jit(solution)/shard_map/ppermute | solution.py:508
  58.8 1.9 %collective-permute-start.12 = (f32[128,384]{1,0:T(8,128)S(1)}, f32[128,384]{1,0:T(8,128)S(1)}, u32[]{:S(2)}, u32[]{:S(2)}) collective-permute-start(f32[128,384]{1,0:T(8,128)S(1)} %get-tuple-element.50), channel_id=1, source_target_pairs={{0,8},{1,9},{2,10},{3,11},{4,12},{5,13},{6,14},{7,15},{16,0},{17,1... | collective-permute-start | bytes 589832 | tf_op jit(solution)/shard_map/ppermute | solution.py:508
  61.4 4.2 %shard_map.144.contact = f32[384,128]{1,0:T(8,128)S(1)} custom-call(s32[128]{0:T(128)S(1)} %copy-done.8, f32[384,128]{1,0:T(8,128)S(1)} %get-tuple-element.52.state, f32[456,256]{1,0:T(8,128)S(1)} %collective-permute-done.9.message.message_near, f32[456,256]{1,0:T(8,128)S(1)} %collective-permute-done.5.message.message_far, ...), custom_call_target="tpu_custom_call" | custom-call | flops 7864320 | bytes 1310720 | tf_op jit(solution)/shard_map/pallas_call | solution.py:36
  65.6 0.8 %collective-permute-done.12.grads_c = f32[128,384]{1,0:T(8,128)S(1)} collective-permute-done((f32[128,384]{1,0:T(8,128)S(1)}, f32[128,384]{1,0:T(8,128)S(1)}, u32[]{:S(2)}, u32[]{:S(2)}) %collective-permute-start.12) | collective-permute-done | bytes 196640 | tf_op jit(solution)/shard_map/ppermute | solution.py:508
  66.4 1.0 %shard_map.145 = f32[3,16384]{1,0:T(4,128)} custom-call(s32[1]{0:T(128)S(6)} %copy.15.count, f32[128,384]{1,0:T(8,128)S(1)} %get-tuple-element.48._.grads_a, f32[128,384]{1,0:T(8,128)S(1)} %collective-permute-done.11.grads_b, f32[128,384]{1,0:T(8,128)S(1)} %collective-permute-done.12.grads_c, f32[128,128]{1,0:T(8,128)S(1)} %get-tuple-element.51.weight, ...), custom_call_target="tpu_custom_call" | custom-call | flops 983040 | bytes 1310720 | tf_op jit(solution)/shard_map/pallas_call | solution.py:36
  (40 shorter events, 1.5 us)
Async XLA Ops:
  0.0 4.5 %copy-start.6 = (f32[16384]{0:T(1024)S(1)}, f32[16384]{0:T(1024)}, u32[]{:S(2)}) copy-start(f32[16384]{0:T(1024)} %param.16) | copy-start | bytes 196612
  0.0 4.5 %copy-start.7 = (f32[16384]{0:T(1024)S(1)}, f32[16384]{0:T(1024)}, u32[]{:S(2)}) copy-start(f32[16384]{0:T(1024)} %param.17) | copy-start | bytes 196612
  2.5 17.9 %collective-permute-start.2 = (f32[5,72,512]{2,1,0:T(8,128)}, f32[5,72,512]{2,1,0:T(8,128)S(1)}, u32[]{:S(2)}, u32[]{:S(2)}) collective-permute-start(f32[5,72,512]{2,1,0:T(8,128)} %get-tuple-element.30.early.pressure), channel_id=1, source_target_pairs={{8,1},{9,0},{10,3},{11,2},{12,5},{13,4},{14,7},{15,6},{24,17},{25,... | collective-permute-start | bytes 2211848 | tf_op jit(solution)/shard_map/ppermute | solution.py:508
  5.1 9.3 %copy-start.3 = (f32[3,16384]{1,0:T(4,128)S(1)}, f32[3,16384]{1,0:T(4,128)}, u32[]{:S(2)}) copy-start(f32[3,16384]{1,0:T(4,128)} %vel.3) | copy-start | bytes 589828
  5.1 9.3 %copy-start.10 = (f32[3,16384]{1,0:T(4,128)S(1)}, f32[3,16384]{1,0:T(4,128)}, u32[]{:S(2)}) copy-start(f32[3,16384]{1,0:T(4,128)} %pos.1) | copy-start | bytes 589828
  5.1 9.3 %copy-start.11 = (s32[2,4096]{1,0:T(2,128)S(1)}, s32[2,4096]{1,0:T(2,128)}, u32[]{:S(2)}) copy-start(s32[2,4096]{1,0:T(2,128)} %lists.1) | copy-start | bytes 98308
  6.8 13.6 %collective-permute-start = (f32[136,256]{1,0:T(8,128)S(1)}, f32[136,256]{1,0:T(8,128)S(1)}, u32[]{:S(2)}, u32[]{:S(2)}) collective-permute-start(f32[136,256]{1,0:T(8,128)S(1)} %get-tuple-element.29.mine), channel_id=1, source_target_pairs={{0,8},{1,9},{2,10},{3,11},{4,12},{5,13},{6,14},{7,15},{8,16},{9,17... | collective-permute-start | bytes 417800 | tf_op jit(solution)/shard_map/ppermute | solution.py:508
  12.5 7.9 %collective-permute-start.1 = (f32[136,256]{1,0:T(8,128)S(1)}, f32[136,256]{1,0:T(8,128)S(1)}, u32[]{:S(2)}, u32[]{:S(2)}) collective-permute-start(f32[136,256]{1,0:T(8,128)S(1)} %get-tuple-element.29.mine), channel_id=1, source_target_pairs={{0,16},{1,17},{2,18},{3,19},{4,20},{5,21},{6,22},{7,23},{8,0},{9,1... | collective-permute-start | bytes 417800 | tf_op jit(solution)/shard_map/ppermute | solution.py:508
  14.5 4.6 %copy-start.9 = (f32[3,72,512]{2,1,0:T(8,128)S(1)}, f32[3,72,512]{2,1,0:T(8,128)}, u32[]{:S(2)}) copy-start(f32[3,72,512]{2,1,0:T(8,128)} %get-tuple-element.31.late) | copy-start | bytes 1327108
  14.5 6.0 %copy-start.4 = (f32[72,512]{1,0:T(8,128)S(1)}, f32[72,512]{1,0:T(8,128)}, u32[]{:S(2)}) copy-start(f32[72,512]{1,0:T(8,128)} %get-tuple-element.35.inner) | copy-start | bytes 442372
  17.7 1.3 %collective-permute-start.3 = (f32[96,128]{1,0:T(8,128)S(1)}, f32[96,128]{1,0:T(8,128)S(1)}, u32[]{:S(2)}, u32[]{:S(2)}) collective-permute-start(f32[96,128]{1,0:T(8,128)S(1)} %get-tuple-element.33.halo_near), channel_id=1, source_target_pairs={{8,9},{9,8},{10,11},{11,10},{12,13},{13,12},{14,15},{15,14}} | collective-permute-start | bytes 147464 | tf_op jit(solution)/shard_map/ppermute | solution.py:508
  18.4 2.0 %collective-permute-start.4 = (f32[96,128]{1,0:T(8,128)S(1)}, f32[96,128]{1,0:T(8,128)S(1)}, u32[]{:S(2)}, u32[]{:S(2)}) collective-permute-start(f32[96,128]{1,0:T(8,128)S(1)} %get-tuple-element.34.halo_far), channel_id=1, source_target_pairs={{9,10},{10,9},{11,12},{12,11},{13,14},{14,13}} | collective-permute-start | bytes 147464 | tf_op jit(solution)/shard_map/ppermute | solution.py:508
  19.1 15.0 %collective-permute-start.7 = (f32[3,72,512]{2,1,0:T(8,128)S(1)}, f32[3,72,512]{2,1,0:T(8,128)S(1)}, u32[]{:S(2)}, u32[]{:S(2)}) collective-permute-start(f32[3,72,512]{2,1,0:T(8,128)S(1)} %copy-done.9), channel_id=1, source_target_pairs={{8,1},{9,0},{10,3},{11,2},{12,5},{13,4},{14,7},{15,6},{24,17},{25,... | collective-permute-start | bytes 1327112 | tf_op jit(solution)/shard_map/ppermute | solution.py:508
  20.5 23.5 %copy-start = (f32[5,72,512]{2,1,0:T(8,128)S(1)}, f32[5,72,512]{2,1,0:T(8,128)}, u32[]{:S(2)}) copy-start(f32[5,72,512]{2,1,0:T(8,128)} %get-tuple-element.30.early.pressure) | copy-start | bytes 2211844
  20.5 31.8 %collective-permute-start.6 = (f32[6,72,512]{2,1,0:T(8,128)S(1)}, f32[6,72,512]{2,1,0:T(8,128)S(1)}, u32[]{:S(2)}, u32[]{:S(2)}) collective-permute-start(f32[6,72,512]{2,1,0:T(8,128)S(1)} %get-tuple-element.41), channel_id=1, source_target_pairs={{0,2},{2,4},{3,1},{4,6},{5,3},{7,5},{16,18},{18,20},{19,17},{20,22... | collective-permute-start | bytes 2654216 | tf_op jit(solution)/shard_map/ppermute | solution.py:508
  24.2 18.4 %copy-start.13 = (f32[72,512]{1,0:T(8,128)S(1)}, f32[72,512]{1,0:T(8,128)}, u32[]{:S(2)}) copy-start(f32[72,512]{1,0:T(8,128)} %get-tuple-element.45) | copy-start | bytes 442372
  24.3 24.8 %collective-permute-start.9 = (f32[456,256]{1,0:T(8,128)S(1)}, f32[456,256]{1,0:T(8,128)S(1)}, u32[]{:S(2)}, u32[]{:S(2)}) collective-permute-start(f32[456,256]{1,0:T(8,128)S(1)} %get-tuple-element.44), channel_id=1, source_target_pairs={{0,1},{1,0},{2,3},{3,2},{4,5},{5,4},{6,7},{7,6},{16,17},{17,16},{1... | collective-permute-start | bytes 1400840 | tf_op jit(solution)/shard_map/ppermute | solution.py:508
  26.2 26.1 %collective-permute-start.5 = (f32[456,256]{1,0:T(8,128)S(1)}, f32[456,256]{1,0:T(8,128)S(1)}, u32[]{:S(2)}, u32[]{:S(2)}) collective-permute-start(f32[456,256]{1,0:T(8,128)S(1)} %get-tuple-element.40), channel_id=1, source_target_pairs={{1,2},{2,1},{3,4},{4,3},{5,6},{6,5},{17,18},{18,17},{19,20},{20,19... | collective-permute-start | bytes 1400840 | tf_op jit(solution)/shard_map/ppermute | solution.py:508
  34.1 18.3 %collective-permute-start.8 = (f32[3,72,512]{2,1,0:T(8,128)S(1)}, f32[3,72,512]{2,1,0:T(8,128)S(1)}, u32[]{:S(2)}, u32[]{:S(2)}) collective-permute-start(f32[3,72,512]{2,1,0:T(8,128)S(1)} %collective-permute-done.7.near_late), channel_id=1, source_target_pairs={{0,2},{2,4},{3,1},{4,6},{5,3},{7,5},{16,18},{18,20},{19,17},{20,22... | collective-permute-start | bytes 1327112 | tf_op jit(solution)/shard_map/ppermute | solution.py:508
  42.6 6.5 %collective-permute-start.10 = (f32[72,512]{1,0:T(8,128)S(1)}, f32[72,512]{1,0:T(8,128)S(1)}, u32[]{:S(2)}, u32[]{:S(2)}) collective-permute-start(f32[72,512]{1,0:T(8,128)S(1)} %copy-done.13), channel_id=1, source_target_pairs={{9,3},{10,0},{11,5},{12,2},{13,7},{14,4},{25,19},{26,16},{27,21},{... | collective-permute-start | bytes 442376 | tf_op jit(solution)/shard_map/ppermute | solution.py:508
  52.4 8.4 %copy-start.1 = (s32[8,16384]{1,0:T(8,128)S(1)}, s32[8,16384]{1,0:T(8,128)}, u32[]{:S(2)}) copy-start(s32[8,16384]{1,0:T(8,128)} %named.1) | copy-start | bytes 1572868
  52.4 8.4 %copy-start.2 = (f32[8,16384]{1,0:T(8,128)S(1)}, f32[8,16384]{1,0:T(8,128)}, u32[]{:S(2)}) copy-start(f32[8,16384]{1,0:T(8,128)} %stiff.1) | copy-start | bytes 1572868
  57.5 8.1 %collective-permute-start.11 = (f32[128,384]{1,0:T(8,128)S(1)}, f32[128,384]{1,0:T(8,128)S(1)}, u32[]{:S(2)}, u32[]{:S(2)}) collective-permute-start(f32[128,384]{1,0:T(8,128)S(1)} %get-tuple-element.49), channel_id=1, source_target_pairs={{0,16},{1,17},{2,18},{3,19},{4,20},{5,21},{6,22},{7,23},{16,8},{17... | collective-permute-start | bytes 589832 | tf_op jit(solution)/shard_map/ppermute | solution.py:508
  58.8 7.6 %collective-permute-start.12 = (f32[128,384]{1,0:T(8,128)S(1)}, f32[128,384]{1,0:T(8,128)S(1)}, u32[]{:S(2)}, u32[]{:S(2)}) collective-permute-start(f32[128,384]{1,0:T(8,128)S(1)} %get-tuple-element.50), channel_id=1, source_target_pairs={{0,8},{1,9},{2,10},{3,11},{4,12},{5,13},{6,14},{7,15},{16,0},{17,1... | collective-permute-start | bytes 589832 | tf_op jit(solution)/shard_map/ppermute | solution.py:508
  (3 other events, 5.8 us)

commit v14 on v13

--- a/solution.py
+++ b/solution.py
@@ -108,7 +108,7 @@
         one.wait()
 
 
-def forward_kernel(near, inner, _halo, _second, _third, _near, _far, out, dummy):
+def forward_kernel(near, inner, _halo, _second, _third, _beyond, out, dummy):
     dummy[...] = jnp.zeros(dummy.shape, F32)
     count = near.shape[0]
     out[:count] = near[...]
@@ -322,7 +322,7 @@
 
 
 def own_kernel(
-    full, mine, second, third, early, late, _message, constant, factor, weight, picks
+    full, mine, second, third, early, late, _message, _near, _far, constant, factor, weight, picks
 ):
     tiles = weight.shape[0]
     planes, height, width = constant.shape
@@ -554,15 +554,15 @@
     halo = shaped(3 * rows, BLOCK)
     state, halo_near, halo_far, after_halo = call(
         halo_kernel, (shaped(3 * tiles, BLOCK), halo, halo, small),
-        [VMEM] * 4, (grain_pos, grain_vel, halo_list, after_deposit), flops=2 * 3 * 8 * BLOCK * BLOCK * slots // 4,
+        [VMEM] * 4, (grain_pos, grain_vel, halo_list, after_deposit), flops=slots,
         size=4 * 4 * 3 * slots,
     )
     others = [g for g in holders if g not in owners]
     came_near = along_reg(halo_near, others, (1, -1))
     came_far = along_reg(halo_far, others, (-1, 1))
     far, after_forward = call(
-        forward_kernel, (shaped(planes + HEAD + 1, height, width), small), [VMEM] * 7,
-        (near, inner, after_halo, second, third, came_near, came_far), size=5 * field_bytes,
+        forward_kernel, (shaped(planes + HEAD + 1, height, width), small), [VMEM] * 6,
+        (near, inner, after_halo, second, third, beyond), size=5 * field_bytes,
     )
     far = along_reg(far, owners, (2, -2))
     far_late = along_reg(near_late, owners, (2, -2))
@@ -579,7 +579,8 @@
             field, field, shaped(tiles, BLOCK),
             jax.ShapeDtypeStruct((3 * tiles, planes * height * width // BLOCK), BF16),
         ),
-        [VMEM] * 6, (mine, second, third, early, late, after_message),
+        [VMEM] * 8,
+        (mine, second, third, early, late, after_message, came_near, came_far),
         flops=planes * height * 4 * 384 * 256 * 6, size=9 * field_bytes,
     )
     window_of = lambda count: pltpu.VMEM((count, height, width), F32)

time: 67.8 us -> 59.1 us (0.87)
  the two profiles are of different devices: /device:TPU:0 before, /device:TPU:16 now
where the time goes in v14:
time: 59.1 us; the launch traced here: 58.7 us
  starting transfers between devices  28.6 us (48%)
  Pallas kernels  22.5 us (38%)
  waiting for transfers between devices  5.29 us (9%)
  local copies, waits for them, and re-layouts  1.3 us (2%)
  between operations  1.06 us (2%)
    ppermute x13, starting transfers between devices, send(): return lax.ppermute(value, ('grp', 'reg'), flat)  28.6 us
    pallas_call x10, Pallas kernels, call(): pl.pallas_call(kernel, out_shape=outs, in_specs=specs, out_specs=jax.tree...  22.5 us
    ppermute x13, waiting for transfers between devices, send(): return lax.ppermute(value, ('grp', 'reg'), flat)  5.29 us
    unnamed x26, local copies, waits for them, and re-layouts  1.3 us
  transfers between devices with their start and end apart: 13, of which 2 were waited for; matrix products, arithmetic and copies ran while one was open for 0% of the time, Pallas kernels for 24%

profile of v14, /device:TPU:16, one launch (start us, length us, event | category | flops | bytes accessed | tf_op | source)
XLA Modules:
  0.0 58.7 jit_solution(13863854038905359801)
XLA Ops:
  0.0 2.5 %shard_map.137 = (f32[5,72,512]{2,1,0:T(8,128)}, f32[3,72,512]{2,1,0:T(8,128)}, f32[72,512]{1,0:T(8,128)}, f32[72,512]{1,0:T(8,128)}) custom-call(f32[4,128,512]{2,1,0:T(8,128)} %pressure_old.1, f32[4,128,512]{2,1,0:T(8,128)} %source.1, f32[4,128,512]{2,1,0:T(8,128)} %solid_before.1), custom_call_target="tpu_custom_call" | custom-call | flops 589824 | bytes 3538944 | tf_op jit(solution)/shard_map/pallas_call | solution.py:36
  2.5 1.3 %collective-permute-start.2 = (f32[5,72,512]{2,1,0:T(8,128)}, f32[5,72,512]{2,1,0:T(8,128)S(1)}, u32[]{:S(2)}, u32[]{:S(2)}) collective-permute-start(f32[5,72,512]{2,1,0:T(8,128)} %get-tuple-element.30.early.pressure), channel_id=1, source_target_pairs={{8,1},{9,0},{10,3},{11,2},{12,5},{13,4},{14,7},{15,6},{24,17},{25,... | collective-permute-start | bytes 2211848 | tf_op jit(solution)/shard_map/ppermute | solution.py:508
  3.8 1.3 %collective-permute-start.3 = (f32[72,512]{1,0:T(8,128)}, f32[72,512]{1,0:T(8,128)S(1)}, u32[]{:S(2)}, u32[]{:S(2)}) collective-permute-start(f32[72,512]{1,0:T(8,128)} %get-tuple-element.37), channel_id=1, source_target_pairs={{9,3},{10,0},{11,5},{12,2},{13,7},{14,4},{25,19},{26,16},{27,21},{... | collective-permute-start | bytes 442376 | tf_op jit(solution)/shard_map/ppermute | solution.py:508
  6.5 1.7 %shard_map.136 = (f32[136,256]{1,0:T(8,128)S(1)}, f32[8,128]{1,0:T(8,128)S(1)}) custom-call(s32[1]{0:T(128)S(6)} %copy.15.count, s32[128,128]{1,0:T(8,128)S(1)} %bitcast.4, f32[128,128]{1,0:T(8,128)S(1)} %bitcast.6, f32[128,128]{1,0:T(8,128)S(1)} %bitcast.8, s32[1,128]{1,0:T(1,128)S(1)} %bitcast.10), custom_call_target="tpu_custom_call" | custom-call | flops 201326592 | bytes 327680 | tf_op jit(solution)/shard_map/pallas_call | solution.py:36
  8.2 4.2 %collective-permute-start = (f32[136,256]{1,0:T(8,128)S(1)}, f32[136,256]{1,0:T(8,128)S(1)}, u32[]{:S(2)}, u32[]{:S(2)}) collective-permute-start(f32[136,256]{1,0:T(8,128)S(1)} %get-tuple-element.29.mine), channel_id=1, source_target_pairs={{0,8},{1,9},{2,10},{3,11},{4,12},{5,13},{6,14},{7,15},{8,16},{9,17... | collective-permute-start | bytes 417800 | tf_op jit(solution)/shard_map/ppermute | solution.py:508
  12.4 1.9 %collective-permute-start.1 = (f32[136,256]{1,0:T(8,128)S(1)}, f32[136,256]{1,0:T(8,128)S(1)}, u32[]{:S(2)}, u32[]{:S(2)}) collective-permute-start(f32[136,256]{1,0:T(8,128)S(1)} %get-tuple-element.29.mine), channel_id=1, source_target_pairs={{0,16},{1,17},{2,18},{3,19},{4,20},{5,21},{6,22},{7,23},{8,0},{9,1... | collective-permute-start | bytes 417800 | tf_op jit(solution)/shard_map/ppermute | solution.py:508
  14.3 1.3 %collective-permute-start.8 = (f32[3,72,512]{2,1,0:T(8,128)}, f32[3,72,512]{2,1,0:T(8,128)S(1)}, u32[]{:S(2)}, u32[]{:S(2)}) collective-permute-start(f32[3,72,512]{2,1,0:T(8,128)} %get-tuple-element.31.late), channel_id=1, source_target_pairs={{8,1},{9,0},{10,3},{11,2},{12,5},{13,4},{14,7},{15,6},{24,17},{25,... | collective-permute-start | bytes 1327112 | tf_op jit(solution)/shard_map/ppermute | solution.py:508
  15.6 3.2 %shard_map.138 = (f32[384,128]{1,0:T(8,128)S(1)}, f32[96,128]{1,0:T(8,128)S(1)}, f32[96,128]{1,0:T(8,128)S(1)}, f32[8,128]{1,0:T(8,128)S(1)}) custom-call(f32[3,16384]{1,0:T(4,128)S(1)} %copy-done.4, f32[3,16384]{1,0:T(4,128)S(1)} %copy-done.1, s32[2,4096]{1,0:T(2,128)S(1)} %copy-done.9, f32[8,128]{1,0:T(8,128)S(1)} %get-tuple-element.32._), custom_call_target="tpu_custom_call" | custom-call | flops 16384 | bytes 786432 | tf_op jit(solution)/shard_map/pallas_call | solution.py:36
  19.0 3.6 %collective-permute-start.7 = (f32[6,72,512]{2,1,0:T(8,128)S(1)}, f32[6,72,512]{2,1,0:T(8,128)S(1)}, u32[]{:S(2)}, u32[]{:S(2)}) collective-permute-start(f32[6,72,512]{2,1,0:T(8,128)S(1)} %get-tuple-element.42), channel_id=1, source_target_pairs={{0,2},{2,4},{3,1},{4,6},{5,3},{7,5},{16,18},{18,20},{19,17},{20,22... | collective-permute-start | bytes 2654216 | tf_op jit(solution)/shard_map/ppermute | solution.py:508
  22.7 2.3 %collective-permute-start.10 = (f32[456,256]{1,0:T(8,128)S(1)}, f32[456,256]{1,0:T(8,128)S(1)}, u32[]{:S(2)}, u32[]{:S(2)}) collective-permute-start(f32[456,256]{1,0:T(8,128)S(1)} %get-tuple-element.45), channel_id=1, source_target_pairs={{0,1},{1,0},{2,3},{3,2},{4,5},{5,4},{6,7},{7,6},{16,17},{17,16},{1... | collective-permute-start | bytes 1400840 | tf_op jit(solution)/shard_map/ppermute | solution.py:508
  25.0 3.4 %collective-permute-start.6 = (f32[456,256]{1,0:T(8,128)S(1)}, f32[456,256]{1,0:T(8,128)S(1)}, u32[]{:S(2)}, u32[]{:S(2)}) collective-permute-start(f32[456,256]{1,0:T(8,128)S(1)} %get-tuple-element.41), channel_id=1, source_target_pairs={{1,2},{2,1},{3,4},{4,3},{5,6},{6,5},{17,18},{18,17},{19,20},{20,19... | collective-permute-start | bytes 1400840 | tf_op jit(solution)/shard_map/ppermute | solution.py:508
  28.5 3.5 %collective-permute-start.9 = (f32[3,72,512]{2,1,0:T(8,128)S(1)}, f32[3,72,512]{2,1,0:T(8,128)S(1)}, u32[]{:S(2)}, u32[]{:S(2)}) collective-permute-start(f32[3,72,512]{2,1,0:T(8,128)S(1)} %collective-permute-done.8.near_late), channel_id=1, source_target_pairs={{0,2},{2,4},{3,1},{4,6},{5,3},{7,5},{16,18},{18,20},{19,17},{20,22... | collective-permute-start | bytes 1327112 | tf_op jit(solution)/shard_map/ppermute | solution.py:508
  32.0 0.7 %collective-permute-start.4 = (f32[96,128]{1,0:T(8,128)S(1)}, f32[96,128]{1,0:T(8,128)S(1)}, u32[]{:S(2)}, u32[]{:S(2)}) collective-permute-start(f32[96,128]{1,0:T(8,128)S(1)} %get-tuple-element.33.halo_near), channel_id=1, source_target_pairs={{8,9},{9,8},{10,11},{11,10},{12,13},{13,12},{14,15},{15,14}} | collective-permute-start | bytes 147464 | tf_op jit(solution)/shard_map/ppermute | solution.py:508
  32.6 0.7 %collective-permute-start.5 = (f32[96,128]{1,0:T(8,128)S(1)}, f32[96,128]{1,0:T(8,128)S(1)}, u32[]{:S(2)}, u32[]{:S(2)}) collective-permute-start(f32[96,128]{1,0:T(8,128)S(1)} %get-tuple-element.34.halo_far), channel_id=1, source_target_pairs={{9,10},{10,9},{11,12},{12,11},{13,14},{14,13}} | collective-permute-start | bytes 147464 | tf_op jit(solution)/shard_map/ppermute | solution.py:508
  33.3 1.4 %shard_map.141 = (f32[4,72,512]{2,1,0:T(8,128)S(1)}, f32[4,72,512]{2,1,0:T(8,128)S(1)}, f32[128,128]{1,0:T(8,128)S(1)}, bf16[384,1152]{1,0:T(8,128)(2,1)S(1)}) custom-call(f32[136,256]{1,0:T(8,128)S(1)} %get-tuple-element.29.mine, f32[136,256]{1,0:T(8,128)S(1)} %collective-permute-done._second.second, f32[136,256]{1,0:T(8,128)S(1)} %collective-permute-done.1._third.third, ...), custom_call_target="tpu_custom_call" | custom-call | flops 679477248 | bytes 5308416 | tf_op jit(solution)/shard_map/pallas_call | solution.py:36
  34.7 4.5 %collective-permute-done.10.message.message_near = f32[456,256]{1,0:T(8,128)S(1)} collective-permute-done((f32[456,256]{1,0:T(8,128)S(1)}, f32[456,256]{1,0:T(8,128)S(1)}, u32[]{:S(2)}, u32[]{:S(2)}) %collective-permute-start.10) | collective-permute-done | bytes 466976 | tf_op jit(solution)/shard_map/ppermute | solution.py:508
  39.2 3.2 %shard_map.142 = (f32[4,72,512]{2,1,0:T(8,128)S(1)}, f32[4,72,512]{2,1,0:T(8,128)S(1)}) custom-call(f32[456,256]{1,0:T(8,128)S(1)} %collective-permute-done.10.message.message_near, f32[5,72,512]{2,1,0:T(8,128)S(1)} %copy-done, f32[5,72,512]{2,1,0:T(8,128)S(1)} %collective-permute-done.2.near, f32[3,72,512]{2,1,0:T(8,128)S(1)} %collective-permute-done.8.near_late, ...), custom_call_target="tpu_custom_call" | custom-call | flops 679477248 | bytes 5308416 | tf_op jit(solution)/shard_map/pallas_call | solution.py:36
  42.5 5.1 %shard_map.143 = (f32[128,384]{1,0:T(8,128)S(1)}, f32[128,384]{1,0:T(8,128)S(1)}, f32[128,384]{1,0:T(8,128)S(1)}) custom-call(bf16[384,1152]{1,0:T(8,128)(2,1)S(1)} %get-tuple-element.40.picks, f32[456,256]{1,0:T(8,128)S(1)} %collective-permute-done.6.message.message_far, f32[5,72,512]{2,1,0:T(8,128)S(1)} %copy-done, ...), custom_call_target="tpu_custom_call" | custom-call | flops 679477248 | bytes 5308416 | tf_op jit(solution)/shard_map/pallas_call | solution.py:36
  47.6 2.5 %collective-permute-start.11 = (f32[128,384]{1,0:T(8,128)S(1)}, f32[128,384]{1,0:T(8,128)S(1)}, u32[]{:S(2)}, u32[]{:S(2)}) collective-permute-start(f32[128,384]{1,0:T(8,128)S(1)} %get-tuple-element.49), channel_id=1, source_target_pairs={{0,16},{1,17},{2,18},{3,19},{4,20},{5,21},{6,22},{7,23},{16,8},{17... | collective-permute-start | bytes 589832 | tf_op jit(solution)/shard_map/ppermute | solution.py:508
  50.1 1.9 %collective-permute-start.12 = (f32[128,384]{1,0:T(8,128)S(1)}, f32[128,384]{1,0:T(8,128)S(1)}, u32[]{:S(2)}, u32[]{:S(2)}) collective-permute-start(f32[128,384]{1,0:T(8,128)S(1)} %get-tuple-element.50), channel_id=1, source_target_pairs={{0,8},{1,9},{2,10},{3,11},{4,12},{5,13},{6,14},{7,15},{16,0},{17,1... | collective-permute-start | bytes 589832 | tf_op jit(solution)/shard_map/ppermute | solution.py:508
  52.1 0.6 %copy-done.10 = s32[128]{0:T(128)S(1)} copy-done((s32[128]{0:T(128)S(1)}, s32[128]{0:T(128)}, u32[]{:S(2)}) %copy-start.10) | copy-done | bytes 536
  52.7 4.2 %shard_map.144.contact = f32[384,128]{1,0:T(8,128)S(1)} custom-call(s32[128]{0:T(128)S(1)} %copy-done.10, f32[384,128]{1,0:T(8,128)S(1)} %get-tuple-element.52.state, f32[456,256]{1,0:T(8,128)S(1)} %collective-permute-done.10.message.message_near, f32[456,256]{1,0:T(8,128)S(1)} %collective-permute-done.6.message.message_far, ...), custom_call_target="tpu_custom_call" | custom-call | flops 7864320 | bytes 1310720 | tf_op jit(solution)/shard_map/pallas_call | solution.py:36
  56.9 0.8 %collective-permute-done.12.grads_c = f32[128,384]{1,0:T(8,128)S(1)} collective-permute-done((f32[128,384]{1,0:T(8,128)S(1)}, f32[128,384]{1,0:T(8,128)S(1)}, u32[]{:S(2)}, u32[]{:S(2)}) %collective-permute-start.12) | collective-permute-done | bytes 196640 | tf_op jit(solution)/shard_map/ppermute | solution.py:508
  57.7 1.0 %shard_map.145 = f32[3,16384]{1,0:T(4,128)} custom-call(s32[1]{0:T(128)S(6)} %copy.15.count, f32[128,384]{1,0:T(8,128)S(1)} %get-tuple-element.48._.grads_a, f32[128,384]{1,0:T(8,128)S(1)} %collective-permute-done.11.grads_b, f32[128,384]{1,0:T(8,128)S(1)} %collective-permute-done.12.grads_c, f32[128,128]{1,0:T(8,128)S(1)} %get-tuple-element.51.weight, ...), custom_call_target="tpu_custom_call" | custom-call | flops 983040 | bytes 1310720 | tf_op jit(solution)/shard_map/pallas_call | solution.py:36
  (38 shorter events, 0.8 us)
Async XLA Ops:
  0.0 5.8 %copy-start.6 = (s32[16384]{0:T(1024)S(1)}, s32[16384]{0:T(1024)}, u32[]{:S(2)}) copy-start(s32[16384]{0:T(1024)} %param.23) | copy-start | bytes 196612
  0.0 5.8 %copy-start.7 = (f32[16384]{0:T(1024)S(1)}, f32[16384]{0:T(1024)}, u32[]{:S(2)}) copy-start(f32[16384]{0:T(1024)} %param.16) | copy-start | bytes 196612
  0.0 5.8 %copy-start.8 = (f32[16384]{0:T(1024)S(1)}, f32[16384]{0:T(1024)}, u32[]{:S(2)}) copy-start(f32[16384]{0:T(1024)} %param.17) | copy-start | bytes 196612
  2.5 16.4 %collective-permute-start.2 = (f32[5,72,512]{2,1,0:T(8,128)}, f32[5,72,512]{2,1,0:T(8,128)S(1)}, u32[]{:S(2)}, u32[]{:S(2)}) collective-permute-start(f32[5,72,512]{2,1,0:T(8,128)} %get-tuple-element.30.early.pressure), channel_id=1, source_target_pairs={{8,1},{9,0},{10,3},{11,2},{12,5},{13,4},{14,7},{15,6},{24,17},{25,... | collective-permute-start | bytes 2211848 | tf_op jit(solution)/shard_map/ppermute | solution.py:508
  3.8 15.1 %collective-permute-start.3 = (f32[72,512]{1,0:T(8,128)}, f32[72,512]{1,0:T(8,128)S(1)}, u32[]{:S(2)}, u32[]{:S(2)}) collective-permute-start(f32[72,512]{1,0:T(8,128)} %get-tuple-element.37), channel_id=1, source_target_pairs={{9,3},{10,0},{11,5},{12,2},{13,7},{14,4},{25,19},{26,16},{27,21},{... | collective-permute-start | bytes 442376 | tf_op jit(solution)/shard_map/ppermute | solution.py:508
  6.5 9.2 %copy-start.1 = (f32[3,16384]{1,0:T(4,128)S(1)}, f32[3,16384]{1,0:T(4,128)}, u32[]{:S(2)}) copy-start(f32[3,16384]{1,0:T(4,128)} %vel.3) | copy-start | bytes 589828
  6.5 9.2 %copy-start.4 = (f32[3,16384]{1,0:T(4,128)S(1)}, f32[3,16384]{1,0:T(4,128)}, u32[]{:S(2)}) copy-start(f32[3,16384]{1,0:T(4,128)} %pos.1) | copy-start | bytes 589828
  6.5 9.2 %copy-start.9 = (s32[2,4096]{1,0:T(2,128)S(1)}, s32[2,4096]{1,0:T(2,128)}, u32[]{:S(2)}) copy-start(s32[2,4096]{1,0:T(2,128)} %lists.1) | copy-start | bytes 98308
  8.2 10.7 %collective-permute-start = (f32[136,256]{1,0:T(8,128)S(1)}, f32[136,256]{1,0:T(8,128)S(1)}, u32[]{:S(2)}, u32[]{:S(2)}) collective-permute-start(f32[136,256]{1,0:T(8,128)S(1)} %get-tuple-element.29.mine), channel_id=1, source_target_pairs={{0,8},{1,9},{2,10},{3,11},{4,12},{5,13},{6,14},{7,15},{8,16},{9,17... | collective-permute-start | bytes 417800 | tf_op jit(solution)/shard_map/ppermute | solution.py:508
  12.4 6.5 %collective-permute-start.1 = (f32[136,256]{1,0:T(8,128)S(1)}, f32[136,256]{1,0:T(8,128)S(1)}, u32[]{:S(2)}, u32[]{:S(2)}) collective-permute-start(f32[136,256]{1,0:T(8,128)S(1)} %get-tuple-element.29.mine), channel_id=1, source_target_pairs={{0,16},{1,17},{2,18},{3,19},{4,20},{5,21},{6,22},{7,23},{8,0},{9,1... | collective-permute-start | bytes 417800 | tf_op jit(solution)/shard_map/ppermute | solution.py:508
  14.3 14.2 %collective-permute-start.8 = (f32[3,72,512]{2,1,0:T(8,128)}, f32[3,72,512]{2,1,0:T(8,128)S(1)}, u32[]{:S(2)}, u32[]{:S(2)}) collective-permute-start(f32[3,72,512]{2,1,0:T(8,128)} %get-tuple-element.31.late), channel_id=1, source_target_pairs={{8,1},{9,0},{10,3},{11,2},{12,5},{13,4},{14,7},{15,6},{24,17},{25,... | collective-permute-start | bytes 1327112 | tf_op jit(solution)/shard_map/ppermute | solution.py:508
  15.6 3.3 %copy-start.5 = (f32[72,512]{1,0:T(8,128)S(1)}, f32[72,512]{1,0:T(8,128)}, u32[]{:S(2)}) copy-start(f32[72,512]{1,0:T(8,128)} %get-tuple-element.35.inner) | copy-start | bytes 442372
  18.9 14.4 %copy-start = (f32[5,72,512]{2,1,0:T(8,128)S(1)}, f32[5,72,512]{2,1,0:T(8,128)}, u32[]{:S(2)}) copy-start(f32[5,72,512]{2,1,0:T(8,128)} %get-tuple-element.30.early.pressure) | copy-start | bytes 2211844
  19.0 14.3 %copy-start.11 = (f32[3,72,512]{2,1,0:T(8,128)S(1)}, f32[3,72,512]{2,1,0:T(8,128)}, u32[]{:S(2)}) copy-start(f32[3,72,512]{2,1,0:T(8,128)} %get-tuple-element.31.late) | copy-start | bytes 1327108
  19.0 23.5 %collective-permute-start.7 = (f32[6,72,512]{2,1,0:T(8,128)S(1)}, f32[6,72,512]{2,1,0:T(8,128)S(1)}, u32[]{:S(2)}, u32[]{:S(2)}) collective-permute-start(f32[6,72,512]{2,1,0:T(8,128)S(1)} %get-tuple-element.42), channel_id=1, source_target_pairs={{0,2},{2,4},{3,1},{4,6},{5,3},{7,5},{16,18},{18,20},{19,17},{20,22... | collective-permute-start | bytes 2654216 | tf_op jit(solution)/shard_map/ppermute | solution.py:508
  22.7 16.5 %collective-permute-start.10 = (f32[456,256]{1,0:T(8,128)S(1)}, f32[456,256]{1,0:T(8,128)S(1)}, u32[]{:S(2)}, u32[]{:S(2)}) collective-permute-start(f32[456,256]{1,0:T(8,128)S(1)} %get-tuple-element.45), channel_id=1, source_target_pairs={{0,1},{1,0},{2,3},{3,2},{4,5},{5,4},{6,7},{7,6},{16,17},{17,16},{1... | collective-permute-start | bytes 1400840 | tf_op jit(solution)/shard_map/ppermute | solution.py:508
  25.0 17.5 %collective-permute-start.6 = (f32[456,256]{1,0:T(8,128)S(1)}, f32[456,256]{1,0:T(8,128)S(1)}, u32[]{:S(2)}, u32[]{:S(2)}) collective-permute-start(f32[456,256]{1,0:T(8,128)S(1)} %get-tuple-element.41), channel_id=1, source_target_pairs={{1,2},{2,1},{3,4},{4,3},{5,6},{6,5},{17,18},{18,17},{19,20},{20,19... | collective-permute-start | bytes 1400840 | tf_op jit(solution)/shard_map/ppermute | solution.py:508
  28.5 14.0 %collective-permute-start.9 = (f32[3,72,512]{2,1,0:T(8,128)S(1)}, f32[3,72,512]{2,1,0:T(8,128)S(1)}, u32[]{:S(2)}, u32[]{:S(2)}) collective-permute-start(f32[3,72,512]{2,1,0:T(8,128)S(1)} %collective-permute-done.8.near_late), channel_id=1, source_target_pairs={{0,2},{2,4},{3,1},{4,6},{5,3},{7,5},{16,18},{18,20},{19,17},{20,22... | collective-permute-start | bytes 1327112 | tf_op jit(solution)/shard_map/ppermute | solution.py:508
  32.0 0.7 %collective-permute-start.4 = (f32[96,128]{1,0:T(8,128)S(1)}, f32[96,128]{1,0:T(8,128)S(1)}, u32[]{:S(2)}, u32[]{:S(2)}) collective-permute-start(f32[96,128]{1,0:T(8,128)S(1)} %get-tuple-element.33.halo_near), channel_id=1, source_target_pairs={{8,9},{9,8},{10,11},{11,10},{12,13},{13,12},{14,15},{15,14}} | collective-permute-start | bytes 147464 | tf_op jit(solution)/shard_map/ppermute | solution.py:508
  32.6 0.7 %collective-permute-start.5 = (f32[96,128]{1,0:T(8,128)S(1)}, f32[96,128]{1,0:T(8,128)S(1)}, u32[]{:S(2)}, u32[]{:S(2)}) collective-permute-start(f32[96,128]{1,0:T(8,128)S(1)} %get-tuple-element.34.halo_far), channel_id=1, source_target_pairs={{9,10},{10,9},{11,12},{12,11},{13,14},{14,13}} | collective-permute-start | bytes 147464 | tf_op jit(solution)/shard_map/ppermute | solution.py:508
  42.5 9.6 %copy-start.2 = (s32[8,16384]{1,0:T(8,128)S(1)}, s32[8,16384]{1,0:T(8,128)}, u32[]{:S(2)}) copy-start(s32[8,16384]{1,0:T(8,128)} %named.1) | copy-start | bytes 1572868
  42.5 9.6 %copy-start.3 = (f32[8,16384]{1,0:T(8,128)S(1)}, f32[8,16384]{1,0:T(8,128)}, u32[]{:S(2)}) copy-start(f32[8,16384]{1,0:T(8,128)} %stiff.1) | copy-start | bytes 1572868
  47.6 9.3 %collective-permute-start.11 = (f32[128,384]{1,0:T(8,128)S(1)}, f32[128,384]{1,0:T(8,128)S(1)}, u32[]{:S(2)}, u32[]{:S(2)}) collective-permute-start(f32[128,384]{1,0:T(8,128)S(1)} %get-tuple-element.49), channel_id=1, source_target_pairs={{0,16},{1,17},{2,18},{3,19},{4,20},{5,21},{6,22},{7,23},{16,8},{17... | collective-permute-start | bytes 589832 | tf_op jit(solution)/shard_map/ppermute | solution.py:508
  50.1 7.6 %collective-permute-start.12 = (f32[128,384]{1,0:T(8,128)S(1)}, f32[128,384]{1,0:T(8,128)S(1)}, u32[]{:S(2)}, u32[]{:S(2)}) collective-permute-start(f32[128,384]{1,0:T(8,128)S(1)} %get-tuple-element.50), channel_id=1, source_target_pairs={{0,8},{1,9},{2,10},{3,11},{4,12},{5,13},{6,14},{7,15},{16,0},{17,1... | collective-permute-start | bytes 589832 | tf_op jit(solution)/shard_map/ppermute | solution.py:508
  (2 other events, 1.3 us)

commit v15 on v14

--- a/solution.py
+++ b/solution.py
@@ -68,7 +68,8 @@
 
 
 def window_kernel(
-    pressure_old, source, solid_before, early, late, ends, inner, pressure, driven, solid, sems
+    pressure_old, source, solid_before, ids, count, early, late, ends, inner, marks,
+    pressure, driven, solid, held, counted, sems,
 ):
     planes, height, _ = solid.shape
     place = Place(pressure_old.shape[1], height)
@@ -90,9 +91,17 @@
         copy(pressure.at[place.parity * (planes - 1)], ends),
         copy(pressure.at[(1 - place.parity) * (planes - 1)], inner),
     )
+    given = (copy(ids, held.at[:1]), copy(count, counted))
+    passed = copy(held, marks)
+    for one in given:
+        one.start()
     for x in range(planes):
         for part in fetched:
             part[x].start()
+    for one in given:
+        one.wait()
+    held[1:2] = jnp.broadcast_to(counted[0], (1, BLOCK))
+    passed.start()
     for x in range(planes):
         fetched[0][x].wait()
         stored[x].start()
@@ -106,6 +115,7 @@
         one.wait()
     for one in sides:
         one.wait()
+    passed.wait()
 
 
 def forward_kernel(near, inner, _halo, _second, _third, _beyond, out, dummy):
@@ -115,7 +125,7 @@
     out[count] = inner[...]
 
 
-def deposit_kernel(count, cell, vol, drag, ids, out, dummy):
+def deposit_kernel(marks, cell, vol, drag, out, dummy):
     dummy[...] = jnp.zeros(dummy.shape, F32)
     tiles = cell.shape[0]
     sub = iota((SUB, BLOCK), 0)
@@ -126,7 +136,7 @@
     def step(group, carry):
         first = pl.multiple_of(group * SUB, SUB)
         slot = (first + sub) * BLOCK + iota((SUB, BLOCK), 1)
-        live = slot < count[0]
+        live = slot < jnp.broadcast_to(marks[1:2, :], slot.shape)
         cells = cell[pl.ds(first, SUB), :]
         parts = halves_of(jnp.where(live, vol[pl.ds(first, SUB), :], 0.0)) + halves_of(
             jnp.where(live, drag[pl.ds(first, SUB), :], 0.0)
@@ -159,7 +169,7 @@
         return carry
 
     lax.fori_loop(0, tiles // SUB, step, 0, unroll=4)
-    out[tiles : tiles + SUB, :BLOCK] = jnp.broadcast_to(ids[...].astype(F32), (SUB, BLOCK))
+    out[tiles : tiles + SUB, :BLOCK] = jnp.broadcast_to(marks[:1, :].astype(F32), (SUB, BLOCK))
     out[tiles : tiles + SUB, BLOCK:] = jnp.zeros((SUB, BLOCK), F32)
 
 
@@ -219,7 +229,8 @@
 
 
 def contact_kernel(
-    partner, state, message_near, message_far, halo_near, halo_far, named, stiff, _, out, extended
+    partner, state, message_near, message_far, halo_near, halo_far, named, stiff, vel, vol, drag,
+    cell, weight, _, out, scale, extended
 ):
     tiles = state.shape[0] // 3
     rows = halo_near.shape[0] // 3
@@ -256,6 +267,15 @@
         return carry
 
     lax.fori_loop(0, tiles, step, 0, unroll=4)
+    volume = vol[...]
+    push = TIME_STEP / volume
+    scale[...] = push * (volume + drag[...] * lanes_of(weight[...], cell[...]))
+    for axis in range(3):
+        own = jnp.concatenate(
+            [vel[axis : axis + 1, t * BLOCK : (t + 1) * BLOCK] for t in range(tiles)], 0
+        )
+        rows = slice(axis * tiles, (axis + 1) * tiles)
+        out[rows, :] = own + push * (out[rows, :] - drag[...] * own)
 
 
 def shifted(plane):
@@ -398,7 +418,7 @@
 
 def far_kernel(
     full, tiles, picks, message, pressure, far, far_late, own_constant, own_factor, kept_even, kept_odd,
-    out_a, out_b, out_c, constant, factor, old, new, fields,
+    out_b, out_c, pieces, constant, factor, old, new, fields,
 ):
     planes, height, width = own_constant.shape
     zones = width // BLOCK
@@ -444,33 +464,31 @@
         return carry
 
     lax.fori_loop(0, planes, gradient, 0, unroll=4)
-    pieces = jnp.concatenate(halves_of(fields[...]), 1)
-    total = jnp.dot(picks[...], pieces, preferred_element_type=F32)
-    total = total[:, : 3 * BLOCK] + total[:, 3 * BLOCK :]
-    for index, out in enumerate((out_a, out_b, out_c)):
-        out[...] = total[index * tiles : (index + 1) * tiles]
-
-
-def final_kernel(
-    count, grads_a, grads_b, grads_c, weight, contact, vel, vol, drag, cell, out,
-):
+    pieces[...] = jnp.concatenate(halves_of(fields[...]), 1)
+    total = picked_rows(picks[tiles:, :], pieces)
+    out_b[...] = total[:tiles]
+    out_c[...] = total[tiles:]
+
+
+def picked_rows(hot, pieces):
+    total = jnp.dot(hot, pieces[...], preferred_element_type=F32)
+    return total[:, : 3 * BLOCK] + total[:, 3 * BLOCK :]
+
+
+def pick_kernel(picks, pieces, out):
+    out[...] = picked_rows(picks[: out.shape[0], :], pieces)
+
+
+def final_kernel(marks, grads_a, grads_b, grads_c, base, scale, cell, out):
     tiles = cell.shape[0]
     cells = cell[...]
-    heft = lanes_of(weight[...], cells)
     slot = iota(cells.shape, 0) * BLOCK + iota(cells.shape, 1)
-    live = slot < count[0]
-    volume = vol[...]
-    push = TIME_STEP / volume
+    live = slot < jnp.broadcast_to(marks[1:2, :], slot.shape)
     for axis in range(3):
         lanes = slice(axis * BLOCK, (axis + 1) * BLOCK)
         gradient = lanes_of(grads_a[:, lanes] + grads_b[:, lanes] + grads_c[:, lanes], cells)
-        own = jnp.concatenate(
-            [vel[axis : axis + 1, t * BLOCK : (t + 1) * BLOCK] for t in range(tiles)], 0
-        )
-        fluid = -gradient * heft
-        force = contact[axis * tiles : (axis + 1) * tiles, :] - volume * gradient
-        force = force + drag[...] * (fluid - own)
-        new = jnp.where(live, own + force * push, 0.0)
+        new = base[axis * tiles : (axis + 1) * tiles, :] - gradient * scale[...]
+        new = jnp.where(live, new, 0.0)
         for t in range(tiles):
             out[axis : axis + 1, t * BLOCK : (t + 1) * BLOCK] = new[t : t + 1, :]
 
@@ -520,7 +538,6 @@
         pairs = [((g, r), ((g + step) % holding, r)) for g in members for r in range(regions)]
         return send(value, pairs)
 
-    count = grain_count
     cell = grain_cell.reshape(tiles, BLOCK)
     vol = grain_vol.reshape(tiles, BLOCK)
     drag = drag_coef.reshape(tiles, BLOCK)
@@ -530,23 +547,25 @@
     field = shaped(planes, height, width)
     plane = shaped(height, width)
     small = shaped(SUB, BLOCK)
-    early, late, ends, inner = call(
+    early, late, ends, inner, marks = call(
         window_kernel,
         (
             shaped(planes + HEAD, height, width), shaped(planes - HEAD, height, width), plane,
-            plane,
+            plane, jax.ShapeDtypeStruct((2, BLOCK), jnp.int32),
         ),
-        [HBM] * 3, (pressure_old, pressure_source, solid_old),
+        [HBM] * 5, (pressure_old, pressure_source, solid_old, ids, grain_count),
         [pltpu.VMEM((planes, height, width), F32)] * 3
-        + [pltpu.SemaphoreType.DMA((5 * planes + 2,))],
+        + [
+            pltpu.VMEM((2, BLOCK), jnp.int32), pltpu.SMEM((1,), jnp.int32),
+            pltpu.SemaphoreType.DMA((5 * planes + 5,)),
+        ],
         flops=field_bytes, size=6 * field_bytes, limit=61_950_000, place=HBM,
     )
     near = along_reg(early, owners, (1, -1), core=1)
     near_late = along_reg(late, owners, (1, -1), core=1)
     beyond = along_reg(ends, owners, (-2, 2), core=1)
     mine, after_deposit = call(
-        deposit_kernel, (shaped(tiles + SUB, 2 * BLOCK), small), [SMEM] + [VMEM] * 4,
-        (count, cell, vol, drag, ids), flops=2 * 32 * 48 * 65536, size=5 * 4 * slots,
+        deposit_kernel, (shaped(tiles + SUB, 2 * BLOCK), small), [VMEM] * 4, (marks, cell, vol, drag), flops=2 * 32 * 48 * 65536, size=5 * 4 * slots,
     )
     second = along_grp(mine, 1, holders)
     third = along_grp(mine, 2, holders)
@@ -591,8 +610,10 @@
         flops=planes * height * 4 * 384 * 256 * 6, size=9 * field_bytes,
     )
     grads = shaped(tiles, 3 * BLOCK)
-    grads_a, grads_b, grads_c = call(
-        functools.partial(far_kernel, full, tiles), (grads,) * 3, [VMEM] * 9,
+    cells_held = planes * height * width // BLOCK
+    grads_b, grads_c, pieces = call(
+        functools.partial(far_kernel, full, tiles),
+        (grads, grads, jax.ShapeDtypeStruct((cells_held, 6 * BLOCK), BF16)), [VMEM] * 9,
         (picks, message_far, early, far, far_late, constant, factor, kept_even, kept_odd),
         [window_of(planes)] * 2
         + [window_of(3 * planes + 2)] * 2
@@ -601,19 +622,21 @@
     )
     grads_b = along_grp(grads_b, -1, owners)
     grads_c = along_grp(grads_c, -2, owners)
-
-    contact = call(
-        contact_kernel, shaped(3 * tiles, BLOCK), [SMEM] + [VMEM] * 7 + [ANY],
+    grads_a = call(pick_kernel, grads, [VMEM] * 2, (picks, pieces), flops=slots, size=slots)
+
+    base, scale = call(
+        contact_kernel, (shaped(3 * tiles, BLOCK), shaped(tiles, BLOCK)),
+        [SMEM] + [VMEM] * 12 + [ANY],
         (
             partner_block, state, message_near, message_far, came_near, came_far, contact_rows,
-            contact_stiff, grads_a,
+            contact_stiff, grain_vel, vol, drag, cell, weight, grads_a,
         ),
         [pltpu.VMEM((3 * (tiles + 2 * rows), BLOCK), F32)],
         flops=60 * 8 * slots, size=4 * 20 * slots,
     )
     return call(
-        final_kernel, shaped(3, slots), [SMEM] + [VMEM] * 9,
-        (count, grads_a, grads_b, grads_c, weight, contact, grain_vel, vol, drag, cell),
+        final_kernel, shaped(3, slots), [VMEM] * 7,
+        (marks, grads_a, grads_b, grads_c, base, scale, cell),
         flops=60 * slots, size=4 * 20 * slots,
     )
 

time: 59.1 us -> 60.2 us (1.019)
    pallas_call x10 -> x11, Pallas kernels: 22.5 us -> 23 us  [call(): pl.pallas_call(kernel, out_shape=outs, in_specs=specs, out_specs=jax.tree...]
    unnamed x26 -> x28, local copies, waits for them, and re-layouts: 1.3 us -> 1.63 us
  transfers between devices with their start and end apart: 13 -> 13, of which waited for: 2 -> 3; matrix products, arithmetic and copies ran while one was open for 0% -> 0% of each run, Pallas kernels for 24% -> 24%
where the time goes in v15:
time: 60.2 us; the launch traced here: 59.8 us
  starting transfers between devices  28.7 us (48%)
  Pallas kernels  23 us (38%)
  waiting for transfers between devices  5.37 us (9%)
  local copies, waits for them, and re-layouts  1.63 us (3%)
  between operations  1.1 us (2%)
    ppermute x13, starting transfers between devices, send(): return lax.ppermute(value, ('grp', 'reg'), flat)  28.7 us
    pallas_call x11, Pallas kernels, call(): pl.pallas_call(kernel, out_shape=outs, in_specs=specs, out_specs=jax.tree...  23 us
    ppermute x13, waiting for transfers between devices, send(): return lax.ppermute(value, ('grp', 'reg'), flat)  5.37 us
    unnamed x28, local copies, waits for them, and re-layouts  1.63 us
  transfers between devices with their start and end apart: 13, of which 3 were waited for; matrix products, arithmetic and copies ran while one was open for 0% of the time, Pallas kernels for 24%

profile of v15, /device:TPU:16, one launch (start us, length us, event | category | flops | bytes accessed | tf_op | source)
XLA Modules:
  0.0 59.8 jit_solution(7071845666471785234)
XLA Ops:
  0.7 2.6 %shard_map.136 = (f32[5,72,512]{2,1,0:T(8,128)}, f32[3,72,512]{2,1,0:T(8,128)}, f32[72,512]{1,0:T(8,128)}, f32[72,512]{1,0:T(8,128)}, s32[2,128]{1,0:T(2,128)}) custom-call(f32[4,128,512]{2,1,0:T(8,128)} %pressure_old.1, f32[4,128,512]{2,1,0:T(8,128)} %source.1, f32[4,128,512]{2,1,0:T(8,128)} %solid_before.1, s32[1,128]{1,0:T(1,128)} %bitcast.11, ...), custom_call_target="tpu_custom_call" | custom-call | flops 589824 | bytes 3538944 | tf_op jit(solution)/shard_map/pallas_call | solution.py:36
  3.3 1.4 %collective-permute-start.2 = (f32[5,72,512]{2,1,0:T(8,128)}, f32[5,72,512]{2,1,0:T(8,128)S(1)}, u32[]{:S(2)}, u32[]{:S(2)}) collective-permute-start(f32[5,72,512]{2,1,0:T(8,128)} %get-tuple-element.34.early.pressure), channel_id=1, source_target_pairs={{8,1},{9,0},{10,3},{11,2},{12,5},{13,4},{14,7},{15,6},{24,17},{25,... | collective-permute-start | bytes 2211848 | tf_op jit(solution)/shard_map/ppermute | solution.py:526
  4.7 1.3 %collective-permute-start.3 = (f32[72,512]{1,0:T(8,128)}, f32[72,512]{1,0:T(8,128)S(1)}, u32[]{:S(2)}, u32[]{:S(2)}) collective-permute-start(f32[72,512]{1,0:T(8,128)} %get-tuple-element.41), channel_id=1, source_target_pairs={{9,3},{10,0},{11,5},{12,2},{13,7},{14,4},{25,19},{26,16},{27,21},{... | collective-permute-start | bytes 442376 | tf_op jit(solution)/shard_map/ppermute | solution.py:526
  6.1 0.7 %copy-done.10 = s32[2,128]{1,0:T(2,128)S(1)} copy-done((s32[2,128]{1,0:T(2,128)S(1)}, s32[2,128]{1,0:T(2,128)}, u32[]{:S(2)}) %copy-start.10) | copy-done | bytes 1048
  6.8 1.7 %shard_map.137 = (f32[136,256]{1,0:T(8,128)S(1)}, f32[8,128]{1,0:T(8,128)S(1)}) custom-call(s32[2,128]{1,0:T(2,128)S(1)} %copy-done.10, s32[128,128]{1,0:T(8,128)S(1)} %bitcast.4, f32[128,128]{1,0:T(8,128)S(1)} %bitcast.7, f32[128,128]{1,0:T(8,128)S(1)} %bitcast.9), custom_call_target="tpu_custom_call" | custom-call | flops 201326592 | bytes 327680 | tf_op jit(solution)/shard_map/pallas_call | solution.py:36
  8.4 3.4 %collective-permute-start.1 = (f32[136,256]{1,0:T(8,128)S(1)}, f32[136,256]{1,0:T(8,128)S(1)}, u32[]{:S(2)}, u32[]{:S(2)}) collective-permute-start(f32[136,256]{1,0:T(8,128)S(1)} %get-tuple-element.33.mine), channel_id=1, source_target_pairs={{0,16},{1,17},{2,18},{3,19},{4,20},{5,21},{6,22},{7,23},{8,0},{9,1... | collective-permute-start | bytes 417800 | tf_op jit(solution)/shard_map/ppermute | solution.py:526
  11.9 2.7 %collective-permute-start = (f32[136,256]{1,0:T(8,128)S(1)}, f32[136,256]{1,0:T(8,128)S(1)}, u32[]{:S(2)}, u32[]{:S(2)}) collective-permute-start(f32[136,256]{1,0:T(8,128)S(1)} %get-tuple-element.33.mine), channel_id=1, source_target_pairs={{0,8},{1,9},{2,10},{3,11},{4,12},{5,13},{6,14},{7,15},{8,16},{9,17... | collective-permute-start | bytes 417800 | tf_op jit(solution)/shard_map/ppermute | solution.py:526
  14.6 1.3 %collective-permute-start.8 = (f32[3,72,512]{2,1,0:T(8,128)}, f32[3,72,512]{2,1,0:T(8,128)S(1)}, u32[]{:S(2)}, u32[]{:S(2)}) collective-permute-start(f32[3,72,512]{2,1,0:T(8,128)} %get-tuple-element.35.late), channel_id=1, source_target_pairs={{8,1},{9,0},{10,3},{11,2},{12,5},{13,4},{14,7},{15,6},{24,17},{25,... | collective-permute-start | bytes 1327112 | tf_op jit(solution)/shard_map/ppermute | solution.py:526
  15.9 3.2 %shard_map.138 = (f32[384,128]{1,0:T(8,128)S(1)}, f32[96,128]{1,0:T(8,128)S(1)}, f32[96,128]{1,0:T(8,128)S(1)}, f32[8,128]{1,0:T(8,128)S(1)}) custom-call(f32[3,16384]{1,0:T(4,128)S(1)} %copy-done.4, f32[3,16384]{1,0:T(4,128)S(1)} %copy-done.1, s32[2,4096]{1,0:T(2,128)S(1)} %copy-done.9, f32[8,128]{1,0:T(8,128)S(1)} %get-tuple-element.36._), custom_call_target="tpu_custom_call" | custom-call | flops 16384 | bytes 786432 | tf_op jit(solution)/shard_map/pallas_call | solution.py:36
  19.2 0.9 %copy-done.6 = f32[72,512]{1,0:T(8,128)S(1)} copy-done((f32[72,512]{1,0:T(8,128)S(1)}, f32[72,512]{1,0:T(8,128)}, u32[]{:S(2)}) %copy-start.6) | copy-done | bytes 147480
  20.2 3.5 %collective-permute-start.7 = (f32[6,72,512]{2,1,0:T(8,128)S(1)}, f32[6,72,512]{2,1,0:T(8,128)S(1)}, u32[]{:S(2)}, u32[]{:S(2)}) collective-permute-start(f32[6,72,512]{2,1,0:T(8,128)S(1)} %get-tuple-element.46), channel_id=1, source_target_pairs={{0,2},{2,4},{3,1},{4,6},{5,3},{7,5},{16,18},{18,20},{19,17},{20,22... | collective-permute-start | bytes 2654216 | tf_op jit(solution)/shard_map/ppermute | solution.py:526
  23.8 2.3 %collective-permute-start.10 = (f32[456,256]{1,0:T(8,128)S(1)}, f32[456,256]{1,0:T(8,128)S(1)}, u32[]{:S(2)}, u32[]{:S(2)}) collective-permute-start(f32[456,256]{1,0:T(8,128)S(1)} %get-tuple-element.49), channel_id=1, source_target_pairs={{0,1},{1,0},{2,3},{3,2},{4,5},{5,4},{6,7},{7,6},{16,17},{17,16},{1... | collective-permute-start | bytes 1400840 | tf_op jit(solution)/shard_map/ppermute | solution.py:526
  26.1 3.4 %collective-permute-start.6 = (f32[456,256]{1,0:T(8,128)S(1)}, f32[456,256]{1,0:T(8,128)S(1)}, u32[]{:S(2)}, u32[]{:S(2)}) collective-permute-start(f32[456,256]{1,0:T(8,128)S(1)} %get-tuple-element.45), channel_id=1, source_target_pairs={{1,2},{2,1},{3,4},{4,3},{5,6},{6,5},{17,18},{18,17},{19,20},{20,19... | collective-permute-start | bytes 1400840 | tf_op jit(solution)/shard_map/ppermute | solution.py:526
  29.5 3.5 %collective-permute-start.9 = (f32[3,72,512]{2,1,0:T(8,128)S(1)}, f32[3,72,512]{2,1,0:T(8,128)S(1)}, u32[]{:S(2)}, u32[]{:S(2)}) collective-permute-start(f32[3,72,512]{2,1,0:T(8,128)S(1)} %collective-permute-done.8.near_late), channel_id=1, source_target_pairs={{0,2},{2,4},{3,1},{4,6},{5,3},{7,5},{16,18},{18,20},{19,17},{20,22... | collective-permute-start | bytes 1327112 | tf_op jit(solution)/shard_map/ppermute | solution.py:526
  33.0 0.7 %collective-permute-start.4 = (f32[96,128]{1,0:T(8,128)S(1)}, f32[96,128]{1,0:T(8,128)S(1)}, u32[]{:S(2)}, u32[]{:S(2)}) collective-permute-start(f32[96,128]{1,0:T(8,128)S(1)} %get-tuple-element.37.halo_near), channel_id=1, source_target_pairs={{8,9},{9,8},{10,11},{11,10},{12,13},{13,12},{14,15},{15,14}} | collective-permute-start | bytes 147464 | tf_op jit(solution)/shard_map/ppermute | solution.py:526
  34.4 1.4 %shard_map.141 = (f32[4,72,512]{2,1,0:T(8,128)S(1)}, f32[4,72,512]{2,1,0:T(8,128)S(1)}, f32[128,128]{1,0:T(8,128)S(1)}, bf16[384,1152]{1,0:T(8,128)(2,1)S(1)}) custom-call(f32[136,256]{1,0:T(8,128)S(1)} %get-tuple-element.33.mine, f32[136,256]{1,0:T(8,128)S(1)} %collective-permute-done._second.second, f32[136,256]{1,0:T(8,128)S(1)} %collective-permute-done.1._third.third, ...), custom_call_target="tpu_custom_call" | custom-call | flops 679477248 | bytes 5308416 | tf_op jit(solution)/shard_map/pallas_call | solution.py:36
  35.8 4.5 %collective-permute-done.10.message.message_near = f32[456,256]{1,0:T(8,128)S(1)} collective-permute-done((f32[456,256]{1,0:T(8,128)S(1)}, f32[456,256]{1,0:T(8,128)S(1)}, u32[]{:S(2)}, u32[]{:S(2)}) %collective-permute-start.10) | collective-permute-done | bytes 466976 | tf_op jit(solution)/shard_map/ppermute | solution.py:526
  40.3 3.3 %shard_map.142 = (f32[4,72,512]{2,1,0:T(8,128)S(1)}, f32[4,72,512]{2,1,0:T(8,128)S(1)}) custom-call(f32[456,256]{1,0:T(8,128)S(1)} %collective-permute-done.10.message.message_near, f32[5,72,512]{2,1,0:T(8,128)S(1)} %copy-done, f32[5,72,512]{2,1,0:T(8,128)S(1)} %collective-permute-done.2.near, f32[3,72,512]{2,1,0:T(8,128)S(1)} %collective-permute-done.8.near_late, ...), custom_call_target="tpu_custom_call" | custom-call | flops 679477248 | bytes 5308416 | tf_op jit(solution)/shard_map/pallas_call | solution.py:36
  43.6 5.0 %shard_map.143 = (f32[128,384]{1,0:T(8,128)S(1)}, f32[128,384]{1,0:T(8,128)S(1)}, bf16[1152,768]{1,0:T(8,128)(2,1)S(1)}) custom-call(bf16[384,1152]{1,0:T(8,128)(2,1)S(1)} %get-tuple-element.44.picks, f32[456,256]{1,0:T(8,128)S(1)} %collective-permute-done.6.message.message_far, f32[5,72,512]{2,1,0:T(8,128)S(1)} %copy-done, ...), custom_call_target="tpu_custom_call" | custom-call | flops 679477248 | bytes 5308416 | tf_op jit(solution)/shard_map/pallas_call | solution.py:36
  48.7 2.6 %collective-permute-start.11 = (f32[128,384]{1,0:T(8,128)S(1)}, f32[128,384]{1,0:T(8,128)S(1)}, u32[]{:S(2)}, u32[]{:S(2)}) collective-permute-start(f32[128,384]{1,0:T(8,128)S(1)} %get-tuple-element.53), channel_id=1, source_target_pairs={{0,16},{1,17},{2,18},{3,19},{4,20},{5,21},{6,22},{7,23},{16,8},{17... | collective-permute-start | bytes 589832 | tf_op jit(solution)/shard_map/ppermute | solution.py:526
  51.3 1.9 %collective-permute-start.12 = (f32[128,384]{1,0:T(8,128)S(1)}, f32[128,384]{1,0:T(8,128)S(1)}, u32[]{:S(2)}, u32[]{:S(2)}) collective-permute-start(f32[128,384]{1,0:T(8,128)S(1)} %get-tuple-element.54), channel_id=1, source_target_pairs={{0,8},{1,9},{2,10},{3,11},{4,12},{5,13},{6,14},{7,15},{16,0},{17,1... | collective-permute-start | bytes 589832 | tf_op jit(solution)/shard_map/ppermute | solution.py:526
  53.7 4.3 %shard_map.145 = (f32[384,128]{1,0:T(8,128)S(1)}, f32[128,128]{1,0:T(8,128)S(1)}) custom-call(s32[128]{0:T(128)S(1)} %copy-done.12, f32[384,128]{1,0:T(8,128)S(1)} %get-tuple-element.55.state, f32[456,256]{1,0:T(8,128)S(1)} %collective-permute-done.10.message.message_near, f32[456,256]{1,0:T(8,128)S(1)} %collective-permute-done.6.message.message_far, ...), custom_call_target="tpu_custom_call" | custom-call | flops 7864320 | bytes 1310720 | tf_op jit(solution)/shard_map/pallas_call | solution.py:36
  58.0 0.8 %collective-permute-done.12.grads_c = f32[128,384]{1,0:T(8,128)S(1)} collective-permute-done((f32[128,384]{1,0:T(8,128)S(1)}, f32[128,384]{1,0:T(8,128)S(1)}, u32[]{:S(2)}, u32[]{:S(2)}) %collective-permute-start.12) | collective-permute-done | bytes 196640 | tf_op jit(solution)/shard_map/ppermute | solution.py:526
  58.8 0.9 %shard_map.146 = f32[3,16384]{1,0:T(4,128)} custom-call(s32[2,128]{1,0:T(2,128)S(1)} %copy-done.11, f32[128,384]{1,0:T(8,128)S(1)} %shard_map.144._.grads_a, f32[128,384]{1,0:T(8,128)S(1)} %collective-permute-done.11.grads_b, f32[128,384]{1,0:T(8,128)S(1)} %collective-permute-done.12.grads_c, f32[384,128]{1,0:T(8,128)S(1)} %get-tuple-element.57.base, ...), custom_call_target="tpu_custom_call" | custom-call | flops 983040 | bytes 1310720 | tf_op jit(solution)/shard_map/pallas_call | solution.py:36
  (41 shorter events, 1.4 us)
Async XLA Ops:
  0.0 6.0 %copy-start.5 = (s32[16384]{0:T(1024)S(1)}, s32[16384]{0:T(1024)}, u32[]{:S(2)}) copy-start(s32[16384]{0:T(1024)} %param.23) | copy-start | bytes 196612
  0.0 6.1 %copy-start.8 = (f32[16384]{0:T(1024)S(1)}, f32[16384]{0:T(1024)}, u32[]{:S(2)}) copy-start(f32[16384]{0:T(1024)} %param.17) | copy-start | bytes 196612
  0.0 6.1 %copy-start.7 = (f32[16384]{0:T(1024)S(1)}, f32[16384]{0:T(1024)}, u32[]{:S(2)}) copy-start(f32[16384]{0:T(1024)} %param.16) | copy-start | bytes 196612
  0.7 15.2 %copy-start.1 = (f32[3,16384]{1,0:T(4,128)S(1)}, f32[3,16384]{1,0:T(4,128)}, u32[]{:S(2)}) copy-start(f32[3,16384]{1,0:T(4,128)} %vel.3) | copy-start | bytes 589828
  0.7 15.2 %copy-start.4 = (f32[3,16384]{1,0:T(4,128)S(1)}, f32[3,16384]{1,0:T(4,128)}, u32[]{:S(2)}) copy-start(f32[3,16384]{1,0:T(4,128)} %pos.1) | copy-start | bytes 589828
  0.7 15.2 %copy-start.9 = (s32[2,4096]{1,0:T(2,128)S(1)}, s32[2,4096]{1,0:T(2,128)}, u32[]{:S(2)}) copy-start(s32[2,4096]{1,0:T(2,128)} %lists.1) | copy-start | bytes 98308
  3.3 31.1 %copy-start = (f32[5,72,512]{2,1,0:T(8,128)S(1)}, f32[5,72,512]{2,1,0:T(8,128)}, u32[]{:S(2)}) copy-start(f32[5,72,512]{2,1,0:T(8,128)} %get-tuple-element.34.early.pressure) | copy-start | bytes 2211844
  3.3 15.9 %collective-permute-start.2 = (f32[5,72,512]{2,1,0:T(8,128)}, f32[5,72,512]{2,1,0:T(8,128)S(1)}, u32[]{:S(2)}, u32[]{:S(2)}) collective-permute-start(f32[5,72,512]{2,1,0:T(8,128)} %get-tuple-element.34.early.pressure), channel_id=1, source_target_pairs={{8,1},{9,0},{10,3},{11,2},{12,5},{13,4},{14,7},{15,6},{24,17},{25,... | collective-permute-start | bytes 2211848 | tf_op jit(solution)/shard_map/ppermute | solution.py:526
  4.7 14.5 %collective-permute-start.3 = (f32[72,512]{1,0:T(8,128)}, f32[72,512]{1,0:T(8,128)S(1)}, u32[]{:S(2)}, u32[]{:S(2)}) collective-permute-start(f32[72,512]{1,0:T(8,128)} %get-tuple-element.41), channel_id=1, source_target_pairs={{9,3},{10,0},{11,5},{12,2},{13,7},{14,4},{25,19},{26,16},{27,21},{... | collective-permute-start | bytes 442376 | tf_op jit(solution)/shard_map/ppermute | solution.py:526
  6.8 27.7 %copy-start.13 = (f32[3,72,512]{2,1,0:T(8,128)S(1)}, f32[3,72,512]{2,1,0:T(8,128)}, u32[]{:S(2)}) copy-start(f32[3,72,512]{2,1,0:T(8,128)} %get-tuple-element.35.late) | copy-start | bytes 1327108
  8.4 10.7 %collective-permute-start.1 = (f32[136,256]{1,0:T(8,128)S(1)}, f32[136,256]{1,0:T(8,128)S(1)}, u32[]{:S(2)}, u32[]{:S(2)}) collective-permute-start(f32[136,256]{1,0:T(8,128)S(1)} %get-tuple-element.33.mine), channel_id=1, source_target_pairs={{0,16},{1,17},{2,18},{3,19},{4,20},{5,21},{6,22},{7,23},{8,0},{9,1... | collective-permute-start | bytes 417800 | tf_op jit(solution)/shard_map/ppermute | solution.py:526
  11.9 7.4 %collective-permute-start = (f32[136,256]{1,0:T(8,128)S(1)}, f32[136,256]{1,0:T(8,128)S(1)}, u32[]{:S(2)}, u32[]{:S(2)}) collective-permute-start(f32[136,256]{1,0:T(8,128)S(1)} %get-tuple-element.33.mine), channel_id=1, source_target_pairs={{0,8},{1,9},{2,10},{3,11},{4,12},{5,13},{6,14},{7,15},{8,16},{9,17... | collective-permute-start | bytes 417800 | tf_op jit(solution)/shard_map/ppermute | solution.py:526
  14.6 14.9 %collective-permute-start.8 = (f32[3,72,512]{2,1,0:T(8,128)}, f32[3,72,512]{2,1,0:T(8,128)S(1)}, u32[]{:S(2)}, u32[]{:S(2)}) collective-permute-start(f32[3,72,512]{2,1,0:T(8,128)} %get-tuple-element.35.late), channel_id=1, source_target_pairs={{8,1},{9,0},{10,3},{11,2},{12,5},{13,4},{14,7},{15,6},{24,17},{25,... | collective-permute-start | bytes 1327112 | tf_op jit(solution)/shard_map/ppermute | solution.py:526
  20.2 23.4 %collective-permute-start.7 = (f32[6,72,512]{2,1,0:T(8,128)S(1)}, f32[6,72,512]{2,1,0:T(8,128)S(1)}, u32[]{:S(2)}, u32[]{:S(2)}) collective-permute-start(f32[6,72,512]{2,1,0:T(8,128)S(1)} %get-tuple-element.46), channel_id=1, source_target_pairs={{0,2},{2,4},{3,1},{4,6},{5,3},{7,5},{16,18},{18,20},{19,17},{20,22... | collective-permute-start | bytes 2654216 | tf_op jit(solution)/shard_map/ppermute | solution.py:526
  23.8 16.5 %collective-permute-start.10 = (f32[456,256]{1,0:T(8,128)S(1)}, f32[456,256]{1,0:T(8,128)S(1)}, u32[]{:S(2)}, u32[]{:S(2)}) collective-permute-start(f32[456,256]{1,0:T(8,128)S(1)} %get-tuple-element.49), channel_id=1, source_target_pairs={{0,1},{1,0},{2,3},{3,2},{4,5},{5,4},{6,7},{7,6},{16,17},{17,16},{1... | collective-permute-start | bytes 1400840 | tf_op jit(solution)/shard_map/ppermute | solution.py:526
  26.1 17.5 %collective-permute-start.6 = (f32[456,256]{1,0:T(8,128)S(1)}, f32[456,256]{1,0:T(8,128)S(1)}, u32[]{:S(2)}, u32[]{:S(2)}) collective-permute-start(f32[456,256]{1,0:T(8,128)S(1)} %get-tuple-element.45), channel_id=1, source_target_pairs={{1,2},{2,1},{3,4},{4,3},{5,6},{6,5},{17,18},{18,17},{19,20},{20,19... | collective-permute-start | bytes 1400840 | tf_op jit(solution)/shard_map/ppermute | solution.py:526
  29.5 14.0 %collective-permute-start.9 = (f32[3,72,512]{2,1,0:T(8,128)S(1)}, f32[3,72,512]{2,1,0:T(8,128)S(1)}, u32[]{:S(2)}, u32[]{:S(2)}) collective-permute-start(f32[3,72,512]{2,1,0:T(8,128)S(1)} %collective-permute-done.8.near_late), channel_id=1, source_target_pairs={{0,2},{2,4},{3,1},{4,6},{5,3},{7,5},{16,18},{18,20},{19,17},{20,22... | collective-permute-start | bytes 1327112 | tf_op jit(solution)/shard_map/ppermute | solution.py:526
  33.0 0.7 %collective-permute-start.4 = (f32[96,128]{1,0:T(8,128)S(1)}, f32[96,128]{1,0:T(8,128)S(1)}, u32[]{:S(2)}, u32[]{:S(2)}) collective-permute-start(f32[96,128]{1,0:T(8,128)S(1)} %get-tuple-element.37.halo_near), channel_id=1, source_target_pairs={{8,9},{9,8},{10,11},{11,10},{12,13},{13,12},{14,15},{15,14}} | collective-permute-start | bytes 147464 | tf_op jit(solution)/shard_map/ppermute | solution.py:526
  33.7 0.7 %collective-permute-start.5 = (f32[96,128]{1,0:T(8,128)S(1)}, f32[96,128]{1,0:T(8,128)S(1)}, u32[]{:S(2)}, u32[]{:S(2)}) collective-permute-start(f32[96,128]{1,0:T(8,128)S(1)} %get-tuple-element.38.halo_far), channel_id=1, source_target_pairs={{9,10},{10,9},{11,12},{12,11},{13,14},{14,13}} | collective-permute-start | bytes 147464 | tf_op jit(solution)/shard_map/ppermute | solution.py:526
  48.6 5.0 %copy-start.2 = (s32[8,16384]{1,0:T(8,128)S(1)}, s32[8,16384]{1,0:T(8,128)}, u32[]{:S(2)}) copy-start(s32[8,16384]{1,0:T(8,128)} %named.1) | copy-start | bytes 1572868
  48.6 5.0 %copy-start.3 = (f32[8,16384]{1,0:T(8,128)S(1)}, f32[8,16384]{1,0:T(8,128)}, u32[]{:S(2)}) copy-start(f32[8,16384]{1,0:T(8,128)} %stiff.1) | copy-start | bytes 1572868
  48.7 9.4 %collective-permute-start.11 = (f32[128,384]{1,0:T(8,128)S(1)}, f32[128,384]{1,0:T(8,128)S(1)}, u32[]{:S(2)}, u32[]{:S(2)}) collective-permute-start(f32[128,384]{1,0:T(8,128)S(1)} %get-tuple-element.53), channel_id=1, source_target_pairs={{0,16},{1,17},{2,18},{3,19},{4,20},{5,21},{6,22},{7,23},{16,8},{17... | collective-permute-start | bytes 589832 | tf_op jit(solution)/shard_map/ppermute | solution.py:526
  51.3 7.6 %collective-permute-start.12 = (f32[128,384]{1,0:T(8,128)S(1)}, f32[128,384]{1,0:T(8,128)S(1)}, u32[]{:S(2)}, u32[]{:S(2)}) collective-permute-start(f32[128,384]{1,0:T(8,128)S(1)} %get-tuple-element.54), channel_id=1, source_target_pairs={{0,8},{1,9},{2,10},{3,11},{4,12},{5,13},{6,14},{7,15},{16,0},{17,1... | collective-permute-start | bytes 589832 | tf_op jit(solution)/shard_map/ppermute | solution.py:526
  53.6 5.2 %copy-start.11 = (s32[2,128]{1,0:T(2,128)S(1)}, s32[2,128]{1,0:T(2,128)}, u32[]{:S(2)}) copy-start(s32[2,128]{1,0:T(2,128)} %get-tuple-element.32.marks) | copy-start | bytes 3076
  (3 other events, 6.6 us)

commit v16 on v14

--- a/solution.py
+++ b/solution.py
@@ -218,8 +218,29 @@
         out[rows:, BLOCK:] = halo[half:, :]
 
 
+def inner_contact_kernel(state, named, stiff, _partner, _weight, out, dummy):
+    dummy[...] = jnp.zeros(dummy.shape, F32)
+    tiles = state.shape[0] // 3
+
+    def step(tile, carry):
+        lanes = pl.ds(pl.multiple_of(tile * BLOCK, BLOCK), BLOCK)
+        entry = named[:, lanes]
+        weight = jnp.where(entry >= 0, stiff[:, lanes], 0.0)
+        own = entry < BLOCK
+        lane = entry & (BLOCK - 1)
+        for axis in range(3):
+            row = pl.ds(axis * tiles + tile, 1)
+            mine = jnp.broadcast_to(state[row, :], entry.shape)
+            met = jnp.where(own, lanes_of(mine, lane), 0.0)
+            out[row, :] = jnp.sum(weight * (mine - met), axis=0, keepdims=True)
+        return carry
+
+    lax.fori_loop(0, tiles, step, 0, unroll=4)
+
+
 def contact_kernel(
-    partner, state, message_near, message_far, halo_near, halo_far, named, stiff, _, out, extended
+    partner, state, message_near, message_far, halo_near, halo_far, named, stiff, inner, _, out,
+    extended,
 ):
     tiles = state.shape[0] // 3
     rows = halo_near.shape[0] // 3
@@ -243,16 +264,14 @@
     def step(tile, carry):
         lanes = pl.ds(pl.multiple_of(tile * BLOCK, BLOCK), BLOCK)
         entry = named[:, lanes]
-        weight = jnp.where(entry >= 0, stiff[:, lanes], 0.0)
-        own = entry < BLOCK
+        weight = jnp.where(entry >= BLOCK, stiff[:, lanes], 0.0)
         lane = entry & (BLOCK - 1)
         other = partner[tile]
         for axis in range(3):
-            mine = jnp.broadcast_to(extended[pl.ds(axis * blocks + tile, 1), :], entry.shape)
             theirs = jnp.broadcast_to(extended[pl.ds(axis * blocks + other, 1), :], entry.shape)
-            met = jnp.where(own, lanes_of(mine, lane), lanes_of(theirs, lane))
-            pull = jnp.sum(weight * (mine - met), axis=0, keepdims=True)
-            out[pl.ds(axis * tiles + tile, 1), :] = pull
+            pull = jnp.sum(weight * lanes_of(theirs, lane), axis=0, keepdims=True)
+            row = pl.ds(axis * tiles + tile, 1)
+            out[row, :] = inner[row, :] - pull
         return carry
 
     lax.fori_loop(0, tiles, step, 0, unroll=4)
@@ -369,7 +388,8 @@
 
 
 def near_kernel(
-    full, tiles, message, pressure, near, near_late, beyond, own_constant, own_factor, kept_even, kept_odd,
+    full, tiles, message, pressure, near, near_late, beyond, own_constant, own_factor, _inner,
+    kept_even, kept_odd,
     constant, factor, old, new,
 ):
     planes, height, width = own_constant.shape
@@ -398,7 +418,7 @@
 
 def far_kernel(
     full, tiles, picks, message, pressure, far, far_late, own_constant, own_factor, kept_even, kept_odd,
-    out_a, out_b, out_c, constant, factor, old, new, fields,
+    out, pieces, constant, factor, old, new, fields,
 ):
     planes, height, width = own_constant.shape
     zones = width // BLOCK
@@ -444,11 +464,18 @@
         return carry
 
     lax.fori_loop(0, planes, gradient, 0, unroll=4)
-    pieces = jnp.concatenate(halves_of(fields[...]), 1)
-    total = jnp.dot(picks[...], pieces, preferred_element_type=F32)
-    total = total[:, : 3 * BLOCK] + total[:, 3 * BLOCK :]
-    for index, out in enumerate((out_a, out_b, out_c)):
-        out[...] = total[index * tiles : (index + 1) * tiles]
+    pieces[...] = jnp.concatenate(halves_of(fields[...]), 1)
+    out[...] = picked_rows(picks[tiles : 2 * tiles, :], pieces)
+
+
+def picked_rows(hot, pieces):
+    total = jnp.dot(hot, pieces[...], preferred_element_type=F32)
+    return total[:, : 3 * BLOCK] + total[:, 3 * BLOCK :]
+
+
+def pick_kernel(place, picks, pieces, _, out):
+    tiles = out.shape[0]
+    out[...] = picked_rows(picks[place * tiles : (place + 1) * tiles, :], pieces)
 
 
 def final_kernel(
@@ -583,37 +610,49 @@
         (mine, second, third, early, late, after_message, came_near, came_far),
         flops=planes * height * 4 * 384 * 256 * 6, size=9 * field_bytes,
     )
+    inner_contact, after_inner = call(
+        inner_contact_kernel, (shaped(3 * tiles, BLOCK), small), [VMEM] * 3 + [SMEM, VMEM],
+        (state, contact_rows, contact_stiff, partner_block, weight),
+        flops=60 * 8 * slots, size=4 * 20 * slots,
+    )
     window_of = lambda count: pltpu.VMEM((count, height, width), F32)
     kept_even, kept_odd = call(
-        functools.partial(near_kernel, full, tiles), (field, field), [VMEM] * 7,
-        (message_near, early, near, near_late, beyond, constant, factor),
+        functools.partial(near_kernel, full, tiles), (field, field), [VMEM] * 8,
+        (message_near, early, near, near_late, beyond, constant, factor, after_inner),
         [window_of(planes)] * 2 + [window_of(2 * planes + 1)] * 2,
         flops=planes * height * 4 * 384 * 256 * 6, size=9 * field_bytes,
     )
     grads = shaped(tiles, 3 * BLOCK)
-    grads_a, grads_b, grads_c = call(
-        functools.partial(far_kernel, full, tiles), (grads,) * 3, [VMEM] * 9,
+    cells_held = planes * height * width // BLOCK
+    grads_b, pieces = call(
+        functools.partial(far_kernel, full, tiles),
+        (grads, jax.ShapeDtypeStruct((cells_held, 6 * BLOCK), BF16)), [VMEM] * 9,
         (picks, message_far, early, far, far_late, constant, factor, kept_even, kept_odd),
         [window_of(planes)] * 2
         + [window_of(3 * planes + 2)] * 2
-        + [pltpu.VMEM((planes * height * width // BLOCK, 3 * BLOCK), F32)],
+        + [pltpu.VMEM((cells_held, 3 * BLOCK), F32)],
         flops=planes * height * 4 * 384 * 256 * 6, size=9 * field_bytes,
     )
-    grads_b = along_grp(grads_b, -1, owners)
-    grads_c = along_grp(grads_c, -2, owners)
-
+    came_b = along_grp(grads_b, -1, owners)
+    pick = lambda place, after: call(
+        functools.partial(pick_kernel, place), grads, [VMEM] * 3, (picks, pieces, after),
+        flops=slots, size=slots,
+    )
+    grads_c = pick(2, after_inner)
+    grads_a = pick(0, after_inner)
+    came_c = along_grp(grads_c, -2, owners)
     contact = call(
-        contact_kernel, shaped(3 * tiles, BLOCK), [SMEM] + [VMEM] * 7 + [ANY],
+        contact_kernel, shaped(3 * tiles, BLOCK), [SMEM] + [VMEM] * 8 + [ANY],
         (
             partner_block, state, message_near, message_far, came_near, came_far, contact_rows,
-            contact_stiff, grads_a,
+            contact_stiff, inner_contact, grads_a,
         ),
         [pltpu.VMEM((3 * (tiles + 2 * rows), BLOCK), F32)],
         flops=60 * 8 * slots, size=4 * 20 * slots,
     )
     return call(
         final_kernel, shaped(3, slots), [SMEM] + [VMEM] * 9,
-        (count, grads_a, grads_b, grads_c, weight, contact, grain_vel, vol, drag, cell),
+        (count, grads_a, came_c, came_b, weight, contact, grain_vel, vol, drag, cell),
         flops=60 * slots, size=4 * 20 * slots,
     )
 

time: 59.1 us -> 60.8 us (1.029)
  the two profiles are of different devices: /device:TPU:16 before, /device:TPU:0 now
where the time goes in v16:
time: 60.8 us; the launch traced here: 60.4 us
  starting transfers between devices  31.5 us (52%)
  Pallas kernels  26.5 us (44%)
  between operations  1.08 us (2%)
  local copies, waits for them, and re-layouts  0.96 us (2%)
    ppermute x13, starting transfers between devices, send(): return lax.ppermute(value, ('grp', 'reg'), flat)  31.5 us
    pallas_call x13, Pallas kernels, call(): pl.pallas_call(kernel, out_shape=outs, in_specs=specs, out_specs=jax.tree...  26.5 us
  transfers between devices with their start and end apart: 13, of which 1 were waited for; matrix products, arithmetic and copies ran while one was open for 0% of the time, Pallas kernels for 29%

profile of v16, /device:TPU:0, one launch (start us, length us, event | category | flops | bytes accessed | tf_op | source)
XLA Modules:
  0.0 60.4 jit_solution(4852443768255604411)
XLA Ops:
  0.0 2.6 %shard_map.137 = (f32[5,72,512]{2,1,0:T(8,128)}, f32[3,72,512]{2,1,0:T(8,128)}, f32[72,512]{1,0:T(8,128)}, f32[72,512]{1,0:T(8,128)}) custom-call(f32[4,128,512]{2,1,0:T(8,128)} %pressure_old.1, f32[4,128,512]{2,1,0:T(8,128)} %source.1, f32[4,128,512]{2,1,0:T(8,128)} %solid_before.1), custom_call_target="tpu_custom_call" | custom-call | flops 589824 | bytes 3538944 | tf_op jit(solution)/shard_map/pallas_call | solution.py:36
  2.6 1.4 %collective-permute-start.2 = (f32[5,72,512]{2,1,0:T(8,128)}, f32[5,72,512]{2,1,0:T(8,128)S(1)}, u32[]{:S(2)}, u32[]{:S(2)}) collective-permute-start(f32[5,72,512]{2,1,0:T(8,128)} %get-tuple-element.31.early.pressure), channel_id=1, source_target_pairs={{8,1},{9,0},{10,3},{11,2},{12,5},{13,4},{14,7},{15,6},{24,17},{25,... | collective-permute-start | bytes 2211848 | tf_op jit(solution)/shard_map/ppermute | solution.py:535
  4.1 1.3 %collective-permute-start.3 = (f32[72,512]{1,0:T(8,128)}, f32[72,512]{1,0:T(8,128)S(1)}, u32[]{:S(2)}, u32[]{:S(2)}) collective-permute-start(f32[72,512]{1,0:T(8,128)} %get-tuple-element.38), channel_id=1, source_target_pairs={{9,3},{10,0},{11,5},{12,2},{13,7},{14,4},{25,19},{26,16},{27,21},{... | collective-permute-start | bytes 442376 | tf_op jit(solution)/shard_map/ppermute | solution.py:535
  6.0 1.7 %shard_map.136 = (f32[136,256]{1,0:T(8,128)S(1)}, f32[8,128]{1,0:T(8,128)S(1)}) custom-call(s32[1]{0:T(128)S(6)} %copy.15.count, s32[128,128]{1,0:T(8,128)S(1)} %bitcast.4, f32[128,128]{1,0:T(8,128)S(1)} %bitcast.6, f32[128,128]{1,0:T(8,128)S(1)} %bitcast.8, s32[1,128]{1,0:T(1,128)S(1)} %bitcast.10), custom_call_target="tpu_custom_call" | custom-call | flops 201326592 | bytes 327680 | tf_op jit(solution)/shard_map/pallas_call | solution.py:36
  7.8 4.9 %collective-permute-start.1 = (f32[136,256]{1,0:T(8,128)S(1)}, f32[136,256]{1,0:T(8,128)S(1)}, u32[]{:S(2)}, u32[]{:S(2)}) collective-permute-start(f32[136,256]{1,0:T(8,128)S(1)} %get-tuple-element.30.mine), channel_id=1, source_target_pairs={{0,16},{1,17},{2,18},{3,19},{4,20},{5,21},{6,22},{7,23},{8,0},{9,1... | collective-permute-start | bytes 417800 | tf_op jit(solution)/shard_map/ppermute | solution.py:535
  12.6 2.1 %collective-permute-start = (f32[136,256]{1,0:T(8,128)S(1)}, f32[136,256]{1,0:T(8,128)S(1)}, u32[]{:S(2)}, u32[]{:S(2)}) collective-permute-start(f32[136,256]{1,0:T(8,128)S(1)} %get-tuple-element.30.mine), channel_id=1, source_target_pairs={{0,8},{1,9},{2,10},{3,11},{4,12},{5,13},{6,14},{7,15},{8,16},{9,17... | collective-permute-start | bytes 417800 | tf_op jit(solution)/shard_map/ppermute | solution.py:535
  14.7 1.3 %collective-permute-start.8 = (f32[3,72,512]{2,1,0:T(8,128)}, f32[3,72,512]{2,1,0:T(8,128)S(1)}, u32[]{:S(2)}, u32[]{:S(2)}) collective-permute-start(f32[3,72,512]{2,1,0:T(8,128)} %get-tuple-element.32.late), channel_id=1, source_target_pairs={{8,1},{9,0},{10,3},{11,2},{12,5},{13,4},{14,7},{15,6},{24,17},{25,... | collective-permute-start | bytes 1327112 | tf_op jit(solution)/shard_map/ppermute | solution.py:535
  16.1 3.2 %shard_map.138 = (f32[384,128]{1,0:T(8,128)S(1)}, f32[96,128]{1,0:T(8,128)S(1)}, f32[96,128]{1,0:T(8,128)S(1)}, f32[8,128]{1,0:T(8,128)S(1)}) custom-call(f32[3,16384]{1,0:T(4,128)S(1)} %copy-done.4, f32[3,16384]{1,0:T(4,128)S(1)} %copy-done.3, s32[2,4096]{1,0:T(2,128)S(1)} %copy-done.9, f32[8,128]{1,0:T(8,128)S(1)} %get-tuple-element.33._), custom_call_target="tpu_custom_call" | custom-call | flops 16384 | bytes 786432 | tf_op jit(solution)/shard_map/pallas_call | solution.py:36
  19.6 0.9 %copy-done.5 = f32[72,512]{1,0:T(8,128)S(1)} copy-done((f32[72,512]{1,0:T(8,128)S(1)}, f32[72,512]{1,0:T(8,128)}, u32[]{:S(2)}) %copy-start.5) | copy-done | bytes 147480
  20.6 4.1 %collective-permute-start.7 = (f32[6,72,512]{2,1,0:T(8,128)S(1)}, f32[6,72,512]{2,1,0:T(8,128)S(1)}, u32[]{:S(2)}, u32[]{:S(2)}) collective-permute-start(f32[6,72,512]{2,1,0:T(8,128)S(1)} %get-tuple-element.43), channel_id=1, source_target_pairs={{0,2},{2,4},{3,1},{4,6},{5,3},{7,5},{16,18},{18,20},{19,17},{20,22... | collective-permute-start | bytes 2654216 | tf_op jit(solution)/shard_map/ppermute | solution.py:535
  24.8 1.9 %collective-permute-start.10 = (f32[456,256]{1,0:T(8,128)S(1)}, f32[456,256]{1,0:T(8,128)S(1)}, u32[]{:S(2)}, u32[]{:S(2)}) collective-permute-start(f32[456,256]{1,0:T(8,128)S(1)} %get-tuple-element.46), channel_id=1, source_target_pairs={{0,1},{1,0},{2,3},{3,2},{4,5},{5,4},{6,7},{7,6},{16,17},{17,16},{1... | collective-permute-start | bytes 1400840 | tf_op jit(solution)/shard_map/ppermute | solution.py:535
  26.7 0.7 %collective-permute-start.6 = (f32[456,256]{1,0:T(8,128)S(1)}, f32[456,256]{1,0:T(8,128)S(1)}, u32[]{:S(2)}, u32[]{:S(2)}) collective-permute-start(f32[456,256]{1,0:T(8,128)S(1)} %get-tuple-element.42), channel_id=1, source_target_pairs={{1,2},{2,1},{3,4},{4,3},{5,6},{6,5},{17,18},{18,17},{19,20},{20,19... | collective-permute-start | bytes 1400840 | tf_op jit(solution)/shard_map/ppermute | solution.py:535
  27.4 6.6 %collective-permute-start.9 = (f32[3,72,512]{2,1,0:T(8,128)S(1)}, f32[3,72,512]{2,1,0:T(8,128)S(1)}, u32[]{:S(2)}, u32[]{:S(2)}) collective-permute-start(f32[3,72,512]{2,1,0:T(8,128)S(1)} %collective-permute-done.8.near_late), channel_id=1, source_target_pairs={{0,2},{2,4},{3,1},{4,6},{5,3},{7,5},{16,18},{18,20},{19,17},{20,22... | collective-permute-start | bytes 1327112 | tf_op jit(solution)/shard_map/ppermute | solution.py:535
  34.0 0.7 %collective-permute-start.4 = (f32[96,128]{1,0:T(8,128)S(1)}, f32[96,128]{1,0:T(8,128)S(1)}, u32[]{:S(2)}, u32[]{:S(2)}) collective-permute-start(f32[96,128]{1,0:T(8,128)S(1)} %get-tuple-element.34.halo_near), channel_id=1, source_target_pairs={{8,9},{9,8},{10,11},{11,10},{12,13},{13,12},{14,15},{15,14}} | collective-permute-start | bytes 147464 | tf_op jit(solution)/shard_map/ppermute | solution.py:535
  34.7 0.7 %collective-permute-start.5 = (f32[96,128]{1,0:T(8,128)S(1)}, f32[96,128]{1,0:T(8,128)S(1)}, u32[]{:S(2)}, u32[]{:S(2)}) collective-permute-start(f32[96,128]{1,0:T(8,128)S(1)} %get-tuple-element.35.halo_far), channel_id=1, source_target_pairs={{9,10},{10,9},{11,12},{12,11},{13,14},{14,13}} | collective-permute-start | bytes 147464 | tf_op jit(solution)/shard_map/ppermute | solution.py:535
  35.4 1.4 %shard_map.141 = (f32[4,72,512]{2,1,0:T(8,128)S(1)}, f32[4,72,512]{2,1,0:T(8,128)S(1)}, f32[128,128]{1,0:T(8,128)S(1)}, bf16[384,1152]{1,0:T(8,128)(2,1)S(1)}) custom-call(f32[136,256]{1,0:T(8,128)S(1)} %get-tuple-element.30.mine, f32[136,256]{1,0:T(8,128)S(1)} %collective-permute-done._second.second, f32[136,256]{1,0:T(8,128)S(1)} %collective-permute-done.1._third.third, ...), custom_call_target="tpu_custom_call" | custom-call | flops 679477248 | bytes 5308416 | tf_op jit(solution)/shard_map/pallas_call | solution.py:36
  36.8 3.8 %shard_map.142 = (f32[384,128]{1,0:T(8,128)S(1)}, f32[8,128]{1,0:T(8,128)S(1)}) custom-call(f32[384,128]{1,0:T(8,128)S(1)} %get-tuple-element.47.state, s32[8,16384]{1,0:T(8,128)S(1)} %copy-done.1, f32[8,16384]{1,0:T(8,128)S(1)} %copy-done.2, s32[128]{0:T(128)S(1)} %copy-done.10, f32[128,128]{1,0:T(8,128)S(1)} %get-tuple-element.48._weight.weight), custom_call_target="tpu_custom_call" | custom-call | flops 7864320 | bytes 1310720 | tf_op jit(solution)/shard_map/pallas_call | solution.py:36
  40.7 3.3 %shard_map.143 = (f32[4,72,512]{2,1,0:T(8,128)S(1)}, f32[4,72,512]{2,1,0:T(8,128)S(1)}) custom-call(f32[456,256]{1,0:T(8,128)S(1)} %collective-permute-done.10.message.message_near, f32[5,72,512]{2,1,0:T(8,128)S(1)} %copy-done, f32[5,72,512]{2,1,0:T(8,128)S(1)} %collective-permute-done.2.near, f32[3,72,512]{2,1,0:T(8,128)S(1)} %collective-permute-done.8.near_late, ...), custom_call_target="tpu_custom_call" | custom-call | flops 679477248 | bytes 5308416 | tf_op jit(solution)/shard_map/pallas_call | solution.py:36
  44.0 4.8 %shard_map.144 = (f32[128,384]{1,0:T(8,128)S(1)}, bf16[1152,768]{1,0:T(8,128)(2,1)S(1)}) custom-call(bf16[384,1152]{1,0:T(8,128)(2,1)S(1)} %get-tuple-element.41.picks, f32[456,256]{1,0:T(8,128)S(1)} %collective-permute-done.6.message.message_far, f32[5,72,512]{2,1,0:T(8,128)S(1)} %copy-done, f32[6,72,512]{2,1,0:T(8,128)S(1)} %collective-permute-done.7.far, ...), custom_call_target="tpu_custom_call" | custom-call | flops 679477248 | bytes 5308416 | tf_op jit(solution)/shard_map/pallas_call | solution.py:36
  48.8 0.4 shard_map.146
  49.2 1.9 %collective-permute-start.11 = (f32[128,384]{1,0:T(8,128)S(1)}, f32[128,384]{1,0:T(8,128)S(1)}, u32[]{:S(2)}, u32[]{:S(2)}) collective-permute-start(f32[128,384]{1,0:T(8,128)S(1)} %shard_map.146), channel_id=1, source_target_pairs={{0,8},{1,9},{2,10},{3,11},{4,12},{5,13},{6,14},{7,15},{16,0},{17,1... | collective-permute-start | bytes 589832 | tf_op jit(solution)/shard_map/ppermute | solution.py:535
  51.2 3.9 %collective-permute-start.12 = (f32[128,384]{1,0:T(8,128)S(1)}, f32[128,384]{1,0:T(8,128)S(1)}, u32[]{:S(2)}, u32[]{:S(2)}) collective-permute-start(f32[128,384]{1,0:T(8,128)S(1)} %get-tuple-element.53), channel_id=1, source_target_pairs={{0,16},{1,17},{2,18},{3,19},{4,20},{5,21},{6,22},{7,23},{16,8},{17... | collective-permute-start | bytes 589832 | tf_op jit(solution)/shard_map/ppermute | solution.py:535
  55.5 3.8 %shard_map.147.contact = f32[384,128]{1,0:T(8,128)S(1)} custom-call(s32[128]{0:T(128)S(1)} %copy-done.10, f32[384,128]{1,0:T(8,128)S(1)} %get-tuple-element.47.state, f32[456,256]{1,0:T(8,128)S(1)} %collective-permute-done.10.message.message_near, f32[456,256]{1,0:T(8,128)S(1)} %collective-permute-done.6.message.message_far, ...), custom_call_target="tpu_custom_call" | custom-call | flops 7864320 | bytes 1310720 | tf_op jit(solution)/shard_map/pallas_call | solution.py:36
  59.4 1.0 %shard_map.148 = f32[3,16384]{1,0:T(4,128)} custom-call(s32[1]{0:T(128)S(6)} %copy.15.count, f32[128,384]{1,0:T(8,128)S(1)} %shard_map.145._.grads_a, f32[128,384]{1,0:T(8,128)S(1)} %collective-permute-done.11.grads_b, f32[128,384]{1,0:T(8,128)S(1)} %collective-permute-done.12.grads_c, f32[128,128]{1,0:T(8,128)S(1)} %get-tuple-element.48._weight.weight, ...), custom_call_target="tpu_custom_call" | custom-call | flops 983040 | bytes 1310720 | tf_op jit(solution)/shard_map/pallas_call | solution.py:36
  (41 shorter events, 0.9 us)
Async XLA Ops:
  0.0 6.0 %copy-start.6 = (s32[16384]{0:T(1024)S(1)}, s32[16384]{0:T(1024)}, u32[]{:S(2)}) copy-start(s32[16384]{0:T(1024)} %param.23) | copy-start | bytes 196612
  0.0 6.0 %copy-start.8 = (f32[16384]{0:T(1024)S(1)}, f32[16384]{0:T(1024)}, u32[]{:S(2)}) copy-start(f32[16384]{0:T(1024)} %param.17) | copy-start | bytes 196612
  0.0 6.0 %copy-start.7 = (f32[16384]{0:T(1024)S(1)}, f32[16384]{0:T(1024)}, u32[]{:S(2)}) copy-start(f32[16384]{0:T(1024)} %param.16) | copy-start | bytes 196612
  0.0 16.0 %copy-start.3 = (f32[3,16384]{1,0:T(4,128)S(1)}, f32[3,16384]{1,0:T(4,128)}, u32[]{:S(2)}) copy-start(f32[3,16384]{1,0:T(4,128)} %vel.3) | copy-start | bytes 589828
  0.0 16.0 %copy-start.9 = (s32[2,4096]{1,0:T(2,128)S(1)}, s32[2,4096]{1,0:T(2,128)}, u32[]{:S(2)}) copy-start(s32[2,4096]{1,0:T(2,128)} %lists.1) | copy-start | bytes 98308
  0.0 16.0 %copy-start.4 = (f32[3,16384]{1,0:T(4,128)S(1)}, f32[3,16384]{1,0:T(4,128)}, u32[]{:S(2)}) copy-start(f32[3,16384]{1,0:T(4,128)} %pos.1) | copy-start | bytes 589828
  2.6 32.8 %copy-start = (f32[5,72,512]{2,1,0:T(8,128)S(1)}, f32[5,72,512]{2,1,0:T(8,128)}, u32[]{:S(2)}) copy-start(f32[5,72,512]{2,1,0:T(8,128)} %get-tuple-element.31.early.pressure) | copy-start | bytes 2211844
  2.6 32.8 %copy-start.11 = (f32[3,72,512]{2,1,0:T(8,128)S(1)}, f32[3,72,512]{2,1,0:T(8,128)}, u32[]{:S(2)}) copy-start(f32[3,72,512]{2,1,0:T(8,128)} %get-tuple-element.32.late) | copy-start | bytes 1327108
  2.6 17.0 %collective-permute-start.2 = (f32[5,72,512]{2,1,0:T(8,128)}, f32[5,72,512]{2,1,0:T(8,128)S(1)}, u32[]{:S(2)}, u32[]{:S(2)}) collective-permute-start(f32[5,72,512]{2,1,0:T(8,128)} %get-tuple-element.31.early.pressure), channel_id=1, source_target_pairs={{8,1},{9,0},{10,3},{11,2},{12,5},{13,4},{14,7},{15,6},{24,17},{25,... | collective-permute-start | bytes 2211848 | tf_op jit(solution)/shard_map/ppermute | solution.py:535
  4.1 15.5 %collective-permute-start.3 = (f32[72,512]{1,0:T(8,128)}, f32[72,512]{1,0:T(8,128)S(1)}, u32[]{:S(2)}, u32[]{:S(2)}) collective-permute-start(f32[72,512]{1,0:T(8,128)} %get-tuple-element.38), channel_id=1, source_target_pairs={{9,3},{10,0},{11,5},{12,2},{13,7},{14,4},{25,19},{26,16},{27,21},{... | collective-permute-start | bytes 442376 | tf_op jit(solution)/shard_map/ppermute | solution.py:535
  7.8 11.6 %collective-permute-start.1 = (f32[136,256]{1,0:T(8,128)S(1)}, f32[136,256]{1,0:T(8,128)S(1)}, u32[]{:S(2)}, u32[]{:S(2)}) collective-permute-start(f32[136,256]{1,0:T(8,128)S(1)} %get-tuple-element.30.mine), channel_id=1, source_target_pairs={{0,16},{1,17},{2,18},{3,19},{4,20},{5,21},{6,22},{7,23},{8,0},{9,1... | collective-permute-start | bytes 417800 | tf_op jit(solution)/shard_map/ppermute | solution.py:535
  12.6 6.9 %collective-permute-start = (f32[136,256]{1,0:T(8,128)S(1)}, f32[136,256]{1,0:T(8,128)S(1)}, u32[]{:S(2)}, u32[]{:S(2)}) collective-permute-start(f32[136,256]{1,0:T(8,128)S(1)} %get-tuple-element.30.mine), channel_id=1, source_target_pairs={{0,8},{1,9},{2,10},{3,11},{4,12},{5,13},{6,14},{7,15},{8,16},{9,17... | collective-permute-start | bytes 417800 | tf_op jit(solution)/shard_map/ppermute | solution.py:535
  14.7 12.7 %collective-permute-start.8 = (f32[3,72,512]{2,1,0:T(8,128)}, f32[3,72,512]{2,1,0:T(8,128)S(1)}, u32[]{:S(2)}, u32[]{:S(2)}) collective-permute-start(f32[3,72,512]{2,1,0:T(8,128)} %get-tuple-element.32.late), channel_id=1, source_target_pairs={{8,1},{9,0},{10,3},{11,2},{12,5},{13,4},{14,7},{15,6},{24,17},{25,... | collective-permute-start | bytes 1327112 | tf_op jit(solution)/shard_map/ppermute | solution.py:535
  20.6 16.3 %copy-start.1 = (s32[8,16384]{1,0:T(8,128)S(1)}, s32[8,16384]{1,0:T(8,128)}, u32[]{:S(2)}) copy-start(s32[8,16384]{1,0:T(8,128)} %named.3) | copy-start | bytes 1572868
  20.6 16.2 %copy-start.2 = (f32[8,16384]{1,0:T(8,128)S(1)}, f32[8,16384]{1,0:T(8,128)}, u32[]{:S(2)}) copy-start(f32[8,16384]{1,0:T(8,128)} %stiff.3) | copy-start | bytes 1572868
  20.6 16.2 %copy-start.10 = (s32[128]{0:T(128)S(1)}, s32[128]{0:T(128)}, u32[]{:S(2)}) copy-start(s32[128]{0:T(128)} %partner.1) | copy-start | bytes 1540
  20.6 23.4 %collective-permute-start.7 = (f32[6,72,512]{2,1,0:T(8,128)S(1)}, f32[6,72,512]{2,1,0:T(8,128)S(1)}, u32[]{:S(2)}, u32[]{:S(2)}) collective-permute-start(f32[6,72,512]{2,1,0:T(8,128)S(1)} %get-tuple-element.43), channel_id=1, source_target_pairs={{0,2},{2,4},{3,1},{4,6},{5,3},{7,5},{16,18},{18,20},{19,17},{20,22... | collective-permute-start | bytes 2654216 | tf_op jit(solution)/shard_map/ppermute | solution.py:535
  24.8 15.9 %collective-permute-start.10 = (f32[456,256]{1,0:T(8,128)S(1)}, f32[456,256]{1,0:T(8,128)S(1)}, u32[]{:S(2)}, u32[]{:S(2)}) collective-permute-start(f32[456,256]{1,0:T(8,128)S(1)} %get-tuple-element.46), channel_id=1, source_target_pairs={{0,1},{1,0},{2,3},{3,2},{4,5},{5,4},{6,7},{7,6},{16,17},{17,16},{1... | collective-permute-start | bytes 1400840 | tf_op jit(solution)/shard_map/ppermute | solution.py:535
  26.7 17.3 %collective-permute-start.6 = (f32[456,256]{1,0:T(8,128)S(1)}, f32[456,256]{1,0:T(8,128)S(1)}, u32[]{:S(2)}, u32[]{:S(2)}) collective-permute-start(f32[456,256]{1,0:T(8,128)S(1)} %get-tuple-element.42), channel_id=1, source_target_pairs={{1,2},{2,1},{3,4},{4,3},{5,6},{6,5},{17,18},{18,17},{19,20},{20,19... | collective-permute-start | bytes 1400840 | tf_op jit(solution)/shard_map/ppermute | solution.py:535
  27.4 16.6 %collective-permute-start.9 = (f32[3,72,512]{2,1,0:T(8,128)S(1)}, f32[3,72,512]{2,1,0:T(8,128)S(1)}, u32[]{:S(2)}, u32[]{:S(2)}) collective-permute-start(f32[3,72,512]{2,1,0:T(8,128)S(1)} %collective-permute-done.8.near_late), channel_id=1, source_target_pairs={{0,2},{2,4},{3,1},{4,6},{5,3},{7,5},{16,18},{18,20},{19,17},{20,22... | collective-permute-start | bytes 1327112 | tf_op jit(solution)/shard_map/ppermute | solution.py:535
  34.0 0.7 %collective-permute-start.4 = (f32[96,128]{1,0:T(8,128)S(1)}, f32[96,128]{1,0:T(8,128)S(1)}, u32[]{:S(2)}, u32[]{:S(2)}) collective-permute-start(f32[96,128]{1,0:T(8,128)S(1)} %get-tuple-element.34.halo_near), channel_id=1, source_target_pairs={{8,9},{9,8},{10,11},{11,10},{12,13},{13,12},{14,15},{15,14}} | collective-permute-start | bytes 147464 | tf_op jit(solution)/shard_map/ppermute | solution.py:535
  34.7 0.7 %collective-permute-start.5 = (f32[96,128]{1,0:T(8,128)S(1)}, f32[96,128]{1,0:T(8,128)S(1)}, u32[]{:S(2)}, u32[]{:S(2)}) collective-permute-start(f32[96,128]{1,0:T(8,128)S(1)} %get-tuple-element.35.halo_far), channel_id=1, source_target_pairs={{9,10},{10,9},{11,12},{12,11},{13,14},{14,13}} | collective-permute-start | bytes 147464 | tf_op jit(solution)/shard_map/ppermute | solution.py:535
  49.2 10.1 %collective-permute-start.11 = (f32[128,384]{1,0:T(8,128)S(1)}, f32[128,384]{1,0:T(8,128)S(1)}, u32[]{:S(2)}, u32[]{:S(2)}) collective-permute-start(f32[128,384]{1,0:T(8,128)S(1)} %shard_map.146), channel_id=1, source_target_pairs={{0,8},{1,9},{2,10},{3,11},{4,12},{5,13},{6,14},{7,15},{16,0},{17,1... | collective-permute-start | bytes 589832 | tf_op jit(solution)/shard_map/ppermute | solution.py:535
  51.2 8.2 %collective-permute-start.12 = (f32[128,384]{1,0:T(8,128)S(1)}, f32[128,384]{1,0:T(8,128)S(1)}, u32[]{:S(2)}, u32[]{:S(2)}) collective-permute-start(f32[128,384]{1,0:T(8,128)S(1)} %get-tuple-element.53), channel_id=1, source_target_pairs={{0,16},{1,17},{2,18},{3,19},{4,20},{5,21},{6,22},{7,23},{16,8},{17... | collective-permute-start | bytes 589832 | tf_op jit(solution)/shard_map/ppermute | solution.py:535
  (2 other events, 6.9 us)

commit v17 on v14

--- a/solution.py
+++ b/solution.py
@@ -218,8 +218,23 @@
         out[rows:, BLOCK:] = halo[half:, :]
 
 
+def merged(parts):
+    sub = iota((SUB, BLOCK), 0)
+    for step in (4, 2, 1):
+        low = (sub & step) == 0
+        paired = []
+        for first, second in zip(parts[:step], parts[step:]):
+            away = jnp.where(low, second, first)
+            back = pltpu.roll(away, step, 0)
+            if step < SUB // 2:
+                back = jnp.where(low, pltpu.roll(away, SUB - step, 0), back)
+            paired.append(jnp.where(low, first, second) + back)
+        parts = paired
+    return parts[0]
+
+
 def contact_kernel(
-    partner, state, message_near, message_far, halo_near, halo_far, named, stiff, _, out, extended
+    partner, state, message_near, message_far, halo_near, halo_far, named, stiff, _, out, extended,
 ):
     tiles = state.shape[0] // 3
     rows = halo_near.shape[0] // 3
@@ -240,22 +255,28 @@
             first = pl.multiple_of(axis * blocks + tiles + upper * rows, SUB)
             extended[pl.ds(first, rows), :] = carried[axis * rows : (axis + 1) * rows]
 
-    def step(tile, carry):
-        lanes = pl.ds(pl.multiple_of(tile * BLOCK, BLOCK), BLOCK)
-        entry = named[:, lanes]
-        weight = jnp.where(entry >= 0, stiff[:, lanes], 0.0)
-        own = entry < BLOCK
-        lane = entry & (BLOCK - 1)
-        other = partner[tile]
+    def step(group, carry):
+        first = pl.multiple_of(group * SUB, SUB)
+        held = [extended[pl.ds(axis * blocks + first, SUB), :] for axis in range(3)]
+        pulls = [[], [], []]
+        for t in range(SUB):
+            lanes = pl.ds(pl.multiple_of((first + t) * BLOCK, BLOCK), BLOCK)
+            entry = named[:, lanes]
+            weight = jnp.where(entry >= 0, stiff[:, lanes], 0.0)
+            own = entry < BLOCK
+            lane = entry & (BLOCK - 1)
+            other = partner[first + t]
+            for axis in range(3):
+                mine = jnp.broadcast_to(held[axis][t : t + 1], entry.shape)
+                theirs = extended[pl.ds(axis * blocks + other, 1), :]
+                theirs = jnp.broadcast_to(theirs, entry.shape)
+                met = jnp.where(own, lanes_of(mine, lane), lanes_of(theirs, lane))
+                pulls[axis].append(weight * (mine - met))
         for axis in range(3):
-            mine = jnp.broadcast_to(extended[pl.ds(axis * blocks + tile, 1), :], entry.shape)
-            theirs = jnp.broadcast_to(extended[pl.ds(axis * blocks + other, 1), :], entry.shape)
-            met = jnp.where(own, lanes_of(mine, lane), lanes_of(theirs, lane))
-            pull = jnp.sum(weight * (mine - met), axis=0, keepdims=True)
-            out[pl.ds(axis * tiles + tile, 1), :] = pull
+            out[pl.ds(axis * tiles + first, SUB), :] = merged(pulls[axis])
         return carry
 
-    lax.fori_loop(0, tiles, step, 0, unroll=4)
+    lax.fori_loop(0, tiles // SUB, step, 0)
 
 
 def shifted(plane):
@@ -322,7 +343,7 @@
 
 
 def own_kernel(
-    full, mine, second, third, early, late, _message, _near, _far, constant, factor, weight, picks
+    full, mine, second, third, early, late, _message, _near, _far, _partner, constant, factor, weight, picks
 ):
     tiles = weight.shape[0]
     planes, height, width = constant.shape
@@ -369,8 +390,7 @@
 
 
 def near_kernel(
-    full, tiles, message, pressure, near, near_late, beyond, own_constant, own_factor, kept_even, kept_odd,
-    constant, factor, old, new,
+    full, tiles, message, pressure, near, near_late, beyond, own_constant, own_factor, kept_even, kept_odd, constant, factor, old, new,
 ):
     planes, height, width = own_constant.shape
     place = Place(full, height)
@@ -398,7 +418,7 @@
 
 def far_kernel(
     full, tiles, picks, message, pressure, far, far_late, own_constant, own_factor, kept_even, kept_odd,
-    out_a, out_b, out_c, constant, factor, old, new, fields,
+    out, pieces, constant, factor, old, new, fields,
 ):
     planes, height, width = own_constant.shape
     zones = width // BLOCK
@@ -444,11 +464,18 @@
         return carry
 
     lax.fori_loop(0, planes, gradient, 0, unroll=4)
-    pieces = jnp.concatenate(halves_of(fields[...]), 1)
-    total = jnp.dot(picks[...], pieces, preferred_element_type=F32)
-    total = total[:, : 3 * BLOCK] + total[:, 3 * BLOCK :]
-    for index, out in enumerate((out_a, out_b, out_c)):
-        out[...] = total[index * tiles : (index + 1) * tiles]
+    pieces[...] = jnp.concatenate(halves_of(fields[...]), 1)
+    out[...] = picked_rows(picks[tiles : 2 * tiles, :], pieces)
+
+
+def picked_rows(hot, pieces):
+    total = jnp.dot(hot, pieces[...], preferred_element_type=F32)
+    return total[:, : 3 * BLOCK] + total[:, 3 * BLOCK :]
+
+
+def pick_kernel(place, picks, pieces, out):
+    tiles = out.shape[0]
+    out[...] = picked_rows(picks[place * tiles : (place + 1) * tiles, :], pieces)
 
 
 def final_kernel(
@@ -579,8 +606,8 @@
             field, field, shaped(tiles, BLOCK),
             jax.ShapeDtypeStruct((3 * tiles, planes * height * width // BLOCK), BF16),
         ),
-        [VMEM] * 8,
-        (mine, second, third, early, late, after_message, came_near, came_far),
+        [VMEM] * 8 + [SMEM],
+        (mine, second, third, early, late, after_message, came_near, came_far, partner_block),
         flops=planes * height * 4 * 384 * 256 * 6, size=9 * field_bytes,
     )
     window_of = lambda count: pltpu.VMEM((count, height, width), F32)
@@ -591,17 +618,24 @@
         flops=planes * height * 4 * 384 * 256 * 6, size=9 * field_bytes,
     )
     grads = shaped(tiles, 3 * BLOCK)
-    grads_a, grads_b, grads_c = call(
-        functools.partial(far_kernel, full, tiles), (grads,) * 3, [VMEM] * 9,
+    cells_held = planes * height * width // BLOCK
+    grads_b, pieces = call(
+        functools.partial(far_kernel, full, tiles),
+        (grads, jax.ShapeDtypeStruct((cells_held, 6 * BLOCK), BF16)), [VMEM] * 9,
         (picks, message_far, early, far, far_late, constant, factor, kept_even, kept_odd),
         [window_of(planes)] * 2
         + [window_of(3 * planes + 2)] * 2
-        + [pltpu.VMEM((planes * height * width // BLOCK, 3 * BLOCK), F32)],
+        + [pltpu.VMEM((cells_held, 3 * BLOCK), F32)],
         flops=planes * height * 4 * 384 * 256 * 6, size=9 * field_bytes,
     )
-    grads_b = along_grp(grads_b, -1, owners)
-    grads_c = along_grp(grads_c, -2, owners)
-
+    came_b = along_grp(grads_b, -1, owners)
+    pick = lambda place: call(
+        functools.partial(pick_kernel, place), grads, [VMEM] * 2, (picks, pieces),
+        flops=slots, size=slots,
+    )
+    grads_c = pick(2)
+    grads_a = pick(0)
+    came_c = along_grp(grads_c, -2, owners)
     contact = call(
         contact_kernel, shaped(3 * tiles, BLOCK), [SMEM] + [VMEM] * 7 + [ANY],
         (
@@ -613,7 +647,7 @@
     )
     return call(
         final_kernel, shaped(3, slots), [SMEM] + [VMEM] * 9,
-        (count, grads_a, grads_b, grads_c, weight, contact, grain_vel, vol, drag, cell),
+        (count, grads_a, came_c, came_b, weight, contact, grain_vel, vol, drag, cell),
         flops=60 * slots, size=4 * 20 * slots,
     )
 

time: 59.1 us -> 59.7 us (1.010)
  the two profiles are of different devices: /device:TPU:16 before, /device:TPU:18 now
where the time goes in v17:
time: 59.7 us; the launch traced here: 59.3 us
  starting transfers between devices  29.7 us (50%)
  Pallas kernels  22.5 us (38%)
  waiting for transfers between devices  5.03 us (8%)
  between operations  1.1 us (2%)
  local copies, waits for them, and re-layouts  0.96 us (2%)
    ppermute x13, starting transfers between devices, send(): return lax.ppermute(value, ('grp', 'reg'), flat)  29.7 us
    pallas_call x12, Pallas kernels, call(): pl.pallas_call(kernel, out_shape=outs, in_specs=specs, out_specs=jax.tree...  22.5 us
    ppermute x13, waiting for transfers between devices, send(): return lax.ppermute(value, ('grp', 'reg'), flat)  5.03 us
  transfers between devices with their start and end apart: 13, of which 2 were waited for; matrix products, arithmetic and copies ran while one was open for 0% of the time, Pallas kernels for 23%

profile of v17, /device:TPU:18, one launch (start us, length us, event | category | flops | bytes accessed | tf_op | source)
XLA Modules:
  0.0 59.3 jit_solution(3853966905592037477)
XLA Ops:
  0.0 2.6 %shard_map.137 = (f32[5,72,512]{2,1,0:T(8,128)}, f32[3,72,512]{2,1,0:T(8,128)}, f32[72,512]{1,0:T(8,128)}, f32[72,512]{1,0:T(8,128)}) custom-call(f32[4,128,512]{2,1,0:T(8,128)} %pressure_old.1, f32[4,128,512]{2,1,0:T(8,128)} %source.1, f32[4,128,512]{2,1,0:T(8,128)} %solid_before.1), custom_call_target="tpu_custom_call" | custom-call | flops 589824 | bytes 3538944 | tf_op jit(solution)/shard_map/pallas_call | solution.py:36
  2.7 1.4 %collective-permute-start.2 = (f32[5,72,512]{2,1,0:T(8,128)}, f32[5,72,512]{2,1,0:T(8,128)S(1)}, u32[]{:S(2)}, u32[]{:S(2)}) collective-permute-start(f32[5,72,512]{2,1,0:T(8,128)} %get-tuple-element.29.early.pressure), channel_id=1, source_target_pairs={{8,1},{9,0},{10,3},{11,2},{12,5},{13,4},{14,7},{15,6},{24,17},{25,... | collective-permute-start | bytes 2211848 | tf_op jit(solution)/shard_map/ppermute | solution.py:535
  4.1 1.3 %collective-permute-start.3 = (f32[72,512]{1,0:T(8,128)}, f32[72,512]{1,0:T(8,128)S(1)}, u32[]{:S(2)}, u32[]{:S(2)}) collective-permute-start(f32[72,512]{1,0:T(8,128)} %get-tuple-element.36), channel_id=1, source_target_pairs={{9,3},{10,0},{11,5},{12,2},{13,7},{14,4},{25,19},{26,16},{27,21},{... | collective-permute-start | bytes 442376 | tf_op jit(solution)/shard_map/ppermute | solution.py:535
  6.1 1.7 %shard_map.136 = (f32[136,256]{1,0:T(8,128)S(1)}, f32[8,128]{1,0:T(8,128)S(1)}) custom-call(s32[1]{0:T(128)S(6)} %copy.15.count, s32[128,128]{1,0:T(8,128)S(1)} %bitcast.4, f32[128,128]{1,0:T(8,128)S(1)} %bitcast.6, f32[128,128]{1,0:T(8,128)S(1)} %bitcast.8, s32[1,128]{1,0:T(1,128)S(1)} %bitcast.10), custom_call_target="tpu_custom_call" | custom-call | flops 201326592 | bytes 327680 | tf_op jit(solution)/shard_map/pallas_call | solution.py:36
  7.8 4.3 %collective-permute-start.1 = (f32[136,256]{1,0:T(8,128)S(1)}, f32[136,256]{1,0:T(8,128)S(1)}, u32[]{:S(2)}, u32[]{:S(2)}) collective-permute-start(f32[136,256]{1,0:T(8,128)S(1)} %get-tuple-element.28.mine), channel_id=1, source_target_pairs={{0,16},{1,17},{2,18},{3,19},{4,20},{5,21},{6,22},{7,23},{8,0},{9,1... | collective-permute-start | bytes 417800 | tf_op jit(solution)/shard_map/ppermute | solution.py:535
  12.1 1.9 %collective-permute-start = (f32[136,256]{1,0:T(8,128)S(1)}, f32[136,256]{1,0:T(8,128)S(1)}, u32[]{:S(2)}, u32[]{:S(2)}) collective-permute-start(f32[136,256]{1,0:T(8,128)S(1)} %get-tuple-element.28.mine), channel_id=1, source_target_pairs={{0,8},{1,9},{2,10},{3,11},{4,12},{5,13},{6,14},{7,15},{8,16},{9,17... | collective-permute-start | bytes 417800 | tf_op jit(solution)/shard_map/ppermute | solution.py:535
  14.1 1.3 %collective-permute-start.8 = (f32[3,72,512]{2,1,0:T(8,128)}, f32[3,72,512]{2,1,0:T(8,128)S(1)}, u32[]{:S(2)}, u32[]{:S(2)}) collective-permute-start(f32[3,72,512]{2,1,0:T(8,128)} %get-tuple-element.30.late), channel_id=1, source_target_pairs={{8,1},{9,0},{10,3},{11,2},{12,5},{13,4},{14,7},{15,6},{24,17},{25,... | collective-permute-start | bytes 1327112 | tf_op jit(solution)/shard_map/ppermute | solution.py:535
  15.4 3.2 %shard_map.138 = (f32[384,128]{1,0:T(8,128)S(1)}, f32[96,128]{1,0:T(8,128)S(1)}, f32[96,128]{1,0:T(8,128)S(1)}, f32[8,128]{1,0:T(8,128)S(1)}) custom-call(f32[3,16384]{1,0:T(4,128)S(1)} %copy-done.4, f32[3,16384]{1,0:T(4,128)S(1)} %copy-done.1, s32[2,4096]{1,0:T(2,128)S(1)} %copy-done.9, f32[8,128]{1,0:T(8,128)S(1)} %get-tuple-element.31._), custom_call_target="tpu_custom_call" | custom-call | flops 16384 | bytes 786432 | tf_op jit(solution)/shard_map/pallas_call | solution.py:36
  18.7 0.9 %copy-done.5 = f32[72,512]{1,0:T(8,128)S(1)} copy-done((f32[72,512]{1,0:T(8,128)S(1)}, f32[72,512]{1,0:T(8,128)}, u32[]{:S(2)}) %copy-start.5) | copy-done | bytes 147480
  19.6 3.5 %collective-permute-start.7 = (f32[6,72,512]{2,1,0:T(8,128)S(1)}, f32[6,72,512]{2,1,0:T(8,128)S(1)}, u32[]{:S(2)}, u32[]{:S(2)}) collective-permute-start(f32[6,72,512]{2,1,0:T(8,128)S(1)} %get-tuple-element.41), channel_id=1, source_target_pairs={{0,2},{2,4},{3,1},{4,6},{5,3},{7,5},{16,18},{18,20},{19,17},{20,22... | collective-permute-start | bytes 2654216 | tf_op jit(solution)/shard_map/ppermute | solution.py:535
  23.2 2.3 %collective-permute-start.10 = (f32[456,256]{1,0:T(8,128)S(1)}, f32[456,256]{1,0:T(8,128)S(1)}, u32[]{:S(2)}, u32[]{:S(2)}) collective-permute-start(f32[456,256]{1,0:T(8,128)S(1)} %get-tuple-element.44), channel_id=1, source_target_pairs={{0,1},{1,0},{2,3},{3,2},{4,5},{5,4},{6,7},{7,6},{16,17},{17,16},{1... | collective-permute-start | bytes 1400840 | tf_op jit(solution)/shard_map/ppermute | solution.py:535
  25.5 3.4 %collective-permute-start.6 = (f32[456,256]{1,0:T(8,128)S(1)}, f32[456,256]{1,0:T(8,128)S(1)}, u32[]{:S(2)}, u32[]{:S(2)}) collective-permute-start(f32[456,256]{1,0:T(8,128)S(1)} %get-tuple-element.40), channel_id=1, source_target_pairs={{1,2},{2,1},{3,4},{4,3},{5,6},{6,5},{17,18},{18,17},{19,20},{20,19... | collective-permute-start | bytes 1400840 | tf_op jit(solution)/shard_map/ppermute | solution.py:535
  29.0 3.5 %collective-permute-start.9 = (f32[3,72,512]{2,1,0:T(8,128)S(1)}, f32[3,72,512]{2,1,0:T(8,128)S(1)}, u32[]{:S(2)}, u32[]{:S(2)}) collective-permute-start(f32[3,72,512]{2,1,0:T(8,128)S(1)} %collective-permute-done.8.near_late), channel_id=1, source_target_pairs={{0,2},{2,4},{3,1},{4,6},{5,3},{7,5},{16,18},{18,20},{19,17},{20,22... | collective-permute-start | bytes 1327112 | tf_op jit(solution)/shard_map/ppermute | solution.py:535
  32.5 0.7 %collective-permute-start.4 = (f32[96,128]{1,0:T(8,128)S(1)}, f32[96,128]{1,0:T(8,128)S(1)}, u32[]{:S(2)}, u32[]{:S(2)}) collective-permute-start(f32[96,128]{1,0:T(8,128)S(1)} %get-tuple-element.32.halo_near), channel_id=1, source_target_pairs={{8,9},{9,8},{10,11},{11,10},{12,13},{13,12},{14,15},{15,14}} | collective-permute-start | bytes 147464 | tf_op jit(solution)/shard_map/ppermute | solution.py:535
  33.1 0.7 %collective-permute-start.5 = (f32[96,128]{1,0:T(8,128)S(1)}, f32[96,128]{1,0:T(8,128)S(1)}, u32[]{:S(2)}, u32[]{:S(2)}) collective-permute-start(f32[96,128]{1,0:T(8,128)S(1)} %get-tuple-element.33.halo_far), channel_id=1, source_target_pairs={{9,10},{10,9},{11,12},{12,11},{13,14},{14,13}} | collective-permute-start | bytes 147464 | tf_op jit(solution)/shard_map/ppermute | solution.py:535
  33.9 1.9 %shard_map.141 = (f32[4,72,512]{2,1,0:T(8,128)S(1)}, f32[4,72,512]{2,1,0:T(8,128)S(1)}, f32[128,128]{1,0:T(8,128)S(1)}, bf16[384,1152]{1,0:T(8,128)(2,1)S(1)}) custom-call(f32[136,256]{1,0:T(8,128)S(1)} %get-tuple-element.28.mine, f32[136,256]{1,0:T(8,128)S(1)} %collective-permute-done._second.second, f32[136,256]{1,0:T(8,128)S(1)} %collective-permute-done.1._third.third, ...), custom_call_target="tpu_custom_call" | custom-call | flops 679477248 | bytes 5308416 | tf_op jit(solution)/shard_map/pallas_call | solution.py:36
  35.8 2.9 %collective-permute-done.10.message.message_near = f32[456,256]{1,0:T(8,128)S(1)} collective-permute-done((f32[456,256]{1,0:T(8,128)S(1)}, f32[456,256]{1,0:T(8,128)S(1)}, u32[]{:S(2)}, u32[]{:S(2)}) %collective-permute-start.10) | collective-permute-done | bytes 466976 | tf_op jit(solution)/shard_map/ppermute | solution.py:535
  38.7 3.3 %shard_map.142 = (f32[4,72,512]{2,1,0:T(8,128)S(1)}, f32[4,72,512]{2,1,0:T(8,128)S(1)}) custom-call(f32[456,256]{1,0:T(8,128)S(1)} %collective-permute-done.10.message.message_near, f32[5,72,512]{2,1,0:T(8,128)S(1)} %copy-done, f32[5,72,512]{2,1,0:T(8,128)S(1)} %collective-permute-done.2.near, f32[3,72,512]{2,1,0:T(8,128)S(1)} %collective-permute-done.8.near_late, ...), custom_call_target="tpu_custom_call" | custom-call | flops 679477248 | bytes 5308416 | tf_op jit(solution)/shard_map/pallas_call | solution.py:36
  42.0 4.7 %shard_map.143 = (f32[128,384]{1,0:T(8,128)S(1)}, bf16[1152,768]{1,0:T(8,128)(2,1)S(1)}) custom-call(bf16[384,1152]{1,0:T(8,128)(2,1)S(1)} %get-tuple-element.39.picks, f32[456,256]{1,0:T(8,128)S(1)} %collective-permute-done.6.message.message_far, f32[5,72,512]{2,1,0:T(8,128)S(1)} %copy-done, f32[6,72,512]{2,1,0:T(8,128)S(1)} %collective-permute-done.7.far, ...), custom_call_target="tpu_custom_call" | custom-call | flops 679477248 | bytes 5308416 | tf_op jit(solution)/shard_map/pallas_call | solution.py:36
  47.2 3.5 %collective-permute-start.11 = (f32[128,384]{1,0:T(8,128)S(1)}, f32[128,384]{1,0:T(8,128)S(1)}, u32[]{:S(2)}, u32[]{:S(2)}) collective-permute-start(f32[128,384]{1,0:T(8,128)S(1)} %shard_map.145), channel_id=1, source_target_pairs={{0,8},{1,9},{2,10},{3,11},{4,12},{5,13},{6,14},{7,15},{16,0},{17,1... | collective-permute-start | bytes 589832 | tf_op jit(solution)/shard_map/ppermute | solution.py:535
  50.7 1.9 %collective-permute-start.12 = (f32[128,384]{1,0:T(8,128)S(1)}, f32[128,384]{1,0:T(8,128)S(1)}, u32[]{:S(2)}, u32[]{:S(2)}) collective-permute-start(f32[128,384]{1,0:T(8,128)S(1)} %get-tuple-element.48), channel_id=1, source_target_pairs={{0,16},{1,17},{2,18},{3,19},{4,20},{5,21},{6,22},{7,23},{16,8},{17... | collective-permute-start | bytes 589832 | tf_op jit(solution)/shard_map/ppermute | solution.py:535
  53.1 3.0 %shard_map.146.contact = f32[384,128]{1,0:T(8,128)S(1)} custom-call(s32[128]{0:T(128)S(1)} %copy-done.10, f32[384,128]{1,0:T(8,128)S(1)} %get-tuple-element.50.state, f32[456,256]{1,0:T(8,128)S(1)} %collective-permute-done.10.message.message_near, f32[456,256]{1,0:T(8,128)S(1)} %collective-permute-done.6.message.message_far, ...), custom_call_target="tpu_custom_call" | custom-call | flops 7864320 | bytes 1310720 | tf_op jit(solution)/shard_map/pallas_call | solution.py:36
  56.2 2.1 %collective-permute-done.12.grads_c = f32[128,384]{1,0:T(8,128)S(1)} collective-permute-done((f32[128,384]{1,0:T(8,128)S(1)}, f32[128,384]{1,0:T(8,128)S(1)}, u32[]{:S(2)}, u32[]{:S(2)}) %collective-permute-start.12) | collective-permute-done | bytes 196640 | tf_op jit(solution)/shard_map/ppermute | solution.py:535
  58.3 1.0 %shard_map.147 = f32[3,16384]{1,0:T(4,128)} custom-call(s32[1]{0:T(128)S(6)} %copy.15.count, f32[128,384]{1,0:T(8,128)S(1)} %shard_map.144._.grads_a, f32[128,384]{1,0:T(8,128)S(1)} %collective-permute-done.11.grads_b, f32[128,384]{1,0:T(8,128)S(1)} %collective-permute-done.12.grads_c, f32[128,128]{1,0:T(8,128)S(1)} %get-tuple-element.49.weight, ...), custom_call_target="tpu_custom_call" | custom-call | flops 983040 | bytes 1310720 | tf_op jit(solution)/shard_map/pallas_call | solution.py:36
  (40 shorter events, 1.1 us)
Async XLA Ops:
  0.0 6.0 %copy-start.12 = (s32[128]{0:T(128)S(1)}, s32[128]{0:T(128)}, u32[]{:S(2)}) copy-start(s32[128]{0:T(128)} %param.24) | copy-start | bytes 1540
  0.0 6.0 %copy-start.6 = (s32[16384]{0:T(1024)S(1)}, s32[16384]{0:T(1024)}, u32[]{:S(2)}) copy-start(s32[16384]{0:T(1024)} %param.23) | copy-start | bytes 196612
  0.0 6.1 %copy-start.8 = (f32[16384]{0:T(1024)S(1)}, f32[16384]{0:T(1024)}, u32[]{:S(2)}) copy-start(f32[16384]{0:T(1024)} %param.17) | copy-start | bytes 196612
  0.0 6.1 %copy-start.7 = (f32[16384]{0:T(1024)S(1)}, f32[16384]{0:T(1024)}, u32[]{:S(2)}) copy-start(f32[16384]{0:T(1024)} %param.16) | copy-start | bytes 196612
  0.0 15.3 %copy-start.1 = (f32[3,16384]{1,0:T(4,128)S(1)}, f32[3,16384]{1,0:T(4,128)}, u32[]{:S(2)}) copy-start(f32[3,16384]{1,0:T(4,128)} %vel.3) | copy-start | bytes 589828
  0.0 15.3 %copy-start.9 = (s32[2,4096]{1,0:T(2,128)S(1)}, s32[2,4096]{1,0:T(2,128)}, u32[]{:S(2)}) copy-start(s32[2,4096]{1,0:T(2,128)} %lists.1) | copy-start | bytes 98308
  0.0 15.3 %copy-start.4 = (f32[3,16384]{1,0:T(4,128)S(1)}, f32[3,16384]{1,0:T(4,128)}, u32[]{:S(2)}) copy-start(f32[3,16384]{1,0:T(4,128)} %pos.1) | copy-start | bytes 589828
  2.6 31.2 %copy-start = (f32[5,72,512]{2,1,0:T(8,128)S(1)}, f32[5,72,512]{2,1,0:T(8,128)}, u32[]{:S(2)}) copy-start(f32[5,72,512]{2,1,0:T(8,128)} %get-tuple-element.29.early.pressure) | copy-start | bytes 2211844
  2.6 31.2 %copy-start.10 = (s32[128]{0:T(128)S(1)}, s32[128]{0:T(128)}, u32[]{:S(2)}) copy-start(s32[128]{0:T(128)} %partner.1) | copy-start | bytes 1540
  2.6 31.2 %copy-start.11 = (f32[3,72,512]{2,1,0:T(8,128)S(1)}, f32[3,72,512]{2,1,0:T(8,128)}, u32[]{:S(2)}) copy-start(f32[3,72,512]{2,1,0:T(8,128)} %get-tuple-element.30.late) | copy-start | bytes 1327108
  2.7 16.0 %collective-permute-start.2 = (f32[5,72,512]{2,1,0:T(8,128)}, f32[5,72,512]{2,1,0:T(8,128)S(1)}, u32[]{:S(2)}, u32[]{:S(2)}) collective-permute-start(f32[5,72,512]{2,1,0:T(8,128)} %get-tuple-element.29.early.pressure), channel_id=1, source_target_pairs={{8,1},{9,0},{10,3},{11,2},{12,5},{13,4},{14,7},{15,6},{24,17},{25,... | collective-permute-start | bytes 2211848 | tf_op jit(solution)/shard_map/ppermute | solution.py:535
  4.1 14.6 %collective-permute-start.3 = (f32[72,512]{1,0:T(8,128)}, f32[72,512]{1,0:T(8,128)S(1)}, u32[]{:S(2)}, u32[]{:S(2)}) collective-permute-start(f32[72,512]{1,0:T(8,128)} %get-tuple-element.36), channel_id=1, source_target_pairs={{9,3},{10,0},{11,5},{12,2},{13,7},{14,4},{25,19},{26,16},{27,21},{... | collective-permute-start | bytes 442376 | tf_op jit(solution)/shard_map/ppermute | solution.py:535
  7.8 10.9 %collective-permute-start.1 = (f32[136,256]{1,0:T(8,128)S(1)}, f32[136,256]{1,0:T(8,128)S(1)}, u32[]{:S(2)}, u32[]{:S(2)}) collective-permute-start(f32[136,256]{1,0:T(8,128)S(1)} %get-tuple-element.28.mine), channel_id=1, source_target_pairs={{0,16},{1,17},{2,18},{3,19},{4,20},{5,21},{6,22},{7,23},{8,0},{9,1... | collective-permute-start | bytes 417800 | tf_op jit(solution)/shard_map/ppermute | solution.py:535
  12.1 6.5 %collective-permute-start = (f32[136,256]{1,0:T(8,128)S(1)}, f32[136,256]{1,0:T(8,128)S(1)}, u32[]{:S(2)}, u32[]{:S(2)}) collective-permute-start(f32[136,256]{1,0:T(8,128)S(1)} %get-tuple-element.28.mine), channel_id=1, source_target_pairs={{0,8},{1,9},{2,10},{3,11},{4,12},{5,13},{6,14},{7,15},{8,16},{9,17... | collective-permute-start | bytes 417800 | tf_op jit(solution)/shard_map/ppermute | solution.py:535
  14.1 14.9 %collective-permute-start.8 = (f32[3,72,512]{2,1,0:T(8,128)}, f32[3,72,512]{2,1,0:T(8,128)S(1)}, u32[]{:S(2)}, u32[]{:S(2)}) collective-permute-start(f32[3,72,512]{2,1,0:T(8,128)} %get-tuple-element.30.late), channel_id=1, source_target_pairs={{8,1},{9,0},{10,3},{11,2},{12,5},{13,4},{14,7},{15,6},{24,17},{25,... | collective-permute-start | bytes 1327112 | tf_op jit(solution)/shard_map/ppermute | solution.py:535
  19.6 22.3 %collective-permute-start.7 = (f32[6,72,512]{2,1,0:T(8,128)S(1)}, f32[6,72,512]{2,1,0:T(8,128)S(1)}, u32[]{:S(2)}, u32[]{:S(2)}) collective-permute-start(f32[6,72,512]{2,1,0:T(8,128)S(1)} %get-tuple-element.41), channel_id=1, source_target_pairs={{0,2},{2,4},{3,1},{4,6},{5,3},{7,5},{16,18},{18,20},{19,17},{20,22... | collective-permute-start | bytes 2654216 | tf_op jit(solution)/shard_map/ppermute | solution.py:535
  23.2 15.5 %collective-permute-start.10 = (f32[456,256]{1,0:T(8,128)S(1)}, f32[456,256]{1,0:T(8,128)S(1)}, u32[]{:S(2)}, u32[]{:S(2)}) collective-permute-start(f32[456,256]{1,0:T(8,128)S(1)} %get-tuple-element.44), channel_id=1, source_target_pairs={{0,1},{1,0},{2,3},{3,2},{4,5},{5,4},{6,7},{7,6},{16,17},{17,16},{1... | collective-permute-start | bytes 1400840 | tf_op jit(solution)/shard_map/ppermute | solution.py:535
  25.5 16.4 %collective-permute-start.6 = (f32[456,256]{1,0:T(8,128)S(1)}, f32[456,256]{1,0:T(8,128)S(1)}, u32[]{:S(2)}, u32[]{:S(2)}) collective-permute-start(f32[456,256]{1,0:T(8,128)S(1)} %get-tuple-element.40), channel_id=1, source_target_pairs={{1,2},{2,1},{3,4},{4,3},{5,6},{6,5},{17,18},{18,17},{19,20},{20,19... | collective-permute-start | bytes 1400840 | tf_op jit(solution)/shard_map/ppermute | solution.py:535
  29.0 13.0 %collective-permute-start.9 = (f32[3,72,512]{2,1,0:T(8,128)S(1)}, f32[3,72,512]{2,1,0:T(8,128)S(1)}, u32[]{:S(2)}, u32[]{:S(2)}) collective-permute-start(f32[3,72,512]{2,1,0:T(8,128)S(1)} %collective-permute-done.8.near_late), channel_id=1, source_target_pairs={{0,2},{2,4},{3,1},{4,6},{5,3},{7,5},{16,18},{18,20},{19,17},{20,22... | collective-permute-start | bytes 1327112 | tf_op jit(solution)/shard_map/ppermute | solution.py:535
  32.5 0.7 %collective-permute-start.4 = (f32[96,128]{1,0:T(8,128)S(1)}, f32[96,128]{1,0:T(8,128)S(1)}, u32[]{:S(2)}, u32[]{:S(2)}) collective-permute-start(f32[96,128]{1,0:T(8,128)S(1)} %get-tuple-element.32.halo_near), channel_id=1, source_target_pairs={{8,9},{9,8},{10,11},{11,10},{12,13},{13,12},{14,15},{15,14}} | collective-permute-start | bytes 147464 | tf_op jit(solution)/shard_map/ppermute | solution.py:535
  33.1 0.7 %collective-permute-start.5 = (f32[96,128]{1,0:T(8,128)S(1)}, f32[96,128]{1,0:T(8,128)S(1)}, u32[]{:S(2)}, u32[]{:S(2)}) collective-permute-start(f32[96,128]{1,0:T(8,128)S(1)} %get-tuple-element.33.halo_far), channel_id=1, source_target_pairs={{9,10},{10,9},{11,12},{12,11},{13,14},{14,13}} | collective-permute-start | bytes 147464 | tf_op jit(solution)/shard_map/ppermute | solution.py:535
  47.2 5.9 %copy-start.2 = (s32[8,16384]{1,0:T(8,128)S(1)}, s32[8,16384]{1,0:T(8,128)}, u32[]{:S(2)}) copy-start(s32[8,16384]{1,0:T(8,128)} %named.1) | copy-start | bytes 1572868
  47.2 9.0 %collective-permute-start.11 = (f32[128,384]{1,0:T(8,128)S(1)}, f32[128,384]{1,0:T(8,128)S(1)}, u32[]{:S(2)}, u32[]{:S(2)}) collective-permute-start(f32[128,384]{1,0:T(8,128)S(1)} %shard_map.145), channel_id=1, source_target_pairs={{0,8},{1,9},{2,10},{3,11},{4,12},{5,13},{6,14},{7,15},{16,0},{17,1... | collective-permute-start | bytes 589832 | tf_op jit(solution)/shard_map/ppermute | solution.py:535
  50.7 7.6 %collective-permute-start.12 = (f32[128,384]{1,0:T(8,128)S(1)}, f32[128,384]{1,0:T(8,128)S(1)}, u32[]{:S(2)}, u32[]{:S(2)}) collective-permute-start(f32[128,384]{1,0:T(8,128)S(1)} %get-tuple-element.48), channel_id=1, source_target_pairs={{0,16},{1,17},{2,18},{3,19},{4,20},{5,21},{6,22},{7,23},{16,8},{17... | collective-permute-start | bytes 589832 | tf_op jit(solution)/shard_map/ppermute | solution.py:535
  (2 other events, 6.8 us)

commit v18 on v17

--- a/solution.py
+++ b/solution.py
@@ -163,7 +163,8 @@
     out[tiles : tiles + SUB, BLOCK:] = jnp.zeros((SUB, BLOCK), F32)
 
 
-def halo_kernel(pos, vel, lists, _, state, near, far, dummy):
+def halo_kernel(pos, vel, lists, _, inner, state, near, far, dummy, held):
+    held[...] = inner[...]
     dummy[...] = jnp.zeros(dummy.shape, F32)
     tiles = pos.shape[1] // BLOCK
     rows = lists.shape[1] // BLOCK
@@ -465,21 +466,26 @@
 
     lax.fori_loop(0, planes, gradient, 0, unroll=4)
     pieces[...] = jnp.concatenate(halves_of(fields[...]), 1)
-    out[...] = picked_rows(picks[tiles : 2 * tiles, :], pieces)
-
-
-def picked_rows(hot, pieces):
+    out[...] = picked_rows(picks, 3 - across_set(), tiles, pieces)
+
+
+def across_set():
+    return jnp.where(lax.axis_index("grp") == 0, 1, 2)
+
+
+def picked_rows(picks, chosen, tiles, pieces):
+    hot = picks[pl.ds(pl.multiple_of(chosen * tiles, tiles), tiles), :]
     total = jnp.dot(hot, pieces[...], preferred_element_type=F32)
     return total[:, : 3 * BLOCK] + total[:, 3 * BLOCK :]
 
 
-def pick_kernel(place, picks, pieces, out):
-    tiles = out.shape[0]
-    out[...] = picked_rows(picks[place * tiles : (place + 1) * tiles, :], pieces)
+def pick_kernel(own, picks, pieces, out):
+    chosen = 0 if own else across_set()
+    out[...] = picked_rows(picks, chosen, out.shape[0], pieces)
 
 
 def final_kernel(
-    count, grads_a, grads_b, grads_c, weight, contact, vel, vol, drag, cell, out,
+    count, grads_a, grads_b, grads_c, grads_d, weight, contact, vel, vol, drag, cell, out,
 ):
     tiles = cell.shape[0]
     cells = cell[...]
@@ -490,7 +496,8 @@
     push = TIME_STEP / volume
     for axis in range(3):
         lanes = slice(axis * BLOCK, (axis + 1) * BLOCK)
-        gradient = lanes_of(grads_a[:, lanes] + grads_b[:, lanes] + grads_c[:, lanes], cells)
+        gradient = grads_a[:, lanes] + grads_b[:, lanes] + (grads_c[:, lanes] + grads_d[:, lanes])
+        gradient = lanes_of(gradient, cells)
         own = jnp.concatenate(
             [vel[axis : axis + 1, t * BLOCK : (t + 1) * BLOCK] for t in range(tiles)], 0
         )
@@ -579,9 +586,9 @@
     third = along_grp(mine, 2, holders)
     rows = halo_list.shape[1] // BLOCK
     halo = shaped(3 * rows, BLOCK)
-    state, halo_near, halo_far, after_halo = call(
-        halo_kernel, (shaped(3 * tiles, BLOCK), halo, halo, small),
-        [VMEM] * 4, (grain_pos, grain_vel, halo_list, after_deposit), flops=slots,
+    state, halo_near, halo_far, after_halo, inner = call(
+        halo_kernel, (shaped(3 * tiles, BLOCK), halo, halo, small, plane),
+        [VMEM] * 5, (grain_pos, grain_vel, halo_list, after_deposit, inner), flops=slots,
         size=4 * 4 * 3 * slots,
     )
     others = [g for g in holders if g not in owners]
@@ -619,7 +626,7 @@
     )
     grads = shaped(tiles, 3 * BLOCK)
     cells_held = planes * height * width // BLOCK
-    grads_b, pieces = call(
+    grads_between, pieces = call(
         functools.partial(far_kernel, full, tiles),
         (grads, jax.ShapeDtypeStruct((cells_held, 6 * BLOCK), BF16)), [VMEM] * 9,
         (picks, message_far, early, far, far_late, constant, factor, kept_even, kept_odd),
@@ -628,14 +635,16 @@
         + [pltpu.VMEM((cells_held, 3 * BLOCK), F32)],
         flops=planes * height * 4 * 384 * 256 * 6, size=9 * field_bytes,
     )
-    came_b = along_grp(grads_b, -1, owners)
-    pick = lambda place: call(
-        functools.partial(pick_kernel, place), grads, [VMEM] * 2, (picks, pieces),
+    ends_of = lambda source, target: [((source, r), (target, r)) for r in range(regions)]
+    low, high, between = 0, CORES, 1
+    came_low = send(grads_between, ends_of(low, between))
+    came_high = send(grads_between, ends_of(high, between))
+    pick = lambda own: call(
+        functools.partial(pick_kernel, own), grads, [VMEM] * 2, (picks, pieces),
         flops=slots, size=slots,
     )
-    grads_c = pick(2)
-    grads_a = pick(0)
-    came_c = along_grp(grads_c, -2, owners)
+    came_across = send(pick(False), ends_of(low, high) + ends_of(high, low))
+    grads_a = pick(True)
     contact = call(
         contact_kernel, shaped(3 * tiles, BLOCK), [SMEM] + [VMEM] * 7 + [ANY],
         (
@@ -646,8 +655,11 @@
         flops=60 * 8 * slots, size=4 * 20 * slots,
     )
     return call(
-        final_kernel, shaped(3, slots), [SMEM] + [VMEM] * 9,
-        (count, grads_a, came_c, came_b, weight, contact, grain_vel, vol, drag, cell),
+        final_kernel, shaped(3, slots), [SMEM] + [VMEM] * 10,
+        (
+            count, grads_a, came_across, came_low, came_high, weight, contact, grain_vel, vol, drag,
+            cell,
+        ),
         flops=60 * slots, size=4 * 20 * slots,
     )
 

time: 59.7 us -> 59.3 us (level)
  the two profiles are of different devices: /device:TPU:18 before, /device:TPU:17 now
where the time goes in v18:
time: 59.3 us; the launch traced here: 58.9 us
  starting transfers between devices  24 us (40%)
  Pallas kernels  22.4 us (38%)
  waiting for transfers between devices  10.4 us (18%)
  between operations  1.08 us (2%)
  local copies, waits for them, and re-layouts  0.96 us (2%)
    ppermute x14, starting transfers between devices, send(): return lax.ppermute(value, ('grp', 'reg'), flat)  24 us
    pallas_call x12, Pallas kernels, call(): pl.pallas_call(kernel, out_shape=outs, in_specs=specs, out_specs=jax.tree...  22.4 us
    ppermute x14, waiting for transfers between devices, send(): return lax.ppermute(value, ('grp', 'reg'), flat)  10.4 us
  transfers between devices with their start and end apart: 14, of which 3 were waited for; matrix products, arithmetic and copies ran while one was open for 0% of the time, Pallas kernels for 23%

profile of v18, /device:TPU:17, one launch (start us, length us, event | category | flops | bytes accessed | tf_op | source)
XLA Modules:
  0.0 58.9 jit_solution(836399947344045953)
XLA Ops:
  0.0 2.6 %shard_map.137 = (f32[5,72,512]{2,1,0:T(8,128)}, f32[3,72,512]{2,1,0:T(8,128)}, f32[72,512]{1,0:T(8,128)}, f32[72,512]{1,0:T(8,128)}) custom-call(f32[4,128,512]{2,1,0:T(8,128)} %pressure_old.1, f32[4,128,512]{2,1,0:T(8,128)} %source.1, f32[4,128,512]{2,1,0:T(8,128)} %solid_before.1), custom_call_target="tpu_custom_call" | custom-call | flops 589824 | bytes 3538944 | tf_op jit(solution)/shard_map/pallas_call | solution.py:36
  2.7 3.9 %collective-permute-start.2 = (f32[5,72,512]{2,1,0:T(8,128)}, f32[5,72,512]{2,1,0:T(8,128)S(1)}, u32[]{:S(2)}, u32[]{:S(2)}) collective-permute-start(f32[5,72,512]{2,1,0:T(8,128)} %get-tuple-element.30.early.pressure), channel_id=1, source_target_pairs={{8,1},{9,0},{10,3},{11,2},{12,5},{13,4},{14,7},{15,6},{24,17},{25,... | collective-permute-start | bytes 2211848 | tf_op jit(solution)/shard_map/ppermute | solution.py:542
  6.5 1.3 %collective-permute-start.3 = (f32[72,512]{1,0:T(8,128)}, f32[72,512]{1,0:T(8,128)S(1)}, u32[]{:S(2)}, u32[]{:S(2)}) collective-permute-start(f32[72,512]{1,0:T(8,128)} %get-tuple-element.38), channel_id=1, source_target_pairs={{9,3},{10,0},{11,5},{12,2},{13,7},{14,4},{25,19},{26,16},{27,21},{... | collective-permute-start | bytes 442376 | tf_op jit(solution)/shard_map/ppermute | solution.py:542
  8.5 1.7 %shard_map.136 = (f32[136,256]{1,0:T(8,128)S(1)}, f32[8,128]{1,0:T(8,128)S(1)}) custom-call(s32[1]{0:T(128)S(6)} %copy.15.count, s32[128,128]{1,0:T(8,128)S(1)} %bitcast.4, f32[128,128]{1,0:T(8,128)S(1)} %bitcast.6, f32[128,128]{1,0:T(8,128)S(1)} %bitcast.8, s32[1,128]{1,0:T(1,128)S(1)} %bitcast.10), custom_call_target="tpu_custom_call" | custom-call | flops 201326592 | bytes 327680 | tf_op jit(solution)/shard_map/pallas_call | solution.py:36
  10.2 1.9 %collective-permute-start.1 = (f32[136,256]{1,0:T(8,128)S(1)}, f32[136,256]{1,0:T(8,128)S(1)}, u32[]{:S(2)}, u32[]{:S(2)}) collective-permute-start(f32[136,256]{1,0:T(8,128)S(1)} %get-tuple-element.29.mine), channel_id=1, source_target_pairs={{0,16},{1,17},{2,18},{3,19},{4,20},{5,21},{6,22},{7,23},{8,0},{9,1... | collective-permute-start | bytes 417800 | tf_op jit(solution)/shard_map/ppermute | solution.py:542
  12.2 3.6 %collective-permute-start = (f32[136,256]{1,0:T(8,128)S(1)}, f32[136,256]{1,0:T(8,128)S(1)}, u32[]{:S(2)}, u32[]{:S(2)}) collective-permute-start(f32[136,256]{1,0:T(8,128)S(1)} %get-tuple-element.29.mine), channel_id=1, source_target_pairs={{0,8},{1,9},{2,10},{3,11},{4,12},{5,13},{6,14},{7,15},{8,16},{9,17... | collective-permute-start | bytes 417800 | tf_op jit(solution)/shard_map/ppermute | solution.py:542
  15.8 1.8 %collective-permute-start.8 = (f32[3,72,512]{2,1,0:T(8,128)}, f32[3,72,512]{2,1,0:T(8,128)S(1)}, u32[]{:S(2)}, u32[]{:S(2)}) collective-permute-start(f32[3,72,512]{2,1,0:T(8,128)} %get-tuple-element.31.late), channel_id=1, source_target_pairs={{8,1},{9,0},{10,3},{11,2},{12,5},{13,4},{14,7},{15,6},{24,17},{25,... | collective-permute-start | bytes 1327112 | tf_op jit(solution)/shard_map/ppermute | solution.py:542
  17.7 0.9 %copy-done.5 = f32[72,512]{1,0:T(8,128)S(1)} copy-done((f32[72,512]{1,0:T(8,128)S(1)}, f32[72,512]{1,0:T(8,128)}, u32[]{:S(2)}) %copy-start.5) | copy-done | bytes 147480
  18.6 3.2 %shard_map.138 = (f32[384,128]{1,0:T(8,128)S(1)}, f32[96,128]{1,0:T(8,128)S(1)}, f32[96,128]{1,0:T(8,128)S(1)}, f32[8,128]{1,0:T(8,128)S(1)}, f32[72,512]{1,0:T(8,128)S(1)}) custom-call(f32[3,16384]{1,0:T(4,128)S(1)} %copy-done.4, f32[3,16384]{1,0:T(4,128)S(1)} %copy-done.1, s32[2,4096]{1,0:T(2,128)S(1)} %copy-done.9, f32[8,128]{1,0:T(8,128)S(1)} %get-tuple-element.32._, ...), custom_call_target="tpu_custom_call" | custom-call | flops 16384 | bytes 786432 | tf_op jit(solution)/shard_map/pallas_call | solution.py:36
  21.9 0.7 %collective-permute-start.7 = (f32[6,72,512]{2,1,0:T(8,128)S(1)}, f32[6,72,512]{2,1,0:T(8,128)S(1)}, u32[]{:S(2)}, u32[]{:S(2)}) collective-permute-start(f32[6,72,512]{2,1,0:T(8,128)S(1)} %get-tuple-element.43), channel_id=1, source_target_pairs={{0,2},{2,4},{3,1},{4,6},{5,3},{7,5},{16,18},{18,20},{19,17},{20,22... | collective-permute-start | bytes 2654216 | tf_op jit(solution)/shard_map/ppermute | solution.py:542
  22.7 0.7 %collective-permute-start.10 = (f32[456,256]{1,0:T(8,128)S(1)}, f32[456,256]{1,0:T(8,128)S(1)}, u32[]{:S(2)}, u32[]{:S(2)}) collective-permute-start(f32[456,256]{1,0:T(8,128)S(1)} %get-tuple-element.46), channel_id=1, source_target_pairs={{0,1},{1,0},{2,3},{3,2},{4,5},{5,4},{6,7},{7,6},{16,17},{17,16},{1... | collective-permute-start | bytes 1400840 | tf_op jit(solution)/shard_map/ppermute | solution.py:542
  24.8 2.6 %collective-permute-start.4 = (f32[96,128]{1,0:T(8,128)S(1)}, f32[96,128]{1,0:T(8,128)S(1)}, u32[]{:S(2)}, u32[]{:S(2)}) collective-permute-start(f32[96,128]{1,0:T(8,128)S(1)} %get-tuple-element.34.halo_near), channel_id=1, source_target_pairs={{8,9},{9,8},{10,11},{11,10},{12,13},{13,12},{14,15},{15,14}} | collective-permute-start | bytes 147464 | tf_op jit(solution)/shard_map/ppermute | solution.py:542
  27.4 3.0 %collective-permute-done.4._near.halo_near = f32[96,128]{1,0:T(8,128)S(1)} collective-permute-done((f32[96,128]{1,0:T(8,128)S(1)}, f32[96,128]{1,0:T(8,128)S(1)}, u32[]{:S(2)}, u32[]{:S(2)}) %collective-permute-start.4) | collective-permute-done | bytes 49184 | tf_op jit(solution)/shard_map/ppermute | solution.py:542
  30.4 2.6 %collective-permute-start.5 = (f32[96,128]{1,0:T(8,128)S(1)}, f32[96,128]{1,0:T(8,128)S(1)}, u32[]{:S(2)}, u32[]{:S(2)}) collective-permute-start(f32[96,128]{1,0:T(8,128)S(1)} %get-tuple-element.35.halo_far), channel_id=1, source_target_pairs={{9,10},{10,9},{11,12},{12,11},{13,14},{14,13}} | collective-permute-start | bytes 147464 | tf_op jit(solution)/shard_map/ppermute | solution.py:542
  33.0 4.0 %collective-permute-done.5._far.halo_far = f32[96,128]{1,0:T(8,128)S(1)} collective-permute-done((f32[96,128]{1,0:T(8,128)S(1)}, f32[96,128]{1,0:T(8,128)S(1)}, u32[]{:S(2)}, u32[]{:S(2)}) %collective-permute-start.5) | collective-permute-done | bytes 49184 | tf_op jit(solution)/shard_map/ppermute | solution.py:542
  37.0 1.9 %shard_map.141 = (f32[4,72,512]{2,1,0:T(8,128)S(1)}, f32[4,72,512]{2,1,0:T(8,128)S(1)}, f32[128,128]{1,0:T(8,128)S(1)}, bf16[384,1152]{1,0:T(8,128)(2,1)S(1)}) custom-call(f32[136,256]{1,0:T(8,128)S(1)} %get-tuple-element.29.mine, f32[136,256]{1,0:T(8,128)S(1)} %collective-permute-done._second.second, f32[136,256]{1,0:T(8,128)S(1)} %collective-permute-done.1._third.third, ...), custom_call_target="tpu_custom_call" | custom-call | flops 679477248 | bytes 5308416 | tf_op jit(solution)/shard_map/pallas_call | solution.py:36
  39.0 3.3 %shard_map.142 = (f32[4,72,512]{2,1,0:T(8,128)S(1)}, f32[4,72,512]{2,1,0:T(8,128)S(1)}) custom-call(f32[456,256]{1,0:T(8,128)S(1)} %collective-permute-done.10.message.message_near, f32[5,72,512]{2,1,0:T(8,128)S(1)} %copy-done, f32[5,72,512]{2,1,0:T(8,128)S(1)} %collective-permute-done.2.near, f32[3,72,512]{2,1,0:T(8,128)S(1)} %collective-permute-done.8.near_late, ...), custom_call_target="tpu_custom_call" | custom-call | flops 679477248 | bytes 5308416 | tf_op jit(solution)/shard_map/pallas_call | solution.py:36
  42.3 4.7 %shard_map.143 = (f32[128,384]{1,0:T(8,128)S(1)}, bf16[1152,768]{1,0:T(8,128)(2,1)S(1)}) custom-call(bf16[384,1152]{1,0:T(8,128)(2,1)S(1)} %get-tuple-element.41.picks, f32[456,256]{1,0:T(8,128)S(1)} %collective-permute-done.6.message.message_far, f32[5,72,512]{2,1,0:T(8,128)S(1)} %copy-done, f32[6,72,512]{2,1,0:T(8,128)S(1)} %collective-permute-done.7.far, ...), custom_call_target="tpu_custom_call" | custom-call | flops 679477248 | bytes 5308416 | tf_op jit(solution)/shard_map/pallas_call | solution.py:36
  47.5 0.8 %collective-permute-start.11 = (f32[128,384]{1,0:T(8,128)S(1)}, f32[128,384]{1,0:T(8,128)S(1)}, u32[]{:S(2)}, u32[]{:S(2)}) collective-permute-start(f32[128,384]{1,0:T(8,128)S(1)} %shard_map.145), channel_id=1, source_target_pairs={{0,16},{1,17},{2,18},{3,19},{4,20},{5,21},{6,22},{7,23},{16,0},{17... | collective-permute-start | bytes 589832 | tf_op jit(solution)/shard_map/ppermute | solution.py:542
  48.3 1.3 %collective-permute-start.13 = (f32[128,384]{1,0:T(8,128)S(1)}, f32[128,384]{1,0:T(8,128)S(1)}, u32[]{:S(2)}, u32[]{:S(2)}) collective-permute-start(f32[128,384]{1,0:T(8,128)S(1)} %get-tuple-element.50), channel_id=1, source_target_pairs={{16,8},{17,9},{18,10},{19,11},{20,12},{21,13},{22,14},{23,15}} | collective-permute-start | bytes 589832 | tf_op jit(solution)/shard_map/ppermute | solution.py:542
  49.6 1.3 %collective-permute-start.12 = (f32[128,384]{1,0:T(8,128)S(1)}, f32[128,384]{1,0:T(8,128)S(1)}, u32[]{:S(2)}, u32[]{:S(2)}) collective-permute-start(f32[128,384]{1,0:T(8,128)S(1)} %get-tuple-element.50), channel_id=1, source_target_pairs={{0,8},{1,9},{2,10},{3,11},{4,12},{5,13},{6,14},{7,15}} | collective-permute-start | bytes 589832 | tf_op jit(solution)/shard_map/ppermute | solution.py:542
  51.4 3.0 %shard_map.146.contact = f32[384,128]{1,0:T(8,128)S(1)} custom-call(s32[128]{0:T(128)S(1)} %copy-done.10, f32[384,128]{1,0:T(8,128)S(1)} %get-tuple-element.52.state, f32[456,256]{1,0:T(8,128)S(1)} %collective-permute-done.10.message.message_near, f32[456,256]{1,0:T(8,128)S(1)} %collective-permute-done.6.message.message_far, ...), custom_call_target="tpu_custom_call" | custom-call | flops 7864320 | bytes 1310720 | tf_op jit(solution)/shard_map/pallas_call | solution.py:36
  54.4 3.4 %collective-permute-done.13.grads_d = f32[128,384]{1,0:T(8,128)S(1)} collective-permute-done((f32[128,384]{1,0:T(8,128)S(1)}, f32[128,384]{1,0:T(8,128)S(1)}, u32[]{:S(2)}, u32[]{:S(2)}) %collective-permute-start.13) | collective-permute-done | bytes 196640 | tf_op jit(solution)/shard_map/ppermute | solution.py:542
  57.8 1.0 %shard_map.147 = f32[3,16384]{1,0:T(4,128)} custom-call(s32[1]{0:T(128)S(6)} %copy.15.count, f32[128,384]{1,0:T(8,128)S(1)} %shard_map.144._.grads_a, f32[128,384]{1,0:T(8,128)S(1)} %collective-permute-done.11.grads_b, f32[128,384]{1,0:T(8,128)S(1)} %collective-permute-done.12.grads_c, f32[128,384]{1,0:T(8,128)S(1)} %collective-permute-done.13.grads_d, ...), custom_call_target="tpu_custom_call" | custom-call | flops 983040 | bytes 1310720 | tf_op jit(solution)/shard_map/pallas_call | solution.py:36
  (42 shorter events, 2.4 us)
Async XLA Ops:
  0.0 8.5 %copy-start.12 = (s32[128]{0:T(128)S(1)}, s32[128]{0:T(128)}, u32[]{:S(2)}) copy-start(s32[128]{0:T(128)} %param.24) | copy-start | bytes 1540
  0.0 8.5 %copy-start.6 = (s32[16384]{0:T(1024)S(1)}, s32[16384]{0:T(1024)}, u32[]{:S(2)}) copy-start(s32[16384]{0:T(1024)} %param.23) | copy-start | bytes 196612
  0.0 8.5 %copy-start.8 = (f32[16384]{0:T(1024)S(1)}, f32[16384]{0:T(1024)}, u32[]{:S(2)}) copy-start(f32[16384]{0:T(1024)} %param.17) | copy-start | bytes 196612
  0.0 8.5 %copy-start.7 = (f32[16384]{0:T(1024)S(1)}, f32[16384]{0:T(1024)}, u32[]{:S(2)}) copy-start(f32[16384]{0:T(1024)} %param.16) | copy-start | bytes 196612
  0.0 17.6 %copy-start.1 = (f32[3,16384]{1,0:T(4,128)S(1)}, f32[3,16384]{1,0:T(4,128)}, u32[]{:S(2)}) copy-start(f32[3,16384]{1,0:T(4,128)} %vel.3) | copy-start | bytes 589828
  0.0 17.6 %copy-start.9 = (s32[2,4096]{1,0:T(2,128)S(1)}, s32[2,4096]{1,0:T(2,128)}, u32[]{:S(2)}) copy-start(s32[2,4096]{1,0:T(2,128)} %lists.1) | copy-start | bytes 98308
  0.0 17.6 %copy-start.4 = (f32[3,16384]{1,0:T(4,128)S(1)}, f32[3,16384]{1,0:T(4,128)}, u32[]{:S(2)}) copy-start(f32[3,16384]{1,0:T(4,128)} %pos.1) | copy-start | bytes 589828
  2.6 34.4 %copy-start = (f32[5,72,512]{2,1,0:T(8,128)S(1)}, f32[5,72,512]{2,1,0:T(8,128)}, u32[]{:S(2)}) copy-start(f32[5,72,512]{2,1,0:T(8,128)} %get-tuple-element.30.early.pressure) | copy-start | bytes 2211844
  2.6 34.4 %copy-start.10 = (s32[128]{0:T(128)S(1)}, s32[128]{0:T(128)}, u32[]{:S(2)}) copy-start(s32[128]{0:T(128)} %partner.1) | copy-start | bytes 1540
  2.7 19.2 %collective-permute-start.2 = (f32[5,72,512]{2,1,0:T(8,128)}, f32[5,72,512]{2,1,0:T(8,128)S(1)}, u32[]{:S(2)}, u32[]{:S(2)}) collective-permute-start(f32[5,72,512]{2,1,0:T(8,128)} %get-tuple-element.30.early.pressure), channel_id=1, source_target_pairs={{8,1},{9,0},{10,3},{11,2},{12,5},{13,4},{14,7},{15,6},{24,17},{25,... | collective-permute-start | bytes 2211848 | tf_op jit(solution)/shard_map/ppermute | solution.py:542
  6.5 15.3 %collective-permute-start.3 = (f32[72,512]{1,0:T(8,128)}, f32[72,512]{1,0:T(8,128)S(1)}, u32[]{:S(2)}, u32[]{:S(2)}) collective-permute-start(f32[72,512]{1,0:T(8,128)} %get-tuple-element.38), channel_id=1, source_target_pairs={{9,3},{10,0},{11,5},{12,2},{13,7},{14,4},{25,19},{26,16},{27,21},{... | collective-permute-start | bytes 442376 | tf_op jit(solution)/shard_map/ppermute | solution.py:542
  10.2 11.6 %collective-permute-start.1 = (f32[136,256]{1,0:T(8,128)S(1)}, f32[136,256]{1,0:T(8,128)S(1)}, u32[]{:S(2)}, u32[]{:S(2)}) collective-permute-start(f32[136,256]{1,0:T(8,128)S(1)} %get-tuple-element.29.mine), channel_id=1, source_target_pairs={{0,16},{1,17},{2,18},{3,19},{4,20},{5,21},{6,22},{7,23},{8,0},{9,1... | collective-permute-start | bytes 417800 | tf_op jit(solution)/shard_map/ppermute | solution.py:542
  12.2 9.6 %collective-permute-start = (f32[136,256]{1,0:T(8,128)S(1)}, f32[136,256]{1,0:T(8,128)S(1)}, u32[]{:S(2)}, u32[]{:S(2)}) collective-permute-start(f32[136,256]{1,0:T(8,128)S(1)} %get-tuple-element.29.mine), channel_id=1, source_target_pairs={{0,8},{1,9},{2,10},{3,11},{4,12},{5,13},{6,14},{7,15},{8,16},{9,17... | collective-permute-start | bytes 417800 | tf_op jit(solution)/shard_map/ppermute | solution.py:542
  15.8 8.3 %collective-permute-start.8 = (f32[3,72,512]{2,1,0:T(8,128)}, f32[3,72,512]{2,1,0:T(8,128)S(1)}, u32[]{:S(2)}, u32[]{:S(2)}) collective-permute-start(f32[3,72,512]{2,1,0:T(8,128)} %get-tuple-element.31.late), channel_id=1, source_target_pairs={{8,1},{9,0},{10,3},{11,2},{12,5},{13,4},{14,7},{15,6},{24,17},{25,... | collective-permute-start | bytes 1327112 | tf_op jit(solution)/shard_map/ppermute | solution.py:542
  18.6 18.4 %copy-start.11 = (f32[3,72,512]{2,1,0:T(8,128)S(1)}, f32[3,72,512]{2,1,0:T(8,128)}, u32[]{:S(2)}) copy-start(f32[3,72,512]{2,1,0:T(8,128)} %get-tuple-element.31.late) | copy-start | bytes 1327108
  21.9 20.4 %collective-permute-start.7 = (f32[6,72,512]{2,1,0:T(8,128)S(1)}, f32[6,72,512]{2,1,0:T(8,128)S(1)}, u32[]{:S(2)}, u32[]{:S(2)}) collective-permute-start(f32[6,72,512]{2,1,0:T(8,128)S(1)} %get-tuple-element.43), channel_id=1, source_target_pairs={{0,2},{2,4},{3,1},{4,6},{5,3},{7,5},{16,18},{18,20},{19,17},{20,22... | collective-permute-start | bytes 2654216 | tf_op jit(solution)/shard_map/ppermute | solution.py:542
  22.7 16.3 %collective-permute-start.10 = (f32[456,256]{1,0:T(8,128)S(1)}, f32[456,256]{1,0:T(8,128)S(1)}, u32[]{:S(2)}, u32[]{:S(2)}) collective-permute-start(f32[456,256]{1,0:T(8,128)S(1)} %get-tuple-element.46), channel_id=1, source_target_pairs={{0,1},{1,0},{2,3},{3,2},{4,5},{5,4},{6,7},{7,6},{16,17},{17,16},{1... | collective-permute-start | bytes 1400840 | tf_op jit(solution)/shard_map/ppermute | solution.py:542
  23.4 18.9 %collective-permute-start.6 = (f32[456,256]{1,0:T(8,128)S(1)}, f32[456,256]{1,0:T(8,128)S(1)}, u32[]{:S(2)}, u32[]{:S(2)}) collective-permute-start(f32[456,256]{1,0:T(8,128)S(1)} %get-tuple-element.42), channel_id=1, source_target_pairs={{1,2},{2,1},{3,4},{4,3},{5,6},{6,5},{17,18},{18,17},{19,20},{20,19... | collective-permute-start | bytes 1400840 | tf_op jit(solution)/shard_map/ppermute | solution.py:542
  24.1 18.1 %collective-permute-start.9 = (f32[3,72,512]{2,1,0:T(8,128)S(1)}, f32[3,72,512]{2,1,0:T(8,128)S(1)}, u32[]{:S(2)}, u32[]{:S(2)}) collective-permute-start(f32[3,72,512]{2,1,0:T(8,128)S(1)} %collective-permute-done.8.near_late), channel_id=1, source_target_pairs={{0,2},{2,4},{3,1},{4,6},{5,3},{7,5},{16,18},{18,20},{19,17},{20,22... | collective-permute-start | bytes 1327112 | tf_op jit(solution)/shard_map/ppermute | solution.py:542
  24.8 5.6 %collective-permute-start.4 = (f32[96,128]{1,0:T(8,128)S(1)}, f32[96,128]{1,0:T(8,128)S(1)}, u32[]{:S(2)}, u32[]{:S(2)}) collective-permute-start(f32[96,128]{1,0:T(8,128)S(1)} %get-tuple-element.34.halo_near), channel_id=1, source_target_pairs={{8,9},{9,8},{10,11},{11,10},{12,13},{13,12},{14,15},{15,14}} | collective-permute-start | bytes 147464 | tf_op jit(solution)/shard_map/ppermute | solution.py:542
  30.4 6.6 %collective-permute-start.5 = (f32[96,128]{1,0:T(8,128)S(1)}, f32[96,128]{1,0:T(8,128)S(1)}, u32[]{:S(2)}, u32[]{:S(2)}) collective-permute-start(f32[96,128]{1,0:T(8,128)S(1)} %get-tuple-element.35.halo_far), channel_id=1, source_target_pairs={{9,10},{10,9},{11,12},{12,11},{13,14},{14,13}} | collective-permute-start | bytes 147464 | tf_op jit(solution)/shard_map/ppermute | solution.py:542
  47.5 6.9 %collective-permute-start.11 = (f32[128,384]{1,0:T(8,128)S(1)}, f32[128,384]{1,0:T(8,128)S(1)}, u32[]{:S(2)}, u32[]{:S(2)}) collective-permute-start(f32[128,384]{1,0:T(8,128)S(1)} %shard_map.145), channel_id=1, source_target_pairs={{0,16},{1,17},{2,18},{3,19},{4,20},{5,21},{6,22},{7,23},{16,0},{17... | collective-permute-start | bytes 589832 | tf_op jit(solution)/shard_map/ppermute | solution.py:542
  48.3 9.5 %collective-permute-start.13 = (f32[128,384]{1,0:T(8,128)S(1)}, f32[128,384]{1,0:T(8,128)S(1)}, u32[]{:S(2)}, u32[]{:S(2)}) collective-permute-start(f32[128,384]{1,0:T(8,128)S(1)} %get-tuple-element.50), channel_id=1, source_target_pairs={{16,8},{17,9},{18,10},{19,11},{20,12},{21,13},{22,14},{23,15}} | collective-permute-start | bytes 589832 | tf_op jit(solution)/shard_map/ppermute | solution.py:542
  49.6 8.2 %collective-permute-start.12 = (f32[128,384]{1,0:T(8,128)S(1)}, f32[128,384]{1,0:T(8,128)S(1)}, u32[]{:S(2)}, u32[]{:S(2)}) collective-permute-start(f32[128,384]{1,0:T(8,128)S(1)} %get-tuple-element.50), channel_id=1, source_target_pairs={{0,8},{1,9},{2,10},{3,11},{4,12},{5,13},{6,14},{7,15}} | collective-permute-start | bytes 589832 | tf_op jit(solution)/shard_map/ppermute | solution.py:542
  (3 other events, 8.7 us)

commit v19 on v18

--- a/solution.py
+++ b/solution.py
@@ -108,11 +108,9 @@
         one.wait()
 
 
-def forward_kernel(near, inner, _halo, _second, _third, _beyond, out, dummy):
+def forward_kernel(near, _halo, _second, _third, _beyond, out, dummy):
     dummy[...] = jnp.zeros(dummy.shape, F32)
-    count = near.shape[0]
-    out[:count] = near[...]
-    out[count] = inner[...]
+    out[...] = near[...]
 
 
 def deposit_kernel(count, cell, vol, drag, ids, out, dummy):
@@ -163,8 +161,7 @@
     out[tiles : tiles + SUB, BLOCK:] = jnp.zeros((SUB, BLOCK), F32)
 
 
-def halo_kernel(pos, vel, lists, _, inner, state, near, far, dummy, held):
-    held[...] = inner[...]
+def halo_kernel(pos, vel, lists, _, state, near, far, dummy):
     dummy[...] = jnp.zeros(dummy.shape, F32)
     tiles = pos.shape[1] // BLOCK
     rows = lists.shape[1] // BLOCK
@@ -418,7 +415,7 @@
 
 
 def far_kernel(
-    full, tiles, picks, message, pressure, far, far_late, own_constant, own_factor, kept_even, kept_odd,
+    full, tiles, picks, message, pressure, far, far_late, outer, own_constant, own_factor, kept_even, kept_odd,
     out, pieces, constant, factor, old, new, fields,
 ):
     planes, height, width = own_constant.shape
@@ -435,7 +432,7 @@
     for x in range(planes):
         at = jnp.where(place.even, planes - 1 - x, x)
         old[rim + planes + x] = far[at]
-    old[rim + 2 * planes] = far[planes + HEAD]
+    old[rim + 2 * planes] = outer[...]
     buffers = (old, new)
     edge = rim + planes
     for index in range(planes):
@@ -586,20 +583,21 @@
     third = along_grp(mine, 2, holders)
     rows = halo_list.shape[1] // BLOCK
     halo = shaped(3 * rows, BLOCK)
-    state, halo_near, halo_far, after_halo, inner = call(
-        halo_kernel, (shaped(3 * tiles, BLOCK), halo, halo, small, plane),
-        [VMEM] * 5, (grain_pos, grain_vel, halo_list, after_deposit, inner), flops=slots,
+    state, halo_near, halo_far, after_halo = call(
+        halo_kernel, (shaped(3 * tiles, BLOCK), halo, halo, small),
+        [VMEM] * 4, (grain_pos, grain_vel, halo_list, after_deposit), flops=slots,
         size=4 * 4 * 3 * slots,
     )
     others = [g for g in holders if g not in owners]
     came_near = along_reg(halo_near, others, (1, -1))
     came_far = along_reg(halo_far, others, (-1, 1))
     far, after_forward = call(
-        forward_kernel, (shaped(planes + HEAD + 1, height, width), small), [VMEM] * 6,
-        (near, inner, after_halo, second, third, beyond), size=5 * field_bytes,
+        forward_kernel, (shaped(planes + HEAD, height, width), small), [VMEM] * 5,
+        (near, after_halo, second, third, beyond), size=5 * field_bytes,
     )
     far = along_reg(far, owners, (2, -2))
     far_late = along_reg(near_late, owners, (2, -2))
+    outer = along_reg(inner, owners, (2, -2), core=1)
     message = shaped(holding * (tiles + SUB) + 3 * rows // 2, 2 * BLOCK)
     message_near, message_far, after_message = call(
         message_kernel, (message, message, small), [VMEM] * 6,
@@ -628,8 +626,8 @@
     cells_held = planes * height * width // BLOCK
     grads_between, pieces = call(
         functools.partial(far_kernel, full, tiles),
-        (grads, jax.ShapeDtypeStruct((cells_held, 6 * BLOCK), BF16)), [VMEM] * 9,
-        (picks, message_far, early, far, far_late, constant, factor, kept_even, kept_odd),
+        (grads, jax.ShapeDtypeStruct((cells_held, 6 * BLOCK), BF16)), [VMEM] * 10,
+        (picks, message_far, early, far, far_late, outer, constant, factor, kept_even, kept_odd),
         [window_of(planes)] * 2
         + [window_of(3 * planes + 2)] * 2
         + [pltpu.VMEM((cells_held, 3 * BLOCK), F32)],

time: 59.3 us -> 59.3 us (level)
  the two profiles are of different devices: /device:TPU:17 before, /device:TPU:0 now
where the time goes in v19:
time: 59.3 us; the launch traced here: 58.3 us
  starting transfers between devices  32.3 us (54%)
  Pallas kernels  22.5 us (38%)
  waiting for transfers between devices  2.36 us (4%)
  between operations  1.11 us (2%)
    ppermute x15, starting transfers between devices, send(): return lax.ppermute(value, ('grp', 'reg'), flat)  32.3 us
    pallas_call x12, Pallas kernels, call(): pl.pallas_call(kernel, out_shape=outs, in_specs=specs, out_specs=jax.tree...  22.5 us
    ppermute x15, waiting for transfers between devices, send(): return lax.ppermute(value, ('grp', 'reg'), flat)  2.36 us
  transfers between devices with their start and end apart: 15, of which 2 were waited for; matrix products, arithmetic and copies ran while one was open for 0% of the time, Pallas kernels for 23%

profile of v19, /device:TPU:0, one launch (start us, length us, event | category | flops | bytes accessed | tf_op | source)
XLA Modules:
  0.0 58.3 jit_solution(18275654436164234213)
XLA Ops:
  0.0 2.6 %shard_map.137 = (f32[5,72,512]{2,1,0:T(8,128)}, f32[3,72,512]{2,1,0:T(8,128)}, f32[72,512]{1,0:T(8,128)}, f32[72,512]{1,0:T(8,128)}) custom-call(f32[4,128,512]{2,1,0:T(8,128)} %pressure_old.1, f32[4,128,512]{2,1,0:T(8,128)} %source.1, f32[4,128,512]{2,1,0:T(8,128)} %solid_before.1), custom_call_target="tpu_custom_call" | custom-call | flops 589824 | bytes 3538944 | tf_op jit(solution)/shard_map/pallas_call | solution.py:36
  2.6 1.4 %collective-permute-start.2 = (f32[5,72,512]{2,1,0:T(8,128)}, f32[5,72,512]{2,1,0:T(8,128)S(1)}, u32[]{:S(2)}, u32[]{:S(2)}) collective-permute-start(f32[5,72,512]{2,1,0:T(8,128)} %get-tuple-element.29.early.pressure), channel_id=1, source_target_pairs={{8,1},{9,0},{10,3},{11,2},{12,5},{13,4},{14,7},{15,6},{24,17},{25,... | collective-permute-start | bytes 2211848 | tf_op jit(solution)/shard_map/ppermute | solution.py:539
  4.1 1.3 %collective-permute-start.3 = (f32[72,512]{1,0:T(8,128)}, f32[72,512]{1,0:T(8,128)S(1)}, u32[]{:S(2)}, u32[]{:S(2)}) collective-permute-start(f32[72,512]{1,0:T(8,128)} %get-tuple-element.35), channel_id=1, source_target_pairs={{9,3},{10,0},{11,5},{12,2},{13,7},{14,4},{25,19},{26,16},{27,21},{... | collective-permute-start | bytes 442376 | tf_op jit(solution)/shard_map/ppermute | solution.py:539
  5.4 1.3 %collective-permute-start.8 = (f32[3,72,512]{2,1,0:T(8,128)}, f32[3,72,512]{2,1,0:T(8,128)S(1)}, u32[]{:S(2)}, u32[]{:S(2)}) collective-permute-start(f32[3,72,512]{2,1,0:T(8,128)} %get-tuple-element.30.late), channel_id=1, source_target_pairs={{8,1},{9,0},{10,3},{11,2},{12,5},{13,4},{14,7},{15,6},{24,17},{25,... | collective-permute-start | bytes 1327112 | tf_op jit(solution)/shard_map/ppermute | solution.py:539
  7.4 1.7 %shard_map.136 = (f32[136,256]{1,0:T(8,128)S(1)}, f32[8,128]{1,0:T(8,128)S(1)}) custom-call(s32[1]{0:T(128)S(6)} %copy.15.count, s32[128,128]{1,0:T(8,128)S(1)} %bitcast.4, f32[128,128]{1,0:T(8,128)S(1)} %bitcast.6, f32[128,128]{1,0:T(8,128)S(1)} %bitcast.8, s32[1,128]{1,0:T(1,128)S(1)} %bitcast.10), custom_call_target="tpu_custom_call" | custom-call | flops 201326592 | bytes 327680 | tf_op jit(solution)/shard_map/pallas_call | solution.py:36
  9.1 4.9 %collective-permute-start.1 = (f32[136,256]{1,0:T(8,128)S(1)}, f32[136,256]{1,0:T(8,128)S(1)}, u32[]{:S(2)}, u32[]{:S(2)}) collective-permute-start(f32[136,256]{1,0:T(8,128)S(1)} %get-tuple-element.28.mine), channel_id=1, source_target_pairs={{0,16},{1,17},{2,18},{3,19},{4,20},{5,21},{6,22},{7,23},{8,0},{9,1... | collective-permute-start | bytes 417800 | tf_op jit(solution)/shard_map/ppermute | solution.py:539
  13.9 2.1 %collective-permute-start = (f32[136,256]{1,0:T(8,128)S(1)}, f32[136,256]{1,0:T(8,128)S(1)}, u32[]{:S(2)}, u32[]{:S(2)}) collective-permute-start(f32[136,256]{1,0:T(8,128)S(1)} %get-tuple-element.28.mine), channel_id=1, source_target_pairs={{0,8},{1,9},{2,10},{3,11},{4,12},{5,13},{6,14},{7,15},{8,16},{9,17... | collective-permute-start | bytes 417800 | tf_op jit(solution)/shard_map/ppermute | solution.py:539
  16.1 3.2 %shard_map.138 = (f32[384,128]{1,0:T(8,128)S(1)}, f32[96,128]{1,0:T(8,128)S(1)}, f32[96,128]{1,0:T(8,128)S(1)}, f32[8,128]{1,0:T(8,128)S(1)}) custom-call(f32[3,16384]{1,0:T(4,128)S(1)} %copy-done.4, f32[3,16384]{1,0:T(4,128)S(1)} %copy-done.1, s32[2,4096]{1,0:T(2,128)S(1)} %copy-done.8, f32[8,128]{1,0:T(8,128)S(1)} %get-tuple-element.31._), custom_call_target="tpu_custom_call" | custom-call | flops 16384 | bytes 786432 | tf_op jit(solution)/shard_map/pallas_call | solution.py:36
  19.4 1.5 %collective-permute-done._second.second = f32[136,256]{1,0:T(8,128)S(1)} collective-permute-done((f32[136,256]{1,0:T(8,128)S(1)}, f32[136,256]{1,0:T(8,128)S(1)}, u32[]{:S(2)}, u32[]{:S(2)}) %collective-permute-start) | collective-permute-done | bytes 139296 | tf_op jit(solution)/shard_map/ppermute | solution.py:539
  21.0 4.0 %collective-permute-start.7 = (f32[5,72,512]{2,1,0:T(8,128)S(1)}, f32[5,72,512]{2,1,0:T(8,128)S(1)}, u32[]{:S(2)}, u32[]{:S(2)}) collective-permute-start(f32[5,72,512]{2,1,0:T(8,128)S(1)} %get-tuple-element.40), channel_id=1, source_target_pairs={{0,2},{2,4},{3,1},{4,6},{5,3},{7,5},{16,18},{18,20},{19,17},{20,22... | collective-permute-start | bytes 2211848 | tf_op jit(solution)/shard_map/ppermute | solution.py:539
  25.0 1.9 %collective-permute-start.11 = (f32[456,256]{1,0:T(8,128)S(1)}, f32[456,256]{1,0:T(8,128)S(1)}, u32[]{:S(2)}, u32[]{:S(2)}) collective-permute-start(f32[456,256]{1,0:T(8,128)S(1)} %get-tuple-element.44), channel_id=1, source_target_pairs={{0,1},{1,0},{2,3},{3,2},{4,5},{5,4},{6,7},{7,6},{16,17},{17,16},{1... | collective-permute-start | bytes 1400840 | tf_op jit(solution)/shard_map/ppermute | solution.py:539
  26.9 0.7 %collective-permute-start.6 = (f32[456,256]{1,0:T(8,128)S(1)}, f32[456,256]{1,0:T(8,128)S(1)}, u32[]{:S(2)}, u32[]{:S(2)}) collective-permute-start(f32[456,256]{1,0:T(8,128)S(1)} %get-tuple-element.39), channel_id=1, source_target_pairs={{1,2},{2,1},{3,4},{4,3},{5,6},{6,5},{17,18},{18,17},{19,20},{20,19... | collective-permute-start | bytes 1400840 | tf_op jit(solution)/shard_map/ppermute | solution.py:539
  27.6 6.6 %collective-permute-start.9 = (f32[3,72,512]{2,1,0:T(8,128)S(1)}, f32[3,72,512]{2,1,0:T(8,128)S(1)}, u32[]{:S(2)}, u32[]{:S(2)}) collective-permute-start(f32[3,72,512]{2,1,0:T(8,128)S(1)} %collective-permute-done.8.near_late), channel_id=1, source_target_pairs={{0,2},{2,4},{3,1},{4,6},{5,3},{7,5},{16,18},{18,20},{19,17},{20,22... | collective-permute-start | bytes 1327112 | tf_op jit(solution)/shard_map/ppermute | solution.py:539
  34.3 0.7 %collective-permute-start.4 = (f32[96,128]{1,0:T(8,128)S(1)}, f32[96,128]{1,0:T(8,128)S(1)}, u32[]{:S(2)}, u32[]{:S(2)}) collective-permute-start(f32[96,128]{1,0:T(8,128)S(1)} %get-tuple-element.32.halo_near), channel_id=1, source_target_pairs={{8,9},{9,8},{10,11},{11,10},{12,13},{13,12},{14,15},{15,14}} | collective-permute-start | bytes 147464 | tf_op jit(solution)/shard_map/ppermute | solution.py:539
  35.7 0.7 %collective-permute-start.10 = (f32[72,512]{1,0:T(8,128)S(1)}, f32[72,512]{1,0:T(8,128)S(1)}, u32[]{:S(2)}, u32[]{:S(2)}) collective-permute-start(f32[72,512]{1,0:T(8,128)S(1)} %copy-done.12), channel_id=1, source_target_pairs={{8,2},{10,4},{11,1},{12,6},{13,3},{15,5},{24,18},{26,20},{27,17},{... | collective-permute-start | bytes 442376 | tf_op jit(solution)/shard_map/ppermute | solution.py:539
  36.4 1.9 %shard_map.141 = (f32[4,72,512]{2,1,0:T(8,128)S(1)}, f32[4,72,512]{2,1,0:T(8,128)S(1)}, f32[128,128]{1,0:T(8,128)S(1)}, bf16[384,1152]{1,0:T(8,128)(2,1)S(1)}) custom-call(f32[136,256]{1,0:T(8,128)S(1)} %get-tuple-element.28.mine, f32[136,256]{1,0:T(8,128)S(1)} %collective-permute-done._second.second, f32[136,256]{1,0:T(8,128)S(1)} %collective-permute-done.1._third.third, ...), custom_call_target="tpu_custom_call" | custom-call | flops 679477248 | bytes 5308416 | tf_op jit(solution)/shard_map/pallas_call | solution.py:36
  38.3 0.8 %collective-permute-done.11.message.message_near = f32[456,256]{1,0:T(8,128)S(1)} collective-permute-done((f32[456,256]{1,0:T(8,128)S(1)}, f32[456,256]{1,0:T(8,128)S(1)}, u32[]{:S(2)}, u32[]{:S(2)}) %collective-permute-start.11) | collective-permute-done | bytes 466976 | tf_op jit(solution)/shard_map/ppermute | solution.py:539
  39.1 3.3 %shard_map.142 = (f32[4,72,512]{2,1,0:T(8,128)S(1)}, f32[4,72,512]{2,1,0:T(8,128)S(1)}) custom-call(f32[456,256]{1,0:T(8,128)S(1)} %collective-permute-done.11.message.message_near, f32[5,72,512]{2,1,0:T(8,128)S(1)} %copy-done, f32[5,72,512]{2,1,0:T(8,128)S(1)} %collective-permute-done.2.near, f32[3,72,512]{2,1,0:T(8,128)S(1)} %collective-permute-done.8.near_late, ...), custom_call_target="tpu_custom_call" | custom-call | flops 679477248 | bytes 5308416 | tf_op jit(solution)/shard_map/pallas_call | solution.py:36
  42.4 4.7 %shard_map.143 = (f32[128,384]{1,0:T(8,128)S(1)}, bf16[1152,768]{1,0:T(8,128)(2,1)S(1)}) custom-call(bf16[384,1152]{1,0:T(8,128)(2,1)S(1)} %get-tuple-element.38.picks, f32[456,256]{1,0:T(8,128)S(1)} %collective-permute-done.6.message.message_far, f32[5,72,512]{2,1,0:T(8,128)S(1)} %copy-done, f32[5,72,512]{2,1,0:T(8,128)S(1)} %collective-permute-done.7.far, ...), custom_call_target="tpu_custom_call" | custom-call | flops 679477248 | bytes 5308416 | tf_op jit(solution)/shard_map/pallas_call | solution.py:36
  47.6 2.7 %collective-permute-start.12 = (f32[128,384]{1,0:T(8,128)S(1)}, f32[128,384]{1,0:T(8,128)S(1)}, u32[]{:S(2)}, u32[]{:S(2)}) collective-permute-start(f32[128,384]{1,0:T(8,128)S(1)} %shard_map.145), channel_id=1, source_target_pairs={{0,16},{1,17},{2,18},{3,19},{4,20},{5,21},{6,22},{7,23},{16,0},{17... | collective-permute-start | bytes 589832 | tf_op jit(solution)/shard_map/ppermute | solution.py:539
  50.3 0.7 %collective-permute-start.14 = (f32[128,384]{1,0:T(8,128)S(1)}, f32[128,384]{1,0:T(8,128)S(1)}, u32[]{:S(2)}, u32[]{:S(2)}) collective-permute-start(f32[128,384]{1,0:T(8,128)S(1)} %get-tuple-element.48), channel_id=1, source_target_pairs={{16,8},{17,9},{18,10},{19,11},{20,12},{21,13},{22,14},{23,15}} | collective-permute-start | bytes 589832 | tf_op jit(solution)/shard_map/ppermute | solution.py:539
  51.0 2.7 %collective-permute-start.13 = (f32[128,384]{1,0:T(8,128)S(1)}, f32[128,384]{1,0:T(8,128)S(1)}, u32[]{:S(2)}, u32[]{:S(2)}) collective-permute-start(f32[128,384]{1,0:T(8,128)S(1)} %get-tuple-element.48), channel_id=1, source_target_pairs={{0,8},{1,9},{2,10},{3,11},{4,12},{5,13},{6,14},{7,15}} | collective-permute-start | bytes 589832 | tf_op jit(solution)/shard_map/ppermute | solution.py:539
  54.2 3.0 %shard_map.146.contact = f32[384,128]{1,0:T(8,128)S(1)} custom-call(s32[128]{0:T(128)S(1)} %copy-done.9, f32[384,128]{1,0:T(8,128)S(1)} %get-tuple-element.50.state, f32[456,256]{1,0:T(8,128)S(1)} %collective-permute-done.11.message.message_near, f32[456,256]{1,0:T(8,128)S(1)} %collective-permute-done.6.message.message_far, ...), custom_call_target="tpu_custom_call" | custom-call | flops 7864320 | bytes 1310720 | tf_op jit(solution)/shard_map/pallas_call | solution.py:36
  57.3 1.0 %shard_map.147 = f32[3,16384]{1,0:T(4,128)} custom-call(s32[1]{0:T(128)S(6)} %copy.15.count, f32[128,384]{1,0:T(8,128)S(1)} %shard_map.144._.grads_a, f32[128,384]{1,0:T(8,128)S(1)} %collective-permute-done.12.grads_b, f32[128,384]{1,0:T(8,128)S(1)} %collective-permute-done.13.grads_c, f32[128,384]{1,0:T(8,128)S(1)} %collective-permute-done.14.grads_d, ...), custom_call_target="tpu_custom_call" | custom-call | flops 983040 | bytes 1310720 | tf_op jit(solution)/shard_map/pallas_call | solution.py:36
  (44 shorter events, 1.7 us)
Async XLA Ops:
  0.0 7.3 %copy-start.7 = (f32[16384]{0:T(1024)S(1)}, f32[16384]{0:T(1024)}, u32[]{:S(2)}) copy-start(f32[16384]{0:T(1024)} %param.17) | copy-start | bytes 196612
  0.0 7.4 %copy-start.6 = (f32[16384]{0:T(1024)S(1)}, f32[16384]{0:T(1024)}, u32[]{:S(2)}) copy-start(f32[16384]{0:T(1024)} %param.16) | copy-start | bytes 196612
  0.0 16.1 %copy-start.1 = (f32[3,16384]{1,0:T(4,128)S(1)}, f32[3,16384]{1,0:T(4,128)}, u32[]{:S(2)}) copy-start(f32[3,16384]{1,0:T(4,128)} %vel.3) | copy-start | bytes 589828
  0.0 16.1 %copy-start.8 = (s32[2,4096]{1,0:T(2,128)S(1)}, s32[2,4096]{1,0:T(2,128)}, u32[]{:S(2)}) copy-start(s32[2,4096]{1,0:T(2,128)} %lists.1) | copy-start | bytes 98308
  0.0 16.1 %copy-start.4 = (f32[3,16384]{1,0:T(4,128)S(1)}, f32[3,16384]{1,0:T(4,128)}, u32[]{:S(2)}) copy-start(f32[3,16384]{1,0:T(4,128)} %pos.1) | copy-start | bytes 589828
  2.6 33.0 %copy-start.12 = (f32[72,512]{1,0:T(8,128)S(1)}, f32[72,512]{1,0:T(8,128)}, u32[]{:S(2)}) copy-start(f32[72,512]{1,0:T(8,128)} %get-tuple-element.41) | copy-start | bytes 442372
  2.6 33.7 %copy-start = (f32[5,72,512]{2,1,0:T(8,128)S(1)}, f32[5,72,512]{2,1,0:T(8,128)}, u32[]{:S(2)}) copy-start(f32[5,72,512]{2,1,0:T(8,128)} %get-tuple-element.29.early.pressure) | copy-start | bytes 2211844
  2.6 33.7 %copy-start.9 = (s32[128]{0:T(128)S(1)}, s32[128]{0:T(128)}, u32[]{:S(2)}) copy-start(s32[128]{0:T(128)} %partner.1) | copy-start | bytes 1540
  2.6 33.7 %copy-start.10 = (f32[3,72,512]{2,1,0:T(8,128)S(1)}, f32[3,72,512]{2,1,0:T(8,128)}, u32[]{:S(2)}) copy-start(f32[3,72,512]{2,1,0:T(8,128)} %get-tuple-element.30.late) | copy-start | bytes 1327108
  2.6 18.3 %collective-permute-start.2 = (f32[5,72,512]{2,1,0:T(8,128)}, f32[5,72,512]{2,1,0:T(8,128)S(1)}, u32[]{:S(2)}, u32[]{:S(2)}) collective-permute-start(f32[5,72,512]{2,1,0:T(8,128)} %get-tuple-element.29.early.pressure), channel_id=1, source_target_pairs={{8,1},{9,0},{10,3},{11,2},{12,5},{13,4},{14,7},{15,6},{24,17},{25,... | collective-permute-start | bytes 2211848 | tf_op jit(solution)/shard_map/ppermute | solution.py:539
  4.1 16.8 %collective-permute-start.3 = (f32[72,512]{1,0:T(8,128)}, f32[72,512]{1,0:T(8,128)S(1)}, u32[]{:S(2)}, u32[]{:S(2)}) collective-permute-start(f32[72,512]{1,0:T(8,128)} %get-tuple-element.35), channel_id=1, source_target_pairs={{9,3},{10,0},{11,5},{12,2},{13,7},{14,4},{25,19},{26,16},{27,21},{... | collective-permute-start | bytes 442376 | tf_op jit(solution)/shard_map/ppermute | solution.py:539
  5.4 22.3 %collective-permute-start.8 = (f32[3,72,512]{2,1,0:T(8,128)}, f32[3,72,512]{2,1,0:T(8,128)S(1)}, u32[]{:S(2)}, u32[]{:S(2)}) collective-permute-start(f32[3,72,512]{2,1,0:T(8,128)} %get-tuple-element.30.late), channel_id=1, source_target_pairs={{8,1},{9,0},{10,3},{11,2},{12,5},{13,4},{14,7},{15,6},{24,17},{25,... | collective-permute-start | bytes 1327112 | tf_op jit(solution)/shard_map/ppermute | solution.py:539
  9.1 10.3 %collective-permute-start.1 = (f32[136,256]{1,0:T(8,128)S(1)}, f32[136,256]{1,0:T(8,128)S(1)}, u32[]{:S(2)}, u32[]{:S(2)}) collective-permute-start(f32[136,256]{1,0:T(8,128)S(1)} %get-tuple-element.28.mine), channel_id=1, source_target_pairs={{0,16},{1,17},{2,18},{3,19},{4,20},{5,21},{6,22},{7,23},{8,0},{9,1... | collective-permute-start | bytes 417800 | tf_op jit(solution)/shard_map/ppermute | solution.py:539
  13.9 6.9 %collective-permute-start = (f32[136,256]{1,0:T(8,128)S(1)}, f32[136,256]{1,0:T(8,128)S(1)}, u32[]{:S(2)}, u32[]{:S(2)}) collective-permute-start(f32[136,256]{1,0:T(8,128)S(1)} %get-tuple-element.28.mine), channel_id=1, source_target_pairs={{0,8},{1,9},{2,10},{3,11},{4,12},{5,13},{6,14},{7,15},{8,16},{9,17... | collective-permute-start | bytes 417800 | tf_op jit(solution)/shard_map/ppermute | solution.py:539
  21.0 21.4 %collective-permute-start.7 = (f32[5,72,512]{2,1,0:T(8,128)S(1)}, f32[5,72,512]{2,1,0:T(8,128)S(1)}, u32[]{:S(2)}, u32[]{:S(2)}) collective-permute-start(f32[5,72,512]{2,1,0:T(8,128)S(1)} %get-tuple-element.40), channel_id=1, source_target_pairs={{0,2},{2,4},{3,1},{4,6},{5,3},{7,5},{16,18},{18,20},{19,17},{20,22... | collective-permute-start | bytes 2211848 | tf_op jit(solution)/shard_map/ppermute | solution.py:539
  25.0 14.1 %collective-permute-start.11 = (f32[456,256]{1,0:T(8,128)S(1)}, f32[456,256]{1,0:T(8,128)S(1)}, u32[]{:S(2)}, u32[]{:S(2)}) collective-permute-start(f32[456,256]{1,0:T(8,128)S(1)} %get-tuple-element.44), channel_id=1, source_target_pairs={{0,1},{1,0},{2,3},{3,2},{4,5},{5,4},{6,7},{7,6},{16,17},{17,16},{1... | collective-permute-start | bytes 1400840 | tf_op jit(solution)/shard_map/ppermute | solution.py:539
  26.9 15.4 %collective-permute-start.6 = (f32[456,256]{1,0:T(8,128)S(1)}, f32[456,256]{1,0:T(8,128)S(1)}, u32[]{:S(2)}, u32[]{:S(2)}) collective-permute-start(f32[456,256]{1,0:T(8,128)S(1)} %get-tuple-element.39), channel_id=1, source_target_pairs={{1,2},{2,1},{3,4},{4,3},{5,6},{6,5},{17,18},{18,17},{19,20},{20,19... | collective-permute-start | bytes 1400840 | tf_op jit(solution)/shard_map/ppermute | solution.py:539
  27.6 14.7 %collective-permute-start.9 = (f32[3,72,512]{2,1,0:T(8,128)S(1)}, f32[3,72,512]{2,1,0:T(8,128)S(1)}, u32[]{:S(2)}, u32[]{:S(2)}) collective-permute-start(f32[3,72,512]{2,1,0:T(8,128)S(1)} %collective-permute-done.8.near_late), channel_id=1, source_target_pairs={{0,2},{2,4},{3,1},{4,6},{5,3},{7,5},{16,18},{18,20},{19,17},{20,22... | collective-permute-start | bytes 1327112 | tf_op jit(solution)/shard_map/ppermute | solution.py:539
  34.3 0.7 %collective-permute-start.4 = (f32[96,128]{1,0:T(8,128)S(1)}, f32[96,128]{1,0:T(8,128)S(1)}, u32[]{:S(2)}, u32[]{:S(2)}) collective-permute-start(f32[96,128]{1,0:T(8,128)S(1)} %get-tuple-element.32.halo_near), channel_id=1, source_target_pairs={{8,9},{9,8},{10,11},{11,10},{12,13},{13,12},{14,15},{15,14}} | collective-permute-start | bytes 147464 | tf_op jit(solution)/shard_map/ppermute | solution.py:539
  35.0 0.7 %collective-permute-start.5 = (f32[96,128]{1,0:T(8,128)S(1)}, f32[96,128]{1,0:T(8,128)S(1)}, u32[]{:S(2)}, u32[]{:S(2)}) collective-permute-start(f32[96,128]{1,0:T(8,128)S(1)} %get-tuple-element.33.halo_far), channel_id=1, source_target_pairs={{9,10},{10,9},{11,12},{12,11},{13,14},{14,13}} | collective-permute-start | bytes 147464 | tf_op jit(solution)/shard_map/ppermute | solution.py:539
  35.7 6.7 %collective-permute-start.10 = (f32[72,512]{1,0:T(8,128)S(1)}, f32[72,512]{1,0:T(8,128)S(1)}, u32[]{:S(2)}, u32[]{:S(2)}) collective-permute-start(f32[72,512]{1,0:T(8,128)S(1)} %copy-done.12), channel_id=1, source_target_pairs={{8,2},{10,4},{11,1},{12,6},{13,3},{15,5},{24,18},{26,20},{27,17},{... | collective-permute-start | bytes 442376 | tf_op jit(solution)/shard_map/ppermute | solution.py:539
  47.6 9.6 %collective-permute-start.12 = (f32[128,384]{1,0:T(8,128)S(1)}, f32[128,384]{1,0:T(8,128)S(1)}, u32[]{:S(2)}, u32[]{:S(2)}) collective-permute-start(f32[128,384]{1,0:T(8,128)S(1)} %shard_map.145), channel_id=1, source_target_pairs={{0,16},{1,17},{2,18},{3,19},{4,20},{5,21},{6,22},{7,23},{16,0},{17... | collective-permute-start | bytes 589832 | tf_op jit(solution)/shard_map/ppermute | solution.py:539
  50.3 6.9 %collective-permute-start.14 = (f32[128,384]{1,0:T(8,128)S(1)}, f32[128,384]{1,0:T(8,128)S(1)}, u32[]{:S(2)}, u32[]{:S(2)}) collective-permute-start(f32[128,384]{1,0:T(8,128)S(1)} %get-tuple-element.48), channel_id=1, source_target_pairs={{16,8},{17,9},{18,10},{19,11},{20,12},{21,13},{22,14},{23,15}} | collective-permute-start | bytes 589832 | tf_op jit(solution)/shard_map/ppermute | solution.py:539
  51.0 6.3 %collective-permute-start.13 = (f32[128,384]{1,0:T(8,128)S(1)}, f32[128,384]{1,0:T(8,128)S(1)}, u32[]{:S(2)}, u32[]{:S(2)}) collective-permute-start(f32[128,384]{1,0:T(8,128)S(1)} %get-tuple-element.48), channel_id=1, source_target_pairs={{0,8},{1,9},{2,10},{3,11},{4,12},{5,13},{6,14},{7,15}} | collective-permute-start | bytes 589832 | tf_op jit(solution)/shard_map/ppermute | solution.py:539
  (4 other events, 27.9 us)

commit v20 on v18

--- a/solution.py
+++ b/solution.py
@@ -68,7 +68,7 @@
 
 
 def window_kernel(
-    pressure_old, source, solid_before, early, late, ends, inner, pressure, driven, solid, sems
+    pressure_old, source, solid_before, early, late, ends, pressure, driven, solid, sems
 ):
     planes, height, _ = solid.shape
     place = Place(pressure_old.shape[1], height)
@@ -86,10 +86,7 @@
     stored = [copy(pressure.at[x], early.at[x]) for x in range(planes)]
     for x in range(planes):
         stored.append(copy(driven.at[x], early.at[planes + x] if x < HEAD else late.at[x - HEAD]))
-    sides = (
-        copy(pressure.at[place.parity * (planes - 1)], ends),
-        copy(pressure.at[(1 - place.parity) * (planes - 1)], inner),
-    )
+    stored.append(copy(pressure.at[place.parity * (planes - 1)], ends))
     for x in range(planes):
         for part in fetched:
             part[x].start()
@@ -100,19 +97,17 @@
         fetched[2][x].wait()
         driven[x] = driven[x] - solid[x]
         stored[planes + x].start()
-    for one in sides:
-        one.start()
+    stored[-1].start()
     for one in stored:
         one.wait()
-    for one in sides:
-        one.wait()
-
-
-def forward_kernel(near, inner, _halo, _second, _third, _beyond, out, dummy):
+
+
+def forward_kernel(near, early, _halo, _second, _third, _beyond, out, dummy):
     dummy[...] = jnp.zeros(dummy.shape, F32)
     count = near.shape[0]
     out[:count] = near[...]
-    out[count] = inner[...]
+    end = (1 - lax.axis_index("reg") % 2) * (count - HEAD - 1)
+    out[count] = early[end]
 
 
 def deposit_kernel(count, cell, vol, drag, ids, out, dummy):
@@ -163,8 +158,7 @@
     out[tiles : tiles + SUB, BLOCK:] = jnp.zeros((SUB, BLOCK), F32)
 
 
-def halo_kernel(pos, vel, lists, _, inner, state, near, far, dummy, held):
-    held[...] = inner[...]
+def halo_kernel(pos, vel, lists, _, state, near, far, dummy):
     dummy[...] = jnp.zeros(dummy.shape, F32)
     tiles = pos.shape[1] // BLOCK
     rows = lists.shape[1] // BLOCK
@@ -564,15 +558,14 @@
     field = shaped(planes, height, width)
     plane = shaped(height, width)
     small = shaped(SUB, BLOCK)
-    early, late, ends, inner = call(
+    early, late, ends = call(
         window_kernel,
         (
             shaped(planes + HEAD, height, width), shaped(planes - HEAD, height, width), plane,
-            plane,
         ),
         [HBM] * 3, (pressure_old, pressure_source, solid_old),
         [pltpu.VMEM((planes, height, width), F32)] * 3
-        + [pltpu.SemaphoreType.DMA((5 * planes + 2,))],
+        + [pltpu.SemaphoreType.DMA((5 * planes + 1,))],
         flops=field_bytes, size=6 * field_bytes, limit=61_950_000, place=HBM,
     )
     near = along_reg(early, owners, (1, -1), core=1)
@@ -586,9 +579,9 @@
     third = along_grp(mine, 2, holders)
     rows = halo_list.shape[1] // BLOCK
     halo = shaped(3 * rows, BLOCK)
-    state, halo_near, halo_far, after_halo, inner = call(
-        halo_kernel, (shaped(3 * tiles, BLOCK), halo, halo, small, plane),
-        [VMEM] * 5, (grain_pos, grain_vel, halo_list, after_deposit, inner), flops=slots,
+    state, halo_near, halo_far, after_halo = call(
+        halo_kernel, (shaped(3 * tiles, BLOCK), halo, halo, small),
+        [VMEM] * 4, (grain_pos, grain_vel, halo_list, after_deposit), flops=slots,
         size=4 * 4 * 3 * slots,
     )
     others = [g for g in holders if g not in owners]
@@ -596,7 +589,7 @@
     came_far = along_reg(halo_far, others, (-1, 1))
     far, after_forward = call(
         forward_kernel, (shaped(planes + HEAD + 1, height, width), small), [VMEM] * 6,
-        (near, inner, after_halo, second, third, beyond), size=5 * field_bytes,
+        (near, early, after_halo, second, third, beyond), size=5 * field_bytes,
     )
     far = along_reg(far, owners, (2, -2))
     far_late = along_reg(near_late, owners, (2, -2))

time: 59.3 us -> 58.4 us (0.985)
  local copies, waits for them, and re-layouts: 0.96 us -> 0.06 us
    unnamed x26 -> x24, local copies, waits for them, and re-layouts: 0.96 us -> 0.06 us
  transfers between devices with their start and end apart: 14 -> 14, of which waited for: 3 -> 3; matrix products, arithmetic and copies ran while one was open for 0% -> 0% of each run, Pallas kernels for 23% -> 24%
where the time goes in v20:
time: 58.4 us; the launch traced here: 58 us
  starting transfers between devices  24 us (41%)
  Pallas kernels  22.4 us (38%)
  waiting for transfers between devices  10.4 us (18%)
  between operations  1.08 us (2%)
    ppermute x14, starting transfers between devices, send(): return lax.ppermute(value, ('grp', 'reg'), flat)  24 us
    pallas_call x12, Pallas kernels, call(): pl.pallas_call(kernel, out_shape=outs, in_specs=specs, out_specs=jax.tree...  22.4 us
    ppermute x14, waiting for transfers between devices, send(): return lax.ppermute(value, ('grp', 'reg'), flat)  10.4 us
  transfers between devices with their start and end apart: 14, of which 3 were waited for; matrix products, arithmetic and copies ran while one was open for 0% of the time, Pallas kernels for 24%

profile of v20, /device:TPU:17, one launch (start us, length us, event | category | flops | bytes accessed | tf_op | source)
XLA Modules:
  0.0 58.0 jit_solution(15524360888295405210)
XLA Ops:
  0.0 2.5 %shard_map.137 = (f32[5,72,512]{2,1,0:T(8,128)}, f32[3,72,512]{2,1,0:T(8,128)}, f32[72,512]{1,0:T(8,128)}) custom-call(f32[4,128,512]{2,1,0:T(8,128)} %pressure_old.1, f32[4,128,512]{2,1,0:T(8,128)} %source.1, f32[4,128,512]{2,1,0:T(8,128)} %solid_before.1), custom_call_target="tpu_custom_call" | custom-call | flops 589824 | bytes 3538944 | tf_op jit(solution)/shard_map/pallas_call | solution.py:36
  2.6 3.9 %collective-permute-start.2 = (f32[5,72,512]{2,1,0:T(8,128)}, f32[5,72,512]{2,1,0:T(8,128)S(1)}, u32[]{:S(2)}, u32[]{:S(2)}) collective-permute-start(f32[5,72,512]{2,1,0:T(8,128)} %get-tuple-element.28.early.pressure), channel_id=1, source_target_pairs={{8,1},{9,0},{10,3},{11,2},{12,5},{13,4},{14,7},{15,6},{24,17},{25,... | collective-permute-start | bytes 2211848 | tf_op jit(solution)/shard_map/ppermute | solution.py:536
  6.5 1.3 %collective-permute-start.3 = (f32[72,512]{1,0:T(8,128)}, f32[72,512]{1,0:T(8,128)S(1)}, u32[]{:S(2)}, u32[]{:S(2)}) collective-permute-start(f32[72,512]{1,0:T(8,128)} %get-tuple-element.34), channel_id=1, source_target_pairs={{9,3},{10,0},{11,5},{12,2},{13,7},{14,4},{25,19},{26,16},{27,21},{... | collective-permute-start | bytes 442376 | tf_op jit(solution)/shard_map/ppermute | solution.py:536
  8.5 1.7 %shard_map.136 = (f32[136,256]{1,0:T(8,128)S(1)}, f32[8,128]{1,0:T(8,128)S(1)}) custom-call(s32[1]{0:T(128)S(6)} %copy.15.count, s32[128,128]{1,0:T(8,128)S(1)} %bitcast.4, f32[128,128]{1,0:T(8,128)S(1)} %bitcast.6, f32[128,128]{1,0:T(8,128)S(1)} %bitcast.8, s32[1,128]{1,0:T(1,128)S(1)} %bitcast.10), custom_call_target="tpu_custom_call" | custom-call | flops 201326592 | bytes 327680 | tf_op jit(solution)/shard_map/pallas_call | solution.py:36
  10.2 1.9 %collective-permute-start.1 = (f32[136,256]{1,0:T(8,128)S(1)}, f32[136,256]{1,0:T(8,128)S(1)}, u32[]{:S(2)}, u32[]{:S(2)}) collective-permute-start(f32[136,256]{1,0:T(8,128)S(1)} %get-tuple-element.27.mine), channel_id=1, source_target_pairs={{0,16},{1,17},{2,18},{3,19},{4,20},{5,21},{6,22},{7,23},{8,0},{9,1... | collective-permute-start | bytes 417800 | tf_op jit(solution)/shard_map/ppermute | solution.py:536
  12.1 3.6 %collective-permute-start = (f32[136,256]{1,0:T(8,128)S(1)}, f32[136,256]{1,0:T(8,128)S(1)}, u32[]{:S(2)}, u32[]{:S(2)}) collective-permute-start(f32[136,256]{1,0:T(8,128)S(1)} %get-tuple-element.27.mine), channel_id=1, source_target_pairs={{0,8},{1,9},{2,10},{3,11},{4,12},{5,13},{6,14},{7,15},{8,16},{9,17... | collective-permute-start | bytes 417800 | tf_op jit(solution)/shard_map/ppermute | solution.py:536
  15.8 1.8 %collective-permute-start.8 = (f32[3,72,512]{2,1,0:T(8,128)}, f32[3,72,512]{2,1,0:T(8,128)S(1)}, u32[]{:S(2)}, u32[]{:S(2)}) collective-permute-start(f32[3,72,512]{2,1,0:T(8,128)} %get-tuple-element.29.late), channel_id=1, source_target_pairs={{8,1},{9,0},{10,3},{11,2},{12,5},{13,4},{14,7},{15,6},{24,17},{25,... | collective-permute-start | bytes 1327112 | tf_op jit(solution)/shard_map/ppermute | solution.py:536
  17.6 3.2 %shard_map.138 = (f32[384,128]{1,0:T(8,128)S(1)}, f32[96,128]{1,0:T(8,128)S(1)}, f32[96,128]{1,0:T(8,128)S(1)}, f32[8,128]{1,0:T(8,128)S(1)}) custom-call(f32[3,16384]{1,0:T(4,128)S(1)} %copy-done.4, f32[3,16384]{1,0:T(4,128)S(1)} %copy-done.1, s32[2,4096]{1,0:T(2,128)S(1)} %copy-done.8, f32[8,128]{1,0:T(8,128)S(1)} %get-tuple-element.30._), custom_call_target="tpu_custom_call" | custom-call | flops 16384 | bytes 786432 | tf_op jit(solution)/shard_map/pallas_call | solution.py:36
  21.0 0.7 %collective-permute-start.7 = (f32[6,72,512]{2,1,0:T(8,128)S(1)}, f32[6,72,512]{2,1,0:T(8,128)S(1)}, u32[]{:S(2)}, u32[]{:S(2)}) collective-permute-start(f32[6,72,512]{2,1,0:T(8,128)S(1)} %get-tuple-element.39), channel_id=1, source_target_pairs={{0,2},{2,4},{3,1},{4,6},{5,3},{7,5},{16,18},{18,20},{19,17},{20,22... | collective-permute-start | bytes 2654216 | tf_op jit(solution)/shard_map/ppermute | solution.py:536
  21.8 0.7 %collective-permute-start.10 = (f32[456,256]{1,0:T(8,128)S(1)}, f32[456,256]{1,0:T(8,128)S(1)}, u32[]{:S(2)}, u32[]{:S(2)}) collective-permute-start(f32[456,256]{1,0:T(8,128)S(1)} %get-tuple-element.42), channel_id=1, source_target_pairs={{0,1},{1,0},{2,3},{3,2},{4,5},{5,4},{6,7},{7,6},{16,17},{17,16},{1... | collective-permute-start | bytes 1400840 | tf_op jit(solution)/shard_map/ppermute | solution.py:536
  22.5 0.7 %collective-permute-start.6 = (f32[456,256]{1,0:T(8,128)S(1)}, f32[456,256]{1,0:T(8,128)S(1)}, u32[]{:S(2)}, u32[]{:S(2)}) collective-permute-start(f32[456,256]{1,0:T(8,128)S(1)} %get-tuple-element.38), channel_id=1, source_target_pairs={{1,2},{2,1},{3,4},{4,3},{5,6},{6,5},{17,18},{18,17},{19,20},{20,19... | collective-permute-start | bytes 1400840 | tf_op jit(solution)/shard_map/ppermute | solution.py:536
  23.9 2.6 %collective-permute-start.4 = (f32[96,128]{1,0:T(8,128)S(1)}, f32[96,128]{1,0:T(8,128)S(1)}, u32[]{:S(2)}, u32[]{:S(2)}) collective-permute-start(f32[96,128]{1,0:T(8,128)S(1)} %get-tuple-element.31.halo_near), channel_id=1, source_target_pairs={{8,9},{9,8},{10,11},{11,10},{12,13},{13,12},{14,15},{15,14}} | collective-permute-start | bytes 147464 | tf_op jit(solution)/shard_map/ppermute | solution.py:536
  26.6 3.0 %collective-permute-done.4._near.halo_near = f32[96,128]{1,0:T(8,128)S(1)} collective-permute-done((f32[96,128]{1,0:T(8,128)S(1)}, f32[96,128]{1,0:T(8,128)S(1)}, u32[]{:S(2)}, u32[]{:S(2)}) %collective-permute-start.4) | collective-permute-done | bytes 49184 | tf_op jit(solution)/shard_map/ppermute | solution.py:536
  29.5 2.6 %collective-permute-start.5 = (f32[96,128]{1,0:T(8,128)S(1)}, f32[96,128]{1,0:T(8,128)S(1)}, u32[]{:S(2)}, u32[]{:S(2)}) collective-permute-start(f32[96,128]{1,0:T(8,128)S(1)} %get-tuple-element.32.halo_far), channel_id=1, source_target_pairs={{9,10},{10,9},{11,12},{12,11},{13,14},{14,13}} | collective-permute-start | bytes 147464 | tf_op jit(solution)/shard_map/ppermute | solution.py:536
  32.1 4.0 %collective-permute-done.5._far.halo_far = f32[96,128]{1,0:T(8,128)S(1)} collective-permute-done((f32[96,128]{1,0:T(8,128)S(1)}, f32[96,128]{1,0:T(8,128)S(1)}, u32[]{:S(2)}, u32[]{:S(2)}) %collective-permute-start.5) | collective-permute-done | bytes 49184 | tf_op jit(solution)/shard_map/ppermute | solution.py:536
  36.1 1.9 %shard_map.141 = (f32[4,72,512]{2,1,0:T(8,128)S(1)}, f32[4,72,512]{2,1,0:T(8,128)S(1)}, f32[128,128]{1,0:T(8,128)S(1)}, bf16[384,1152]{1,0:T(8,128)(2,1)S(1)}) custom-call(f32[136,256]{1,0:T(8,128)S(1)} %get-tuple-element.27.mine, f32[136,256]{1,0:T(8,128)S(1)} %collective-permute-done._second.second, f32[136,256]{1,0:T(8,128)S(1)} %collective-permute-done.1._third.third, ...), custom_call_target="tpu_custom_call" | custom-call | flops 679477248 | bytes 5308416 | tf_op jit(solution)/shard_map/pallas_call | solution.py:36
  38.1 3.3 %shard_map.142 = (f32[4,72,512]{2,1,0:T(8,128)S(1)}, f32[4,72,512]{2,1,0:T(8,128)S(1)}) custom-call(f32[456,256]{1,0:T(8,128)S(1)} %collective-permute-done.10.message.message_near, f32[5,72,512]{2,1,0:T(8,128)S(1)} %copy-done, f32[5,72,512]{2,1,0:T(8,128)S(1)} %collective-permute-done.2.near, f32[3,72,512]{2,1,0:T(8,128)S(1)} %collective-permute-done.8.near_late, ...), custom_call_target="tpu_custom_call" | custom-call | flops 679477248 | bytes 5308416 | tf_op jit(solution)/shard_map/pallas_call | solution.py:36
  41.4 4.7 %shard_map.143 = (f32[128,384]{1,0:T(8,128)S(1)}, bf16[1152,768]{1,0:T(8,128)(2,1)S(1)}) custom-call(bf16[384,1152]{1,0:T(8,128)(2,1)S(1)} %get-tuple-element.37.picks, f32[456,256]{1,0:T(8,128)S(1)} %collective-permute-done.6.message.message_far, f32[5,72,512]{2,1,0:T(8,128)S(1)} %copy-done, f32[6,72,512]{2,1,0:T(8,128)S(1)} %collective-permute-done.7.far, ...), custom_call_target="tpu_custom_call" | custom-call | flops 679477248 | bytes 5308416 | tf_op jit(solution)/shard_map/pallas_call | solution.py:36
  46.6 0.8 %collective-permute-start.11 = (f32[128,384]{1,0:T(8,128)S(1)}, f32[128,384]{1,0:T(8,128)S(1)}, u32[]{:S(2)}, u32[]{:S(2)}) collective-permute-start(f32[128,384]{1,0:T(8,128)S(1)} %shard_map.145), channel_id=1, source_target_pairs={{0,16},{1,17},{2,18},{3,19},{4,20},{5,21},{6,22},{7,23},{16,0},{17... | collective-permute-start | bytes 589832 | tf_op jit(solution)/shard_map/ppermute | solution.py:536
  47.4 1.3 %collective-permute-start.13 = (f32[128,384]{1,0:T(8,128)S(1)}, f32[128,384]{1,0:T(8,128)S(1)}, u32[]{:S(2)}, u32[]{:S(2)}) collective-permute-start(f32[128,384]{1,0:T(8,128)S(1)} %get-tuple-element.46), channel_id=1, source_target_pairs={{16,8},{17,9},{18,10},{19,11},{20,12},{21,13},{22,14},{23,15}} | collective-permute-start | bytes 589832 | tf_op jit(solution)/shard_map/ppermute | solution.py:536
  48.7 1.3 %collective-permute-start.12 = (f32[128,384]{1,0:T(8,128)S(1)}, f32[128,384]{1,0:T(8,128)S(1)}, u32[]{:S(2)}, u32[]{:S(2)}) collective-permute-start(f32[128,384]{1,0:T(8,128)S(1)} %get-tuple-element.46), channel_id=1, source_target_pairs={{0,8},{1,9},{2,10},{3,11},{4,12},{5,13},{6,14},{7,15}} | collective-permute-start | bytes 589832 | tf_op jit(solution)/shard_map/ppermute | solution.py:536
  50.5 3.0 %shard_map.146.contact = f32[384,128]{1,0:T(8,128)S(1)} custom-call(s32[128]{0:T(128)S(1)} %copy-done.9, f32[384,128]{1,0:T(8,128)S(1)} %get-tuple-element.48.state, f32[456,256]{1,0:T(8,128)S(1)} %collective-permute-done.10.message.message_near, f32[456,256]{1,0:T(8,128)S(1)} %collective-permute-done.6.message.message_far, ...), custom_call_target="tpu_custom_call" | custom-call | flops 7864320 | bytes 1310720 | tf_op jit(solution)/shard_map/pallas_call | solution.py:36
  53.5 3.5 %collective-permute-done.13.grads_d = f32[128,384]{1,0:T(8,128)S(1)} collective-permute-done((f32[128,384]{1,0:T(8,128)S(1)}, f32[128,384]{1,0:T(8,128)S(1)}, u32[]{:S(2)}, u32[]{:S(2)}) %collective-permute-start.13) | collective-permute-done | bytes 196640 | tf_op jit(solution)/shard_map/ppermute | solution.py:536
  57.0 1.0 %shard_map.147 = f32[3,16384]{1,0:T(4,128)} custom-call(s32[1]{0:T(128)S(6)} %copy.15.count, f32[128,384]{1,0:T(8,128)S(1)} %shard_map.144._.grads_a, f32[128,384]{1,0:T(8,128)S(1)} %collective-permute-done.11.grads_b, f32[128,384]{1,0:T(8,128)S(1)} %collective-permute-done.12.grads_c, f32[128,384]{1,0:T(8,128)S(1)} %collective-permute-done.13.grads_d, ...), custom_call_target="tpu_custom_call" | custom-call | flops 983040 | bytes 1310720 | tf_op jit(solution)/shard_map/pallas_call | solution.py:36
  (40 shorter events, 1.8 us)
Async XLA Ops:
  0.0 8.4 %copy-start.11 = (s32[128]{0:T(128)S(1)}, s32[128]{0:T(128)}, u32[]{:S(2)}) copy-start(s32[128]{0:T(128)} %param.24) | copy-start | bytes 1540
  0.0 8.4 %copy-start.5 = (s32[16384]{0:T(1024)S(1)}, s32[16384]{0:T(1024)}, u32[]{:S(2)}) copy-start(s32[16384]{0:T(1024)} %param.23) | copy-start | bytes 196612
  0.0 8.4 %copy-start.7 = (f32[16384]{0:T(1024)S(1)}, f32[16384]{0:T(1024)}, u32[]{:S(2)}) copy-start(f32[16384]{0:T(1024)} %param.17) | copy-start | bytes 196612
  0.0 8.4 %copy-start.6 = (f32[16384]{0:T(1024)S(1)}, f32[16384]{0:T(1024)}, u32[]{:S(2)}) copy-start(f32[16384]{0:T(1024)} %param.16) | copy-start | bytes 196612
  0.0 17.6 %copy-start.1 = (f32[3,16384]{1,0:T(4,128)S(1)}, f32[3,16384]{1,0:T(4,128)}, u32[]{:S(2)}) copy-start(f32[3,16384]{1,0:T(4,128)} %vel.3) | copy-start | bytes 589828
  0.0 17.6 %copy-start.8 = (s32[2,4096]{1,0:T(2,128)S(1)}, s32[2,4096]{1,0:T(2,128)}, u32[]{:S(2)}) copy-start(s32[2,4096]{1,0:T(2,128)} %lists.1) | copy-start | bytes 98308
  0.0 17.6 %copy-start.4 = (f32[3,16384]{1,0:T(4,128)S(1)}, f32[3,16384]{1,0:T(4,128)}, u32[]{:S(2)}) copy-start(f32[3,16384]{1,0:T(4,128)} %pos.1) | copy-start | bytes 589828
  2.6 18.4 %copy-start = (f32[5,72,512]{2,1,0:T(8,128)S(1)}, f32[5,72,512]{2,1,0:T(8,128)}, u32[]{:S(2)}) copy-start(f32[5,72,512]{2,1,0:T(8,128)} %get-tuple-element.28.early.pressure) | copy-start | bytes 2211844
  2.6 18.3 %collective-permute-start.2 = (f32[5,72,512]{2,1,0:T(8,128)}, f32[5,72,512]{2,1,0:T(8,128)S(1)}, u32[]{:S(2)}, u32[]{:S(2)}) collective-permute-start(f32[5,72,512]{2,1,0:T(8,128)} %get-tuple-element.28.early.pressure), channel_id=1, source_target_pairs={{8,1},{9,0},{10,3},{11,2},{12,5},{13,4},{14,7},{15,6},{24,17},{25,... | collective-permute-start | bytes 2211848 | tf_op jit(solution)/shard_map/ppermute | solution.py:536
  6.5 14.4 %collective-permute-start.3 = (f32[72,512]{1,0:T(8,128)}, f32[72,512]{1,0:T(8,128)S(1)}, u32[]{:S(2)}, u32[]{:S(2)}) collective-permute-start(f32[72,512]{1,0:T(8,128)} %get-tuple-element.34), channel_id=1, source_target_pairs={{9,3},{10,0},{11,5},{12,2},{13,7},{14,4},{25,19},{26,16},{27,21},{... | collective-permute-start | bytes 442376 | tf_op jit(solution)/shard_map/ppermute | solution.py:536
  8.5 27.7 %copy-start.9 = (s32[128]{0:T(128)S(1)}, s32[128]{0:T(128)}, u32[]{:S(2)}) copy-start(s32[128]{0:T(128)} %partner.1) | copy-start | bytes 1540
  8.5 27.6 %copy-start.10 = (f32[3,72,512]{2,1,0:T(8,128)S(1)}, f32[3,72,512]{2,1,0:T(8,128)}, u32[]{:S(2)}) copy-start(f32[3,72,512]{2,1,0:T(8,128)} %get-tuple-element.29.late) | copy-start | bytes 1327108
  10.2 10.7 %collective-permute-start.1 = (f32[136,256]{1,0:T(8,128)S(1)}, f32[136,256]{1,0:T(8,128)S(1)}, u32[]{:S(2)}, u32[]{:S(2)}) collective-permute-start(f32[136,256]{1,0:T(8,128)S(1)} %get-tuple-element.27.mine), channel_id=1, source_target_pairs={{0,16},{1,17},{2,18},{3,19},{4,20},{5,21},{6,22},{7,23},{8,0},{9,1... | collective-permute-start | bytes 417800 | tf_op jit(solution)/shard_map/ppermute | solution.py:536
  12.1 8.8 %collective-permute-start = (f32[136,256]{1,0:T(8,128)S(1)}, f32[136,256]{1,0:T(8,128)S(1)}, u32[]{:S(2)}, u32[]{:S(2)}) collective-permute-start(f32[136,256]{1,0:T(8,128)S(1)} %get-tuple-element.27.mine), channel_id=1, source_target_pairs={{0,8},{1,9},{2,10},{3,11},{4,12},{5,13},{6,14},{7,15},{8,16},{9,17... | collective-permute-start | bytes 417800 | tf_op jit(solution)/shard_map/ppermute | solution.py:536
  15.8 7.4 %collective-permute-start.8 = (f32[3,72,512]{2,1,0:T(8,128)}, f32[3,72,512]{2,1,0:T(8,128)S(1)}, u32[]{:S(2)}, u32[]{:S(2)}) collective-permute-start(f32[3,72,512]{2,1,0:T(8,128)} %get-tuple-element.29.late), channel_id=1, source_target_pairs={{8,1},{9,0},{10,3},{11,2},{12,5},{13,4},{14,7},{15,6},{24,17},{25,... | collective-permute-start | bytes 1327112 | tf_op jit(solution)/shard_map/ppermute | solution.py:536
  21.0 20.4 %collective-permute-start.7 = (f32[6,72,512]{2,1,0:T(8,128)S(1)}, f32[6,72,512]{2,1,0:T(8,128)S(1)}, u32[]{:S(2)}, u32[]{:S(2)}) collective-permute-start(f32[6,72,512]{2,1,0:T(8,128)S(1)} %get-tuple-element.39), channel_id=1, source_target_pairs={{0,2},{2,4},{3,1},{4,6},{5,3},{7,5},{16,18},{18,20},{19,17},{20,22... | collective-permute-start | bytes 2654216 | tf_op jit(solution)/shard_map/ppermute | solution.py:536
  21.8 16.3 %collective-permute-start.10 = (f32[456,256]{1,0:T(8,128)S(1)}, f32[456,256]{1,0:T(8,128)S(1)}, u32[]{:S(2)}, u32[]{:S(2)}) collective-permute-start(f32[456,256]{1,0:T(8,128)S(1)} %get-tuple-element.42), channel_id=1, source_target_pairs={{0,1},{1,0},{2,3},{3,2},{4,5},{5,4},{6,7},{7,6},{16,17},{17,16},{1... | collective-permute-start | bytes 1400840 | tf_op jit(solution)/shard_map/ppermute | solution.py:536
  22.5 18.8 %collective-permute-start.6 = (f32[456,256]{1,0:T(8,128)S(1)}, f32[456,256]{1,0:T(8,128)S(1)}, u32[]{:S(2)}, u32[]{:S(2)}) collective-permute-start(f32[456,256]{1,0:T(8,128)S(1)} %get-tuple-element.38), channel_id=1, source_target_pairs={{1,2},{2,1},{3,4},{4,3},{5,6},{6,5},{17,18},{18,17},{19,20},{20,19... | collective-permute-start | bytes 1400840 | tf_op jit(solution)/shard_map/ppermute | solution.py:536
  23.2 18.1 %collective-permute-start.9 = (f32[3,72,512]{2,1,0:T(8,128)S(1)}, f32[3,72,512]{2,1,0:T(8,128)S(1)}, u32[]{:S(2)}, u32[]{:S(2)}) collective-permute-start(f32[3,72,512]{2,1,0:T(8,128)S(1)} %collective-permute-done.8.near_late), channel_id=1, source_target_pairs={{0,2},{2,4},{3,1},{4,6},{5,3},{7,5},{16,18},{18,20},{19,17},{20,22... | collective-permute-start | bytes 1327112 | tf_op jit(solution)/shard_map/ppermute | solution.py:536
  23.9 5.6 %collective-permute-start.4 = (f32[96,128]{1,0:T(8,128)S(1)}, f32[96,128]{1,0:T(8,128)S(1)}, u32[]{:S(2)}, u32[]{:S(2)}) collective-permute-start(f32[96,128]{1,0:T(8,128)S(1)} %get-tuple-element.31.halo_near), channel_id=1, source_target_pairs={{8,9},{9,8},{10,11},{11,10},{12,13},{13,12},{14,15},{15,14}} | collective-permute-start | bytes 147464 | tf_op jit(solution)/shard_map/ppermute | solution.py:536
  29.5 6.6 %collective-permute-start.5 = (f32[96,128]{1,0:T(8,128)S(1)}, f32[96,128]{1,0:T(8,128)S(1)}, u32[]{:S(2)}, u32[]{:S(2)}) collective-permute-start(f32[96,128]{1,0:T(8,128)S(1)} %get-tuple-element.32.halo_far), channel_id=1, source_target_pairs={{9,10},{10,9},{11,12},{12,11},{13,14},{14,13}} | collective-permute-start | bytes 147464 | tf_op jit(solution)/shard_map/ppermute | solution.py:536
  46.6 6.9 %collective-permute-start.11 = (f32[128,384]{1,0:T(8,128)S(1)}, f32[128,384]{1,0:T(8,128)S(1)}, u32[]{:S(2)}, u32[]{:S(2)}) collective-permute-start(f32[128,384]{1,0:T(8,128)S(1)} %shard_map.145), channel_id=1, source_target_pairs={{0,16},{1,17},{2,18},{3,19},{4,20},{5,21},{6,22},{7,23},{16,0},{17... | collective-permute-start | bytes 589832 | tf_op jit(solution)/shard_map/ppermute | solution.py:536
  47.4 9.6 %collective-permute-start.13 = (f32[128,384]{1,0:T(8,128)S(1)}, f32[128,384]{1,0:T(8,128)S(1)}, u32[]{:S(2)}, u32[]{:S(2)}) collective-permute-start(f32[128,384]{1,0:T(8,128)S(1)} %get-tuple-element.46), channel_id=1, source_target_pairs={{16,8},{17,9},{18,10},{19,11},{20,12},{21,13},{22,14},{23,15}} | collective-permute-start | bytes 589832 | tf_op jit(solution)/shard_map/ppermute | solution.py:536
  48.7 8.3 %collective-permute-start.12 = (f32[128,384]{1,0:T(8,128)S(1)}, f32[128,384]{1,0:T(8,128)S(1)}, u32[]{:S(2)}, u32[]{:S(2)}) collective-permute-start(f32[128,384]{1,0:T(8,128)S(1)} %get-tuple-element.46), channel_id=1, source_target_pairs={{0,8},{1,9},{2,10},{3,11},{4,12},{5,13},{6,14},{7,15}} | collective-permute-start | bytes 589832 | tf_op jit(solution)/shard_map/ppermute | solution.py:536
  (2 other events, 7.7 us)

commit v21 on v20

--- a/solution.py
+++ b/solution.py
@@ -203,12 +203,18 @@
 
 def message_kernel(mine, second, third, halo_near, halo_far, _, near, far, dummy):
     dummy[...] = jnp.zeros(dummy.shape, F32)
-    stride = mine.shape[0]
+    tiles = mine.shape[0] - SUB
     half = halo_near.shape[0] // 2
     rows = near.shape[0] - half
+    groups = (mine, second, third)
+    sub = iota((SUB, 2 * BLOCK), 0)
+    ids = groups[0][tiles:, :]
+    for index in (1, 2):
+        ids = jnp.where(sub == index, groups[index][tiles:, :], ids)
     for halo, out in ((halo_near, near), (halo_far, far)):
-        for index, group in enumerate((mine, second, third)):
-            out[index * stride : (index + 1) * stride, :] = group[...]
+        for index, group in enumerate(groups):
+            out[index * tiles : (index + 1) * tiles, :] = group[:tiles, :]
+        out[rows - SUB : rows, :] = ids
         out[rows:, :BLOCK] = halo[:half, :]
         out[rows:, BLOCK:] = halo[half:, :]
 
@@ -294,11 +300,10 @@
     return near * (2.0 - value * near)
 
 
-def placed(groups, tiles):
+def placed(groups, ids, tiles):
     parts = [halves_of(group[:tiles, :]) for group in groups]
     loads = jnp.concatenate([part[i] for i in range(2) for part in parts], 0)
-    ids = jnp.concatenate([group[tiles : tiles + 1, :BLOCK] for group in groups], 1)
-    ids = ids.astype(jnp.int32)
+    ids = jnp.concatenate(ids, 1).astype(jnp.int32)
 
     def gathered(wanted):
         hot = jnp.where(wanted == jnp.broadcast_to(ids, wanted.shape), 1.0, 0.0).astype(BF16)
@@ -344,7 +349,9 @@
     planes, height, width = constant.shape
     place = Place(full, height)
     zones = width // BLOCK
-    ids, gathered = placed((mine, second, third), tiles)
+    groups = (mine, second, third)
+    ids = [group[tiles : tiles + 1, :BLOCK] for group in groups]
+    ids, gathered = placed(groups, ids, tiles)
     coefficients(
         gathered, tiles, place.first, full, driven_of(early, late, planes), constant, factor,
         place.even, None,
@@ -380,8 +387,9 @@
 
 
 def deposits_of(message, tiles):
-    stride = tiles + SUB
-    return placed([message.at[i * stride : (i + 1) * stride] for i in range(3)], tiles)[1]
+    groups = [message.at[i * tiles : (i + 1) * tiles] for i in range(3)]
+    ids = [message[3 * tiles + i : 3 * tiles + i + 1, :BLOCK] for i in range(3)]
+    return placed(groups, ids, tiles)[1]
 
 
 def near_kernel(
@@ -413,7 +421,7 @@
 
 def far_kernel(
     full, tiles, picks, message, pressure, far, far_late, own_constant, own_factor, kept_even, kept_odd,
-    out, pieces, constant, factor, old, new, fields,
+    across, between, pieces, constant, factor, old, new, fields,
 ):
     planes, height, width = own_constant.shape
     zones = width // BLOCK
@@ -460,22 +468,20 @@
 
     lax.fori_loop(0, planes, gradient, 0, unroll=4)
     pieces[...] = jnp.concatenate(halves_of(fields[...]), 1)
-    out[...] = picked_rows(picks, 3 - across_set(), tiles, pieces)
-
-
-def across_set():
-    return jnp.where(lax.axis_index("grp") == 0, 1, 2)
-
-
-def picked_rows(picks, chosen, tiles, pieces):
-    hot = picks[pl.ds(pl.multiple_of(chosen * tiles, tiles), tiles), :]
+    total = picked_rows(picks[tiles:, :], pieces)
+    first, second = total[:tiles], total[tiles:]
+    low = lax.axis_index("grp") == 0
+    across[...] = jnp.where(low, first, second)
+    between[...] = jnp.where(low, second, first)
+
+
+def picked_rows(hot, pieces):
     total = jnp.dot(hot, pieces[...], preferred_element_type=F32)
     return total[:, : 3 * BLOCK] + total[:, 3 * BLOCK :]
 
 
-def pick_kernel(own, picks, pieces, out):
-    chosen = 0 if own else across_set()
-    out[...] = picked_rows(picks, chosen, out.shape[0], pieces)
+def pick_kernel(picks, pieces, out):
+    out[...] = picked_rows(picks[: out.shape[0], :], pieces)
 
 
 def final_kernel(
@@ -593,7 +599,7 @@
     )
     far = along_reg(far, owners, (2, -2))
     far_late = along_reg(near_late, owners, (2, -2))
-    message = shaped(holding * (tiles + SUB) + 3 * rows // 2, 2 * BLOCK)
+    message = shaped(holding * tiles + SUB + 3 * rows // 2, 2 * BLOCK)
     message_near, message_far, after_message = call(
         message_kernel, (message, message, small), [VMEM] * 6,
         (mine, second, third, halo_near, halo_far, after_forward), size=8 * 2 * BLOCK * 500,
@@ -619,9 +625,9 @@
     )
     grads = shaped(tiles, 3 * BLOCK)
     cells_held = planes * height * width // BLOCK
-    grads_between, pieces = call(
+    grads_across, grads_between, pieces = call(
         functools.partial(far_kernel, full, tiles),
-        (grads, jax.ShapeDtypeStruct((cells_held, 6 * BLOCK), BF16)), [VMEM] * 9,
+        (grads, grads, jax.ShapeDtypeStruct((cells_held, 6 * BLOCK), BF16)), [VMEM] * 9,
         (picks, message_far, early, far, far_late, constant, factor, kept_even, kept_odd),
         [window_of(planes)] * 2
         + [window_of(3 * planes + 2)] * 2
@@ -632,12 +638,8 @@
     low, high, between = 0, CORES, 1
     came_low = send(grads_between, ends_of(low, between))
     came_high = send(grads_between, ends_of(high, between))
-    pick = lambda own: call(
-        functools.partial(pick_kernel, own), grads, [VMEM] * 2, (picks, pieces),
-        flops=slots, size=slots,
-    )
-    came_across = send(pick(False), ends_of(low, high) + ends_of(high, low))
-    grads_a = pick(True)
+    came_across = send(grads_across, ends_of(low, high) + ends_of(high, low))
+    grads_a = call(pick_kernel, grads, [VMEM] * 2, (picks, pieces), flops=slots, size=slots)
     contact = call(
         contact_kernel, shaped(3 * tiles, BLOCK), [SMEM] + [VMEM] * 7 + [ANY],
         (

time: 58.4 us -> 57.9 us (level)
    pallas_call x12 -> x11, Pallas kernels: 22.4 us -> 22.2 us  [call(): pl.pallas_call(kernel, out_shape=outs, in_specs=specs, out_specs=jax.tree...]
where the time goes in v21:
time: 57.9 us; the launch traced here: 57.4 us
  starting transfers between devices  24 us (41%)
  Pallas kernels  22.2 us (38%)
  waiting for transfers between devices  10.1 us (17%)
  between operations  1.07 us (2%)
    ppermute x14, starting transfers between devices, send(): return lax.ppermute(value, ('grp', 'reg'), flat)  24 us
    pallas_call x11, Pallas kernels, call(): pl.pallas_call(kernel, out_shape=outs, in_specs=specs, out_specs=jax.tree...  22.2 us
    ppermute x14, waiting for transfers between devices, send(): return lax.ppermute(value, ('grp', 'reg'), flat)  10.1 us
  transfers between devices with their start and end apart: 14, of which 3 were waited for; matrix products, arithmetic and copies ran while one was open for 0% of the time, Pallas kernels for 24%

profile of v21, /device:TPU:17, one launch (start us, length us, event | category | flops | bytes accessed | tf_op | source)
XLA Modules:
  0.0 57.4 jit_solution(16162680803050772977)
XLA Ops:
  0.0 2.5 %shard_map.137 = (f32[5,72,512]{2,1,0:T(8,128)}, f32[3,72,512]{2,1,0:T(8,128)}, f32[72,512]{1,0:T(8,128)}) custom-call(f32[4,128,512]{2,1,0:T(8,128)} %pressure_old.1, f32[4,128,512]{2,1,0:T(8,128)} %source.1, f32[4,128,512]{2,1,0:T(8,128)} %solid_before.1), custom_call_target="tpu_custom_call" | custom-call | flops 589824 | bytes 3538944 | tf_op jit(solution)/shard_map/pallas_call | solution.py:36
  2.6 3.9 %collective-permute-start.2 = (f32[5,72,512]{2,1,0:T(8,128)}, f32[5,72,512]{2,1,0:T(8,128)S(1)}, u32[]{:S(2)}, u32[]{:S(2)}) collective-permute-start(f32[5,72,512]{2,1,0:T(8,128)} %get-tuple-element.29.early.pressure), channel_id=1, source_target_pairs={{8,1},{9,0},{10,3},{11,2},{12,5},{13,4},{14,7},{15,6},{24,17},{25,... | collective-permute-start | bytes 2211848 | tf_op jit(solution)/shard_map/ppermute | solution.py:542
  6.5 1.3 %collective-permute-start.3 = (f32[72,512]{1,0:T(8,128)}, f32[72,512]{1,0:T(8,128)S(1)}, u32[]{:S(2)}, u32[]{:S(2)}) collective-permute-start(f32[72,512]{1,0:T(8,128)} %get-tuple-element.35), channel_id=1, source_target_pairs={{9,3},{10,0},{11,5},{12,2},{13,7},{14,4},{25,19},{26,16},{27,21},{... | collective-permute-start | bytes 442376 | tf_op jit(solution)/shard_map/ppermute | solution.py:542
  8.5 1.7 %shard_map.136 = (f32[136,256]{1,0:T(8,128)S(1)}, f32[8,128]{1,0:T(8,128)S(1)}) custom-call(s32[1]{0:T(128)S(6)} %copy.15.count, s32[128,128]{1,0:T(8,128)S(1)} %bitcast.4, f32[128,128]{1,0:T(8,128)S(1)} %bitcast.6, f32[128,128]{1,0:T(8,128)S(1)} %bitcast.8, s32[1,128]{1,0:T(1,128)S(1)} %bitcast.10), custom_call_target="tpu_custom_call" | custom-call | flops 201326592 | bytes 327680 | tf_op jit(solution)/shard_map/pallas_call | solution.py:36
  10.2 1.9 %collective-permute-start.1 = (f32[136,256]{1,0:T(8,128)S(1)}, f32[136,256]{1,0:T(8,128)S(1)}, u32[]{:S(2)}, u32[]{:S(2)}) collective-permute-start(f32[136,256]{1,0:T(8,128)S(1)} %get-tuple-element.28.mine), channel_id=1, source_target_pairs={{0,16},{1,17},{2,18},{3,19},{4,20},{5,21},{6,22},{7,23},{8,0},{9,1... | collective-permute-start | bytes 417800 | tf_op jit(solution)/shard_map/ppermute | solution.py:542
  12.1 3.6 %collective-permute-start = (f32[136,256]{1,0:T(8,128)S(1)}, f32[136,256]{1,0:T(8,128)S(1)}, u32[]{:S(2)}, u32[]{:S(2)}) collective-permute-start(f32[136,256]{1,0:T(8,128)S(1)} %get-tuple-element.28.mine), channel_id=1, source_target_pairs={{0,8},{1,9},{2,10},{3,11},{4,12},{5,13},{6,14},{7,15},{8,16},{9,17... | collective-permute-start | bytes 417800 | tf_op jit(solution)/shard_map/ppermute | solution.py:542
  15.8 1.8 %collective-permute-start.8 = (f32[3,72,512]{2,1,0:T(8,128)}, f32[3,72,512]{2,1,0:T(8,128)S(1)}, u32[]{:S(2)}, u32[]{:S(2)}) collective-permute-start(f32[3,72,512]{2,1,0:T(8,128)} %get-tuple-element.30.late), channel_id=1, source_target_pairs={{8,1},{9,0},{10,3},{11,2},{12,5},{13,4},{14,7},{15,6},{24,17},{25,... | collective-permute-start | bytes 1327112 | tf_op jit(solution)/shard_map/ppermute | solution.py:542
  17.6 3.2 %shard_map.138 = (f32[384,128]{1,0:T(8,128)S(1)}, f32[96,128]{1,0:T(8,128)S(1)}, f32[96,128]{1,0:T(8,128)S(1)}, f32[8,128]{1,0:T(8,128)S(1)}) custom-call(f32[3,16384]{1,0:T(4,128)S(1)} %copy-done.4, f32[3,16384]{1,0:T(4,128)S(1)} %copy-done.1, s32[2,4096]{1,0:T(2,128)S(1)} %copy-done.8, f32[8,128]{1,0:T(8,128)S(1)} %get-tuple-element.31._), custom_call_target="tpu_custom_call" | custom-call | flops 16384 | bytes 786432 | tf_op jit(solution)/shard_map/pallas_call | solution.py:36
  21.0 0.7 %collective-permute-start.7 = (f32[6,72,512]{2,1,0:T(8,128)S(1)}, f32[6,72,512]{2,1,0:T(8,128)S(1)}, u32[]{:S(2)}, u32[]{:S(2)}) collective-permute-start(f32[6,72,512]{2,1,0:T(8,128)S(1)} %get-tuple-element.40), channel_id=1, source_target_pairs={{0,2},{2,4},{3,1},{4,6},{5,3},{7,5},{16,18},{18,20},{19,17},{20,22... | collective-permute-start | bytes 2654216 | tf_op jit(solution)/shard_map/ppermute | solution.py:542
  21.8 0.7 %collective-permute-start.10 = (f32[440,256]{1,0:T(8,128)S(1)}, f32[440,256]{1,0:T(8,128)S(1)}, u32[]{:S(2)}, u32[]{:S(2)}) collective-permute-start(f32[440,256]{1,0:T(8,128)S(1)} %get-tuple-element.43), channel_id=1, source_target_pairs={{0,1},{1,0},{2,3},{3,2},{4,5},{5,4},{6,7},{7,6},{16,17},{17,16},{1... | collective-permute-start | bytes 1351688 | tf_op jit(solution)/shard_map/ppermute | solution.py:542
  22.5 0.7 %collective-permute-start.6 = (f32[440,256]{1,0:T(8,128)S(1)}, f32[440,256]{1,0:T(8,128)S(1)}, u32[]{:S(2)}, u32[]{:S(2)}) collective-permute-start(f32[440,256]{1,0:T(8,128)S(1)} %get-tuple-element.39), channel_id=1, source_target_pairs={{1,2},{2,1},{3,4},{4,3},{5,6},{6,5},{17,18},{18,17},{19,20},{20,19... | collective-permute-start | bytes 1351688 | tf_op jit(solution)/shard_map/ppermute | solution.py:542
  23.9 2.6 %collective-permute-start.4 = (f32[96,128]{1,0:T(8,128)S(1)}, f32[96,128]{1,0:T(8,128)S(1)}, u32[]{:S(2)}, u32[]{:S(2)}) collective-permute-start(f32[96,128]{1,0:T(8,128)S(1)} %get-tuple-element.32.halo_near), channel_id=1, source_target_pairs={{8,9},{9,8},{10,11},{11,10},{12,13},{13,12},{14,15},{15,14}} | collective-permute-start | bytes 147464 | tf_op jit(solution)/shard_map/ppermute | solution.py:542
  26.6 3.0 %collective-permute-done.4._near.halo_near = f32[96,128]{1,0:T(8,128)S(1)} collective-permute-done((f32[96,128]{1,0:T(8,128)S(1)}, f32[96,128]{1,0:T(8,128)S(1)}, u32[]{:S(2)}, u32[]{:S(2)}) %collective-permute-start.4) | collective-permute-done | bytes 49184 | tf_op jit(solution)/shard_map/ppermute | solution.py:542
  29.5 2.6 %collective-permute-start.5 = (f32[96,128]{1,0:T(8,128)S(1)}, f32[96,128]{1,0:T(8,128)S(1)}, u32[]{:S(2)}, u32[]{:S(2)}) collective-permute-start(f32[96,128]{1,0:T(8,128)S(1)} %get-tuple-element.33.halo_far), channel_id=1, source_target_pairs={{9,10},{10,9},{11,12},{12,11},{13,14},{14,13}} | collective-permute-start | bytes 147464 | tf_op jit(solution)/shard_map/ppermute | solution.py:542
  32.1 4.0 %collective-permute-done.5._far.halo_far = f32[96,128]{1,0:T(8,128)S(1)} collective-permute-done((f32[96,128]{1,0:T(8,128)S(1)}, f32[96,128]{1,0:T(8,128)S(1)}, u32[]{:S(2)}, u32[]{:S(2)}) %collective-permute-start.5) | collective-permute-done | bytes 49184 | tf_op jit(solution)/shard_map/ppermute | solution.py:542
  36.1 1.9 %shard_map.141 = (f32[4,72,512]{2,1,0:T(8,128)S(1)}, f32[4,72,512]{2,1,0:T(8,128)S(1)}, f32[128,128]{1,0:T(8,128)S(1)}, bf16[384,1152]{1,0:T(8,128)(2,1)S(1)}) custom-call(f32[136,256]{1,0:T(8,128)S(1)} %get-tuple-element.28.mine, f32[136,256]{1,0:T(8,128)S(1)} %collective-permute-done._second.second, f32[136,256]{1,0:T(8,128)S(1)} %collective-permute-done.1._third.third, ...), custom_call_target="tpu_custom_call" | custom-call | flops 679477248 | bytes 5308416 | tf_op jit(solution)/shard_map/pallas_call | solution.py:36
  38.1 3.3 %shard_map.142 = (f32[4,72,512]{2,1,0:T(8,128)S(1)}, f32[4,72,512]{2,1,0:T(8,128)S(1)}) custom-call(f32[440,256]{1,0:T(8,128)S(1)} %collective-permute-done.10.message.message_near, f32[5,72,512]{2,1,0:T(8,128)S(1)} %copy-done, f32[5,72,512]{2,1,0:T(8,128)S(1)} %collective-permute-done.2.near, f32[3,72,512]{2,1,0:T(8,128)S(1)} %collective-permute-done.8.near_late, ...), custom_call_target="tpu_custom_call" | custom-call | flops 679477248 | bytes 5308416 | tf_op jit(solution)/shard_map/pallas_call | solution.py:36
  41.4 5.0 %shard_map.143 = (f32[128,384]{1,0:T(8,128)S(1)}, f32[128,384]{1,0:T(8,128)S(1)}, bf16[1152,768]{1,0:T(8,128)(2,1)S(1)}) custom-call(bf16[384,1152]{1,0:T(8,128)(2,1)S(1)} %get-tuple-element.38.picks, f32[440,256]{1,0:T(8,128)S(1)} %collective-permute-done.6.message.message_far, f32[5,72,512]{2,1,0:T(8,128)S(1)} %copy-done, ...), custom_call_target="tpu_custom_call" | custom-call | flops 679477248 | bytes 5308416 | tf_op jit(solution)/shard_map/pallas_call | solution.py:36
  46.4 0.8 %collective-permute-start.11 = (f32[128,384]{1,0:T(8,128)S(1)}, f32[128,384]{1,0:T(8,128)S(1)}, u32[]{:S(2)}, u32[]{:S(2)}) collective-permute-start(f32[128,384]{1,0:T(8,128)S(1)} %get-tuple-element.47), channel_id=1, source_target_pairs={{0,16},{1,17},{2,18},{3,19},{4,20},{5,21},{6,22},{7,23},{16,0},{17... | collective-permute-start | bytes 589832 | tf_op jit(solution)/shard_map/ppermute | solution.py:542
  47.2 1.3 %collective-permute-start.13 = (f32[128,384]{1,0:T(8,128)S(1)}, f32[128,384]{1,0:T(8,128)S(1)}, u32[]{:S(2)}, u32[]{:S(2)}) collective-permute-start(f32[128,384]{1,0:T(8,128)S(1)} %get-tuple-element.48), channel_id=1, source_target_pairs={{16,8},{17,9},{18,10},{19,11},{20,12},{21,13},{22,14},{23,15}} | collective-permute-start | bytes 589832 | tf_op jit(solution)/shard_map/ppermute | solution.py:542
  48.5 1.3 %collective-permute-start.12 = (f32[128,384]{1,0:T(8,128)S(1)}, f32[128,384]{1,0:T(8,128)S(1)}, u32[]{:S(2)}, u32[]{:S(2)}) collective-permute-start(f32[128,384]{1,0:T(8,128)S(1)} %get-tuple-element.48), channel_id=1, source_target_pairs={{0,8},{1,9},{2,10},{3,11},{4,12},{5,13},{6,14},{7,15}} | collective-permute-start | bytes 589832 | tf_op jit(solution)/shard_map/ppermute | solution.py:542
  50.2 3.0 %shard_map.145.contact = f32[384,128]{1,0:T(8,128)S(1)} custom-call(s32[128]{0:T(128)S(1)} %copy-done.9, f32[384,128]{1,0:T(8,128)S(1)} %get-tuple-element.50.state, f32[440,256]{1,0:T(8,128)S(1)} %collective-permute-done.10.message.message_near, f32[440,256]{1,0:T(8,128)S(1)} %collective-permute-done.6.message.message_far, ...), custom_call_target="tpu_custom_call" | custom-call | flops 7864320 | bytes 1310720 | tf_op jit(solution)/shard_map/pallas_call | solution.py:36
  53.3 3.1 %collective-permute-done.13.grads_d = f32[128,384]{1,0:T(8,128)S(1)} collective-permute-done((f32[128,384]{1,0:T(8,128)S(1)}, f32[128,384]{1,0:T(8,128)S(1)}, u32[]{:S(2)}, u32[]{:S(2)}) %collective-permute-start.13) | collective-permute-done | bytes 196640 | tf_op jit(solution)/shard_map/ppermute | solution.py:542
  56.4 1.0 %shard_map.146 = f32[3,16384]{1,0:T(4,128)} custom-call(s32[1]{0:T(128)S(6)} %copy.15.count, f32[128,384]{1,0:T(8,128)S(1)} %shard_map.144._.grads_a, f32[128,384]{1,0:T(8,128)S(1)} %collective-permute-done.11.grads_b, f32[128,384]{1,0:T(8,128)S(1)} %collective-permute-done.12.grads_c, f32[128,384]{1,0:T(8,128)S(1)} %collective-permute-done.13.grads_d, ...), custom_call_target="tpu_custom_call" | custom-call | flops 983040 | bytes 1310720 | tf_op jit(solution)/shard_map/pallas_call | solution.py:36
  (39 shorter events, 1.3 us)
Async XLA Ops:
  0.0 8.4 %copy-start.11 = (s32[128]{0:T(128)S(1)}, s32[128]{0:T(128)}, u32[]{:S(2)}) copy-start(s32[128]{0:T(128)} %param.24) | copy-start | bytes 1540
  0.0 8.4 %copy-start.5 = (s32[16384]{0:T(1024)S(1)}, s32[16384]{0:T(1024)}, u32[]{:S(2)}) copy-start(s32[16384]{0:T(1024)} %param.23) | copy-start | bytes 196612
  0.0 8.4 %copy-start.7 = (f32[16384]{0:T(1024)S(1)}, f32[16384]{0:T(1024)}, u32[]{:S(2)}) copy-start(f32[16384]{0:T(1024)} %param.17) | copy-start | bytes 196612
  0.0 8.4 %copy-start.6 = (f32[16384]{0:T(1024)S(1)}, f32[16384]{0:T(1024)}, u32[]{:S(2)}) copy-start(f32[16384]{0:T(1024)} %param.16) | copy-start | bytes 196612
  0.0 17.6 %copy-start.1 = (f32[3,16384]{1,0:T(4,128)S(1)}, f32[3,16384]{1,0:T(4,128)}, u32[]{:S(2)}) copy-start(f32[3,16384]{1,0:T(4,128)} %vel.3) | copy-start | bytes 589828
  0.0 17.6 %copy-start.8 = (s32[2,4096]{1,0:T(2,128)S(1)}, s32[2,4096]{1,0:T(2,128)}, u32[]{:S(2)}) copy-start(s32[2,4096]{1,0:T(2,128)} %lists.1) | copy-start | bytes 98308
  0.0 17.6 %copy-start.4 = (f32[3,16384]{1,0:T(4,128)S(1)}, f32[3,16384]{1,0:T(4,128)}, u32[]{:S(2)}) copy-start(f32[3,16384]{1,0:T(4,128)} %pos.1) | copy-start | bytes 589828
  2.6 18.4 %copy-start = (f32[5,72,512]{2,1,0:T(8,128)S(1)}, f32[5,72,512]{2,1,0:T(8,128)}, u32[]{:S(2)}) copy-start(f32[5,72,512]{2,1,0:T(8,128)} %get-tuple-element.29.early.pressure) | copy-start | bytes 2211844
  2.6 18.3 %collective-permute-start.2 = (f32[5,72,512]{2,1,0:T(8,128)}, f32[5,72,512]{2,1,0:T(8,128)S(1)}, u32[]{:S(2)}, u32[]{:S(2)}) collective-permute-start(f32[5,72,512]{2,1,0:T(8,128)} %get-tuple-element.29.early.pressure), channel_id=1, source_target_pairs={{8,1},{9,0},{10,3},{11,2},{12,5},{13,4},{14,7},{15,6},{24,17},{25,... | collective-permute-start | bytes 2211848 | tf_op jit(solution)/shard_map/ppermute | solution.py:542
  6.5 14.4 %collective-permute-start.3 = (f32[72,512]{1,0:T(8,128)}, f32[72,512]{1,0:T(8,128)S(1)}, u32[]{:S(2)}, u32[]{:S(2)}) collective-permute-start(f32[72,512]{1,0:T(8,128)} %get-tuple-element.35), channel_id=1, source_target_pairs={{9,3},{10,0},{11,5},{12,2},{13,7},{14,4},{25,19},{26,16},{27,21},{... | collective-permute-start | bytes 442376 | tf_op jit(solution)/shard_map/ppermute | solution.py:542
  8.5 27.6 %copy-start.9 = (s32[128]{0:T(128)S(1)}, s32[128]{0:T(128)}, u32[]{:S(2)}) copy-start(s32[128]{0:T(128)} %partner.1) | copy-start | bytes 1540
  8.5 27.6 %copy-start.10 = (f32[3,72,512]{2,1,0:T(8,128)S(1)}, f32[3,72,512]{2,1,0:T(8,128)}, u32[]{:S(2)}) copy-start(f32[3,72,512]{2,1,0:T(8,128)} %get-tuple-element.30.late) | copy-start | bytes 1327108
  10.2 10.7 %collective-permute-start.1 = (f32[136,256]{1,0:T(8,128)S(1)}, f32[136,256]{1,0:T(8,128)S(1)}, u32[]{:S(2)}, u32[]{:S(2)}) collective-permute-start(f32[136,256]{1,0:T(8,128)S(1)} %get-tuple-element.28.mine), channel_id=1, source_target_pairs={{0,16},{1,17},{2,18},{3,19},{4,20},{5,21},{6,22},{7,23},{8,0},{9,1... | collective-permute-start | bytes 417800 | tf_op jit(solution)/shard_map/ppermute | solution.py:542
  12.1 8.8 %collective-permute-start = (f32[136,256]{1,0:T(8,128)S(1)}, f32[136,256]{1,0:T(8,128)S(1)}, u32[]{:S(2)}, u32[]{:S(2)}) collective-permute-start(f32[136,256]{1,0:T(8,128)S(1)} %get-tuple-element.28.mine), channel_id=1, source_target_pairs={{0,8},{1,9},{2,10},{3,11},{4,12},{5,13},{6,14},{7,15},{8,16},{9,17... | collective-permute-start | bytes 417800 | tf_op jit(solution)/shard_map/ppermute | solution.py:542
  15.8 7.4 %collective-permute-start.8 = (f32[3,72,512]{2,1,0:T(8,128)}, f32[3,72,512]{2,1,0:T(8,128)S(1)}, u32[]{:S(2)}, u32[]{:S(2)}) collective-permute-start(f32[3,72,512]{2,1,0:T(8,128)} %get-tuple-element.30.late), channel_id=1, source_target_pairs={{8,1},{9,0},{10,3},{11,2},{12,5},{13,4},{14,7},{15,6},{24,17},{25,... | collective-permute-start | bytes 1327112 | tf_op jit(solution)/shard_map/ppermute | solution.py:542
  21.0 20.4 %collective-permute-start.7 = (f32[6,72,512]{2,1,0:T(8,128)S(1)}, f32[6,72,512]{2,1,0:T(8,128)S(1)}, u32[]{:S(2)}, u32[]{:S(2)}) collective-permute-start(f32[6,72,512]{2,1,0:T(8,128)S(1)} %get-tuple-element.40), channel_id=1, source_target_pairs={{0,2},{2,4},{3,1},{4,6},{5,3},{7,5},{16,18},{18,20},{19,17},{20,22... | collective-permute-start | bytes 2654216 | tf_op jit(solution)/shard_map/ppermute | solution.py:542
  21.8 16.3 %collective-permute-start.10 = (f32[440,256]{1,0:T(8,128)S(1)}, f32[440,256]{1,0:T(8,128)S(1)}, u32[]{:S(2)}, u32[]{:S(2)}) collective-permute-start(f32[440,256]{1,0:T(8,128)S(1)} %get-tuple-element.43), channel_id=1, source_target_pairs={{0,1},{1,0},{2,3},{3,2},{4,5},{5,4},{6,7},{7,6},{16,17},{17,16},{1... | collective-permute-start | bytes 1351688 | tf_op jit(solution)/shard_map/ppermute | solution.py:542
  22.5 18.9 %collective-permute-start.6 = (f32[440,256]{1,0:T(8,128)S(1)}, f32[440,256]{1,0:T(8,128)S(1)}, u32[]{:S(2)}, u32[]{:S(2)}) collective-permute-start(f32[440,256]{1,0:T(8,128)S(1)} %get-tuple-element.39), channel_id=1, source_target_pairs={{1,2},{2,1},{3,4},{4,3},{5,6},{6,5},{17,18},{18,17},{19,20},{20,19... | collective-permute-start | bytes 1351688 | tf_op jit(solution)/shard_map/ppermute | solution.py:542
  23.2 18.1 %collective-permute-start.9 = (f32[3,72,512]{2,1,0:T(8,128)S(1)}, f32[3,72,512]{2,1,0:T(8,128)S(1)}, u32[]{:S(2)}, u32[]{:S(2)}) collective-permute-start(f32[3,72,512]{2,1,0:T(8,128)S(1)} %collective-permute-done.8.near_late), channel_id=1, source_target_pairs={{0,2},{2,4},{3,1},{4,6},{5,3},{7,5},{16,18},{18,20},{19,17},{20,22... | collective-permute-start | bytes 1327112 | tf_op jit(solution)/shard_map/ppermute | solution.py:542
  23.9 5.6 %collective-permute-start.4 = (f32[96,128]{1,0:T(8,128)S(1)}, f32[96,128]{1,0:T(8,128)S(1)}, u32[]{:S(2)}, u32[]{:S(2)}) collective-permute-start(f32[96,128]{1,0:T(8,128)S(1)} %get-tuple-element.32.halo_near), channel_id=1, source_target_pairs={{8,9},{9,8},{10,11},{11,10},{12,13},{13,12},{14,15},{15,14}} | collective-permute-start | bytes 147464 | tf_op jit(solution)/shard_map/ppermute | solution.py:542
  29.5 6.6 %collective-permute-start.5 = (f32[96,128]{1,0:T(8,128)S(1)}, f32[96,128]{1,0:T(8,128)S(1)}, u32[]{:S(2)}, u32[]{:S(2)}) collective-permute-start(f32[96,128]{1,0:T(8,128)S(1)} %get-tuple-element.33.halo_far), channel_id=1, source_target_pairs={{9,10},{10,9},{11,12},{12,11},{13,14},{14,13}} | collective-permute-start | bytes 147464 | tf_op jit(solution)/shard_map/ppermute | solution.py:542
  46.4 6.9 %collective-permute-start.11 = (f32[128,384]{1,0:T(8,128)S(1)}, f32[128,384]{1,0:T(8,128)S(1)}, u32[]{:S(2)}, u32[]{:S(2)}) collective-permute-start(f32[128,384]{1,0:T(8,128)S(1)} %get-tuple-element.47), channel_id=1, source_target_pairs={{0,16},{1,17},{2,18},{3,19},{4,20},{5,21},{6,22},{7,23},{16,0},{17... | collective-permute-start | bytes 589832 | tf_op jit(solution)/shard_map/ppermute | solution.py:542
  47.2 9.2 %collective-permute-start.13 = (f32[128,384]{1,0:T(8,128)S(1)}, f32[128,384]{1,0:T(8,128)S(1)}, u32[]{:S(2)}, u32[]{:S(2)}) collective-permute-start(f32[128,384]{1,0:T(8,128)S(1)} %get-tuple-element.48), channel_id=1, source_target_pairs={{16,8},{17,9},{18,10},{19,11},{20,12},{21,13},{22,14},{23,15}} | collective-permute-start | bytes 589832 | tf_op jit(solution)/shard_map/ppermute | solution.py:542
  48.5 7.9 %collective-permute-start.12 = (f32[128,384]{1,0:T(8,128)S(1)}, f32[128,384]{1,0:T(8,128)S(1)}, u32[]{:S(2)}, u32[]{:S(2)}) collective-permute-start(f32[128,384]{1,0:T(8,128)S(1)} %get-tuple-element.48), channel_id=1, source_target_pairs={{0,8},{1,9},{2,10},{3,11},{4,12},{5,13},{6,14},{7,15}} | collective-permute-start | bytes 589832 | tf_op jit(solution)/shard_map/ppermute | solution.py:542
  (2 other events, 7.7 us)

commit v22 on v21

--- a/solution.py
+++ b/solution.py
@@ -102,7 +102,7 @@
         one.wait()
 
 
-def forward_kernel(near, early, _halo, _second, _third, _beyond, out, dummy):
+def forward_kernel(near, early, _halo, _second, _third, out, dummy):
     dummy[...] = jnp.zeros(dummy.shape, F32)
     count = near.shape[0]
     out[:count] = near[...]
@@ -594,8 +594,8 @@
     came_near = along_reg(halo_near, others, (1, -1))
     came_far = along_reg(halo_far, others, (-1, 1))
     far, after_forward = call(
-        forward_kernel, (shaped(planes + HEAD + 1, height, width), small), [VMEM] * 6,
-        (near, early, after_halo, second, third, beyond), size=5 * field_bytes,
+        forward_kernel, (shaped(planes + HEAD + 1, height, width), small), [VMEM] * 5,
+        (near, early, after_halo, second, third), size=5 * field_bytes,
     )
     far = along_reg(far, owners, (2, -2))
     far_late = along_reg(near_late, owners, (2, -2))

time: 57.9 us -> 59.8 us (1.033)
  the two profiles are of different devices: /device:TPU:17 before, /device:TPU:1 now
where the time goes in v22:
time: 59.8 us; the launch traced here: 59.4 us
  Pallas kernels  22.2 us (37%)
  starting transfers between devices  21.7 us (36%)
  waiting for transfers between devices  14.3 us (24%)
  between operations  1.11 us (2%)
    pallas_call x11, Pallas kernels, call(): pl.pallas_call(kernel, out_shape=outs, in_specs=specs, out_specs=jax.tree...  22.2 us
    ppermute x14, starting transfers between devices, send(): return lax.ppermute(value, ('grp', 'reg'), flat)  21.7 us
    ppermute x14, waiting for transfers between devices, send(): return lax.ppermute(value, ('grp', 'reg'), flat)  14.3 us
  transfers between devices with their start and end apart: 14, of which 2 were waited for; matrix products, arithmetic and copies ran while one was open for 0% of the time, Pallas kernels for 23%

profile of v22, /device:TPU:1, one launch (start us, length us, event | category | flops | bytes accessed | tf_op | source)
XLA Modules:
  0.0 59.4 jit_solution(7969276595499795375)
XLA Ops:
  0.0 2.5 %shard_map.137 = (f32[5,72,512]{2,1,0:T(8,128)}, f32[3,72,512]{2,1,0:T(8,128)}, f32[72,512]{1,0:T(8,128)}) custom-call(f32[4,128,512]{2,1,0:T(8,128)} %pressure_old.1, f32[4,128,512]{2,1,0:T(8,128)} %source.1, f32[4,128,512]{2,1,0:T(8,128)} %solid_before.1), custom_call_target="tpu_custom_call" | custom-call | flops 589824 | bytes 3538944 | tf_op jit(solution)/shard_map/pallas_call | solution.py:36
  2.6 4.7 %collective-permute-start.2 = (f32[5,72,512]{2,1,0:T(8,128)}, f32[5,72,512]{2,1,0:T(8,128)S(1)}, u32[]{:S(2)}, u32[]{:S(2)}) collective-permute-start(f32[5,72,512]{2,1,0:T(8,128)} %get-tuple-element.29.early.pressure), channel_id=1, source_target_pairs={{8,1},{9,0},{10,3},{11,2},{12,5},{13,4},{14,7},{15,6},{24,17},{25,... | collective-permute-start | bytes 2211848 | tf_op jit(solution)/shard_map/ppermute | solution.py:542
  8.0 1.7 %shard_map.136 = (f32[136,256]{1,0:T(8,128)S(1)}, f32[8,128]{1,0:T(8,128)S(1)}) custom-call(s32[1]{0:T(128)S(6)} %copy.15.count, s32[128,128]{1,0:T(8,128)S(1)} %bitcast.4, f32[128,128]{1,0:T(8,128)S(1)} %bitcast.6, f32[128,128]{1,0:T(8,128)S(1)} %bitcast.8, s32[1,128]{1,0:T(1,128)S(1)} %bitcast.10), custom_call_target="tpu_custom_call" | custom-call | flops 201326592 | bytes 327680 | tf_op jit(solution)/shard_map/pallas_call | solution.py:36
  9.7 1.9 %collective-permute-start.1 = (f32[136,256]{1,0:T(8,128)S(1)}, f32[136,256]{1,0:T(8,128)S(1)}, u32[]{:S(2)}, u32[]{:S(2)}) collective-permute-start(f32[136,256]{1,0:T(8,128)S(1)} %get-tuple-element.28.mine), channel_id=1, source_target_pairs={{0,16},{1,17},{2,18},{3,19},{4,20},{5,21},{6,22},{7,23},{8,0},{9,1... | collective-permute-start | bytes 417800 | tf_op jit(solution)/shard_map/ppermute | solution.py:542
  11.6 3.6 %collective-permute-start = (f32[136,256]{1,0:T(8,128)S(1)}, f32[136,256]{1,0:T(8,128)S(1)}, u32[]{:S(2)}, u32[]{:S(2)}) collective-permute-start(f32[136,256]{1,0:T(8,128)S(1)} %get-tuple-element.28.mine), channel_id=1, source_target_pairs={{0,8},{1,9},{2,10},{3,11},{4,12},{5,13},{6,14},{7,15},{8,16},{9,17... | collective-permute-start | bytes 417800 | tf_op jit(solution)/shard_map/ppermute | solution.py:542
  15.3 1.3 %collective-permute-start.7 = (f32[3,72,512]{2,1,0:T(8,128)}, f32[3,72,512]{2,1,0:T(8,128)S(1)}, u32[]{:S(2)}, u32[]{:S(2)}) collective-permute-start(f32[3,72,512]{2,1,0:T(8,128)} %get-tuple-element.30.late), channel_id=1, source_target_pairs={{8,1},{9,0},{10,3},{11,2},{12,5},{13,4},{14,7},{15,6},{24,17},{25,... | collective-permute-start | bytes 1327112 | tf_op jit(solution)/shard_map/ppermute | solution.py:542
  16.7 3.2 %shard_map.138 = (f32[384,128]{1,0:T(8,128)S(1)}, f32[96,128]{1,0:T(8,128)S(1)}, f32[96,128]{1,0:T(8,128)S(1)}, f32[8,128]{1,0:T(8,128)S(1)}) custom-call(f32[3,16384]{1,0:T(4,128)S(1)} %copy-done.4, f32[3,16384]{1,0:T(4,128)S(1)} %copy-done.1, s32[2,4096]{1,0:T(2,128)S(1)} %copy-done.8, f32[8,128]{1,0:T(8,128)S(1)} %get-tuple-element.31._), custom_call_target="tpu_custom_call" | custom-call | flops 16384 | bytes 786432 | tf_op jit(solution)/shard_map/pallas_call | solution.py:36
  20.0 0.7 %collective-permute-start.6 = (f32[6,72,512]{2,1,0:T(8,128)S(1)}, f32[6,72,512]{2,1,0:T(8,128)S(1)}, u32[]{:S(2)}, u32[]{:S(2)}) collective-permute-start(f32[6,72,512]{2,1,0:T(8,128)S(1)} %get-tuple-element.39), channel_id=1, source_target_pairs={{0,2},{2,4},{3,1},{4,6},{5,3},{7,5},{16,18},{18,20},{19,17},{20,22... | collective-permute-start | bytes 2654216 | tf_op jit(solution)/shard_map/ppermute | solution.py:542
  20.8 0.7 %collective-permute-start.9 = (f32[440,256]{1,0:T(8,128)S(1)}, f32[440,256]{1,0:T(8,128)S(1)}, u32[]{:S(2)}, u32[]{:S(2)}) collective-permute-start(f32[440,256]{1,0:T(8,128)S(1)} %get-tuple-element.42), channel_id=1, source_target_pairs={{0,1},{1,0},{2,3},{3,2},{4,5},{5,4},{6,7},{7,6},{16,17},{17,16},{1... | collective-permute-start | bytes 1351688 | tf_op jit(solution)/shard_map/ppermute | solution.py:542
  21.5 0.7 %collective-permute-start.5 = (f32[440,256]{1,0:T(8,128)S(1)}, f32[440,256]{1,0:T(8,128)S(1)}, u32[]{:S(2)}, u32[]{:S(2)}) collective-permute-start(f32[440,256]{1,0:T(8,128)S(1)} %get-tuple-element.38), channel_id=1, source_target_pairs={{1,2},{2,1},{3,4},{4,3},{5,6},{6,5},{17,18},{18,17},{19,20},{20,19... | collective-permute-start | bytes 1351688 | tf_op jit(solution)/shard_map/ppermute | solution.py:542
  22.2 0.7 %collective-permute-start.8 = (f32[3,72,512]{2,1,0:T(8,128)S(1)}, f32[3,72,512]{2,1,0:T(8,128)S(1)}, u32[]{:S(2)}, u32[]{:S(2)}) collective-permute-start(f32[3,72,512]{2,1,0:T(8,128)S(1)} %collective-permute-done.7.near_late), channel_id=1, source_target_pairs={{0,2},{2,4},{3,1},{4,6},{5,3},{7,5},{16,18},{18,20},{19,17},{20,22... | collective-permute-start | bytes 1327112 | tf_op jit(solution)/shard_map/ppermute | solution.py:542
  22.9 2.6 %collective-permute-start.3 = (f32[96,128]{1,0:T(8,128)S(1)}, f32[96,128]{1,0:T(8,128)S(1)}, u32[]{:S(2)}, u32[]{:S(2)}) collective-permute-start(f32[96,128]{1,0:T(8,128)S(1)} %get-tuple-element.32.halo_near), channel_id=1, source_target_pairs={{8,9},{9,8},{10,11},{11,10},{12,13},{13,12},{14,15},{15,14}} | collective-permute-start | bytes 147464 | tf_op jit(solution)/shard_map/ppermute | solution.py:542
  25.6 3.0 %collective-permute-done.3._near.halo_near = f32[96,128]{1,0:T(8,128)S(1)} collective-permute-done((f32[96,128]{1,0:T(8,128)S(1)}, f32[96,128]{1,0:T(8,128)S(1)}, u32[]{:S(2)}, u32[]{:S(2)}) %collective-permute-start.3) | collective-permute-done | bytes 49184 | tf_op jit(solution)/shard_map/ppermute | solution.py:542
  28.6 0.7 %collective-permute-start.4 = (f32[96,128]{1,0:T(8,128)S(1)}, f32[96,128]{1,0:T(8,128)S(1)}, u32[]{:S(2)}, u32[]{:S(2)}) collective-permute-start(f32[96,128]{1,0:T(8,128)S(1)} %get-tuple-element.33.halo_far), channel_id=1, source_target_pairs={{9,10},{10,9},{11,12},{12,11},{13,14},{14,13}} | collective-permute-start | bytes 147464 | tf_op jit(solution)/shard_map/ppermute | solution.py:542
  29.2 0.7 %collective-permute-start.10 = (f32[72,512]{1,0:T(8,128)S(1)}, f32[72,512]{1,0:T(8,128)S(1)}, u32[]{:S(2)}, u32[]{:S(2)}) collective-permute-start(f32[72,512]{1,0:T(8,128)S(1)} %copy-done.12), channel_id=1, source_target_pairs={{9,3},{10,0},{11,5},{12,2},{13,7},{14,4},{25,19},{26,16},{27,21},{... | collective-permute-start | bytes 442376 | tf_op jit(solution)/shard_map/ppermute | solution.py:542
  29.9 1.9 %shard_map.141 = (f32[4,72,512]{2,1,0:T(8,128)S(1)}, f32[4,72,512]{2,1,0:T(8,128)S(1)}, f32[128,128]{1,0:T(8,128)S(1)}, bf16[384,1152]{1,0:T(8,128)(2,1)S(1)}) custom-call(f32[136,256]{1,0:T(8,128)S(1)} %get-tuple-element.28.mine, f32[136,256]{1,0:T(8,128)S(1)} %collective-permute-done._second.second, f32[136,256]{1,0:T(8,128)S(1)} %collective-permute-done.1._third.third, ...), custom_call_target="tpu_custom_call" | custom-call | flops 679477248 | bytes 5308416 | tf_op jit(solution)/shard_map/pallas_call | solution.py:36
  31.9 3.3 %shard_map.142 = (f32[4,72,512]{2,1,0:T(8,128)S(1)}, f32[4,72,512]{2,1,0:T(8,128)S(1)}) custom-call(f32[440,256]{1,0:T(8,128)S(1)} %collective-permute-done.9.message.message_near, f32[5,72,512]{2,1,0:T(8,128)S(1)} %copy-done, f32[5,72,512]{2,1,0:T(8,128)S(1)} %collective-permute-done.2.near, f32[3,72,512]{2,1,0:T(8,128)S(1)} %collective-permute-done.7.near_late, ...), custom_call_target="tpu_custom_call" | custom-call | flops 679477248 | bytes 5308416 | tf_op jit(solution)/shard_map/pallas_call | solution.py:36
  35.2 5.0 %shard_map.143 = (f32[128,384]{1,0:T(8,128)S(1)}, f32[128,384]{1,0:T(8,128)S(1)}, bf16[1152,768]{1,0:T(8,128)(2,1)S(1)}) custom-call(bf16[384,1152]{1,0:T(8,128)(2,1)S(1)} %get-tuple-element.37.picks, f32[440,256]{1,0:T(8,128)S(1)} %collective-permute-done.5.message.message_far, f32[5,72,512]{2,1,0:T(8,128)S(1)} %copy-done, ...), custom_call_target="tpu_custom_call" | custom-call | flops 679477248 | bytes 5308416 | tf_op jit(solution)/shard_map/pallas_call | solution.py:36
  40.2 0.8 %collective-permute-start.11 = (f32[128,384]{1,0:T(8,128)S(1)}, f32[128,384]{1,0:T(8,128)S(1)}, u32[]{:S(2)}, u32[]{:S(2)}) collective-permute-start(f32[128,384]{1,0:T(8,128)S(1)} %get-tuple-element.47), channel_id=1, source_target_pairs={{0,16},{1,17},{2,18},{3,19},{4,20},{5,21},{6,22},{7,23},{16,0},{17... | collective-permute-start | bytes 589832 | tf_op jit(solution)/shard_map/ppermute | solution.py:542
  41.0 1.3 %collective-permute-start.13 = (f32[128,384]{1,0:T(8,128)S(1)}, f32[128,384]{1,0:T(8,128)S(1)}, u32[]{:S(2)}, u32[]{:S(2)}) collective-permute-start(f32[128,384]{1,0:T(8,128)S(1)} %get-tuple-element.48), channel_id=1, source_target_pairs={{16,8},{17,9},{18,10},{19,11},{20,12},{21,13},{22,14},{23,15}} | collective-permute-start | bytes 589832 | tf_op jit(solution)/shard_map/ppermute | solution.py:542
  42.3 1.3 %collective-permute-start.12 = (f32[128,384]{1,0:T(8,128)S(1)}, f32[128,384]{1,0:T(8,128)S(1)}, u32[]{:S(2)}, u32[]{:S(2)}) collective-permute-start(f32[128,384]{1,0:T(8,128)S(1)} %get-tuple-element.48), channel_id=1, source_target_pairs={{0,8},{1,9},{2,10},{3,11},{4,12},{5,13},{6,14},{7,15}} | collective-permute-start | bytes 589832 | tf_op jit(solution)/shard_map/ppermute | solution.py:542
  44.1 3.0 %shard_map.145.contact = f32[384,128]{1,0:T(8,128)S(1)} custom-call(s32[128]{0:T(128)S(1)} %copy-done.9, f32[384,128]{1,0:T(8,128)S(1)} %get-tuple-element.50.state, f32[440,256]{1,0:T(8,128)S(1)} %collective-permute-done.9.message.message_near, f32[440,256]{1,0:T(8,128)S(1)} %collective-permute-done.5.message.message_far, ...), custom_call_target="tpu_custom_call" | custom-call | flops 7864320 | bytes 1310720 | tf_op jit(solution)/shard_map/pallas_call | solution.py:36
  47.1 11.2 %collective-permute-done.13.grads_d = f32[128,384]{1,0:T(8,128)S(1)} collective-permute-done((f32[128,384]{1,0:T(8,128)S(1)}, f32[128,384]{1,0:T(8,128)S(1)}, u32[]{:S(2)}, u32[]{:S(2)}) %collective-permute-start.13) | collective-permute-done | bytes 196640 | tf_op jit(solution)/shard_map/ppermute | solution.py:542
  58.4 1.0 %shard_map.146 = f32[3,16384]{1,0:T(4,128)} custom-call(s32[1]{0:T(128)S(6)} %copy.15.count, f32[128,384]{1,0:T(8,128)S(1)} %shard_map.144._.grads_a, f32[128,384]{1,0:T(8,128)S(1)} %collective-permute-done.11.grads_b, f32[128,384]{1,0:T(8,128)S(1)} %collective-permute-done.12.grads_c, f32[128,384]{1,0:T(8,128)S(1)} %collective-permute-done.13.grads_d, ...), custom_call_target="tpu_custom_call" | custom-call | flops 983040 | bytes 1310720 | tf_op jit(solution)/shard_map/pallas_call | solution.py:36
  (41 shorter events, 0.6 us)
Async XLA Ops:
  0.0 8.0 %copy-start.5 = (s32[16384]{0:T(1024)S(1)}, s32[16384]{0:T(1024)}, u32[]{:S(2)}) copy-start(s32[16384]{0:T(1024)} %param.23) | copy-start | bytes 196612
  0.0 8.0 %copy-start.7 = (f32[16384]{0:T(1024)S(1)}, f32[16384]{0:T(1024)}, u32[]{:S(2)}) copy-start(f32[16384]{0:T(1024)} %param.17) | copy-start | bytes 196612
  0.0 8.0 %copy-start.6 = (f32[16384]{0:T(1024)S(1)}, f32[16384]{0:T(1024)}, u32[]{:S(2)}) copy-start(f32[16384]{0:T(1024)} %param.16) | copy-start | bytes 196612
  0.0 16.6 %copy-start.1 = (f32[3,16384]{1,0:T(4,128)S(1)}, f32[3,16384]{1,0:T(4,128)}, u32[]{:S(2)}) copy-start(f32[3,16384]{1,0:T(4,128)} %vel.3) | copy-start | bytes 589828
  0.0 16.6 %copy-start.8 = (s32[2,4096]{1,0:T(2,128)S(1)}, s32[2,4096]{1,0:T(2,128)}, u32[]{:S(2)}) copy-start(s32[2,4096]{1,0:T(2,128)} %lists.1) | copy-start | bytes 98308
  0.0 16.6 %copy-start.4 = (f32[3,16384]{1,0:T(4,128)S(1)}, f32[3,16384]{1,0:T(4,128)}, u32[]{:S(2)}) copy-start(f32[3,16384]{1,0:T(4,128)} %pos.1) | copy-start | bytes 589828
  2.6 17.4 %copy-start = (f32[5,72,512]{2,1,0:T(8,128)S(1)}, f32[5,72,512]{2,1,0:T(8,128)}, u32[]{:S(2)}) copy-start(f32[5,72,512]{2,1,0:T(8,128)} %get-tuple-element.29.early.pressure) | copy-start | bytes 2211844
  2.6 17.3 %collective-permute-start.2 = (f32[5,72,512]{2,1,0:T(8,128)}, f32[5,72,512]{2,1,0:T(8,128)S(1)}, u32[]{:S(2)}, u32[]{:S(2)}) collective-permute-start(f32[5,72,512]{2,1,0:T(8,128)} %get-tuple-element.29.early.pressure), channel_id=1, source_target_pairs={{8,1},{9,0},{10,3},{11,2},{12,5},{13,4},{14,7},{15,6},{24,17},{25,... | collective-permute-start | bytes 2211848 | tf_op jit(solution)/shard_map/ppermute | solution.py:542
  8.0 21.2 %copy-start.12 = (f32[72,512]{1,0:T(8,128)S(1)}, f32[72,512]{1,0:T(8,128)}, u32[]{:S(2)}) copy-start(f32[72,512]{1,0:T(8,128)} %get-tuple-element.43) | copy-start | bytes 442372
  8.0 21.9 %copy-start.9 = (s32[128]{0:T(128)S(1)}, s32[128]{0:T(128)}, u32[]{:S(2)}) copy-start(s32[128]{0:T(128)} %partner.1) | copy-start | bytes 1540
  8.0 21.9 %copy-start.10 = (f32[3,72,512]{2,1,0:T(8,128)S(1)}, f32[3,72,512]{2,1,0:T(8,128)}, u32[]{:S(2)}) copy-start(f32[3,72,512]{2,1,0:T(8,128)} %get-tuple-element.30.late) | copy-start | bytes 1327108
  9.7 10.2 %collective-permute-start.1 = (f32[136,256]{1,0:T(8,128)S(1)}, f32[136,256]{1,0:T(8,128)S(1)}, u32[]{:S(2)}, u32[]{:S(2)}) collective-permute-start(f32[136,256]{1,0:T(8,128)S(1)} %get-tuple-element.28.mine), channel_id=1, source_target_pairs={{0,16},{1,17},{2,18},{3,19},{4,20},{5,21},{6,22},{7,23},{8,0},{9,1... | collective-permute-start | bytes 417800 | tf_op jit(solution)/shard_map/ppermute | solution.py:542
  11.6 8.3 %collective-permute-start = (f32[136,256]{1,0:T(8,128)S(1)}, f32[136,256]{1,0:T(8,128)S(1)}, u32[]{:S(2)}, u32[]{:S(2)}) collective-permute-start(f32[136,256]{1,0:T(8,128)S(1)} %get-tuple-element.28.mine), channel_id=1, source_target_pairs={{0,8},{1,9},{2,10},{3,11},{4,12},{5,13},{6,14},{7,15},{8,16},{9,17... | collective-permute-start | bytes 417800 | tf_op jit(solution)/shard_map/ppermute | solution.py:542
  15.3 6.9 %collective-permute-start.7 = (f32[3,72,512]{2,1,0:T(8,128)}, f32[3,72,512]{2,1,0:T(8,128)S(1)}, u32[]{:S(2)}, u32[]{:S(2)}) collective-permute-start(f32[3,72,512]{2,1,0:T(8,128)} %get-tuple-element.30.late), channel_id=1, source_target_pairs={{8,1},{9,0},{10,3},{11,2},{12,5},{13,4},{14,7},{15,6},{24,17},{25,... | collective-permute-start | bytes 1327112 | tf_op jit(solution)/shard_map/ppermute | solution.py:542
  20.0 15.2 %collective-permute-start.6 = (f32[6,72,512]{2,1,0:T(8,128)S(1)}, f32[6,72,512]{2,1,0:T(8,128)S(1)}, u32[]{:S(2)}, u32[]{:S(2)}) collective-permute-start(f32[6,72,512]{2,1,0:T(8,128)S(1)} %get-tuple-element.39), channel_id=1, source_target_pairs={{0,2},{2,4},{3,1},{4,6},{5,3},{7,5},{16,18},{18,20},{19,17},{20,22... | collective-permute-start | bytes 2654216 | tf_op jit(solution)/shard_map/ppermute | solution.py:542
  20.8 11.1 %collective-permute-start.9 = (f32[440,256]{1,0:T(8,128)S(1)}, f32[440,256]{1,0:T(8,128)S(1)}, u32[]{:S(2)}, u32[]{:S(2)}) collective-permute-start(f32[440,256]{1,0:T(8,128)S(1)} %get-tuple-element.42), channel_id=1, source_target_pairs={{0,1},{1,0},{2,3},{3,2},{4,5},{5,4},{6,7},{7,6},{16,17},{17,16},{1... | collective-permute-start | bytes 1351688 | tf_op jit(solution)/shard_map/ppermute | solution.py:542
  21.5 13.7 %collective-permute-start.5 = (f32[440,256]{1,0:T(8,128)S(1)}, f32[440,256]{1,0:T(8,128)S(1)}, u32[]{:S(2)}, u32[]{:S(2)}) collective-permute-start(f32[440,256]{1,0:T(8,128)S(1)} %get-tuple-element.38), channel_id=1, source_target_pairs={{1,2},{2,1},{3,4},{4,3},{5,6},{6,5},{17,18},{18,17},{19,20},{20,19... | collective-permute-start | bytes 1351688 | tf_op jit(solution)/shard_map/ppermute | solution.py:542
  22.2 13.0 %collective-permute-start.8 = (f32[3,72,512]{2,1,0:T(8,128)S(1)}, f32[3,72,512]{2,1,0:T(8,128)S(1)}, u32[]{:S(2)}, u32[]{:S(2)}) collective-permute-start(f32[3,72,512]{2,1,0:T(8,128)S(1)} %collective-permute-done.7.near_late), channel_id=1, source_target_pairs={{0,2},{2,4},{3,1},{4,6},{5,3},{7,5},{16,18},{18,20},{19,17},{20,22... | collective-permute-start | bytes 1327112 | tf_op jit(solution)/shard_map/ppermute | solution.py:542
  22.9 5.7 %collective-permute-start.3 = (f32[96,128]{1,0:T(8,128)S(1)}, f32[96,128]{1,0:T(8,128)S(1)}, u32[]{:S(2)}, u32[]{:S(2)}) collective-permute-start(f32[96,128]{1,0:T(8,128)S(1)} %get-tuple-element.32.halo_near), channel_id=1, source_target_pairs={{8,9},{9,8},{10,11},{11,10},{12,13},{13,12},{14,15},{15,14}} | collective-permute-start | bytes 147464 | tf_op jit(solution)/shard_map/ppermute | solution.py:542
  28.6 0.7 %collective-permute-start.4 = (f32[96,128]{1,0:T(8,128)S(1)}, f32[96,128]{1,0:T(8,128)S(1)}, u32[]{:S(2)}, u32[]{:S(2)}) collective-permute-start(f32[96,128]{1,0:T(8,128)S(1)} %get-tuple-element.33.halo_far), channel_id=1, source_target_pairs={{9,10},{10,9},{11,12},{12,11},{13,14},{14,13}} | collective-permute-start | bytes 147464 | tf_op jit(solution)/shard_map/ppermute | solution.py:542
  29.2 2.6 %collective-permute-start.10 = (f32[72,512]{1,0:T(8,128)S(1)}, f32[72,512]{1,0:T(8,128)S(1)}, u32[]{:S(2)}, u32[]{:S(2)}) collective-permute-start(f32[72,512]{1,0:T(8,128)S(1)} %copy-done.12), channel_id=1, source_target_pairs={{9,3},{10,0},{11,5},{12,2},{13,7},{14,4},{25,19},{26,16},{27,21},{... | collective-permute-start | bytes 442376 | tf_op jit(solution)/shard_map/ppermute | solution.py:542
  40.2 6.9 %collective-permute-start.11 = (f32[128,384]{1,0:T(8,128)S(1)}, f32[128,384]{1,0:T(8,128)S(1)}, u32[]{:S(2)}, u32[]{:S(2)}) collective-permute-start(f32[128,384]{1,0:T(8,128)S(1)} %get-tuple-element.47), channel_id=1, source_target_pairs={{0,16},{1,17},{2,18},{3,19},{4,20},{5,21},{6,22},{7,23},{16,0},{17... | collective-permute-start | bytes 589832 | tf_op jit(solution)/shard_map/ppermute | solution.py:542
  41.0 17.4 %collective-permute-start.13 = (f32[128,384]{1,0:T(8,128)S(1)}, f32[128,384]{1,0:T(8,128)S(1)}, u32[]{:S(2)}, u32[]{:S(2)}) collective-permute-start(f32[128,384]{1,0:T(8,128)S(1)} %get-tuple-element.48), channel_id=1, source_target_pairs={{16,8},{17,9},{18,10},{19,11},{20,12},{21,13},{22,14},{23,15}} | collective-permute-start | bytes 589832 | tf_op jit(solution)/shard_map/ppermute | solution.py:542
  42.3 16.1 %collective-permute-start.12 = (f32[128,384]{1,0:T(8,128)S(1)}, f32[128,384]{1,0:T(8,128)S(1)}, u32[]{:S(2)}, u32[]{:S(2)}) collective-permute-start(f32[128,384]{1,0:T(8,128)S(1)} %get-tuple-element.48), channel_id=1, source_target_pairs={{0,8},{1,9},{2,10},{3,11},{4,12},{5,13},{6,14},{7,15}} | collective-permute-start | bytes 589832 | tf_op jit(solution)/shard_map/ppermute | solution.py:542
  (3 other events, 15.7 us)

commit v23 on v21

--- a/solution.py
+++ b/solution.py
@@ -277,7 +277,7 @@
             out[pl.ds(axis * tiles + first, SUB), :] = merged(pulls[axis])
         return carry
 
-    lax.fori_loop(0, tiles // SUB, step, 0)
+    lax.fori_loop(0, tiles // SUB, step, 0, unroll=2)
 
 
 def shifted(plane):

time: 57.9 us -> 57.9 us (level)
  waiting for transfers between devices: 10.1 us -> 10.7 us
  Pallas kernels: 22.2 us -> 21.6 us
    ppermute x14, waiting for transfers between devices: 10.1 us -> 10.7 us  [send(): return lax.ppermute(value, ('grp', 'reg'), flat)]
    pallas_call x11, Pallas kernels: 22.2 us -> 21.6 us  [call(): pl.pallas_call(kernel, out_shape=outs, in_specs=specs, out_specs=jax.tree...]
  transfers between devices with their start and end apart: 14 -> 14, of which waited for: 3 -> 3; matrix products, arithmetic and copies ran while one was open for 0% -> 0% of each run, Pallas kernels for 24% -> 23%
where the time goes in v23:
time: 57.9 us; the launch traced here: 57.4 us
  starting transfers between devices  24 us (41%)
  Pallas kernels  21.6 us (37%)
  waiting for transfers between devices  10.7 us (18%)
  between operations  1.07 us (2%)
    ppermute x14, starting transfers between devices, send(): return lax.ppermute(value, ('grp', 'reg'), flat)  24 us
    pallas_call x11, Pallas kernels, call(): pl.pallas_call(kernel, out_shape=outs, in_specs=specs, out_specs=jax.tree...  21.6 us
    ppermute x14, waiting for transfers between devices, send(): return lax.ppermute(value, ('grp', 'reg'), flat)  10.7 us
  transfers between devices with their start and end apart: 14, of which 3 were waited for; matrix products, arithmetic and copies ran while one was open for 0% of the time, Pallas kernels for 23%

profile of v23, /device:TPU:17, one launch (start us, length us, event | category | flops | bytes accessed | tf_op | source)
XLA Modules:
  0.0 57.4 jit_solution(17395669263088337110)
XLA Ops:
  0.0 2.5 %shard_map.137 = (f32[5,72,512]{2,1,0:T(8,128)}, f32[3,72,512]{2,1,0:T(8,128)}, f32[72,512]{1,0:T(8,128)}) custom-call(f32[4,128,512]{2,1,0:T(8,128)} %pressure_old.1, f32[4,128,512]{2,1,0:T(8,128)} %source.1, f32[4,128,512]{2,1,0:T(8,128)} %solid_before.1), custom_call_target="tpu_custom_call" | custom-call | flops 589824 | bytes 3538944 | tf_op jit(solution)/shard_map/pallas_call | solution.py:36
  2.6 3.9 %collective-permute-start.2 = (f32[5,72,512]{2,1,0:T(8,128)}, f32[5,72,512]{2,1,0:T(8,128)S(1)}, u32[]{:S(2)}, u32[]{:S(2)}) collective-permute-start(f32[5,72,512]{2,1,0:T(8,128)} %get-tuple-element.29.early.pressure), channel_id=1, source_target_pairs={{8,1},{9,0},{10,3},{11,2},{12,5},{13,4},{14,7},{15,6},{24,17},{25,... | collective-permute-start | bytes 2211848 | tf_op jit(solution)/shard_map/ppermute | solution.py:542
  6.5 1.3 %collective-permute-start.3 = (f32[72,512]{1,0:T(8,128)}, f32[72,512]{1,0:T(8,128)S(1)}, u32[]{:S(2)}, u32[]{:S(2)}) collective-permute-start(f32[72,512]{1,0:T(8,128)} %get-tuple-element.35), channel_id=1, source_target_pairs={{9,3},{10,0},{11,5},{12,2},{13,7},{14,4},{25,19},{26,16},{27,21},{... | collective-permute-start | bytes 442376 | tf_op jit(solution)/shard_map/ppermute | solution.py:542
  8.5 1.7 %shard_map.136 = (f32[136,256]{1,0:T(8,128)S(1)}, f32[8,128]{1,0:T(8,128)S(1)}) custom-call(s32[1]{0:T(128)S(6)} %copy.15.count, s32[128,128]{1,0:T(8,128)S(1)} %bitcast.4, f32[128,128]{1,0:T(8,128)S(1)} %bitcast.6, f32[128,128]{1,0:T(8,128)S(1)} %bitcast.8, s32[1,128]{1,0:T(1,128)S(1)} %bitcast.10), custom_call_target="tpu_custom_call" | custom-call | flops 201326592 | bytes 327680 | tf_op jit(solution)/shard_map/pallas_call | solution.py:36
  10.2 1.9 %collective-permute-start.1 = (f32[136,256]{1,0:T(8,128)S(1)}, f32[136,256]{1,0:T(8,128)S(1)}, u32[]{:S(2)}, u32[]{:S(2)}) collective-permute-start(f32[136,256]{1,0:T(8,128)S(1)} %get-tuple-element.28.mine), channel_id=1, source_target_pairs={{0,16},{1,17},{2,18},{3,19},{4,20},{5,21},{6,22},{7,23},{8,0},{9,1... | collective-permute-start | bytes 417800 | tf_op jit(solution)/shard_map/ppermute | solution.py:542
  12.1 3.6 %collective-permute-start = (f32[136,256]{1,0:T(8,128)S(1)}, f32[136,256]{1,0:T(8,128)S(1)}, u32[]{:S(2)}, u32[]{:S(2)}) collective-permute-start(f32[136,256]{1,0:T(8,128)S(1)} %get-tuple-element.28.mine), channel_id=1, source_target_pairs={{0,8},{1,9},{2,10},{3,11},{4,12},{5,13},{6,14},{7,15},{8,16},{9,17... | collective-permute-start | bytes 417800 | tf_op jit(solution)/shard_map/ppermute | solution.py:542
  15.8 1.8 %collective-permute-start.8 = (f32[3,72,512]{2,1,0:T(8,128)}, f32[3,72,512]{2,1,0:T(8,128)S(1)}, u32[]{:S(2)}, u32[]{:S(2)}) collective-permute-start(f32[3,72,512]{2,1,0:T(8,128)} %get-tuple-element.30.late), channel_id=1, source_target_pairs={{8,1},{9,0},{10,3},{11,2},{12,5},{13,4},{14,7},{15,6},{24,17},{25,... | collective-permute-start | bytes 1327112 | tf_op jit(solution)/shard_map/ppermute | solution.py:542
  17.6 3.2 %shard_map.138 = (f32[384,128]{1,0:T(8,128)S(1)}, f32[96,128]{1,0:T(8,128)S(1)}, f32[96,128]{1,0:T(8,128)S(1)}, f32[8,128]{1,0:T(8,128)S(1)}) custom-call(f32[3,16384]{1,0:T(4,128)S(1)} %copy-done.4, f32[3,16384]{1,0:T(4,128)S(1)} %copy-done.1, s32[2,4096]{1,0:T(2,128)S(1)} %copy-done.8, f32[8,128]{1,0:T(8,128)S(1)} %get-tuple-element.31._), custom_call_target="tpu_custom_call" | custom-call | flops 16384 | bytes 786432 | tf_op jit(solution)/shard_map/pallas_call | solution.py:36
  21.0 0.7 %collective-permute-start.7 = (f32[6,72,512]{2,1,0:T(8,128)S(1)}, f32[6,72,512]{2,1,0:T(8,128)S(1)}, u32[]{:S(2)}, u32[]{:S(2)}) collective-permute-start(f32[6,72,512]{2,1,0:T(8,128)S(1)} %get-tuple-element.40), channel_id=1, source_target_pairs={{0,2},{2,4},{3,1},{4,6},{5,3},{7,5},{16,18},{18,20},{19,17},{20,22... | collective-permute-start | bytes 2654216 | tf_op jit(solution)/shard_map/ppermute | solution.py:542
  21.8 0.7 %collective-permute-start.10 = (f32[440,256]{1,0:T(8,128)S(1)}, f32[440,256]{1,0:T(8,128)S(1)}, u32[]{:S(2)}, u32[]{:S(2)}) collective-permute-start(f32[440,256]{1,0:T(8,128)S(1)} %get-tuple-element.43), channel_id=1, source_target_pairs={{0,1},{1,0},{2,3},{3,2},{4,5},{5,4},{6,7},{7,6},{16,17},{17,16},{1... | collective-permute-start | bytes 1351688 | tf_op jit(solution)/shard_map/ppermute | solution.py:542
  22.5 0.7 %collective-permute-start.6 = (f32[440,256]{1,0:T(8,128)S(1)}, f32[440,256]{1,0:T(8,128)S(1)}, u32[]{:S(2)}, u32[]{:S(2)}) collective-permute-start(f32[440,256]{1,0:T(8,128)S(1)} %get-tuple-element.39), channel_id=1, source_target_pairs={{1,2},{2,1},{3,4},{4,3},{5,6},{6,5},{17,18},{18,17},{19,20},{20,19... | collective-permute-start | bytes 1351688 | tf_op jit(solution)/shard_map/ppermute | solution.py:542
  23.9 2.6 %collective-permute-start.4 = (f32[96,128]{1,0:T(8,128)S(1)}, f32[96,128]{1,0:T(8,128)S(1)}, u32[]{:S(2)}, u32[]{:S(2)}) collective-permute-start(f32[96,128]{1,0:T(8,128)S(1)} %get-tuple-element.32.halo_near), channel_id=1, source_target_pairs={{8,9},{9,8},{10,11},{11,10},{12,13},{13,12},{14,15},{15,14}} | collective-permute-start | bytes 147464 | tf_op jit(solution)/shard_map/ppermute | solution.py:542
  26.6 3.0 %collective-permute-done.4._near.halo_near = f32[96,128]{1,0:T(8,128)S(1)} collective-permute-done((f32[96,128]{1,0:T(8,128)S(1)}, f32[96,128]{1,0:T(8,128)S(1)}, u32[]{:S(2)}, u32[]{:S(2)}) %collective-permute-start.4) | collective-permute-done | bytes 49184 | tf_op jit(solution)/shard_map/ppermute | solution.py:542
  29.5 2.6 %collective-permute-start.5 = (f32[96,128]{1,0:T(8,128)S(1)}, f32[96,128]{1,0:T(8,128)S(1)}, u32[]{:S(2)}, u32[]{:S(2)}) collective-permute-start(f32[96,128]{1,0:T(8,128)S(1)} %get-tuple-element.33.halo_far), channel_id=1, source_target_pairs={{9,10},{10,9},{11,12},{12,11},{13,14},{14,13}} | collective-permute-start | bytes 147464 | tf_op jit(solution)/shard_map/ppermute | solution.py:542
  32.1 4.0 %collective-permute-done.5._far.halo_far = f32[96,128]{1,0:T(8,128)S(1)} collective-permute-done((f32[96,128]{1,0:T(8,128)S(1)}, f32[96,128]{1,0:T(8,128)S(1)}, u32[]{:S(2)}, u32[]{:S(2)}) %collective-permute-start.5) | collective-permute-done | bytes 49184 | tf_op jit(solution)/shard_map/ppermute | solution.py:542
  36.1 1.9 %shard_map.141 = (f32[4,72,512]{2,1,0:T(8,128)S(1)}, f32[4,72,512]{2,1,0:T(8,128)S(1)}, f32[128,128]{1,0:T(8,128)S(1)}, bf16[384,1152]{1,0:T(8,128)(2,1)S(1)}) custom-call(f32[136,256]{1,0:T(8,128)S(1)} %get-tuple-element.28.mine, f32[136,256]{1,0:T(8,128)S(1)} %collective-permute-done._second.second, f32[136,256]{1,0:T(8,128)S(1)} %collective-permute-done.1._third.third, ...), custom_call_target="tpu_custom_call" | custom-call | flops 679477248 | bytes 5308416 | tf_op jit(solution)/shard_map/pallas_call | solution.py:36
  38.1 3.3 %shard_map.142 = (f32[4,72,512]{2,1,0:T(8,128)S(1)}, f32[4,72,512]{2,1,0:T(8,128)S(1)}) custom-call(f32[440,256]{1,0:T(8,128)S(1)} %collective-permute-done.10.message.message_near, f32[5,72,512]{2,1,0:T(8,128)S(1)} %copy-done, f32[5,72,512]{2,1,0:T(8,128)S(1)} %collective-permute-done.2.near, f32[3,72,512]{2,1,0:T(8,128)S(1)} %collective-permute-done.8.near_late, ...), custom_call_target="tpu_custom_call" | custom-call | flops 679477248 | bytes 5308416 | tf_op jit(solution)/shard_map/pallas_call | solution.py:36
  41.4 5.0 %shard_map.143 = (f32[128,384]{1,0:T(8,128)S(1)}, f32[128,384]{1,0:T(8,128)S(1)}, bf16[1152,768]{1,0:T(8,128)(2,1)S(1)}) custom-call(bf16[384,1152]{1,0:T(8,128)(2,1)S(1)} %get-tuple-element.38.picks, f32[440,256]{1,0:T(8,128)S(1)} %collective-permute-done.6.message.message_far, f32[5,72,512]{2,1,0:T(8,128)S(1)} %copy-done, ...), custom_call_target="tpu_custom_call" | custom-call | flops 679477248 | bytes 5308416 | tf_op jit(solution)/shard_map/pallas_call | solution.py:36
  46.4 0.8 %collective-permute-start.11 = (f32[128,384]{1,0:T(8,128)S(1)}, f32[128,384]{1,0:T(8,128)S(1)}, u32[]{:S(2)}, u32[]{:S(2)}) collective-permute-start(f32[128,384]{1,0:T(8,128)S(1)} %get-tuple-element.47), channel_id=1, source_target_pairs={{0,16},{1,17},{2,18},{3,19},{4,20},{5,21},{6,22},{7,23},{16,0},{17... | collective-permute-start | bytes 589832 | tf_op jit(solution)/shard_map/ppermute | solution.py:542
  47.2 1.3 %collective-permute-start.13 = (f32[128,384]{1,0:T(8,128)S(1)}, f32[128,384]{1,0:T(8,128)S(1)}, u32[]{:S(2)}, u32[]{:S(2)}) collective-permute-start(f32[128,384]{1,0:T(8,128)S(1)} %get-tuple-element.48), channel_id=1, source_target_pairs={{16,8},{17,9},{18,10},{19,11},{20,12},{21,13},{22,14},{23,15}} | collective-permute-start | bytes 589832 | tf_op jit(solution)/shard_map/ppermute | solution.py:542
  48.5 1.3 %collective-permute-start.12 = (f32[128,384]{1,0:T(8,128)S(1)}, f32[128,384]{1,0:T(8,128)S(1)}, u32[]{:S(2)}, u32[]{:S(2)}) collective-permute-start(f32[128,384]{1,0:T(8,128)S(1)} %get-tuple-element.48), channel_id=1, source_target_pairs={{0,8},{1,9},{2,10},{3,11},{4,12},{5,13},{6,14},{7,15}} | collective-permute-start | bytes 589832 | tf_op jit(solution)/shard_map/ppermute | solution.py:542
  50.2 2.4 %shard_map.145.contact = f32[384,128]{1,0:T(8,128)S(1)} custom-call(s32[128]{0:T(128)S(1)} %copy-done.9, f32[384,128]{1,0:T(8,128)S(1)} %get-tuple-element.50.state, f32[440,256]{1,0:T(8,128)S(1)} %collective-permute-done.10.message.message_near, f32[440,256]{1,0:T(8,128)S(1)} %collective-permute-done.6.message.message_far, ...), custom_call_target="tpu_custom_call" | custom-call | flops 7864320 | bytes 1310720 | tf_op jit(solution)/shard_map/pallas_call | solution.py:36
  52.7 3.7 %collective-permute-done.13.grads_d = f32[128,384]{1,0:T(8,128)S(1)} collective-permute-done((f32[128,384]{1,0:T(8,128)S(1)}, f32[128,384]{1,0:T(8,128)S(1)}, u32[]{:S(2)}, u32[]{:S(2)}) %collective-permute-start.13) | collective-permute-done | bytes 196640 | tf_op jit(solution)/shard_map/ppermute | solution.py:542
  56.4 1.0 %shard_map.146 = f32[3,16384]{1,0:T(4,128)} custom-call(s32[1]{0:T(128)S(6)} %copy.15.count, f32[128,384]{1,0:T(8,128)S(1)} %shard_map.144._.grads_a, f32[128,384]{1,0:T(8,128)S(1)} %collective-permute-done.11.grads_b, f32[128,384]{1,0:T(8,128)S(1)} %collective-permute-done.12.grads_c, f32[128,384]{1,0:T(8,128)S(1)} %collective-permute-done.13.grads_d, ...), custom_call_target="tpu_custom_call" | custom-call | flops 983040 | bytes 1310720 | tf_op jit(solution)/shard_map/pallas_call | solution.py:36
  (39 shorter events, 1.3 us)
Async XLA Ops:
  0.0 8.4 %copy-start.11 = (s32[128]{0:T(128)S(1)}, s32[128]{0:T(128)}, u32[]{:S(2)}) copy-start(s32[128]{0:T(128)} %param.24) | copy-start | bytes 1540
  0.0 8.4 %copy-start.5 = (s32[16384]{0:T(1024)S(1)}, s32[16384]{0:T(1024)}, u32[]{:S(2)}) copy-start(s32[16384]{0:T(1024)} %param.23) | copy-start | bytes 196612
  0.0 8.4 %copy-start.7 = (f32[16384]{0:T(1024)S(1)}, f32[16384]{0:T(1024)}, u32[]{:S(2)}) copy-start(f32[16384]{0:T(1024)} %param.17) | copy-start | bytes 196612
  0.0 8.4 %copy-start.6 = (f32[16384]{0:T(1024)S(1)}, f32[16384]{0:T(1024)}, u32[]{:S(2)}) copy-start(f32[16384]{0:T(1024)} %param.16) | copy-start | bytes 196612
  0.0 17.6 %copy-start.1 = (f32[3,16384]{1,0:T(4,128)S(1)}, f32[3,16384]{1,0:T(4,128)}, u32[]{:S(2)}) copy-start(f32[3,16384]{1,0:T(4,128)} %vel.3) | copy-start | bytes 589828
  0.0 17.6 %copy-start.8 = (s32[2,4096]{1,0:T(2,128)S(1)}, s32[2,4096]{1,0:T(2,128)}, u32[]{:S(2)}) copy-start(s32[2,4096]{1,0:T(2,128)} %lists.1) | copy-start | bytes 98308
  0.0 17.6 %copy-start.4 = (f32[3,16384]{1,0:T(4,128)S(1)}, f32[3,16384]{1,0:T(4,128)}, u32[]{:S(2)}) copy-start(f32[3,16384]{1,0:T(4,128)} %pos.1) | copy-start | bytes 589828
  2.6 18.4 %copy-start = (f32[5,72,512]{2,1,0:T(8,128)S(1)}, f32[5,72,512]{2,1,0:T(8,128)}, u32[]{:S(2)}) copy-start(f32[5,72,512]{2,1,0:T(8,128)} %get-tuple-element.29.early.pressure) | copy-start | bytes 2211844
  2.6 18.3 %collective-permute-start.2 = (f32[5,72,512]{2,1,0:T(8,128)}, f32[5,72,512]{2,1,0:T(8,128)S(1)}, u32[]{:S(2)}, u32[]{:S(2)}) collective-permute-start(f32[5,72,512]{2,1,0:T(8,128)} %get-tuple-element.29.early.pressure), channel_id=1, source_target_pairs={{8,1},{9,0},{10,3},{11,2},{12,5},{13,4},{14,7},{15,6},{24,17},{25,... | collective-permute-start | bytes 2211848 | tf_op jit(solution)/shard_map/ppermute | solution.py:542
  6.5 14.4 %collective-permute-start.3 = (f32[72,512]{1,0:T(8,128)}, f32[72,512]{1,0:T(8,128)S(1)}, u32[]{:S(2)}, u32[]{:S(2)}) collective-permute-start(f32[72,512]{1,0:T(8,128)} %get-tuple-element.35), channel_id=1, source_target_pairs={{9,3},{10,0},{11,5},{12,2},{13,7},{14,4},{25,19},{26,16},{27,21},{... | collective-permute-start | bytes 442376 | tf_op jit(solution)/shard_map/ppermute | solution.py:542
  8.5 27.6 %copy-start.9 = (s32[128]{0:T(128)S(1)}, s32[128]{0:T(128)}, u32[]{:S(2)}) copy-start(s32[128]{0:T(128)} %partner.1) | copy-start | bytes 1540
  8.5 27.6 %copy-start.10 = (f32[3,72,512]{2,1,0:T(8,128)S(1)}, f32[3,72,512]{2,1,0:T(8,128)}, u32[]{:S(2)}) copy-start(f32[3,72,512]{2,1,0:T(8,128)} %get-tuple-element.30.late) | copy-start | bytes 1327108
  10.2 10.7 %collective-permute-start.1 = (f32[136,256]{1,0:T(8,128)S(1)}, f32[136,256]{1,0:T(8,128)S(1)}, u32[]{:S(2)}, u32[]{:S(2)}) collective-permute-start(f32[136,256]{1,0:T(8,128)S(1)} %get-tuple-element.28.mine), channel_id=1, source_target_pairs={{0,16},{1,17},{2,18},{3,19},{4,20},{5,21},{6,22},{7,23},{8,0},{9,1... | collective-permute-start | bytes 417800 | tf_op jit(solution)/shard_map/ppermute | solution.py:542
  12.1 8.8 %collective-permute-start = (f32[136,256]{1,0:T(8,128)S(1)}, f32[136,256]{1,0:T(8,128)S(1)}, u32[]{:S(2)}, u32[]{:S(2)}) collective-permute-start(f32[136,256]{1,0:T(8,128)S(1)} %get-tuple-element.28.mine), channel_id=1, source_target_pairs={{0,8},{1,9},{2,10},{3,11},{4,12},{5,13},{6,14},{7,15},{8,16},{9,17... | collective-permute-start | bytes 417800 | tf_op jit(solution)/shard_map/ppermute | solution.py:542
  15.8 7.4 %collective-permute-start.8 = (f32[3,72,512]{2,1,0:T(8,128)}, f32[3,72,512]{2,1,0:T(8,128)S(1)}, u32[]{:S(2)}, u32[]{:S(2)}) collective-permute-start(f32[3,72,512]{2,1,0:T(8,128)} %get-tuple-element.30.late), channel_id=1, source_target_pairs={{8,1},{9,0},{10,3},{11,2},{12,5},{13,4},{14,7},{15,6},{24,17},{25,... | collective-permute-start | bytes 1327112 | tf_op jit(solution)/shard_map/ppermute | solution.py:542
  21.0 20.4 %collective-permute-start.7 = (f32[6,72,512]{2,1,0:T(8,128)S(1)}, f32[6,72,512]{2,1,0:T(8,128)S(1)}, u32[]{:S(2)}, u32[]{:S(2)}) collective-permute-start(f32[6,72,512]{2,1,0:T(8,128)S(1)} %get-tuple-element.40), channel_id=1, source_target_pairs={{0,2},{2,4},{3,1},{4,6},{5,3},{7,5},{16,18},{18,20},{19,17},{20,22... | collective-permute-start | bytes 2654216 | tf_op jit(solution)/shard_map/ppermute | solution.py:542
  21.8 16.3 %collective-permute-start.10 = (f32[440,256]{1,0:T(8,128)S(1)}, f32[440,256]{1,0:T(8,128)S(1)}, u32[]{:S(2)}, u32[]{:S(2)}) collective-permute-start(f32[440,256]{1,0:T(8,128)S(1)} %get-tuple-element.43), channel_id=1, source_target_pairs={{0,1},{1,0},{2,3},{3,2},{4,5},{5,4},{6,7},{7,6},{16,17},{17,16},{1... | collective-permute-start | bytes 1351688 | tf_op jit(solution)/shard_map/ppermute | solution.py:542
  22.5 18.9 %collective-permute-start.6 = (f32[440,256]{1,0:T(8,128)S(1)}, f32[440,256]{1,0:T(8,128)S(1)}, u32[]{:S(2)}, u32[]{:S(2)}) collective-permute-start(f32[440,256]{1,0:T(8,128)S(1)} %get-tuple-element.39), channel_id=1, source_target_pairs={{1,2},{2,1},{3,4},{4,3},{5,6},{6,5},{17,18},{18,17},{19,20},{20,19... | collective-permute-start | bytes 1351688 | tf_op jit(solution)/shard_map/ppermute | solution.py:542
  23.2 18.1 %collective-permute-start.9 = (f32[3,72,512]{2,1,0:T(8,128)S(1)}, f32[3,72,512]{2,1,0:T(8,128)S(1)}, u32[]{:S(2)}, u32[]{:S(2)}) collective-permute-start(f32[3,72,512]{2,1,0:T(8,128)S(1)} %collective-permute-done.8.near_late), channel_id=1, source_target_pairs={{0,2},{2,4},{3,1},{4,6},{5,3},{7,5},{16,18},{18,20},{19,17},{20,22... | collective-permute-start | bytes 1327112 | tf_op jit(solution)/shard_map/ppermute | solution.py:542
  23.9 5.6 %collective-permute-start.4 = (f32[96,128]{1,0:T(8,128)S(1)}, f32[96,128]{1,0:T(8,128)S(1)}, u32[]{:S(2)}, u32[]{:S(2)}) collective-permute-start(f32[96,128]{1,0:T(8,128)S(1)} %get-tuple-element.32.halo_near), channel_id=1, source_target_pairs={{8,9},{9,8},{10,11},{11,10},{12,13},{13,12},{14,15},{15,14}} | collective-permute-start | bytes 147464 | tf_op jit(solution)/shard_map/ppermute | solution.py:542
  29.5 6.6 %collective-permute-start.5 = (f32[96,128]{1,0:T(8,128)S(1)}, f32[96,128]{1,0:T(8,128)S(1)}, u32[]{:S(2)}, u32[]{:S(2)}) collective-permute-start(f32[96,128]{1,0:T(8,128)S(1)} %get-tuple-element.33.halo_far), channel_id=1, source_target_pairs={{9,10},{10,9},{11,12},{12,11},{13,14},{14,13}} | collective-permute-start | bytes 147464 | tf_op jit(solution)/shard_map/ppermute | solution.py:542
  46.4 6.3 %collective-permute-start.11 = (f32[128,384]{1,0:T(8,128)S(1)}, f32[128,384]{1,0:T(8,128)S(1)}, u32[]{:S(2)}, u32[]{:S(2)}) collective-permute-start(f32[128,384]{1,0:T(8,128)S(1)} %get-tuple-element.47), channel_id=1, source_target_pairs={{0,16},{1,17},{2,18},{3,19},{4,20},{5,21},{6,22},{7,23},{16,0},{17... | collective-permute-start | bytes 589832 | tf_op jit(solution)/shard_map/ppermute | solution.py:542
  47.2 9.2 %collective-permute-start.13 = (f32[128,384]{1,0:T(8,128)S(1)}, f32[128,384]{1,0:T(8,128)S(1)}, u32[]{:S(2)}, u32[]{:S(2)}) collective-permute-start(f32[128,384]{1,0:T(8,128)S(1)} %get-tuple-element.48), channel_id=1, source_target_pairs={{16,8},{17,9},{18,10},{19,11},{20,12},{21,13},{22,14},{23,15}} | collective-permute-start | bytes 589832 | tf_op jit(solution)/shard_map/ppermute | solution.py:542
  48.5 7.9 %collective-permute-start.12 = (f32[128,384]{1,0:T(8,128)S(1)}, f32[128,384]{1,0:T(8,128)S(1)}, u32[]{:S(2)}, u32[]{:S(2)}) collective-permute-start(f32[128,384]{1,0:T(8,128)S(1)} %get-tuple-element.48), channel_id=1, source_target_pairs={{0,8},{1,9},{2,10},{3,11},{4,12},{5,13},{6,14},{7,15}} | collective-permute-start | bytes 589832 | tf_op jit(solution)/shard_map/ppermute | solution.py:542
  (2 other events, 7.7 us)
